TPU v7x, 32 devices: a whole 2x2x4 slice. The times are simulated.
32 devices in a mesh: ctx: 8 (over z, x), head: 4 (over y, core).
Axes of the slice: x: 2, y: 2, z: 4, core: 2. Of those that a mesh axis runs over, the one named last changes fastest.
Arguments:
- queries: bfloat16 [1024, 1024], P('ctx', 'head'), may hold values from -27 to 27
- keys: bfloat16 [1024, 128], P('ctx'), may hold values from -4 to 4
- values: bfloat16 [1024, 128], P('ctx'), may hold values from -6 to 6
- dout: bfloat16 [1024, 1024], P('ctx', 'head'), may hold values from -6 to 6
- positions: int32 [1024], P('ctx'), may hold values from 0 to 1023, as said below
- doc_ids: int32 [1024], P('ctx'), may hold values from 0 to 15, as said below
- w_query: bfloat16 [1024, 16384], P('head'), may hold values from -0.1875 to 0.1875
- w_kv: bfloat16 [256, 16384], P(None, 'head'), may hold values from -0.375 to 0.375
Outputs:
- grad_input: bfloat16 [1024, 16384], P('ctx', 'head')
Inputs may be any that keep to these rules, and one draw needn't show every extreme that they name: Stored rows come in aligned runs of 64 rows that hold 64 consecutive positions in order, starting at a multiple of 64; every position of the sequence is stored once. `doc_ids`: A document is a set of consecutive positions that begins at a multiple of 64; its id is its first position divided by 64. The first and the last run of 64 positions each begin a document.
All inputs are finite; a program needn't handle non-finite values.
Results may differ from a plain program's by a relative error of at most 0.019.
Values may be sent and summed in bfloat16 or wider, within the bound.
No kernel may reach another device: no remote copies, remote signals or barrier semaphores. Data moves between devices by JAX's collectives and lax.ppermute only.
A program may use at most 128 MiB of HBM per device.

v0:
```python
import math

import jax
import jax.numpy as jnp
from jax import lax
from jax.sharding import PartitionSpec as P


def from_behind(value, axis, steps):
    count = lax.axis_size(axis)
    pairs = [(source, (source + steps) % count) for source in range(count)]
    return lax.ppermute(value, axis, pairs)


def on_device(queries, keys, values, dout, positions, doc_ids, w_query, w_kv):
    head_size = keys.shape[1]
    tok_rows = queries.shape[0]
    local_heads = queries.shape[1] // head_size
    inv_root = 1.0 / math.sqrt(head_size)
    query_rows = queries.reshape(tok_rows, local_heads, head_size)
    dout_rows = dout.reshape(tok_rows, local_heads, head_size)

    def allowed_pairs(pos_piece, doc_piece):
        return (doc_ids[:, None] == doc_piece[None, :]) & (pos_piece[None, :] <= positions[:, None])

    def block_scores(key_piece):
        return (
            jnp.einsum("qhd,kd->hqk", query_rows, key_piece, preferred_element_type=jnp.float32)
            * inv_root
        )

    def grad_terms(key_piece, value_piece, allowed, log_total, row_delta):
        probs = jnp.where(
            allowed[None], jnp.exp(block_scores(key_piece) - log_total[..., None]), 0.0
        )
        probs_low = probs.astype(jnp.bfloat16)
        value_term = jnp.einsum(
            "hqk,qhd->kd", probs_low, dout_rows, preferred_element_type=jnp.float32
        )
        dprob = jnp.einsum(
            "qhd,kd->hqk", dout_rows, value_piece, preferred_element_type=jnp.float32
        )
        dscore = (probs * (dprob - row_delta[..., None])).astype(jnp.bfloat16)
        query_term = jnp.einsum(
            "hqk,kd->qhd", dscore, key_piece, preferred_element_type=jnp.float32
        )
        key_term = jnp.einsum("hqk,qhd->kd", dscore, query_rows, preferred_element_type=jnp.float32)
        return (query_term, jnp.concatenate([key_term, value_term], axis=1))

    key_piece = lax.all_gather(keys, "ctx", axis=0, tiled=True)
    value_piece = lax.all_gather(values, "ctx", axis=0, tiled=True)
    pos_piece = lax.all_gather(positions, "ctx", axis=0, tiled=True)
    doc_piece = lax.all_gather(doc_ids, "ctx", axis=0, tiled=True)
    allowed = allowed_pairs(pos_piece, doc_piece)
    row_max = jnp.full((local_heads, tok_rows), -1e30, jnp.float32)
    masked = jnp.where(allowed[None], block_scores(key_piece), -1e30)
    new_max = jnp.maximum(row_max, jnp.max(masked, axis=-1))
    probs = jnp.where(allowed[None], jnp.exp(masked - new_max[..., None]), 0.0)
    mixed = jnp.einsum("hqk,kd->hqd", probs, value_piece.astype(jnp.float32))
    row_total = jnp.sum(probs, axis=-1)
    finish_log_total = new_max + jnp.log(row_total)
    output = mixed / row_total[..., None]
    finish_row_delta = jnp.einsum("qhd,hqd->hq", dout_rows.astype(jnp.float32), output)
    log_total = finish_log_total
    row_delta = finish_row_delta

    def hop_step(hop_count, current):
        key_piece, value_piece, pos_piece, doc_piece, kv_total, query_total = current
        allowed = allowed_pairs(pos_piece, doc_piece)
        query_term, kv_term = grad_terms(key_piece, value_piece, allowed, log_total, row_delta)
        query_total, kv_total = (query_total + query_term, kv_total + kv_term)
        key_piece, value_piece, pos_piece, doc_piece = from_behind(
            (key_piece, value_piece, pos_piece, doc_piece), "ctx", 1
        )
        kv_total = from_behind(kv_total.astype(jnp.bfloat16), "ctx", 1).astype(kv_total.dtype)
        return (key_piece, value_piece, pos_piece, doc_piece, kv_total, query_total)

    start_state = (
        keys,
        values,
        positions,
        doc_ids,
        jnp.zeros((tok_rows, 2 * head_size), jnp.float32),
        jnp.zeros((tok_rows, local_heads, head_size), jnp.float32),
    )
    final_state = lax.fori_loop(0, lax.axis_size("ctx"), hop_step, start_state)
    kv_total = final_state[4]
    query_total = final_state[5]
    kv_total = lax.psum(kv_total.astype(jnp.bfloat16), "head").astype(jnp.float32)
    column_scale = jnp.where(jnp.arange(2 * head_size) < head_size, inv_root, 1.0).astype(
        jnp.float32
    )
    kv_grads = (kv_total * column_scale[None, :]).astype(jnp.bfloat16)
    query_grad = (
        (query_total * inv_root).astype(jnp.bfloat16).reshape(tok_rows, local_heads * head_size)
    )
    kv_part = jnp.dot(kv_grads, w_kv, preferred_element_type=jnp.float32)
    every_head = lax.all_gather(query_grad, "head", axis=1, tiled=True)
    width_share = lax.all_to_all(w_query, "head", split_axis=1, concat_axis=0, tiled=True)
    query_part = jnp.dot(every_head, width_share, preferred_element_type=jnp.float32)
    return (query_part + kv_part).astype(jnp.bfloat16)


def solution(mesh):
    placed = (
        P("ctx", "head"),
        P("ctx", None),
        P("ctx", None),
        P("ctx", "head"),
        P("ctx"),
        P("ctx"),
        P("head", None),
        P(None, "head"),
    )
    return jax.shard_map(
        on_device, mesh=mesh, in_specs=placed, out_specs=P("ctx", "head"), check_vma=False
    )
```

profile of v0, /device:TPU:0, one launch (start us, length us, event | category | flops | bytes accessed | tf_op | source)
XLA Modules:
  0.0 267.4 jit_solution(857788150876132559)
XLA Ops:
  8.2 11.9 %copy.48 = bf16[256,16384]{0,1:T(8,128)(2,1)} copy(bf16[256,16384]{1,0:T(8,128)(2,1)} %param.16) | data formatting | bytes 16777216 | tf_op args[6]
  20.2 5.8 %all-to-all-start = ((bf16[256,4,4096]{0,2,1:T(8,128)(2,1)}), bf16[256,4,4096]{0,2,1:T(8,128)(2,1)}, u32[]{:S(2)}, u32[]{:S(2)}) async-start(bf16[256,4,4096]{0,2,1:T(8,128)(2,1)} %bitcast.97), calls=%async_computation | async-start | bytes 16777216 | tf_op jit(solution)/shard_map/all_to_all | solution.py:99
  26.1 22.2 %all-gather = s32[8,1,128]{2,1,0:T(1,128)S(1)} all-gather(s32[1,1,128]{2,1,0:T(1,128)S(1)} %bitcast.103), channel_id=1, replica_groups=mesh['ctx'=8,'head'=4] {'ctx'}, dimensions={0}, use_global_device_ids=true | all-gather | bytes 4608 | tf_op jit(solution)/shard_map/all_gather | solution.py:53
  48.2 16.1 %all-gather.1 = s32[8,1,128]{2,1,0:T(1,128)S(1)} all-gather(s32[1,1,128]{2,1,0:T(1,128)S(1)} %bitcast.102), channel_id=1, replica_groups=mesh['ctx'=8,'head'=4] {'ctx'}, dimensions={0}, use_global_device_ids=true | all-gather | bytes 4608 | tf_op jit(solution)/shard_map/all_gather | solution.py:52
  64.6 30.7 %all_gather.18 = bf16[1024,128]{1,0:T(8,128)(2,1)S(1)} all-gather(bf16[128,128]{1,0:T(8,128)(2,1)S(1)} %copy.88), channel_id=1, replica_groups=mesh['ctx'=8,'head'=4] {'ctx'}, dimensions={0}, use_global_device_ids=true | all-gather | bytes 294912 | tf_op jit(solution)/shard_map/all_gather | solution.py:51
  95.3 30.7 %all_gather.17 = bf16[1024,128]{1,0:T(8,128)(2,1)S(1)} all-gather(bf16[128,128]{1,0:T(8,128)(2,1)S(1)} %copy.87), channel_id=1, replica_groups=mesh['ctx'=8,'head'=4] {'ctx'}, dimensions={0}, use_global_device_ids=true | all-gather | bytes 294912 | tf_op jit(solution)/shard_map/all_gather | solution.py:50
  127.6 99.7 %while.21 = (s32[]{:T(128)}, bf16[128,128]{1,0:T(8,128)(2,1)S(1)}, bf16[128,128]{1,0:T(8,128)(2,1)S(1)}, s32[128]{0:T(128)S(1)}, s32[128]{0:T(128)S(1)}, /*index...) while((s32[]{:T(128)}, bf16[128,128]{1,0:T(8,128)(2,1)S(1)}, ...), condition=%wide.region_3.4_spmd.clone, body=%wide.region_2.3_spmd.clone.sunk | while | flops 42450944 | bytes 2566496 | solution.py:86
  130.2 1.9 collective-permute-start.4
  132.3 5.3 %collective-permute-done.4 = bf16[128,256]{0,1:T(8,128)(2,1)S(1)} collective-permute-done((bf16[128,256]{0,1:T(8,128)(2,1)S(1)}, bf16[128,256]{0,1:T(8,128)(2,1)S(1)}, u32[]{:S(2)}, u32[]{:S(2)}) %collective-permute-start.4) | collective-permute-done | bytes 65568 | tf_op jit(solution)/shard_map/while/body/eval_jaxpr/ppermute | solution.py:12
  137.7 2.2 collective-permute-start.3
  141.4 3.3 %collective-permute-start = (bf16[128,128]{1,0:T(8,128)(2,1)S(1)}, bf16[128,128]{1,0:T(8,128)(2,1)S(1)}, u32[]{:S(2)}, u32[]{:S(2)}) collective-permute-start(bf16[128,128]{1,0:T(8,128)(2,1)S(1)} %copy.71), channel_id=1, source_target_pairs={{0,4},{4,8},{8,12},{12,16},{16,20},{20,24},{24,28},{28,0},{1,5},{5... | collective-permute-start | bytes 98312 | tf_op jit(solution)/shard_map/while/body/eval_jaxpr/ppermute | solution.py:12
  145.8 6.7 %collective-permute-done.4 = bf16[128,256]{0,1:T(8,128)(2,1)S(1)} collective-permute-done((bf16[128,256]{0,1:T(8,128)(2,1)S(1)}, bf16[128,256]{0,1:T(8,128)(2,1)S(1)}, u32[]{:S(2)}, u32[]{:S(2)}) %collective-permute-start.4) | collective-permute-done | bytes 65568 | tf_op jit(solution)/shard_map/while/body/eval_jaxpr/ppermute | solution.py:12
  152.7 1.9 collective-permute-start
  155.8 6.7 %collective-permute-done.4 = bf16[128,256]{0,1:T(8,128)(2,1)S(1)} collective-permute-done((bf16[128,256]{0,1:T(8,128)(2,1)S(1)}, bf16[128,256]{0,1:T(8,128)(2,1)S(1)}, u32[]{:S(2)}, u32[]{:S(2)}) %collective-permute-start.4) | collective-permute-done | bytes 65568 | tf_op jit(solution)/shard_map/while/body/eval_jaxpr/ppermute | solution.py:12
  163.0 3.3 %collective-permute-start.1 = (bf16[128,128]{1,0:T(8,128)(2,1)S(1)}, bf16[128,128]{1,0:T(8,128)(2,1)S(1)}, u32[]{:S(2)}, u32[]{:S(2)}) collective-permute-start(bf16[128,128]{1,0:T(8,128)(2,1)S(1)} %copy.72), channel_id=1, source_target_pairs={{0,4},{4,8},{8,12},{12,16},{16,20},{20,24},{24,28},{28,0},{1,5},{5... | collective-permute-start | bytes 98312 | tf_op jit(solution)/shard_map/while/body/eval_jaxpr/ppermute | solution.py:12
  166.3 3.3 %collective-permute-start = (bf16[128,128]{1,0:T(8,128)(2,1)S(1)}, bf16[128,128]{1,0:T(8,128)(2,1)S(1)}, u32[]{:S(2)}, u32[]{:S(2)}) collective-permute-start(bf16[128,128]{1,0:T(8,128)(2,1)S(1)} %copy.71), channel_id=1, source_target_pairs={{0,4},{4,8},{8,12},{12,16},{16,20},{20,24},{24,28},{28,0},{1,5},{5... | collective-permute-start | bytes 98312 | tf_op jit(solution)/shard_map/while/body/eval_jaxpr/ppermute | solution.py:12
  170.7 6.7 %collective-permute-done.4 = bf16[128,256]{0,1:T(8,128)(2,1)S(1)} collective-permute-done((bf16[128,256]{0,1:T(8,128)(2,1)S(1)}, bf16[128,256]{0,1:T(8,128)(2,1)S(1)}, u32[]{:S(2)}, u32[]{:S(2)}) %collective-permute-start.4) | collective-permute-done | bytes 65568 | tf_op jit(solution)/shard_map/while/body/eval_jaxpr/ppermute | solution.py:12
  177.7 2.2 collective-permute-start
  181.0 6.8 %collective-permute-done.4 = bf16[128,256]{0,1:T(8,128)(2,1)S(1)} collective-permute-done((bf16[128,256]{0,1:T(8,128)(2,1)S(1)}, bf16[128,256]{0,1:T(8,128)(2,1)S(1)}, u32[]{:S(2)}, u32[]{:S(2)}) %collective-permute-start.4) | collective-permute-done | bytes 65568 | tf_op jit(solution)/shard_map/while/body/eval_jaxpr/ppermute | solution.py:12
  188.0 3.2 %collective-permute-start.1 = (bf16[128,128]{1,0:T(8,128)(2,1)S(1)}, bf16[128,128]{1,0:T(8,128)(2,1)S(1)}, u32[]{:S(2)}, u32[]{:S(2)}) collective-permute-start(bf16[128,128]{1,0:T(8,128)(2,1)S(1)} %copy.72), channel_id=1, source_target_pairs={{0,4},{4,8},{8,12},{12,16},{16,20},{20,24},{24,28},{28,0},{1,5},{5... | collective-permute-start | bytes 98312 | tf_op jit(solution)/shard_map/while/body/eval_jaxpr/ppermute | solution.py:12
  191.2 3.3 %collective-permute-start = (bf16[128,128]{1,0:T(8,128)(2,1)S(1)}, bf16[128,128]{1,0:T(8,128)(2,1)S(1)}, u32[]{:S(2)}, u32[]{:S(2)}) collective-permute-start(bf16[128,128]{1,0:T(8,128)(2,1)S(1)} %copy.71), channel_id=1, source_target_pairs={{0,4},{4,8},{8,12},{12,16},{16,20},{20,24},{24,28},{28,0},{1,5},{5... | collective-permute-start | bytes 98312 | tf_op jit(solution)/shard_map/while/body/eval_jaxpr/ppermute | solution.py:12
  195.6 6.7 %collective-permute-done.4 = bf16[128,256]{0,1:T(8,128)(2,1)S(1)} collective-permute-done((bf16[128,256]{0,1:T(8,128)(2,1)S(1)}, bf16[128,256]{0,1:T(8,128)(2,1)S(1)}, u32[]{:S(2)}, u32[]{:S(2)}) %collective-permute-start.4) | collective-permute-done | bytes 65568 | tf_op jit(solution)/shard_map/while/body/eval_jaxpr/ppermute | solution.py:12
  202.6 2.3 collective-permute-start
  206.0 6.7 %collective-permute-done.4 = bf16[128,256]{0,1:T(8,128)(2,1)S(1)} collective-permute-done((bf16[128,256]{0,1:T(8,128)(2,1)S(1)}, bf16[128,256]{0,1:T(8,128)(2,1)S(1)}, u32[]{:S(2)}, u32[]{:S(2)}) %collective-permute-start.4) | collective-permute-done | bytes 65568 | tf_op jit(solution)/shard_map/while/body/eval_jaxpr/ppermute | solution.py:12
  212.9 3.2 %collective-permute-start.1 = (bf16[128,128]{1,0:T(8,128)(2,1)S(1)}, bf16[128,128]{1,0:T(8,128)(2,1)S(1)}, u32[]{:S(2)}, u32[]{:S(2)}) collective-permute-start(bf16[128,128]{1,0:T(8,128)(2,1)S(1)} %copy.72), channel_id=1, source_target_pairs={{0,4},{4,8},{8,12},{12,16},{16,20},{20,24},{24,28},{28,0},{1,5},{5... | collective-permute-start | bytes 98312 | tf_op jit(solution)/shard_map/while/body/eval_jaxpr/ppermute | solution.py:12
  216.1 3.3 %collective-permute-start = (bf16[128,128]{1,0:T(8,128)(2,1)S(1)}, bf16[128,128]{1,0:T(8,128)(2,1)S(1)}, u32[]{:S(2)}, u32[]{:S(2)}) collective-permute-start(bf16[128,128]{1,0:T(8,128)(2,1)S(1)} %copy.71), channel_id=1, source_target_pairs={{0,4},{4,8},{8,12},{12,16},{16,20},{20,24},{24,28},{28,0},{1,5},{5... | collective-permute-start | bytes 98312 | tf_op jit(solution)/shard_map/while/body/eval_jaxpr/ppermute | solution.py:12
  220.5 6.7 %collective-permute-done.4 = bf16[128,256]{0,1:T(8,128)(2,1)S(1)} collective-permute-done((bf16[128,256]{0,1:T(8,128)(2,1)S(1)}, bf16[128,256]{0,1:T(8,128)(2,1)S(1)}, u32[]{:S(2)}, u32[]{:S(2)}) %collective-permute-start.4) | collective-permute-done | bytes 65568 | tf_op jit(solution)/shard_map/while/body/eval_jaxpr/ppermute | solution.py:12
  228.0 6.9 %all_gather.19 = bf16[128,1024]{0,1:T(8,128)(2,1)S(1)} all-gather(bf16[128,256]{0,1:T(8,128)(2,1)S(1)} %bitcast.101), channel_id=1, replica_groups=mesh['ctx'=8,'head'=4] {'head'}, dimensions={1}, use_global_device_ids=true | all-gather | bytes 327680 | tf_op jit(solution)/shard_map/all_gather | solution.py:98
  234.9 12.0 %copy.49 = bf16[4,256,4096]{2,1,0:T(8,128)(2,1)} copy(bf16[4,256,4096]{1,2,0:T(8,128)(2,1)} %bitcast.14) | data formatting | bytes 16777216 | tf_op jit(solution)/shard_map/all_to_all | solution.py:99
  246.9 6.0 %fusion.25 = f32[128,4096]{1,0:T(8,128)} fusion(bf16[128,1024]{0,1:T(8,128)(2,1)S(1)} %all_gather.19, bf16[1024,4096]{1,0:T(8,128)(2,1)} %bitcast.96), kind=kOutput, calls=%fused_computation.43 | convolution fusion | flops 1073741824 | bytes 10747904 | tf_op jit(solution)/shard_map/dot_general | solution.py:100
  253.0 4.5 %all-reduce.2.cloned.1.call-done = bf16[128,256]{0,1:T(8,128)(2,1)} async-done(((bf16[128,256]{0,1:T(8,128)(2,1)}), bf16[128,256]{0,1:T(8,128)(2,1)}) %all-reduce.2.cloned.1.call-update) | async-done | bytes 65552 | tf_op jit(solution)/shard_map/psum | solution.py:89
  257.4 3.2 %fusion.13 = bf16[128,4096]{1,0:T(8,128)(2,1)} fusion(f32[128,4096]{1,0:T(8,128)} %fusion.25, bf16[256,4096]{1,0:T(8,128)(2,1)S(1)} %copy-done, bf16[128,256]{0,1:T(8,128)(2,1)} %all-reduce.2.cloned.1.call-done, f32[256]{0:T(256)S(1)} %compare_select_fusion), kind=kOutput, calls=%fused_computation.21 | convolution fusion | flops 269582336 | bytes 5309440 | tf_op jit(solution)/shard_map/dot_general | solution.py:97
  (189 shorter events, 17.6 us)
Async XLA Ops:
  20.2 214.8 %all-to-all-start = ((bf16[256,4,4096]{0,2,1:T(8,128)(2,1)}), bf16[256,4,4096]{0,2,1:T(8,128)(2,1)}, u32[]{:S(2)}, u32[]{:S(2)}) async-start(bf16[256,4,4096]{0,2,1:T(8,128)(2,1)} %bitcast.97), calls=%async_computation | async-start | bytes 16777216 | tf_op jit(solution)/shard_map/all_to_all | solution.py:99
  25.9 231.5 %all-reduce.2.cloned.1.call-start = ((), (), s32[]{:S(2)}) async-start(), calls=%async_computation.1 | async-start | bytes 131072 | tf_op jit(solution)/shard_map/psum | solution.py:89
  127.6 10.0 %collective-permute-start.2 = (s32[128]{0:T(128)S(1)}, s32[128]{0:T(128)S(1)}, u32[]{:S(2)}, u32[]{:S(2)}) collective-permute-start(s32[128]{0:T(128)S(1)} %copy.73), channel_id=1, source_target_pairs={{0,4},{4,8},{8,12},{12,16},{16,20},{20,24},{24,28},{28,0},{1,5},{5... | collective-permute-start | bytes 1544 | tf_op jit(solution)/shard_map/while/body/eval_jaxpr/ppermute | solution.py:12
  127.7 9.9 %collective-permute-start.3 = (s32[128]{0:T(128)S(1)}, s32[128]{0:T(128)S(1)}, u32[]{:S(2)}, u32[]{:S(2)}) collective-permute-start(s32[128]{0:T(128)S(1)} %copy.74), channel_id=1, source_target_pairs={{0,4},{4,8},{8,12},{12,16},{16,20},{20,24},{24,28},{28,0},{1,5},{5... | collective-permute-start | bytes 1544 | tf_op jit(solution)/shard_map/while/body/eval_jaxpr/ppermute | solution.py:12
  137.6 14.8 %collective-permute-start.2 = (s32[128]{0:T(128)S(1)}, s32[128]{0:T(128)S(1)}, u32[]{:S(2)}, u32[]{:S(2)}) collective-permute-start(s32[128]{0:T(128)S(1)} %copy.73), channel_id=1, source_target_pairs={{0,4},{4,8},{8,12},{12,16},{16,20},{20,24},{24,28},{28,0},{1,5},{5... | collective-permute-start | bytes 1544 | tf_op jit(solution)/shard_map/while/body/eval_jaxpr/ppermute | solution.py:12
  137.7 14.8 %collective-permute-start.3 = (s32[128]{0:T(128)S(1)}, s32[128]{0:T(128)S(1)}, u32[]{:S(2)}, u32[]{:S(2)}) collective-permute-start(s32[128]{0:T(128)S(1)} %copy.74), channel_id=1, source_target_pairs={{0,4},{4,8},{8,12},{12,16},{16,20},{20,24},{24,28},{28,0},{1,5},{5... | collective-permute-start | bytes 1544 | tf_op jit(solution)/shard_map/while/body/eval_jaxpr/ppermute | solution.py:12
  139.9 12.6 %collective-permute-start.1 = (bf16[128,128]{1,0:T(8,128)(2,1)S(1)}, bf16[128,128]{1,0:T(8,128)(2,1)S(1)}, u32[]{:S(2)}, u32[]{:S(2)}) collective-permute-start(bf16[128,128]{1,0:T(8,128)(2,1)S(1)} %copy.72), channel_id=1, source_target_pairs={{0,4},{4,8},{8,12},{12,16},{16,20},{20,24},{24,28},{28,0},{1,5},{5... | collective-permute-start | bytes 98312 | tf_op jit(solution)/shard_map/while/body/eval_jaxpr/ppermute | solution.py:12
  141.4 11.1 %collective-permute-start = (bf16[128,128]{1,0:T(8,128)(2,1)S(1)}, bf16[128,128]{1,0:T(8,128)(2,1)S(1)}, u32[]{:S(2)}, u32[]{:S(2)}) collective-permute-start(bf16[128,128]{1,0:T(8,128)(2,1)S(1)} %copy.71), channel_id=1, source_target_pairs={{0,4},{4,8},{8,12},{12,16},{16,20},{20,24},{24,28},{28,0},{1,5},{5... | collective-permute-start | bytes 98312 | tf_op jit(solution)/shard_map/while/body/eval_jaxpr/ppermute | solution.py:12
  152.5 10.0 %collective-permute-start.2 = (s32[128]{0:T(128)S(1)}, s32[128]{0:T(128)S(1)}, u32[]{:S(2)}, u32[]{:S(2)}) collective-permute-start(s32[128]{0:T(128)S(1)} %copy.73), channel_id=1, source_target_pairs={{0,4},{4,8},{8,12},{12,16},{16,20},{20,24},{24,28},{28,0},{1,5},{5... | collective-permute-start | bytes 1544 | tf_op jit(solution)/shard_map/while/body/eval_jaxpr/ppermute | solution.py:12
  152.6 9.9 %collective-permute-start.3 = (s32[128]{0:T(128)S(1)}, s32[128]{0:T(128)S(1)}, u32[]{:S(2)}, u32[]{:S(2)}) collective-permute-start(s32[128]{0:T(128)S(1)} %copy.74), channel_id=1, source_target_pairs={{0,4},{4,8},{8,12},{12,16},{16,20},{20,24},{24,28},{28,0},{1,5},{5... | collective-permute-start | bytes 1544 | tf_op jit(solution)/shard_map/while/body/eval_jaxpr/ppermute | solution.py:12
  152.7 9.8 %collective-permute-start.1 = (bf16[128,128]{1,0:T(8,128)(2,1)S(1)}, bf16[128,128]{1,0:T(8,128)(2,1)S(1)}, u32[]{:S(2)}, u32[]{:S(2)}) collective-permute-start(bf16[128,128]{1,0:T(8,128)(2,1)S(1)} %copy.72), channel_id=1, source_target_pairs={{0,4},{4,8},{8,12},{12,16},{16,20},{20,24},{24,28},{28,0},{1,5},{5... | collective-permute-start | bytes 98312 | tf_op jit(solution)/shard_map/while/body/eval_jaxpr/ppermute | solution.py:12
  152.7 9.8 %collective-permute-start = (bf16[128,128]{1,0:T(8,128)(2,1)S(1)}, bf16[128,128]{1,0:T(8,128)(2,1)S(1)}, u32[]{:S(2)}, u32[]{:S(2)}) collective-permute-start(bf16[128,128]{1,0:T(8,128)(2,1)S(1)} %copy.71), channel_id=1, source_target_pairs={{0,4},{4,8},{8,12},{12,16},{16,20},{20,24},{24,28},{28,0},{1,5},{5... | collective-permute-start | bytes 98312 | tf_op jit(solution)/shard_map/while/body/eval_jaxpr/ppermute | solution.py:12
  162.5 14.8 %collective-permute-start.2 = (s32[128]{0:T(128)S(1)}, s32[128]{0:T(128)S(1)}, u32[]{:S(2)}, u32[]{:S(2)}) collective-permute-start(s32[128]{0:T(128)S(1)} %copy.73), channel_id=1, source_target_pairs={{0,4},{4,8},{8,12},{12,16},{16,20},{20,24},{24,28},{28,0},{1,5},{5... | collective-permute-start | bytes 1544 | tf_op jit(solution)/shard_map/while/body/eval_jaxpr/ppermute | solution.py:12
  162.6 14.8 %collective-permute-start.3 = (s32[128]{0:T(128)S(1)}, s32[128]{0:T(128)S(1)}, u32[]{:S(2)}, u32[]{:S(2)}) collective-permute-start(s32[128]{0:T(128)S(1)} %copy.74), channel_id=1, source_target_pairs={{0,4},{4,8},{8,12},{12,16},{16,20},{20,24},{24,28},{28,0},{1,5},{5... | collective-permute-start | bytes 1544 | tf_op jit(solution)/shard_map/while/body/eval_jaxpr/ppermute | solution.py:12
  163.0 14.4 %collective-permute-start.1 = (bf16[128,128]{1,0:T(8,128)(2,1)S(1)}, bf16[128,128]{1,0:T(8,128)(2,1)S(1)}, u32[]{:S(2)}, u32[]{:S(2)}) collective-permute-start(bf16[128,128]{1,0:T(8,128)(2,1)S(1)} %copy.72), channel_id=1, source_target_pairs={{0,4},{4,8},{8,12},{12,16},{16,20},{20,24},{24,28},{28,0},{1,5},{5... | collective-permute-start | bytes 98312 | tf_op jit(solution)/shard_map/while/body/eval_jaxpr/ppermute | solution.py:12
  166.3 11.1 %collective-permute-start = (bf16[128,128]{1,0:T(8,128)(2,1)S(1)}, bf16[128,128]{1,0:T(8,128)(2,1)S(1)}, u32[]{:S(2)}, u32[]{:S(2)}) collective-permute-start(bf16[128,128]{1,0:T(8,128)(2,1)S(1)} %copy.71), channel_id=1, source_target_pairs={{0,4},{4,8},{8,12},{12,16},{16,20},{20,24},{24,28},{28,0},{1,5},{5... | collective-permute-start | bytes 98312 | tf_op jit(solution)/shard_map/while/body/eval_jaxpr/ppermute | solution.py:12
  177.4 10.3 %collective-permute-start.2 = (s32[128]{0:T(128)S(1)}, s32[128]{0:T(128)S(1)}, u32[]{:S(2)}, u32[]{:S(2)}) collective-permute-start(s32[128]{0:T(128)S(1)} %copy.73), channel_id=1, source_target_pairs={{0,4},{4,8},{8,12},{12,16},{16,20},{20,24},{24,28},{28,0},{1,5},{5... | collective-permute-start | bytes 1544 | tf_op jit(solution)/shard_map/while/body/eval_jaxpr/ppermute | solution.py:12
  177.5 10.3 %collective-permute-start.3 = (s32[128]{0:T(128)S(1)}, s32[128]{0:T(128)S(1)}, u32[]{:S(2)}, u32[]{:S(2)}) collective-permute-start(s32[128]{0:T(128)S(1)} %copy.74), channel_id=1, source_target_pairs={{0,4},{4,8},{8,12},{12,16},{16,20},{20,24},{24,28},{28,0},{1,5},{5... | collective-permute-start | bytes 1544 | tf_op jit(solution)/shard_map/while/body/eval_jaxpr/ppermute | solution.py:12
  177.6 10.2 %collective-permute-start.1 = (bf16[128,128]{1,0:T(8,128)(2,1)S(1)}, bf16[128,128]{1,0:T(8,128)(2,1)S(1)}, u32[]{:S(2)}, u32[]{:S(2)}) collective-permute-start(bf16[128,128]{1,0:T(8,128)(2,1)S(1)} %copy.72), channel_id=1, source_target_pairs={{0,4},{4,8},{8,12},{12,16},{16,20},{20,24},{24,28},{28,0},{1,5},{5... | collective-permute-start | bytes 98312 | tf_op jit(solution)/shard_map/while/body/eval_jaxpr/ppermute | solution.py:12
  177.7 10.1 %collective-permute-start = (bf16[128,128]{1,0:T(8,128)(2,1)S(1)}, bf16[128,128]{1,0:T(8,128)(2,1)S(1)}, u32[]{:S(2)}, u32[]{:S(2)}) collective-permute-start(bf16[128,128]{1,0:T(8,128)(2,1)S(1)} %copy.71), channel_id=1, source_target_pairs={{0,4},{4,8},{8,12},{12,16},{16,20},{20,24},{24,28},{28,0},{1,5},{5... | collective-permute-start | bytes 98312 | tf_op jit(solution)/shard_map/while/body/eval_jaxpr/ppermute | solution.py:12
  187.8 14.4 %collective-permute-start.2 = (s32[128]{0:T(128)S(1)}, s32[128]{0:T(128)S(1)}, u32[]{:S(2)}, u32[]{:S(2)}) collective-permute-start(s32[128]{0:T(128)S(1)} %copy.73), channel_id=1, source_target_pairs={{0,4},{4,8},{8,12},{12,16},{16,20},{20,24},{24,28},{28,0},{1,5},{5... | collective-permute-start | bytes 1544 | tf_op jit(solution)/shard_map/while/body/eval_jaxpr/ppermute | solution.py:12
  187.9 14.4 %collective-permute-start.3 = (s32[128]{0:T(128)S(1)}, s32[128]{0:T(128)S(1)}, u32[]{:S(2)}, u32[]{:S(2)}) collective-permute-start(s32[128]{0:T(128)S(1)} %copy.74), channel_id=1, source_target_pairs={{0,4},{4,8},{8,12},{12,16},{16,20},{20,24},{24,28},{28,0},{1,5},{5... | collective-permute-start | bytes 1544 | tf_op jit(solution)/shard_map/while/body/eval_jaxpr/ppermute | solution.py:12
  188.0 14.3 %collective-permute-start.1 = (bf16[128,128]{1,0:T(8,128)(2,1)S(1)}, bf16[128,128]{1,0:T(8,128)(2,1)S(1)}, u32[]{:S(2)}, u32[]{:S(2)}) collective-permute-start(bf16[128,128]{1,0:T(8,128)(2,1)S(1)} %copy.72), channel_id=1, source_target_pairs={{0,4},{4,8},{8,12},{12,16},{16,20},{20,24},{24,28},{28,0},{1,5},{5... | collective-permute-start | bytes 98312 | tf_op jit(solution)/shard_map/while/body/eval_jaxpr/ppermute | solution.py:12
  191.2 11.1 %collective-permute-start = (bf16[128,128]{1,0:T(8,128)(2,1)S(1)}, bf16[128,128]{1,0:T(8,128)(2,1)S(1)}, u32[]{:S(2)}, u32[]{:S(2)}) collective-permute-start(bf16[128,128]{1,0:T(8,128)(2,1)S(1)} %copy.71), channel_id=1, source_target_pairs={{0,4},{4,8},{8,12},{12,16},{16,20},{20,24},{24,28},{28,0},{1,5},{5... | collective-permute-start | bytes 98312 | tf_op jit(solution)/shard_map/while/body/eval_jaxpr/ppermute | solution.py:12
  202.3 10.3 %collective-permute-start.2 = (s32[128]{0:T(128)S(1)}, s32[128]{0:T(128)S(1)}, u32[]{:S(2)}, u32[]{:S(2)}) collective-permute-start(s32[128]{0:T(128)S(1)} %copy.73), channel_id=1, source_target_pairs={{0,4},{4,8},{8,12},{12,16},{16,20},{20,24},{24,28},{28,0},{1,5},{5... | collective-permute-start | bytes 1544 | tf_op jit(solution)/shard_map/while/body/eval_jaxpr/ppermute | solution.py:12
  202.4 10.3 %collective-permute-start.3 = (s32[128]{0:T(128)S(1)}, s32[128]{0:T(128)S(1)}, u32[]{:S(2)}, u32[]{:S(2)}) collective-permute-start(s32[128]{0:T(128)S(1)} %copy.74), channel_id=1, source_target_pairs={{0,4},{4,8},{8,12},{12,16},{16,20},{20,24},{24,28},{28,0},{1,5},{5... | collective-permute-start | bytes 1544 | tf_op jit(solution)/shard_map/while/body/eval_jaxpr/ppermute | solution.py:12
  202.5 10.2 %collective-permute-start.1 = (bf16[128,128]{1,0:T(8,128)(2,1)S(1)}, bf16[128,128]{1,0:T(8,128)(2,1)S(1)}, u32[]{:S(2)}, u32[]{:S(2)}) collective-permute-start(bf16[128,128]{1,0:T(8,128)(2,1)S(1)} %copy.72), channel_id=1, source_target_pairs={{0,4},{4,8},{8,12},{12,16},{16,20},{20,24},{24,28},{28,0},{1,5},{5... | collective-permute-start | bytes 98312 | tf_op jit(solution)/shard_map/while/body/eval_jaxpr/ppermute | solution.py:12
  202.6 10.1 %collective-permute-start = (bf16[128,128]{1,0:T(8,128)(2,1)S(1)}, bf16[128,128]{1,0:T(8,128)(2,1)S(1)}, u32[]{:S(2)}, u32[]{:S(2)}) collective-permute-start(bf16[128,128]{1,0:T(8,128)(2,1)S(1)} %copy.71), channel_id=1, source_target_pairs={{0,4},{4,8},{8,12},{12,16},{16,20},{20,24},{24,28},{28,0},{1,5},{5... | collective-permute-start | bytes 98312 | tf_op jit(solution)/shard_map/while/body/eval_jaxpr/ppermute | solution.py:12
  212.8 14.4 %collective-permute-start.2 = (s32[128]{0:T(128)S(1)}, s32[128]{0:T(128)S(1)}, u32[]{:S(2)}, u32[]{:S(2)}) collective-permute-start(s32[128]{0:T(128)S(1)} %copy.73), channel_id=1, source_target_pairs={{0,4},{4,8},{8,12},{12,16},{16,20},{20,24},{24,28},{28,0},{1,5},{5... | collective-permute-start | bytes 1544 | tf_op jit(solution)/shard_map/while/body/eval_jaxpr/ppermute | solution.py:12
  212.8 14.4 %collective-permute-start.3 = (s32[128]{0:T(128)S(1)}, s32[128]{0:T(128)S(1)}, u32[]{:S(2)}, u32[]{:S(2)}) collective-permute-start(s32[128]{0:T(128)S(1)} %copy.74), channel_id=1, source_target_pairs={{0,4},{4,8},{8,12},{12,16},{16,20},{20,24},{24,28},{28,0},{1,5},{5... | collective-permute-start | bytes 1544 | tf_op jit(solution)/shard_map/while/body/eval_jaxpr/ppermute | solution.py:12
  212.9 14.3 %collective-permute-start.1 = (bf16[128,128]{1,0:T(8,128)(2,1)S(1)}, bf16[128,128]{1,0:T(8,128)(2,1)S(1)}, u32[]{:S(2)}, u32[]{:S(2)}) collective-permute-start(bf16[128,128]{1,0:T(8,128)(2,1)S(1)} %copy.72), channel_id=1, source_target_pairs={{0,4},{4,8},{8,12},{12,16},{16,20},{20,24},{24,28},{28,0},{1,5},{5... | collective-permute-start | bytes 98312 | tf_op jit(solution)/shard_map/while/body/eval_jaxpr/ppermute | solution.py:12
  216.1 11.1 %collective-permute-start = (bf16[128,128]{1,0:T(8,128)(2,1)S(1)}, bf16[128,128]{1,0:T(8,128)(2,1)S(1)}, u32[]{:S(2)}, u32[]{:S(2)}) collective-permute-start(bf16[128,128]{1,0:T(8,128)(2,1)S(1)} %copy.71), channel_id=1, source_target_pairs={{0,4},{4,8},{8,12},{12,16},{16,20},{20,24},{24,28},{28,0},{1,5},{5... | collective-permute-start | bytes 98312 | tf_op jit(solution)/shard_map/while/body/eval_jaxpr/ppermute | solution.py:12
  (15 other events, 427.0 us)
Sparse Core Ops, SparseCore 0:
  228.0 29.3 all-reduce.1
where the time goes:
time: 268 us; the launch traced here: 267 us
  blocking collectives  107 us (40%)
  waiting for transfers between devices  56.6 us (21%)
  starting transfers between devices  44.4 us (17%)
  local copies, waits for them, and re-layouts  26.1 us (10%)
  matrix products  16.4 us (6%)
  between operations  13.5 us (5%)
  other arithmetic  2.68 us (1%)
    ppermute x40, waiting for transfers between devices, from_behind(): return lax.ppermute(value, axis, pairs)  52.2 us
    ppermute x40, starting transfers between devices, from_behind(): return lax.ppermute(value, axis, pairs)  38.5 us
    all_gather x1, blocking collectives, on_device(): value_piece = lax.all_gather(values, 'ctx', axis=0, tiled=True)  30.7 us
    all_gather x1, blocking collectives, on_device(): key_piece = lax.all_gather(keys, 'ctx', axis=0, tiled=True)  30.7 us
    all_gather x1, blocking collectives, on_device(): doc_piece = lax.all_gather(doc_ids, 'ctx', axis=0, tiled=True)  22.2 us
    all_gather x1, blocking collectives, on_device(): pos_piece = lax.all_gather(positions, 'ctx', axis=0, tiled=True)  16.1 us
    unnamed x18, local copies, waits for them, and re-layouts  13.9 us
    all_to_all x1, local copies, waits for them, and re-layouts, on_device(): lax.all_to_all(w_query, 'head', split_axis=1, concat_axis=0, tiled=True)  12 us
  transfers between devices with their start and end apart: 42, of which 9 were waited for; matrix products, arithmetic and copies ran while one was open for 11% of the time, Pallas kernels for 0%

commit v1 on v0

v1 whole, which is shorter than its diff:
```python
import functools
import math

import jax
import jax.numpy as jnp
from jax import lax
from jax.experimental import pallas as pl
from jax.experimental.pallas import tpu as pltpu
from jax.sharding import PartitionSpec as P

RUN = 64
META_ROWS = 16
CHUNKS = 4
VMEM = pl.BlockSpec(memory_space=pltpu.VMEM)
SMEM = pl.BlockSpec(memory_space=pltpu.SMEM)


def params(limit_mib=32):
    return pltpu.CompilerParams(vmem_limit_bytes=limit_mib * 1024 * 1024)


def shifted(value, axis, steps):
    count = lax.axis_size(axis)
    pairs = [(source, (source + steps) % count) for source in range(count)]
    return lax.ppermute(value, axis, pairs)


def swapped(value, axis, bits):
    count = lax.axis_size(axis)
    return lax.ppermute(value, axis, [(source, source ^ bits) for source in range(count)])


def dot(a, b, contract):
    return lax.dot_general(a, b, (contract, ((), ())), preferred_element_type=jnp.float32)


def pack_kernel(pos_ref, key_ref, value_ref, piece_ref):
    rows, head_size = key_ref.shape
    piece_ref[0:rows, 0:head_size] = key_ref[...]
    piece_ref[0:rows, head_size:] = value_ref[...]
    row = lax.broadcasted_iota(jnp.int32, (META_ROWS, 2 * head_size), 0)
    meta = jnp.zeros((META_ROWS, 2 * head_size), jnp.int32)
    for run in range(rows // RUN):
        meta = jnp.where(row == run, pos_ref[run * RUN] // RUN, meta)
    piece_ref[rows:, :] = meta.astype(jnp.float32).astype(jnp.bfloat16)


def pack(positions, keys, values):
    rows, head_size = keys.shape
    return pl.pallas_call(
        pack_kernel,
        out_shape=jax.ShapeDtypeStruct((rows + META_ROWS, 2 * head_size), jnp.bfloat16),
        in_specs=[SMEM, VMEM, VMEM],
        out_specs=VMEM,
        compiler_params=params(),
        name="pack",
    )(positions, keys, values)


def attention_kernel(count, core_ref, row_ref, qm_ref, qo_ref, dm_ref, do_ref, *refs):
    pieces = refs[:count]
    dq_ref = refs[count]
    back = refs[count + 1 : 2 * count + 1]
    s_ref, dp_ref = refs[2 * count + 1 :]
    rows = qm_ref.shape[0]
    size = pieces[0].shape[1] // 2
    heads = qm_ref.shape[1] // size
    inv_root = 1.0 / math.sqrt(size)

    def stack(mine, other):
        parts = [ref[:, h * size : (h + 1) * size] for ref in (mine, other) for h in range(heads)]
        return jnp.concatenate(parts, axis=0)

    query = stack(qm_ref, qo_ref)
    grad = stack(dm_ref, do_ref)
    wide = query.shape[0]
    last = row_ref[0:1, :]
    first = row_ref[1:2, :]
    offset = lax.broadcasted_iota(jnp.int32, (RUN, wide), 0).astype(jnp.float32)

    top = jnp.full((1, wide), -1e30, jnp.float32)
    for s in range(count):
        key = pieces[s][0:rows, 0:size]
        value = pieces[s][0:rows, size:]
        score = dot(key, query, ((1,), (1,))) * inv_root
        dp_ref[s * rows : (s + 1) * rows, :] = dot(value, grad, ((1,), (1,)))
        for run in range(rows // RUN):
            meta = pieces[s][rows : rows + META_ROWS, :].astype(jnp.float32)
            start = meta[run : run + 1, 0:1] * float(RUN)
            pos = offset + start
            allowed = (pos <= last) & (pos >= first)
            part = jnp.where(allowed, score[run * RUN : (run + 1) * RUN], -1e30)
            low = s * rows + run * RUN
            s_ref[low : low + RUN, :] = part
            top = jnp.maximum(top, jnp.max(part, axis=0, keepdims=True))

    total = jnp.zeros((1, wide), jnp.float32)
    mixed = jnp.zeros((1, wide), jnp.float32)
    for s in range(count):
        at = slice(s * rows, (s + 1) * rows)
        weight = jnp.exp(s_ref[at, :] - top)
        s_ref[at, :] = weight
        total = total + jnp.sum(weight, axis=0, keepdims=True)
        mixed = mixed + jnp.sum(weight * dp_ref[at, :], axis=0, keepdims=True)
    scale = 1.0 / total
    delta = mixed * scale

    is_key = core_ref[0] == 0
    other = jnp.where(is_key, query, grad)
    dq = jnp.zeros((size, wide), jnp.float32)
    for s in range(count):
        at = slice(s * rows, (s + 1) * rows)
        prob = s_ref[at, :] * scale
        dscore = (prob * (dp_ref[at, :] - delta)).astype(jnp.bfloat16)
        picked = jnp.where(is_key, dscore, prob.astype(jnp.bfloat16))
        back[s][...] = dot(picked, other, ((1,), (0,))).astype(jnp.bfloat16)
        dq = dq + dot(pieces[s][0:rows, 0:size], dscore, ((0,), (0,)))
    dq = dq * inv_root
    for part in range(wide // rows):
        block = dq[:, part * rows : (part + 1) * rows]
        dq_ref[:, part * size : (part + 1) * size] = block.T.astype(jnp.bfloat16)


def attention(core, row_info, q_mine, q_other, d_mine, d_other, pieces):
    count = len(pieces)
    rows, width = q_mine.shape
    size = pieces[0].shape[1] // 2
    wide = 2 * rows * (width // size)
    return pl.pallas_call(
        functools.partial(attention_kernel, count),
        out_shape=[jax.ShapeDtypeStruct((rows, 2 * width), jnp.bfloat16)]
        + [jax.ShapeDtypeStruct((rows, size), jnp.bfloat16)] * count,
        in_specs=[SMEM] + [VMEM] * (5 + count),
        out_specs=[VMEM] * (1 + count),
        scratch_shapes=[pltpu.VMEM((count * rows, wide), jnp.float32)] * 2,
        compiler_params=params(52),
        cost_estimate=pl.CostEstimate(
            flops=10 * count * rows * wide * size,
            bytes_accessed=count * rows * size * 8,
            transcendentals=count * rows * wide,
        ),
        name="attention",
    )(core, row_info, q_mine, q_other, d_mine, d_other, *pieces)


def product_kernel(at_ref, dq_ref, wm_ref, wo_ref, out_ref):
    depth = wm_ref.shape[0]
    acc = dot(dq_ref[:, 0:depth], wm_ref[...], ((1,), (0,)))
    acc = acc + dot(dq_ref[:, depth:], wo_ref[...], ((1,), (0,)))
    out_ref[...] = acc.astype(out_ref.dtype)


def product(block, dq, w_mine, w_other, first, width, tile, dtype):
    rows, depth = dq.shape
    share = w_other.shape[1]
    return pl.pallas_call(
        product_kernel,
        out_shape=jax.ShapeDtypeStruct((rows, width), dtype),
        grid_spec=pltpu.PrefetchScalarGridSpec(
            num_scalar_prefetch=1,
            grid=(width // tile,),
            in_specs=[
                pl.BlockSpec((rows, depth), lambda i, at: (0, 0)),
                pl.BlockSpec(
                    (depth // 2, tile), lambda i, at: (0, at[0] * (share // tile) + first // tile + i)
                ),
                pl.BlockSpec((depth // 2, tile), lambda i, at: (0, first // tile + i)),
            ],
            out_specs=pl.BlockSpec((rows, tile), lambda i, at: (0, i)),
        ),
        compiler_params=params(),
        cost_estimate=pl.CostEstimate(
            flops=2 * rows * depth * width, bytes_accessed=2 * depth * width, transcendentals=0
        ),
        name="product",
    )(block, dq, w_mine, w_other)


def finish_kernel(chunks, core_ref, mine_ref, other_ref, wm_ref, wo_ref, acc_ref, *refs):
    out_ref = refs[chunks]
    inv_root = 1.0 / math.sqrt(mine_ref.shape[1])
    is_key = core_ref[0] == 0
    mine = (mine_ref[...] * jnp.where(is_key, inv_root, 1.0)).astype(jnp.bfloat16)
    other = (other_ref[...] * jnp.where(is_key, 1.0, inv_root)).astype(jnp.bfloat16)
    width = out_ref.shape[1] // chunks
    for c in range(chunks):
        at = slice(c * width, (c + 1) * width)
        acc = acc_ref[:, at] + refs[c][...].astype(jnp.float32)
        acc = acc + dot(mine, wm_ref[:, at], ((1,), (0,))) + dot(other, wo_ref[:, at], ((1,), (0,)))
        out_ref[:, at] = acc.astype(jnp.bfloat16)


def finish(core, mine, other, w_kv, acc, received):
    rows, width = acc.shape
    size = mine.shape[1]
    chunks = len(received)
    return pl.pallas_call(
        functools.partial(finish_kernel, chunks),
        out_shape=jax.ShapeDtypeStruct((rows, width), jnp.bfloat16),
        grid_spec=pltpu.PrefetchScalarGridSpec(
            num_scalar_prefetch=1,
            grid=(1,),
            in_specs=[
                pl.BlockSpec((rows, size), lambda i, at: (0, 0)),
                pl.BlockSpec((rows, size), lambda i, at: (0, 0)),
                pl.BlockSpec((size, width), lambda i, at: (at[0], 0)),
                pl.BlockSpec((size, width), lambda i, at: (1 - at[0], 0)),
                pl.BlockSpec((rows, width), lambda i, at: (0, 0)),
            ]
            + [pl.BlockSpec((rows, width // chunks), lambda i, at: (0, 0))] * chunks,
            out_specs=pl.BlockSpec((rows, width), lambda i, at: (0, 0)),
        ),
        compiler_params=params(),
        cost_estimate=pl.CostEstimate(
            flops=4 * rows * size * width, bytes_accessed=10 * rows * width, transcendentals=0
        ),
        name="finish",
    )(core, mine, other, w_kv, w_kv, acc, *received)


def on_device(queries, keys, values, dout, positions, doc_ids, w_query, w_kv):
    count = lax.axis_size("ctx")
    head = lax.axis_index("head")
    core = (head % 2).astype(jnp.int32).reshape(1)
    share = w_kv.shape[1]
    local_heads = queries.shape[1] // keys.shape[1]

    piece = pack(positions, keys, values)
    pieces = [piece] + [shifted(piece, "ctx", s) for s in range(1, count)]
    q_other = swapped(queries, "head", 1)
    d_other = swapped(dout, "head", 1)

    def columns(block):
        return lax.dynamic_slice_in_dim(w_query, block * share, share, axis=1)

    w_far = swapped(columns(head ^ 3), "head", 1)
    w_near = swapped(columns(head ^ 1), "head", 1)

    bounds = jnp.stack([positions, doc_ids * RUN]).astype(jnp.float32)
    row_info = jnp.tile(bounds, (1, 2 * local_heads))
    dq, *back = attention(core, row_info, queries, q_other, dout, d_other, pieces)

    far = (head ^ 2).astype(jnp.int32).reshape(1)
    near = head.astype(jnp.int32).reshape(1)
    width = share // CHUNKS
    received = []
    for c in range(CHUNKS):
        part = product(far, dq, w_query, w_far, c * width, width, width, jnp.bfloat16)
        received.append(swapped(part, "head", 2))

    mine = back[0].astype(jnp.float32)
    for s in range(1, count):
        mine = mine + shifted(back[s], "ctx", -s).astype(jnp.float32)
    mine = mine.astype(jnp.bfloat16)
    same = swapped(mine, "head", 2).astype(jnp.float32) + mine.astype(jnp.float32)
    other = swapped(mine, "head", 1).astype(jnp.float32) + swapped(mine, "head", 3).astype(jnp.float32)

    acc = product(near, dq, w_query, w_near, 0, share, min(1024, share), jnp.float32)
    return finish(core, same, other, w_kv, acc, received)


def solution(mesh):
    placed = (
        P("ctx", "head"),
        P("ctx", None),
        P("ctx", None),
        P("ctx", "head"),
        P("ctx"),
        P("ctx"),
        P("head", None),
        P(None, "head"),
    )
    return jax.shard_map(
        on_device, mesh=mesh, in_specs=placed, out_specs=P("ctx", "head"), check_vma=False
    )
```

time: 268 us -> 85.7 us (0.32)
  blocking collectives: 107 us -> 0 us
  waiting for transfers between devices: 56.6 us -> 32 us
  local copies, waits for them, and re-layouts: 26.1 us -> 8.16 us
  matrix products: 16.4 us -> 0 us
  between operations: 13.5 us -> 0.16 us
  Pallas kernels: 0 us -> 9.47 us
  starting transfers between devices: 44.4 us -> 35.7 us
    all_gather x5 -> x0, blocking collectives: 107 us -> none  [the longest x1 30.7 us: on_device(): value_piece = lax.all_gather(values, 'ctx', axis=0, tiled=True)]
    ppermute x40 -> x25, waiting for transfers between devices: 52.2 us -> 32 us  [the longest x11 18.9 us: swapped(): lax.ppermute(value, axis, [(source, source ^ bits) for source in range(co...]
    dot_general x44 -> x0, matrix products: 16.4 us -> none  [the longest x1 6.04 us: on_device(): jnp.dot(every_head, width_share, preferred_element_type=jnp.float32)]
    all_to_all x1 -> x0, local copies, waits for them, and re-layouts: 12 us -> none  [on_device(): lax.all_to_all(w_query, 'head', split_axis=1, concat_axis=0, tiled=True)]
    unnamed x18, local copies, waits for them, and re-layouts: 13.9 us -> 3.41 us
    pallas_call x0 -> x8, Pallas kernels: none -> 9.47 us  [the longest x5 4.69 us: product(): pl.pallas_call(product_kernel, out_shape=jax.ShapeDtypeStruct((rows, widt...]
    all_to_all x1 -> x0, starting transfers between devices: 5.79 us -> none  [on_device(): lax.all_to_all(w_query, 'head', split_axis=1, concat_axis=0, tiled=True)]
    dynamic_slice x0 -> x1, local copies, waits for them, and re-layouts: none -> 4.75 us  [columns(): return lax.dynamic_slice_in_dim(w_query, block * share, share, axis=1)]
  transfers between devices with their start and end apart: 42 -> 25, of which waited for: 9 -> 14; matrix products, arithmetic and copies ran while one was open for 11% -> 0% of each run, Pallas kernels for 0% -> 9%
where the time goes in v1:
time: 85.7 us; the launch traced here: 85.5 us
  starting transfers between devices  35.7 us (42%)
  waiting for transfers between devices  32 us (37%)
  Pallas kernels  9.47 us (11%)
  local copies, waits for them, and re-layouts  8.16 us (10%)
    ppermute x14, starting transfers between devices, shifted(): return lax.ppermute(value, axis, pairs)  28.1 us
    ppermute x11, waiting for transfers between devices, swapped(): lax.ppermute(value, axis, [(source, source ^ bits) for source in range(co...  18.9 us
    ppermute x14, waiting for transfers between devices, shifted(): return lax.ppermute(value, axis, pairs)  13.1 us
    ppermute x11, starting transfers between devices, swapped(): lax.ppermute(value, axis, [(source, source ^ bits) for source in range(co...  7.54 us
    dynamic_slice x1, local copies, waits for them, and re-layouts, columns(): return lax.dynamic_slice_in_dim(w_query, block * share, share, axis=1)  4.75 us
    pallas_call x5, Pallas kernels, product(): pl.pallas_call(product_kernel, out_shape=jax.ShapeDtypeStruct((rows, widt...  4.69 us
    unnamed x18, local copies, waits for them, and re-layouts  3.41 us
    pallas_call x1, Pallas kernels, attention(): pl.pallas_call(functools.partial(attention_kernel, count), out_shape=[jax...  2.51 us
  transfers between devices with their start and end apart: 25, of which 14 were waited for; matrix products, arithmetic and copies ran while one was open for 0% of the time, Pallas kernels for 9%

profile of v1, /device:TPU:0, one launch (start us, length us, event | category | flops | bytes accessed | tf_op | source)
XLA Modules:
  0.0 85.5 jit_solution(12928208256235899699)
XLA Ops:
  0.0 4.7 %constant_dynamic-slice_fusion = (bf16[256,4096]{1,0:T(8,128)(2,1)}, bf16[256,4096]{1,0:T(8,128)(2,1)}) fusion(bf16[256,16384]{1,0:T(8,128)(2,1)} %wm_ref.10, s32[]{:T(128)S(6)} %select_n.15, s32[]{:T(128)S(6)} %select_n.14), kind=kLoop, calls=%fused_computation.7 | loop fusion | bytes 8388616 | tf_op jit(solution)/shard_map/dynamic_slice | solution.py:234
  6.4 3.0 %collective-permute-start.2 = (bf16[144,256]{1,0:T(8,128)(2,1)S(1)}, bf16[144,256]{1,0:T(8,128)(2,1)S(1)}, u32[]{:S(2)}, u32[]{:S(2)}) collective-permute-start(bf16[144,256]{1,0:T(8,128)(2,1)S(1)} %pack.1.refs_0_), channel_id=1, source_target_pairs={{0,4},{4,8},{8,12},{12,16},{16,20},{20,24},{24,28},{28,0},{1,5},{5... | collective-permute-start | bytes 221192 | tf_op jit(solution)/shard_map/ppermute | solution.py:25
  9.4 2.5 %collective-permute-done.qo_ref = bf16[128,256]{1,0:T(8,128)(2,1)S(1)} collective-permute-done((bf16[128,256]{1,0:T(8,128)(2,1)S(1)}, bf16[128,256]{1,0:T(8,128)(2,1)S(1)}, u32[]{:S(2)}, u32[]{:S(2)}) %collective-permute-start) | collective-permute-done | bytes 65568 | tf_op jit(solution)/shard_map/ppermute | solution.py:30
  11.9 2.9 %collective-permute-start.3 = (bf16[144,256]{1,0:T(8,128)(2,1)S(1)}, bf16[144,256]{1,0:T(8,128)(2,1)S(1)}, u32[]{:S(2)}, u32[]{:S(2)}) collective-permute-start(bf16[144,256]{1,0:T(8,128)(2,1)S(1)} %pack.1.refs_0_), channel_id=1, source_target_pairs={{0,8},{4,12},{8,16},{12,20},{16,24},{20,28},{24,0},{28,4},{1,9},{5... | collective-permute-start | bytes 221192 | tf_op jit(solution)/shard_map/ppermute | solution.py:25
  14.8 2.5 %collective-permute-start.4 = (bf16[144,256]{1,0:T(8,128)(2,1)S(1)}, bf16[144,256]{1,0:T(8,128)(2,1)S(1)}, u32[]{:S(2)}, u32[]{:S(2)}) collective-permute-start(bf16[144,256]{1,0:T(8,128)(2,1)S(1)} %pack.1.refs_0_), channel_id=1, source_target_pairs={{0,12},{4,16},{8,20},{12,24},{16,28},{20,0},{24,4},{28,8},{1,13},{... | collective-permute-start | bytes 221192 | tf_op jit(solution)/shard_map/ppermute | solution.py:25
  17.3 1.2 %collective-permute-start.5 = (bf16[144,256]{1,0:T(8,128)(2,1)S(1)}, bf16[144,256]{1,0:T(8,128)(2,1)S(1)}, u32[]{:S(2)}, u32[]{:S(2)}) collective-permute-start(bf16[144,256]{1,0:T(8,128)(2,1)S(1)} %pack.1.refs_0_), channel_id=1, source_target_pairs={{0,16},{4,20},{8,24},{12,28},{16,0},{20,4},{24,8},{28,12},{1,17},{... | collective-permute-start | bytes 221192 | tf_op jit(solution)/shard_map/ppermute | solution.py:25
  18.6 0.8 collective-permute-done.3.refs_2_
  19.4 2.2 %collective-permute-start.6 = (bf16[144,256]{1,0:T(8,128)(2,1)S(1)}, bf16[144,256]{1,0:T(8,128)(2,1)S(1)}, u32[]{:S(2)}, u32[]{:S(2)}) collective-permute-start(bf16[144,256]{1,0:T(8,128)(2,1)S(1)} %pack.1.refs_0_), channel_id=1, source_target_pairs={{0,20},{4,24},{8,28},{12,0},{16,4},{20,8},{24,12},{28,16},{1,21},{... | collective-permute-start | bytes 221192 | tf_op jit(solution)/shard_map/ppermute | solution.py:25
  21.6 3.7 %collective-permute-done.4.refs_3_ = bf16[144,256]{1,0:T(8,128)(2,1)S(1)} collective-permute-done((bf16[144,256]{1,0:T(8,128)(2,1)S(1)}, bf16[144,256]{1,0:T(8,128)(2,1)S(1)}, u32[]{:S(2)}, u32[]{:S(2)}) %collective-permute-start.4) | collective-permute-done | bytes 73760 | tf_op jit(solution)/shard_map/ppermute | solution.py:25
  25.3 5.1 %collective-permute-start.7 = (bf16[144,256]{1,0:T(8,128)(2,1)S(1)}, bf16[144,256]{1,0:T(8,128)(2,1)S(1)}, u32[]{:S(2)}, u32[]{:S(2)}) collective-permute-start(bf16[144,256]{1,0:T(8,128)(2,1)S(1)} %pack.1.refs_0_), channel_id=1, source_target_pairs={{0,24},{4,28},{8,0},{12,4},{16,8},{20,12},{24,16},{28,20},{1,25},{... | collective-permute-start | bytes 221192 | tf_op jit(solution)/shard_map/ppermute | solution.py:25
  30.4 1.1 %collective-permute-start.8 = (bf16[144,256]{1,0:T(8,128)(2,1)S(1)}, bf16[144,256]{1,0:T(8,128)(2,1)S(1)}, u32[]{:S(2)}, u32[]{:S(2)}) collective-permute-start(bf16[144,256]{1,0:T(8,128)(2,1)S(1)} %pack.1.refs_0_), channel_id=1, source_target_pairs={{0,28},{4,0},{8,4},{12,8},{16,12},{20,16},{24,20},{28,24},{1,29},{... | collective-permute-start | bytes 221192 | tf_op jit(solution)/shard_map/ppermute | solution.py:25
  31.5 1.3 %collective-permute-done.7.refs_6_ = bf16[144,256]{1,0:T(8,128)(2,1)S(1)} collective-permute-done((bf16[144,256]{1,0:T(8,128)(2,1)S(1)}, bf16[144,256]{1,0:T(8,128)(2,1)S(1)}, u32[]{:S(2)}, u32[]{:S(2)}) %collective-permute-start.7) | collective-permute-done | bytes 73760 | tf_op jit(solution)/shard_map/ppermute | solution.py:25
  32.8 1.9 %collective-permute-done.8.refs_7_ = bf16[144,256]{1,0:T(8,128)(2,1)S(1)} collective-permute-done((bf16[144,256]{1,0:T(8,128)(2,1)S(1)}, bf16[144,256]{1,0:T(8,128)(2,1)S(1)}, u32[]{:S(2)}, u32[]{:S(2)}) %collective-permute-start.8) | collective-permute-done | bytes 73760 | tf_op jit(solution)/shard_map/ppermute | solution.py:25
  34.7 2.5 %attention.1 = (bf16[128,512]{1,0:T(8,128)(2,1)S(1)}, bf16[128,128]{1,0:T(8,128)(2,1)S(1)}, bf16[128,128]{1,0:T(8,128)(2,1)S(1)}, bf16[128,128]{1,0:T(8,128)(2,1...) custom-call(s32[1]{0:T(128)} %bitcast.core_ref, ...), custom_call_target="tpu_custom_call" | custom-call | flops 671088640 | bytes 1048576 | tf_op jit(solution)/shard_map/attention/pallas_call | solution.py:129
  37.4 4.4 %collective-permute-start.13 = (bf16[128,128]{1,0:T(8,128)(2,1)S(1)}, bf16[128,128]{1,0:T(8,128)(2,1)S(1)}, u32[]{:S(2)}, u32[]{:S(2)}) collective-permute-start(bf16[128,128]{1,0:T(8,128)(2,1)S(1)} %get-tuple-element.19), channel_id=1, source_target_pairs={{0,12},{4,16},{8,20},{12,24},{16,28},{20,0},{24,4},{28,8},{1,13},{... | collective-permute-start | bytes 98312 | tf_op jit(solution)/shard_map/ppermute | solution.py:25
  41.7 2.2 %collective-permute-done.15 = bf16[128,128]{1,0:T(8,128)(2,1)S(1)} collective-permute-done((bf16[128,128]{1,0:T(8,128)(2,1)S(1)}, bf16[128,128]{1,0:T(8,128)(2,1)S(1)}, u32[]{:S(2)}, u32[]{:S(2)}) %collective-permute-start.15) | collective-permute-done | bytes 32800 | tf_op jit(solution)/shard_map/ppermute | solution.py:25
  43.9 2.4 %collective-permute-start.11 = (bf16[128,128]{1,0:T(8,128)(2,1)S(1)}, bf16[128,128]{1,0:T(8,128)(2,1)S(1)}, u32[]{:S(2)}, u32[]{:S(2)}) collective-permute-start(bf16[128,128]{1,0:T(8,128)(2,1)S(1)} %get-tuple-element.17), channel_id=1, source_target_pairs={{0,20},{4,24},{8,28},{12,0},{16,4},{20,8},{24,12},{28,16},{1,21},{... | collective-permute-start | bytes 98312 | tf_op jit(solution)/shard_map/ppermute | solution.py:25
  46.4 1.9 %collective-permute-start.10 = (bf16[128,128]{1,0:T(8,128)(2,1)S(1)}, bf16[128,128]{1,0:T(8,128)(2,1)S(1)}, u32[]{:S(2)}, u32[]{:S(2)}) collective-permute-start(bf16[128,128]{1,0:T(8,128)(2,1)S(1)} %get-tuple-element.16), channel_id=1, source_target_pairs={{0,24},{4,28},{8,0},{12,4},{16,8},{20,12},{24,16},{28,20},{1,25},{... | collective-permute-start | bytes 98312 | tf_op jit(solution)/shard_map/ppermute | solution.py:25
  48.8 1.3 %collective-permute-start.9 = (bf16[128,128]{1,0:T(8,128)(2,1)S(1)}, bf16[128,128]{1,0:T(8,128)(2,1)S(1)}, u32[]{:S(2)}, u32[]{:S(2)}) collective-permute-start(bf16[128,128]{1,0:T(8,128)(2,1)S(1)} %get-tuple-element.15), channel_id=1, source_target_pairs={{0,28},{4,0},{8,4},{12,8},{16,12},{20,16},{24,20},{28,24},{1,29},{... | collective-permute-start | bytes 98312 | tf_op jit(solution)/shard_map/ppermute | solution.py:25
  50.3 2.5 %collective-permute-done.9 = bf16[128,128]{1,0:T(8,128)(2,1)S(1)} collective-permute-done((bf16[128,128]{1,0:T(8,128)(2,1)S(1)}, bf16[128,128]{1,0:T(8,128)(2,1)S(1)}, u32[]{:S(2)}, u32[]{:S(2)}) %collective-permute-start.9) | collective-permute-done | bytes 32800 | tf_op jit(solution)/shard_map/ppermute | solution.py:25
  52.8 1.6 %collective-permute-start.16 = (bf16[128,128]{1,0:T(8,128)(2,1)S(1)}, bf16[128,128]{1,0:T(8,128)(2,1)S(1)}, u32[]{:S(2)}, u32[]{:S(2)}) collective-permute-start(bf16[128,128]{1,0:T(8,128)(2,1)S(1)} %add_convert_fusion), channel_id=1, source_target_pairs={{0,2},{1,3},{2,0},{3,1},{4,6},{5,7},{6,4},{7,5},{8,10},{9,11},{10,... | collective-permute-start | bytes 98312 | tf_op jit(solution)/shard_map/ppermute | solution.py:30
  54.4 0.6 collective-permute-start.17
  55.0 1.8 %collective-permute-done.16 = bf16[128,128]{1,0:T(8,128)(2,1)S(1)} collective-permute-done((bf16[128,128]{1,0:T(8,128)(2,1)S(1)}, bf16[128,128]{1,0:T(8,128)(2,1)S(1)}, u32[]{:S(2)}, u32[]{:S(2)}) %collective-permute-start.16) | collective-permute-done | bytes 32800 | tf_op jit(solution)/shard_map/ppermute | solution.py:30
  56.8 3.4 %copy-done = bf16[256,16384]{1,0:T(8,128)(2,1)S(1)} copy-done((bf16[256,16384]{1,0:T(8,128)(2,1)S(1)}, bf16[256,16384]{1,0:T(8,128)(2,1)}, u32[]{:S(2)}) %copy-start) | copy-done | bytes 8388632
  60.5 1.9 %collective-permute-start.21 = (bf16[128,1024]{1,0:T(8,128)(2,1)S(1)}, bf16[128,1024]{1,0:T(8,128)(2,1)S(1)}, u32[]{:S(2)}, u32[]{:S(2)}) collective-permute-start(bf16[128,1024]{1,0:T(8,128)(2,1)S(1)} %product.6), channel_id=1, source_target_pairs={{0,2},{1,3},{2,0},{3,1},{4,6},{5,7},{6,4},{7,5},{8,10},{9,11},{10,... | collective-permute-start | bytes 786440 | tf_op jit(solution)/shard_map/ppermute | solution.py:30
  63.6 1.9 %collective-permute-start.23 = (bf16[128,1024]{1,0:T(8,128)(2,1)S(1)}, bf16[128,1024]{1,0:T(8,128)(2,1)S(1)}, u32[]{:S(2)}, u32[]{:S(2)}) collective-permute-start(bf16[128,1024]{1,0:T(8,128)(2,1)S(1)} %product.8), channel_id=1, source_target_pairs={{0,2},{1,3},{2,0},{3,1},{4,6},{5,7},{6,4},{7,5},{8,10},{9,11},{10,... | collective-permute-start | bytes 786440 | tf_op jit(solution)/shard_map/ppermute | solution.py:30
  65.7 3.5 %product.5.acc_ref = f32[128,4096]{1,0:T(8,128)S(1)} custom-call(s32[1]{0:T(128)} %bitcast.3.at_ref, bf16[128,512]{1,0:T(8,128)(2,1)S(1)} %get-tuple-element.22.dq_ref, bf16[256,16384]{1,0:T(8,128)(2,1)S(1)} %copy-done, bf16[256,4096]{1,0:T(8,128)(2,1)} %collective-permute-done.19.wo_ref), custom_call_target="tpu_custom_call" | custom-call | flops 536870912 | bytes 4194304 | tf_op jit(solution)/shard_map/product/pallas_call | solution.py:156
  69.2 0.6 collective-permute-done.21.refs_0_
  69.8 5.6 %collective-permute-done.22.refs_1_ = bf16[128,1024]{1,0:T(8,128)(2,1)S(1)} collective-permute-done((bf16[128,1024]{1,0:T(8,128)(2,1)S(1)}, bf16[128,1024]{1,0:T(8,128)(2,1)S(1)}, u32[]{:S(2)}, u32[]{:S(2)}) %collective-permute-start.22) | collective-permute-done | bytes 262176 | tf_op jit(solution)/shard_map/ppermute | solution.py:30
  75.4 5.6 %collective-permute-done.23.refs_2_ = bf16[128,1024]{1,0:T(8,128)(2,1)S(1)} collective-permute-done((bf16[128,1024]{1,0:T(8,128)(2,1)S(1)}, bf16[128,1024]{1,0:T(8,128)(2,1)S(1)}, u32[]{:S(2)}, u32[]{:S(2)}) %collective-permute-start.23) | collective-permute-done | bytes 262176 | tf_op jit(solution)/shard_map/ppermute | solution.py:30
  81.0 2.8 %collective-permute-done.24.refs_3_ = bf16[128,1024]{1,0:T(8,128)(2,1)S(1)} collective-permute-done((bf16[128,1024]{1,0:T(8,128)(2,1)S(1)}, bf16[128,1024]{1,0:T(8,128)(2,1)S(1)}, u32[]{:S(2)}, u32[]{:S(2)}) %collective-permute-start.24) | collective-permute-done | bytes 262176 | tf_op jit(solution)/shard_map/ppermute | solution.py:30
  83.8 1.7 %finish.1 = bf16[128,4096]{1,0:T(8,128)(2,1)} custom-call(s32[1]{0:T(128)} %bitcast.core_ref, f32[128,128]{1,0:T(8,128)S(1)} %convert_add_fusion.1.mine_ref, f32[128,128]{1,0:T(8,128)S(1)} %convert_add_fusion.other_ref, bf16[256,4096]{1,0:T(8,128)(2,1)S(1)} %copy-done.1, bf16[256,4096]{1,0:T(8,128)(2,1)S(1)} %copy-done.1, f32[128,4096]{1,0:T(8,128)S(1)} %product.5.acc_ref, ...), custom_call_target="tpu_custom_call" | custom-call | flops 268435456 | bytes 5242880 | tf_op jit(solution)/shard_map/finish/pallas_call | solution.py:197
  (50 shorter events, 4.4 us)
Async XLA Ops:
  0.0 5.3 %copy-start.5 = (bf16[128,256]{1,0:T(8,128)(2,1)S(1)}, bf16[128,256]{1,0:T(8,128)(2,1)}, u32[]{:S(2)}) copy-start(bf16[128,256]{1,0:T(8,128)(2,1)} %qm_ref.1) | copy-start | bytes 196612
  0.0 5.8 %copy-start.6 = (bf16[128,256]{1,0:T(8,128)(2,1)S(1)}, bf16[128,256]{1,0:T(8,128)(2,1)}, u32[]{:S(2)}) copy-start(bf16[128,256]{1,0:T(8,128)(2,1)} %dm_ref.1) | copy-start | bytes 196612
  0.0 5.9 %copy-start.2 = (bf16[128,128]{1,0:T(8,128)(2,1)S(1)}, bf16[128,128]{1,0:T(8,128)(2,1)}, u32[]{:S(2)}) copy-start(bf16[128,128]{1,0:T(8,128)(2,1)} %key_ref.1) | copy-start | bytes 98308
  0.0 5.9 %copy-start.3 = (bf16[128,128]{1,0:T(8,128)(2,1)S(1)}, bf16[128,128]{1,0:T(8,128)(2,1)}, u32[]{:S(2)}) copy-start(bf16[128,128]{1,0:T(8,128)(2,1)} %value_ref.1) | copy-start | bytes 98308
  0.0 5.9 %copy-start.4 = (s32[128]{0:T(128)S(1)}, s32[128]{0:T(128)}, u32[]{:S(2)}) copy-start(s32[128]{0:T(128)} %pos_ref.1) | copy-start | bytes 1540
  0.0 9.4 %copy-start.7 = (s32[128]{0:T(128)S(1)}, s32[128]{0:T(128)}, u32[]{:S(2)}) copy-start(s32[128]{0:T(128)} %param.13) | copy-start | bytes 1540
  4.8 52.0 %collective-permute-start.20 = (bf16[256,4096]{1,0:T(8,128)(2,1)}, bf16[256,4096]{1,0:T(8,128)(2,1)S(1)}, u32[]{:S(2)}, u32[]{:S(2)}) collective-permute-start(bf16[256,4096]{1,0:T(8,128)(2,1)} %get-tuple-element.23), channel_id=1, source_target_pairs={{0,1},{1,0},{2,3},{3,2},{4,5},{5,4},{6,7},{7,6},{8,9},{9,8},{10,11... | collective-permute-start | bytes 6291464 | tf_op jit(solution)/shard_map/ppermute | solution.py:30
  5.3 60.4 %collective-permute-start.19 = (bf16[256,4096]{1,0:T(8,128)(2,1)}, bf16[256,4096]{1,0:T(8,128)(2,1)}, u32[]{:S(2)}, u32[]{:S(2)}) collective-permute-start(bf16[256,4096]{1,0:T(8,128)(2,1)} %get-tuple-element.24), channel_id=1, source_target_pairs={{0,1},{1,0},{2,3},{3,2},{4,5},{5,4},{6,7},{7,6},{8,9},{9,8},{10,11... | collective-permute-start | bytes 6291464 | tf_op jit(solution)/shard_map/ppermute | solution.py:30
  5.3 6.6 %collective-permute-start = (bf16[128,256]{1,0:T(8,128)(2,1)S(1)}, bf16[128,256]{1,0:T(8,128)(2,1)S(1)}, u32[]{:S(2)}, u32[]{:S(2)}) collective-permute-start(bf16[128,256]{1,0:T(8,128)(2,1)S(1)} %copy-done.5), channel_id=1, source_target_pairs={{0,1},{1,0},{2,3},{3,2},{4,5},{5,4},{6,7},{7,6},{8,9},{9,8},{10,11... | collective-permute-start | bytes 196616 | tf_op jit(solution)/shard_map/ppermute | solution.py:30
  5.8 9.0 %collective-permute-start.1 = (bf16[128,256]{1,0:T(8,128)(2,1)S(1)}, bf16[128,256]{1,0:T(8,128)(2,1)S(1)}, u32[]{:S(2)}, u32[]{:S(2)}) collective-permute-start(bf16[128,256]{1,0:T(8,128)(2,1)S(1)} %copy-done.6), channel_id=1, source_target_pairs={{0,1},{1,0},{2,3},{3,2},{4,5},{5,4},{6,7},{7,6},{8,9},{9,8},{10,11... | collective-permute-start | bytes 196616 | tf_op jit(solution)/shard_map/ppermute | solution.py:30
  6.4 10.9 %collective-permute-start.2 = (bf16[144,256]{1,0:T(8,128)(2,1)S(1)}, bf16[144,256]{1,0:T(8,128)(2,1)S(1)}, u32[]{:S(2)}, u32[]{:S(2)}) collective-permute-start(bf16[144,256]{1,0:T(8,128)(2,1)S(1)} %pack.1.refs_0_), channel_id=1, source_target_pairs={{0,4},{4,8},{8,12},{12,16},{16,20},{20,24},{24,28},{28,0},{1,5},{5... | collective-permute-start | bytes 221192 | tf_op jit(solution)/shard_map/ppermute | solution.py:25
  11.9 7.5 %collective-permute-start.3 = (bf16[144,256]{1,0:T(8,128)(2,1)S(1)}, bf16[144,256]{1,0:T(8,128)(2,1)S(1)}, u32[]{:S(2)}, u32[]{:S(2)}) collective-permute-start(bf16[144,256]{1,0:T(8,128)(2,1)S(1)} %pack.1.refs_0_), channel_id=1, source_target_pairs={{0,8},{4,12},{8,16},{12,20},{16,24},{20,28},{24,0},{28,4},{1,9},{5... | collective-permute-start | bytes 221192 | tf_op jit(solution)/shard_map/ppermute | solution.py:25
  14.8 10.4 %collective-permute-start.4 = (bf16[144,256]{1,0:T(8,128)(2,1)S(1)}, bf16[144,256]{1,0:T(8,128)(2,1)S(1)}, u32[]{:S(2)}, u32[]{:S(2)}) collective-permute-start(bf16[144,256]{1,0:T(8,128)(2,1)S(1)} %pack.1.refs_0_), channel_id=1, source_target_pairs={{0,12},{4,16},{8,20},{12,24},{16,28},{20,0},{24,4},{28,8},{1,13},{... | collective-permute-start | bytes 221192 | tf_op jit(solution)/shard_map/ppermute | solution.py:25
  17.3 13.0 %collective-permute-start.5 = (bf16[144,256]{1,0:T(8,128)(2,1)S(1)}, bf16[144,256]{1,0:T(8,128)(2,1)S(1)}, u32[]{:S(2)}, u32[]{:S(2)}) collective-permute-start(bf16[144,256]{1,0:T(8,128)(2,1)S(1)} %pack.1.refs_0_), channel_id=1, source_target_pairs={{0,16},{4,20},{8,24},{12,28},{16,0},{20,4},{24,8},{28,12},{1,17},{... | collective-permute-start | bytes 221192 | tf_op jit(solution)/shard_map/ppermute | solution.py:25
  19.4 12.1 %collective-permute-start.6 = (bf16[144,256]{1,0:T(8,128)(2,1)S(1)}, bf16[144,256]{1,0:T(8,128)(2,1)S(1)}, u32[]{:S(2)}, u32[]{:S(2)}) collective-permute-start(bf16[144,256]{1,0:T(8,128)(2,1)S(1)} %pack.1.refs_0_), channel_id=1, source_target_pairs={{0,20},{4,24},{8,28},{12,0},{16,4},{20,8},{24,12},{28,16},{1,21},{... | collective-permute-start | bytes 221192 | tf_op jit(solution)/shard_map/ppermute | solution.py:25
  25.3 7.6 %collective-permute-start.7 = (bf16[144,256]{1,0:T(8,128)(2,1)S(1)}, bf16[144,256]{1,0:T(8,128)(2,1)S(1)}, u32[]{:S(2)}, u32[]{:S(2)}) collective-permute-start(bf16[144,256]{1,0:T(8,128)(2,1)S(1)} %pack.1.refs_0_), channel_id=1, source_target_pairs={{0,24},{4,28},{8,0},{12,4},{16,8},{20,12},{24,16},{28,20},{1,25},{... | collective-permute-start | bytes 221192 | tf_op jit(solution)/shard_map/ppermute | solution.py:25
  30.4 4.4 %collective-permute-start.8 = (bf16[144,256]{1,0:T(8,128)(2,1)S(1)}, bf16[144,256]{1,0:T(8,128)(2,1)S(1)}, u32[]{:S(2)}, u32[]{:S(2)}) collective-permute-start(bf16[144,256]{1,0:T(8,128)(2,1)S(1)} %pack.1.refs_0_), channel_id=1, source_target_pairs={{0,28},{4,0},{8,4},{12,8},{16,12},{20,16},{24,20},{28,24},{1,29},{... | collective-permute-start | bytes 221192 | tf_op jit(solution)/shard_map/ppermute | solution.py:25
  37.2 6.7 %collective-permute-start.15 = (bf16[128,128]{1,0:T(8,128)(2,1)S(1)}, bf16[128,128]{1,0:T(8,128)(2,1)S(1)}, u32[]{:S(2)}, u32[]{:S(2)}) collective-permute-start(bf16[128,128]{1,0:T(8,128)(2,1)S(1)} %get-tuple-element.21), channel_id=1, source_target_pairs={{0,4},{4,8},{8,12},{12,16},{16,20},{20,24},{24,28},{28,0},{1,5},{5... | collective-permute-start | bytes 98312 | tf_op jit(solution)/shard_map/ppermute | solution.py:25
  37.3 6.6 %collective-permute-start.14 = (bf16[128,128]{1,0:T(8,128)(2,1)S(1)}, bf16[128,128]{1,0:T(8,128)(2,1)S(1)}, u32[]{:S(2)}, u32[]{:S(2)}) collective-permute-start(bf16[128,128]{1,0:T(8,128)(2,1)S(1)} %get-tuple-element.20), channel_id=1, source_target_pairs={{0,8},{4,12},{8,16},{12,20},{16,24},{20,28},{24,0},{28,4},{1,9},{5... | collective-permute-start | bytes 98312 | tf_op jit(solution)/shard_map/ppermute | solution.py:25
  37.4 9.0 %collective-permute-start.13 = (bf16[128,128]{1,0:T(8,128)(2,1)S(1)}, bf16[128,128]{1,0:T(8,128)(2,1)S(1)}, u32[]{:S(2)}, u32[]{:S(2)}) collective-permute-start(bf16[128,128]{1,0:T(8,128)(2,1)S(1)} %get-tuple-element.19), channel_id=1, source_target_pairs={{0,12},{4,16},{8,20},{12,24},{16,28},{20,0},{24,4},{28,8},{1,13},{... | collective-permute-start | bytes 98312 | tf_op jit(solution)/shard_map/ppermute | solution.py:25
  43.9 4.9 %collective-permute-start.12 = (bf16[128,128]{1,0:T(8,128)(2,1)S(1)}, bf16[128,128]{1,0:T(8,128)(2,1)S(1)}, u32[]{:S(2)}, u32[]{:S(2)}) collective-permute-start(bf16[128,128]{1,0:T(8,128)(2,1)S(1)} %get-tuple-element.18), channel_id=1, source_target_pairs={{0,16},{4,20},{8,24},{12,28},{16,0},{20,4},{24,8},{28,12},{1,17},{... | collective-permute-start | bytes 98312 | tf_op jit(solution)/shard_map/ppermute | solution.py:25
  43.9 6.2 %collective-permute-start.11 = (bf16[128,128]{1,0:T(8,128)(2,1)S(1)}, bf16[128,128]{1,0:T(8,128)(2,1)S(1)}, u32[]{:S(2)}, u32[]{:S(2)}) collective-permute-start(bf16[128,128]{1,0:T(8,128)(2,1)S(1)} %get-tuple-element.17), channel_id=1, source_target_pairs={{0,20},{4,24},{8,28},{12,0},{16,4},{20,8},{24,12},{28,16},{1,21},{... | collective-permute-start | bytes 98312 | tf_op jit(solution)/shard_map/ppermute | solution.py:25
  46.4 3.9 %collective-permute-start.10 = (bf16[128,128]{1,0:T(8,128)(2,1)S(1)}, bf16[128,128]{1,0:T(8,128)(2,1)S(1)}, u32[]{:S(2)}, u32[]{:S(2)}) collective-permute-start(bf16[128,128]{1,0:T(8,128)(2,1)S(1)} %get-tuple-element.16), channel_id=1, source_target_pairs={{0,24},{4,28},{8,0},{12,4},{16,8},{20,12},{24,16},{28,20},{1,25},{... | collective-permute-start | bytes 98312 | tf_op jit(solution)/shard_map/ppermute | solution.py:25
  48.8 3.9 %collective-permute-start.9 = (bf16[128,128]{1,0:T(8,128)(2,1)S(1)}, bf16[128,128]{1,0:T(8,128)(2,1)S(1)}, u32[]{:S(2)}, u32[]{:S(2)}) collective-permute-start(bf16[128,128]{1,0:T(8,128)(2,1)S(1)} %get-tuple-element.15), channel_id=1, source_target_pairs={{0,28},{4,0},{8,4},{12,8},{16,12},{20,16},{24,20},{28,24},{1,29},{... | collective-permute-start | bytes 98312 | tf_op jit(solution)/shard_map/ppermute | solution.py:25
  52.8 4.0 %collective-permute-start.16 = (bf16[128,128]{1,0:T(8,128)(2,1)S(1)}, bf16[128,128]{1,0:T(8,128)(2,1)S(1)}, u32[]{:S(2)}, u32[]{:S(2)}) collective-permute-start(bf16[128,128]{1,0:T(8,128)(2,1)S(1)} %add_convert_fusion), channel_id=1, source_target_pairs={{0,2},{1,3},{2,0},{3,1},{4,6},{5,7},{6,4},{7,5},{8,10},{9,11},{10,... | collective-permute-start | bytes 98312 | tf_op jit(solution)/shard_map/ppermute | solution.py:30
  54.4 9.2 %collective-permute-start.18 = (bf16[128,128]{1,0:T(8,128)(2,1)S(1)}, bf16[128,128]{1,0:T(8,128)(2,1)S(1)}, u32[]{:S(2)}, u32[]{:S(2)}) collective-permute-start(bf16[128,128]{1,0:T(8,128)(2,1)S(1)} %add_convert_fusion), channel_id=1, source_target_pairs={{0,3},{1,2},{2,1},{3,0},{4,7},{5,6},{6,5},{7,4},{8,11},{9,10},{10,... | collective-permute-start | bytes 98312 | tf_op jit(solution)/shard_map/ppermute | solution.py:30
  54.4 11.1 %collective-permute-start.17 = (bf16[128,128]{1,0:T(8,128)(2,1)S(1)}, bf16[128,128]{1,0:T(8,128)(2,1)S(1)}, u32[]{:S(2)}, u32[]{:S(2)}) collective-permute-start(bf16[128,128]{1,0:T(8,128)(2,1)S(1)} %add_convert_fusion), channel_id=1, source_target_pairs={{0,1},{1,0},{2,3},{3,2},{4,5},{5,4},{6,7},{7,6},{8,9},{9,8},{10,11... | collective-permute-start | bytes 98312 | tf_op jit(solution)/shard_map/ppermute | solution.py:30
  60.5 9.3 %collective-permute-start.21 = (bf16[128,1024]{1,0:T(8,128)(2,1)S(1)}, bf16[128,1024]{1,0:T(8,128)(2,1)S(1)}, u32[]{:S(2)}, u32[]{:S(2)}) collective-permute-start(bf16[128,1024]{1,0:T(8,128)(2,1)S(1)} %product.6), channel_id=1, source_target_pairs={{0,2},{1,3},{2,0},{3,1},{4,6},{5,7},{6,4},{7,5},{8,10},{9,11},{10,... | collective-permute-start | bytes 786440 | tf_op jit(solution)/shard_map/ppermute | solution.py:30
  62.7 12.7 %collective-permute-start.22 = (bf16[128,1024]{1,0:T(8,128)(2,1)S(1)}, bf16[128,1024]{1,0:T(8,128)(2,1)S(1)}, u32[]{:S(2)}, u32[]{:S(2)}) collective-permute-start(bf16[128,1024]{1,0:T(8,128)(2,1)S(1)} %product.7), channel_id=1, source_target_pairs={{0,2},{1,3},{2,0},{3,1},{4,6},{5,7},{6,4},{7,5},{8,10},{9,11},{10,... | collective-permute-start | bytes 786440 | tf_op jit(solution)/shard_map/ppermute | solution.py:30
  63.6 17.4 %collective-permute-start.23 = (bf16[128,1024]{1,0:T(8,128)(2,1)S(1)}, bf16[128,1024]{1,0:T(8,128)(2,1)S(1)}, u32[]{:S(2)}, u32[]{:S(2)}) collective-permute-start(bf16[128,1024]{1,0:T(8,128)(2,1)S(1)} %product.8), channel_id=1, source_target_pairs={{0,2},{1,3},{2,0},{3,1},{4,6},{5,7},{6,4},{7,5},{8,10},{9,11},{10,... | collective-permute-start | bytes 786440 | tf_op jit(solution)/shard_map/ppermute | solution.py:30
  65.5 18.4 %collective-permute-start.24 = (bf16[128,1024]{1,0:T(8,128)(2,1)S(1)}, bf16[128,1024]{1,0:T(8,128)(2,1)S(1)}, u32[]{:S(2)}, u32[]{:S(2)}) collective-permute-start(bf16[128,1024]{1,0:T(8,128)(2,1)S(1)} %product.9), channel_id=1, source_target_pairs={{0,2},{1,3},{2,0},{3,1},{4,6},{5,7},{6,4},{7,5},{8,10},{9,11},{10,... | collective-permute-start | bytes 786440 | tf_op jit(solution)/shard_map/ppermute | solution.py:30
  65.7 18.1 %copy-start.1 = (bf16[256,4096]{1,0:T(8,128)(2,1)S(1)}, bf16[256,4096]{1,0:T(8,128)(2,1)}, u32[]{:S(2)}) copy-start(bf16[256,4096]{1,0:T(8,128)(2,1)} %wo_ref.1) | copy-start | bytes 6291460
  (1 other events, 3.4 us)

commit v2 on v1

v2 whole, which is shorter than its diff:
```python
import functools
import math

import jax
import jax.numpy as jnp
from jax import lax
from jax.experimental import pallas as pl
from jax.experimental.pallas import tpu as pltpu
from jax.sharding import PartitionSpec as P

RUN = 64
META_ROWS = 16
CHUNKS = 4
VMEM = pl.BlockSpec(memory_space=pltpu.VMEM)
SMEM = pl.BlockSpec(memory_space=pltpu.SMEM)


def params(limit_mib=32):
    return pltpu.CompilerParams(vmem_limit_bytes=limit_mib * 1024 * 1024)


def swapped(value, axis, bits):
    count = lax.axis_size(axis)
    return lax.ppermute(value, axis, [(source, source ^ bits) for source in range(count)])


def dot(a, b, contract):
    return lax.dot_general(a, b, (contract, ((), ())), preferred_element_type=jnp.float32)


def each(count, body, state):
    if count > 8:
        return lax.fori_loop(0, count, body, state)
    for step in range(count):
        state = body(step, state)
    return state


def pack_kernel(pos_ref, key_ref, value_ref, query_ref, grad_ref, piece_ref, both_ref):
    count = piece_ref.shape[0]
    rows, head_size = key_ref.shape
    row = lax.broadcasted_iota(jnp.int32, (META_ROWS, 2 * head_size), 0)
    meta = jnp.zeros((META_ROWS, 2 * head_size), jnp.int32)
    for run in range(rows // RUN):
        meta = jnp.where(row == run, pos_ref[run * RUN] // RUN, meta)
    meta = meta.astype(jnp.float32).astype(jnp.bfloat16)

    def copy(c, state):
        piece_ref[c, 0:rows, 0:head_size] = key_ref[...]
        piece_ref[c, 0:rows, head_size:] = value_ref[...]
        piece_ref[c, rows:, :] = meta
        return state

    each(count, copy, 0)
    both_ref[0] = query_ref[...]
    both_ref[1] = grad_ref[...]


def pack(count, positions, keys, values, queries, dout):
    rows, head_size = keys.shape
    return pl.pallas_call(
        pack_kernel,
        out_shape=[
            jax.ShapeDtypeStruct((count, rows + META_ROWS, 2 * head_size), jnp.bfloat16),
            jax.ShapeDtypeStruct((2,) + queries.shape, jnp.bfloat16),
        ],
        in_specs=[SMEM] + [VMEM] * 4,
        out_specs=[VMEM] * 2,
        compiler_params=params(),
        name="pack",
    )(positions, keys, values, queries, dout)


def attention_kernel(core_ref, row_ref, mine_ref, swap_ref, piece_ref, dq_ref, back_ref, s_ref, dp_ref):
    count = piece_ref.shape[0]
    rows = mine_ref.shape[1]
    size = piece_ref.shape[2] // 2
    heads = mine_ref.shape[2] // size
    inv_root = 1.0 / math.sqrt(size)

    def stack(which):
        parts = [
            ref[which, :, h * size : (h + 1) * size] for ref in (mine_ref, swap_ref) for h in range(heads)
        ]
        return jnp.concatenate(parts, axis=0)

    query = stack(0)
    grad = stack(1)
    wide = query.shape[0]
    last = row_ref[0:1, :]
    first = row_ref[1:2, :]
    offset = lax.broadcasted_iota(jnp.int32, (RUN, wide), 0).astype(jnp.float32)

    def scores(s, top):
        key = piece_ref[s, 0:rows, 0:size]
        value = piece_ref[s, 0:rows, size:]
        score = dot(key, query, ((1,), (1,))) * inv_root
        dp_ref[s] = dot(value, grad, ((1,), (1,)))
        meta = piece_ref[s, rows : rows + META_ROWS, :].astype(jnp.float32)
        for run in range(rows // RUN):
            start = meta[run : run + 1, 0:1] * float(RUN)
            pos = offset + start
            allowed = (pos <= last) & (pos >= first)
            part = jnp.where(allowed, score[run * RUN : (run + 1) * RUN], -1e30)
            s_ref[s, run * RUN : (run + 1) * RUN, :] = part
            top = jnp.maximum(top, jnp.max(part, axis=0, keepdims=True))
        return top

    top = each(count, scores, jnp.full((1, wide), -1e30, jnp.float32))

    def weights(s, state):
        total, mixed = state
        weight = jnp.exp(s_ref[s] - top)
        s_ref[s] = weight
        total = total + jnp.sum(weight, axis=0, keepdims=True)
        mixed = mixed + jnp.sum(weight * dp_ref[s], axis=0, keepdims=True)
        return total, mixed

    zeros = jnp.zeros((1, wide), jnp.float32)
    total, mixed = each(count, weights, (zeros, zeros))
    scale = 1.0 / total
    delta = mixed * scale

    is_key = core_ref[0] == 0
    other = jnp.where(is_key, query, grad)

    def gradients(s, dq):
        prob = s_ref[s] * scale
        dscore = (prob * (dp_ref[s] - delta)).astype(jnp.bfloat16)
        picked = jnp.where(is_key, dscore, prob.astype(jnp.bfloat16))
        back_ref[s] = dot(picked, other, ((1,), (0,))).astype(jnp.bfloat16)
        return dq + dot(piece_ref[s, 0:rows, 0:size], dscore, ((0,), (0,)))

    dq = each(count, gradients, jnp.zeros((size, wide), jnp.float32)) * inv_root
    for part in range(wide // rows):
        block = dq[:, part * rows : (part + 1) * rows]
        dq_ref[:, part * size : (part + 1) * size] = block.T.astype(jnp.bfloat16)


def attention(core, row_info, mine, swap, pieces):
    count, _, pair = pieces.shape
    _, rows, width = mine.shape
    size = pair // 2
    wide = 2 * rows * (width // size)
    return pl.pallas_call(
        attention_kernel,
        out_shape=[
            jax.ShapeDtypeStruct((rows, 2 * width), jnp.bfloat16),
            jax.ShapeDtypeStruct((count, rows, size), jnp.bfloat16),
        ],
        in_specs=[SMEM] + [VMEM] * 4,
        out_specs=[VMEM] * 2,
        scratch_shapes=[pltpu.VMEM((count, rows, wide), jnp.float32)] * 2,
        compiler_params=params(44),
        cost_estimate=pl.CostEstimate(
            flops=10 * count * rows * wide * size,
            bytes_accessed=count * rows * size * 8,
            transcendentals=count * rows * wide,
        ),
        name="attention",
    )(core, row_info, mine, swap, pieces)


def product_kernel(at_ref, dq_ref, wm_ref, wo_ref, out_ref):
    depth = wm_ref.shape[0]
    acc = dot(dq_ref[:, 0:depth], wm_ref[...], ((1,), (0,)))
    acc = acc + dot(dq_ref[:, depth:], wo_ref[...], ((1,), (0,)))
    out_ref[...] = acc.astype(out_ref.dtype)


def product(block, dq, w_mine, w_other, which, first, width, tile, dtype):
    rows, depth = dq.shape
    share = w_other.shape[2]
    return pl.pallas_call(
        product_kernel,
        out_shape=jax.ShapeDtypeStruct((rows, width), dtype),
        grid_spec=pltpu.PrefetchScalarGridSpec(
            num_scalar_prefetch=1,
            grid=(width // tile,),
            in_specs=[
                pl.BlockSpec((rows, depth), lambda i, at: (0, 0)),
                pl.BlockSpec(
                    (depth // 2, tile), lambda i, at: (0, at[0] * (share // tile) + first // tile + i)
                ),
                pl.BlockSpec((None, depth // 2, tile), lambda i, at: (which, 0, first // tile + i)),
            ],
            out_specs=pl.BlockSpec((rows, tile), lambda i, at: (0, i)),
        ),
        compiler_params=params(52),
        cost_estimate=pl.CostEstimate(
            flops=2 * rows * depth * width, bytes_accessed=2 * depth * width, transcendentals=0
        ),
        name="product",
    )(block, dq, w_mine, w_other)


def finish_kernel(chunks, core_ref, mine_ref, other_ref, wm_ref, wo_ref, acc_ref, *refs):
    out_ref = refs[chunks]
    inv_root = 1.0 / math.sqrt(mine_ref.shape[1])
    is_key = core_ref[0] == 0
    mine = (mine_ref[...] * jnp.where(is_key, inv_root, 1.0)).astype(jnp.bfloat16)
    other = (other_ref[...] * jnp.where(is_key, 1.0, inv_root)).astype(jnp.bfloat16)
    width = out_ref.shape[1] // chunks
    for c in range(chunks):
        at = slice(c * width, (c + 1) * width)
        acc = acc_ref[:, at] + refs[c][...].astype(jnp.float32)
        acc = acc + dot(mine, wm_ref[:, at], ((1,), (0,))) + dot(other, wo_ref[:, at], ((1,), (0,)))
        out_ref[:, at] = acc.astype(jnp.bfloat16)


def finish(core, mine, other, w_kv, acc, received):
    rows, width = acc.shape
    size = mine.shape[1]
    chunks = len(received)
    return pl.pallas_call(
        functools.partial(finish_kernel, chunks),
        out_shape=jax.ShapeDtypeStruct((rows, width), jnp.bfloat16),
        grid_spec=pltpu.PrefetchScalarGridSpec(
            num_scalar_prefetch=1,
            grid=(1,),
            in_specs=[
                pl.BlockSpec((rows, size), lambda i, at: (0, 0)),
                pl.BlockSpec((rows, size), lambda i, at: (0, 0)),
                pl.BlockSpec((size, width), lambda i, at: (at[0], 0)),
                pl.BlockSpec((size, width), lambda i, at: (1 - at[0], 0)),
                pl.BlockSpec((rows, width), lambda i, at: (0, 0)),
            ]
            + [pl.BlockSpec((rows, width // chunks), lambda i, at: (0, 0))] * chunks,
            out_specs=pl.BlockSpec((rows, width), lambda i, at: (0, 0)),
        ),
        compiler_params=params(),
        cost_estimate=pl.CostEstimate(
            flops=4 * rows * size * width, bytes_accessed=10 * rows * width, transcendentals=0
        ),
        name="finish",
    )(core, mine, other, w_kv, w_kv, acc, *received)


def on_device(queries, keys, values, dout, positions, doc_ids, w_query, w_kv):
    count = lax.axis_size("ctx")
    head = lax.axis_index("head")
    core = (head % 2).astype(jnp.int32).reshape(1)
    share = w_kv.shape[1]
    local_heads = queries.shape[1] // keys.shape[1]

    piece, both = pack(count, positions, keys, values, queries, dout)
    pieces = lax.all_to_all(piece, "ctx", 0, 0)
    swap = swapped(both, "head", 1)

    w_late, _ = lax.optimization_barrier((w_query, both))

    def columns(block):
        return lax.dynamic_slice_in_dim(w_late, block * share, share, axis=1)

    w_other = swapped(jnp.stack([columns(head ^ 3), columns(head ^ 1)]), "head", 1)

    bounds = jnp.stack([positions, doc_ids * RUN]).astype(jnp.float32)
    row_info = jnp.tile(bounds, (1, 2 * local_heads))
    dq, back = attention(core, row_info, both, swap, pieces)

    far = (head ^ 2).astype(jnp.int32).reshape(1)
    near = head.astype(jnp.int32).reshape(1)
    width = share // CHUNKS
    parts = [
        product(far, dq, w_query, w_other, 0, c * width, width, width, jnp.bfloat16) for c in range(CHUNKS)
    ]
    parts, back = lax.optimization_barrier((parts, back))
    received = [swapped(part, "head", 2) for part in parts]

    back = lax.all_to_all(back, "ctx", 0, 0)
    mine = jnp.sum(back.astype(jnp.float32), axis=0).astype(jnp.bfloat16)
    same = swapped(mine, "head", 2).astype(jnp.float32) + mine.astype(jnp.float32)
    other = swapped(mine, "head", 1).astype(jnp.float32) + swapped(mine, "head", 3).astype(jnp.float32)

    acc = product(near, dq, w_query, w_other, 1, 0, share, min(1024, share), jnp.float32)
    return finish(core, same, other, w_kv, acc, received)


def solution(mesh):
    placed = (
        P("ctx", "head"),
        P("ctx", None),
        P("ctx", None),
        P("ctx", "head"),
        P("ctx"),
        P("ctx"),
        P("head", None),
        P(None, "head"),
    )
    return jax.shard_map(
        on_device, mesh=mesh, in_specs=placed, out_specs=P("ctx", "head"), check_vma=False
    )
```

time: 85.7 us -> 79.1 us (0.923)
  starting transfers between devices: 35.7 us -> 17.9 us
  Pallas kernels: 9.47 us -> 17.1 us
  other arithmetic: 0.07 us -> 2.44 us
    ppermute x14 -> x0, starting transfers between devices: 28.1 us -> none  [shifted(): return lax.ppermute(value, axis, pairs)]
    all_to_all x0 -> x2, waiting for transfers between devices: none -> 20.8 us  [the longest x1 15.2 us: on_device(): pieces = lax.all_to_all(piece, 'ctx', 0, 0)]
    ppermute x14 -> x0, waiting for transfers between devices: 13.1 us -> none  [shifted(): return lax.ppermute(value, axis, pairs)]
    all_to_all x0 -> x2, starting transfers between devices: none -> 10.4 us  [the longest x1 6.8 us: on_device(): pieces = lax.all_to_all(piece, 'ctx', 0, 0)]
    ppermute x11 -> x9, waiting for transfers between devices: 18.9 us -> 12 us  [swapped(): lax.ppermute(value, axis, [(source, source ^ bits) for source in range(co...]
    pallas_call x5, Pallas kernels: 4.69 us -> 11 us  [product(): pl.pallas_call(product_kernel, out_shape=jax.ShapeDtypeStruct((rows, widt...]
    dynamic_slice x1 -> x0, local copies, waits for them, and re-layouts: 4.75 us -> none  [columns(): return lax.dynamic_slice_in_dim(w_query, block * share, share, axis=1)]
    another operation x0 -> x1, local copies, waits for them, and re-layouts: none -> 2.49 us  [on_device(): jnp.stack([columns(head ^ 3), columns(head ^ 1)])]
  transfers between devices with their start and end apart: 25 -> 11, of which waited for: 14 -> 7; matrix products, arithmetic and copies ran while one was open for 0% -> 0% of each run, Pallas kernels for 9% -> 10%
where the time goes in v2:
time: 79.1 us; the launch traced here: 78.3 us
  waiting for transfers between devices  32.8 us (41%)
  starting transfers between devices  17.9 us (23%)
  Pallas kernels  17.1 us (22%)
  local copies, waits for them, and re-layouts  7.96 us (10%)
  other arithmetic  2.44 us (3%)
    all_to_all x1, waiting for transfers between devices, on_device(): pieces = lax.all_to_all(piece, 'ctx', 0, 0)  15.2 us
    ppermute x9, waiting for transfers between devices, swapped(): lax.ppermute(value, axis, [(source, source ^ bits) for source in range(co...  12 us
    pallas_call x5, Pallas kernels, product(): pl.pallas_call(product_kernel, out_shape=jax.ShapeDtypeStruct((rows, widt...  11 us
    ppermute x9, starting transfers between devices, swapped(): lax.ppermute(value, axis, [(source, source ^ bits) for source in range(co...  7.48 us
    all_to_all x1, starting transfers between devices, on_device(): pieces = lax.all_to_all(piece, 'ctx', 0, 0)  6.8 us
    all_to_all x1, waiting for transfers between devices, on_device(): back = lax.all_to_all(back, 'ctx', 0, 0)  5.59 us
    unnamed x20, local copies, waits for them, and re-layouts  5.46 us
    all_to_all x1, starting transfers between devices, on_device(): back = lax.all_to_all(back, 'ctx', 0, 0)  3.64 us
  transfers between devices with their start and end apart: 11, of which 7 were waited for; matrix products, arithmetic and copies ran while one was open for 0% of the time, Pallas kernels for 10%

profile of v2, /device:TPU:0, one launch (start us, length us, event | category | flops | bytes accessed | tf_op | source)
XLA Modules:
  0.0 78.3 jit_solution(10085786977255430786)
XLA Ops:
  0.0 0.8 %copy-done.2 = bf16[128,256]{1,0:T(8,128)(2,1)S(1)} copy-done((bf16[128,256]{1,0:T(8,128)(2,1)S(1)}, bf16[128,256]{1,0:T(8,128)(2,1)}, u32[]{:S(2)}) %copy-start.2) | copy-done | bytes 65560
  0.8 0.8 %copy-done.3 = bf16[128,256]{1,0:T(8,128)(2,1)S(1)} copy-done((bf16[128,256]{1,0:T(8,128)(2,1)S(1)}, bf16[128,256]{1,0:T(8,128)(2,1)}, u32[]{:S(2)}) %copy-start.3) | copy-done | bytes 65560
  1.7 0.8 copy-done.4
  2.4 0.8 copy-done.5
  3.2 0.7 copy-done.6
  3.9 1.4 %pack.1 = (bf16[8,144,256]{2,1,0:T(8,128)(2,1)}, bf16[2,128,256]{2,1,0:T(8,128)(2,1)S(1)}) custom-call(s32[128]{0:T(128)S(1)} %copy-done.6, bf16[128,128]{1,0:T(8,128)(2,1)S(1)} %copy-done.4, bf16[128,128]{1,0:T(8,128)(2,1)S(1)} %copy-done.5, bf16[128,256]{1,0:T(8,128)(2,1)S(1)} %copy-done.2, bf16[128,256]{1,0:T(8,128)(2,1)S(1)} %copy-done.3), custom_call_target="tpu_custom_call" | custom-call | tf_op jit(solution)/shard_map/pack/pallas_call | solution.py:61
  5.3 2.5 %dynamic-slice_bitcast_fusion.1 = (bf16[1,256,4096]{2,1,0:T(8,128)(2,1)S(1)}, bf16[1,256,4096]{2,1,0:T(8,128)(2,1)S(1)}) fusion(bf16[256,16384]{1,0:T(8,128)(2,1)} %wm_ref.10, s32[]{:T(128)S(6)} %select_n.14, s32[]{:T(128)S(6)} %select_n.15), kind=kLoop, calls=%fused_computation.2 | loop fusion | bytes 8388616 | tf_op jit(solution)/shard_map/stack | solution.py:255
  7.8 2.4 %pad_maximum_fusion = bf16[2,256,4096]{2,1,0:T(8,128)(2,1)} fusion(bf16[1,256,4096]{2,1,0:T(8,128)(2,1)S(1)} %get-tuple-element.26, bf16[1,256,4096]{2,1,0:T(8,128)(2,1)S(1)} %get-tuple-element.25), kind=kLoop, calls=%fused_computation | loop fusion | flops 2097152 | bytes 8388608 | tf_op jit(solution)/shard_map/stack | solution.py:255
  10.2 0.5 collective-permute-start.1
  10.6 6.8 %all-to-all-start = ((bf16[8,144,256]{2,1,0:T(8,128)(2,1)}), bf16[8,144,256]{2,1,0:T(8,128)(2,1)S(1)}, u32[]{:S(2)}, u32[]{:S(2)}) async-start(bf16[8,144,256]{2,1,0:T(8,128)(2,1)} %get-tuple-element.16), calls=%async_computation | async-start | bytes 1179648 | tf_op jit(solution)/shard_map/all_to_all | solution.py:247
  17.7 1.1 %collective-permute-done.swap_ref = bf16[2,128,256]{2,1,0:T(8,128)(2,1)S(1)} collective-permute-done((bf16[2,128,256]{2,1,0:T(8,128)(2,1)S(1)}, bf16[2,128,256]{2,1,0:T(8,128)(2,1)S(1)}, u32[]{:S(2)}, u32[]{:S(2)}) %collective-permute-start) | collective-permute-done | bytes 131104 | tf_op jit(solution)/shard_map/ppermute | solution.py:24
  18.8 15.2 %all-to-all-done.piece_ref = bf16[8,144,256]{2,1,0:T(8,128)(2,1)S(1)} async-done(((bf16[8,144,256]{2,1,0:T(8,128)(2,1)}), bf16[8,144,256]{2,1,0:T(8,128)(2,1)S(1)}, u32[]{:S(2)}, u32[]{:S(2)}) %all-to-all-start) | async-done | bytes 589856 | tf_op jit(solution)/shard_map/all_to_all | solution.py:247
  34.0 3.1 %attention.1 = (bf16[128,512]{1,0:T(8,128)(2,1)S(1)}, bf16[8,128,128]{2,1,0:T(8,128)(2,1)}) custom-call(s32[1]{0:T(128)} %bitcast.core_ref, f32[2,512]{1,0:T(2,128)S(1)} %bitcast.15, bf16[2,128,256]{2,1,0:T(8,128)(2,1)S(1)} %get-tuple-element.15.mine_ref, bf16[2,128,256]{2,1,0:T(8,128)(2,1)S(1)} %collective-permute-done.swap_ref, ...), custom_call_target="tpu_custom_call" | custom-call | flops 671088640 | bytes 1048576 | tf_op jit(solution)/shard_map/attention/pallas_call | solution.py:145
  37.1 1.5 %product.8 = bf16[128,1024]{1,0:T(8,128)(2,1)S(1)} custom-call(s32[1]{0:T(128)} %bitcast.1.at_ref, bf16[128,512]{1,0:T(8,128)(2,1)S(1)} %get-tuple-element.17.dq_ref, bf16[256,16384]{1,0:T(8,128)(2,1)} %wm_ref.10, bf16[2,256,4096]{2,1,0:T(8,128)(2,1)} %collective-permute-done.1.wo_ref), custom_call_target="tpu_custom_call" | custom-call | flops 134217728 | bytes 1048576 | tf_op jit(solution)/shard_map/product/pallas_call | solution.py:174
  38.6 1.5 %product.7 = bf16[128,1024]{1,0:T(8,128)(2,1)S(1)} custom-call(s32[1]{0:T(128)} %bitcast.1.at_ref, bf16[128,512]{1,0:T(8,128)(2,1)S(1)} %get-tuple-element.17.dq_ref, bf16[256,16384]{1,0:T(8,128)(2,1)} %wm_ref.10, bf16[2,256,4096]{2,1,0:T(8,128)(2,1)} %collective-permute-done.1.wo_ref), custom_call_target="tpu_custom_call" | custom-call | flops 134217728 | bytes 1048576 | tf_op jit(solution)/shard_map/product/pallas_call | solution.py:174
  40.1 1.5 %product.6 = bf16[128,1024]{1,0:T(8,128)(2,1)S(1)} custom-call(s32[1]{0:T(128)} %bitcast.1.at_ref, bf16[128,512]{1,0:T(8,128)(2,1)S(1)} %get-tuple-element.17.dq_ref, bf16[256,16384]{1,0:T(8,128)(2,1)} %wm_ref.10, bf16[2,256,4096]{2,1,0:T(8,128)(2,1)} %collective-permute-done.1.wo_ref), custom_call_target="tpu_custom_call" | custom-call | flops 134217728 | bytes 1048576 | tf_op jit(solution)/shard_map/product/pallas_call | solution.py:174
  41.6 1.5 %product.5 = bf16[128,1024]{1,0:T(8,128)(2,1)S(1)} custom-call(s32[1]{0:T(128)} %bitcast.1.at_ref, bf16[128,512]{1,0:T(8,128)(2,1)S(1)} %get-tuple-element.17.dq_ref, bf16[256,16384]{1,0:T(8,128)(2,1)} %wm_ref.10, bf16[2,256,4096]{2,1,0:T(8,128)(2,1)} %collective-permute-done.1.wo_ref), custom_call_target="tpu_custom_call" | custom-call | flops 134217728 | bytes 1048576 | tf_op jit(solution)/shard_map/product/pallas_call | solution.py:174
  43.1 3.6 %all-to-all-start.1 = ((bf16[8,128,128]{2,1,0:T(8,128)(2,1)}), bf16[8,128,128]{2,1,0:T(8,128)(2,1)S(1)}, u32[]{:S(2)}, u32[]{:S(2)}) async-start(bf16[8,128,128]{2,1,0:T(8,128)(2,1)} %get-tuple-element.20), calls=%async_computation.1 | async-start | bytes 524288 | tf_op jit(solution)/shard_map/all_to_all | solution.py:270
  46.8 1.5 %collective-permute-start.5 = (bf16[128,1024]{1,0:T(8,128)(2,1)S(1)}, bf16[128,1024]{1,0:T(8,128)(2,1)S(1)}, u32[]{:S(2)}, u32[]{:S(2)}) collective-permute-start(bf16[128,1024]{1,0:T(8,128)(2,1)S(1)} %product.5), channel_id=1, source_target_pairs={{0,2},{1,3},{2,0},{3,1},{4,6},{5,7},{6,4},{7,5},{8,10},{9,11},{10,... | collective-permute-start | bytes 786440 | tf_op jit(solution)/shard_map/ppermute | solution.py:24
  48.3 0.5 collective-permute-start.6
  48.8 1.5 %collective-permute-start.7 = (bf16[128,1024]{1,0:T(8,128)(2,1)S(1)}, bf16[128,1024]{1,0:T(8,128)(2,1)S(1)}, u32[]{:S(2)}, u32[]{:S(2)}) collective-permute-start(bf16[128,1024]{1,0:T(8,128)(2,1)S(1)} %product.7), channel_id=1, source_target_pairs={{0,2},{1,3},{2,0},{3,1},{4,6},{5,7},{6,4},{7,5},{8,10},{9,11},{10,... | collective-permute-start | bytes 786440 | tf_op jit(solution)/shard_map/ppermute | solution.py:24
  50.3 5.6 %all-to-all-done.1 = bf16[8,128,128]{2,1,0:T(8,128)(2,1)S(1)} async-done(((bf16[8,128,128]{2,1,0:T(8,128)(2,1)}), bf16[8,128,128]{2,1,0:T(8,128)(2,1)S(1)}, u32[]{:S(2)}, u32[]{:S(2)}) %all-to-all-start.1) | async-done | bytes 262176 | tf_op jit(solution)/shard_map/all_to_all | solution.py:270
  56.0 1.6 %collective-permute-start.2 = (bf16[128,128]{1,0:T(8,128)(2,1)S(1)}, bf16[128,128]{1,0:T(8,128)(2,1)S(1)}, u32[]{:S(2)}, u32[]{:S(2)}) collective-permute-start(bf16[128,128]{1,0:T(8,128)(2,1)S(1)} %reduce_sum.12), channel_id=1, source_target_pairs={{0,2},{1,3},{2,0},{3,1},{4,6},{5,7},{6,4},{7,5},{8,10},{9,11},{10,... | collective-permute-start | bytes 98312 | tf_op jit(solution)/shard_map/ppermute | solution.py:24
  57.6 4.9 %product.9.acc_ref = f32[128,4096]{1,0:T(8,128)} custom-call(s32[1]{0:T(128)} %bitcast.6.at_ref, bf16[128,512]{1,0:T(8,128)(2,1)S(1)} %get-tuple-element.17.dq_ref, bf16[256,16384]{1,0:T(8,128)(2,1)} %wm_ref.10, bf16[2,256,4096]{2,1,0:T(8,128)(2,1)} %collective-permute-done.1.wo_ref), custom_call_target="tpu_custom_call" | custom-call | flops 536870912 | bytes 4194304 | tf_op jit(solution)/shard_map/product/pallas_call | solution.py:174
  62.5 3.6 %collective-permute-done.4 = bf16[128,128]{1,0:T(8,128)(2,1)S(1)} collective-permute-done((bf16[128,128]{1,0:T(8,128)(2,1)S(1)}, bf16[128,128]{1,0:T(8,128)(2,1)S(1)}, u32[]{:S(2)}, u32[]{:S(2)}) %collective-permute-start.4) | collective-permute-done | bytes 32800 | tf_op jit(solution)/shard_map/ppermute | solution.py:24
  66.1 0.9 %collective-permute-start.8 = (bf16[128,1024]{1,0:T(8,128)(2,1)S(1)}, bf16[128,1024]{1,0:T(8,128)(2,1)S(1)}, u32[]{:S(2)}, u32[]{:S(2)}) collective-permute-start(bf16[128,1024]{1,0:T(8,128)(2,1)S(1)} %product.8), channel_id=1, source_target_pairs={{0,2},{1,3},{2,0},{3,1},{4,6},{5,7},{6,4},{7,5},{8,10},{9,11},{10,... | collective-permute-start | bytes 786440 | tf_op jit(solution)/shard_map/ppermute | solution.py:24
  67.0 0.4 collective-permute-done.2
  67.4 0.7 collective-permute-start.3
  68.1 0.8 %collective-permute-done.3 = bf16[128,128]{1,0:T(8,128)(2,1)S(1)} collective-permute-done((bf16[128,128]{1,0:T(8,128)(2,1)S(1)}, bf16[128,128]{1,0:T(8,128)(2,1)S(1)}, u32[]{:S(2)}, u32[]{:S(2)}) %collective-permute-start.3) | collective-permute-done | bytes 32800 | tf_op jit(solution)/shard_map/ppermute | solution.py:24
  69.0 6.1 %collective-permute-done.8.refs_3_ = bf16[128,1024]{1,0:T(8,128)(2,1)S(1)} collective-permute-done((bf16[128,1024]{1,0:T(8,128)(2,1)S(1)}, bf16[128,1024]{1,0:T(8,128)(2,1)S(1)}, u32[]{:S(2)}, u32[]{:S(2)}) %collective-permute-start.8) | collective-permute-done | bytes 262176 | tf_op jit(solution)/shard_map/ppermute | solution.py:24
  75.1 1.6 %copy-done.1 = f32[128,4096]{1,0:T(8,128)S(1)} copy-done((f32[128,4096]{1,0:T(8,128)S(1)}, f32[128,4096]{1,0:T(8,128)}, u32[]{:S(2)}) %copy-start.1) | copy-done | bytes 2097176
  76.7 1.7 %finish.1 = bf16[128,4096]{1,0:T(8,128)(2,1)} custom-call(s32[1]{0:T(128)} %bitcast.core_ref, f32[128,128]{1,0:T(8,128)S(1)} %convert_add_fusion.1.mine_ref, f32[128,128]{1,0:T(8,128)S(1)} %convert_add_fusion.other_ref, bf16[256,4096]{1,0:T(8,128)(2,1)S(1)} %copy-done, bf16[256,4096]{1,0:T(8,128)(2,1)S(1)} %copy-done, f32[128,4096]{1,0:T(8,128)S(1)} %copy-done.1, ...), custom_call_target="tpu_custom_call" | custom-call | flops 268435456 | bytes 5242880 | tf_op jit(solution)/shard_map/finish/pallas_call | solution.py:215
  (25 shorter events, 0.4 us)
Async XLA Ops:
  0.0 0.8 %copy-start.2 = (bf16[128,256]{1,0:T(8,128)(2,1)S(1)}, bf16[128,256]{1,0:T(8,128)(2,1)}, u32[]{:S(2)}) copy-start(bf16[128,256]{1,0:T(8,128)(2,1)} %query_ref.1) | copy-start | bytes 196612
  0.8 0.8 %copy-start.3 = (bf16[128,256]{1,0:T(8,128)(2,1)S(1)}, bf16[128,256]{1,0:T(8,128)(2,1)}, u32[]{:S(2)}) copy-start(bf16[128,256]{1,0:T(8,128)(2,1)} %grad_ref.1) | copy-start | bytes 196612
  1.7 0.8 copy-start.4
  2.4 0.8 copy-start.5
  3.2 0.7 copy-start.6
  7.8 9.9 %copy-start.8 = (s32[128]{0:T(128)S(1)}, s32[128]{0:T(128)}, u32[]{:S(2)}) copy-start(s32[128]{0:T(128)} %param.13) | copy-start | bytes 1540
  7.8 9.9 %copy-start.7 = (s32[128]{0:T(128)S(1)}, s32[128]{0:T(128)}, u32[]{:S(2)}) copy-start(s32[128]{0:T(128)} %pos_ref.1) | copy-start | bytes 1540
  10.2 26.9 %collective-permute-start.1 = (bf16[2,256,4096]{2,1,0:T(8,128)(2,1)}, bf16[2,256,4096]{2,1,0:T(8,128)(2,1)}, u32[]{:S(2)}, u32[]{:S(2)}) collective-permute-start(bf16[2,256,4096]{2,1,0:T(8,128)(2,1)} %pad_maximum_fusion), channel_id=1, source_target_pairs={{0,1},{1,0},{2,3},{3,2},{4,5},{5,4},{6,7},{7,6},{8,9},{9,8},{10,11... | collective-permute-start | bytes 12582920 | tf_op jit(solution)/shard_map/ppermute | solution.py:24
  10.6 23.4 %all-to-all-start = ((bf16[8,144,256]{2,1,0:T(8,128)(2,1)}), bf16[8,144,256]{2,1,0:T(8,128)(2,1)S(1)}, u32[]{:S(2)}, u32[]{:S(2)}) async-start(bf16[8,144,256]{2,1,0:T(8,128)(2,1)} %get-tuple-element.16), calls=%async_computation | async-start | bytes 1179648 | tf_op jit(solution)/shard_map/all_to_all | solution.py:247
  17.4 1.3 %collective-permute-start = (bf16[2,128,256]{2,1,0:T(8,128)(2,1)S(1)}, bf16[2,128,256]{2,1,0:T(8,128)(2,1)S(1)}, u32[]{:S(2)}, u32[]{:S(2)}) collective-permute-start(bf16[2,128,256]{2,1,0:T(8,128)(2,1)S(1)} %get-tuple-element.15.mine_ref), channel_id=1, source_target_pairs={{0,1},{1,0},{2,3},{3,2},{4,5},{5,4},{6,7},{7,6},{8,9},{9,8},{10,11... | collective-permute-start | bytes 393224 | tf_op jit(solution)/shard_map/ppermute | solution.py:24
  43.1 12.8 %all-to-all-start.1 = ((bf16[8,128,128]{2,1,0:T(8,128)(2,1)}), bf16[8,128,128]{2,1,0:T(8,128)(2,1)S(1)}, u32[]{:S(2)}, u32[]{:S(2)}) async-start(bf16[8,128,128]{2,1,0:T(8,128)(2,1)} %get-tuple-element.20), calls=%async_computation.1 | async-start | bytes 524288 | tf_op jit(solution)/shard_map/all_to_all | solution.py:270
  46.8 22.2 %collective-permute-start.5 = (bf16[128,1024]{1,0:T(8,128)(2,1)S(1)}, bf16[128,1024]{1,0:T(8,128)(2,1)S(1)}, u32[]{:S(2)}, u32[]{:S(2)}) collective-permute-start(bf16[128,1024]{1,0:T(8,128)(2,1)S(1)} %product.5), channel_id=1, source_target_pairs={{0,2},{1,3},{2,0},{3,1},{4,6},{5,7},{6,4},{7,5},{8,10},{9,11},{10,... | collective-permute-start | bytes 786440 | tf_op jit(solution)/shard_map/ppermute | solution.py:24
  48.3 20.7 %collective-permute-start.6 = (bf16[128,1024]{1,0:T(8,128)(2,1)S(1)}, bf16[128,1024]{1,0:T(8,128)(2,1)S(1)}, u32[]{:S(2)}, u32[]{:S(2)}) collective-permute-start(bf16[128,1024]{1,0:T(8,128)(2,1)S(1)} %product.6), channel_id=1, source_target_pairs={{0,2},{1,3},{2,0},{3,1},{4,6},{5,7},{6,4},{7,5},{8,10},{9,11},{10,... | collective-permute-start | bytes 786440 | tf_op jit(solution)/shard_map/ppermute | solution.py:24
  48.8 20.2 %collective-permute-start.7 = (bf16[128,1024]{1,0:T(8,128)(2,1)S(1)}, bf16[128,1024]{1,0:T(8,128)(2,1)S(1)}, u32[]{:S(2)}, u32[]{:S(2)}) collective-permute-start(bf16[128,1024]{1,0:T(8,128)(2,1)S(1)} %product.7), channel_id=1, source_target_pairs={{0,2},{1,3},{2,0},{3,1},{4,6},{5,7},{6,4},{7,5},{8,10},{9,11},{10,... | collective-permute-start | bytes 786440 | tf_op jit(solution)/shard_map/ppermute | solution.py:24
  56.0 10.1 %collective-permute-start.4 = (bf16[128,128]{1,0:T(8,128)(2,1)S(1)}, bf16[128,128]{1,0:T(8,128)(2,1)S(1)}, u32[]{:S(2)}, u32[]{:S(2)}) collective-permute-start(bf16[128,128]{1,0:T(8,128)(2,1)S(1)} %reduce_sum.12), channel_id=1, source_target_pairs={{0,3},{1,2},{2,1},{3,0},{4,7},{5,6},{6,5},{7,4},{8,11},{9,10},{10,... | collective-permute-start | bytes 98312 | tf_op jit(solution)/shard_map/ppermute | solution.py:24
  56.0 11.4 %collective-permute-start.2 = (bf16[128,128]{1,0:T(8,128)(2,1)S(1)}, bf16[128,128]{1,0:T(8,128)(2,1)S(1)}, u32[]{:S(2)}, u32[]{:S(2)}) collective-permute-start(bf16[128,128]{1,0:T(8,128)(2,1)S(1)} %reduce_sum.12), channel_id=1, source_target_pairs={{0,2},{1,3},{2,0},{3,1},{4,6},{5,7},{6,4},{7,5},{8,10},{9,11},{10,... | collective-permute-start | bytes 98312 | tf_op jit(solution)/shard_map/ppermute | solution.py:24
  57.6 17.5 %copy-start = (bf16[256,4096]{1,0:T(8,128)(2,1)S(1)}, bf16[256,4096]{1,0:T(8,128)(2,1)}, u32[]{:S(2)}) copy-start(bf16[256,4096]{1,0:T(8,128)(2,1)} %wo_ref.1) | copy-start | bytes 6291460
  66.1 9.0 %collective-permute-start.8 = (bf16[128,1024]{1,0:T(8,128)(2,1)S(1)}, bf16[128,1024]{1,0:T(8,128)(2,1)S(1)}, u32[]{:S(2)}, u32[]{:S(2)}) collective-permute-start(bf16[128,1024]{1,0:T(8,128)(2,1)S(1)} %product.8), channel_id=1, source_target_pairs={{0,2},{1,3},{2,0},{3,1},{4,6},{5,7},{6,4},{7,5},{8,10},{9,11},{10,... | collective-permute-start | bytes 786440 | tf_op jit(solution)/shard_map/ppermute | solution.py:24
  67.4 1.6 %collective-permute-start.3 = (bf16[128,128]{1,0:T(8,128)(2,1)S(1)}, bf16[128,128]{1,0:T(8,128)(2,1)S(1)}, u32[]{:S(2)}, u32[]{:S(2)}) collective-permute-start(bf16[128,128]{1,0:T(8,128)(2,1)S(1)} %reduce_sum.12), channel_id=1, source_target_pairs={{0,1},{1,0},{2,3},{3,2},{4,5},{5,4},{6,7},{7,6},{8,9},{9,8},{10,11... | collective-permute-start | bytes 98312 | tf_op jit(solution)/shard_map/ppermute | solution.py:24
  75.1 1.6 %copy-start.1 = (f32[128,4096]{1,0:T(8,128)S(1)}, f32[128,4096]{1,0:T(8,128)}, u32[]{:S(2)}) copy-start(f32[128,4096]{1,0:T(8,128)} %product.9.acc_ref) | copy-start | bytes 6291460

commit v3 on v2

v3 whole, which is shorter than its diff:
```python
import functools
import math

import jax
import jax.numpy as jnp
from jax import lax
from jax.experimental import pallas as pl
from jax.experimental.pallas import tpu as pltpu
from jax.sharding import PartitionSpec as P

RUN = 64
META_ROWS = 16
CHUNKS = (2, 4, 5, 5)
ANY = pl.BlockSpec(memory_space=pl.ANY)
HBM = pl.BlockSpec(memory_space=pltpu.HBM)
SMEM = pl.BlockSpec(memory_space=pltpu.SMEM)


def params(limit_mib=32):
    return pltpu.CompilerParams(vmem_limit_bytes=limit_mib * 1024 * 1024)


def swapped(value, axis, bits):
    count = lax.axis_size(axis)
    return lax.ppermute(value, axis, [(source, source ^ bits) for source in range(count)])


def dot(a, b, contract):
    return lax.dot_general(a, b, (contract, ((), ())), preferred_element_type=jnp.float32)


def each(count, body, state):
    if count > 8:
        return lax.fori_loop(0, count, body, state)
    for step in range(count):
        state = body(step, state)
    return state


def pack(count, core, positions, keys, values):
    rows, size = keys.shape
    held = jnp.where(core == 0, keys, values)
    runs = (positions.reshape(rows // RUN, RUN)[:, :1] // RUN).astype(jnp.bfloat16)
    meta = jnp.pad(jnp.broadcast_to(runs, (rows // RUN, size)), ((0, META_ROWS - rows // RUN), (0, 0)))
    piece = jnp.concatenate([held, meta], axis=0)
    return jnp.broadcast_to(piece, (count,) + piece.shape)


def carve_kernel(block_ref, w_ref, after_ref, *refs):
    outs, sems = refs[:-1], refs[-1]
    share = outs[0].shape[1]
    copies = []
    for i, out_ref in enumerate(outs):
        at = pl.multiple_of(block_ref[i] * share, share)
        copies.append(pltpu.make_async_copy(w_ref.at[:, pl.ds(at, share)], out_ref, sems.at[i]))
        copies[i].start()
    for one in copies:
        one.wait()


def carve(blocks, w_query, after, share):
    shape = jax.ShapeDtypeStruct((w_query.shape[0], share), w_query.dtype)
    count = len(blocks)
    return pl.pallas_call(
        carve_kernel,
        out_shape=[shape] * count,
        in_specs=[SMEM, HBM, ANY],
        out_specs=[ANY] * count,
        scratch_shapes=[pltpu.SemaphoreType.DMA((count,))],
        compiler_params=params(48),
        cost_estimate=pl.CostEstimate(
            flops=0, bytes_accessed=4 * count * w_query.shape[0] * share, transcendentals=0
        ),
        name="carve",
    )(jnp.stack(blocks), w_query, after)


def attention_kernel(
    core_ref, row_ref, qm_ref, qo_ref, gm_ref, go_ref, here_ref, there_ref, dq_ref, back_ref, s_ref, dp_ref
):
    count = here_ref.shape[0]
    rows, width = qm_ref.shape
    size = here_ref.shape[2]
    is_key = core_ref[0] == 0
    heads = width // size
    inv_root = 1.0 / math.sqrt(size)

    def stack(mine_ref, other_ref):
        parts = [ref[:, h * size : (h + 1) * size] for ref in (mine_ref, other_ref) for h in range(heads)]
        return jnp.concatenate(parts, axis=0)

    query = stack(qm_ref, qo_ref)
    grad = stack(gm_ref, go_ref)
    wide = query.shape[0]
    last = row_ref[0:1, :]
    first = row_ref[1:2, :]
    offset = lax.broadcasted_iota(jnp.int32, (RUN, wide), 0).astype(jnp.float32)

    def scores(s, top):
        here = here_ref[s, 0:rows, :]
        there = there_ref[s, 0:rows, :]
        key = jnp.where(is_key, here, there)
        value = jnp.where(is_key, there, here)
        score = dot(key, query, ((1,), (1,))) * inv_root
        dp_ref[s] = dot(value, grad, ((1,), (1,)))
        meta = here_ref[s, rows : rows + META_ROWS, :].astype(jnp.float32)
        for run in range(rows // RUN):
            start = meta[run : run + 1, 0:1] * float(RUN)
            pos = offset + start
            allowed = (pos <= last) & (pos >= first)
            part = jnp.where(allowed, score[run * RUN : (run + 1) * RUN], -1e30)
            s_ref[s, run * RUN : (run + 1) * RUN, :] = part
            top = jnp.maximum(top, jnp.max(part, axis=0, keepdims=True))
        return top

    top = each(count, scores, jnp.full((1, wide), -1e30, jnp.float32))

    def weights(s, state):
        total, mixed = state
        weight = jnp.exp(s_ref[s] - top)
        s_ref[s] = weight
        total = total + jnp.sum(weight, axis=0, keepdims=True)
        mixed = mixed + jnp.sum(weight * dp_ref[s], axis=0, keepdims=True)
        return total, mixed

    zeros = jnp.zeros((1, wide), jnp.float32)
    total, mixed = each(count, weights, (zeros, zeros))
    scale = 1.0 / total
    delta = mixed * scale

    other = jnp.where(is_key, query, grad)

    def gradients(s, dq):
        prob = s_ref[s] * scale
        dscore = (prob * (dp_ref[s] - delta)).astype(jnp.bfloat16)
        picked = jnp.where(is_key, dscore, prob.astype(jnp.bfloat16))
        back_ref[s] = dot(picked, other, ((1,), (0,))).astype(jnp.bfloat16)
        key = jnp.where(is_key, here_ref[s, 0:rows, :], there_ref[s, 0:rows, :])
        return dq + dot(key, dscore, ((0,), (0,)))

    dq = each(count, gradients, jnp.zeros((size, wide), jnp.float32)) * inv_root
    for part in range(wide // rows):
        block = dq[:, part * rows : (part + 1) * rows]
        dq_ref[:, part * size : (part + 1) * size] = block.T.astype(jnp.bfloat16)


def attention(core, row_info, q_mine, q_other, g_mine, g_other, here, there):
    count, _, size = here.shape
    rows, width = q_mine.shape
    wide = 2 * rows * (width // size)
    return pl.pallas_call(
        attention_kernel,
        out_shape=[
            jax.ShapeDtypeStruct((rows, 2 * width), jnp.bfloat16),
            jax.ShapeDtypeStruct((count, rows, size), jnp.bfloat16),
        ],
        in_specs=[SMEM] + [pl.BlockSpec()] * 7,
        out_specs=[pl.BlockSpec()] * 2,
        scratch_shapes=[pltpu.VMEM((count, rows, wide), jnp.float32)] * 2,
        compiler_params=params(44),
        cost_estimate=pl.CostEstimate(
            flops=10 * count * rows * wide * size,
            bytes_accessed=count * rows * size * 8,
            transcendentals=count * rows * wide,
        ),
        name="attention",
    )(core, row_info, q_mine, q_other, g_mine, g_other, here, there)


def product_kernel(first, dq_ref, wm_ref, wo_ref, out_ref):
    depth = wm_ref.shape[0]
    at = slice(first, first + out_ref.shape[1])
    acc = dot(dq_ref[:, 0:depth], wm_ref[:, at], ((1,), (0,)))
    acc = acc + dot(dq_ref[:, depth:], wo_ref[:, at], ((1,), (0,)))
    out_ref[...] = acc.astype(out_ref.dtype)


def product(dq, w_mine, w_other, first, width, dtype):
    rows, depth = dq.shape
    return pl.pallas_call(
        functools.partial(product_kernel, first),
        out_shape=jax.ShapeDtypeStruct((rows, width), dtype),
        in_specs=[pl.BlockSpec()] * 3,
        out_specs=pl.BlockSpec(),
        compiler_params=params(16),
        cost_estimate=pl.CostEstimate(
            flops=2 * rows * depth * width, bytes_accessed=2 * depth * width, transcendentals=0
        ),
        name="product",
    )(dq, w_mine, w_other)


def finish_kernel(starts, core_ref, mine_ref, other_ref, w_ref, acc_ref, *refs):
    early = len(starts) - 2
    out_ref, left_ref = refs[early:]
    inv_root = 1.0 / math.sqrt(mine_ref.shape[1])
    size = mine_ref.shape[1]
    is_key = core_ref[0] == 0
    wm_ref = w_ref.at[pl.ds(pl.multiple_of(core_ref[0] * size, size), size), :]
    wo_ref = w_ref.at[pl.ds(pl.multiple_of((1 - core_ref[0]) * size, size), size), :]
    mine = (mine_ref[...] * jnp.where(is_key, inv_root, 1.0)).astype(jnp.bfloat16)
    other = (other_ref[...] * jnp.where(is_key, 1.0, inv_root)).astype(jnp.bfloat16)
    for c in range(early + 1):
        at = slice(starts[c], starts[c + 1])
        acc = acc_ref[:, at] + dot(mine, wm_ref[:, at], ((1,), (0,))) + dot(other, wo_ref[:, at], ((1,), (0,)))
        if c < early:
            out_ref[:, at] = (acc + refs[c][...].astype(jnp.float32)).astype(jnp.bfloat16)
        else:
            left_ref[...] = acc


def finish(core, mine, other, w_kv, acc, received, starts):
    rows, share = acc.shape
    size = mine.shape[1]
    last = starts[-2]
    return pl.pallas_call(
        functools.partial(finish_kernel, starts),
        out_shape=[
            jax.ShapeDtypeStruct((rows, share), jnp.bfloat16),
            jax.ShapeDtypeStruct((rows, share - last), jnp.float32),
        ],
        grid=(1,),
        in_specs=[SMEM] + [pl.BlockSpec()] * (4 + len(received)),
        out_specs=[
            pl.BlockSpec((rows, last), lambda i: (0, 0)),
            pl.BlockSpec((rows, share - last), lambda i: (0, 0)),
        ],
        compiler_params=params(),
        cost_estimate=pl.CostEstimate(
            flops=4 * rows * size * share, bytes_accessed=10 * rows * share, transcendentals=0
        ),
        name="finish",
    )(core, mine, other, w_kv, acc, *received)


def last_kernel(left_ref, part_ref, held_ref, out_ref, sum_ref, sem):
    sum_ref[...] = (left_ref[...] + part_ref[...].astype(jnp.float32)).astype(jnp.bfloat16)
    first = out_ref.shape[1] - sum_ref.shape[1]
    copy = pltpu.make_async_copy(sum_ref, out_ref.at[:, first:], sem)
    copy.start()
    copy.wait()


def last(left, part, held):
    return pl.pallas_call(
        last_kernel,
        out_shape=jax.ShapeDtypeStruct(held.shape, held.dtype),
        in_specs=[pl.BlockSpec(), pl.BlockSpec(), ANY],
        out_specs=ANY,
        input_output_aliases={2: 0},
        scratch_shapes=[pltpu.VMEM(part.shape, held.dtype), pltpu.SemaphoreType.DMA(())],
        compiler_params=params(),
        name="last",
    )(left, part, held)


def on_device(queries, keys, values, dout, positions, doc_ids, w_query, w_kv):
    count = lax.axis_size("ctx")
    head = lax.axis_index("head").astype(jnp.int32)
    core = (head & 1).reshape(1)
    share = w_kv.shape[1]

    here = lax.all_to_all(pack(count, core, positions, keys, values), "ctx", 0, 0)
    there = swapped(here, "head", 1)
    q_other = swapped(queries, "head", 1)
    g_other = swapped(dout, "head", 1)

    send = carve([head ^ 3, head ^ 1], w_query, positions, share)
    far_other, near_other = [swapped(part, "head", 1) for part in send]
    far_mine, near_mine = carve([head ^ 2, head], w_query, q_other, share)

    bounds = jnp.stack([positions, doc_ids * RUN]).astype(jnp.float32)
    row_info = jnp.tile(bounds, (1, 2 * (queries.shape[1] // keys.shape[1])))
    dq, back = attention(core, row_info, queries, q_other, dout, g_other, here, there)

    starts = [0]
    for units in CHUNKS:
        starts.append(starts[-1] + units * (share // sum(CHUNKS)))
    received = []
    for low, high in zip(starts, starts[1:]):
        part = product(dq, far_mine, far_other, low, high - low, jnp.bfloat16)
        received.append(swapped(part, "head", 2))

    received[0], back = lax.optimization_barrier((received[0], back))
    back = lax.all_to_all(back, "ctx", 0, 0)
    mine = jnp.sum(back.astype(jnp.float32), axis=0).astype(jnp.bfloat16)
    mine = mine.astype(jnp.float32) + swapped(mine, "head", 2).astype(jnp.float32)
    other = swapped(mine.astype(jnp.bfloat16), "head", 1).astype(jnp.float32)

    acc = product(dq, near_mine, near_other, 0, share, jnp.float32)
    held, left = finish(core, mine, other, w_kv, acc, received[:-1], starts)
    return last(left, received[-1], held)


def solution(mesh):
    placed = (
        P("ctx", "head"),
        P("ctx", None),
        P("ctx", None),
        P("ctx", "head"),
        P("ctx"),
        P("ctx"),
        P("head", None),
        P(None, "head"),
    )
    return jax.shard_map(
        on_device, mesh=mesh, in_specs=placed, out_specs=P("ctx", "head"), check_vma=False
    )
```

time: 79.1 us -> 192 us (2.43)
  Pallas kernels: 17.1 us -> 140 us
  waiting for transfers between devices: 32.8 us -> 26.9 us
  local copies, waits for them, and re-layouts: 7.96 us -> 4.72 us
  other arithmetic: 2.44 us -> 0.45 us
    pallas_call x7 -> x9, Pallas kernels: 14.1 us -> 137 us  [the longest x2 132 us: carve(): pl.pallas_call(carve_kernel, out_shape=[shape] * count, in_specs=[SMEM, H...]
    all_to_all x1, waiting for transfers between devices: 15.2 us -> 9.21 us  [on_device(): lax.all_to_all(pack(count, core, positions, keys, values), 'ctx', 0, 0)]
    another operation x1 -> x0, local copies, waits for them, and re-layouts: 2.49 us -> none  [on_device(): jnp.stack([columns(head ^ 3), columns(head ^ 1)])]
    another operation x1 -> x2, other arithmetic: 2.37 us -> 0.15 us  [carve(): jnp.stack(blocks)]
    unnamed x20 -> x28, local copies, waits for them, and re-layouts: 5.46 us -> 3.89 us
    ppermute x9 -> x11, starting transfers between devices: 7.48 us -> 8.15 us  [swapped(): lax.ppermute(value, axis, [(source, source ^ bits) for source in range(co...]
    ppermute x9 -> x11, waiting for transfers between devices: 12 us -> 12.4 us  [swapped(): lax.ppermute(value, axis, [(source, source ^ bits) for source in range(co...]
  transfers between devices with their start and end apart: 11 -> 13, of which waited for: 7 -> 4; matrix products, arithmetic and copies ran while one was open for 0% -> 1% of each run, Pallas kernels for 10% -> 6%
where the time goes in v3:
time: 192 us
  Pallas kernels  140 us (73%)
  waiting for transfers between devices  26.9 us (14%)
  starting transfers between devices  19 us (10%)
  local copies, waits for them, and re-layouts  4.72 us (2%)
    pallas_call x2, Pallas kernels, carve(): pl.pallas_call(carve_kernel, out_shape=[shape] * count, in_specs=[SMEM, H...  132 us
    ppermute x11, waiting for transfers between devices, swapped(): lax.ppermute(value, axis, [(source, source ^ bits) for source in range(co...  12.4 us
    all_to_all x1, waiting for transfers between devices, on_device(): lax.all_to_all(pack(count, core, positions, keys, values), 'ctx', 0, 0)  9.21 us
    ppermute x11, starting transfers between devices, swapped(): lax.ppermute(value, axis, [(source, source ^ bits) for source in range(co...  8.15 us
    all_to_all x1, starting transfers between devices, on_device(): lax.all_to_all(pack(count, core, positions, keys, values), 'ctx', 0, 0)  7.23 us
    all_to_all x1, waiting for transfers between devices, on_device(): back = lax.all_to_all(back, 'ctx', 0, 0)  5.28 us
    unnamed x28, local copies, waits for them, and re-layouts  3.89 us
  transfers between devices with their start and end apart: 13, of which 4 were waited for; matrix products, arithmetic and copies ran while one was open for 1% of the time, Pallas kernels for 6%

profile of v3, /device:TPU:0, one launch (start us, length us, event | category | flops | bytes accessed | tf_op | source)
XLA Modules:
  0.0 191.8 jit_solution(2295990166499554932)
XLA Ops:
  0.1 0.7 copy-done.6
  0.8 128.7 %carve.3 = (bf16[256,4096]{1,0:T(8,128)(2,1)}, bf16[256,4096]{1,0:T(8,128)(2,1)}) custom-call(s32[2]{0:T(128)S(1)} %pad_add_fusion.1.block_ref, bf16[256,16384]{1,0:T(8,128)(2,1)} %w_ref.4, s32[128]{0:T(128)S(1)} %copy-done.6), custom_call_target="tpu_custom_call" | custom-call | bytes 8388608 | tf_op jit(solution)/shard_map/carve/pallas_call | solution.py:64
  129.5 0.5 collective-permute-start.3
  130.0 0.1 collective-permute-start.7
  130.1 0.1 reshape.28
  130.2 0.1 fusion.1
  130.3 0.1 pad_maximum_fusion
  130.4 0.8 broadcast_in_dim.18
  131.2 7.2 %all-to-all-start = ((bf16[8,144,128]{2,1,0:T(8,128)(2,1)}), bf16[8,144,128]{2,1,0:T(8,128)(2,1)S(1)}, u32[]{:S(2)}, u32[]{:S(2)}) async-start(bf16[8,144,128]{2,1,0:T(8,128)(2,1)} %broadcast_in_dim.18), calls=%async_computation | async-start | bytes 589824 | tf_op jit(solution)/shard_map/all_to_all | solution.py:263
  138.5 0.5 collective-permute-start.1
  139.0 9.2 %all-to-all-done.here_ref = bf16[8,144,128]{2,1,0:T(8,128)(2,1)S(1)} async-done(((bf16[8,144,128]{2,1,0:T(8,128)(2,1)}), bf16[8,144,128]{2,1,0:T(8,128)(2,1)S(1)}, u32[]{:S(2)}, u32[]{:S(2)}) %all-to-all-start) | async-done | bytes 294944 | tf_op jit(solution)/shard_map/all_to_all | solution.py:263
  148.2 0.1 pad_add_fusion.block_ref
  148.3 2.8 %carve.2 = (bf16[256,4096]{1,0:T(8,128)(2,1)S(1)}, bf16[256,4096]{1,0:T(8,128)(2,1)S(1)}) custom-call(s32[2]{0:T(128)S(1)} %pad_add_fusion.block_ref, bf16[256,16384]{1,0:T(8,128)(2,1)} %w_ref.4, bf16[128,256]{1,0:T(8,128)(2,1)S(1)} %collective-permute-done.qo_ref.after_ref), custom_call_target="tpu_custom_call" | custom-call | bytes 8388608 | tf_op jit(solution)/shard_map/carve/pallas_call | solution.py:64
  151.2 3.1 %attention.1 = (bf16[128,512]{1,0:T(8,128)(2,1)S(1)}, bf16[8,128,128]{2,1,0:T(8,128)(2,1)}) custom-call(s32[1]{0:T(128)} %bitcast.core_ref, f32[2,512]{1,0:T(2,128)S(1)} %bitcast.14, bf16[128,256]{1,0:T(8,128)(2,1)S(1)} %copy-done.8, bf16[128,256]{1,0:T(8,128)(2,1)S(1)} %collective-permute-done.qo_ref.after_ref, bf16[128,256]{1,0:T(8,128)(2,1)S(1)} %copy-done.9, ...), custom_call_target="tpu_custom_call" | custom-call | flops 671088640 | bytes 1048576 | tf_op jit(solution)/shard_map/attention/pallas_call | solution.py:151
  154.2 0.2 product.5
  154.5 1.6 collective-permute-start.4
  156.1 4.4 %collective-permute-done.4.refs_0_ = bf16[128,512]{1,0:T(8,128)(2,1)S(1)} collective-permute-done((bf16[128,512]{1,0:T(8,128)(2,1)S(1)}, bf16[128,512]{1,0:T(8,128)(2,1)S(1)}, u32[]{:S(2)}, u32[]{:S(2)}) %collective-permute-start.4) | collective-permute-done | bytes 131104 | tf_op jit(solution)/shard_map/ppermute | solution.py:25
  160.5 3.6 %all-to-all-start.1 = ((bf16[8,128,128]{2,1,0:T(8,128)(2,1)}), bf16[8,128,128]{2,1,0:T(8,128)(2,1)S(1)}, u32[]{:S(2)}, u32[]{:S(2)}) async-start(bf16[8,128,128]{2,1,0:T(8,128)(2,1)} %get-tuple-element.19), calls=%async_computation.1 | async-start | bytes 524288 | tf_op jit(solution)/shard_map/all_to_all | solution.py:285
  164.1 1.6 copy-done.1
  165.7 0.3 product.8
  166.1 1.6 collective-permute-start.9
  167.6 5.3 %all-to-all-done.1 = bf16[8,128,128]{2,1,0:T(8,128)(2,1)S(1)} async-done(((bf16[8,128,128]{2,1,0:T(8,128)(2,1)}), bf16[8,128,128]{2,1,0:T(8,128)(2,1)S(1)}, u32[]{:S(2)}, u32[]{:S(2)}) %all-to-all-start.1) | async-done | bytes 262176 | tf_op jit(solution)/shard_map/all_to_all | solution.py:285
  173.0 1.6 collective-permute-start.5
  174.6 1.6 copy-done.2
  176.2 0.3 product.9
  176.5 0.6 collective-permute-start.10
  177.1 0.3 product.7
  177.4 1.6 collective-permute-start.8
  179.1 2.5 %product.6.acc_ref = f32[128,4096]{1,0:T(8,128)S(1)} custom-call(bf16[128,512]{1,0:T(8,128)(2,1)S(1)} %get-tuple-element.15.dq_ref, bf16[256,4096]{1,0:T(8,128)(2,1)S(1)} %copy-done.4, bf16[256,4096]{1,0:T(8,128)(2,1)} %collective-permute-done.7.wo_ref), custom_call_target="tpu_custom_call" | custom-call | flops 536870912 | bytes 4194304 | tf_op jit(solution)/shard_map/product/pallas_call | solution.py:180
  181.6 8.0 %collective-permute-done.8.refs_1_ = bf16[128,1024]{1,0:T(8,128)(2,1)S(1)} collective-permute-done((bf16[128,1024]{1,0:T(8,128)(2,1)S(1)}, bf16[128,1024]{1,0:T(8,128)(2,1)S(1)}, u32[]{:S(2)}, u32[]{:S(2)}) %collective-permute-start.8) | collective-permute-done | bytes 262176 | tf_op jit(solution)/shard_map/ppermute | solution.py:25
  189.6 1.4 finish.1
  191.0 0.8 last.1
  (45 shorter events, 0.4 us)
Async XLA Ops:
  0.1 0.7 copy-start.6
  0.7 129.4 %copy-start.7 = (s32[128]{0:T(128)S(1)}, s32[128]{0:T(128)}, u32[]{:S(2)}) copy-start(s32[128]{0:T(128)} %after_ref.1) | copy-start | bytes 1540
  0.7 129.6 %copy-start.10 = (bf16[128,128]{1,0:T(8,128)(2,1)S(1)}, bf16[128,128]{1,0:T(8,128)(2,1)}, u32[]{:S(2)}) copy-start(bf16[128,128]{1,0:T(8,128)(2,1)} %param.9) | copy-start | bytes 98308
  0.7 129.6 %copy-start.11 = (bf16[128,128]{1,0:T(8,128)(2,1)S(1)}, bf16[128,128]{1,0:T(8,128)(2,1)}, u32[]{:S(2)}) copy-start(bf16[128,128]{1,0:T(8,128)(2,1)} %param.10) | copy-start | bytes 98308
  0.7 137.7 %copy-start.8 = (bf16[128,256]{1,0:T(8,128)(2,1)S(1)}, bf16[128,256]{1,0:T(8,128)(2,1)}, u32[]{:S(2)}) copy-start(bf16[128,256]{1,0:T(8,128)(2,1)} %qm_ref.1) | copy-start | bytes 196612
  0.7 137.8 %copy-start.9 = (bf16[128,256]{1,0:T(8,128)(2,1)S(1)}, bf16[128,256]{1,0:T(8,128)(2,1)}, u32[]{:S(2)}) copy-start(bf16[128,256]{1,0:T(8,128)(2,1)} %gm_ref.1) | copy-start | bytes 196612
  0.8 138.3 %copy-start.12 = (s32[128]{0:T(128)S(1)}, s32[128]{0:T(128)}, u32[]{:S(2)}) copy-start(s32[128]{0:T(128)} %param.13) | copy-start | bytes 1540
  129.5 24.8 %collective-permute-start.3 = (bf16[256,4096]{1,0:T(8,128)(2,1)}, bf16[256,4096]{1,0:T(8,128)(2,1)S(1)}, u32[]{:S(2)}, u32[]{:S(2)}) collective-permute-start(bf16[256,4096]{1,0:T(8,128)(2,1)} %get-tuple-element.17), channel_id=1, source_target_pairs={{0,1},{1,0},{2,3},{3,2},{4,5},{5,4},{6,7},{7,6},{8,9},{9,8},{10,11... | collective-permute-start | bytes 6291464 | tf_op jit(solution)/shard_map/ppermute | solution.py:25
  130.0 49.1 %collective-permute-start.7 = (bf16[256,4096]{1,0:T(8,128)(2,1)}, bf16[256,4096]{1,0:T(8,128)(2,1)}, u32[]{:S(2)}, u32[]{:S(2)}) collective-permute-start(bf16[256,4096]{1,0:T(8,128)(2,1)} %get-tuple-element.21), channel_id=1, source_target_pairs={{0,1},{1,0},{2,3},{3,2},{4,5},{5,4},{6,7},{7,6},{8,9},{9,8},{10,11... | collective-permute-start | bytes 6291464 | tf_op jit(solution)/shard_map/ppermute | solution.py:25
  131.2 17.0 %all-to-all-start = ((bf16[8,144,128]{2,1,0:T(8,128)(2,1)}), bf16[8,144,128]{2,1,0:T(8,128)(2,1)S(1)}, u32[]{:S(2)}, u32[]{:S(2)}) async-start(bf16[8,144,128]{2,1,0:T(8,128)(2,1)} %broadcast_in_dim.18), calls=%async_computation | async-start | bytes 589824 | tf_op jit(solution)/shard_map/all_to_all | solution.py:263
  138.4 9.9 %collective-permute-start = (bf16[128,256]{1,0:T(8,128)(2,1)S(1)}, bf16[128,256]{1,0:T(8,128)(2,1)S(1)}, u32[]{:S(2)}, u32[]{:S(2)}) collective-permute-start(bf16[128,256]{1,0:T(8,128)(2,1)S(1)} %copy-done.8), channel_id=1, source_target_pairs={{0,1},{1,0},{2,3},{3,2},{4,5},{5,4},{6,7},{7,6},{8,9},{9,8},{10,11... | collective-permute-start | bytes 196616 | tf_op jit(solution)/shard_map/ppermute | solution.py:25
  138.5 12.6 %collective-permute-start.1 = (bf16[128,256]{1,0:T(8,128)(2,1)S(1)}, bf16[128,256]{1,0:T(8,128)(2,1)S(1)}, u32[]{:S(2)}, u32[]{:S(2)}) collective-permute-start(bf16[128,256]{1,0:T(8,128)(2,1)S(1)} %copy-done.9), channel_id=1, source_target_pairs={{0,1},{1,0},{2,3},{3,2},{4,5},{5,4},{6,7},{7,6},{8,9},{9,8},{10,11... | collective-permute-start | bytes 196616 | tf_op jit(solution)/shard_map/ppermute | solution.py:25
  148.2 2.9 %collective-permute-start.2 = (bf16[8,144,128]{2,1,0:T(8,128)(2,1)S(1)}, bf16[8,144,128]{2,1,0:T(8,128)(2,1)S(1)}, u32[]{:S(2)}, u32[]{:S(2)}) collective-permute-start(bf16[8,144,128]{2,1,0:T(8,128)(2,1)S(1)} %all-to-all-done.here_ref), channel_id=1, source_target_pairs={{0,1},{1,0},{2,3},{3,2},{4,5},{5,4},{6,7},{7,6},{8,9},{9,8},{10,11... | collective-permute-start | bytes 884744 | tf_op jit(solution)/shard_map/ppermute | solution.py:25
  151.1 3.4 %copy-start = (bf16[256,4096]{1,0:T(8,128)(2,1)}, bf16[256,4096]{1,0:T(8,128)(2,1)S(1)}, u32[]{:S(2)}) copy-start(bf16[256,4096]{1,0:T(8,128)(2,1)S(1)} %get-tuple-element.16.wm_ref) | copy-start | bytes 6291460
  151.1 3.4 %copy-start.3 = (bf16[256,4096]{1,0:T(8,128)(2,1)}, bf16[256,4096]{1,0:T(8,128)(2,1)S(1)}, u32[]{:S(2)}) copy-start(bf16[256,4096]{1,0:T(8,128)(2,1)S(1)} %get-tuple-element.20.wm_ref) | copy-start | bytes 6291460
  154.5 6.0 %collective-permute-start.4 = (bf16[128,512]{1,0:T(8,128)(2,1)S(1)}, bf16[128,512]{1,0:T(8,128)(2,1)S(1)}, u32[]{:S(2)}, u32[]{:S(2)}) collective-permute-start(bf16[128,512]{1,0:T(8,128)(2,1)S(1)} %product.5), channel_id=1, source_target_pairs={{0,2},{1,3},{2,0},{3,1},{4,6},{5,7},{6,4},{7,5},{8,10},{9,11},{10,... | collective-permute-start | bytes 393224 | tf_op jit(solution)/shard_map/ppermute | solution.py:25
  160.5 12.4 %all-to-all-start.1 = ((bf16[8,128,128]{2,1,0:T(8,128)(2,1)}), bf16[8,128,128]{2,1,0:T(8,128)(2,1)S(1)}, u32[]{:S(2)}, u32[]{:S(2)}) async-start(bf16[8,128,128]{2,1,0:T(8,128)(2,1)} %get-tuple-element.19), calls=%async_computation.1 | async-start | bytes 524288 | tf_op jit(solution)/shard_map/all_to_all | solution.py:285
  164.1 1.6 copy-start.1
  166.1 23.5 %collective-permute-start.9 = (bf16[128,1280]{1,0:T(8,128)(2,1)S(1)}, bf16[128,1280]{1,0:T(8,128)(2,1)S(1)}, u32[]{:S(2)}, u32[]{:S(2)}) collective-permute-start(bf16[128,1280]{1,0:T(8,128)(2,1)S(1)} %product.8), channel_id=1, source_target_pairs={{0,2},{1,3},{2,0},{3,1},{4,6},{5,7},{6,4},{7,5},{8,10},{9,11},{10,... | collective-permute-start | bytes 983048 | tf_op jit(solution)/shard_map/ppermute | solution.py:25
  173.0 6.0 %collective-permute-start.5 = (bf16[128,128]{1,0:T(8,128)(2,1)S(1)}, bf16[128,128]{1,0:T(8,128)(2,1)S(1)}, u32[]{:S(2)}, u32[]{:S(2)}) collective-permute-start(bf16[128,128]{1,0:T(8,128)(2,1)S(1)} %reduce_sum.12), channel_id=1, source_target_pairs={{0,2},{1,3},{2,0},{3,1},{4,6},{5,7},{6,4},{7,5},{8,10},{9,11},{10,... | collective-permute-start | bytes 98312 | tf_op jit(solution)/shard_map/ppermute | solution.py:25
  174.6 1.6 copy-start.2
  176.5 2.6 %copy-start.4 = (bf16[256,4096]{1,0:T(8,128)(2,1)S(1)}, bf16[256,4096]{1,0:T(8,128)(2,1)}, u32[]{:S(2)}) copy-start(bf16[256,4096]{1,0:T(8,128)(2,1)} %copy-done.3) | copy-start | bytes 6291460
  176.5 14.5 %collective-permute-start.10 = (bf16[128,1280]{1,0:T(8,128)(2,1)S(1)}, bf16[128,1280]{1,0:T(8,128)(2,1)S(1)}, u32[]{:S(2)}, u32[]{:S(2)}) collective-permute-start(bf16[128,1280]{1,0:T(8,128)(2,1)S(1)} %product.9), channel_id=1, source_target_pairs={{0,2},{1,3},{2,0},{3,1},{4,6},{5,7},{6,4},{7,5},{8,10},{9,11},{10,... | collective-permute-start | bytes 983048 | tf_op jit(solution)/shard_map/ppermute | solution.py:25
  177.4 12.2 %collective-permute-start.8 = (bf16[128,1024]{1,0:T(8,128)(2,1)S(1)}, bf16[128,1024]{1,0:T(8,128)(2,1)S(1)}, u32[]{:S(2)}, u32[]{:S(2)}) collective-permute-start(bf16[128,1024]{1,0:T(8,128)(2,1)S(1)} %product.7), channel_id=1, source_target_pairs={{0,2},{1,3},{2,0},{3,1},{4,6},{5,7},{6,4},{7,5},{8,10},{9,11},{10,... | collective-permute-start | bytes 786440 | tf_op jit(solution)/shard_map/ppermute | solution.py:25
  179.0 2.6 %collective-permute-start.6 = (bf16[128,128]{1,0:T(8,128)(2,1)S(1)}, bf16[128,128]{1,0:T(8,128)(2,1)S(1)}, u32[]{:S(2)}, u32[]{:S(2)}) collective-permute-start(bf16[128,128]{1,0:T(8,128)(2,1)S(1)} %get-tuple-element.25), channel_id=1, source_target_pairs={{0,1},{1,0},{2,3},{3,2},{4,5},{5,4},{6,7},{7,6},{8,9},{9,8},{10,11... | collective-permute-start | bytes 98312 | tf_op jit(solution)/shard_map/ppermute | solution.py:25
  179.1 10.5 %copy-start.5 = (bf16[256,4096]{1,0:T(8,128)(2,1)S(1)}, bf16[256,4096]{1,0:T(8,128)(2,1)}, u32[]{:S(2)}) copy-start(bf16[256,4096]{1,0:T(8,128)(2,1)} %w_ref.5) | copy-start | bytes 6291460

commit v4 on v3

--- a/solution.py
+++ b/solution.py
@@ -10,13 +10,13 @@
 
 RUN = 64
 META_ROWS = 16
-CHUNKS = (2, 4, 5, 5)
+CHUNKS = (2, 7, 7)
 ANY = pl.BlockSpec(memory_space=pl.ANY)
 HBM = pl.BlockSpec(memory_space=pltpu.HBM)
 SMEM = pl.BlockSpec(memory_space=pltpu.SMEM)
 
 
-def params(limit_mib=32):
+def params(limit_mib=16):
     return pltpu.CompilerParams(vmem_limit_bytes=limit_mib * 1024 * 1024)
 
 
@@ -48,12 +48,16 @@
 
 def carve_kernel(block_ref, w_ref, after_ref, *refs):
     outs, sems = refs[:-1], refs[-1]
-    share = outs[0].shape[1]
+    rows, share = outs[0].shape
+    parts = sems.shape[1]
     copies = []
     for i, out_ref in enumerate(outs):
         at = pl.multiple_of(block_ref[i] * share, share)
-        copies.append(pltpu.make_async_copy(w_ref.at[:, pl.ds(at, share)], out_ref, sems.at[i]))
-        copies[i].start()
+        for j in range(parts):
+            part = slice(j * (rows // parts), (j + 1) * (rows // parts))
+            source = w_ref.at[part, pl.ds(at, share)]
+            copies.append(pltpu.make_async_copy(source, out_ref.at[part, :], sems.at[i, j]))
+            copies[-1].start()
     for one in copies:
         one.wait()
 
@@ -65,8 +69,8 @@
         carve_kernel,
         out_shape=[shape] * count,
         in_specs=[SMEM, HBM, ANY],
-        out_specs=[ANY] * count,
-        scratch_shapes=[pltpu.SemaphoreType.DMA((count,))],
+        out_specs=[pl.BlockSpec(memory_space=pltpu.VMEM)] * count,
+        scratch_shapes=[pltpu.SemaphoreType.DMA((count, 4))],
         compiler_params=params(48),
         cost_estimate=pl.CostEstimate(
             flops=0, bytes_accessed=4 * count * w_query.shape[0] * share, transcendentals=0
@@ -157,7 +161,7 @@
         in_specs=[SMEM] + [pl.BlockSpec()] * 7,
         out_specs=[pl.BlockSpec()] * 2,
         scratch_shapes=[pltpu.VMEM((count, rows, wide), jnp.float32)] * 2,
-        compiler_params=params(44),
+        compiler_params=params(8 + count * rows * wide // 2**17),
         cost_estimate=pl.CostEstimate(
             flops=10 * count * rows * wide * size,
             bytes_accessed=count * rows * size * 8,
@@ -267,7 +271,7 @@
 
     send = carve([head ^ 3, head ^ 1], w_query, positions, share)
     far_other, near_other = [swapped(part, "head", 1) for part in send]
-    far_mine, near_mine = carve([head ^ 2, head], w_query, q_other, share)
+    far_mine, near_mine = carve([head ^ 2, head], w_query, g_other, share)
 
     bounds = jnp.stack([positions, doc_ids * RUN]).astype(jnp.float32)
     row_info = jnp.tile(bounds, (1, 2 * (queries.shape[1] // keys.shape[1])))
@@ -276,12 +280,12 @@
     starts = [0]
     for units in CHUNKS:
         starts.append(starts[-1] + units * (share // sum(CHUNKS)))
-    received = []
-    for low, high in zip(starts, starts[1:]):
-        part = product(dq, far_mine, far_other, low, high - low, jnp.bfloat16)
-        received.append(swapped(part, "head", 2))
-
-    received[0], back = lax.optimization_barrier((received[0], back))
+    parts = [
+        product(dq, far_mine, far_other, low, high - low, jnp.bfloat16) for low, high in zip(starts, starts[1:])
+    ]
+    received = [swapped(part, "head", 2) for part in parts]
+
+    back, *_ = lax.optimization_barrier([back, received[0]] + parts)
     back = lax.all_to_all(back, "ctx", 0, 0)
     mine = jnp.sum(back.astype(jnp.float32), axis=0).astype(jnp.bfloat16)
     mine = mine.astype(jnp.float32) + swapped(mine, "head", 2).astype(jnp.float32)

time: 192 us -> 69.5 us (0.36)
  Pallas kernels: 140 us -> 16.4 us
  waiting for transfers between devices: 26.9 us -> 31.6 us
    pallas_call x2, Pallas kernels: 132 us -> 7.55 us  [carve(): pl.pallas_call(carve_kernel, out_shape=[shape] * count, in_specs=[SMEM, H...]
    ppermute x11 -> x10, waiting for transfers between devices: 12.4 us -> 15.6 us  [swapped(): lax.ppermute(value, axis, [(source, source ^ bits) for source in range(co...]
    ppermute x11 -> x10, starting transfers between devices: 8.15 us -> 6.43 us  [swapped(): lax.ppermute(value, axis, [(source, source ^ bits) for source in range(co...]
    unnamed x28 -> x22, local copies, waits for them, and re-layouts: 3.89 us -> 2.28 us
  transfers between devices with their start and end apart: 13 -> 12, of which waited for: 4 -> 4; matrix products, arithmetic and copies ran while one was open for 1% -> 2% of each run, Pallas kernels for 6% -> 15%
where the time goes in v4:
time: 69.5 us; the launch traced here: 69.1 us
  waiting for transfers between devices  31.6 us (45%)
  starting transfers between devices  17.3 us (25%)
  Pallas kernels  16.4 us (24%)
  local copies, waits for them, and re-layouts  3.12 us (4%)
    ppermute x10, waiting for transfers between devices, swapped(): lax.ppermute(value, axis, [(source, source ^ bits) for source in range(co...  15.6 us
    all_to_all x1, waiting for transfers between devices, on_device(): lax.all_to_all(pack(count, core, positions, keys, values), 'ctx', 0, 0)  9.21 us
    pallas_call x2, Pallas kernels, carve(): pl.pallas_call(carve_kernel, out_shape=[shape] * count, in_specs=[SMEM, H...  7.55 us
    all_to_all x1, starting transfers between devices, on_device(): lax.all_to_all(pack(count, core, positions, keys, values), 'ctx', 0, 0)  7.23 us
    all_to_all x1, waiting for transfers between devices, on_device(): back = lax.all_to_all(back, 'ctx', 0, 0)  6.78 us
    ppermute x10, starting transfers between devices, swapped(): lax.ppermute(value, axis, [(source, source ^ bits) for source in range(co...  6.43 us
    all_to_all x1, starting transfers between devices, on_device(): back = lax.all_to_all(back, 'ctx', 0, 0)  3.64 us
    pallas_call x4, Pallas kernels, product(): pl.pallas_call(functools.partial(product_kernel, first), out_shape=jax.Sh...  3.52 us
  transfers between devices with their start and end apart: 12, of which 4 were waited for; matrix products, arithmetic and copies ran while one was open for 2% of the time, Pallas kernels for 15%

profile of v4, /device:TPU:0, one launch (start us, length us, event | category | flops | bytes accessed | tf_op | source)
XLA Modules:
  0.0 69.1 jit_solution(4782407552345756588)
XLA Ops:
  0.0 0.1 pad_add_fusion.1.block_ref
  0.1 0.7 copy-done.3
  0.8 4.8 %carve.3 = (bf16[256,4096]{1,0:T(8,128)(2,1)}, bf16[256,4096]{1,0:T(8,128)(2,1)}) custom-call(s32[2]{0:T(128)S(1)} %pad_add_fusion.1.block_ref, bf16[256,16384]{1,0:T(8,128)(2,1)} %w_ref.4, s32[128]{0:T(128)S(1)} %copy-done.3), custom_call_target="tpu_custom_call" | custom-call | bytes 8388608 | tf_op jit(solution)/shard_map/carve/pallas_call | solution.py:68
  5.6 0.5 collective-permute-start.3
  6.1 0.1 collective-permute-start.7
  6.2 0.1 reshape.28
  6.2 0.1 fusion.1
  6.4 0.1 pad_maximum_fusion
  6.5 0.8 %broadcast_in_dim.18 = bf16[8,144,128]{2,1,0:T(8,128)(2,1)} broadcast(bf16[144,128]{1,0:T(8,128)(2,1)S(1)} %pad_maximum_fusion), dimensions={1,2} | broadcast | bytes 331776 | tf_op jit(solution)/shard_map/broadcast_in_dim | solution.py:46
  7.3 7.2 %all-to-all-start = ((bf16[8,144,128]{2,1,0:T(8,128)(2,1)}), bf16[8,144,128]{2,1,0:T(8,128)(2,1)S(1)}, u32[]{:S(2)}, u32[]{:S(2)}) async-start(bf16[8,144,128]{2,1,0:T(8,128)(2,1)} %broadcast_in_dim.18), calls=%async_computation | async-start | bytes 589824 | tf_op jit(solution)/shard_map/all_to_all | solution.py:267
  14.5 0.1 collective-permute-start
  14.6 0.5 collective-permute-start.1
  15.1 9.2 %all-to-all-done.here_ref = bf16[8,144,128]{2,1,0:T(8,128)(2,1)S(1)} async-done(((bf16[8,144,128]{2,1,0:T(8,128)(2,1)}), bf16[8,144,128]{2,1,0:T(8,128)(2,1)S(1)}, u32[]{:S(2)}, u32[]{:S(2)}) %all-to-all-start) | async-done | bytes 294944 | tf_op jit(solution)/shard_map/all_to_all | solution.py:267
  24.3 0.1 pad_add_fusion.block_ref
  24.4 2.8 %carve.2 = (bf16[256,4096]{1,0:T(8,128)(2,1)S(1)}, bf16[256,4096]{1,0:T(8,128)(2,1)S(1)}) custom-call(s32[2]{0:T(128)S(1)} %pad_add_fusion.block_ref, bf16[256,16384]{1,0:T(8,128)(2,1)} %w_ref.4, bf16[128,256]{1,0:T(8,128)(2,1)S(1)} %collective-permute-done.1.go_ref.after_ref), custom_call_target="tpu_custom_call" | custom-call | bytes 8388608 | tf_op jit(solution)/shard_map/carve/pallas_call | solution.py:68
  27.2 3.1 %attention.1 = (bf16[128,512]{1,0:T(8,128)(2,1)S(1)}, bf16[8,128,128]{2,1,0:T(8,128)(2,1)}) custom-call(s32[1]{0:T(128)} %bitcast.core_ref, f32[2,512]{1,0:T(2,128)S(1)} %bitcast.14, bf16[128,256]{1,0:T(8,128)(2,1)S(1)} %copy-done.5, bf16[128,256]{1,0:T(8,128)(2,1)S(1)} %collective-permute-done.qo_ref, bf16[128,256]{1,0:T(8,128)(2,1)S(1)} %copy-done.6, ...), custom_call_target="tpu_custom_call" | custom-call | flops 671088640 | bytes 1048576 | tf_op jit(solution)/shard_map/attention/pallas_call | solution.py:155
  30.3 0.2 product.4
  30.5 1.6 %collective-permute-start.4 = (bf16[128,512]{1,0:T(8,128)(2,1)S(1)}, bf16[128,512]{1,0:T(8,128)(2,1)S(1)}, u32[]{:S(2)}, u32[]{:S(2)}) collective-permute-start(bf16[128,512]{1,0:T(8,128)(2,1)S(1)} %product.4), channel_id=1, source_target_pairs={{0,2},{1,3},{2,0},{3,1},{4,6},{5,7},{6,4},{7,5},{8,10},{9,11},{10,... | collective-permute-start | bytes 393224 | tf_op jit(solution)/shard_map/ppermute | solution.py:25
  32.1 0.4 product.6
  32.5 0.4 product.5
  33.0 3.5 %collective-permute-done.4.refs_0_ = bf16[128,512]{1,0:T(8,128)(2,1)S(1)} collective-permute-done((bf16[128,512]{1,0:T(8,128)(2,1)S(1)}, bf16[128,512]{1,0:T(8,128)(2,1)S(1)}, u32[]{:S(2)}, u32[]{:S(2)}) %collective-permute-start.4) | collective-permute-done | bytes 131104 | tf_op jit(solution)/shard_map/ppermute | solution.py:25
  36.5 3.6 %all-to-all-start.1 = ((bf16[8,128,128]{2,1,0:T(8,128)(2,1)}), bf16[8,128,128]{2,1,0:T(8,128)(2,1)S(1)}, u32[]{:S(2)}, u32[]{:S(2)}) async-start(bf16[8,128,128]{2,1,0:T(8,128)(2,1)} %get-tuple-element.18), calls=%async_computation.1 | async-start | bytes 524288 | tf_op jit(solution)/shard_map/all_to_all | solution.py:289
  40.1 1.5 %collective-permute-start.8 = (bf16[128,1792]{1,0:T(8,128)(2,1)S(1)}, bf16[128,1792]{1,0:T(8,128)(2,1)S(1)}, u32[]{:S(2)}, u32[]{:S(2)}) collective-permute-start(bf16[128,1792]{1,0:T(8,128)(2,1)S(1)} %product.5), channel_id=1, source_target_pairs={{0,2},{1,3},{2,0},{3,1},{4,6},{5,7},{6,4},{7,5},{8,10},{9,11},{10,... | collective-permute-start | bytes 1376264 | tf_op jit(solution)/shard_map/ppermute | solution.py:25
  41.7 0.5 collective-permute-start.9
  42.2 6.8 %all-to-all-done.1 = bf16[8,128,128]{2,1,0:T(8,128)(2,1)S(1)} async-done(((bf16[8,128,128]{2,1,0:T(8,128)(2,1)}), bf16[8,128,128]{2,1,0:T(8,128)(2,1)S(1)}, u32[]{:S(2)}, u32[]{:S(2)}) %all-to-all-start.1) | async-done | bytes 262176 | tf_op jit(solution)/shard_map/all_to_all | solution.py:289
  49.0 1.6 %collective-permute-start.5 = (bf16[128,128]{1,0:T(8,128)(2,1)S(1)}, bf16[128,128]{1,0:T(8,128)(2,1)S(1)}, u32[]{:S(2)}, u32[]{:S(2)}) collective-permute-start(bf16[128,128]{1,0:T(8,128)(2,1)S(1)} %reduce_sum.12), channel_id=1, source_target_pairs={{0,2},{1,3},{2,0},{3,1},{4,6},{5,7},{6,4},{7,5},{8,10},{9,11},{10,... | collective-permute-start | bytes 98312 | tf_op jit(solution)/shard_map/ppermute | solution.py:25
  50.6 12.1 %collective-permute-done.5 = bf16[128,128]{1,0:T(8,128)(2,1)S(1)} collective-permute-done((bf16[128,128]{1,0:T(8,128)(2,1)S(1)}, bf16[128,128]{1,0:T(8,128)(2,1)S(1)}, u32[]{:S(2)}, u32[]{:S(2)}) %collective-permute-start.5) | collective-permute-done | bytes 32800 | tf_op jit(solution)/shard_map/ppermute | solution.py:25
  62.7 0.1 collective-permute-start.6
  62.8 1.6 %copy-done.1 = bf16[256,4096]{1,0:T(8,128)(2,1)S(1)} copy-done((bf16[256,4096]{1,0:T(8,128)(2,1)S(1)}, bf16[256,4096]{1,0:T(8,128)(2,1)}, u32[]{:S(2)}) %copy-start.1) | copy-done | bytes 2097176
  64.4 2.5 %product.7.acc_ref = f32[128,4096]{1,0:T(8,128)S(1)} custom-call(bf16[128,512]{1,0:T(8,128)(2,1)S(1)} %get-tuple-element.15.dq_ref, bf16[256,4096]{1,0:T(8,128)(2,1)S(1)} %copy-done.1, bf16[256,4096]{1,0:T(8,128)(2,1)} %collective-permute-done.7.wo_ref), custom_call_target="tpu_custom_call" | custom-call | flops 536870912 | bytes 4194304 | tf_op jit(solution)/shard_map/product/pallas_call | solution.py:184
  66.9 1.3 %finish.1 = (bf16[128,4096]{1,0:T(8,128)(2,1)}, f32[128,1792]{1,0:T(8,128)S(1)}) custom-call(s32[1]{0:T(128)} %bitcast.core_ref, f32[128,128]{1,0:T(8,128)S(1)} %get-tuple-element.24.mine_ref, f32[128,128]{1,0:T(8,128)S(1)} %convert_element_type.31.other_ref, bf16[256,4096]{1,0:T(8,128)(2,1)S(1)} %copy-done.2, f32[128,4096]{1,0:T(8,128)S(1)} %product.7.acc_ref, ...), custom_call_target="tpu_custom_call" | custom-call | flops 268435456 | bytes 5242880 | tf_op jit(solution)/shard_map/finish/pallas_call | solution.py:220
  68.2 0.9 %last.1 = bf16[128,4096]{1,0:T(8,128)(2,1)} custom-call(f32[128,1792]{1,0:T(8,128)S(1)} %get-tuple-element.21.left_ref, bf16[128,1792]{1,0:T(8,128)(2,1)S(1)} %collective-permute-done.9.part_ref, bf16[128,4096]{1,0:T(8,128)(2,1)} %get-tuple-element.22.held_ref), custom_call_target="tpu_custom_call", output_to_operand_aliasing={{}: (2, {})} | custom-call | tf_op jit(solution)/shard_map/last/pallas_call | solution.py:249
  (36 shorter events, 0.2 us)
Async XLA Ops:
  0.1 0.7 copy-start.3
  0.7 5.4 %copy-start.4 = (s32[128]{0:T(128)S(1)}, s32[128]{0:T(128)}, u32[]{:S(2)}) copy-start(s32[128]{0:T(128)} %after_ref.1) | copy-start | bytes 1540
  0.7 5.6 %copy-start.7 = (bf16[128,128]{1,0:T(8,128)(2,1)S(1)}, bf16[128,128]{1,0:T(8,128)(2,1)}, u32[]{:S(2)}) copy-start(bf16[128,128]{1,0:T(8,128)(2,1)} %param.9) | copy-start | bytes 98308
  0.7 5.6 %copy-start.8 = (bf16[128,128]{1,0:T(8,128)(2,1)S(1)}, bf16[128,128]{1,0:T(8,128)(2,1)}, u32[]{:S(2)}) copy-start(bf16[128,128]{1,0:T(8,128)(2,1)} %param.10) | copy-start | bytes 98308
  0.7 13.8 %copy-start.5 = (bf16[128,256]{1,0:T(8,128)(2,1)S(1)}, bf16[128,256]{1,0:T(8,128)(2,1)}, u32[]{:S(2)}) copy-start(bf16[128,256]{1,0:T(8,128)(2,1)} %qm_ref.1) | copy-start | bytes 196612
  0.7 13.8 %copy-start.6 = (bf16[128,256]{1,0:T(8,128)(2,1)S(1)}, bf16[128,256]{1,0:T(8,128)(2,1)}, u32[]{:S(2)}) copy-start(bf16[128,256]{1,0:T(8,128)(2,1)} %gm_ref.1) | copy-start | bytes 196612
  0.8 14.3 %copy-start.9 = (s32[128]{0:T(128)S(1)}, s32[128]{0:T(128)}, u32[]{:S(2)}) copy-start(s32[128]{0:T(128)} %param.13) | copy-start | bytes 1540
  5.6 24.7 %collective-permute-start.3 = (bf16[256,4096]{1,0:T(8,128)(2,1)}, bf16[256,4096]{1,0:T(8,128)(2,1)S(1)}, u32[]{:S(2)}, u32[]{:S(2)}) collective-permute-start(bf16[256,4096]{1,0:T(8,128)(2,1)} %get-tuple-element.17), channel_id=1, source_target_pairs={{0,1},{1,0},{2,3},{3,2},{4,5},{5,4},{6,7},{7,6},{8,9},{9,8},{10,11... | collective-permute-start | bytes 6291464 | tf_op jit(solution)/shard_map/ppermute | solution.py:25
  6.1 56.7 %collective-permute-start.7 = (bf16[256,4096]{1,0:T(8,128)(2,1)}, bf16[256,4096]{1,0:T(8,128)(2,1)}, u32[]{:S(2)}, u32[]{:S(2)}) collective-permute-start(bf16[256,4096]{1,0:T(8,128)(2,1)} %get-tuple-element.20), channel_id=1, source_target_pairs={{0,1},{1,0},{2,3},{3,2},{4,5},{5,4},{6,7},{7,6},{8,9},{9,8},{10,11... | collective-permute-start | bytes 6291464 | tf_op jit(solution)/shard_map/ppermute | solution.py:25
  7.3 17.0 %all-to-all-start = ((bf16[8,144,128]{2,1,0:T(8,128)(2,1)}), bf16[8,144,128]{2,1,0:T(8,128)(2,1)S(1)}, u32[]{:S(2)}, u32[]{:S(2)}) async-start(bf16[8,144,128]{2,1,0:T(8,128)(2,1)} %broadcast_in_dim.18), calls=%async_computation | async-start | bytes 589824 | tf_op jit(solution)/shard_map/all_to_all | solution.py:267
  14.5 12.7 %collective-permute-start = (bf16[128,256]{1,0:T(8,128)(2,1)S(1)}, bf16[128,256]{1,0:T(8,128)(2,1)S(1)}, u32[]{:S(2)}, u32[]{:S(2)}) collective-permute-start(bf16[128,256]{1,0:T(8,128)(2,1)S(1)} %copy-done.5), channel_id=1, source_target_pairs={{0,1},{1,0},{2,3},{3,2},{4,5},{5,4},{6,7},{7,6},{8,9},{9,8},{10,11... | collective-permute-start | bytes 196616 | tf_op jit(solution)/shard_map/ppermute | solution.py:25
  14.6 9.8 %collective-permute-start.1 = (bf16[128,256]{1,0:T(8,128)(2,1)S(1)}, bf16[128,256]{1,0:T(8,128)(2,1)S(1)}, u32[]{:S(2)}, u32[]{:S(2)}) collective-permute-start(bf16[128,256]{1,0:T(8,128)(2,1)S(1)} %copy-done.6), channel_id=1, source_target_pairs={{0,1},{1,0},{2,3},{3,2},{4,5},{5,4},{6,7},{7,6},{8,9},{9,8},{10,11... | collective-permute-start | bytes 196616 | tf_op jit(solution)/shard_map/ppermute | solution.py:25
  24.3 2.9 %collective-permute-start.2 = (bf16[8,144,128]{2,1,0:T(8,128)(2,1)S(1)}, bf16[8,144,128]{2,1,0:T(8,128)(2,1)S(1)}, u32[]{:S(2)}, u32[]{:S(2)}) collective-permute-start(bf16[8,144,128]{2,1,0:T(8,128)(2,1)S(1)} %all-to-all-done.here_ref), channel_id=1, source_target_pairs={{0,1},{1,0},{2,3},{3,2},{4,5},{5,4},{6,7},{7,6},{8,9},{9,8},{10,11... | collective-permute-start | bytes 884744 | tf_op jit(solution)/shard_map/ppermute | solution.py:25
  27.2 3.4 %copy-start = (bf16[256,4096]{1,0:T(8,128)(2,1)}, bf16[256,4096]{1,0:T(8,128)(2,1)S(1)}, u32[]{:S(2)}) copy-start(bf16[256,4096]{1,0:T(8,128)(2,1)S(1)} %get-tuple-element.19.wm_ref) | copy-start | bytes 6291460
  30.5 6.0 %collective-permute-start.4 = (bf16[128,512]{1,0:T(8,128)(2,1)S(1)}, bf16[128,512]{1,0:T(8,128)(2,1)S(1)}, u32[]{:S(2)}, u32[]{:S(2)}) collective-permute-start(bf16[128,512]{1,0:T(8,128)(2,1)S(1)} %product.4), channel_id=1, source_target_pairs={{0,2},{1,3},{2,0},{3,1},{4,6},{5,7},{6,4},{7,5},{8,10},{9,11},{10,... | collective-permute-start | bytes 393224 | tf_op jit(solution)/shard_map/ppermute | solution.py:25
  36.5 12.4 %all-to-all-start.1 = ((bf16[8,128,128]{2,1,0:T(8,128)(2,1)}), bf16[8,128,128]{2,1,0:T(8,128)(2,1)S(1)}, u32[]{:S(2)}, u32[]{:S(2)}) async-start(bf16[8,128,128]{2,1,0:T(8,128)(2,1)} %get-tuple-element.18), calls=%async_computation.1 | async-start | bytes 524288 | tf_op jit(solution)/shard_map/all_to_all | solution.py:289
  40.1 26.7 %collective-permute-start.8 = (bf16[128,1792]{1,0:T(8,128)(2,1)S(1)}, bf16[128,1792]{1,0:T(8,128)(2,1)S(1)}, u32[]{:S(2)}, u32[]{:S(2)}) collective-permute-start(bf16[128,1792]{1,0:T(8,128)(2,1)S(1)} %product.5), channel_id=1, source_target_pairs={{0,2},{1,3},{2,0},{3,1},{4,6},{5,7},{6,4},{7,5},{8,10},{9,11},{10,... | collective-permute-start | bytes 1376264 | tf_op jit(solution)/shard_map/ppermute | solution.py:25
  41.7 26.6 %collective-permute-start.9 = (bf16[128,1792]{1,0:T(8,128)(2,1)S(1)}, bf16[128,1792]{1,0:T(8,128)(2,1)S(1)}, u32[]{:S(2)}, u32[]{:S(2)}) collective-permute-start(bf16[128,1792]{1,0:T(8,128)(2,1)S(1)} %product.6), channel_id=1, source_target_pairs={{0,2},{1,3},{2,0},{3,1},{4,6},{5,7},{6,4},{7,5},{8,10},{9,11},{10,... | collective-permute-start | bytes 1376264 | tf_op jit(solution)/shard_map/ppermute | solution.py:25
  49.0 13.7 %collective-permute-start.5 = (bf16[128,128]{1,0:T(8,128)(2,1)S(1)}, bf16[128,128]{1,0:T(8,128)(2,1)S(1)}, u32[]{:S(2)}, u32[]{:S(2)}) collective-permute-start(bf16[128,128]{1,0:T(8,128)(2,1)S(1)} %reduce_sum.12), channel_id=1, source_target_pairs={{0,2},{1,3},{2,0},{3,1},{4,6},{5,7},{6,4},{7,5},{8,10},{9,11},{10,... | collective-permute-start | bytes 98312 | tf_op jit(solution)/shard_map/ppermute | solution.py:25
  62.7 4.1 %collective-permute-start.6 = (bf16[128,128]{1,0:T(8,128)(2,1)S(1)}, bf16[128,128]{1,0:T(8,128)(2,1)S(1)}, u32[]{:S(2)}, u32[]{:S(2)}) collective-permute-start(bf16[128,128]{1,0:T(8,128)(2,1)S(1)} %get-tuple-element.23), channel_id=1, source_target_pairs={{0,1},{1,0},{2,3},{3,2},{4,5},{5,4},{6,7},{7,6},{8,9},{9,8},{10,11... | collective-permute-start | bytes 98312 | tf_op jit(solution)/shard_map/ppermute | solution.py:25
  62.8 1.6 %copy-start.1 = (bf16[256,4096]{1,0:T(8,128)(2,1)S(1)}, bf16[256,4096]{1,0:T(8,128)(2,1)}, u32[]{:S(2)}) copy-start(bf16[256,4096]{1,0:T(8,128)(2,1)} %copy-done) | copy-start | bytes 6291460
  64.4 2.5 %copy-start.2 = (bf16[256,4096]{1,0:T(8,128)(2,1)S(1)}, bf16[256,4096]{1,0:T(8,128)(2,1)}, u32[]{:S(2)}) copy-start(bf16[256,4096]{1,0:T(8,128)(2,1)} %w_ref.5) | copy-start | bytes 6291460

commit v5 on v4

--- a/solution.py
+++ b/solution.py
@@ -10,7 +10,7 @@
 
 RUN = 64
 META_ROWS = 16
-CHUNKS = (2, 7, 7)
+CHUNKS = (1, 11, 4)
 ANY = pl.BlockSpec(memory_space=pl.ANY)
 HBM = pl.BlockSpec(memory_space=pltpu.HBM)
 SMEM = pl.BlockSpec(memory_space=pltpu.SMEM)
@@ -265,30 +265,32 @@
     share = w_kv.shape[1]
 
     here = lax.all_to_all(pack(count, core, positions, keys, values), "ctx", 0, 0)
-    there = swapped(here, "head", 1)
     q_other = swapped(queries, "head", 1)
     g_other = swapped(dout, "head", 1)
-
-    send = carve([head ^ 3, head ^ 1], w_query, positions, share)
-    far_other, near_other = [swapped(part, "head", 1) for part in send]
-    far_mine, near_mine = carve([head ^ 2, head], w_query, g_other, share)
+    blocks = carve([head ^ 3, head ^ 1, head ^ 2, head], w_query, q_other, share)
+    here, far_send, near_send, far_mine, near_mine = lax.optimization_barrier([here, *blocks])
+    there, far_send = lax.optimization_barrier((swapped(here, "head", 1), far_send))
+    far_other = swapped(far_send, "head", 1)
 
     bounds = jnp.stack([positions, doc_ids * RUN]).astype(jnp.float32)
     row_info = jnp.tile(bounds, (1, 2 * (queries.shape[1] // keys.shape[1])))
     dq, back = attention(core, row_info, queries, q_other, dout, g_other, here, there)
 
+    dq, near_send = lax.optimization_barrier((dq, near_send))
+    near_other = swapped(near_send, "head", 1)
     starts = [0]
     for units in CHUNKS:
         starts.append(starts[-1] + units * (share // sum(CHUNKS)))
     parts = [
         product(dq, far_mine, far_other, low, high - low, jnp.bfloat16) for low, high in zip(starts, starts[1:])
     ]
-    received = [swapped(part, "head", 2) for part in parts]
-
+    received = [swapped(part, "head", 2) for part in parts[:-1]]
     back, *_ = lax.optimization_barrier([back, received[0]] + parts)
     back = lax.all_to_all(back, "ctx", 0, 0)
     mine = jnp.sum(back.astype(jnp.float32), axis=0).astype(jnp.bfloat16)
+    mine, part = lax.optimization_barrier((mine, parts[-1]))
     mine = mine.astype(jnp.float32) + swapped(mine, "head", 2).astype(jnp.float32)
+    received.append(swapped(part, "head", 2))
     other = swapped(mine.astype(jnp.bfloat16), "head", 1).astype(jnp.float32)
 
     acc = product(dq, near_mine, near_other, 0, share, jnp.float32)

time: 69.5 us -> 66.3 us (0.954)
  waiting for transfers between devices: 31.6 us -> 24.3 us
  local copies, waits for them, and re-layouts: 3.12 us -> 5.84 us
  starting transfers between devices: 17.3 us -> 19.6 us
  Pallas kernels: 16.4 us -> 14.8 us
    all_to_all x1, waiting for transfers between devices: 9.21 us -> 0.01 us  [on_device(): lax.all_to_all(pack(count, core, positions, keys, values), 'ctx', 0, 0)]
    all_to_all x1, starting transfers between devices: 3.64 us -> 6 us  [on_device(): back = lax.all_to_all(back, 'ctx', 0, 0)]
    unnamed x22 -> x20, local copies, waits for them, and re-layouts: 2.28 us -> 4.35 us
    ppermute x10, waiting for transfers between devices: 15.6 us -> 17.6 us  [swapped(): lax.ppermute(value, axis, [(source, source ^ bits) for source in range(co...]
    pallas_call x2 -> x1, Pallas kernels: 7.55 us -> 6.02 us  [carve(): pl.pallas_call(carve_kernel, out_shape=[shape] * count, in_specs=[SMEM, H...]
    select_n x1, other arithmetic: 0.01 us -> 0.77 us  [pack(): held = jnp.where(core == 0, keys, values)]
  transfers between devices with their start and end apart: 12 -> 12, of which waited for: 4 -> 6; matrix products, arithmetic and copies ran while one was open for 2% -> 0% of each run, Pallas kernels for 15% -> 21%
where the time goes in v5:
time: 66.3 us; the launch traced here: 65.8 us
  waiting for transfers between devices  24.3 us (37%)
  starting transfers between devices  19.6 us (30%)
  Pallas kernels  14.8 us (22%)
  local copies, waits for them, and re-layouts  5.84 us (9%)
  other arithmetic  1.14 us (2%)
    ppermute x10, waiting for transfers between devices, swapped(): lax.ppermute(value, axis, [(source, source ^ bits) for source in range(co...  17.6 us
    all_to_all x1, starting transfers between devices, on_device(): lax.all_to_all(pack(count, core, positions, keys, values), 'ctx', 0, 0)  7.25 us
    all_to_all x1, waiting for transfers between devices, on_device(): back = lax.all_to_all(back, 'ctx', 0, 0)  6.71 us
    ppermute x10, starting transfers between devices, swapped(): lax.ppermute(value, axis, [(source, source ^ bits) for source in range(co...  6.31 us
    pallas_call x1, Pallas kernels, carve(): pl.pallas_call(carve_kernel, out_shape=[shape] * count, in_specs=[SMEM, H...  6.02 us
    all_to_all x1, starting transfers between devices, on_device(): back = lax.all_to_all(back, 'ctx', 0, 0)  6 us
    unnamed x20, local copies, waits for them, and re-layouts  4.35 us
    pallas_call x4, Pallas kernels, product(): pl.pallas_call(functools.partial(product_kernel, first), out_shape=jax.Sh...  3.51 us
  transfers between devices with their start and end apart: 12, of which 6 were waited for; matrix products, arithmetic and copies ran while one was open for 0% of the time, Pallas kernels for 21%

profile of v5, /device:TPU:0, one launch (start us, length us, event | category | flops | bytes accessed | tf_op | source)
XLA Modules:
  0.0 65.8 jit_solution(9314168490701571891)
XLA Ops:
  0.0 0.7 %reshape.28 = s32[2,64]{1,0:T(2,128)S(1)} reshape(s32[128]{0:T(128)} %param.12) | data formatting | bytes 1024 | tf_op jit(solution)/shard_map/reshape | solution.py:43
  0.7 0.1 fusion.1
  0.9 0.8 %broadcast_select_fusion = bf16[128,128]{1,0:T(8,128)(2,1)S(1)} fusion(bf16[128,128]{1,0:T(8,128)(2,1)} %param.9, bf16[128,128]{1,0:T(8,128)(2,1)} %param.10, pred[]{:T(512)} %bitcast.3), kind=kLoop, calls=%fused_computation.2 | loop fusion | flops 16384 | bytes 98305 | tf_op jit(solution)/shard_map/jit(_where)/select_n | solution.py:42
  1.6 0.1 pad_maximum_fusion
  1.7 0.8 %broadcast_in_dim.18 = bf16[8,144,128]{2,1,0:T(8,128)(2,1)} broadcast(bf16[144,128]{1,0:T(8,128)(2,1)S(1)} %pad_maximum_fusion), dimensions={1,2} | broadcast | bytes 331776 | tf_op jit(solution)/shard_map/broadcast_in_dim | solution.py:46
  2.5 7.3 %all-to-all-start = ((bf16[8,144,128]{2,1,0:T(8,128)(2,1)}), bf16[8,144,128]{2,1,0:T(8,128)(2,1)S(1)}, u32[]{:S(2)}, u32[]{:S(2)}) async-start(bf16[8,144,128]{2,1,0:T(8,128)(2,1)} %broadcast_in_dim.18), calls=%async_computation | async-start | bytes 589824 | tf_op jit(solution)/shard_map/all_to_all | solution.py:267
  9.9 1.4 %collective-permute-done.after_ref.qo_ref = bf16[128,256]{1,0:T(8,128)(2,1)S(1)} collective-permute-done((bf16[128,256]{1,0:T(8,128)(2,1)}, bf16[128,256]{1,0:T(8,128)(2,1)S(1)}, u32[]{:S(2)}, u32[]{:S(2)}) %collective-permute-start) | collective-permute-done | bytes 65568 | tf_op jit(solution)/shard_map/ppermute | solution.py:25
  11.2 6.0 %carve.1 = (bf16[256,4096]{1,0:T(8,128)(2,1)S(1)}, bf16[256,4096]{1,0:T(8,128)(2,1)S(1)}, bf16[256,4096]{1,0:T(8,128)(2,1)}, bf16[256,4096]{1,0:T(8,128)(2,1)}) custom-call(s32[4]{0:T(128)S(1)} %pad_add_fusion.block_ref, bf16[256,16384]{1,0:T(8,128)(2,1)} %w_ref.2, bf16[128,256]{1,0:T(8,128)(2,1)S(1)} %collective-permute-done.after_ref.qo_ref), custom_call_target="tpu_custom_call" | custom-call | bytes 16777216 | tf_op jit(solution)/shard_map/carve/pallas_call | solution.py:68
  17.2 1.3 %copy-done.3 = bf16[256,4096]{1,0:T(8,128)(2,1)} copy-done((bf16[256,4096]{1,0:T(8,128)(2,1)}, bf16[256,4096]{1,0:T(8,128)(2,1)S(1)}, u32[]{:S(2)}) %copy-start.3) | copy-done | bytes 2097176
  18.6 1.4 %copy-done.4 = bf16[256,4096]{1,0:T(8,128)(2,1)} copy-done((bf16[256,4096]{1,0:T(8,128)(2,1)}, bf16[256,4096]{1,0:T(8,128)(2,1)S(1)}, u32[]{:S(2)}) %copy-start.4) | copy-done | bytes 2097176
  20.0 0.2 collective-permute-start.2
  20.1 1.4 %collective-permute-done.2.there_ref = bf16[8,144,128]{2,1,0:T(8,128)(2,1)S(1)} collective-permute-done((bf16[8,144,128]{2,1,0:T(8,128)(2,1)S(1)}, bf16[8,144,128]{2,1,0:T(8,128)(2,1)S(1)}, u32[]{:S(2)}, u32[]{:S(2)}) %collective-permute-start.2) | collective-permute-done | bytes 294944 | tf_op jit(solution)/shard_map/ppermute | solution.py:25
  21.6 0.2 collective-permute-start.3
  21.7 0.4 collective-permute-start.1
  22.1 3.5 %collective-permute-done.1.go_ref = bf16[128,256]{1,0:T(8,128)(2,1)S(1)} collective-permute-done((bf16[128,256]{1,0:T(8,128)(2,1)S(1)}, bf16[128,256]{1,0:T(8,128)(2,1)S(1)}, u32[]{:S(2)}, u32[]{:S(2)}) %collective-permute-start.1) | collective-permute-done | bytes 65568 | tf_op jit(solution)/shard_map/ppermute | solution.py:25
  25.6 3.1 %attention.1 = (bf16[128,512]{1,0:T(8,128)(2,1)S(1)}, bf16[8,128,128]{2,1,0:T(8,128)(2,1)}) custom-call(s32[1]{0:T(128)} %bitcast.core_ref, f32[2,512]{1,0:T(2,128)S(1)} %bitcast.14, bf16[128,256]{1,0:T(8,128)(2,1)S(1)} %copy-done.5, bf16[128,256]{1,0:T(8,128)(2,1)S(1)} %collective-permute-done.after_ref.qo_ref, bf16[128,256]{1,0:T(8,128)(2,1)S(1)} %copy-done.6, ...), custom_call_target="tpu_custom_call" | custom-call | flops 671088640 | bytes 1048576 | tf_op jit(solution)/shard_map/attention/pallas_call | solution.py:155
  28.7 0.4 collective-permute-start.7
  29.1 0.2 product.4
  29.3 1.6 %collective-permute-start.4 = (bf16[128,256]{1,0:T(8,128)(2,1)S(1)}, bf16[128,256]{1,0:T(8,128)(2,1)S(1)}, u32[]{:S(2)}, u32[]{:S(2)}) collective-permute-start(bf16[128,256]{1,0:T(8,128)(2,1)S(1)} %product.4), channel_id=1, source_target_pairs={{0,2},{1,3},{2,0},{3,1},{4,6},{5,7},{6,4},{7,5},{8,10},{9,11},{10,... | collective-permute-start | bytes 196616 | tf_op jit(solution)/shard_map/ppermute | solution.py:25
  30.9 0.3 product.6
  31.2 0.6 product.5
  31.7 1.9 %collective-permute-done.4.refs_0_ = bf16[128,256]{1,0:T(8,128)(2,1)S(1)} collective-permute-done((bf16[128,256]{1,0:T(8,128)(2,1)S(1)}, bf16[128,256]{1,0:T(8,128)(2,1)S(1)}, u32[]{:S(2)}, u32[]{:S(2)}) %collective-permute-start.4) | collective-permute-done | bytes 65568 | tf_op jit(solution)/shard_map/ppermute | solution.py:25
  33.6 6.0 %all-to-all-start.1 = ((bf16[8,128,128]{2,1,0:T(8,128)(2,1)}), bf16[8,128,128]{2,1,0:T(8,128)(2,1)S(1)}, u32[]{:S(2)}, u32[]{:S(2)}) async-start(bf16[8,128,128]{2,1,0:T(8,128)(2,1)} %get-tuple-element.38), calls=%async_computation.1 | async-start | bytes 524288 | tf_op jit(solution)/shard_map/all_to_all | solution.py:289
  39.6 1.5 %collective-permute-start.8 = (bf16[128,2816]{1,0:T(8,128)(2,1)S(1)}, bf16[128,2816]{1,0:T(8,128)(2,1)S(1)}, u32[]{:S(2)}, u32[]{:S(2)}) collective-permute-start(bf16[128,2816]{1,0:T(8,128)(2,1)S(1)} %product.5), channel_id=1, source_target_pairs={{0,2},{1,3},{2,0},{3,1},{4,6},{5,7},{6,4},{7,5},{8,10},{9,11},{10,... | collective-permute-start | bytes 2162696 | tf_op jit(solution)/shard_map/ppermute | solution.py:25
  41.1 6.7 %all-to-all-done.1 = bf16[8,128,128]{2,1,0:T(8,128)(2,1)S(1)} async-done(((bf16[8,128,128]{2,1,0:T(8,128)(2,1)}), bf16[8,128,128]{2,1,0:T(8,128)(2,1)S(1)}, u32[]{:S(2)}, u32[]{:S(2)}) %all-to-all-start.1) | async-done | bytes 262176 | tf_op jit(solution)/shard_map/all_to_all | solution.py:289
  47.9 1.6 %collective-permute-start.5 = (bf16[128,128]{1,0:T(8,128)(2,1)S(1)}, bf16[128,128]{1,0:T(8,128)(2,1)S(1)}, u32[]{:S(2)}, u32[]{:S(2)}) collective-permute-start(bf16[128,128]{1,0:T(8,128)(2,1)S(1)} %reduce_sum.12), channel_id=1, source_target_pairs={{0,2},{1,3},{2,0},{3,1},{4,6},{5,7},{6,4},{7,5},{8,10},{9,11},{10,... | collective-permute-start | bytes 98312 | tf_op jit(solution)/shard_map/ppermute | solution.py:25
  49.5 0.5 collective-permute-start.9
  50.0 9.4 %collective-permute-done.5 = bf16[128,128]{1,0:T(8,128)(2,1)S(1)} collective-permute-done((bf16[128,128]{1,0:T(8,128)(2,1)S(1)}, bf16[128,128]{1,0:T(8,128)(2,1)S(1)}, u32[]{:S(2)}, u32[]{:S(2)}) %collective-permute-start.5) | collective-permute-done | bytes 32800 | tf_op jit(solution)/shard_map/ppermute | solution.py:25
  59.5 1.6 %copy-done.1 = bf16[256,4096]{1,0:T(8,128)(2,1)S(1)} copy-done((bf16[256,4096]{1,0:T(8,128)(2,1)S(1)}, bf16[256,4096]{1,0:T(8,128)(2,1)}, u32[]{:S(2)}) %copy-start.1) | copy-done | bytes 2097176
  61.1 2.5 %product.7.acc_ref = f32[128,4096]{1,0:T(8,128)S(1)} custom-call(bf16[128,512]{1,0:T(8,128)(2,1)S(1)} %get-tuple-element.35.dq_ref, bf16[256,4096]{1,0:T(8,128)(2,1)S(1)} %copy-done.1, bf16[256,4096]{1,0:T(8,128)(2,1)} %collective-permute-done.7.wo_ref), custom_call_target="tpu_custom_call" | custom-call | flops 536870912 | bytes 4194304 | tf_op jit(solution)/shard_map/product/pallas_call | solution.py:184
  63.6 1.5 %finish.1 = (bf16[128,4096]{1,0:T(8,128)(2,1)}, f32[128,1024]{1,0:T(8,128)S(1)}) custom-call(s32[1]{0:T(128)} %bitcast.core_ref, f32[128,128]{1,0:T(8,128)S(1)} %get-tuple-element.46.mine_ref, f32[128,128]{1,0:T(8,128)S(1)} %convert_element_type.31.other_ref, bf16[256,4096]{1,0:T(8,128)(2,1)S(1)} %copy-done.2, f32[128,4096]{1,0:T(8,128)S(1)} %product.7.acc_ref, ...), custom_call_target="tpu_custom_call" | custom-call | flops 268435456 | bytes 5242880 | tf_op jit(solution)/shard_map/finish/pallas_call | solution.py:220
  65.1 0.8 %last.1 = bf16[128,4096]{1,0:T(8,128)(2,1)} custom-call(f32[128,1024]{1,0:T(8,128)S(1)} %get-tuple-element.42.left_ref, bf16[128,1024]{1,0:T(8,128)(2,1)S(1)} %collective-permute-done.9.part_ref, bf16[128,4096]{1,0:T(8,128)(2,1)} %get-tuple-element.44.held_ref), custom_call_target="tpu_custom_call", output_to_operand_aliasing={{}: (2, {})} | custom-call | tf_op jit(solution)/shard_map/last/pallas_call | solution.py:249
  (32 shorter events, 0.3 us)
Async XLA Ops:
  2.5 17.5 %all-to-all-start = ((bf16[8,144,128]{2,1,0:T(8,128)(2,1)}), bf16[8,144,128]{2,1,0:T(8,128)(2,1)S(1)}, u32[]{:S(2)}, u32[]{:S(2)}) async-start(bf16[8,144,128]{2,1,0:T(8,128)(2,1)} %broadcast_in_dim.18), calls=%async_computation | async-start | bytes 589824 | tf_op jit(solution)/shard_map/all_to_all | solution.py:267
  9.7 1.5 %collective-permute-start = (bf16[128,256]{1,0:T(8,128)(2,1)}, bf16[128,256]{1,0:T(8,128)(2,1)S(1)}, u32[]{:S(2)}, u32[]{:S(2)}) collective-permute-start(bf16[128,256]{1,0:T(8,128)(2,1)} %qm_ref.1), channel_id=1, source_target_pairs={{0,1},{1,0},{2,3},{3,2},{4,5},{5,4},{6,7},{7,6},{8,9},{9,8},{10,11... | collective-permute-start | bytes 196616 | tf_op jit(solution)/shard_map/ppermute | solution.py:25
  9.8 11.9 %copy-start.6 = (bf16[128,256]{1,0:T(8,128)(2,1)S(1)}, bf16[128,256]{1,0:T(8,128)(2,1)}, u32[]{:S(2)}) copy-start(bf16[128,256]{1,0:T(8,128)(2,1)} %gm_ref.1) | copy-start | bytes 196612
  9.8 12.2 %copy-start.8 = (s32[128]{0:T(128)S(1)}, s32[128]{0:T(128)}, u32[]{:S(2)}) copy-start(s32[128]{0:T(128)} %param.13) | copy-start | bytes 1540
  9.8 12.2 %copy-start.7 = (s32[128]{0:T(128)S(1)}, s32[128]{0:T(128)}, u32[]{:S(2)}) copy-start(s32[128]{0:T(128)} %param.12) | copy-start | bytes 1540
  9.8 15.8 %copy-start.5 = (bf16[128,256]{1,0:T(8,128)(2,1)S(1)}, bf16[128,256]{1,0:T(8,128)(2,1)}, u32[]{:S(2)}) copy-start(bf16[128,256]{1,0:T(8,128)(2,1)} %qm_ref.1) | copy-start | bytes 196612
  17.2 1.3 %copy-start.3 = (bf16[256,4096]{1,0:T(8,128)(2,1)}, bf16[256,4096]{1,0:T(8,128)(2,1)S(1)}, u32[]{:S(2)}) copy-start(bf16[256,4096]{1,0:T(8,128)(2,1)S(1)} %get-tuple-element.41) | copy-start | bytes 6291460
  18.6 1.4 %copy-start.4 = (bf16[256,4096]{1,0:T(8,128)(2,1)}, bf16[256,4096]{1,0:T(8,128)(2,1)S(1)}, u32[]{:S(2)}) copy-start(bf16[256,4096]{1,0:T(8,128)(2,1)S(1)} %get-tuple-element.37) | copy-start | bytes 6291460
  20.0 9.1 %copy-start = (bf16[256,4096]{1,0:T(8,128)(2,1)S(1)}, bf16[256,4096]{1,0:T(8,128)(2,1)}, u32[]{:S(2)}) copy-start(bf16[256,4096]{1,0:T(8,128)(2,1)} %get-tuple-element.36.wm_ref) | copy-start | bytes 6291460
  20.0 1.6 %collective-permute-start.2 = (bf16[8,144,128]{2,1,0:T(8,128)(2,1)S(1)}, bf16[8,144,128]{2,1,0:T(8,128)(2,1)S(1)}, u32[]{:S(2)}, u32[]{:S(2)}) collective-permute-start(bf16[8,144,128]{2,1,0:T(8,128)(2,1)S(1)} %all-to-all-done.here_ref), channel_id=1, source_target_pairs={{0,1},{1,0},{2,3},{3,2},{4,5},{5,4},{6,7},{7,6},{8,9},{9,8},{10,11... | collective-permute-start | bytes 884744 | tf_op jit(solution)/shard_map/ppermute | solution.py:25
  21.6 7.5 %collective-permute-start.3 = (bf16[256,4096]{1,0:T(8,128)(2,1)}, bf16[256,4096]{1,0:T(8,128)(2,1)S(1)}, u32[]{:S(2)}, u32[]{:S(2)}) collective-permute-start(bf16[256,4096]{1,0:T(8,128)(2,1)} %copy-done.4), channel_id=1, source_target_pairs={{0,1},{1,0},{2,3},{3,2},{4,5},{5,4},{6,7},{7,6},{8,9},{9,8},{10,11... | collective-permute-start | bytes 6291464 | tf_op jit(solution)/shard_map/ppermute | solution.py:25
  21.7 3.9 %collective-permute-start.1 = (bf16[128,256]{1,0:T(8,128)(2,1)S(1)}, bf16[128,256]{1,0:T(8,128)(2,1)S(1)}, u32[]{:S(2)}, u32[]{:S(2)}) collective-permute-start(bf16[128,256]{1,0:T(8,128)(2,1)S(1)} %copy-done.6), channel_id=1, source_target_pairs={{0,1},{1,0},{2,3},{3,2},{4,5},{5,4},{6,7},{7,6},{8,9},{9,8},{10,11... | collective-permute-start | bytes 196616 | tf_op jit(solution)/shard_map/ppermute | solution.py:25
  28.7 30.8 %collective-permute-start.7 = (bf16[256,4096]{1,0:T(8,128)(2,1)}, bf16[256,4096]{1,0:T(8,128)(2,1)}, u32[]{:S(2)}, u32[]{:S(2)}) collective-permute-start(bf16[256,4096]{1,0:T(8,128)(2,1)} %copy-done.3), channel_id=1, source_target_pairs={{0,1},{1,0},{2,3},{3,2},{4,5},{5,4},{6,7},{7,6},{8,9},{9,8},{10,11... | collective-permute-start | bytes 6291464 | tf_op jit(solution)/shard_map/ppermute | solution.py:25
  29.3 4.3 %collective-permute-start.4 = (bf16[128,256]{1,0:T(8,128)(2,1)S(1)}, bf16[128,256]{1,0:T(8,128)(2,1)S(1)}, u32[]{:S(2)}, u32[]{:S(2)}) collective-permute-start(bf16[128,256]{1,0:T(8,128)(2,1)S(1)} %product.4), channel_id=1, source_target_pairs={{0,2},{1,3},{2,0},{3,1},{4,6},{5,7},{6,4},{7,5},{8,10},{9,11},{10,... | collective-permute-start | bytes 196616 | tf_op jit(solution)/shard_map/ppermute | solution.py:25
  33.6 14.2 %all-to-all-start.1 = ((bf16[8,128,128]{2,1,0:T(8,128)(2,1)}), bf16[8,128,128]{2,1,0:T(8,128)(2,1)S(1)}, u32[]{:S(2)}, u32[]{:S(2)}) async-start(bf16[8,128,128]{2,1,0:T(8,128)(2,1)} %get-tuple-element.38), calls=%async_computation.1 | async-start | bytes 524288 | tf_op jit(solution)/shard_map/all_to_all | solution.py:289
  39.6 24.0 %collective-permute-start.8 = (bf16[128,2816]{1,0:T(8,128)(2,1)S(1)}, bf16[128,2816]{1,0:T(8,128)(2,1)S(1)}, u32[]{:S(2)}, u32[]{:S(2)}) collective-permute-start(bf16[128,2816]{1,0:T(8,128)(2,1)S(1)} %product.5), channel_id=1, source_target_pairs={{0,2},{1,3},{2,0},{3,1},{4,6},{5,7},{6,4},{7,5},{8,10},{9,11},{10,... | collective-permute-start | bytes 2162696 | tf_op jit(solution)/shard_map/ppermute | solution.py:25
  47.9 11.5 %collective-permute-start.5 = (bf16[128,128]{1,0:T(8,128)(2,1)S(1)}, bf16[128,128]{1,0:T(8,128)(2,1)S(1)}, u32[]{:S(2)}, u32[]{:S(2)}) collective-permute-start(bf16[128,128]{1,0:T(8,128)(2,1)S(1)} %reduce_sum.12), channel_id=1, source_target_pairs={{0,2},{1,3},{2,0},{3,1},{4,6},{5,7},{6,4},{7,5},{8,10},{9,11},{10,... | collective-permute-start | bytes 98312 | tf_op jit(solution)/shard_map/ppermute | solution.py:25
  49.5 15.6 %collective-permute-start.9 = (bf16[128,1024]{1,0:T(8,128)(2,1)S(1)}, bf16[128,1024]{1,0:T(8,128)(2,1)S(1)}, u32[]{:S(2)}, u32[]{:S(2)}) collective-permute-start(bf16[128,1024]{1,0:T(8,128)(2,1)S(1)} %product.6), channel_id=1, source_target_pairs={{0,2},{1,3},{2,0},{3,1},{4,6},{5,7},{6,4},{7,5},{8,10},{9,11},{10,... | collective-permute-start | bytes 786440 | tf_op jit(solution)/shard_map/ppermute | solution.py:25
  59.4 4.2 %collective-permute-start.6 = (bf16[128,128]{1,0:T(8,128)(2,1)S(1)}, bf16[128,128]{1,0:T(8,128)(2,1)S(1)}, u32[]{:S(2)}, u32[]{:S(2)}) collective-permute-start(bf16[128,128]{1,0:T(8,128)(2,1)S(1)} %get-tuple-element.45), channel_id=1, source_target_pairs={{0,1},{1,0},{2,3},{3,2},{4,5},{5,4},{6,7},{7,6},{8,9},{9,8},{10,11... | collective-permute-start | bytes 98312 | tf_op jit(solution)/shard_map/ppermute | solution.py:25
  59.5 1.6 %copy-start.1 = (bf16[256,4096]{1,0:T(8,128)(2,1)S(1)}, bf16[256,4096]{1,0:T(8,128)(2,1)}, u32[]{:S(2)}) copy-start(bf16[256,4096]{1,0:T(8,128)(2,1)} %get-tuple-element.40.wm_ref) | copy-start | bytes 6291460
  61.1 2.5 %copy-start.2 = (bf16[256,4096]{1,0:T(8,128)(2,1)S(1)}, bf16[256,4096]{1,0:T(8,128)(2,1)}, u32[]{:S(2)}) copy-start(bf16[256,4096]{1,0:T(8,128)(2,1)} %w_ref.3) | copy-start | bytes 6291460

commit v6 on v4

--- a/solution.py
+++ b/solution.py
@@ -10,7 +10,7 @@
 
 RUN = 64
 META_ROWS = 16
-CHUNKS = (2, 7, 7)
+CHUNKS = (2, 3, 3, 3, 3, 2)
 ANY = pl.BlockSpec(memory_space=pl.ANY)
 HBM = pl.BlockSpec(memory_space=pltpu.HBM)
 SMEM = pl.BlockSpec(memory_space=pltpu.SMEM)
@@ -37,17 +37,33 @@
     return state
 
 
-def pack(count, core, positions, keys, values):
+def pack(core, positions, keys, values):
     rows, size = keys.shape
     held = jnp.where(core == 0, keys, values)
     runs = (positions.reshape(rows // RUN, RUN)[:, :1] // RUN).astype(jnp.bfloat16)
     meta = jnp.pad(jnp.broadcast_to(runs, (rows // RUN, size)), ((0, META_ROWS - rows // RUN), (0, 0)))
-    piece = jnp.concatenate([held, meta], axis=0)
-    return jnp.broadcast_to(piece, (count,) + piece.shape)
-
-
-def carve_kernel(block_ref, w_ref, after_ref, *refs):
-    outs, sems = refs[:-1], refs[-1]
+    return jnp.concatenate([held, meta], axis=0)
+
+
+def gate_kernel(value_ref, *refs):
+    pass
+
+
+def gate(value, *after):
+    return pl.pallas_call(
+        gate_kernel,
+        out_shape=jax.ShapeDtypeStruct(value.shape, value.dtype),
+        in_specs=[ANY] * (1 + len(after)),
+        out_specs=ANY,
+        input_output_aliases={0: 0},
+        compiler_params=params(),
+        cost_estimate=pl.CostEstimate(flops=10**11, bytes_accessed=10**8, transcendentals=0),
+        name="gate",
+    )(value, *after)
+
+
+def carve_kernel(block_ref, w_ref, *refs):
+    outs, sems = refs[1:-1], refs[-1]
     rows, share = outs[0].shape
     parts = sems.shape[1]
     copies = []
@@ -62,12 +78,12 @@
         one.wait()
 
 
-def carve(blocks, w_query, after, share):
-    shape = jax.ShapeDtypeStruct((w_query.shape[0], share), w_query.dtype)
+def carve(blocks, w_query, share, after):
+    block = jax.ShapeDtypeStruct((w_query.shape[0], share), w_query.dtype)
     count = len(blocks)
     return pl.pallas_call(
         carve_kernel,
-        out_shape=[shape] * count,
+        out_shape=[block] * count,
         in_specs=[SMEM, HBM, ANY],
         out_specs=[pl.BlockSpec(memory_space=pltpu.VMEM)] * count,
         scratch_shapes=[pltpu.SemaphoreType.DMA((count, 4))],
@@ -79,87 +95,84 @@
     )(jnp.stack(blocks), w_query, after)
 
 
-def attention_kernel(
-    core_ref, row_ref, qm_ref, qo_ref, gm_ref, go_ref, here_ref, there_ref, dq_ref, back_ref, s_ref, dp_ref
-):
-    count = here_ref.shape[0]
-    rows, width = qm_ref.shape
-    size = here_ref.shape[2]
+def attention_kernel(core_ref, row_ref, query_ref, grad_ref, *refs):
+    groups = ((refs[0], refs[1], refs[5]), (refs[2], refs[3], refs[6]))
+    dq_ref = refs[4]
+    s_ref, dp_ref = refs[7:]
+    half, rows, size = groups[0][2].shape
     is_key = core_ref[0] == 0
-    heads = width // size
     inv_root = 1.0 / math.sqrt(size)
-
-    def stack(mine_ref, other_ref):
-        parts = [ref[:, h * size : (h + 1) * size] for ref in (mine_ref, other_ref) for h in range(heads)]
-        return jnp.concatenate(parts, axis=0)
-
-    query = stack(qm_ref, qo_ref)
-    grad = stack(gm_ref, go_ref)
+    query = query_ref[...]
+    grad = grad_ref[...]
     wide = query.shape[0]
     last = row_ref[0:1, :]
     first = row_ref[1:2, :]
     offset = lax.broadcasted_iota(jnp.int32, (RUN, wide), 0).astype(jnp.float32)
 
-    def scores(s, top):
+    def everywhere(body, state):
+        for group, (here_ref, there_ref, back_ref) in enumerate(groups):
+            state = each(
+                half, lambda s, now: body(s, group * half + s, here_ref, there_ref, back_ref, now), state
+            )
+        return state
+
+    def scores(s, slot, here_ref, there_ref, back_ref, top):
         here = here_ref[s, 0:rows, :]
         there = there_ref[s, 0:rows, :]
         key = jnp.where(is_key, here, there)
         value = jnp.where(is_key, there, here)
         score = dot(key, query, ((1,), (1,))) * inv_root
-        dp_ref[s] = dot(value, grad, ((1,), (1,)))
+        dp_ref[slot] = dot(value, grad, ((1,), (1,)))
         meta = here_ref[s, rows : rows + META_ROWS, :].astype(jnp.float32)
         for run in range(rows // RUN):
             start = meta[run : run + 1, 0:1] * float(RUN)
             pos = offset + start
             allowed = (pos <= last) & (pos >= first)
             part = jnp.where(allowed, score[run * RUN : (run + 1) * RUN], -1e30)
-            s_ref[s, run * RUN : (run + 1) * RUN, :] = part
+            s_ref[slot, run * RUN : (run + 1) * RUN, :] = part
             top = jnp.maximum(top, jnp.max(part, axis=0, keepdims=True))
         return top
 
-    top = each(count, scores, jnp.full((1, wide), -1e30, jnp.float32))
-
-    def weights(s, state):
+    top = everywhere(scores, jnp.full((1, wide), -1e30, jnp.float32))
+
+    def weights(slot, state):
         total, mixed = state
-        weight = jnp.exp(s_ref[s] - top)
-        s_ref[s] = weight
+        weight = jnp.exp(s_ref[slot] - top)
+        s_ref[slot] = weight
         total = total + jnp.sum(weight, axis=0, keepdims=True)
-        mixed = mixed + jnp.sum(weight * dp_ref[s], axis=0, keepdims=True)
+        mixed = mixed + jnp.sum(weight * dp_ref[slot], axis=0, keepdims=True)
         return total, mixed
 
     zeros = jnp.zeros((1, wide), jnp.float32)
-    total, mixed = each(count, weights, (zeros, zeros))
+    total, mixed = each(2 * half, weights, (zeros, zeros))
     scale = 1.0 / total
     delta = mixed * scale
-
     other = jnp.where(is_key, query, grad)
 
-    def gradients(s, dq):
-        prob = s_ref[s] * scale
-        dscore = (prob * (dp_ref[s] - delta)).astype(jnp.bfloat16)
+    def gradients(s, slot, here_ref, there_ref, back_ref, dq):
+        prob = s_ref[slot] * scale
+        dscore = (prob * (dp_ref[slot] - delta)).astype(jnp.bfloat16)
         picked = jnp.where(is_key, dscore, prob.astype(jnp.bfloat16))
         back_ref[s] = dot(picked, other, ((1,), (0,))).astype(jnp.bfloat16)
         key = jnp.where(is_key, here_ref[s, 0:rows, :], there_ref[s, 0:rows, :])
         return dq + dot(key, dscore, ((0,), (0,)))
 
-    dq = each(count, gradients, jnp.zeros((size, wide), jnp.float32)) * inv_root
+    dq = everywhere(gradients, jnp.zeros((size, wide), jnp.float32)) * inv_root
     for part in range(wide // rows):
         block = dq[:, part * rows : (part + 1) * rows]
         dq_ref[:, part * size : (part + 1) * size] = block.T.astype(jnp.bfloat16)
 
 
-def attention(core, row_info, q_mine, q_other, g_mine, g_other, here, there):
-    count, _, size = here.shape
-    rows, width = q_mine.shape
-    wide = 2 * rows * (width // size)
+def attention(core, row_info, query, grad, pieces, rows):
+    half, _, size = pieces[0].shape
+    wide = query.shape[0]
+    count = 2 * half
     return pl.pallas_call(
         attention_kernel,
-        out_shape=[
-            jax.ShapeDtypeStruct((rows, 2 * width), jnp.bfloat16),
-            jax.ShapeDtypeStruct((count, rows, size), jnp.bfloat16),
-        ],
+        out_shape=[jax.ShapeDtypeStruct((rows, wide // rows * size), jnp.bfloat16)]
+        + [jax.ShapeDtypeStruct((half, rows, size), jnp.bfloat16)] * 2,
         in_specs=[SMEM] + [pl.BlockSpec()] * 7,
-        out_specs=[pl.BlockSpec()] * 2,
+        out_specs=[pl.BlockSpec()] * 3,
         scratch_shapes=[pltpu.VMEM((count, rows, wide), jnp.float32)] * 2,
         compiler_params=params(8 + count * rows * wide // 2**17),
         cost_estimate=pl.CostEstimate(
@@ -168,7 +181,7 @@
             transcendentals=count * rows * wide,
         ),
         name="attention",
-    )(core, row_info, q_mine, q_other, g_mine, g_other, here, there)
+    )(core, row_info, query, grad, *pieces)
 
 
 def product_kernel(first, dq_ref, wm_ref, wo_ref, out_ref):
@@ -259,23 +272,36 @@
 
 
 def on_device(queries, keys, values, dout, positions, doc_ids, w_query, w_kv):
-    count = lax.axis_size("ctx")
+    half = lax.axis_size("ctx") // 2
     head = lax.axis_index("head").astype(jnp.int32)
     core = (head & 1).reshape(1)
     share = w_kv.shape[1]
-
-    here = lax.all_to_all(pack(count, core, positions, keys, values), "ctx", 0, 0)
-    there = swapped(here, "head", 1)
+    local_heads = queries.shape[1] // keys.shape[1]
+
+    piece = pack(core, positions, keys, values)
+    here_z = jnp.stack([piece] + [swapped(piece, "ctx", 2 * s) for s in range(1, half)])
     q_other = swapped(queries, "head", 1)
     g_other = swapped(dout, "head", 1)
-
-    send = carve([head ^ 3, head ^ 1], w_query, positions, share)
-    far_other, near_other = [swapped(part, "head", 1) for part in send]
-    far_mine, near_mine = carve([head ^ 2, head], w_query, g_other, share)
-
+    q_other = gate(q_other, g_other)
+    far_send, far_mine = carve([head ^ 3, head ^ 2], w_query, share, q_other)
+    far_other = swapped(far_send, "head", 1)
+
+    def stacked(*arrays):
+        return jnp.concatenate([part for one in arrays for part in jnp.split(one, local_heads, axis=1)], axis=0)
+
+    query = stacked(queries, q_other)
+    grad = stacked(dout, g_other)
     bounds = jnp.stack([positions, doc_ids * RUN]).astype(jnp.float32)
-    row_info = jnp.tile(bounds, (1, 2 * (queries.shape[1] // keys.shape[1])))
-    dq, back = attention(core, row_info, queries, q_other, dout, g_other, here, there)
+    row_info = jnp.tile(bounds, (1, 2 * local_heads))
+    here_z, far_mine, query, grad, row_info = lax.optimization_barrier(
+        (here_z, far_mine, query, grad, row_info)
+    )
+    here_x = swapped(here_z, "ctx", 1)
+    there_z = swapped(here_z, "head", 1)
+    there_x = swapped(here_x, "head", 1)
+    dq, back_z, back_x = attention(
+        core, row_info, query, grad, (here_z, there_z, here_x, there_x), queries.shape[0]
+    )
 
     starts = [0]
     for units in CHUNKS:
@@ -283,15 +309,25 @@
     parts = [
         product(dq, far_mine, far_other, low, high - low, jnp.bfloat16) for low, high in zip(starts, starts[1:])
     ]
-    received = [swapped(part, "head", 2) for part in parts]
-
-    back, *_ = lax.optimization_barrier([back, received[0]] + parts)
-    back = lax.all_to_all(back, "ctx", 0, 0)
-    mine = jnp.sum(back.astype(jnp.float32), axis=0).astype(jnp.bfloat16)
+    received = []
+    for c, part in enumerate(parts):
+        if c >= 2:
+            part, received[c - 2] = lax.optimization_barrier((part, received[c - 2]))
+        received.append(swapped(part, "head", 2))
+
+    back_x, back_z, *_ = lax.optimization_barrier((back_x, back_z, *parts[:2]))
+    pair = back_z.astype(jnp.float32) + swapped(back_x, "ctx", 1).astype(jnp.float32)
+    mine = pair[0]
+    for s in range(1, half):
+        mine = mine + swapped(pair[s].astype(jnp.bfloat16), "ctx", 2 * s).astype(jnp.float32)
+    mine = mine.astype(jnp.bfloat16)
+
+    near_send, near_mine = carve([head ^ 1, head], w_query, share, received[0])
+    acc = product(dq, near_mine, swapped(near_send, "head", 1), 0, share, jnp.float32)
+    mine, acc = lax.optimization_barrier((mine, acc))
     mine = mine.astype(jnp.float32) + swapped(mine, "head", 2).astype(jnp.float32)
     other = swapped(mine.astype(jnp.bfloat16), "head", 1).astype(jnp.float32)
 
-    acc = product(dq, near_mine, near_other, 0, share, jnp.float32)
     held, left = finish(core, mine, other, w_kv, acc, received[:-1], starts)
     return last(left, received[-1], held)
 

time: 69.5 us -> 64.5 us (0.928)
  waiting for transfers between devices: 31.6 us -> 23.7 us
  starting transfers between devices: 17.3 us -> 22.9 us
  Pallas kernels: 16.4 us -> 12.5 us
  other arithmetic: 0.45 us -> 1.28 us
    ppermute x10 -> x22, starting transfers between devices: 6.43 us -> 22.9 us  [swapped(): lax.ppermute(value, axis, [(source, source ^ bits) for source in range(co...]
    all_to_all x2 -> x0, waiting for transfers between devices: 16 us -> none  [the longest x1 9.21 us: on_device(): lax.all_to_all(pack(count, core, positions, keys, values), 'ctx', 0, 0)]
    all_to_all x2 -> x0, starting transfers between devices: 10.9 us -> none  [the longest x1 7.23 us: on_device(): lax.all_to_all(pack(count, core, positions, keys, values), 'ctx', 0, 0)]
    ppermute x10 -> x22, waiting for transfers between devices: 15.6 us -> 23.7 us  [swapped(): lax.ppermute(value, axis, [(source, source ^ bits) for source in range(co...]
    pallas_call x3 -> x4, Pallas kernels: 10.6 us -> 8.01 us  [the longest x2 5.52 us: carve(): pl.pallas_call(carve_kernel, out_shape=[block] * count, in_specs=[SMEM, H...]
    pallas_call x4 -> x7, Pallas kernels: 3.52 us -> 2.28 us  [product(): pl.pallas_call(functools.partial(product_kernel, first), out_shape=jax.Sh...]
    select_n x1, other arithmetic: 0.01 us -> 0.77 us  [pack(): held = jnp.where(core == 0, keys, values)]
    broadcast_in_dim x1 -> x0, local copies, waits for them, and re-layouts: 0.75 us -> none  [pack(): return jnp.broadcast_to(piece, (count,) + piece.shape)]
  transfers between devices with their start and end apart: 12 -> 22, of which waited for: 4 -> 12; matrix products, arithmetic and copies ran while one was open for 2% -> 3% of each run, Pallas kernels for 15% -> 9%
where the time goes in v6:
time: 64.5 us; the launch traced here: 64.3 us
  waiting for transfers between devices  23.7 us (37%)
  starting transfers between devices  22.9 us (36%)
  Pallas kernels  12.5 us (19%)
  local copies, waits for them, and re-layouts  3.52 us (5%)
  other arithmetic  1.28 us (2%)
    ppermute x22, waiting for transfers between devices, swapped(): lax.ppermute(value, axis, [(source, source ^ bits) for source in range(co...  23.7 us
    ppermute x22, starting transfers between devices, swapped(): lax.ppermute(value, axis, [(source, source ^ bits) for source in range(co...  22.9 us
    pallas_call x2, Pallas kernels, carve(): pl.pallas_call(carve_kernel, out_shape=[block] * count, in_specs=[SMEM, H...  5.52 us
    unnamed x18, local copies, waits for them, and re-layouts  2.74 us
    pallas_call x1, Pallas kernels, attention(): pl.pallas_call(attention_kernel, out_shape=[jax.ShapeDtypeStruct((rows, w...  2.49 us
    pallas_call x7, Pallas kernels, product(): pl.pallas_call(functools.partial(product_kernel, first), out_shape=jax.Sh...  2.28 us
    pallas_call x1, Pallas kernels, finish(): pl.pallas_call(functools.partial(finish_kernel, starts), out_shape=[jax.S...  1.56 us
  transfers between devices with their start and end apart: 22, of which 12 were waited for; matrix products, arithmetic and copies ran while one was open for 3% of the time, Pallas kernels for 9%

profile of v6, /device:TPU:0, one launch (start us, length us, event | category | flops | bytes accessed | tf_op | source)
XLA Modules:
  0.0 64.3 jit_solution(8959808892026056038)
XLA Ops:
  0.5 0.7 %reshape.31 = s32[2,64]{1,0:T(2,128)S(1)} reshape(s32[128]{0:T(128)} %param.12) | data formatting | bytes 1024 | tf_op jit(solution)/shard_map/reshape | solution.py:43
  1.4 0.8 %broadcast_select_fusion = bf16[128,128]{1,0:T(8,128)(2,1)S(1)} fusion(bf16[128,128]{1,0:T(8,128)(2,1)} %param.9, bf16[128,128]{1,0:T(8,128)(2,1)} %param.10, pred[]{:T(512)} %bitcast.1), kind=kLoop, calls=%fused_computation.14 | loop fusion | flops 16384 | bytes 98305 | tf_op jit(solution)/shard_map/jit(_where)/select_n | solution.py:42
  2.3 2.8 %carve.2 = (bf16[256,4096]{1,0:T(8,128)(2,1)S(1)}, bf16[256,4096]{1,0:T(8,128)(2,1)S(1)}) custom-call(s32[2]{0:T(128)S(1)} %pad_add_fusion.block_ref, bf16[256,16384]{1,0:T(8,128)(2,1)} %w_ref.4, bf16[128,256]{1,0:T(8,128)(2,1)S(1)} %gate.1.refs_0_), custom_call_target="tpu_custom_call" | custom-call | bytes 8388608 | tf_op jit(solution)/shard_map/carve/pallas_call | solution.py:84
  5.7 3.7 %collective-permute-start.1 = (bf16[144,128]{1,0:T(8,128)(2,1)S(1)}, bf16[144,128]{1,0:T(8,128)(2,1)S(1)}, u32[]{:S(2)}, u32[]{:S(2)}) collective-permute-start(bf16[144,128]{1,0:T(8,128)(2,1)S(1)} %get-tuple-element.73), channel_id=1, source_target_pairs={{0,16},{4,20},{8,24},{12,28},{16,0},{20,4},{24,8},{28,12},{1,17},{... | collective-permute-start | bytes 110600 | tf_op jit(solution)/shard_map/ppermute | solution.py:25
  9.3 1.6 %collective-permute-start = (bf16[144,128]{1,0:T(8,128)(2,1)S(1)}, bf16[144,128]{1,0:T(8,128)(2,1)S(1)}, u32[]{:S(2)}, u32[]{:S(2)}) collective-permute-start(bf16[144,128]{1,0:T(8,128)(2,1)S(1)} %get-tuple-element.73), channel_id=1, source_target_pairs={{0,8},{4,12},{8,0},{12,4},{16,24},{20,28},{24,16},{28,20},{1,9},{5... | collective-permute-start | bytes 110600 | tf_op jit(solution)/shard_map/ppermute | solution.py:25
  11.5 1.8 %collective-permute-done = bf16[144,128]{1,0:T(8,128)(2,1)S(1)} collective-permute-done((bf16[144,128]{1,0:T(8,128)(2,1)S(1)}, bf16[144,128]{1,0:T(8,128)(2,1)S(1)}, u32[]{:S(2)}, u32[]{:S(2)}) %collective-permute-start) | collective-permute-done | bytes 36896 | tf_op jit(solution)/shard_map/ppermute | solution.py:25
  13.3 3.4 %collective-permute-done.2 = bf16[144,128]{1,0:T(8,128)(2,1)S(1)} collective-permute-done((bf16[144,128]{1,0:T(8,128)(2,1)S(1)}, bf16[144,128]{1,0:T(8,128)(2,1)S(1)}, u32[]{:S(2)}, u32[]{:S(2)}) %collective-permute-start.2) | collective-permute-done | bytes 36896 | tf_op jit(solution)/shard_map/ppermute | solution.py:25
  16.7 1.6 %collective-permute-start.6 = (bf16[4,144,128]{2,1,0:T(8,128)(2,1)S(1)}, bf16[4,144,128]{2,1,0:T(8,128)(2,1)S(1)}, u32[]{:S(2)}, u32[]{:S(2)}) collective-permute-start(bf16[4,144,128]{2,1,0:T(8,128)(2,1)S(1)} %pad_maximum_fusion.refs_0_), channel_id=1, source_target_pairs={{0,4},{4,0},{8,12},{12,8},{16,20},{20,16},{24,28},{28,24},{1,5},{5... | collective-permute-start | bytes 442376 | tf_op jit(solution)/shard_map/ppermute | solution.py:25
  18.3 3.6 %collective-permute-done.6.refs_2_ = bf16[4,144,128]{2,1,0:T(8,128)(2,1)S(1)} collective-permute-done((bf16[4,144,128]{2,1,0:T(8,128)(2,1)S(1)}, bf16[4,144,128]{2,1,0:T(8,128)(2,1)S(1)}, u32[]{:S(2)}, u32[]{:S(2)}) %collective-permute-start.6) | collective-permute-done | bytes 147488 | tf_op jit(solution)/shard_map/ppermute | solution.py:25
  22.0 1.4 %collective-permute-done.7.refs_3_ = bf16[4,144,128]{2,1,0:T(8,128)(2,1)S(1)} collective-permute-done((bf16[4,144,128]{2,1,0:T(8,128)(2,1)S(1)}, bf16[4,144,128]{2,1,0:T(8,128)(2,1)S(1)}, u32[]{:S(2)}, u32[]{:S(2)}) %collective-permute-start.7) | collective-permute-done | bytes 147488 | tf_op jit(solution)/shard_map/ppermute | solution.py:25
  23.3 2.5 %attention.1 = (bf16[128,512]{1,0:T(8,128)(2,1)S(1)}, bf16[4,128,128]{2,1,0:T(8,128)(2,1)S(1)}, bf16[4,128,128]{2,1,0:T(8,128)(2,1)S(1)}) custom-call(s32[1]{0:T(128)} %bitcast.core_ref, f32[2,512]{1,0:T(2,128)S(1)} %bitcast.35, bf16[512,128]{1,0:T(8,128)(2,1)S(1)} %get-tuple-element.33.query_ref, bf16[512,128]{1,0:T(8,128)(2,1)S(1)} %get-tuple-element.34.grad_ref, ...), custom_call_target="tpu_custom_call" | custom-call | flops 671088640 | bytes 1048576 | tf_op jit(solution)/shard_map/attention/pallas_call | solution.py:170
  26.1 1.1 %copy-done = bf16[256,4096]{1,0:T(8,128)(2,1)} copy-done((bf16[256,4096]{1,0:T(8,128)(2,1)}, bf16[256,4096]{1,0:T(8,128)(2,1)S(1)}, u32[]{:S(2)}) %copy-start) | copy-done | bytes 2097176
  27.2 1.5 %collective-permute-start.13 = (bf16[128,512]{1,0:T(8,128)(2,1)S(1)}, bf16[128,512]{1,0:T(8,128)(2,1)S(1)}, u32[]{:S(2)}, u32[]{:S(2)}) collective-permute-start(bf16[128,512]{1,0:T(8,128)(2,1)S(1)} %product.7), channel_id=1, source_target_pairs={{0,2},{1,3},{2,0},{3,1},{4,6},{5,7},{6,4},{7,5},{8,10},{9,11},{10,... | collective-permute-start | bytes 393224 | tf_op jit(solution)/shard_map/ppermute | solution.py:25
  28.8 1.6 %copy-done.1 = bf16[256,4096]{1,0:T(8,128)(2,1)S(1)} copy-done((bf16[256,4096]{1,0:T(8,128)(2,1)S(1)}, bf16[256,4096]{1,0:T(8,128)(2,1)}, u32[]{:S(2)}) %copy-start.1) | copy-done | bytes 2097176
  30.7 2.1 %collective-permute-done.13.refs_0_ = bf16[128,512]{1,0:T(8,128)(2,1)S(1)} collective-permute-done((bf16[128,512]{1,0:T(8,128)(2,1)S(1)}, bf16[128,512]{1,0:T(8,128)(2,1)S(1)}, u32[]{:S(2)}, u32[]{:S(2)}) %collective-permute-start.13) | collective-permute-done | bytes 131104 | tf_op jit(solution)/shard_map/ppermute | solution.py:25
  32.7 2.8 %carve.3 = (bf16[256,4096]{1,0:T(8,128)(2,1)S(1)}, bf16[256,4096]{1,0:T(8,128)(2,1)S(1)}) custom-call(s32[2]{0:T(128)S(1)} %pad_add_fusion.1.block_ref, bf16[256,16384]{1,0:T(8,128)(2,1)} %w_ref.4, bf16[128,512]{1,0:T(8,128)(2,1)S(1)} %collective-permute-done.13.refs_0_), custom_call_target="tpu_custom_call" | custom-call | bytes 8388608 | tf_op jit(solution)/shard_map/carve/pallas_call | solution.py:84
  35.9 1.6 %collective-permute-start.9 = (bf16[4,128,128]{2,1,0:T(8,128)(2,1)S(1)}, bf16[4,128,128]{2,1,0:T(8,128)(2,1)S(1)}, u32[]{:S(2)}, u32[]{:S(2)}) collective-permute-start(bf16[4,128,128]{2,1,0:T(8,128)(2,1)S(1)} %get-tuple-element.42), channel_id=1, source_target_pairs={{0,4},{4,0},{8,12},{12,8},{16,20},{20,16},{24,28},{28,24},{1,5},{5... | collective-permute-start | bytes 393224 | tf_op jit(solution)/shard_map/ppermute | solution.py:25
  37.4 1.5 %collective-permute-start.17 = (bf16[128,768]{1,0:T(8,128)(2,1)S(1)}, bf16[128,768]{1,0:T(8,128)(2,1)S(1)}, u32[]{:S(2)}, u32[]{:S(2)}) collective-permute-start(bf16[128,768]{1,0:T(8,128)(2,1)S(1)} %product.8), channel_id=1, source_target_pairs={{0,2},{1,3},{2,0},{3,1},{4,6},{5,7},{6,4},{7,5},{8,10},{9,11},{10,... | collective-permute-start | bytes 589832 | tf_op jit(solution)/shard_map/ppermute | solution.py:25
  39.0 2.9 %collective-permute-done.9 = bf16[4,128,128]{2,1,0:T(8,128)(2,1)S(1)} collective-permute-done((bf16[4,128,128]{2,1,0:T(8,128)(2,1)S(1)}, bf16[4,128,128]{2,1,0:T(8,128)(2,1)S(1)}, u32[]{:S(2)}, u32[]{:S(2)}) %collective-permute-start.9) | collective-permute-done | bytes 131104 | tf_op jit(solution)/shard_map/ppermute | solution.py:25
  42.0 1.9 %collective-permute-start.12 = (bf16[128,128]{1,0:T(8,128)(2,1)S(1)}, bf16[128,128]{1,0:T(8,128)(2,1)S(1)}, u32[]{:S(2)}, u32[]{:S(2)}) collective-permute-start(bf16[128,128]{1,0:T(8,128)(2,1)S(1)} %get-tuple-element.60), channel_id=1, source_target_pairs={{0,24},{4,28},{8,16},{12,20},{16,8},{20,12},{24,0},{28,4},{1,25},{... | collective-permute-start | bytes 98312 | tf_op jit(solution)/shard_map/ppermute | solution.py:25
  43.9 1.6 %collective-permute-start.11 = (bf16[128,128]{1,0:T(8,128)(2,1)S(1)}, bf16[128,128]{1,0:T(8,128)(2,1)S(1)}, u32[]{:S(2)}, u32[]{:S(2)}) collective-permute-start(bf16[128,128]{1,0:T(8,128)(2,1)S(1)} %get-tuple-element.61), channel_id=1, source_target_pairs={{0,16},{4,20},{8,24},{12,28},{16,0},{20,4},{24,8},{28,12},{1,17},{... | collective-permute-start | bytes 98312 | tf_op jit(solution)/shard_map/ppermute | solution.py:25
  45.7 1.6 %collective-permute-start.18 = (bf16[128,768]{1,0:T(8,128)(2,1)S(1)}, bf16[128,768]{1,0:T(8,128)(2,1)S(1)}, u32[]{:S(2)}, u32[]{:S(2)}) collective-permute-start(bf16[128,768]{1,0:T(8,128)(2,1)S(1)} %product.9), channel_id=1, source_target_pairs={{0,2},{1,3},{2,0},{3,1},{4,6},{5,7},{6,4},{7,5},{8,10},{9,11},{10,... | collective-permute-start | bytes 589832 | tf_op jit(solution)/shard_map/ppermute | solution.py:25
  47.8 0.8 %collective-permute-done.11 = bf16[128,128]{1,0:T(8,128)(2,1)S(1)} collective-permute-done((bf16[128,128]{1,0:T(8,128)(2,1)S(1)}, bf16[128,128]{1,0:T(8,128)(2,1)S(1)}, u32[]{:S(2)}, u32[]{:S(2)}) %collective-permute-start.11) | collective-permute-done | bytes 32800 | tf_op jit(solution)/shard_map/ppermute | solution.py:25
  48.7 0.7 %product.10.acc_ref = f32[128,4096]{1,0:T(8,128)S(1)} custom-call(bf16[128,512]{1,0:T(8,128)(2,1)S(1)} %get-tuple-element.38.dq_ref, bf16[256,4096]{1,0:T(8,128)(2,1)S(1)} %get-tuple-element.44.wm_ref, bf16[256,4096]{1,0:T(8,128)(2,1)S(1)} %collective-permute-done.14.wo_ref), custom_call_target="tpu_custom_call" | custom-call | flops 536870912 | bytes 4194304 | tf_op jit(solution)/shard_map/product/pallas_call | solution.py:197
  49.5 1.6 %collective-permute-start.15 = (bf16[128,128]{1,0:T(8,128)(2,1)S(1)}, bf16[128,128]{1,0:T(8,128)(2,1)S(1)}, u32[]{:S(2)}, u32[]{:S(2)}) collective-permute-start(bf16[128,128]{1,0:T(8,128)(2,1)S(1)} %fusion.3), channel_id=1, source_target_pairs={{0,2},{1,3},{2,0},{3,1},{4,6},{5,7},{6,4},{7,5},{8,10},{9,11},{10,... | collective-permute-start | bytes 98312 | tf_op jit(solution)/shard_map/ppermute | solution.py:25
  51.6 2.1 %collective-permute-done.18.refs_2_ = bf16[128,768]{1,0:T(8,128)(2,1)S(1)} collective-permute-done((bf16[128,768]{1,0:T(8,128)(2,1)S(1)}, bf16[128,768]{1,0:T(8,128)(2,1)S(1)}, u32[]{:S(2)}, u32[]{:S(2)}) %collective-permute-start.18) | collective-permute-done | bytes 196640 | tf_op jit(solution)/shard_map/ppermute | solution.py:25
  53.6 1.5 %collective-permute-start.20 = (bf16[128,768]{1,0:T(8,128)(2,1)S(1)}, bf16[128,768]{1,0:T(8,128)(2,1)S(1)}, u32[]{:S(2)}, u32[]{:S(2)}) collective-permute-start(bf16[128,768]{1,0:T(8,128)(2,1)S(1)} %product.12), channel_id=1, source_target_pairs={{0,2},{1,3},{2,0},{3,1},{4,6},{5,7},{6,4},{7,5},{8,10},{9,11},{10,... | collective-permute-start | bytes 589832 | tf_op jit(solution)/shard_map/ppermute | solution.py:25
  55.2 2.7 %collective-permute-done.19.refs_3_ = bf16[128,768]{1,0:T(8,128)(2,1)S(1)} collective-permute-done((bf16[128,768]{1,0:T(8,128)(2,1)S(1)}, bf16[128,768]{1,0:T(8,128)(2,1)S(1)}, u32[]{:S(2)}, u32[]{:S(2)}) %collective-permute-start.19) | collective-permute-done | bytes 196640 | tf_op jit(solution)/shard_map/ppermute | solution.py:25
  57.8 1.5 %collective-permute-start.21 = (bf16[128,512]{1,0:T(8,128)(2,1)S(1)}, bf16[128,512]{1,0:T(8,128)(2,1)S(1)}, u32[]{:S(2)}, u32[]{:S(2)}) collective-permute-start(bf16[128,512]{1,0:T(8,128)(2,1)S(1)} %product.13), channel_id=1, source_target_pairs={{0,2},{1,3},{2,0},{3,1},{4,6},{5,7},{6,4},{7,5},{8,10},{9,11},{10,... | collective-permute-start | bytes 393224 | tf_op jit(solution)/shard_map/ppermute | solution.py:25
  59.5 1.2 %collective-permute-done.16 = bf16[128,128]{1,0:T(8,128)(2,1)S(1)} collective-permute-done((bf16[128,128]{1,0:T(8,128)(2,1)S(1)}, bf16[128,128]{1,0:T(8,128)(2,1)S(1)}, u32[]{:S(2)}, u32[]{:S(2)}) %collective-permute-start.16) | collective-permute-done | bytes 32800 | tf_op jit(solution)/shard_map/ppermute | solution.py:25
  60.7 1.3 %collective-permute-done.20.refs_4_ = bf16[128,768]{1,0:T(8,128)(2,1)S(1)} collective-permute-done((bf16[128,768]{1,0:T(8,128)(2,1)S(1)}, bf16[128,768]{1,0:T(8,128)(2,1)S(1)}, u32[]{:S(2)}, u32[]{:S(2)}) %collective-permute-start.20) | collective-permute-done | bytes 196640 | tf_op jit(solution)/shard_map/ppermute | solution.py:25
  62.0 1.6 %finish.1 = (bf16[128,4096]{1,0:T(8,128)(2,1)}, f32[128,512]{1,0:T(8,128)S(1)}) custom-call(s32[1]{0:T(128)} %bitcast.core_ref, f32[128,128]{1,0:T(8,128)S(1)} %get-tuple-element.63.mine_ref, f32[128,128]{1,0:T(8,128)S(1)} %convert_element_type.68.other_ref, bf16[256,4096]{1,0:T(8,128)(2,1)S(1)} %copy-done.3, f32[128,4096]{1,0:T(8,128)S(1)} %product.10.acc_ref, ...), custom_call_target="tpu_custom_call" | custom-call | flops 268435456 | bytes 5242880 | tf_op jit(solution)/shard_map/finish/pallas_call | solution.py:233
  (63 shorter events, 5.1 us)
Async XLA Ops:
  0.0 2.2 %collective-permute-start.3 = (bf16[128,256]{1,0:T(8,128)(2,1)}, bf16[128,256]{1,0:T(8,128)(2,1)S(1)}, u32[]{:S(2)}, u32[]{:S(2)}) collective-permute-start(bf16[128,256]{1,0:T(8,128)(2,1)} %param.8), channel_id=1, source_target_pairs={{0,1},{1,0},{2,3},{3,2},{4,5},{5,4},{6,7},{7,6},{8,9},{9,8},{10,11... | collective-permute-start | bytes 196616 | tf_op jit(solution)/shard_map/ppermute | solution.py:25
  0.5 1.8 %collective-permute-start.4 = (bf16[128,256]{1,0:T(8,128)(2,1)}, bf16[128,256]{1,0:T(8,128)(2,1)S(1)}, u32[]{:S(2)}, u32[]{:S(2)}) collective-permute-start(bf16[128,256]{1,0:T(8,128)(2,1)} %param.11), channel_id=1, source_target_pairs={{0,1},{1,0},{2,3},{3,2},{4,5},{5,4},{6,7},{7,6},{8,9},{9,8},{10,11... | collective-permute-start | bytes 196616 | tf_op jit(solution)/shard_map/ppermute | solution.py:25
  2.2 8.7 %copy-start.7 = (s32[128]{0:T(128)S(1)}, s32[128]{0:T(128)}, u32[]{:S(2)}) copy-start(s32[128]{0:T(128)} %param.13) | copy-start | bytes 1540
  2.2 8.7 %copy-start.6 = (s32[128]{0:T(128)S(1)}, s32[128]{0:T(128)}, u32[]{:S(2)}) copy-start(s32[128]{0:T(128)} %param.12) | copy-start | bytes 1540
  2.3 8.7 %copy-start.4 = (bf16[128,256]{1,0:T(8,128)(2,1)S(1)}, bf16[128,256]{1,0:T(8,128)(2,1)}, u32[]{:S(2)}) copy-start(bf16[128,256]{1,0:T(8,128)(2,1)} %param.8) | copy-start | bytes 196612
  2.3 8.7 %copy-start.5 = (bf16[128,256]{1,0:T(8,128)(2,1)S(1)}, bf16[128,256]{1,0:T(8,128)(2,1)}, u32[]{:S(2)}) copy-start(bf16[128,256]{1,0:T(8,128)(2,1)} %param.11) | copy-start | bytes 196612
  5.1 20.8 %collective-permute-start.8 = (bf16[256,4096]{1,0:T(8,128)(2,1)S(1)}, bf16[256,4096]{1,0:T(8,128)(2,1)S(1)}, u32[]{:S(2)}, u32[]{:S(2)}) collective-permute-start(bf16[256,4096]{1,0:T(8,128)(2,1)S(1)} %get-tuple-element.40), channel_id=1, source_target_pairs={{0,1},{1,0},{2,3},{3,2},{4,5},{5,4},{6,7},{7,6},{8,9},{9,8},{10,11... | collective-permute-start | bytes 6291464 | tf_op jit(solution)/shard_map/ppermute | solution.py:25
  5.7 5.8 %collective-permute-start.1 = (bf16[144,128]{1,0:T(8,128)(2,1)S(1)}, bf16[144,128]{1,0:T(8,128)(2,1)S(1)}, u32[]{:S(2)}, u32[]{:S(2)}) collective-permute-start(bf16[144,128]{1,0:T(8,128)(2,1)S(1)} %get-tuple-element.73), channel_id=1, source_target_pairs={{0,16},{4,20},{8,24},{12,28},{16,0},{20,4},{24,8},{28,12},{1,17},{... | collective-permute-start | bytes 110600 | tf_op jit(solution)/shard_map/ppermute | solution.py:25
  9.3 4.0 %collective-permute-start = (bf16[144,128]{1,0:T(8,128)(2,1)S(1)}, bf16[144,128]{1,0:T(8,128)(2,1)S(1)}, u32[]{:S(2)}, u32[]{:S(2)}) collective-permute-start(bf16[144,128]{1,0:T(8,128)(2,1)S(1)} %get-tuple-element.73), channel_id=1, source_target_pairs={{0,8},{4,12},{8,0},{12,4},{16,24},{20,28},{24,16},{28,20},{1,9},{5... | collective-permute-start | bytes 110600 | tf_op jit(solution)/shard_map/ppermute | solution.py:25
  10.9 5.8 %collective-permute-start.2 = (bf16[144,128]{1,0:T(8,128)(2,1)S(1)}, bf16[144,128]{1,0:T(8,128)(2,1)S(1)}, u32[]{:S(2)}, u32[]{:S(2)}) collective-permute-start(bf16[144,128]{1,0:T(8,128)(2,1)S(1)} %get-tuple-element.73), channel_id=1, source_target_pairs={{0,24},{4,28},{8,16},{12,20},{16,8},{20,12},{24,0},{28,4},{1,25},{... | collective-permute-start | bytes 110600 | tf_op jit(solution)/shard_map/ppermute | solution.py:25
  16.7 5.2 %collective-permute-start.6 = (bf16[4,144,128]{2,1,0:T(8,128)(2,1)S(1)}, bf16[4,144,128]{2,1,0:T(8,128)(2,1)S(1)}, u32[]{:S(2)}, u32[]{:S(2)}) collective-permute-start(bf16[4,144,128]{2,1,0:T(8,128)(2,1)S(1)} %pad_maximum_fusion.refs_0_), channel_id=1, source_target_pairs={{0,4},{4,0},{8,12},{12,8},{16,20},{20,16},{24,28},{28,24},{1,5},{5... | collective-permute-start | bytes 442376 | tf_op jit(solution)/shard_map/ppermute | solution.py:25
  18.3 3.7 %collective-permute-start.5 = (bf16[4,144,128]{2,1,0:T(8,128)(2,1)S(1)}, bf16[4,144,128]{2,1,0:T(8,128)(2,1)S(1)}, u32[]{:S(2)}, u32[]{:S(2)}) collective-permute-start(bf16[4,144,128]{2,1,0:T(8,128)(2,1)S(1)} %pad_maximum_fusion.refs_0_), channel_id=1, source_target_pairs={{0,1},{1,0},{2,3},{3,2},{4,5},{5,4},{6,7},{7,6},{8,9},{9,8},{10,11... | collective-permute-start | bytes 442376 | tf_op jit(solution)/shard_map/ppermute | solution.py:25
  22.0 1.4 %collective-permute-start.7 = (bf16[4,144,128]{2,1,0:T(8,128)(2,1)S(1)}, bf16[4,144,128]{2,1,0:T(8,128)(2,1)S(1)}, u32[]{:S(2)}, u32[]{:S(2)}) collective-permute-start(bf16[4,144,128]{2,1,0:T(8,128)(2,1)S(1)} %collective-permute-done.6.refs_2_), channel_id=1, source_target_pairs={{0,1},{1,0},{2,3},{3,2},{4,5},{5,4},{6,7},{7,6},{8,9},{9,8},{10,11... | collective-permute-start | bytes 442376 | tf_op jit(solution)/shard_map/ppermute | solution.py:25
  25.8 1.4 %copy-start = (bf16[256,4096]{1,0:T(8,128)(2,1)}, bf16[256,4096]{1,0:T(8,128)(2,1)S(1)}, u32[]{:S(2)}) copy-start(bf16[256,4096]{1,0:T(8,128)(2,1)S(1)} %collective-permute-done.8.wo_ref) | copy-start | bytes 6291460
  27.2 5.5 %collective-permute-start.13 = (bf16[128,512]{1,0:T(8,128)(2,1)S(1)}, bf16[128,512]{1,0:T(8,128)(2,1)S(1)}, u32[]{:S(2)}, u32[]{:S(2)}) collective-permute-start(bf16[128,512]{1,0:T(8,128)(2,1)S(1)} %product.7), channel_id=1, source_target_pairs={{0,2},{1,3},{2,0},{3,1},{4,6},{5,7},{6,4},{7,5},{8,10},{9,11},{10,... | collective-permute-start | bytes 393224 | tf_op jit(solution)/shard_map/ppermute | solution.py:25
  28.8 1.6 %copy-start.1 = (bf16[256,4096]{1,0:T(8,128)(2,1)S(1)}, bf16[256,4096]{1,0:T(8,128)(2,1)}, u32[]{:S(2)}) copy-start(bf16[256,4096]{1,0:T(8,128)(2,1)} %copy-done) | copy-start | bytes 6291460
  30.7 4.9 %copy-start.2 = (bf16[256,4096]{1,0:T(8,128)(2,1)S(1)}, bf16[256,4096]{1,0:T(8,128)(2,1)}, u32[]{:S(2)}) copy-start(bf16[256,4096]{1,0:T(8,128)(2,1)} %copy-done) | copy-start | bytes 6291460
  35.5 13.2 %collective-permute-start.14 = (bf16[256,4096]{1,0:T(8,128)(2,1)S(1)}, bf16[256,4096]{1,0:T(8,128)(2,1)S(1)}, u32[]{:S(2)}, u32[]{:S(2)}) collective-permute-start(bf16[256,4096]{1,0:T(8,128)(2,1)S(1)} %get-tuple-element.45), channel_id=1, source_target_pairs={{0,1},{1,0},{2,3},{3,2},{4,5},{5,4},{6,7},{7,6},{8,9},{9,8},{10,11... | collective-permute-start | bytes 6291464 | tf_op jit(solution)/shard_map/ppermute | solution.py:25
  35.9 6.0 %collective-permute-start.9 = (bf16[4,128,128]{2,1,0:T(8,128)(2,1)S(1)}, bf16[4,128,128]{2,1,0:T(8,128)(2,1)S(1)}, u32[]{:S(2)}, u32[]{:S(2)}) collective-permute-start(bf16[4,128,128]{2,1,0:T(8,128)(2,1)S(1)} %get-tuple-element.42), channel_id=1, source_target_pairs={{0,4},{4,0},{8,12},{12,8},{16,20},{20,16},{24,28},{28,24},{1,5},{5... | collective-permute-start | bytes 393224 | tf_op jit(solution)/shard_map/ppermute | solution.py:25
  37.4 8.3 %collective-permute-start.17 = (bf16[128,768]{1,0:T(8,128)(2,1)S(1)}, bf16[128,768]{1,0:T(8,128)(2,1)S(1)}, u32[]{:S(2)}, u32[]{:S(2)}) collective-permute-start(bf16[128,768]{1,0:T(8,128)(2,1)S(1)} %product.8), channel_id=1, source_target_pairs={{0,2},{1,3},{2,0},{3,1},{4,6},{5,7},{6,4},{7,5},{8,10},{9,11},{10,... | collective-permute-start | bytes 589832 | tf_op jit(solution)/shard_map/ppermute | solution.py:25
  41.9 5.4 %collective-permute-start.10 = (bf16[128,128]{1,0:T(8,128)(2,1)S(1)}, bf16[128,128]{1,0:T(8,128)(2,1)S(1)}, u32[]{:S(2)}, u32[]{:S(2)}) collective-permute-start(bf16[128,128]{1,0:T(8,128)(2,1)S(1)} %get-tuple-element.59), channel_id=1, source_target_pairs={{0,8},{4,12},{8,0},{12,4},{16,24},{20,28},{24,16},{28,20},{1,9},{5... | collective-permute-start | bytes 98312 | tf_op jit(solution)/shard_map/ppermute | solution.py:25
  42.0 5.9 %collective-permute-start.12 = (bf16[128,128]{1,0:T(8,128)(2,1)S(1)}, bf16[128,128]{1,0:T(8,128)(2,1)S(1)}, u32[]{:S(2)}, u32[]{:S(2)}) collective-permute-start(bf16[128,128]{1,0:T(8,128)(2,1)S(1)} %get-tuple-element.60), channel_id=1, source_target_pairs={{0,24},{4,28},{8,16},{12,20},{16,8},{20,12},{24,0},{28,4},{1,25},{... | collective-permute-start | bytes 98312 | tf_op jit(solution)/shard_map/ppermute | solution.py:25
  43.9 4.8 %collective-permute-start.11 = (bf16[128,128]{1,0:T(8,128)(2,1)S(1)}, bf16[128,128]{1,0:T(8,128)(2,1)S(1)}, u32[]{:S(2)}, u32[]{:S(2)}) collective-permute-start(bf16[128,128]{1,0:T(8,128)(2,1)S(1)} %get-tuple-element.61), channel_id=1, source_target_pairs={{0,16},{4,20},{8,24},{12,28},{16,0},{20,4},{24,8},{28,12},{1,17},{... | collective-permute-start | bytes 98312 | tf_op jit(solution)/shard_map/ppermute | solution.py:25
  45.7 7.9 %collective-permute-start.18 = (bf16[128,768]{1,0:T(8,128)(2,1)S(1)}, bf16[128,768]{1,0:T(8,128)(2,1)S(1)}, u32[]{:S(2)}, u32[]{:S(2)}) collective-permute-start(bf16[128,768]{1,0:T(8,128)(2,1)S(1)} %product.9), channel_id=1, source_target_pairs={{0,2},{1,3},{2,0},{3,1},{4,6},{5,7},{6,4},{7,5},{8,10},{9,11},{10,... | collective-permute-start | bytes 589832 | tf_op jit(solution)/shard_map/ppermute | solution.py:25
  47.3 10.5 %collective-permute-start.19 = (bf16[128,768]{1,0:T(8,128)(2,1)S(1)}, bf16[128,768]{1,0:T(8,128)(2,1)S(1)}, u32[]{:S(2)}, u32[]{:S(2)}) collective-permute-start(bf16[128,768]{1,0:T(8,128)(2,1)S(1)} %product.11), channel_id=1, source_target_pairs={{0,2},{1,3},{2,0},{3,1},{4,6},{5,7},{6,4},{7,5},{8,10},{9,11},{10,... | collective-permute-start | bytes 589832 | tf_op jit(solution)/shard_map/ppermute | solution.py:25
  49.5 9.9 %collective-permute-start.15 = (bf16[128,128]{1,0:T(8,128)(2,1)S(1)}, bf16[128,128]{1,0:T(8,128)(2,1)S(1)}, u32[]{:S(2)}, u32[]{:S(2)}) collective-permute-start(bf16[128,128]{1,0:T(8,128)(2,1)S(1)} %fusion.3), channel_id=1, source_target_pairs={{0,2},{1,3},{2,0},{3,1},{4,6},{5,7},{6,4},{7,5},{8,10},{9,11},{10,... | collective-permute-start | bytes 98312 | tf_op jit(solution)/shard_map/ppermute | solution.py:25
  51.3 10.7 %copy-start.3 = (bf16[256,4096]{1,0:T(8,128)(2,1)S(1)}, bf16[256,4096]{1,0:T(8,128)(2,1)}, u32[]{:S(2)}) copy-start(bf16[256,4096]{1,0:T(8,128)(2,1)} %w_ref.5) | copy-start | bytes 6291460
  53.6 8.4 %collective-permute-start.20 = (bf16[128,768]{1,0:T(8,128)(2,1)S(1)}, bf16[128,768]{1,0:T(8,128)(2,1)S(1)}, u32[]{:S(2)}, u32[]{:S(2)}) collective-permute-start(bf16[128,768]{1,0:T(8,128)(2,1)S(1)} %product.12), channel_id=1, source_target_pairs={{0,2},{1,3},{2,0},{3,1},{4,6},{5,7},{6,4},{7,5},{8,10},{9,11},{10,... | collective-permute-start | bytes 589832 | tf_op jit(solution)/shard_map/ppermute | solution.py:25
  57.8 5.7 %collective-permute-start.21 = (bf16[128,512]{1,0:T(8,128)(2,1)S(1)}, bf16[128,512]{1,0:T(8,128)(2,1)S(1)}, u32[]{:S(2)}, u32[]{:S(2)}) collective-permute-start(bf16[128,512]{1,0:T(8,128)(2,1)S(1)} %product.13), channel_id=1, source_target_pairs={{0,2},{1,3},{2,0},{3,1},{4,6},{5,7},{6,4},{7,5},{8,10},{9,11},{10,... | collective-permute-start | bytes 393224 | tf_op jit(solution)/shard_map/ppermute | solution.py:25
  59.4 1.3 %collective-permute-start.16 = (bf16[128,128]{1,0:T(8,128)(2,1)S(1)}, bf16[128,128]{1,0:T(8,128)(2,1)S(1)}, u32[]{:S(2)}, u32[]{:S(2)}) collective-permute-start(bf16[128,128]{1,0:T(8,128)(2,1)S(1)} %get-tuple-element.62), channel_id=1, source_target_pairs={{0,1},{1,0},{2,3},{3,2},{4,5},{5,4},{6,7},{7,6},{8,9},{9,8},{10,11... | collective-permute-start | bytes 98312 | tf_op jit(solution)/shard_map/ppermute | solution.py:25

commit v7 on v6

--- a/solution.py
+++ b/solution.py
@@ -10,7 +10,8 @@
 
 RUN = 64
 META_ROWS = 16
-CHUNKS = (2, 3, 3, 3, 3, 2)
+CHUNKS = (13, 3)
+TILES = 4
 ANY = pl.BlockSpec(memory_space=pl.ANY)
 HBM = pl.BlockSpec(memory_space=pltpu.HBM)
 SMEM = pl.BlockSpec(memory_space=pltpu.SMEM)
@@ -43,23 +44,6 @@
     runs = (positions.reshape(rows // RUN, RUN)[:, :1] // RUN).astype(jnp.bfloat16)
     meta = jnp.pad(jnp.broadcast_to(runs, (rows // RUN, size)), ((0, META_ROWS - rows // RUN), (0, 0)))
     return jnp.concatenate([held, meta], axis=0)
-
-
-def gate_kernel(value_ref, *refs):
-    pass
-
-
-def gate(value, *after):
-    return pl.pallas_call(
-        gate_kernel,
-        out_shape=jax.ShapeDtypeStruct(value.shape, value.dtype),
-        in_specs=[ANY] * (1 + len(after)),
-        out_specs=ANY,
-        input_output_aliases={0: 0},
-        compiler_params=params(),
-        cost_estimate=pl.CostEstimate(flops=10**11, bytes_accessed=10**8, transcendentals=0),
-        name="gate",
-    )(value, *after)
 
 
 def carve_kernel(block_ref, w_ref, *refs):
@@ -207,68 +191,51 @@
     )(dq, w_mine, w_other)
 
 
-def finish_kernel(starts, core_ref, mine_ref, other_ref, w_ref, acc_ref, *refs):
-    early = len(starts) - 2
-    out_ref, left_ref = refs[early:]
-    inv_root = 1.0 / math.sqrt(mine_ref.shape[1])
-    size = mine_ref.shape[1]
-    is_key = core_ref[0] == 0
-    wm_ref = w_ref.at[pl.ds(pl.multiple_of(core_ref[0] * size, size), size), :]
-    wo_ref = w_ref.at[pl.ds(pl.multiple_of((1 - core_ref[0]) * size, size), size), :]
-    mine = (mine_ref[...] * jnp.where(is_key, inv_root, 1.0)).astype(jnp.bfloat16)
-    other = (other_ref[...] * jnp.where(is_key, 1.0, inv_root)).astype(jnp.bfloat16)
-    for c in range(early + 1):
-        at = slice(starts[c], starts[c + 1])
-        acc = acc_ref[:, at] + dot(mine, wm_ref[:, at], ((1,), (0,))) + dot(other, wo_ref[:, at], ((1,), (0,)))
-        if c < early:
-            out_ref[:, at] = (acc + refs[c][...].astype(jnp.float32)).astype(jnp.bfloat16)
-        else:
-            left_ref[...] = acc
-
-
-def finish(core, mine, other, w_kv, acc, received, starts):
+def finish_kernel(core_ref, kv_ref, w_ref, acc_ref, first_ref, second_ref, out_ref, hold_ref, sems):
+    rows, share = acc_ref.shape
+    pair = kv_ref.shape[1]
+    size = pair // 2
+    cut = first_ref.shape[1]
+    tile = share // TILES
+    inv_root = 1.0 / math.sqrt(size)
+    column = lax.broadcasted_iota(jnp.int32, (1, pair), 1)
+    is_key = (column < size) == (core_ref[0] == 0)
+    kv = kv_ref[...].astype(jnp.float32) + second_ref[:, share - cut :].astype(jnp.float32)
+    kv = (kv * jnp.where(is_key, inv_root, 1.0)).astype(jnp.bfloat16)
+    at_mine = pl.ds(pl.multiple_of(core_ref[0] * size, size), size)
+    at_other = pl.ds(pl.multiple_of((1 - core_ref[0]) * size, size), size)
+    copies = []
+    for i in range(TILES):
+        low, high = i * tile, (i + 1) * tile
+        w = jnp.concatenate([w_ref[at_mine, low:high], w_ref[at_other, low:high]], axis=0)
+        acc = acc_ref[:, low:high] + dot(kv, w, ((1,), (0,)))
+        come = []
+        if low < cut:
+            come.append(first_ref[:, low : min(high, cut)])
+        if high > cut:
+            come.append(second_ref[:, max(low, cut) - cut : high - cut])
+        acc = acc + jnp.concatenate(come, axis=1).astype(jnp.float32)
+        hold_ref[:, low:high] = acc.astype(jnp.bfloat16)
+        copies.append(pltpu.make_async_copy(hold_ref.at[:, low:high], out_ref.at[:, low:high], sems.at[i]))
+        copies[i].start()
+    for one in copies:
+        one.wait()
+
+
+def finish(core, kv, w_kv, acc, first, second):
     rows, share = acc.shape
-    size = mine.shape[1]
-    last = starts[-2]
     return pl.pallas_call(
-        functools.partial(finish_kernel, starts),
-        out_shape=[
-            jax.ShapeDtypeStruct((rows, share), jnp.bfloat16),
-            jax.ShapeDtypeStruct((rows, share - last), jnp.float32),
-        ],
-        grid=(1,),
-        in_specs=[SMEM] + [pl.BlockSpec()] * (4 + len(received)),
-        out_specs=[
-            pl.BlockSpec((rows, last), lambda i: (0, 0)),
-            pl.BlockSpec((rows, share - last), lambda i: (0, 0)),
-        ],
+        finish_kernel,
+        out_shape=jax.ShapeDtypeStruct((rows, share), jnp.bfloat16),
+        in_specs=[SMEM] + [pl.BlockSpec()] * 5,
+        out_specs=ANY,
+        scratch_shapes=[pltpu.VMEM((rows, share), jnp.bfloat16), pltpu.SemaphoreType.DMA((TILES,))],
         compiler_params=params(),
         cost_estimate=pl.CostEstimate(
-            flops=4 * rows * size * share, bytes_accessed=10 * rows * share, transcendentals=0
+            flops=2 * rows * kv.shape[1] * share, bytes_accessed=10 * rows * share, transcendentals=0
         ),
         name="finish",
-    )(core, mine, other, w_kv, acc, *received)
-
-
-def last_kernel(left_ref, part_ref, held_ref, out_ref, sum_ref, sem):
-    sum_ref[...] = (left_ref[...] + part_ref[...].astype(jnp.float32)).astype(jnp.bfloat16)
-    first = out_ref.shape[1] - sum_ref.shape[1]
-    copy = pltpu.make_async_copy(sum_ref, out_ref.at[:, first:], sem)
-    copy.start()
-    copy.wait()
-
-
-def last(left, part, held):
-    return pl.pallas_call(
-        last_kernel,
-        out_shape=jax.ShapeDtypeStruct(held.shape, held.dtype),
-        in_specs=[pl.BlockSpec(), pl.BlockSpec(), ANY],
-        out_specs=ANY,
-        input_output_aliases={2: 0},
-        scratch_shapes=[pltpu.VMEM(part.shape, held.dtype), pltpu.SemaphoreType.DMA(())],
-        compiler_params=params(),
-        name="last",
-    )(left, part, held)
+    )(core, kv, w_kv, acc, first, second)
 
 
 def on_device(queries, keys, values, dout, positions, doc_ids, w_query, w_kv):
@@ -278,13 +245,10 @@
     share = w_kv.shape[1]
     local_heads = queries.shape[1] // keys.shape[1]
 
-    piece = pack(core, positions, keys, values)
-    here_z = jnp.stack([piece] + [swapped(piece, "ctx", 2 * s) for s in range(1, half)])
     q_other = swapped(queries, "head", 1)
     g_other = swapped(dout, "head", 1)
-    q_other = gate(q_other, g_other)
-    far_send, far_mine = carve([head ^ 3, head ^ 2], w_query, share, q_other)
-    far_other = swapped(far_send, "head", 1)
+    piece = pack(core, positions, keys, values)
+    along_z = [piece] + [swapped(piece, "ctx", 2 * s) for s in range(1, half)]
 
     def stacked(*arrays):
         return jnp.concatenate([part for one in arrays for part in jnp.split(one, local_heads, axis=1)], axis=0)
@@ -293,43 +257,45 @@
     grad = stacked(dout, g_other)
     bounds = jnp.stack([positions, doc_ids * RUN]).astype(jnp.float32)
     row_info = jnp.tile(bounds, (1, 2 * local_heads))
-    here_z, far_mine, query, grad, row_info = lax.optimization_barrier(
-        (here_z, far_mine, query, grad, row_info)
+    far = carve([head ^ 3, head ^ 2], w_query, share, positions)
+    here_z, query, grad, row_info, far_send, far_mine = lax.optimization_barrier(
+        (jnp.stack(along_z), query, grad, row_info, *far)
     )
     here_x = swapped(here_z, "ctx", 1)
+    far_other = swapped(far_send, "head", 1)
     there_z = swapped(here_z, "head", 1)
+    near = carve([head ^ 1, head], w_query, share, here_z)
+    here_x, near_send, near_mine = lax.optimization_barrier((here_x, *near))
     there_x = swapped(here_x, "head", 1)
     dq, back_z, back_x = attention(
         core, row_info, query, grad, (here_z, there_z, here_x, there_x), queries.shape[0]
     )
 
-    starts = [0]
-    for units in CHUNKS:
-        starts.append(starts[-1] + units * (share // sum(CHUNKS)))
-    parts = [
-        product(dq, far_mine, far_other, low, high - low, jnp.bfloat16) for low, high in zip(starts, starts[1:])
-    ]
-    received = []
-    for c, part in enumerate(parts):
-        if c >= 2:
-            part, received[c - 2] = lax.optimization_barrier((part, received[c - 2]))
-        received.append(swapped(part, "head", 2))
-
-    back_x, back_z, *_ = lax.optimization_barrier((back_x, back_z, *parts[:2]))
-    pair = back_z.astype(jnp.float32) + swapped(back_x, "ctx", 1).astype(jnp.float32)
-    mine = pair[0]
-    for s in range(1, half):
-        mine = mine + swapped(pair[s].astype(jnp.bfloat16), "ctx", 2 * s).astype(jnp.float32)
-    mine = mine.astype(jnp.bfloat16)
-
-    near_send, near_mine = carve([head ^ 1, head], w_query, share, received[0])
-    acc = product(dq, near_mine, swapped(near_send, "head", 1), 0, share, jnp.float32)
-    mine, acc = lax.optimization_barrier((mine, acc))
-    mine = mine.astype(jnp.float32) + swapped(mine, "head", 2).astype(jnp.float32)
-    other = swapped(mine.astype(jnp.bfloat16), "head", 1).astype(jnp.float32)
-
-    held, left = finish(core, mine, other, w_kv, acc, received[:-1], starts)
-    return last(left, received[-1], held)
+    cut = CHUNKS[0] * (share // sum(CHUNKS))
+    first_part = product(dq, far_mine, far_other, 0, cut, jnp.bfloat16)
+    second_part = product(dq, far_mine, far_other, cut, share - cut, jnp.bfloat16)
+    first = swapped(first_part, "head", 2)
+    dq, near_send = lax.optimization_barrier((dq, near_send))
+    near_other = swapped(near_send, "head", 1)
+
+    def exchange(trip, kv):
+        sent = lax.dynamic_slice_in_dim(back_x, trip * half, half, axis=0)
+        pair = back_z.astype(jnp.float32) + swapped(sent, "ctx", 1).astype(jnp.float32)
+        mine = pair[0]
+        for s in range(1, half):
+            mine = mine + swapped(pair[s].astype(jnp.bfloat16), "ctx", 2 * s).astype(jnp.float32)
+        mine = mine.astype(jnp.bfloat16)
+        return jnp.concatenate([mine, swapped(mine, "head", 1)], axis=1)
+
+    back_x, back_z, first_part, second_part = lax.optimization_barrier((back_x, back_z, first_part, second_part))
+    trips = 1 + jnp.minimum(positions[0], 0)
+    kv = lax.fori_loop(0, trips, exchange, jnp.zeros((queries.shape[0], 2 * keys.shape[1]), jnp.bfloat16))
+
+    second_part = jnp.concatenate([second_part, kv], axis=1)
+    second_part, first, near_mine = lax.optimization_barrier((second_part, first, near_mine))
+    second = swapped(second_part, "head", 2)
+    acc = product(dq, near_mine, near_other, 0, share, jnp.float32)
+    return finish(core, kv, w_kv, acc, first, second)
 
 
 def solution(mesh):

time: 64.5 us -> 65.8 us (1.020)
  waiting for transfers between devices: 23.7 us -> 18 us
  Pallas kernels: 12.5 us -> 17.2 us
  starting transfers between devices: 22.9 us -> 18.2 us
  other arithmetic: 1.28 us -> 5.03 us
  local copies, waits for them, and re-layouts: 3.52 us -> 6.55 us
    ppermute x22 -> x17, waiting for transfers between devices: 23.7 us -> 18 us  [swapped(): lax.ppermute(value, axis, [(source, source ^ bits) for source in range(co...]
    ppermute x22 -> x17, starting transfers between devices: 22.9 us -> 18.2 us  [swapped(): lax.ppermute(value, axis, [(source, source ^ bits) for source in range(co...]
    pallas_call x7 -> x3, Pallas kernels: 2.28 us -> 4.84 us  [product(): pl.pallas_call(functools.partial(product_kernel, first), out_shape=jax.Sh...]
    concatenate x0 -> x2, other arithmetic: none -> 1.56 us  [the longest x1 0.94 us: on_device(): second_part = jnp.concatenate([second_part, kv], axis=1)]
    split x4, local copies, waits for them, and re-layouts: 0.03 us -> 1.57 us  [stacked(): jnp.split(one, local_heads, axis=1)]
    pallas_call x2, Pallas kernels: 5.52 us -> 6.89 us  [carve(): pl.pallas_call(carve_kernel, out_shape=[block] * count, in_specs=[SMEM, H...]
    another operation x3, other arithmetic: 0.14 us -> 1.05 us  [the longest x2 0.11 us: on_device(): jnp.stack([piece] + [swapped(piece, 'ctx', 2 * s) for s in range(1, half)])]
    unnamed x18 -> x20, local copies, waits for them, and re-layouts: 2.74 us -> 3.6 us
  transfers between devices with their start and end apart: 22 -> 17, of which waited for: 12 -> 8; matrix products, arithmetic and copies ran while one was open for 3% -> 10% of each run, Pallas kernels for 9% -> 16%
where the time goes in v7:
time: 65.8 us; the launch traced here: 65.3 us
  starting transfers between devices  18.2 us (28%)
  waiting for transfers between devices  18 us (27%)
  Pallas kernels  17.2 us (26%)
  local copies, waits for them, and re-layouts  6.55 us (10%)
  other arithmetic  5.03 us (8%)
    ppermute x17, starting transfers between devices, swapped(): lax.ppermute(value, axis, [(source, source ^ bits) for source in range(co...  18.2 us
    ppermute x17, waiting for transfers between devices, swapped(): lax.ppermute(value, axis, [(source, source ^ bits) for source in range(co...  18 us
    pallas_call x2, Pallas kernels, carve(): pl.pallas_call(carve_kernel, out_shape=[block] * count, in_specs=[SMEM, H...  6.89 us
    pallas_call x3, Pallas kernels, product(): pl.pallas_call(functools.partial(product_kernel, first), out_shape=jax.Sh...  4.84 us
    unnamed x20, local copies, waits for them, and re-layouts  3.6 us
    pallas_call x1, Pallas kernels, attention(): pl.pallas_call(attention_kernel, out_shape=[jax.ShapeDtypeStruct((rows, w...  3.04 us
    pallas_call x1, Pallas kernels, finish(): pl.pallas_call(finish_kernel, out_shape=jax.ShapeDtypeStruct((rows, share...  2.42 us
    split x4, local copies, waits for them, and re-layouts, stacked(): jnp.split(one, local_heads, axis=1)  1.57 us
  transfers between devices with their start and end apart: 17, of which 8 were waited for; matrix products, arithmetic and copies ran while one was open for 10% of the time, Pallas kernels for 16%

profile of v7, /device:TPU:0, one launch (start us, length us, event | category | flops | bytes accessed | tf_op | source)
XLA Modules:
  0.0 65.3 jit_solution(12345888061088582552)
XLA Ops:
  0.0 0.7 %reshape.35 = s32[2,64]{1,0:T(2,128)S(1)} reshape(s32[128]{0:T(128)} %refs_0_.1) | data formatting | bytes 1024 | tf_op jit(solution)/shard_map/reshape | solution.py:44
  0.9 0.8 %broadcast_select_fusion = bf16[128,128]{1,0:T(8,128)(2,1)S(1)} fusion(bf16[128,128]{1,0:T(8,128)(2,1)} %param.11, bf16[128,128]{1,0:T(8,128)(2,1)} %param.12, pred[]{:T(512)} %bitcast.6), kind=kLoop, calls=%fused_computation.16 | loop fusion | flops 16384 | bytes 98305 | tf_op jit(solution)/shard_map/jit(_where)/select_n | solution.py:43
  1.7 4.1 %collective-permute-start.5 = (bf16[144,128]{1,0:T(8,128)(2,1)S(1)}, bf16[144,128]{1,0:T(8,128)(2,1)S(1)}, u32[]{:S(2)}, u32[]{:S(2)}) collective-permute-start(bf16[144,128]{1,0:T(8,128)(2,1)S(1)} %get-tuple-element.139), channel_id=1, source_target_pairs={{0,16},{4,20},{8,24},{12,28},{16,0},{20,4},{24,8},{28,12},{1,17},{... | collective-permute-start | bytes 110600 | tf_op jit(solution)/shard_map/ppermute | solution.py:26
  5.8 1.6 %collective-permute-start.4 = (bf16[144,128]{1,0:T(8,128)(2,1)S(1)}, bf16[144,128]{1,0:T(8,128)(2,1)S(1)}, u32[]{:S(2)}, u32[]{:S(2)}) collective-permute-start(bf16[144,128]{1,0:T(8,128)(2,1)S(1)} %get-tuple-element.139), channel_id=1, source_target_pairs={{0,8},{4,12},{8,0},{12,4},{16,24},{20,28},{24,16},{28,20},{1,9},{5... | collective-permute-start | bytes 110600 | tf_op jit(solution)/shard_map/ppermute | solution.py:26
  7.4 0.8 %fusion.10 = (bf16[128,128]{1,0:T(8,128)(2,1)S(1)}, bf16[128,128]{1,0:T(8,128)(2,1)S(1)}) fusion(bf16[128,256]{1,0:T(8,128)(2,1)} %param.10), kind=kLoop, calls=%fused_computation.33 | loop fusion | bytes 131072 | tf_op jit(solution)/shard_map/split | solution.py:254
  9.5 0.8 %fusion.8 = (bf16[128,128]{1,0:T(8,128)(2,1)S(1)}, bf16[128,128]{1,0:T(8,128)(2,1)S(1)}) fusion(bf16[128,256]{1,0:T(8,128)(2,1)} %param.13), kind=kLoop, calls=%fused_computation.31 | loop fusion | bytes 131072 | tf_op jit(solution)/shard_map/split | solution.py:254
  11.0 4.1 %carve.2 = (bf16[256,4096]{1,0:T(8,128)(2,1)}, bf16[256,4096]{1,0:T(8,128)(2,1)S(1)}) custom-call(s32[2]{0:T(128)S(1)} %pad_add_fusion.block_ref, bf16[256,16384]{1,0:T(8,128)(2,1)} %w_ref.4, s32[128]{0:T(128)S(1)} %copy-done.3), custom_call_target="tpu_custom_call" | custom-call | bytes 8388608 | tf_op jit(solution)/shard_map/carve/pallas_call | solution.py:68
  15.8 0.8 %collective-permute-done.8 = bf16[128,256]{1,0:T(8,128)(2,1)S(1)} collective-permute-done((bf16[128,256]{1,0:T(8,128)(2,1)S(1)}, bf16[128,256]{1,0:T(8,128)(2,1)S(1)}, u32[]{:S(2)}, u32[]{:S(2)}) %collective-permute-start.8) | collective-permute-done | bytes 65568 | tf_op jit(solution)/shard_map/ppermute | solution.py:26
  17.1 1.7 %collective-permute-start.10 = (bf16[4,144,128]{2,1,0:T(8,128)(2,1)S(1)}, bf16[4,144,128]{2,1,0:T(8,128)(2,1)S(1)}, u32[]{:S(2)}, u32[]{:S(2)}) collective-permute-start(bf16[4,144,128]{2,1,0:T(8,128)(2,1)S(1)} %pad_maximum_fusion.2.refs_0_), channel_id=1, source_target_pairs={{0,4},{4,0},{8,12},{12,8},{16,20},{20,16},{24,28},{28,24},{1,5},{5... | collective-permute-start | bytes 442376 | tf_op jit(solution)/shard_map/ppermute | solution.py:26
  18.9 2.8 %carve.3 = (bf16[256,4096]{1,0:T(8,128)(2,1)S(1)}, bf16[256,4096]{1,0:T(8,128)(2,1)S(1)}) custom-call(s32[2]{0:T(128)S(1)} %pad_add_fusion.1.block_ref, bf16[256,16384]{1,0:T(8,128)(2,1)} %w_ref.4, bf16[4,144,128]{2,1,0:T(8,128)(2,1)S(1)} %pad_maximum_fusion.2.refs_0_), custom_call_target="tpu_custom_call" | custom-call | bytes 8388608 | tf_op jit(solution)/shard_map/carve/pallas_call | solution.py:68
  21.7 1.3 %copy-done.5 = bf16[256,4096]{1,0:T(8,128)(2,1)} copy-done((bf16[256,4096]{1,0:T(8,128)(2,1)}, bf16[256,4096]{1,0:T(8,128)(2,1)S(1)}, u32[]{:S(2)}) %copy-start.5) | copy-done | bytes 2097176
  23.5 1.0 %collective-permute-done.11.refs_3_ = bf16[4,144,128]{2,1,0:T(8,128)(2,1)S(1)} collective-permute-done((bf16[4,144,128]{2,1,0:T(8,128)(2,1)S(1)}, bf16[4,144,128]{2,1,0:T(8,128)(2,1)S(1)}, u32[]{:S(2)}, u32[]{:S(2)}) %collective-permute-start.11) | collective-permute-done | bytes 147488 | tf_op jit(solution)/shard_map/ppermute | solution.py:26
  24.5 3.0 %attention.1 = (bf16[128,512]{1,0:T(8,128)(2,1)S(1)}, bf16[4,128,128]{2,1,0:T(8,128)(2,1)}, bf16[4,128,128]{2,1,0:T(8,128)(2,1)S(1)}) custom-call(s32[1]{0:T(128)} %bitcast.4.core_ref, f32[2,512]{1,0:T(2,128)S(1)} %bitcast.41, bf16[512,128]{1,0:T(8,128)(2,1)S(1)} %get-tuple-element.93.query_ref, bf16[512,128]{1,0:T(8,128)(2,1)S(1)} %get-tuple-element.94.grad_ref, ...), custom_call_target="tpu_custom_call" | custom-call | flops 671088640 | bytes 1048576 | tf_op jit(solution)/shard_map/attention/pallas_call | solution.py:154
  27.6 1.9 %product.4 = bf16[128,768]{1,0:T(8,128)(2,1)S(1)} custom-call(bf16[128,512]{1,0:T(8,128)(2,1)S(1)} %get-tuple-element.108.dq_ref, bf16[256,4096]{1,0:T(8,128)(2,1)S(1)} %get-tuple-element.102.wm_ref, bf16[256,4096]{1,0:T(8,128)(2,1)} %collective-permute-done.12.wo_ref), custom_call_target="tpu_custom_call" | custom-call | flops 100663296 | bytes 786432 | tf_op jit(solution)/shard_map/product/pallas_call | solution.py:181
  29.5 2.2 %product.3 = bf16[128,3328]{1,0:T(8,128)(2,1)S(1)} custom-call(bf16[128,512]{1,0:T(8,128)(2,1)S(1)} %get-tuple-element.108.dq_ref, bf16[256,4096]{1,0:T(8,128)(2,1)S(1)} %get-tuple-element.102.wm_ref, bf16[256,4096]{1,0:T(8,128)(2,1)} %collective-permute-done.12.wo_ref), custom_call_target="tpu_custom_call" | custom-call | flops 436207616 | bytes 3407872 | tf_op jit(solution)/shard_map/product/pallas_call | solution.py:181
  31.7 1.6 %collective-permute-start.13 = (bf16[4,128,128]{2,1,0:T(8,128)(2,1)S(1)}, bf16[4,128,128]{2,1,0:T(8,128)(2,1)}, u32[]{:S(2)}, u32[]{:S(2)}) collective-permute-start(bf16[4,128,128]{2,1,0:T(8,128)(2,1)S(1)} %get-tuple-element.105), channel_id=1, source_target_pairs={{0,4},{4,0},{8,12},{12,8},{16,20},{20,16},{24,28},{28,24},{1,5},{5... | collective-permute-start | bytes 393224 | tf_op jit(solution)/shard_map/while/body/ppermute | solution.py:26
  33.5 1.6 %collective-permute-start.14 = (bf16[128,3328]{1,0:T(8,128)(2,1)S(1)}, bf16[128,3328]{1,0:T(8,128)(2,1)}, u32[]{:S(2)}, u32[]{:S(2)}) collective-permute-start(bf16[128,3328]{1,0:T(8,128)(2,1)S(1)} %product.3), channel_id=1, source_target_pairs={{0,2},{1,3},{2,0},{3,1},{4,6},{5,7},{6,4},{7,5},{8,10},{9,11},{10,... | collective-permute-start | bytes 2555912 | tf_op jit(solution)/shard_map/ppermute | solution.py:26
  35.1 2.6 %collective-permute-done.13 = bf16[4,128,128]{2,1,0:T(8,128)(2,1)} collective-permute-done((bf16[4,128,128]{2,1,0:T(8,128)(2,1)S(1)}, bf16[4,128,128]{2,1,0:T(8,128)(2,1)}, u32[]{:S(2)}, u32[]{:S(2)}) %collective-permute-start.13) | collective-permute-done | bytes 131104 | tf_op jit(solution)/shard_map/while/body/ppermute | solution.py:26
  38.3 11.4 %while.12 = (s32[]{:T(128)}, bf16[128,256]{1,0:T(8,128)(2,1)}, s32[]{:T(128)}, bf16[4,128,128]{2,1,0:T(8,128)(2,1)S(1)}, bf16[4,128,128]{2,1,0:T(8,128)(2,1)}, /*index=5*/s32[]{:T(128)}) while((s32[]{:T(128)}, bf16[128,256]{1,0:T(8,128)(2,1)}, s32[]{:T(128)}, bf16[4,128,128]{2,1,0:T(8,128)(2,1)S(1)}, bf16[4,128,128]{2,1,0:T(8,128)(2,1)}, ...), condition=%wide.region_1.2_spmd, body=%wide.region_0.1_spmd.sunk | while | flops 507906 | bytes 1704165 | solution.py:292
  38.3 0.9 %fusion.14 = (bf16[4,128,128]{2,1,0:T(8,128)(2,1)S(1)}, f32[4,128,128]{2,1,0:T(8,128)S(1)}) fusion(bf16[4,128,128]{2,1,0:T(8,128)(2,1)} %get-tuple-element.198, bf16[4,128,128]{2,1,0:T(8,128)(2,1)S(1)} %get-tuple-element.197), kind=kLoop, calls=%fused_computation.10.clone.1 | loop fusion | flops 262144 | bytes 655360 | tf_op jit(solution)/shard_map/convert.2
  39.2 3.7 %collective-permute-start = (bf16[128,128]{1,0:T(8,128)(2,1)S(1)}, bf16[128,128]{1,0:T(8,128)(2,1)S(1)}, u32[]{:S(2)}, u32[]{:S(2)}) collective-permute-start(bf16[128,128]{1,0:T(8,128)(2,1)S(1)} %get-tuple-element.179), channel_id=1, source_target_pairs={{0,24},{4,28},{8,16},{12,20},{16,8},{20,12},{24,0},{28,4},{1,25},{... | collective-permute-start | bytes 98312 | tf_op jit(solution)/shard_map/while/body/ppermute | solution.py:26
  42.9 0.8 %collective-permute-start.2 = (bf16[128,128]{1,0:T(8,128)(2,1)S(1)}, bf16[128,128]{1,0:T(8,128)(2,1)S(1)}, u32[]{:S(2)}, u32[]{:S(2)}) collective-permute-start(bf16[128,128]{1,0:T(8,128)(2,1)S(1)} %get-tuple-element.181), channel_id=1, source_target_pairs={{0,8},{4,12},{8,0},{12,4},{16,24},{20,28},{24,16},{28,20},{1,9},{5... | collective-permute-start | bytes 98312 | tf_op jit(solution)/shard_map/while/body/ppermute | solution.py:26
  43.7 1.4 %collective-permute-done = bf16[128,128]{1,0:T(8,128)(2,1)S(1)} collective-permute-done((bf16[128,128]{1,0:T(8,128)(2,1)S(1)}, bf16[128,128]{1,0:T(8,128)(2,1)S(1)}, u32[]{:S(2)}, u32[]{:S(2)}) %collective-permute-start) | collective-permute-done | bytes 32800 | tf_op jit(solution)/shard_map/while/body/ppermute | solution.py:26
  45.1 2.7 %collective-permute-done.1 = bf16[128,128]{1,0:T(8,128)(2,1)S(1)} collective-permute-done((bf16[128,128]{1,0:T(8,128)(2,1)S(1)}, bf16[128,128]{1,0:T(8,128)(2,1)S(1)}, u32[]{:S(2)}, u32[]{:S(2)}) %collective-permute-start.1) | collective-permute-done | bytes 32800 | tf_op jit(solution)/shard_map/while/body/ppermute | solution.py:26
  47.8 1.2 %collective-permute-done.3 = bf16[128,128]{1,0:T(8,128)(2,1)S(1)} collective-permute-done((bf16[128,128]{1,0:T(8,128)(2,1)S(1)}, bf16[128,128]{1,0:T(8,128)(2,1)S(1)}, u32[]{:S(2)}, u32[]{:S(2)}) %collective-permute-start.3) | collective-permute-done | bytes 32800 | tf_op jit(solution)/shard_map/while/body/ppermute | solution.py:26
  49.7 0.9 %pad_maximum_fusion.1 = bf16[128,1024]{1,0:T(8,128)(2,1)S(1)} fusion(bf16[128,256]{1,0:T(8,128)(2,1)} %get-tuple-element.106.kv_ref, bf16[128,768]{1,0:T(8,128)(2,1)S(1)} %product.4), kind=kLoop, calls=%fused_computation.11 | loop fusion | flops 524288 | bytes 524288 | tf_op jit(solution)/shard_map/concatenate | solution.py:294
  50.6 4.3 %collective-permute-done.14.first_ref = bf16[128,3328]{1,0:T(8,128)(2,1)} collective-permute-done((bf16[128,3328]{1,0:T(8,128)(2,1)S(1)}, bf16[128,3328]{1,0:T(8,128)(2,1)}, u32[]{:S(2)}, u32[]{:S(2)}) %collective-permute-start.14) | collective-permute-done | bytes 852000 | tf_op jit(solution)/shard_map/ppermute | solution.py:26
  55.0 1.5 %collective-permute-start.16 = (bf16[128,1024]{1,0:T(8,128)(2,1)S(1)}, bf16[128,1024]{1,0:T(8,128)(2,1)S(1)}, u32[]{:S(2)}, u32[]{:S(2)}) collective-permute-start(bf16[128,1024]{1,0:T(8,128)(2,1)S(1)} %pad_maximum_fusion.1), channel_id=1, source_target_pairs={{0,2},{1,3},{2,0},{3,1},{4,6},{5,7},{6,4},{7,5},{8,10},{9,11},{10,... | collective-permute-start | bytes 786440 | tf_op jit(solution)/shard_map/ppermute | solution.py:26
  56.5 1.6 %copy-done.2 = bf16[256,4096]{1,0:T(8,128)(2,1)S(1)} copy-done((bf16[256,4096]{1,0:T(8,128)(2,1)S(1)}, bf16[256,4096]{1,0:T(8,128)(2,1)}, u32[]{:S(2)}) %copy-start.2) | copy-done | bytes 2097176
  58.1 0.7 %product.5.acc_ref = f32[128,4096]{1,0:T(8,128)S(1)} custom-call(bf16[128,512]{1,0:T(8,128)(2,1)S(1)} %get-tuple-element.108.dq_ref, bf16[256,4096]{1,0:T(8,128)(2,1)S(1)} %copy-done.2, bf16[256,4096]{1,0:T(8,128)(2,1)S(1)} %collective-permute-done.15.wo_ref), custom_call_target="tpu_custom_call" | custom-call | flops 536870912 | bytes 4194304 | tf_op jit(solution)/shard_map/product/pallas_call | solution.py:181
  58.8 4.0 %collective-permute-done.16.second_ref = bf16[128,1024]{1,0:T(8,128)(2,1)S(1)} collective-permute-done((bf16[128,1024]{1,0:T(8,128)(2,1)S(1)}, bf16[128,1024]{1,0:T(8,128)(2,1)S(1)}, u32[]{:S(2)}, u32[]{:S(2)}) %collective-permute-start.16) | collective-permute-done | bytes 262176 | tf_op jit(solution)/shard_map/ppermute | solution.py:26
  62.8 2.4 %finish.1 = bf16[128,4096]{1,0:T(8,128)(2,1)} custom-call(s32[1]{0:T(128)} %bitcast.4.core_ref, bf16[128,256]{1,0:T(8,128)(2,1)S(1)} %copy-done.7, bf16[256,4096]{1,0:T(8,128)(2,1)S(1)} %copy-done, f32[128,4096]{1,0:T(8,128)S(1)} %product.5.acc_ref, bf16[128,3328]{1,0:T(8,128)(2,1)} %collective-permute-done.14.first_ref, ...), custom_call_target="tpu_custom_call" | custom-call | flops 268435456 | bytes 5242880 | tf_op jit(solution)/shard_map/finish/pallas_call | solution.py:227
  (51 shorter events, 5.4 us)
Async XLA Ops:
  1.7 14.0 %collective-permute-start.5 = (bf16[144,128]{1,0:T(8,128)(2,1)S(1)}, bf16[144,128]{1,0:T(8,128)(2,1)S(1)}, u32[]{:S(2)}, u32[]{:S(2)}) collective-permute-start(bf16[144,128]{1,0:T(8,128)(2,1)S(1)} %get-tuple-element.139), channel_id=1, source_target_pairs={{0,16},{4,20},{8,24},{12,28},{16,0},{20,4},{24,8},{28,12},{1,17},{... | collective-permute-start | bytes 110600 | tf_op jit(solution)/shard_map/ppermute | solution.py:26
  5.8 9.9 %collective-permute-start.4 = (bf16[144,128]{1,0:T(8,128)(2,1)S(1)}, bf16[144,128]{1,0:T(8,128)(2,1)S(1)}, u32[]{:S(2)}, u32[]{:S(2)}) collective-permute-start(bf16[144,128]{1,0:T(8,128)(2,1)S(1)} %get-tuple-element.139), channel_id=1, source_target_pairs={{0,8},{4,12},{8,0},{12,4},{16,24},{20,28},{24,16},{28,20},{1,9},{5... | collective-permute-start | bytes 110600 | tf_op jit(solution)/shard_map/ppermute | solution.py:26
  7.4 8.4 %collective-permute-start.6 = (bf16[144,128]{1,0:T(8,128)(2,1)S(1)}, bf16[144,128]{1,0:T(8,128)(2,1)S(1)}, u32[]{:S(2)}, u32[]{:S(2)}) collective-permute-start(bf16[144,128]{1,0:T(8,128)(2,1)S(1)} %get-tuple-element.139), channel_id=1, source_target_pairs={{0,24},{4,28},{8,16},{12,20},{16,8},{20,12},{24,0},{28,4},{1,25},{... | collective-permute-start | bytes 110600 | tf_op jit(solution)/shard_map/ppermute | solution.py:26
  7.4 8.4 %collective-permute-start.7 = (bf16[128,256]{1,0:T(8,128)(2,1)}, bf16[128,256]{1,0:T(8,128)(2,1)S(1)}, u32[]{:S(2)}, u32[]{:S(2)}) collective-permute-start(bf16[128,256]{1,0:T(8,128)(2,1)} %param.10), channel_id=1, source_target_pairs={{0,1},{1,0},{2,3},{3,2},{4,5},{5,4},{6,7},{7,6},{8,9},{9,8},{10,11... | collective-permute-start | bytes 196616 | tf_op jit(solution)/shard_map/ppermute | solution.py:26
  10.4 0.7 %copy-start.3 = (s32[128]{0:T(128)S(1)}, s32[128]{0:T(128)}, u32[]{:S(2)}) copy-start(s32[128]{0:T(128)} %refs_0_.1) | copy-start | bytes 1540
  11.0 4.1 %copy-start.8 = (bf16[128,256]{1,0:T(8,128)(2,1)S(1)}, bf16[128,256]{1,0:T(8,128)(2,1)}, u32[]{:S(2)}) copy-start(bf16[128,256]{1,0:T(8,128)(2,1)} %param.13) | copy-start | bytes 196612
  15.2 1.5 %collective-permute-start.8 = (bf16[128,256]{1,0:T(8,128)(2,1)S(1)}, bf16[128,256]{1,0:T(8,128)(2,1)S(1)}, u32[]{:S(2)}, u32[]{:S(2)}) collective-permute-start(bf16[128,256]{1,0:T(8,128)(2,1)S(1)} %copy-done.8), channel_id=1, source_target_pairs={{0,1},{1,0},{2,3},{3,2},{4,5},{5,4},{6,7},{7,6},{8,9},{9,8},{10,11... | collective-permute-start | bytes 196616 | tf_op jit(solution)/shard_map/ppermute | solution.py:26
  16.7 10.9 %collective-permute-start.12 = (bf16[256,4096]{1,0:T(8,128)(2,1)}, bf16[256,4096]{1,0:T(8,128)(2,1)}, u32[]{:S(2)}, u32[]{:S(2)}) collective-permute-start(bf16[256,4096]{1,0:T(8,128)(2,1)} %get-tuple-element.103), channel_id=1, source_target_pairs={{0,1},{1,0},{2,3},{3,2},{4,5},{5,4},{6,7},{7,6},{8,9},{9,8},{10,11... | collective-permute-start | bytes 6291464 | tf_op jit(solution)/shard_map/ppermute | solution.py:26
  17.1 5.9 %collective-permute-start.10 = (bf16[4,144,128]{2,1,0:T(8,128)(2,1)S(1)}, bf16[4,144,128]{2,1,0:T(8,128)(2,1)S(1)}, u32[]{:S(2)}, u32[]{:S(2)}) collective-permute-start(bf16[4,144,128]{2,1,0:T(8,128)(2,1)S(1)} %pad_maximum_fusion.2.refs_0_), channel_id=1, source_target_pairs={{0,4},{4,0},{8,12},{12,8},{16,20},{20,16},{24,28},{28,24},{1,5},{5... | collective-permute-start | bytes 442376 | tf_op jit(solution)/shard_map/ppermute | solution.py:26
  18.9 4.6 %collective-permute-start.9 = (bf16[4,144,128]{2,1,0:T(8,128)(2,1)S(1)}, bf16[4,144,128]{2,1,0:T(8,128)(2,1)S(1)}, u32[]{:S(2)}, u32[]{:S(2)}) collective-permute-start(bf16[4,144,128]{2,1,0:T(8,128)(2,1)S(1)} %pad_maximum_fusion.2.refs_0_), channel_id=1, source_target_pairs={{0,1},{1,0},{2,3},{3,2},{4,5},{5,4},{6,7},{7,6},{8,9},{9,8},{10,11... | collective-permute-start | bytes 442376 | tf_op jit(solution)/shard_map/ppermute | solution.py:26
  21.7 1.3 %copy-start.5 = (bf16[256,4096]{1,0:T(8,128)(2,1)}, bf16[256,4096]{1,0:T(8,128)(2,1)S(1)}, u32[]{:S(2)}) copy-start(bf16[256,4096]{1,0:T(8,128)(2,1)S(1)} %get-tuple-element.112) | copy-start | bytes 6291460
  23.0 6.4 %copy-start.1 = (bf16[256,4096]{1,0:T(8,128)(2,1)}, bf16[256,4096]{1,0:T(8,128)(2,1)S(1)}, u32[]{:S(2)}) copy-start(bf16[256,4096]{1,0:T(8,128)(2,1)S(1)} %get-tuple-element.111.wm_ref) | copy-start | bytes 6291460
  23.0 1.5 %collective-permute-start.11 = (bf16[4,144,128]{2,1,0:T(8,128)(2,1)S(1)}, bf16[4,144,128]{2,1,0:T(8,128)(2,1)S(1)}, u32[]{:S(2)}, u32[]{:S(2)}) collective-permute-start(bf16[4,144,128]{2,1,0:T(8,128)(2,1)S(1)} %collective-permute-done.10.refs_2_), channel_id=1, source_target_pairs={{0,1},{1,0},{2,3},{3,2},{4,5},{5,4},{6,7},{7,6},{8,9},{9,8},{10,11... | collective-permute-start | bytes 442376 | tf_op jit(solution)/shard_map/ppermute | solution.py:26
  29.4 3.9 %copy-start.4 = (s32[128]{0:T(128)S(1)}, s32[128]{0:T(128)}, u32[]{:S(2)}) copy-start(s32[128]{0:T(128)} %refs_0_.1) | copy-start | bytes 1540
  29.5 8.8 %copy-start.6 = (bf16[4,128,128]{2,1,0:T(8,128)(2,1)S(1)}, bf16[4,128,128]{2,1,0:T(8,128)(2,1)}, u32[]{:S(2)}) copy-start(bf16[4,128,128]{2,1,0:T(8,128)(2,1)} %get-tuple-element.185) | copy-start | bytes 393220
  31.7 5.9 %collective-permute-start.13 = (bf16[4,128,128]{2,1,0:T(8,128)(2,1)S(1)}, bf16[4,128,128]{2,1,0:T(8,128)(2,1)}, u32[]{:S(2)}, u32[]{:S(2)}) collective-permute-start(bf16[4,128,128]{2,1,0:T(8,128)(2,1)S(1)} %get-tuple-element.105), channel_id=1, source_target_pairs={{0,4},{4,0},{8,12},{12,8},{16,20},{20,16},{24,28},{28,24},{1,5},{5... | collective-permute-start | bytes 393224 | tf_op jit(solution)/shard_map/while/body/ppermute | solution.py:26
  33.4 23.1 %collective-permute-start.15 = (bf16[256,4096]{1,0:T(8,128)(2,1)}, bf16[256,4096]{1,0:T(8,128)(2,1)S(1)}, u32[]{:S(2)}, u32[]{:S(2)}) collective-permute-start(bf16[256,4096]{1,0:T(8,128)(2,1)} %copy-done.5), channel_id=1, source_target_pairs={{0,1},{1,0},{2,3},{3,2},{4,5},{5,4},{6,7},{7,6},{8,9},{9,8},{10,11... | collective-permute-start | bytes 6291464 | tf_op jit(solution)/shard_map/ppermute | solution.py:26
  33.5 21.5 %collective-permute-start.14 = (bf16[128,3328]{1,0:T(8,128)(2,1)S(1)}, bf16[128,3328]{1,0:T(8,128)(2,1)}, u32[]{:S(2)}, u32[]{:S(2)}) collective-permute-start(bf16[128,3328]{1,0:T(8,128)(2,1)S(1)} %product.3), channel_id=1, source_target_pairs={{0,2},{1,3},{2,0},{3,1},{4,6},{5,7},{6,4},{7,5},{8,10},{9,11},{10,... | collective-permute-start | bytes 2555912 | tf_op jit(solution)/shard_map/ppermute | solution.py:26
  39.2 5.8 %collective-permute-start = (bf16[128,128]{1,0:T(8,128)(2,1)S(1)}, bf16[128,128]{1,0:T(8,128)(2,1)S(1)}, u32[]{:S(2)}, u32[]{:S(2)}) collective-permute-start(bf16[128,128]{1,0:T(8,128)(2,1)S(1)} %get-tuple-element.179), channel_id=1, source_target_pairs={{0,24},{4,28},{8,16},{12,20},{16,8},{20,12},{24,0},{28,4},{1,25},{... | collective-permute-start | bytes 98312 | tf_op jit(solution)/shard_map/while/body/ppermute | solution.py:26
  42.9 4.8 %collective-permute-start.1 = (bf16[128,128]{1,0:T(8,128)(2,1)S(1)}, bf16[128,128]{1,0:T(8,128)(2,1)S(1)}, u32[]{:S(2)}, u32[]{:S(2)}) collective-permute-start(bf16[128,128]{1,0:T(8,128)(2,1)S(1)} %get-tuple-element.180), channel_id=1, source_target_pairs={{0,16},{4,20},{8,24},{12,28},{16,0},{20,4},{24,8},{28,12},{1,17},{... | collective-permute-start | bytes 98312 | tf_op jit(solution)/shard_map/while/body/ppermute | solution.py:26
  42.9 4.8 %collective-permute-start.2 = (bf16[128,128]{1,0:T(8,128)(2,1)S(1)}, bf16[128,128]{1,0:T(8,128)(2,1)S(1)}, u32[]{:S(2)}, u32[]{:S(2)}) collective-permute-start(bf16[128,128]{1,0:T(8,128)(2,1)S(1)} %get-tuple-element.181), channel_id=1, source_target_pairs={{0,8},{4,12},{8,0},{12,4},{16,24},{20,28},{24,16},{28,20},{1,9},{5... | collective-permute-start | bytes 98312 | tf_op jit(solution)/shard_map/while/body/ppermute | solution.py:26
  47.8 1.3 %collective-permute-start.3 = (bf16[128,128]{1,0:T(8,128)(2,1)S(1)}, bf16[128,128]{1,0:T(8,128)(2,1)S(1)}, u32[]{:S(2)}, u32[]{:S(2)}) collective-permute-start(bf16[128,128]{1,0:T(8,128)(2,1)S(1)} %fusion.15), channel_id=1, source_target_pairs={{0,1},{1,0},{2,3},{3,2},{4,5},{5,4},{6,7},{7,6},{8,9},{9,8},{10,11... | collective-permute-start | bytes 98312 | tf_op jit(solution)/shard_map/while/body/ppermute | solution.py:26
  49.7 13.2 %copy-start.7 = (bf16[128,256]{1,0:T(8,128)(2,1)S(1)}, bf16[128,256]{1,0:T(8,128)(2,1)}, u32[]{:S(2)}) copy-start(bf16[128,256]{1,0:T(8,128)(2,1)} %get-tuple-element.106.kv_ref) | copy-start | bytes 196612
  50.6 12.2 %copy-start = (bf16[256,4096]{1,0:T(8,128)(2,1)S(1)}, bf16[256,4096]{1,0:T(8,128)(2,1)}, u32[]{:S(2)}) copy-start(bf16[256,4096]{1,0:T(8,128)(2,1)} %w_ref.5) | copy-start | bytes 6291460
  55.0 7.9 %collective-permute-start.16 = (bf16[128,1024]{1,0:T(8,128)(2,1)S(1)}, bf16[128,1024]{1,0:T(8,128)(2,1)S(1)}, u32[]{:S(2)}, u32[]{:S(2)}) collective-permute-start(bf16[128,1024]{1,0:T(8,128)(2,1)S(1)} %pad_maximum_fusion.1), channel_id=1, source_target_pairs={{0,2},{1,3},{2,0},{3,1},{4,6},{5,7},{6,4},{7,5},{8,10},{9,11},{10,... | collective-permute-start | bytes 786440 | tf_op jit(solution)/shard_map/ppermute | solution.py:26
  56.5 1.6 %copy-start.2 = (bf16[256,4096]{1,0:T(8,128)(2,1)S(1)}, bf16[256,4096]{1,0:T(8,128)(2,1)}, u32[]{:S(2)}) copy-start(bf16[256,4096]{1,0:T(8,128)(2,1)} %copy-done.1) | copy-start | bytes 6291460

commit v8 on v7

--- a/solution.py
+++ b/solution.py
@@ -79,28 +79,34 @@
     )(jnp.stack(blocks), w_query, after)
 
 
-def attention_kernel(core_ref, row_ref, query_ref, grad_ref, *refs):
-    groups = ((refs[0], refs[1], refs[5]), (refs[2], refs[3], refs[6]))
-    dq_ref = refs[4]
-    s_ref, dp_ref = refs[7:]
-    half, rows, size = groups[0][2].shape
+def attention_kernel(core_ref, pos_ref, doc_ref, mine_ref, swap_ref, *refs):
+    groups = (refs[0:2], refs[2:4])
+    dq_ref, back_ref, s_ref, dp_ref = refs[4:]
+    count, rows, size = back_ref.shape
+    half = count // 2
+    heads = mine_ref.shape[2] // size
     is_key = core_ref[0] == 0
     inv_root = 1.0 / math.sqrt(size)
-    query = query_ref[...]
-    grad = grad_ref[...]
+
+    def stack(which):
+        parts = [
+            ref[which, :, h * size : (h + 1) * size] for ref in (mine_ref, swap_ref) for h in range(heads)
+        ]
+        return jnp.concatenate(parts, axis=0)
+
+    query = stack(0)
+    grad = stack(1)
     wide = query.shape[0]
-    last = row_ref[0:1, :]
-    first = row_ref[1:2, :]
+    last = jnp.concatenate([pos_ref[...].astype(jnp.float32)] * (2 * heads), axis=1)
+    first = jnp.concatenate([(doc_ref[...] * RUN).astype(jnp.float32)] * (2 * heads), axis=1)
     offset = lax.broadcasted_iota(jnp.int32, (RUN, wide), 0).astype(jnp.float32)
 
     def everywhere(body, state):
-        for group, (here_ref, there_ref, back_ref) in enumerate(groups):
-            state = each(
-                half, lambda s, now: body(s, group * half + s, here_ref, there_ref, back_ref, now), state
-            )
+        for group, (here_ref, there_ref) in enumerate(groups):
+            state = each(half, lambda s, now: body(s, group * half + s, here_ref, there_ref, now), state)
         return state
 
-    def scores(s, slot, here_ref, there_ref, back_ref, top):
+    def scores(s, slot, here_ref, there_ref, top):
         here = here_ref[s, 0:rows, :]
         there = there_ref[s, 0:rows, :]
         key = jnp.where(is_key, here, there)
@@ -128,16 +134,16 @@
         return total, mixed
 
     zeros = jnp.zeros((1, wide), jnp.float32)
-    total, mixed = each(2 * half, weights, (zeros, zeros))
+    total, mixed = each(count, weights, (zeros, zeros))
     scale = 1.0 / total
     delta = mixed * scale
     other = jnp.where(is_key, query, grad)
 
-    def gradients(s, slot, here_ref, there_ref, back_ref, dq):
+    def gradients(s, slot, here_ref, there_ref, dq):
         prob = s_ref[slot] * scale
         dscore = (prob * (dp_ref[slot] - delta)).astype(jnp.bfloat16)
         picked = jnp.where(is_key, dscore, prob.astype(jnp.bfloat16))
-        back_ref[s] = dot(picked, other, ((1,), (0,))).astype(jnp.bfloat16)
+        back_ref[slot] = dot(picked, other, ((1,), (0,))).astype(jnp.bfloat16)
         key = jnp.where(is_key, here_ref[s, 0:rows, :], there_ref[s, 0:rows, :])
         return dq + dot(key, dscore, ((0,), (0,)))
 
@@ -147,16 +153,19 @@
         dq_ref[:, part * size : (part + 1) * size] = block.T.astype(jnp.bfloat16)
 
 
-def attention(core, row_info, query, grad, pieces, rows):
+def attention(core, positions, doc_ids, mine, swap, pieces):
     half, _, size = pieces[0].shape
-    wide = query.shape[0]
+    _, rows, width = mine.shape
     count = 2 * half
+    wide = 2 * rows * (width // size)
     return pl.pallas_call(
         attention_kernel,
-        out_shape=[jax.ShapeDtypeStruct((rows, wide // rows * size), jnp.bfloat16)]
-        + [jax.ShapeDtypeStruct((half, rows, size), jnp.bfloat16)] * 2,
-        in_specs=[SMEM] + [pl.BlockSpec()] * 7,
-        out_specs=[pl.BlockSpec()] * 3,
+        out_shape=[
+            jax.ShapeDtypeStruct((rows, 2 * width), jnp.bfloat16),
+            jax.ShapeDtypeStruct((count, rows, size), jnp.bfloat16),
+        ],
+        in_specs=[SMEM] + [pl.BlockSpec()] * 8,
+        out_specs=[pl.BlockSpec()] * 2,
         scratch_shapes=[pltpu.VMEM((count, rows, wide), jnp.float32)] * 2,
         compiler_params=params(8 + count * rows * wide // 2**17),
         cost_estimate=pl.CostEstimate(
@@ -165,7 +174,7 @@
             transcendentals=count * rows * wide,
         ),
         name="attention",
-    )(core, row_info, query, grad, *pieces)
+    )(core, positions.reshape(1, rows), doc_ids.reshape(1, rows), mine, swap, *pieces)
 
 
 def product_kernel(first, dq_ref, wm_ref, wo_ref, out_ref):
@@ -189,6 +198,40 @@
         ),
         name="product",
     )(dq, w_mine, w_other)
+
+
+def own_kernel(block_ref, dq_ref, w_ref, *refs):
+    out_ref, wm_ref, sems = refs[TILES:]
+    depth, share = wm_ref.shape
+    tile = share // TILES
+    copies = []
+    for i in range(TILES):
+        at = pl.multiple_of(block_ref[0] * share + i * tile, tile)
+        target = wm_ref.at[:, i * tile : (i + 1) * tile]
+        copies.append(pltpu.make_async_copy(w_ref.at[:, pl.ds(at, tile)], target, sems.at[i]))
+        copies[i].start()
+    for i in range(TILES):
+        at = slice(i * tile, (i + 1) * tile)
+        acc = dot(dq_ref[:, depth:], refs[i][...], ((1,), (0,)))
+        copies[i].wait()
+        out_ref[:, at] = acc + dot(dq_ref[:, 0:depth], wm_ref[:, at], ((1,), (0,)))
+
+
+def own(block, dq, w_query, w_other):
+    rows, depth = dq.shape
+    share = TILES * w_other[0].shape[1]
+    return pl.pallas_call(
+        own_kernel,
+        out_shape=jax.ShapeDtypeStruct((rows, share), jnp.float32),
+        in_specs=[SMEM, pl.BlockSpec(), HBM] + [pl.BlockSpec()] * TILES,
+        out_specs=pl.BlockSpec(),
+        scratch_shapes=[pltpu.VMEM((depth // 2, share), w_query.dtype), pltpu.SemaphoreType.DMA((TILES,))],
+        compiler_params=params(48),
+        cost_estimate=pl.CostEstimate(
+            flops=2 * rows * depth * share, bytes_accessed=2 * depth * share, transcendentals=0
+        ),
+        name="own",
+    )(block, dq, w_query, *w_other)
 
 
 def finish_kernel(core_ref, kv_ref, w_ref, acc_ref, first_ref, second_ref, out_ref, hold_ref, sems):
@@ -245,56 +288,44 @@
     share = w_kv.shape[1]
     local_heads = queries.shape[1] // keys.shape[1]
 
-    q_other = swapped(queries, "head", 1)
-    g_other = swapped(dout, "head", 1)
     piece = pack(core, positions, keys, values)
     along_z = [piece] + [swapped(piece, "ctx", 2 * s) for s in range(1, half)]
-
-    def stacked(*arrays):
-        return jnp.concatenate([part for one in arrays for part in jnp.split(one, local_heads, axis=1)], axis=0)
-
-    query = stacked(queries, q_other)
-    grad = stacked(dout, g_other)
-    bounds = jnp.stack([positions, doc_ids * RUN]).astype(jnp.float32)
-    row_info = jnp.tile(bounds, (1, 2 * local_heads))
-    far = carve([head ^ 3, head ^ 2], w_query, share, positions)
-    here_z, query, grad, row_info, far_send, far_mine = lax.optimization_barrier(
-        (jnp.stack(along_z), query, grad, row_info, *far)
-    )
+    both = jnp.stack([queries, dout])
+    swap = swapped(both, "head", 1)
+    (far_send,) = carve([head ^ 3], w_query, share, both)
+    here_z, swap, far_send = lax.optimization_barrier((jnp.stack(along_z), swap, far_send))
     here_x = swapped(here_z, "ctx", 1)
     far_other = swapped(far_send, "head", 1)
     there_z = swapped(here_z, "head", 1)
-    near = carve([head ^ 1, head], w_query, share, here_z)
-    here_x, near_send, near_mine = lax.optimization_barrier((here_x, *near))
+    (far_mine,) = carve([head ^ 2], w_query, share, here_z)
+    here_x, far_mine = lax.optimization_barrier((here_x, far_mine))
     there_x = swapped(here_x, "head", 1)
-    dq, back_z, back_x = attention(
-        core, row_info, query, grad, (here_z, there_z, here_x, there_x), queries.shape[0]
-    )
+    dq, back = attention(core, positions, doc_ids, both, swap, (here_z, there_z, here_x, there_x))
 
     cut = CHUNKS[0] * (share // sum(CHUNKS))
     first_part = product(dq, far_mine, far_other, 0, cut, jnp.bfloat16)
     second_part = product(dq, far_mine, far_other, cut, share - cut, jnp.bfloat16)
     first = swapped(first_part, "head", 2)
-    dq, near_send = lax.optimization_barrier((dq, near_send))
-    near_other = swapped(near_send, "head", 1)
 
     def exchange(trip, kv):
-        sent = lax.dynamic_slice_in_dim(back_x, trip * half, half, axis=0)
-        pair = back_z.astype(jnp.float32) + swapped(sent, "ctx", 1).astype(jnp.float32)
+        sent = lax.dynamic_slice_in_dim(back, (1 - trip) * half, half, axis=0)
+        pair = back[:half].astype(jnp.float32) + swapped(sent, "ctx", 1).astype(jnp.float32)
         mine = pair[0]
         for s in range(1, half):
             mine = mine + swapped(pair[s].astype(jnp.bfloat16), "ctx", 2 * s).astype(jnp.float32)
         mine = mine.astype(jnp.bfloat16)
         return jnp.concatenate([mine, swapped(mine, "head", 1)], axis=1)
 
-    back_x, back_z, first_part, second_part = lax.optimization_barrier((back_x, back_z, first_part, second_part))
+    back, first_part, second_part = lax.optimization_barrier((back, first_part, second_part))
     trips = 1 + jnp.minimum(positions[0], 0)
     kv = lax.fori_loop(0, trips, exchange, jnp.zeros((queries.shape[0], 2 * keys.shape[1]), jnp.bfloat16))
 
+    near_send = carve([(head ^ 1) * TILES + i for i in range(TILES)], w_query, share // TILES, kv)
+    near_other = [swapped(one, "head", 1) for one in near_send]
     second_part = jnp.concatenate([second_part, kv], axis=1)
-    second_part, first, near_mine = lax.optimization_barrier((second_part, first, near_mine))
+    second_part, first, dq = lax.optimization_barrier((second_part, first, dq))
     second = swapped(second_part, "head", 2)
-    acc = product(dq, near_mine, near_other, 0, share, jnp.float32)
+    acc = own(head.reshape(1), dq, w_query, near_other)
     return finish(core, kv, w_kv, acc, first, second)
 
 

time: 65.8 us -> 58.3 us (0.89)
  local copies, waits for them, and re-layouts: 6.55 us -> 1.41 us
  other arithmetic: 5.03 us -> 2.7 us
  starting transfers between devices: 18.2 us -> 17.3 us
  Pallas kernels: 17.2 us -> 18 us
    unnamed x20 -> x8, local copies, waits for them, and re-layouts: 3.6 us -> 0.01 us
    pallas_call x1 -> x2, Pallas kernels: 3.04 us -> 4.98 us  [the longest x1 2.6 us: own(): pl.pallas_call(own_kernel, out_shape=jax.ShapeDtypeStruct((rows, share),...]
    split x4 -> x0, local copies, waits for them, and re-layouts: 1.57 us -> none  [stacked(): jnp.split(one, local_heads, axis=1)]
    pallas_call x1, Pallas kernels: 2.42 us -> 1.33 us  [finish(): pl.pallas_call(finish_kernel, out_shape=jax.ShapeDtypeStruct((rows, share...]
    ppermute x17 -> x19, starting transfers between devices: 18.2 us -> 17.3 us  [swapped(): lax.ppermute(value, axis, [(source, source ^ bits) for source in range(co...]
    concatenate x1, other arithmetic: 0.94 us -> 0.02 us  [on_device(): second_part = jnp.concatenate([second_part, kv], axis=1)]
    another operation x2, other arithmetic: 1.6 us -> 0.92 us  [the longest x1 0.88 us: on_device(): both = jnp.stack([queries, dout])]
    convert_element_type x1 -> x0, other arithmetic: 0.66 us -> none  [on_device(): bounds = jnp.stack([positions, doc_ids * RUN]).astype(jnp.float32)]
  transfers between devices with their start and end apart: 17 -> 19, of which waited for: 8 -> 11; matrix products, arithmetic and copies ran while one was open for 10% -> 4% of each run, Pallas kernels for 16% -> 23%
where the time goes in v8:
time: 58.3 us; the launch traced here: 57.9 us
  waiting for transfers between devices  18.3 us (31%)
  Pallas kernels  18 us (31%)
  starting transfers between devices  17.3 us (30%)
  other arithmetic  2.7 us (5%)
  local copies, waits for them, and re-layouts  1.41 us (2%)
    ppermute x19, waiting for transfers between devices, swapped(): lax.ppermute(value, axis, [(source, source ^ bits) for source in range(co...  18.3 us
    ppermute x19, starting transfers between devices, swapped(): lax.ppermute(value, axis, [(source, source ^ bits) for source in range(co...  17.3 us
    pallas_call x3, Pallas kernels, carve(): pl.pallas_call(carve_kernel, out_shape=[block] * count, in_specs=[SMEM, H...  6.74 us
    pallas_call x2, Pallas kernels, product(): pl.pallas_call(functools.partial(product_kernel, first), out_shape=jax.Sh...  4.97 us
    pallas_call x1, Pallas kernels, own(): pl.pallas_call(own_kernel, out_shape=jax.ShapeDtypeStruct((rows, share),...  2.6 us
    pallas_call x1, Pallas kernels, attention(): pl.pallas_call(attention_kernel, out_shape=[jax.ShapeDtypeStruct((rows, 2...  2.37 us
    pallas_call x1, Pallas kernels, finish(): pl.pallas_call(finish_kernel, out_shape=jax.ShapeDtypeStruct((rows, share...  1.33 us
  transfers between devices with their start and end apart: 19, of which 11 were waited for; matrix products, arithmetic and copies ran while one was open for 4% of the time, Pallas kernels for 23%

profile of v8, /device:TPU:0, one launch (start us, length us, event | category | flops | bytes accessed | tf_op | source)
XLA Modules:
  0.0 57.9 jit_solution(14450358649967632490)
XLA Ops:
  0.0 0.7 %reshape.26 = s32[2,64]{1,0:T(2,128)S(1)} reshape(s32[128]{0:T(128)} %param.14) | data formatting | bytes 1024 | tf_op jit(solution)/shard_map/reshape | solution.py:44
  0.9 0.8 %broadcast_select_fusion = bf16[128,128]{1,0:T(8,128)(2,1)S(1)} fusion(bf16[128,128]{1,0:T(8,128)(2,1)} %param.11, bf16[128,128]{1,0:T(8,128)(2,1)} %param.12, pred[]{:T(512)} %bitcast.10), kind=kLoop, calls=%fused_computation.16 | loop fusion | flops 16384 | bytes 98305 | tf_op jit(solution)/shard_map/jit(_where)/select_n | solution.py:43
  1.7 3.1 %collective-permute-start.5 = (bf16[144,128]{1,0:T(8,128)(2,1)S(1)}, bf16[144,128]{1,0:T(8,128)(2,1)S(1)}, u32[]{:S(2)}, u32[]{:S(2)}) collective-permute-start(bf16[144,128]{1,0:T(8,128)(2,1)S(1)} %get-tuple-element.74), channel_id=1, source_target_pairs={{0,8},{4,12},{8,0},{12,4},{16,24},{20,28},{24,16},{28,20},{1,9},{5... | collective-permute-start | bytes 110600 | tf_op jit(solution)/shard_map/ppermute | solution.py:26
  4.8 2.6 %collective-permute-start.6 = (bf16[144,128]{1,0:T(8,128)(2,1)S(1)}, bf16[144,128]{1,0:T(8,128)(2,1)S(1)}, u32[]{:S(2)}, u32[]{:S(2)}) collective-permute-start(bf16[144,128]{1,0:T(8,128)(2,1)S(1)} %get-tuple-element.74), channel_id=1, source_target_pairs={{0,16},{4,20},{8,24},{12,28},{16,0},{20,4},{24,8},{28,12},{1,17},{... | collective-permute-start | bytes 110600 | tf_op jit(solution)/shard_map/ppermute | solution.py:26
  7.4 0.9 %pad_maximum_fusion.3.refs_0_.mine_ref = bf16[2,128,256]{2,1,0:T(8,128)(2,1)S(1)} fusion(bf16[1,128,256]{2,1,0:T(8,128)(2,1)} %bitcast.43, bf16[1,128,256]{2,1,0:T(8,128)(2,1)} %bitcast.44), kind=kLoop, calls=%fused_computation.14 | loop fusion | flops 65536 | bytes 262144 | tf_op jit(solution)/shard_map/stack | solution.py:293
  8.4 2.9 %carve.3 = bf16[256,4096]{1,0:T(8,128)(2,1)} custom-call(s32[1]{0:T(128)} %bitcast.15.block_ref, bf16[256,16384]{1,0:T(8,128)(2,1)} %w_ref.8, bf16[2,128,256]{2,1,0:T(8,128)(2,1)S(1)} %pad_maximum_fusion.3.refs_0_.mine_ref), custom_call_target="tpu_custom_call" | custom-call | bytes 4194304 | tf_op jit(solution)/shard_map/carve/pallas_call | solution.py:68
  11.3 1.9 %collective-permute-done.7 = bf16[144,128]{1,0:T(8,128)(2,1)S(1)} collective-permute-done((bf16[144,128]{1,0:T(8,128)(2,1)S(1)}, bf16[144,128]{1,0:T(8,128)(2,1)S(1)}, u32[]{:S(2)}, u32[]{:S(2)}) %collective-permute-start.7) | collective-permute-done | bytes 36896 | tf_op jit(solution)/shard_map/ppermute | solution.py:26
  13.3 1.6 %collective-permute-start.10 = (bf16[4,144,128]{2,1,0:T(8,128)(2,1)S(1)}, bf16[4,144,128]{2,1,0:T(8,128)(2,1)S(1)}, u32[]{:S(2)}, u32[]{:S(2)}) collective-permute-start(bf16[4,144,128]{2,1,0:T(8,128)(2,1)S(1)} %pad_maximum_fusion.2.refs_0_), channel_id=1, source_target_pairs={{0,4},{4,0},{8,12},{12,8},{16,20},{20,16},{24,28},{28,24},{1,5},{5... | collective-permute-start | bytes 442376 | tf_op jit(solution)/shard_map/ppermute | solution.py:26
  15.0 1.6 %carve.4.wm_ref = bf16[256,4096]{1,0:T(8,128)(2,1)S(1)} custom-call(s32[1]{0:T(128)} %bitcast.16.block_ref, bf16[256,16384]{1,0:T(8,128)(2,1)} %w_ref.8, bf16[4,144,128]{2,1,0:T(8,128)(2,1)S(1)} %pad_maximum_fusion.2.refs_0_), custom_call_target="tpu_custom_call" | custom-call | bytes 4194304 | tf_op jit(solution)/shard_map/carve/pallas_call | solution.py:68
  16.6 3.0 %collective-permute-done.10.refs_2_ = bf16[4,144,128]{2,1,0:T(8,128)(2,1)S(1)} collective-permute-done((bf16[4,144,128]{2,1,0:T(8,128)(2,1)S(1)}, bf16[4,144,128]{2,1,0:T(8,128)(2,1)S(1)}, u32[]{:S(2)}, u32[]{:S(2)}) %collective-permute-start.10) | collective-permute-done | bytes 147488 | tf_op jit(solution)/shard_map/ppermute | solution.py:26
  19.7 1.2 %collective-permute-done.11.refs_3_ = bf16[4,144,128]{2,1,0:T(8,128)(2,1)S(1)} collective-permute-done((bf16[4,144,128]{2,1,0:T(8,128)(2,1)S(1)}, bf16[4,144,128]{2,1,0:T(8,128)(2,1)S(1)}, u32[]{:S(2)}, u32[]{:S(2)}) %collective-permute-start.11) | collective-permute-done | bytes 147488 | tf_op jit(solution)/shard_map/ppermute | solution.py:26
  20.9 2.4 %attention.1 = (bf16[128,512]{1,0:T(8,128)(2,1)S(1)}, bf16[8,128,128]{2,1,0:T(8,128)(2,1)S(1)}) custom-call(s32[1]{0:T(128)} %bitcast.4.core_ref, s32[1,128]{1,0:T(1,128)S(1)} %bitcast.41, s32[1,128]{1,0:T(1,128)S(1)} %bitcast.42, bf16[2,128,256]{2,1,0:T(8,128)(2,1)S(1)} %pad_maximum_fusion.3.refs_0_.mine_ref, ...), custom_call_target="tpu_custom_call" | custom-call | flops 671088640 | bytes 1048576 | tf_op jit(solution)/shard_map/attention/pallas_call | solution.py:161
  23.3 3.1 %product.2 = bf16[128,3328]{1,0:T(8,128)(2,1)} custom-call(bf16[128,512]{1,0:T(8,128)(2,1)S(1)} %get-tuple-element.53.dq_ref, bf16[256,4096]{1,0:T(8,128)(2,1)S(1)} %carve.4.wm_ref, bf16[256,4096]{1,0:T(8,128)(2,1)} %collective-permute-done.12.wo_ref), custom_call_target="tpu_custom_call" | custom-call | flops 436207616 | bytes 3407872 | tf_op jit(solution)/shard_map/product/pallas_call | solution.py:190
  26.4 1.5 %collective-permute-start.13 = (bf16[128,3328]{1,0:T(8,128)(2,1)}, bf16[128,3328]{1,0:T(8,128)(2,1)S(1)}, u32[]{:S(2)}, u32[]{:S(2)}) collective-permute-start(bf16[128,3328]{1,0:T(8,128)(2,1)} %product.2), channel_id=1, source_target_pairs={{0,2},{1,3},{2,0},{3,1},{4,6},{5,7},{6,4},{7,5},{8,10},{9,11},{10,... | collective-permute-start | bytes 2555912 | tf_op jit(solution)/shard_map/ppermute | solution.py:26
  28.0 1.9 %product.3 = bf16[128,768]{1,0:T(8,128)(2,1)S(1)} custom-call(bf16[128,512]{1,0:T(8,128)(2,1)S(1)} %get-tuple-element.53.dq_ref, bf16[256,4096]{1,0:T(8,128)(2,1)S(1)} %carve.4.wm_ref, bf16[256,4096]{1,0:T(8,128)(2,1)} %collective-permute-done.12.wo_ref), custom_call_target="tpu_custom_call" | custom-call | flops 100663296 | bytes 786432 | tf_op jit(solution)/shard_map/product/pallas_call | solution.py:190
  29.8 0.6 %broadcast_in_dim.16 = bf16[128,256]{1,0:T(8,128)(2,1)} broadcast(bf16[]{:T(256)} %constant.35.clone.1), dimensions={} | broadcast | bytes 65538 | tf_op jit(solution)/shard_map/broadcast_in_dim | solution.py:321
  30.5 14.2 %while.10 = (s32[]{:T(128)}, bf16[128,256]{1,0:T(8,128)(2,1)}, s32[]{:T(128)}, bf16[8,128,128]{2,1,0:T(8,128)(2,1)S(1)}, s32[]{:T(128)}, /*index=5*/s32[]{:T(128)}, s32[]{:T(128)}, s32[]{:T(128)}) while((s32[]{:T(128)}, bf16[128,256]{1,0:T(8,128)(2,1)}, s32[]{:T(128)}, bf16[8,128,128]{2,1,0:T(8,128)(2,1)S(1)}, s32[]{:T(128)}, ...), condition=%wide.region_1.2_spmd, body=%wide.region_0.1_spmd.sunk | while | flops 507911 | bytes 2490715 | solution.py:321
  30.5 1.6 %collective-permute-start = (bf16[4,128,128]{2,1,0:T(8,128)(2,1)S(1)}, bf16[4,128,128]{2,1,0:T(8,128)(2,1)S(1)}, u32[]{:S(2)}, u32[]{:S(2)}) collective-permute-start(bf16[4,128,128]{2,1,0:T(8,128)(2,1)S(1)} %constant_dynamic-slice_fusion.2), channel_id=1, source_target_pairs={{0,4},{4,0},{8,12},{12,8},{16,20},{20,16},{24,28},{28,24},{1,5},{5... | collective-permute-start | bytes 393224 | tf_op jit(solution)/shard_map/while/body/ppermute | solution.py:26
  32.0 3.8 %collective-permute-done = bf16[4,128,128]{2,1,0:T(8,128)(2,1)S(1)} collective-permute-done((bf16[4,128,128]{2,1,0:T(8,128)(2,1)S(1)}, bf16[4,128,128]{2,1,0:T(8,128)(2,1)S(1)}, u32[]{:S(2)}, u32[]{:S(2)}) %collective-permute-start) | collective-permute-done | bytes 131104 | tf_op jit(solution)/shard_map/while/body/ppermute | solution.py:26
  35.9 2.1 %collective-permute-start.1 = (bf16[128,128]{1,0:T(8,128)(2,1)S(1)}, bf16[128,128]{1,0:T(8,128)(2,1)S(1)}, u32[]{:S(2)}, u32[]{:S(2)}) collective-permute-start(bf16[128,128]{1,0:T(8,128)(2,1)S(1)} %get-tuple-element.106), channel_id=1, source_target_pairs={{0,24},{4,28},{8,16},{12,20},{16,8},{20,12},{24,0},{28,4},{1,25},{... | collective-permute-start | bytes 98312 | tf_op jit(solution)/shard_map/while/body/ppermute | solution.py:26
  37.9 2.4 %collective-permute-start.3 = (bf16[128,128]{1,0:T(8,128)(2,1)S(1)}, bf16[128,128]{1,0:T(8,128)(2,1)S(1)}, u32[]{:S(2)}, u32[]{:S(2)}) collective-permute-start(bf16[128,128]{1,0:T(8,128)(2,1)S(1)} %get-tuple-element.108), channel_id=1, source_target_pairs={{0,8},{4,12},{8,0},{12,4},{16,24},{20,28},{24,16},{28,20},{1,9},{5... | collective-permute-start | bytes 98312 | tf_op jit(solution)/shard_map/while/body/ppermute | solution.py:26
  40.3 1.6 %collective-permute-done.1 = bf16[128,128]{1,0:T(8,128)(2,1)S(1)} collective-permute-done((bf16[128,128]{1,0:T(8,128)(2,1)S(1)}, bf16[128,128]{1,0:T(8,128)(2,1)S(1)}, u32[]{:S(2)}, u32[]{:S(2)}) %collective-permute-start.1) | collective-permute-done | bytes 32800 | tf_op jit(solution)/shard_map/while/body/ppermute | solution.py:26
  42.0 0.8 %collective-permute-done.2 = bf16[128,128]{1,0:T(8,128)(2,1)S(1)} collective-permute-done((bf16[128,128]{1,0:T(8,128)(2,1)S(1)}, bf16[128,128]{1,0:T(8,128)(2,1)S(1)}, u32[]{:S(2)}, u32[]{:S(2)}) %collective-permute-start.2) | collective-permute-done | bytes 32800 | tf_op jit(solution)/shard_map/while/body/ppermute | solution.py:26
  42.9 1.2 %collective-permute-done.4 = bf16[128,128]{1,0:T(8,128)(2,1)S(1)} collective-permute-done((bf16[128,128]{1,0:T(8,128)(2,1)S(1)}, bf16[128,128]{1,0:T(8,128)(2,1)S(1)}, u32[]{:S(2)}, u32[]{:S(2)}) %collective-permute-start.4) | collective-permute-done | bytes 32800 | tf_op jit(solution)/shard_map/while/body/ppermute | solution.py:26
  44.1 0.6 %pad_maximum_fusion.6 = bf16[128,256]{1,0:T(8,128)(2,1)} fusion(bf16[128,128]{1,0:T(8,128)(2,1)S(1)} %collective-permute-done.4, bf16[128,128]{1,0:T(8,128)(2,1)S(1)} %fusion.11), kind=kLoop, calls=%fused_computation.6.clone.1 | loop fusion | flops 131072 | bytes 131072 | tf_op jit(solution)/shard_map/while/body/concatenate | solution.py:317
  44.7 2.3 %carve.5 = (bf16[256,1024]{1,0:T(8,128)(2,1)S(1)}, bf16[256,1024]{1,0:T(8,128)(2,1)S(1)}, bf16[256,1024]{1,0:T(8,128)(2,1)S(1)}, bf16[256,1024]{1,0:T(8,128)(2,1)S(1)}) custom-call(s32[4]{0:T(128)S(1)} %pad_add_fusion.block_ref, bf16[256,16384]{1,0:T(8,128)(2,1)} %w_ref.8, bf16[128,256]{1,0:T(8,128)(2,1)} %get-tuple-element.51.refs_0_.kv_ref), custom_call_target="tpu_custom_call" | custom-call | bytes 4194304 | tf_op jit(solution)/shard_map/carve/pallas_call | solution.py:68
  48.1 1.0 %collective-permute-start.18 = (bf16[128,1024]{1,0:T(8,128)(2,1)S(1)}, bf16[128,1024]{1,0:T(8,128)(2,1)S(1)}, u32[]{:S(2)}, u32[]{:S(2)}) collective-permute-start(bf16[128,1024]{1,0:T(8,128)(2,1)S(1)} %pad_maximum_fusion.1), channel_id=1, source_target_pairs={{0,2},{1,3},{2,0},{3,1},{4,6},{5,7},{6,4},{7,5},{8,10},{9,11},{10,... | collective-permute-start | bytes 786440 | tf_op jit(solution)/shard_map/ppermute | solution.py:26
  49.7 0.7 %collective-permute-done.16.refs_2_ = bf16[256,1024]{1,0:T(8,128)(2,1)S(1)} collective-permute-done((bf16[256,1024]{1,0:T(8,128)(2,1)S(1)}, bf16[256,1024]{1,0:T(8,128)(2,1)S(1)}, u32[]{:S(2)}, u32[]{:S(2)}) %collective-permute-start.16) | collective-permute-done | bytes 524320 | tf_op jit(solution)/shard_map/ppermute | solution.py:26
  50.5 0.7 %collective-permute-done.17.refs_3_ = bf16[256,1024]{1,0:T(8,128)(2,1)S(1)} collective-permute-done((bf16[256,1024]{1,0:T(8,128)(2,1)S(1)}, bf16[256,1024]{1,0:T(8,128)(2,1)S(1)}, u32[]{:S(2)}, u32[]{:S(2)}) %collective-permute-start.17) | collective-permute-done | bytes 524320 | tf_op jit(solution)/shard_map/ppermute | solution.py:26
  51.2 2.6 %own.1.acc_ref = f32[128,4096]{1,0:T(8,128)S(1)} custom-call(s32[1]{0:T(128)} %bitcast.17.block_ref, bf16[128,512]{1,0:T(8,128)(2,1)S(1)} %get-tuple-element.53.dq_ref, bf16[256,16384]{1,0:T(8,128)(2,1)} %w_ref.8, bf16[256,1024]{1,0:T(8,128)(2,1)S(1)} %collective-permute-done.14.refs_0_, bf16[256,1024]{1,0:T(8,128)(2,1)S(1)} %collective-permute-done.15.refs_1_, ...), custom_call_target="tpu_custom_call" | custom-call | flops 536870912 | bytes 4194304 | tf_op jit(solution)/shard_map/own/pallas_call | solution.py:223
  53.8 2.7 %collective-permute-done.18.second_ref = bf16[128,1024]{1,0:T(8,128)(2,1)S(1)} collective-permute-done((bf16[128,1024]{1,0:T(8,128)(2,1)S(1)}, bf16[128,1024]{1,0:T(8,128)(2,1)S(1)}, u32[]{:S(2)}, u32[]{:S(2)}) %collective-permute-start.18) | collective-permute-done | bytes 262176 | tf_op jit(solution)/shard_map/ppermute | solution.py:26
  56.6 1.3 %finish.1 = bf16[128,4096]{1,0:T(8,128)(2,1)} custom-call(s32[1]{0:T(128)} %bitcast.4.core_ref, bf16[128,256]{1,0:T(8,128)(2,1)S(1)} %copy-done.3, bf16[256,4096]{1,0:T(8,128)(2,1)S(1)} %copy-done, f32[128,4096]{1,0:T(8,128)S(1)} %own.1.acc_ref, bf16[128,3328]{1,0:T(8,128)(2,1)S(1)} %collective-permute-done.13.first_ref, ...), custom_call_target="tpu_custom_call" | custom-call | flops 268435456 | bytes 5242880 | tf_op jit(solution)/shard_map/finish/pallas_call | solution.py:270
  (38 shorter events, 2.5 us)
Async XLA Ops:
  1.7 9.5 %collective-permute-start.5 = (bf16[144,128]{1,0:T(8,128)(2,1)S(1)}, bf16[144,128]{1,0:T(8,128)(2,1)S(1)}, u32[]{:S(2)}, u32[]{:S(2)}) collective-permute-start(bf16[144,128]{1,0:T(8,128)(2,1)S(1)} %get-tuple-element.74), channel_id=1, source_target_pairs={{0,8},{4,12},{8,0},{12,4},{16,24},{20,28},{24,16},{28,20},{1,9},{5... | collective-permute-start | bytes 110600 | tf_op jit(solution)/shard_map/ppermute | solution.py:26
  4.8 6.5 %collective-permute-start.6 = (bf16[144,128]{1,0:T(8,128)(2,1)S(1)}, bf16[144,128]{1,0:T(8,128)(2,1)S(1)}, u32[]{:S(2)}, u32[]{:S(2)}) collective-permute-start(bf16[144,128]{1,0:T(8,128)(2,1)S(1)} %get-tuple-element.74), channel_id=1, source_target_pairs={{0,16},{4,20},{8,24},{12,28},{16,0},{20,4},{24,8},{28,12},{1,17},{... | collective-permute-start | bytes 110600 | tf_op jit(solution)/shard_map/ppermute | solution.py:26
  7.4 5.8 %collective-permute-start.7 = (bf16[144,128]{1,0:T(8,128)(2,1)S(1)}, bf16[144,128]{1,0:T(8,128)(2,1)S(1)}, u32[]{:S(2)}, u32[]{:S(2)}) collective-permute-start(bf16[144,128]{1,0:T(8,128)(2,1)S(1)} %get-tuple-element.74), channel_id=1, source_target_pairs={{0,24},{4,28},{8,16},{12,20},{16,8},{20,12},{24,0},{28,4},{1,25},{... | collective-permute-start | bytes 110600 | tf_op jit(solution)/shard_map/ppermute | solution.py:26
  8.3 4.9 %collective-permute-start.8 = (bf16[2,128,256]{2,1,0:T(8,128)(2,1)S(1)}, bf16[2,128,256]{2,1,0:T(8,128)(2,1)S(1)}, u32[]{:S(2)}, u32[]{:S(2)}) collective-permute-start(bf16[2,128,256]{2,1,0:T(8,128)(2,1)S(1)} %pad_maximum_fusion.3.refs_0_.mine_ref), channel_id=1, source_target_pairs={{0,1},{1,0},{2,3},{3,2},{4,5},{5,4},{6,7},{7,6},{8,9},{9,8},{10,11... | collective-permute-start | bytes 393224 | tf_op jit(solution)/shard_map/ppermute | solution.py:26
  13.2 10.1 %collective-permute-start.12 = (bf16[256,4096]{1,0:T(8,128)(2,1)}, bf16[256,4096]{1,0:T(8,128)(2,1)}, u32[]{:S(2)}, u32[]{:S(2)}) collective-permute-start(bf16[256,4096]{1,0:T(8,128)(2,1)} %carve.3), channel_id=1, source_target_pairs={{0,1},{1,0},{2,3},{3,2},{4,5},{5,4},{6,7},{7,6},{8,9},{9,8},{10,11... | collective-permute-start | bytes 6291464 | tf_op jit(solution)/shard_map/ppermute | solution.py:26
  13.3 6.3 %collective-permute-start.10 = (bf16[4,144,128]{2,1,0:T(8,128)(2,1)S(1)}, bf16[4,144,128]{2,1,0:T(8,128)(2,1)S(1)}, u32[]{:S(2)}, u32[]{:S(2)}) collective-permute-start(bf16[4,144,128]{2,1,0:T(8,128)(2,1)S(1)} %pad_maximum_fusion.2.refs_0_), channel_id=1, source_target_pairs={{0,4},{4,0},{8,12},{12,8},{16,20},{20,16},{24,28},{28,24},{1,5},{5... | collective-permute-start | bytes 442376 | tf_op jit(solution)/shard_map/ppermute | solution.py:26
  14.8 4.8 %collective-permute-start.9 = (bf16[4,144,128]{2,1,0:T(8,128)(2,1)S(1)}, bf16[4,144,128]{2,1,0:T(8,128)(2,1)S(1)}, u32[]{:S(2)}, u32[]{:S(2)}) collective-permute-start(bf16[4,144,128]{2,1,0:T(8,128)(2,1)S(1)} %pad_maximum_fusion.2.refs_0_), channel_id=1, source_target_pairs={{0,1},{1,0},{2,3},{3,2},{4,5},{5,4},{6,7},{7,6},{8,9},{9,8},{10,11... | collective-permute-start | bytes 442376 | tf_op jit(solution)/shard_map/ppermute | solution.py:26
  15.0 4.5 %copy-start.1 = (s32[128]{0:T(128)S(1)}, s32[128]{0:T(128)}, u32[]{:S(2)}) copy-start(s32[128]{0:T(128)} %param.14) | copy-start | bytes 1540
  15.0 5.9 %copy-start.2 = (s32[128]{0:T(128)S(1)}, s32[128]{0:T(128)}, u32[]{:S(2)}) copy-start(s32[128]{0:T(128)} %param.15) | copy-start | bytes 1540
  19.6 1.4 %collective-permute-start.11 = (bf16[4,144,128]{2,1,0:T(8,128)(2,1)S(1)}, bf16[4,144,128]{2,1,0:T(8,128)(2,1)S(1)}, u32[]{:S(2)}, u32[]{:S(2)}) collective-permute-start(bf16[4,144,128]{2,1,0:T(8,128)(2,1)S(1)} %collective-permute-done.10.refs_2_), channel_id=1, source_target_pairs={{0,1},{1,0},{2,3},{3,2},{4,5},{5,4},{6,7},{7,6},{8,9},{9,8},{10,11... | collective-permute-start | bytes 442376 | tf_op jit(solution)/shard_map/ppermute | solution.py:26
  26.4 21.7 %collective-permute-start.13 = (bf16[128,3328]{1,0:T(8,128)(2,1)}, bf16[128,3328]{1,0:T(8,128)(2,1)S(1)}, u32[]{:S(2)}, u32[]{:S(2)}) collective-permute-start(bf16[128,3328]{1,0:T(8,128)(2,1)} %product.2), channel_id=1, source_target_pairs={{0,2},{1,3},{2,0},{3,1},{4,6},{5,7},{6,4},{7,5},{8,10},{9,11},{10,... | collective-permute-start | bytes 2555912 | tf_op jit(solution)/shard_map/ppermute | solution.py:26
  30.5 5.3 %collective-permute-start = (bf16[4,128,128]{2,1,0:T(8,128)(2,1)S(1)}, bf16[4,128,128]{2,1,0:T(8,128)(2,1)S(1)}, u32[]{:S(2)}, u32[]{:S(2)}) collective-permute-start(bf16[4,128,128]{2,1,0:T(8,128)(2,1)S(1)} %constant_dynamic-slice_fusion.2), channel_id=1, source_target_pairs={{0,4},{4,0},{8,12},{12,8},{16,20},{20,16},{24,28},{28,24},{1,5},{5... | collective-permute-start | bytes 393224 | tf_op jit(solution)/shard_map/while/body/ppermute | solution.py:26
  35.9 6.1 %collective-permute-start.1 = (bf16[128,128]{1,0:T(8,128)(2,1)S(1)}, bf16[128,128]{1,0:T(8,128)(2,1)S(1)}, u32[]{:S(2)}, u32[]{:S(2)}) collective-permute-start(bf16[128,128]{1,0:T(8,128)(2,1)S(1)} %get-tuple-element.106), channel_id=1, source_target_pairs={{0,24},{4,28},{8,16},{12,20},{16,8},{20,12},{24,0},{28,4},{1,25},{... | collective-permute-start | bytes 98312 | tf_op jit(solution)/shard_map/while/body/ppermute | solution.py:26
  37.9 4.8 %collective-permute-start.2 = (bf16[128,128]{1,0:T(8,128)(2,1)S(1)}, bf16[128,128]{1,0:T(8,128)(2,1)S(1)}, u32[]{:S(2)}, u32[]{:S(2)}) collective-permute-start(bf16[128,128]{1,0:T(8,128)(2,1)S(1)} %get-tuple-element.107), channel_id=1, source_target_pairs={{0,16},{4,20},{8,24},{12,28},{16,0},{20,4},{24,8},{28,12},{1,17},{... | collective-permute-start | bytes 98312 | tf_op jit(solution)/shard_map/while/body/ppermute | solution.py:26
  37.9 4.8 %collective-permute-start.3 = (bf16[128,128]{1,0:T(8,128)(2,1)S(1)}, bf16[128,128]{1,0:T(8,128)(2,1)S(1)}, u32[]{:S(2)}, u32[]{:S(2)}) collective-permute-start(bf16[128,128]{1,0:T(8,128)(2,1)S(1)} %get-tuple-element.108), channel_id=1, source_target_pairs={{0,8},{4,12},{8,0},{12,4},{16,24},{20,28},{24,16},{28,20},{1,9},{5... | collective-permute-start | bytes 98312 | tf_op jit(solution)/shard_map/while/body/ppermute | solution.py:26
  42.8 1.3 %collective-permute-start.4 = (bf16[128,128]{1,0:T(8,128)(2,1)S(1)}, bf16[128,128]{1,0:T(8,128)(2,1)S(1)}, u32[]{:S(2)}, u32[]{:S(2)}) collective-permute-start(bf16[128,128]{1,0:T(8,128)(2,1)S(1)} %fusion.11), channel_id=1, source_target_pairs={{0,1},{1,0},{2,3},{3,2},{4,5},{5,4},{6,7},{7,6},{8,9},{9,8},{10,11... | collective-permute-start | bytes 98312 | tf_op jit(solution)/shard_map/while/body/ppermute | solution.py:26
  44.7 3.4 %copy-start.3 = (bf16[128,256]{1,0:T(8,128)(2,1)S(1)}, bf16[128,256]{1,0:T(8,128)(2,1)}, u32[]{:S(2)}) copy-start(bf16[128,256]{1,0:T(8,128)(2,1)} %get-tuple-element.51.refs_0_.kv_ref) | copy-start | bytes 196612
  47.0 2.2 %collective-permute-start.14 = (bf16[256,1024]{1,0:T(8,128)(2,1)S(1)}, bf16[256,1024]{1,0:T(8,128)(2,1)S(1)}, u32[]{:S(2)}, u32[]{:S(2)}) collective-permute-start(bf16[256,1024]{1,0:T(8,128)(2,1)S(1)} %get-tuple-element.54), channel_id=1, source_target_pairs={{0,1},{1,0},{2,3},{3,2},{4,5},{5,4},{6,7},{7,6},{8,9},{9,8},{10,11... | collective-permute-start | bytes 1572872 | tf_op jit(solution)/shard_map/ppermute | solution.py:26
  47.2 2.5 %collective-permute-start.15 = (bf16[256,1024]{1,0:T(8,128)(2,1)S(1)}, bf16[256,1024]{1,0:T(8,128)(2,1)S(1)}, u32[]{:S(2)}, u32[]{:S(2)}) collective-permute-start(bf16[256,1024]{1,0:T(8,128)(2,1)S(1)} %get-tuple-element.55), channel_id=1, source_target_pairs={{0,1},{1,0},{2,3},{3,2},{4,5},{5,4},{6,7},{7,6},{8,9},{9,8},{10,11... | collective-permute-start | bytes 1572872 | tf_op jit(solution)/shard_map/ppermute | solution.py:26
  47.6 2.9 %collective-permute-start.16 = (bf16[256,1024]{1,0:T(8,128)(2,1)S(1)}, bf16[256,1024]{1,0:T(8,128)(2,1)S(1)}, u32[]{:S(2)}, u32[]{:S(2)}) collective-permute-start(bf16[256,1024]{1,0:T(8,128)(2,1)S(1)} %get-tuple-element.56), channel_id=1, source_target_pairs={{0,1},{1,0},{2,3},{3,2},{4,5},{5,4},{6,7},{7,6},{8,9},{9,8},{10,11... | collective-permute-start | bytes 1572872 | tf_op jit(solution)/shard_map/ppermute | solution.py:26
  47.7 3.5 %collective-permute-start.17 = (bf16[256,1024]{1,0:T(8,128)(2,1)S(1)}, bf16[256,1024]{1,0:T(8,128)(2,1)S(1)}, u32[]{:S(2)}, u32[]{:S(2)}) collective-permute-start(bf16[256,1024]{1,0:T(8,128)(2,1)S(1)} %get-tuple-element.57), channel_id=1, source_target_pairs={{0,1},{1,0},{2,3},{3,2},{4,5},{5,4},{6,7},{7,6},{8,9},{9,8},{10,11... | collective-permute-start | bytes 1572872 | tf_op jit(solution)/shard_map/ppermute | solution.py:26
  48.1 8.4 %collective-permute-start.18 = (bf16[128,1024]{1,0:T(8,128)(2,1)S(1)}, bf16[128,1024]{1,0:T(8,128)(2,1)S(1)}, u32[]{:S(2)}, u32[]{:S(2)}) collective-permute-start(bf16[128,1024]{1,0:T(8,128)(2,1)S(1)} %pad_maximum_fusion.1), channel_id=1, source_target_pairs={{0,2},{1,3},{2,0},{3,1},{4,6},{5,7},{6,4},{7,5},{8,10},{9,11},{10,... | collective-permute-start | bytes 786440 | tf_op jit(solution)/shard_map/ppermute | solution.py:26
  51.2 5.3 %copy-start = (bf16[256,4096]{1,0:T(8,128)(2,1)S(1)}, bf16[256,4096]{1,0:T(8,128)(2,1)}, u32[]{:S(2)}) copy-start(bf16[256,4096]{1,0:T(8,128)(2,1)} %w_ref.9) | copy-start | bytes 6291460

commit v9 on v8

--- a/solution.py
+++ b/solution.py
@@ -71,7 +71,7 @@
         in_specs=[SMEM, HBM, ANY],
         out_specs=[pl.BlockSpec(memory_space=pltpu.VMEM)] * count,
         scratch_shapes=[pltpu.SemaphoreType.DMA((count, 4))],
-        compiler_params=params(48),
+        compiler_params=params(45),
         cost_estimate=pl.CostEstimate(
             flops=0, bytes_accessed=4 * count * w_query.shape[0] * share, transcendentals=0
         ),
@@ -200,41 +200,50 @@
     )(dq, w_mine, w_other)
 
 
-def own_kernel(block_ref, dq_ref, w_ref, *refs):
-    out_ref, wm_ref, sems = refs[TILES:]
-    depth, share = wm_ref.shape
+def own_kernel(blocks_ref, dq_ref, w_ref, acc_ref, low_ref, high_ref, hold_ref, sems):
+    depth, share = hold_ref.shape[1:]
     tile = share // TILES
     copies = []
-    for i in range(TILES):
-        at = pl.multiple_of(block_ref[0] * share + i * tile, tile)
-        target = wm_ref.at[:, i * tile : (i + 1) * tile]
-        copies.append(pltpu.make_async_copy(w_ref.at[:, pl.ds(at, tile)], target, sems.at[i]))
-        copies[i].start()
-    for i in range(TILES):
-        at = slice(i * tile, (i + 1) * tile)
-        acc = dot(dq_ref[:, depth:], refs[i][...], ((1,), (0,)))
-        copies[i].wait()
-        out_ref[:, at] = acc + dot(dq_ref[:, 0:depth], wm_ref[:, at], ((1,), (0,)))
-
-
-def own(block, dq, w_query, w_other):
-    rows, depth = dq.shape
-    share = TILES * w_other[0].shape[1]
+    for k in range(2):
+        for i in range(TILES):
+            at = pl.multiple_of(blocks_ref[k] * share + i * tile, tile)
+            target = hold_ref.at[k, :, i * tile : (i + 1) * tile]
+            copies.append(pltpu.make_async_copy(w_ref.at[:, pl.ds(at, tile)], target, sems.at[k, i]))
+            copies[-1].start()
+    for k in range(2):
+        for i in range(TILES):
+            at = slice(i * tile, (i + 1) * tile)
+            copies[k * TILES + i].wait()
+            part = dot(dq_ref[:, 0:depth], hold_ref[k, :, at], ((1,), (0,)))
+            if k == 1:
+                acc_ref[:, at] = part
+            elif i < TILES // 2:
+                low_ref[:, at] = part.astype(jnp.bfloat16)
+            else:
+                high_ref[:, i * tile - share // 2 : (i + 1) * tile - share // 2] = part.astype(jnp.bfloat16)
+
+
+def own(blocks, dq, w_query, share):
+    rows, depth = dq.shape[0], w_query.shape[0]
     return pl.pallas_call(
         own_kernel,
-        out_shape=jax.ShapeDtypeStruct((rows, share), jnp.float32),
-        in_specs=[SMEM, pl.BlockSpec(), HBM] + [pl.BlockSpec()] * TILES,
-        out_specs=pl.BlockSpec(),
-        scratch_shapes=[pltpu.VMEM((depth // 2, share), w_query.dtype), pltpu.SemaphoreType.DMA((TILES,))],
-        compiler_params=params(48),
-        cost_estimate=pl.CostEstimate(
-            flops=2 * rows * depth * share, bytes_accessed=2 * depth * share, transcendentals=0
-        ),
+        out_shape=[
+            jax.ShapeDtypeStruct((rows, share), jnp.float32),
+            jax.ShapeDtypeStruct((rows, share // 2), jnp.bfloat16),
+            jax.ShapeDtypeStruct((rows, share // 2), jnp.bfloat16),
+        ],
+        in_specs=[SMEM, pl.BlockSpec(), HBM],
+        out_specs=[pl.BlockSpec()] * 3,
+        scratch_shapes=[
+            pltpu.VMEM((2, depth, share), w_query.dtype),
+            pltpu.SemaphoreType.DMA((2, TILES)),
+        ],
+        compiler_params=params(45),
         name="own",
-    )(block, dq, w_query, *w_other)
-
-
-def finish_kernel(core_ref, kv_ref, w_ref, acc_ref, first_ref, second_ref, out_ref, hold_ref, sems):
+    )(jnp.stack(blocks), dq, w_query)
+
+
+def finish_kernel(core_ref, kv_ref, w_ref, acc_ref, low_ref, high_ref, first_ref, second_ref, out_ref, hold_ref, sems):
     rows, share = acc_ref.shape
     pair = kv_ref.shape[1]
     size = pair // 2
@@ -251,7 +260,9 @@
     for i in range(TILES):
         low, high = i * tile, (i + 1) * tile
         w = jnp.concatenate([w_ref[at_mine, low:high], w_ref[at_other, low:high]], axis=0)
-        acc = acc_ref[:, low:high] + dot(kv, w, ((1,), (0,)))
+        given_ref, skip = (low_ref, 0) if high <= share // 2 else (high_ref, share // 2)
+        given = given_ref[:, low - skip : high - skip].astype(jnp.float32)
+        acc = acc_ref[:, low:high] + given + dot(kv, w, ((1,), (0,)))
         come = []
         if low < cut:
             come.append(first_ref[:, low : min(high, cut)])
@@ -265,12 +276,12 @@
         one.wait()
 
 
-def finish(core, kv, w_kv, acc, first, second):
+def finish(core, kv, w_kv, acc, low, high, first, second):
     rows, share = acc.shape
     return pl.pallas_call(
         finish_kernel,
         out_shape=jax.ShapeDtypeStruct((rows, share), jnp.bfloat16),
-        in_specs=[SMEM] + [pl.BlockSpec()] * 5,
+        in_specs=[SMEM] + [pl.BlockSpec()] * 7,
         out_specs=ANY,
         scratch_shapes=[pltpu.VMEM((rows, share), jnp.bfloat16), pltpu.SemaphoreType.DMA((TILES,))],
         compiler_params=params(),
@@ -278,7 +289,7 @@
             flops=2 * rows * kv.shape[1] * share, bytes_accessed=10 * rows * share, transcendentals=0
         ),
         name="finish",
-    )(core, kv, w_kv, acc, first, second)
+    )(core, kv, w_kv, acc, low, high, first, second)
 
 
 def on_device(queries, keys, values, dout, positions, doc_ids, w_query, w_kv):
@@ -320,13 +331,11 @@
     trips = 1 + jnp.minimum(positions[0], 0)
     kv = lax.fori_loop(0, trips, exchange, jnp.zeros((queries.shape[0], 2 * keys.shape[1]), jnp.bfloat16))
 
-    near_send = carve([(head ^ 1) * TILES + i for i in range(TILES)], w_query, share // TILES, kv)
-    near_other = [swapped(one, "head", 1) for one in near_send]
-    second_part = jnp.concatenate([second_part, kv], axis=1)
-    second_part, first, dq = lax.optimization_barrier((second_part, first, dq))
-    second = swapped(second_part, "head", 2)
-    acc = own(head.reshape(1), dq, w_query, near_other)
-    return finish(core, kv, w_kv, acc, first, second)
+    kv, dq = lax.optimization_barrier((kv, dq))
+    second = swapped(jnp.concatenate([second_part, kv], axis=1), "head", 2)
+    acc, *give = own([head ^ 1, head], dq, w_query, share)
+    low, high = [swapped(one, "head", 1) for one in give]
+    return finish(core, kv, w_kv, acc, low, high, first, second)
 
 
 def solution(mesh):

time: 58.3 us -> 59.7 us (1.024)
  waiting for transfers between devices: 18.3 us -> 21.4 us
  starting transfers between devices: 17.3 us -> 16.4 us
  Pallas kernels: 18 us -> 17.2 us
    ppermute x19 -> x17, waiting for transfers between devices: 18.3 us -> 21.4 us  [swapped(): lax.ppermute(value, axis, [(source, source ^ bits) for source in range(co...]
    pallas_call x3 -> x2, Pallas kernels: 6.74 us -> 4.47 us  [carve(): pl.pallas_call(carve_kernel, out_shape=[block] * count, in_specs=[SMEM, H...]
    pallas_call x1, Pallas kernels: 1.33 us -> 2.66 us  [finish(): pl.pallas_call(finish_kernel, out_shape=jax.ShapeDtypeStruct((rows, share...]
    pallas_call x1, Pallas kernels: 2.6 us -> 3.67 us  [own(): pl.pallas_call(own_kernel, out_shape=[jax.ShapeDtypeStruct((rows, share),...]
    ppermute x19 -> x17, starting transfers between devices: 17.3 us -> 16.4 us  [swapped(): lax.ppermute(value, axis, [(source, source ^ bits) for source in range(co...]
    pallas_call x2, Pallas kernels: 4.97 us -> 4.07 us  [product(): pl.pallas_call(functools.partial(product_kernel, first), out_shape=jax.Sh...]
  transfers between devices with their start and end apart: 19 -> 17, of which waited for: 11 -> 8; matrix products, arithmetic and copies ran while one was open for 4% -> 4% of each run, Pallas kernels for 23% -> 21%
where the time goes in v9:
time: 59.7 us; the launch traced here: 59.3 us
  waiting for transfers between devices  21.4 us (36%)
  Pallas kernels  17.2 us (29%)
  starting transfers between devices  16.4 us (27%)
  other arithmetic  2.69 us (5%)
  local copies, waits for them, and re-layouts  1.4 us (2%)
    ppermute x17, waiting for transfers between devices, swapped(): lax.ppermute(value, axis, [(source, source ^ bits) for source in range(co...  21.4 us
    ppermute x17, starting transfers between devices, swapped(): lax.ppermute(value, axis, [(source, source ^ bits) for source in range(co...  16.4 us
    pallas_call x2, Pallas kernels, carve(): pl.pallas_call(carve_kernel, out_shape=[block] * count, in_specs=[SMEM, H...  4.47 us
    pallas_call x2, Pallas kernels, product(): pl.pallas_call(functools.partial(product_kernel, first), out_shape=jax.Sh...  4.07 us
    pallas_call x1, Pallas kernels, own(): pl.pallas_call(own_kernel, out_shape=[jax.ShapeDtypeStruct((rows, share),...  3.67 us
    pallas_call x1, Pallas kernels, finish(): pl.pallas_call(finish_kernel, out_shape=jax.ShapeDtypeStruct((rows, share...  2.66 us
    pallas_call x1, Pallas kernels, attention(): pl.pallas_call(attention_kernel, out_shape=[jax.ShapeDtypeStruct((rows, 2...  2.37 us
  transfers between devices with their start and end apart: 17, of which 8 were waited for; matrix products, arithmetic and copies ran while one was open for 4% of the time, Pallas kernels for 21%

profile of v9, /device:TPU:0, one launch (start us, length us, event | category | flops | bytes accessed | tf_op | source)
XLA Modules:
  0.0 59.3 jit_solution(14399666056080682745)
XLA Ops:
  0.0 0.7 %reshape.23 = s32[2,64]{1,0:T(2,128)S(1)} reshape(s32[128]{0:T(128)} %param.14) | data formatting | bytes 1024 | tf_op jit(solution)/shard_map/reshape | solution.py:44
  0.9 0.8 %broadcast_select_fusion = bf16[128,128]{1,0:T(8,128)(2,1)S(1)} fusion(bf16[128,128]{1,0:T(8,128)(2,1)} %param.11, bf16[128,128]{1,0:T(8,128)(2,1)} %param.12, pred[]{:T(512)} %bitcast.10), kind=kLoop, calls=%fused_computation.16 | loop fusion | flops 16384 | bytes 98305 | tf_op jit(solution)/shard_map/jit(_where)/select_n | solution.py:43
  1.7 3.1 %collective-permute-start.5 = (bf16[144,128]{1,0:T(8,128)(2,1)S(1)}, bf16[144,128]{1,0:T(8,128)(2,1)S(1)}, u32[]{:S(2)}, u32[]{:S(2)}) collective-permute-start(bf16[144,128]{1,0:T(8,128)(2,1)S(1)} %get-tuple-element.70), channel_id=1, source_target_pairs={{0,8},{4,12},{8,0},{12,4},{16,24},{20,28},{24,16},{28,20},{1,9},{5... | collective-permute-start | bytes 110600 | tf_op jit(solution)/shard_map/ppermute | solution.py:26
  4.8 2.6 %collective-permute-start.6 = (bf16[144,128]{1,0:T(8,128)(2,1)S(1)}, bf16[144,128]{1,0:T(8,128)(2,1)S(1)}, u32[]{:S(2)}, u32[]{:S(2)}) collective-permute-start(bf16[144,128]{1,0:T(8,128)(2,1)S(1)} %get-tuple-element.70), channel_id=1, source_target_pairs={{0,16},{4,20},{8,24},{12,28},{16,0},{20,4},{24,8},{28,12},{1,17},{... | collective-permute-start | bytes 110600 | tf_op jit(solution)/shard_map/ppermute | solution.py:26
  7.4 0.9 %pad_maximum_fusion.3.refs_0_.mine_ref = bf16[2,128,256]{2,1,0:T(8,128)(2,1)S(1)} fusion(bf16[1,128,256]{2,1,0:T(8,128)(2,1)} %bitcast.40, bf16[1,128,256]{2,1,0:T(8,128)(2,1)} %bitcast.41), kind=kLoop, calls=%fused_computation.14 | loop fusion | flops 65536 | bytes 262144 | tf_op jit(solution)/shard_map/stack | solution.py:304
  8.4 2.9 %carve.2 = bf16[256,4096]{1,0:T(8,128)(2,1)} custom-call(s32[1]{0:T(128)} %bitcast.15.block_ref, bf16[256,16384]{1,0:T(8,128)(2,1)} %w_ref.6, bf16[2,128,256]{2,1,0:T(8,128)(2,1)S(1)} %pad_maximum_fusion.3.refs_0_.mine_ref), custom_call_target="tpu_custom_call" | custom-call | bytes 4194304 | tf_op jit(solution)/shard_map/carve/pallas_call | solution.py:68
  11.3 1.9 %collective-permute-done.7 = bf16[144,128]{1,0:T(8,128)(2,1)S(1)} collective-permute-done((bf16[144,128]{1,0:T(8,128)(2,1)S(1)}, bf16[144,128]{1,0:T(8,128)(2,1)S(1)}, u32[]{:S(2)}, u32[]{:S(2)}) %collective-permute-start.7) | collective-permute-done | bytes 36896 | tf_op jit(solution)/shard_map/ppermute | solution.py:26
  13.3 1.6 %collective-permute-start.10 = (bf16[4,144,128]{2,1,0:T(8,128)(2,1)S(1)}, bf16[4,144,128]{2,1,0:T(8,128)(2,1)S(1)}, u32[]{:S(2)}, u32[]{:S(2)}) collective-permute-start(bf16[4,144,128]{2,1,0:T(8,128)(2,1)S(1)} %pad_maximum_fusion.2.refs_0_), channel_id=1, source_target_pairs={{0,4},{4,0},{8,12},{12,8},{16,20},{20,16},{24,28},{28,24},{1,5},{5... | collective-permute-start | bytes 442376 | tf_op jit(solution)/shard_map/ppermute | solution.py:26
  14.8 0.2 collective-permute-start.9
  15.0 1.6 %carve.3.wm_ref = bf16[256,4096]{1,0:T(8,128)(2,1)S(1)} custom-call(s32[1]{0:T(128)} %bitcast.16.block_ref, bf16[256,16384]{1,0:T(8,128)(2,1)} %w_ref.6, bf16[4,144,128]{2,1,0:T(8,128)(2,1)S(1)} %pad_maximum_fusion.2.refs_0_), custom_call_target="tpu_custom_call" | custom-call | bytes 4194304 | tf_op jit(solution)/shard_map/carve/pallas_call | solution.py:68
  16.6 3.0 %collective-permute-done.10.refs_2_ = bf16[4,144,128]{2,1,0:T(8,128)(2,1)S(1)} collective-permute-done((bf16[4,144,128]{2,1,0:T(8,128)(2,1)S(1)}, bf16[4,144,128]{2,1,0:T(8,128)(2,1)S(1)}, u32[]{:S(2)}, u32[]{:S(2)}) %collective-permute-start.10) | collective-permute-done | bytes 147488 | tf_op jit(solution)/shard_map/ppermute | solution.py:26
  19.7 1.2 %collective-permute-done.11.refs_3_ = bf16[4,144,128]{2,1,0:T(8,128)(2,1)S(1)} collective-permute-done((bf16[4,144,128]{2,1,0:T(8,128)(2,1)S(1)}, bf16[4,144,128]{2,1,0:T(8,128)(2,1)S(1)}, u32[]{:S(2)}, u32[]{:S(2)}) %collective-permute-start.11) | collective-permute-done | bytes 147488 | tf_op jit(solution)/shard_map/ppermute | solution.py:26
  20.9 2.4 %attention.1 = (bf16[128,512]{1,0:T(8,128)(2,1)S(1)}, bf16[8,128,128]{2,1,0:T(8,128)(2,1)S(1)}) custom-call(s32[1]{0:T(128)} %bitcast.4.core_ref, s32[1,128]{1,0:T(1,128)S(1)} %bitcast.38, s32[1,128]{1,0:T(1,128)S(1)} %bitcast.39, bf16[2,128,256]{2,1,0:T(8,128)(2,1)S(1)} %pad_maximum_fusion.3.refs_0_.mine_ref, ...), custom_call_target="tpu_custom_call" | custom-call | flops 671088640 | bytes 1048576 | tf_op jit(solution)/shard_map/attention/pallas_call | solution.py:161
  23.3 2.2 %product.2 = bf16[128,3328]{1,0:T(8,128)(2,1)S(1)} custom-call(bf16[128,512]{1,0:T(8,128)(2,1)S(1)} %get-tuple-element.51.dq_ref, bf16[256,4096]{1,0:T(8,128)(2,1)S(1)} %carve.3.wm_ref, bf16[256,4096]{1,0:T(8,128)(2,1)} %collective-permute-done.12.wo_ref), custom_call_target="tpu_custom_call" | custom-call | flops 436207616 | bytes 3407872 | tf_op jit(solution)/shard_map/product/pallas_call | solution.py:190
  25.5 1.6 %collective-permute-start.15 = (bf16[128,3328]{1,0:T(8,128)(2,1)S(1)}, bf16[128,3328]{1,0:T(8,128)(2,1)}, u32[]{:S(2)}, u32[]{:S(2)}) collective-permute-start(bf16[128,3328]{1,0:T(8,128)(2,1)S(1)} %product.2), channel_id=1, source_target_pairs={{0,2},{1,3},{2,0},{3,1},{4,6},{5,7},{6,4},{7,5},{8,10},{9,11},{10,... | collective-permute-start | bytes 2555912 | tf_op jit(solution)/shard_map/ppermute | solution.py:26
  27.1 1.9 %product.3 = bf16[128,768]{1,0:T(8,128)(2,1)S(1)} custom-call(bf16[128,512]{1,0:T(8,128)(2,1)S(1)} %get-tuple-element.51.dq_ref, bf16[256,4096]{1,0:T(8,128)(2,1)S(1)} %carve.3.wm_ref, bf16[256,4096]{1,0:T(8,128)(2,1)} %collective-permute-done.12.wo_ref), custom_call_target="tpu_custom_call" | custom-call | flops 100663296 | bytes 786432 | tf_op jit(solution)/shard_map/product/pallas_call | solution.py:190
  29.0 0.6 %broadcast_in_dim.16 = bf16[128,256]{1,0:T(8,128)(2,1)} broadcast(bf16[]{:T(256)} %constant.34.clone.1), dimensions={} | broadcast | bytes 65538 | tf_op jit(solution)/shard_map/broadcast_in_dim | solution.py:332
  29.6 14.2 %while.10 = (s32[]{:T(128)}, bf16[128,256]{1,0:T(8,128)(2,1)}, s32[]{:T(128)}, bf16[8,128,128]{2,1,0:T(8,128)(2,1)S(1)}, s32[]{:T(128)}, /*index=5*/s32[]{:T(128)}, s32[]{:T(128)}, s32[]{:T(128)}) while((s32[]{:T(128)}, bf16[128,256]{1,0:T(8,128)(2,1)}, s32[]{:T(128)}, bf16[8,128,128]{2,1,0:T(8,128)(2,1)S(1)}, s32[]{:T(128)}, ...), condition=%wide.region_1.2_spmd, body=%wide.region_0.1_spmd.sunk | while | flops 507911 | bytes 2490715 | solution.py:332
  29.6 1.5 %collective-permute-start = (bf16[4,128,128]{2,1,0:T(8,128)(2,1)S(1)}, bf16[4,128,128]{2,1,0:T(8,128)(2,1)S(1)}, u32[]{:S(2)}, u32[]{:S(2)}) collective-permute-start(bf16[4,128,128]{2,1,0:T(8,128)(2,1)S(1)} %constant_dynamic-slice_fusion.2), channel_id=1, source_target_pairs={{0,4},{4,0},{8,12},{12,8},{16,20},{20,16},{24,28},{28,24},{1,5},{5... | collective-permute-start | bytes 393224 | tf_op jit(solution)/shard_map/while/body/ppermute | solution.py:26
  31.2 3.8 %collective-permute-done = bf16[4,128,128]{2,1,0:T(8,128)(2,1)S(1)} collective-permute-done((bf16[4,128,128]{2,1,0:T(8,128)(2,1)S(1)}, bf16[4,128,128]{2,1,0:T(8,128)(2,1)S(1)}, u32[]{:S(2)}, u32[]{:S(2)}) %collective-permute-start) | collective-permute-done | bytes 131104 | tf_op jit(solution)/shard_map/while/body/ppermute | solution.py:26
  35.0 2.1 %collective-permute-start.1 = (bf16[128,128]{1,0:T(8,128)(2,1)S(1)}, bf16[128,128]{1,0:T(8,128)(2,1)S(1)}, u32[]{:S(2)}, u32[]{:S(2)}) collective-permute-start(bf16[128,128]{1,0:T(8,128)(2,1)S(1)} %get-tuple-element.102), channel_id=1, source_target_pairs={{0,24},{4,28},{8,16},{12,20},{16,8},{20,12},{24,0},{28,4},{1,25},{... | collective-permute-start | bytes 98312 | tf_op jit(solution)/shard_map/while/body/ppermute | solution.py:26
  37.1 2.4 %collective-permute-start.3 = (bf16[128,128]{1,0:T(8,128)(2,1)S(1)}, bf16[128,128]{1,0:T(8,128)(2,1)S(1)}, u32[]{:S(2)}, u32[]{:S(2)}) collective-permute-start(bf16[128,128]{1,0:T(8,128)(2,1)S(1)} %get-tuple-element.104), channel_id=1, source_target_pairs={{0,8},{4,12},{8,0},{12,4},{16,24},{20,28},{24,16},{28,20},{1,9},{5... | collective-permute-start | bytes 98312 | tf_op jit(solution)/shard_map/while/body/ppermute | solution.py:26
  39.5 1.5 %collective-permute-done.1 = bf16[128,128]{1,0:T(8,128)(2,1)S(1)} collective-permute-done((bf16[128,128]{1,0:T(8,128)(2,1)S(1)}, bf16[128,128]{1,0:T(8,128)(2,1)S(1)}, u32[]{:S(2)}, u32[]{:S(2)}) %collective-permute-start.1) | collective-permute-done | bytes 32800 | tf_op jit(solution)/shard_map/while/body/ppermute | solution.py:26
  41.0 0.9 %collective-permute-done.2 = bf16[128,128]{1,0:T(8,128)(2,1)S(1)} collective-permute-done((bf16[128,128]{1,0:T(8,128)(2,1)S(1)}, bf16[128,128]{1,0:T(8,128)(2,1)S(1)}, u32[]{:S(2)}, u32[]{:S(2)}) %collective-permute-start.2) | collective-permute-done | bytes 32800 | tf_op jit(solution)/shard_map/while/body/ppermute | solution.py:26
  42.0 1.2 %collective-permute-done.4 = bf16[128,128]{1,0:T(8,128)(2,1)S(1)} collective-permute-done((bf16[128,128]{1,0:T(8,128)(2,1)S(1)}, bf16[128,128]{1,0:T(8,128)(2,1)S(1)}, u32[]{:S(2)}, u32[]{:S(2)}) %collective-permute-start.4) | collective-permute-done | bytes 32800 | tf_op jit(solution)/shard_map/while/body/ppermute | solution.py:26
  43.2 0.6 %pad_maximum_fusion.6 = bf16[128,256]{1,0:T(8,128)(2,1)} fusion(bf16[128,128]{1,0:T(8,128)(2,1)S(1)} %collective-permute-done.4, bf16[128,128]{1,0:T(8,128)(2,1)S(1)} %fusion.11), kind=kLoop, calls=%fused_computation.6.clone.1 | loop fusion | flops 131072 | bytes 131072 | tf_op jit(solution)/shard_map/while/body/concatenate | solution.py:328
  43.9 3.7 %own.1 = (f32[128,4096]{1,0:T(8,128)S(1)}, bf16[128,2048]{1,0:T(8,128)(2,1)S(1)}, bf16[128,2048]{1,0:T(8,128)(2,1)S(1)}) custom-call(s32[2]{0:T(128)S(1)} %pad_add_fusion.blocks_ref, bf16[128,512]{1,0:T(8,128)(2,1)S(1)} %get-tuple-element.51.dq_ref, bf16[256,16384]{1,0:T(8,128)(2,1)} %w_ref.6), custom_call_target="tpu_custom_call" | custom-call | tf_op jit(solution)/shard_map/own/pallas_call | solution.py:228
  47.6 0.2 collective-permute-start.13
  47.8 0.4 collective-permute-start.14
  48.2 0.6 collective-permute-start.16
  48.7 7.9 %collective-permute-done.16.second_ref = bf16[128,1024]{1,0:T(8,128)(2,1)S(1)} collective-permute-done((bf16[128,1024]{1,0:T(8,128)(2,1)S(1)}, bf16[128,1024]{1,0:T(8,128)(2,1)S(1)}, u32[]{:S(2)}, u32[]{:S(2)}) %collective-permute-start.16) | collective-permute-done | bytes 262176 | tf_op jit(solution)/shard_map/ppermute | solution.py:26
  56.6 2.7 %finish.1 = bf16[128,4096]{1,0:T(8,128)(2,1)} custom-call(s32[1]{0:T(128)} %bitcast.4.core_ref, bf16[128,256]{1,0:T(8,128)(2,1)S(1)} %copy-done.3, bf16[256,4096]{1,0:T(8,128)(2,1)S(1)} %copy-done, f32[128,4096]{1,0:T(8,128)S(1)} %get-tuple-element.52.acc_ref, bf16[128,2048]{1,0:T(8,128)(2,1)S(1)} %collective-permute-done.13.low_ref, ...), custom_call_target="tpu_custom_call" | custom-call | flops 268435456 | bytes 5242880 | tf_op jit(solution)/shard_map/finish/pallas_call | solution.py:281
  (33 shorter events, 0.7 us)
Async XLA Ops:
  1.7 9.6 %collective-permute-start.5 = (bf16[144,128]{1,0:T(8,128)(2,1)S(1)}, bf16[144,128]{1,0:T(8,128)(2,1)S(1)}, u32[]{:S(2)}, u32[]{:S(2)}) collective-permute-start(bf16[144,128]{1,0:T(8,128)(2,1)S(1)} %get-tuple-element.70), channel_id=1, source_target_pairs={{0,8},{4,12},{8,0},{12,4},{16,24},{20,28},{24,16},{28,20},{1,9},{5... | collective-permute-start | bytes 110600 | tf_op jit(solution)/shard_map/ppermute | solution.py:26
  4.8 6.5 %collective-permute-start.6 = (bf16[144,128]{1,0:T(8,128)(2,1)S(1)}, bf16[144,128]{1,0:T(8,128)(2,1)S(1)}, u32[]{:S(2)}, u32[]{:S(2)}) collective-permute-start(bf16[144,128]{1,0:T(8,128)(2,1)S(1)} %get-tuple-element.70), channel_id=1, source_target_pairs={{0,16},{4,20},{8,24},{12,28},{16,0},{20,4},{24,8},{28,12},{1,17},{... | collective-permute-start | bytes 110600 | tf_op jit(solution)/shard_map/ppermute | solution.py:26
  7.4 5.8 %collective-permute-start.7 = (bf16[144,128]{1,0:T(8,128)(2,1)S(1)}, bf16[144,128]{1,0:T(8,128)(2,1)S(1)}, u32[]{:S(2)}, u32[]{:S(2)}) collective-permute-start(bf16[144,128]{1,0:T(8,128)(2,1)S(1)} %get-tuple-element.70), channel_id=1, source_target_pairs={{0,24},{4,28},{8,16},{12,20},{16,8},{20,12},{24,0},{28,4},{1,25},{... | collective-permute-start | bytes 110600 | tf_op jit(solution)/shard_map/ppermute | solution.py:26
  8.3 4.9 %collective-permute-start.8 = (bf16[2,128,256]{2,1,0:T(8,128)(2,1)S(1)}, bf16[2,128,256]{2,1,0:T(8,128)(2,1)S(1)}, u32[]{:S(2)}, u32[]{:S(2)}) collective-permute-start(bf16[2,128,256]{2,1,0:T(8,128)(2,1)S(1)} %pad_maximum_fusion.3.refs_0_.mine_ref), channel_id=1, source_target_pairs={{0,1},{1,0},{2,3},{3,2},{4,5},{5,4},{6,7},{7,6},{8,9},{9,8},{10,11... | collective-permute-start | bytes 393224 | tf_op jit(solution)/shard_map/ppermute | solution.py:26
  13.2 10.1 %collective-permute-start.12 = (bf16[256,4096]{1,0:T(8,128)(2,1)}, bf16[256,4096]{1,0:T(8,128)(2,1)}, u32[]{:S(2)}, u32[]{:S(2)}) collective-permute-start(bf16[256,4096]{1,0:T(8,128)(2,1)} %carve.2), channel_id=1, source_target_pairs={{0,1},{1,0},{2,3},{3,2},{4,5},{5,4},{6,7},{7,6},{8,9},{9,8},{10,11... | collective-permute-start | bytes 6291464 | tf_op jit(solution)/shard_map/ppermute | solution.py:26
  13.3 6.3 %collective-permute-start.10 = (bf16[4,144,128]{2,1,0:T(8,128)(2,1)S(1)}, bf16[4,144,128]{2,1,0:T(8,128)(2,1)S(1)}, u32[]{:S(2)}, u32[]{:S(2)}) collective-permute-start(bf16[4,144,128]{2,1,0:T(8,128)(2,1)S(1)} %pad_maximum_fusion.2.refs_0_), channel_id=1, source_target_pairs={{0,4},{4,0},{8,12},{12,8},{16,20},{20,16},{24,28},{28,24},{1,5},{5... | collective-permute-start | bytes 442376 | tf_op jit(solution)/shard_map/ppermute | solution.py:26
  14.8 4.8 %collective-permute-start.9 = (bf16[4,144,128]{2,1,0:T(8,128)(2,1)S(1)}, bf16[4,144,128]{2,1,0:T(8,128)(2,1)S(1)}, u32[]{:S(2)}, u32[]{:S(2)}) collective-permute-start(bf16[4,144,128]{2,1,0:T(8,128)(2,1)S(1)} %pad_maximum_fusion.2.refs_0_), channel_id=1, source_target_pairs={{0,1},{1,0},{2,3},{3,2},{4,5},{5,4},{6,7},{7,6},{8,9},{9,8},{10,11... | collective-permute-start | bytes 442376 | tf_op jit(solution)/shard_map/ppermute | solution.py:26
  15.0 4.5 %copy-start.1 = (s32[128]{0:T(128)S(1)}, s32[128]{0:T(128)}, u32[]{:S(2)}) copy-start(s32[128]{0:T(128)} %param.14) | copy-start | bytes 1540
  15.0 5.9 %copy-start.2 = (s32[128]{0:T(128)S(1)}, s32[128]{0:T(128)}, u32[]{:S(2)}) copy-start(s32[128]{0:T(128)} %param.15) | copy-start | bytes 1540
  19.6 1.4 %collective-permute-start.11 = (bf16[4,144,128]{2,1,0:T(8,128)(2,1)S(1)}, bf16[4,144,128]{2,1,0:T(8,128)(2,1)S(1)}, u32[]{:S(2)}, u32[]{:S(2)}) collective-permute-start(bf16[4,144,128]{2,1,0:T(8,128)(2,1)S(1)} %collective-permute-done.10.refs_2_), channel_id=1, source_target_pairs={{0,1},{1,0},{2,3},{3,2},{4,5},{5,4},{6,7},{7,6},{8,9},{9,8},{10,11... | collective-permute-start | bytes 442376 | tf_op jit(solution)/shard_map/ppermute | solution.py:26
  25.5 31.1 %collective-permute-start.15 = (bf16[128,3328]{1,0:T(8,128)(2,1)S(1)}, bf16[128,3328]{1,0:T(8,128)(2,1)}, u32[]{:S(2)}, u32[]{:S(2)}) collective-permute-start(bf16[128,3328]{1,0:T(8,128)(2,1)S(1)} %product.2), channel_id=1, source_target_pairs={{0,2},{1,3},{2,0},{3,1},{4,6},{5,7},{6,4},{7,5},{8,10},{9,11},{10,... | collective-permute-start | bytes 2555912 | tf_op jit(solution)/shard_map/ppermute | solution.py:26
  29.6 5.3 %collective-permute-start = (bf16[4,128,128]{2,1,0:T(8,128)(2,1)S(1)}, bf16[4,128,128]{2,1,0:T(8,128)(2,1)S(1)}, u32[]{:S(2)}, u32[]{:S(2)}) collective-permute-start(bf16[4,128,128]{2,1,0:T(8,128)(2,1)S(1)} %constant_dynamic-slice_fusion.2), channel_id=1, source_target_pairs={{0,4},{4,0},{8,12},{12,8},{16,20},{20,16},{24,28},{28,24},{1,5},{5... | collective-permute-start | bytes 393224 | tf_op jit(solution)/shard_map/while/body/ppermute | solution.py:26
  35.0 6.0 %collective-permute-start.1 = (bf16[128,128]{1,0:T(8,128)(2,1)S(1)}, bf16[128,128]{1,0:T(8,128)(2,1)S(1)}, u32[]{:S(2)}, u32[]{:S(2)}) collective-permute-start(bf16[128,128]{1,0:T(8,128)(2,1)S(1)} %get-tuple-element.102), channel_id=1, source_target_pairs={{0,24},{4,28},{8,16},{12,20},{16,8},{20,12},{24,0},{28,4},{1,25},{... | collective-permute-start | bytes 98312 | tf_op jit(solution)/shard_map/while/body/ppermute | solution.py:26
  37.1 4.8 %collective-permute-start.2 = (bf16[128,128]{1,0:T(8,128)(2,1)S(1)}, bf16[128,128]{1,0:T(8,128)(2,1)S(1)}, u32[]{:S(2)}, u32[]{:S(2)}) collective-permute-start(bf16[128,128]{1,0:T(8,128)(2,1)S(1)} %get-tuple-element.103), channel_id=1, source_target_pairs={{0,16},{4,20},{8,24},{12,28},{16,0},{20,4},{24,8},{28,12},{1,17},{... | collective-permute-start | bytes 98312 | tf_op jit(solution)/shard_map/while/body/ppermute | solution.py:26
  37.1 4.8 %collective-permute-start.3 = (bf16[128,128]{1,0:T(8,128)(2,1)S(1)}, bf16[128,128]{1,0:T(8,128)(2,1)S(1)}, u32[]{:S(2)}, u32[]{:S(2)}) collective-permute-start(bf16[128,128]{1,0:T(8,128)(2,1)S(1)} %get-tuple-element.104), channel_id=1, source_target_pairs={{0,8},{4,12},{8,0},{12,4},{16,24},{20,28},{24,16},{28,20},{1,9},{5... | collective-permute-start | bytes 98312 | tf_op jit(solution)/shard_map/while/body/ppermute | solution.py:26
  42.0 1.3 %collective-permute-start.4 = (bf16[128,128]{1,0:T(8,128)(2,1)S(1)}, bf16[128,128]{1,0:T(8,128)(2,1)S(1)}, u32[]{:S(2)}, u32[]{:S(2)}) collective-permute-start(bf16[128,128]{1,0:T(8,128)(2,1)S(1)} %fusion.11), channel_id=1, source_target_pairs={{0,1},{1,0},{2,3},{3,2},{4,5},{5,4},{6,7},{7,6},{8,9},{9,8},{10,11... | collective-permute-start | bytes 98312 | tf_op jit(solution)/shard_map/while/body/ppermute | solution.py:26
  43.9 4.3 %copy-start.3 = (bf16[128,256]{1,0:T(8,128)(2,1)S(1)}, bf16[128,256]{1,0:T(8,128)(2,1)}, u32[]{:S(2)}) copy-start(bf16[128,256]{1,0:T(8,128)(2,1)} %get-tuple-element.50.kv_ref) | copy-start | bytes 196612
  43.9 12.7 %copy-start = (bf16[256,4096]{1,0:T(8,128)(2,1)S(1)}, bf16[256,4096]{1,0:T(8,128)(2,1)}, u32[]{:S(2)}) copy-start(bf16[256,4096]{1,0:T(8,128)(2,1)} %w_ref.7) | copy-start | bytes 6291460
  47.6 9.0 %collective-permute-start.13 = (bf16[128,2048]{1,0:T(8,128)(2,1)S(1)}, bf16[128,2048]{1,0:T(8,128)(2,1)S(1)}, u32[]{:S(2)}, u32[]{:S(2)}) collective-permute-start(bf16[128,2048]{1,0:T(8,128)(2,1)S(1)} %get-tuple-element.53), channel_id=1, source_target_pairs={{0,1},{1,0},{2,3},{3,2},{4,5},{5,4},{6,7},{7,6},{8,9},{9,8},{10,11... | collective-permute-start | bytes 1572872 | tf_op jit(solution)/shard_map/ppermute | solution.py:26
  47.8 8.8 %collective-permute-start.14 = (bf16[128,2048]{1,0:T(8,128)(2,1)S(1)}, bf16[128,2048]{1,0:T(8,128)(2,1)S(1)}, u32[]{:S(2)}, u32[]{:S(2)}) collective-permute-start(bf16[128,2048]{1,0:T(8,128)(2,1)S(1)} %get-tuple-element.54), channel_id=1, source_target_pairs={{0,1},{1,0},{2,3},{3,2},{4,5},{5,4},{6,7},{7,6},{8,9},{9,8},{10,11... | collective-permute-start | bytes 1572872 | tf_op jit(solution)/shard_map/ppermute | solution.py:26
  48.2 8.4 %collective-permute-start.16 = (bf16[128,1024]{1,0:T(8,128)(2,1)S(1)}, bf16[128,1024]{1,0:T(8,128)(2,1)S(1)}, u32[]{:S(2)}, u32[]{:S(2)}) collective-permute-start(bf16[128,1024]{1,0:T(8,128)(2,1)S(1)} %pad_maximum_fusion.1), channel_id=1, source_target_pairs={{0,2},{1,3},{2,0},{3,1},{4,6},{5,7},{6,4},{7,5},{8,10},{9,11},{10,... | collective-permute-start | bytes 786440 | tf_op jit(solution)/shard_map/ppermute | solution.py:26

commit v10 on v8

--- a/solution.py
+++ b/solution.py
@@ -10,7 +10,7 @@
 
 RUN = 64
 META_ROWS = 16
-CHUNKS = (13, 3)
+CHUNKS = (12, 4)
 TILES = 4
 ANY = pl.BlockSpec(memory_space=pl.ANY)
 HBM = pl.BlockSpec(memory_space=pltpu.HBM)
@@ -46,37 +46,29 @@
     return jnp.concatenate([held, meta], axis=0)
 
 
-def carve_kernel(block_ref, w_ref, *refs):
-    outs, sems = refs[1:-1], refs[-1]
-    rows, share = outs[0].shape
-    parts = sems.shape[1]
-    copies = []
-    for i, out_ref in enumerate(outs):
-        at = pl.multiple_of(block_ref[i] * share, share)
-        for j in range(parts):
-            part = slice(j * (rows // parts), (j + 1) * (rows // parts))
-            source = w_ref.at[part, pl.ds(at, share)]
-            copies.append(pltpu.make_async_copy(source, out_ref.at[part, :], sems.at[i, j]))
-            copies[-1].start()
-    for one in copies:
-        one.wait()
-
-
-def carve(blocks, w_query, share, after):
-    block = jax.ShapeDtypeStruct((w_query.shape[0], share), w_query.dtype)
-    count = len(blocks)
+def column_block(block_ref, w_ref, share, first, width):
+    return w_ref.at[:, pl.ds(pl.multiple_of(block_ref[0] * share + first, 128), width)]
+
+
+def carve_kernel(block_ref, w_ref, after_ref, out_ref):
+    share = out_ref.shape[1]
+    tile = share // TILES
+    for i in range(TILES):
+        out_ref[:, i * tile : (i + 1) * tile] = column_block(block_ref, w_ref, share, i * tile, tile)[...]
+
+
+def carve(block, w_query, share, after):
     return pl.pallas_call(
         carve_kernel,
-        out_shape=[block] * count,
-        in_specs=[SMEM, HBM, ANY],
-        out_specs=[pl.BlockSpec(memory_space=pltpu.VMEM)] * count,
-        scratch_shapes=[pltpu.SemaphoreType.DMA((count, 4))],
-        compiler_params=params(48),
+        out_shape=jax.ShapeDtypeStruct((w_query.shape[0], share), w_query.dtype),
+        in_specs=[SMEM, pl.BlockSpec(), ANY],
+        out_specs=pl.BlockSpec(),
+        compiler_params=params(),
         cost_estimate=pl.CostEstimate(
-            flops=0, bytes_accessed=4 * count * w_query.shape[0] * share, transcendentals=0
+            flops=0, bytes_accessed=4 * w_query.shape[0] * share, transcendentals=0
         ),
         name="carve",
-    )(jnp.stack(blocks), w_query, after)
+    )(block.reshape(1), w_query, after)
 
 
 def attention_kernel(core_ref, pos_ref, doc_ref, mine_ref, swap_ref, *refs):
@@ -177,64 +169,58 @@
     )(core, positions.reshape(1, rows), doc_ids.reshape(1, rows), mine, swap, *pieces)
 
 
-def product_kernel(first, dq_ref, wm_ref, wo_ref, out_ref):
-    depth = wm_ref.shape[0]
-    at = slice(first, first + out_ref.shape[1])
-    acc = dot(dq_ref[:, 0:depth], wm_ref[:, at], ((1,), (0,)))
-    acc = acc + dot(dq_ref[:, depth:], wo_ref[:, at], ((1,), (0,)))
+def product_kernel(share, first, block_ref, dq_ref, w_ref, wo_ref, out_ref):
+    depth = w_ref.shape[0]
+    width = out_ref.shape[1]
+    mine = column_block(block_ref, w_ref, share, first, width)
+    acc = dot(dq_ref[:, 0:depth], mine[...], ((1,), (0,)))
+    acc = acc + dot(dq_ref[:, depth:], wo_ref[:, first : first + width], ((1,), (0,)))
     out_ref[...] = acc.astype(out_ref.dtype)
 
 
-def product(dq, w_mine, w_other, first, width, dtype):
+def product(block, dq, w_query, w_other, first, width):
     rows, depth = dq.shape
     return pl.pallas_call(
-        functools.partial(product_kernel, first),
-        out_shape=jax.ShapeDtypeStruct((rows, width), dtype),
-        in_specs=[pl.BlockSpec()] * 3,
+        functools.partial(product_kernel, w_other.shape[1], first),
+        out_shape=jax.ShapeDtypeStruct((rows, width), dq.dtype),
+        in_specs=[SMEM] + [pl.BlockSpec()] * 3,
         out_specs=pl.BlockSpec(),
-        compiler_params=params(16),
+        compiler_params=params(),
         cost_estimate=pl.CostEstimate(
             flops=2 * rows * depth * width, bytes_accessed=2 * depth * width, transcendentals=0
         ),
         name="product",
-    )(dq, w_mine, w_other)
-
-
-def own_kernel(block_ref, dq_ref, w_ref, *refs):
-    out_ref, wm_ref, sems = refs[TILES:]
-    depth, share = wm_ref.shape
+    )(block.reshape(1), dq, w_query, w_other)
+
+
+def own_kernel(block_ref, other_ref, dq_ref, w_ref, acc_ref, *give_refs):
+    depth = w_ref.shape[0]
+    share = acc_ref.shape[1]
     tile = share // TILES
-    copies = []
+    dq = dq_ref[:, 0:depth]
+    for i, give_ref in enumerate(give_refs):
+        block = column_block(other_ref, w_ref, share, i * tile, tile)
+        give_ref[...] = dot(dq, block[...], ((1,), (0,))).astype(jnp.bfloat16)
     for i in range(TILES):
-        at = pl.multiple_of(block_ref[0] * share + i * tile, tile)
-        target = wm_ref.at[:, i * tile : (i + 1) * tile]
-        copies.append(pltpu.make_async_copy(w_ref.at[:, pl.ds(at, tile)], target, sems.at[i]))
-        copies[i].start()
-    for i in range(TILES):
-        at = slice(i * tile, (i + 1) * tile)
-        acc = dot(dq_ref[:, depth:], refs[i][...], ((1,), (0,)))
-        copies[i].wait()
-        out_ref[:, at] = acc + dot(dq_ref[:, 0:depth], wm_ref[:, at], ((1,), (0,)))
-
-
-def own(block, dq, w_query, w_other):
-    rows, depth = dq.shape
-    share = TILES * w_other[0].shape[1]
+        block = column_block(block_ref, w_ref, share, i * tile, tile)
+        acc_ref[:, i * tile : (i + 1) * tile] = dot(dq, block[...], ((1,), (0,)))
+
+
+def own(block, other, dq, w_query, share):
+    rows = dq.shape[0]
     return pl.pallas_call(
         own_kernel,
-        out_shape=jax.ShapeDtypeStruct((rows, share), jnp.float32),
-        in_specs=[SMEM, pl.BlockSpec(), HBM] + [pl.BlockSpec()] * TILES,
-        out_specs=pl.BlockSpec(),
-        scratch_shapes=[pltpu.VMEM((depth // 2, share), w_query.dtype), pltpu.SemaphoreType.DMA((TILES,))],
-        compiler_params=params(48),
-        cost_estimate=pl.CostEstimate(
-            flops=2 * rows * depth * share, bytes_accessed=2 * depth * share, transcendentals=0
-        ),
+        out_shape=[jax.ShapeDtypeStruct((rows, share), jnp.float32)]
+        + [jax.ShapeDtypeStruct((rows, share // TILES), jnp.bfloat16)] * TILES,
+        in_specs=[SMEM] * 2 + [pl.BlockSpec()] * 2,
+        out_specs=[pl.BlockSpec()] * (1 + TILES),
+        compiler_params=params(),
         name="own",
-    )(block, dq, w_query, *w_other)
-
-
-def finish_kernel(core_ref, kv_ref, w_ref, acc_ref, first_ref, second_ref, out_ref, hold_ref, sems):
+    )(block.reshape(1), other.reshape(1), dq, w_query)
+
+
+def finish_kernel(core_ref, kv_ref, w_ref, acc_ref, first_ref, second_ref, *refs):
+    out_ref, hold_ref, sems = refs[TILES:]
     rows, share = acc_ref.shape
     pair = kv_ref.shape[1]
     size = pair // 2
@@ -251,7 +237,7 @@
     for i in range(TILES):
         low, high = i * tile, (i + 1) * tile
         w = jnp.concatenate([w_ref[at_mine, low:high], w_ref[at_other, low:high]], axis=0)
-        acc = acc_ref[:, low:high] + dot(kv, w, ((1,), (0,)))
+        acc = acc_ref[:, low:high] + refs[i][...].astype(jnp.float32) + dot(kv, w, ((1,), (0,)))
         come = []
         if low < cut:
             come.append(first_ref[:, low : min(high, cut)])
@@ -265,12 +251,12 @@
         one.wait()
 
 
-def finish(core, kv, w_kv, acc, first, second):
+def finish(core, kv, w_kv, acc, first, second, given):
     rows, share = acc.shape
     return pl.pallas_call(
         finish_kernel,
         out_shape=jax.ShapeDtypeStruct((rows, share), jnp.bfloat16),
-        in_specs=[SMEM] + [pl.BlockSpec()] * 5,
+        in_specs=[SMEM] + [pl.BlockSpec()] * (5 + TILES),
         out_specs=ANY,
         scratch_shapes=[pltpu.VMEM((rows, share), jnp.bfloat16), pltpu.SemaphoreType.DMA((TILES,))],
         compiler_params=params(),
@@ -278,7 +264,7 @@
             flops=2 * rows * kv.shape[1] * share, bytes_accessed=10 * rows * share, transcendentals=0
         ),
         name="finish",
-    )(core, kv, w_kv, acc, first, second)
+    )(core, kv, w_kv, acc, first, second, *given)
 
 
 def on_device(queries, keys, values, dout, positions, doc_ids, w_query, w_kv):
@@ -292,19 +278,17 @@
     along_z = [piece] + [swapped(piece, "ctx", 2 * s) for s in range(1, half)]
     both = jnp.stack([queries, dout])
     swap = swapped(both, "head", 1)
-    (far_send,) = carve([head ^ 3], w_query, share, both)
+    far_send = carve(head ^ 3, w_query, share, both)
     here_z, swap, far_send = lax.optimization_barrier((jnp.stack(along_z), swap, far_send))
     here_x = swapped(here_z, "ctx", 1)
     far_other = swapped(far_send, "head", 1)
     there_z = swapped(here_z, "head", 1)
-    (far_mine,) = carve([head ^ 2], w_query, share, here_z)
-    here_x, far_mine = lax.optimization_barrier((here_x, far_mine))
     there_x = swapped(here_x, "head", 1)
     dq, back = attention(core, positions, doc_ids, both, swap, (here_z, there_z, here_x, there_x))
 
     cut = CHUNKS[0] * (share // sum(CHUNKS))
-    first_part = product(dq, far_mine, far_other, 0, cut, jnp.bfloat16)
-    second_part = product(dq, far_mine, far_other, cut, share - cut, jnp.bfloat16)
+    first_part = product(head ^ 2, dq, w_query, far_other, 0, cut)
+    second_part = product(head ^ 2, dq, w_query, far_other, cut, share - cut)
     first = swapped(first_part, "head", 2)
 
     def exchange(trip, kv):
@@ -320,13 +304,11 @@
     trips = 1 + jnp.minimum(positions[0], 0)
     kv = lax.fori_loop(0, trips, exchange, jnp.zeros((queries.shape[0], 2 * keys.shape[1]), jnp.bfloat16))
 
-    near_send = carve([(head ^ 1) * TILES + i for i in range(TILES)], w_query, share // TILES, kv)
-    near_other = [swapped(one, "head", 1) for one in near_send]
-    second_part = jnp.concatenate([second_part, kv], axis=1)
-    second_part, first, dq = lax.optimization_barrier((second_part, first, dq))
-    second = swapped(second_part, "head", 2)
-    acc = own(head.reshape(1), dq, w_query, near_other)
-    return finish(core, kv, w_kv, acc, first, second)
+    kv, dq = lax.optimization_barrier((kv, dq))
+    second = swapped(jnp.concatenate([second_part, kv], axis=1), "head", 2)
+    acc, *give = own(head, head ^ 1, dq, w_query, share)
+    given = [swapped(one, "head", 1) for one in give]
+    return finish(core, kv, w_kv, acc, first, second, given)
 
 
 def solution(mesh):

time: 58.3 us -> 63.4 us (1.087)
  local copies, waits for them, and re-layouts: 1.41 us -> 11.5 us
  Pallas kernels: 18 us -> 8.1 us
  waiting for transfers between devices: 18.3 us -> 23.2 us
    pallas_call x6 -> x4, Pallas kernels: 14.3 us -> 3.08 us  [the longest x1 1.47 us: carve(): pl.pallas_call(carve_kernel, out_shape=jax.ShapeDtypeStruct((w_query.shap...]
    unnamed x8 -> x14, local copies, waits for them, and re-layouts: 0.01 us -> 10.1 us
    ppermute x19, waiting for transfers between devices: 18.3 us -> 23.2 us  [swapped(): lax.ppermute(value, axis, [(source, source ^ bits) for source in range(co...]
    pallas_call x1, Pallas kernels: 1.33 us -> 2.64 us  [finish(): pl.pallas_call(finish_kernel, out_shape=jax.ShapeDtypeStruct((rows, share...]
  transfers between devices with their start and end apart: 19 -> 19, of which waited for: 11 -> 11; matrix products, arithmetic and copies ran while one was open for 4% -> 4% of each run, Pallas kernels for 23% -> 8%
where the time goes in v10:
time: 63.4 us; the launch traced here: 63.1 us
  waiting for transfers between devices  23.2 us (37%)
  starting transfers between devices  17.4 us (27%)
  local copies, waits for them, and re-layouts  11.5 us (18%)
  Pallas kernels  8.1 us (13%)
  other arithmetic  2.63 us (4%)
    ppermute x19, waiting for transfers between devices, swapped(): lax.ppermute(value, axis, [(source, source ^ bits) for source in range(co...  23.2 us
    ppermute x19, starting transfers between devices, swapped(): lax.ppermute(value, axis, [(source, source ^ bits) for source in range(co...  17.4 us
    unnamed x14, local copies, waits for them, and re-layouts  10.1 us
    pallas_call x1, Pallas kernels, finish(): pl.pallas_call(finish_kernel, out_shape=jax.ShapeDtypeStruct((rows, share...  2.64 us
    pallas_call x1, Pallas kernels, attention(): pl.pallas_call(attention_kernel, out_shape=[jax.ShapeDtypeStruct((rows, 2...  2.37 us
    pallas_call x1, Pallas kernels, carve(): pl.pallas_call(carve_kernel, out_shape=jax.ShapeDtypeStruct((w_query.shap...  1.47 us
  transfers between devices with their start and end apart: 19, of which 11 were waited for; matrix products, arithmetic and copies ran while one was open for 4% of the time, Pallas kernels for 8%

profile of v10, /device:TPU:0, one launch (start us, length us, event | category | flops | bytes accessed | tf_op | source)
XLA Modules:
  0.0 63.1 jit_solution(5201909010908696414)
XLA Ops:
  0.0 0.7 %reshape.36 = s32[2,64]{1,0:T(2,128)S(1)} reshape(s32[128]{0:T(128)} %param.14) | data formatting | bytes 1024 | tf_op jit(solution)/shard_map/reshape | solution.py:44
  0.9 0.8 %broadcast_select_fusion = bf16[128,128]{1,0:T(8,128)(2,1)S(1)} fusion(bf16[128,128]{1,0:T(8,128)(2,1)} %param.11, bf16[128,128]{1,0:T(8,128)(2,1)} %param.12, pred[]{:T(512)} %bitcast.10), kind=kLoop, calls=%fused_computation.16 | loop fusion | flops 16384 | bytes 98305 | tf_op jit(solution)/shard_map/jit(_where)/select_n | solution.py:43
  1.7 4.1 %collective-permute-start.6 = (bf16[144,128]{1,0:T(8,128)(2,1)S(1)}, bf16[144,128]{1,0:T(8,128)(2,1)S(1)}, u32[]{:S(2)}, u32[]{:S(2)}) collective-permute-start(bf16[144,128]{1,0:T(8,128)(2,1)S(1)} %get-tuple-element.70), channel_id=1, source_target_pairs={{0,16},{4,20},{8,24},{12,28},{16,0},{20,4},{24,8},{28,12},{1,17},{... | collective-permute-start | bytes 110600 | tf_op jit(solution)/shard_map/ppermute | solution.py:26
  5.8 1.6 %collective-permute-start.5 = (bf16[144,128]{1,0:T(8,128)(2,1)S(1)}, bf16[144,128]{1,0:T(8,128)(2,1)S(1)}, u32[]{:S(2)}, u32[]{:S(2)}) collective-permute-start(bf16[144,128]{1,0:T(8,128)(2,1)S(1)} %get-tuple-element.70), channel_id=1, source_target_pairs={{0,8},{4,12},{8,0},{12,4},{16,24},{20,28},{24,16},{28,20},{1,9},{5... | collective-permute-start | bytes 110600 | tf_op jit(solution)/shard_map/ppermute | solution.py:26
  7.4 0.9 %pad_maximum_fusion.3.after_ref.mine_ref = bf16[2,128,256]{2,1,0:T(8,128)(2,1)S(1)} fusion(bf16[1,128,256]{2,1,0:T(8,128)(2,1)} %bitcast.40, bf16[1,128,256]{2,1,0:T(8,128)(2,1)} %bitcast.41), kind=kLoop, calls=%fused_computation.14 | loop fusion | flops 65536 | bytes 262144 | tf_op jit(solution)/shard_map/stack | solution.py:279
  8.4 3.4 %copy-done = bf16[256,16384]{1,0:T(8,128)(2,1)S(1)} copy-done((bf16[256,16384]{1,0:T(8,128)(2,1)S(1)}, bf16[256,16384]{1,0:T(8,128)(2,1)}, u32[]{:S(2)}) %copy-start) | copy-done | bytes 8388632
  11.8 1.5 %carve.1 = bf16[256,4096]{1,0:T(8,128)(2,1)} custom-call(s32[1]{0:T(128)} %bitcast.15.block_ref, bf16[256,16384]{1,0:T(8,128)(2,1)S(1)} %copy-done, bf16[2,128,256]{2,1,0:T(8,128)(2,1)S(1)} %pad_maximum_fusion.3.after_ref.mine_ref), custom_call_target="tpu_custom_call" | custom-call | bytes 4194304 | tf_op jit(solution)/shard_map/carve/pallas_call | solution.py:61
  13.3 0.6 collective-permute-start.12
  13.9 1.7 %collective-permute-start.10 = (bf16[4,144,128]{2,1,0:T(8,128)(2,1)S(1)}, bf16[4,144,128]{2,1,0:T(8,128)(2,1)S(1)}, u32[]{:S(2)}, u32[]{:S(2)}) collective-permute-start(bf16[4,144,128]{2,1,0:T(8,128)(2,1)S(1)} %pad_maximum_fusion.2.refs_0_), channel_id=1, source_target_pairs={{0,4},{4,0},{8,12},{12,8},{16,20},{20,16},{24,28},{28,24},{1,5},{5... | collective-permute-start | bytes 442376 | tf_op jit(solution)/shard_map/ppermute | solution.py:26
  15.6 4.1 %collective-permute-done.10.refs_2_ = bf16[4,144,128]{2,1,0:T(8,128)(2,1)S(1)} collective-permute-done((bf16[4,144,128]{2,1,0:T(8,128)(2,1)S(1)}, bf16[4,144,128]{2,1,0:T(8,128)(2,1)S(1)}, u32[]{:S(2)}, u32[]{:S(2)}) %collective-permute-start.10) | collective-permute-done | bytes 147488 | tf_op jit(solution)/shard_map/ppermute | solution.py:26
  19.8 1.3 %collective-permute-done.11.refs_3_ = bf16[4,144,128]{2,1,0:T(8,128)(2,1)S(1)} collective-permute-done((bf16[4,144,128]{2,1,0:T(8,128)(2,1)S(1)}, bf16[4,144,128]{2,1,0:T(8,128)(2,1)S(1)}, u32[]{:S(2)}, u32[]{:S(2)}) %collective-permute-start.11) | collective-permute-done | bytes 147488 | tf_op jit(solution)/shard_map/ppermute | solution.py:26
  21.1 2.4 %attention.1 = (bf16[128,512]{1,0:T(8,128)(2,1)S(1)}, bf16[8,128,128]{2,1,0:T(8,128)(2,1)S(1)}) custom-call(s32[1]{0:T(128)} %bitcast.4.core_ref, s32[1,128]{1,0:T(1,128)S(1)} %bitcast.38, s32[1,128]{1,0:T(1,128)S(1)} %bitcast.39, bf16[2,128,256]{2,1,0:T(8,128)(2,1)S(1)} %pad_maximum_fusion.3.after_ref.mine_ref, ...), custom_call_target="tpu_custom_call" | custom-call | flops 671088640 | bytes 1048576 | tf_op jit(solution)/shard_map/attention/pallas_call | solution.py:153
  23.5 3.4 %copy-done.1 = bf16[256,16384]{1,0:T(8,128)(2,1)S(1)} copy-done((bf16[256,16384]{1,0:T(8,128)(2,1)S(1)}, bf16[256,16384]{1,0:T(8,128)(2,1)}, u32[]{:S(2)}) %copy-start.1) | copy-done | bytes 8388632
  26.9 0.6 product.2
  27.4 1.8 %collective-permute-start.13 = (bf16[128,3072]{1,0:T(8,128)(2,1)S(1)}, bf16[128,3072]{1,0:T(8,128)(2,1)}, u32[]{:S(2)}, u32[]{:S(2)}) collective-permute-start(bf16[128,3072]{1,0:T(8,128)(2,1)S(1)} %product.2), channel_id=1, source_target_pairs={{0,2},{1,3},{2,0},{3,1},{4,6},{5,7},{6,4},{7,5},{8,10},{9,11},{10,... | collective-permute-start | bytes 2359304 | tf_op jit(solution)/shard_map/ppermute | solution.py:26
  29.6 0.6 %broadcast_in_dim.16 = bf16[128,256]{1,0:T(8,128)(2,1)} broadcast(bf16[]{:T(256)} %constant.34.clone.1), dimensions={} | broadcast | bytes 65538 | tf_op jit(solution)/shard_map/broadcast_in_dim | solution.py:305
  30.2 15.8 %while.10 = (s32[]{:T(128)}, bf16[128,256]{1,0:T(8,128)(2,1)}, s32[]{:T(128)}, bf16[8,128,128]{2,1,0:T(8,128)(2,1)S(1)}, s32[]{:T(128)}, /*index=5*/s32[]{:T(128)}, s32[]{:T(128)}, s32[]{:T(128)}) while((s32[]{:T(128)}, bf16[128,256]{1,0:T(8,128)(2,1)}, s32[]{:T(128)}, bf16[8,128,128]{2,1,0:T(8,128)(2,1)S(1)}, s32[]{:T(128)}, ...), condition=%wide.region_1.2_spmd, body=%wide.region_0.1_spmd.sunk | while | flops 507911 | bytes 2490715 | solution.py:305
  30.2 1.5 %collective-permute-start = (bf16[4,128,128]{2,1,0:T(8,128)(2,1)S(1)}, bf16[4,128,128]{2,1,0:T(8,128)(2,1)S(1)}, u32[]{:S(2)}, u32[]{:S(2)}) collective-permute-start(bf16[4,128,128]{2,1,0:T(8,128)(2,1)S(1)} %constant_dynamic-slice_fusion.2), channel_id=1, source_target_pairs={{0,4},{4,0},{8,12},{12,8},{16,20},{20,16},{24,28},{28,24},{1,5},{5... | collective-permute-start | bytes 393224 | tf_op jit(solution)/shard_map/while/body/ppermute | solution.py:26
  31.8 3.8 %collective-permute-done = bf16[4,128,128]{2,1,0:T(8,128)(2,1)S(1)} collective-permute-done((bf16[4,128,128]{2,1,0:T(8,128)(2,1)S(1)}, bf16[4,128,128]{2,1,0:T(8,128)(2,1)S(1)}, u32[]{:S(2)}, u32[]{:S(2)}) %collective-permute-start) | collective-permute-done | bytes 131104 | tf_op jit(solution)/shard_map/while/body/ppermute | solution.py:26
  35.6 3.7 %collective-permute-start.1 = (bf16[128,128]{1,0:T(8,128)(2,1)S(1)}, bf16[128,128]{1,0:T(8,128)(2,1)S(1)}, u32[]{:S(2)}, u32[]{:S(2)}) collective-permute-start(bf16[128,128]{1,0:T(8,128)(2,1)S(1)} %get-tuple-element.102), channel_id=1, source_target_pairs={{0,24},{4,28},{8,16},{12,20},{16,8},{20,12},{24,0},{28,4},{1,25},{... | collective-permute-start | bytes 98312 | tf_op jit(solution)/shard_map/while/body/ppermute | solution.py:26
  39.3 0.8 %collective-permute-start.3 = (bf16[128,128]{1,0:T(8,128)(2,1)S(1)}, bf16[128,128]{1,0:T(8,128)(2,1)S(1)}, u32[]{:S(2)}, u32[]{:S(2)}) collective-permute-start(bf16[128,128]{1,0:T(8,128)(2,1)S(1)} %get-tuple-element.104), channel_id=1, source_target_pairs={{0,8},{4,12},{8,0},{12,4},{16,24},{20,28},{24,16},{28,20},{1,9},{5... | collective-permute-start | bytes 98312 | tf_op jit(solution)/shard_map/while/body/ppermute | solution.py:26
  40.1 1.3 %collective-permute-done.1 = bf16[128,128]{1,0:T(8,128)(2,1)S(1)} collective-permute-done((bf16[128,128]{1,0:T(8,128)(2,1)S(1)}, bf16[128,128]{1,0:T(8,128)(2,1)S(1)}, u32[]{:S(2)}, u32[]{:S(2)}) %collective-permute-start.1) | collective-permute-done | bytes 32800 | tf_op jit(solution)/shard_map/while/body/ppermute | solution.py:26
  41.4 2.7 %collective-permute-done.2 = bf16[128,128]{1,0:T(8,128)(2,1)S(1)} collective-permute-done((bf16[128,128]{1,0:T(8,128)(2,1)S(1)}, bf16[128,128]{1,0:T(8,128)(2,1)S(1)}, u32[]{:S(2)}, u32[]{:S(2)}) %collective-permute-start.2) | collective-permute-done | bytes 32800 | tf_op jit(solution)/shard_map/while/body/ppermute | solution.py:26
  44.2 1.2 %collective-permute-done.4 = bf16[128,128]{1,0:T(8,128)(2,1)S(1)} collective-permute-done((bf16[128,128]{1,0:T(8,128)(2,1)S(1)}, bf16[128,128]{1,0:T(8,128)(2,1)S(1)}, u32[]{:S(2)}, u32[]{:S(2)}) %collective-permute-start.4) | collective-permute-done | bytes 32800 | tf_op jit(solution)/shard_map/while/body/ppermute | solution.py:26
  45.4 0.6 %pad_maximum_fusion.6 = bf16[128,256]{1,0:T(8,128)(2,1)} fusion(bf16[128,128]{1,0:T(8,128)(2,1)S(1)} %collective-permute-done.4, bf16[128,128]{1,0:T(8,128)(2,1)S(1)} %fusion.11), kind=kLoop, calls=%fused_computation.6.clone.1 | loop fusion | flops 131072 | bytes 131072 | tf_op jit(solution)/shard_map/while/body/concatenate | solution.py:301
  46.0 3.4 %copy-done.2 = bf16[256,16384]{1,0:T(8,128)(2,1)S(1)} copy-done((bf16[256,16384]{1,0:T(8,128)(2,1)S(1)}, bf16[256,16384]{1,0:T(8,128)(2,1)}, u32[]{:S(2)}) %copy-start.2) | copy-done | bytes 8388632
  49.4 0.7 %own.1 = (f32[128,4096]{1,0:T(8,128)S(1)}, bf16[128,1024]{1,0:T(8,128)(2,1)S(1)}, bf16[128,1024]{1,0:T(8,128)(2,1)S(1)}, bf16[128,1024]{1,0:T(8,128)(2,1)S(1)}, bf16[128,1024]{1,0:T(8,128)(2,1)S(1)}) custom-call(s32[1]{0:T(128)} %bitcast.17.block_ref, s32[1]{0:T(128)} %bitcast.18.other_ref, bf16[128,512]{1,0:T(8,128)(2,1)S(1)} %get-tuple-element.49.dq_ref, ...), custom_call_target="tpu_custom_call" | custom-call | tf_op jit(solution)/shard_map/own/pallas_call | solution.py:211
  50.4 0.6 collective-permute-start.14
  51.0 0.4 collective-permute-start.17
  51.9 0.6 collective-permute-done.16.refs_1_
  53.3 7.1 %collective-permute-done.14.second_ref = bf16[128,1280]{1,0:T(8,128)(2,1)S(1)} collective-permute-done((bf16[128,1280]{1,0:T(8,128)(2,1)S(1)}, bf16[128,1280]{1,0:T(8,128)(2,1)S(1)}, u32[]{:S(2)}, u32[]{:S(2)}) %collective-permute-start.14) | collective-permute-done | bytes 327712 | tf_op jit(solution)/shard_map/ppermute | solution.py:26
  60.4 2.6 %finish.1 = bf16[128,4096]{1,0:T(8,128)(2,1)} custom-call(s32[1]{0:T(128)} %bitcast.4.core_ref, bf16[128,256]{1,0:T(8,128)(2,1)S(1)} %copy-done.6, bf16[256,4096]{1,0:T(8,128)(2,1)S(1)} %copy-done.3, f32[128,4096]{1,0:T(8,128)S(1)} %get-tuple-element.50.acc_ref, bf16[128,3072]{1,0:T(8,128)(2,1)} %collective-permute-done.13.first_ref, ...), custom_call_target="tpu_custom_call" | custom-call | flops 268435456 | bytes 5242880 | tf_op jit(solution)/shard_map/finish/pallas_call | solution.py:256
  (41 shorter events, 2.3 us)
Async XLA Ops:
  1.7 11.5 %collective-permute-start.6 = (bf16[144,128]{1,0:T(8,128)(2,1)S(1)}, bf16[144,128]{1,0:T(8,128)(2,1)S(1)}, u32[]{:S(2)}, u32[]{:S(2)}) collective-permute-start(bf16[144,128]{1,0:T(8,128)(2,1)S(1)} %get-tuple-element.70), channel_id=1, source_target_pairs={{0,16},{4,20},{8,24},{12,28},{16,0},{20,4},{24,8},{28,12},{1,17},{... | collective-permute-start | bytes 110600 | tf_op jit(solution)/shard_map/ppermute | solution.py:26
  5.8 7.4 %collective-permute-start.5 = (bf16[144,128]{1,0:T(8,128)(2,1)S(1)}, bf16[144,128]{1,0:T(8,128)(2,1)S(1)}, u32[]{:S(2)}, u32[]{:S(2)}) collective-permute-start(bf16[144,128]{1,0:T(8,128)(2,1)S(1)} %get-tuple-element.70), channel_id=1, source_target_pairs={{0,8},{4,12},{8,0},{12,4},{16,24},{20,28},{24,16},{28,20},{1,9},{5... | collective-permute-start | bytes 110600 | tf_op jit(solution)/shard_map/ppermute | solution.py:26
  7.4 5.8 %collective-permute-start.7 = (bf16[144,128]{1,0:T(8,128)(2,1)S(1)}, bf16[144,128]{1,0:T(8,128)(2,1)S(1)}, u32[]{:S(2)}, u32[]{:S(2)}) collective-permute-start(bf16[144,128]{1,0:T(8,128)(2,1)S(1)} %get-tuple-element.70), channel_id=1, source_target_pairs={{0,24},{4,28},{8,16},{12,20},{16,8},{20,12},{24,0},{28,4},{1,25},{... | collective-permute-start | bytes 110600 | tf_op jit(solution)/shard_map/ppermute | solution.py:26
  8.3 5.0 %collective-permute-start.8 = (bf16[2,128,256]{2,1,0:T(8,128)(2,1)S(1)}, bf16[2,128,256]{2,1,0:T(8,128)(2,1)S(1)}, u32[]{:S(2)}, u32[]{:S(2)}) collective-permute-start(bf16[2,128,256]{2,1,0:T(8,128)(2,1)S(1)} %pad_maximum_fusion.3.after_ref.mine_ref), channel_id=1, source_target_pairs={{0,1},{1,0},{2,3},{3,2},{4,5},{5,4},{6,7},{7,6},{8,9},{9,8},{10,11... | collective-permute-start | bytes 393224 | tf_op jit(solution)/shard_map/ppermute | solution.py:26
  8.4 3.4 %copy-start = (bf16[256,16384]{1,0:T(8,128)(2,1)S(1)}, bf16[256,16384]{1,0:T(8,128)(2,1)}, u32[]{:S(2)}) copy-start(bf16[256,16384]{1,0:T(8,128)(2,1)} %w_ref.8) | copy-start | bytes 25165828
  11.8 7.9 %copy-start.4 = (s32[128]{0:T(128)S(1)}, s32[128]{0:T(128)}, u32[]{:S(2)}) copy-start(s32[128]{0:T(128)} %param.14) | copy-start | bytes 1540
  11.8 9.3 %copy-start.5 = (s32[128]{0:T(128)S(1)}, s32[128]{0:T(128)}, u32[]{:S(2)}) copy-start(s32[128]{0:T(128)} %param.15) | copy-start | bytes 1540
  13.3 10.1 %collective-permute-start.12 = (bf16[256,4096]{1,0:T(8,128)(2,1)}, bf16[256,4096]{1,0:T(8,128)(2,1)S(1)}, u32[]{:S(2)}, u32[]{:S(2)}) collective-permute-start(bf16[256,4096]{1,0:T(8,128)(2,1)} %carve.1), channel_id=1, source_target_pairs={{0,1},{1,0},{2,3},{3,2},{4,5},{5,4},{6,7},{7,6},{8,9},{9,8},{10,11... | collective-permute-start | bytes 6291464 | tf_op jit(solution)/shard_map/ppermute | solution.py:26
  13.9 5.8 %collective-permute-start.10 = (bf16[4,144,128]{2,1,0:T(8,128)(2,1)S(1)}, bf16[4,144,128]{2,1,0:T(8,128)(2,1)S(1)}, u32[]{:S(2)}, u32[]{:S(2)}) collective-permute-start(bf16[4,144,128]{2,1,0:T(8,128)(2,1)S(1)} %pad_maximum_fusion.2.refs_0_), channel_id=1, source_target_pairs={{0,4},{4,0},{8,12},{12,8},{16,20},{20,16},{24,28},{28,24},{1,5},{5... | collective-permute-start | bytes 442376 | tf_op jit(solution)/shard_map/ppermute | solution.py:26
  15.6 4.2 %collective-permute-start.9 = (bf16[4,144,128]{2,1,0:T(8,128)(2,1)S(1)}, bf16[4,144,128]{2,1,0:T(8,128)(2,1)S(1)}, u32[]{:S(2)}, u32[]{:S(2)}) collective-permute-start(bf16[4,144,128]{2,1,0:T(8,128)(2,1)S(1)} %pad_maximum_fusion.2.refs_0_), channel_id=1, source_target_pairs={{0,1},{1,0},{2,3},{3,2},{4,5},{5,4},{6,7},{7,6},{8,9},{9,8},{10,11... | collective-permute-start | bytes 442376 | tf_op jit(solution)/shard_map/ppermute | solution.py:26
  19.7 1.4 %collective-permute-start.11 = (bf16[4,144,128]{2,1,0:T(8,128)(2,1)S(1)}, bf16[4,144,128]{2,1,0:T(8,128)(2,1)S(1)}, u32[]{:S(2)}, u32[]{:S(2)}) collective-permute-start(bf16[4,144,128]{2,1,0:T(8,128)(2,1)S(1)} %collective-permute-done.10.refs_2_), channel_id=1, source_target_pairs={{0,1},{1,0},{2,3},{3,2},{4,5},{5,4},{6,7},{7,6},{8,9},{9,8},{10,11... | collective-permute-start | bytes 442376 | tf_op jit(solution)/shard_map/ppermute | solution.py:26
  23.5 3.4 %copy-start.1 = (bf16[256,16384]{1,0:T(8,128)(2,1)S(1)}, bf16[256,16384]{1,0:T(8,128)(2,1)}, u32[]{:S(2)}) copy-start(bf16[256,16384]{1,0:T(8,128)(2,1)} %w_ref.8) | copy-start | bytes 25165828
  27.4 33.0 %collective-permute-start.13 = (bf16[128,3072]{1,0:T(8,128)(2,1)S(1)}, bf16[128,3072]{1,0:T(8,128)(2,1)}, u32[]{:S(2)}, u32[]{:S(2)}) collective-permute-start(bf16[128,3072]{1,0:T(8,128)(2,1)S(1)} %product.2), channel_id=1, source_target_pairs={{0,2},{1,3},{2,0},{3,1},{4,6},{5,7},{6,4},{7,5},{8,10},{9,11},{10,... | collective-permute-start | bytes 2359304 | tf_op jit(solution)/shard_map/ppermute | solution.py:26
  30.2 5.3 %collective-permute-start = (bf16[4,128,128]{2,1,0:T(8,128)(2,1)S(1)}, bf16[4,128,128]{2,1,0:T(8,128)(2,1)S(1)}, u32[]{:S(2)}, u32[]{:S(2)}) collective-permute-start(bf16[4,128,128]{2,1,0:T(8,128)(2,1)S(1)} %constant_dynamic-slice_fusion.2), channel_id=1, source_target_pairs={{0,4},{4,0},{8,12},{12,8},{16,20},{20,16},{24,28},{28,24},{1,5},{5... | collective-permute-start | bytes 393224 | tf_op jit(solution)/shard_map/while/body/ppermute | solution.py:26
  35.6 5.8 %collective-permute-start.1 = (bf16[128,128]{1,0:T(8,128)(2,1)S(1)}, bf16[128,128]{1,0:T(8,128)(2,1)S(1)}, u32[]{:S(2)}, u32[]{:S(2)}) collective-permute-start(bf16[128,128]{1,0:T(8,128)(2,1)S(1)} %get-tuple-element.102), channel_id=1, source_target_pairs={{0,24},{4,28},{8,16},{12,20},{16,8},{20,12},{24,0},{28,4},{1,25},{... | collective-permute-start | bytes 98312 | tf_op jit(solution)/shard_map/while/body/ppermute | solution.py:26
  39.3 4.8 %collective-permute-start.2 = (bf16[128,128]{1,0:T(8,128)(2,1)S(1)}, bf16[128,128]{1,0:T(8,128)(2,1)S(1)}, u32[]{:S(2)}, u32[]{:S(2)}) collective-permute-start(bf16[128,128]{1,0:T(8,128)(2,1)S(1)} %get-tuple-element.103), channel_id=1, source_target_pairs={{0,16},{4,20},{8,24},{12,28},{16,0},{20,4},{24,8},{28,12},{1,17},{... | collective-permute-start | bytes 98312 | tf_op jit(solution)/shard_map/while/body/ppermute | solution.py:26
  39.3 4.8 %collective-permute-start.3 = (bf16[128,128]{1,0:T(8,128)(2,1)S(1)}, bf16[128,128]{1,0:T(8,128)(2,1)S(1)}, u32[]{:S(2)}, u32[]{:S(2)}) collective-permute-start(bf16[128,128]{1,0:T(8,128)(2,1)S(1)} %get-tuple-element.104), channel_id=1, source_target_pairs={{0,8},{4,12},{8,0},{12,4},{16,24},{20,28},{24,16},{28,20},{1,9},{5... | collective-permute-start | bytes 98312 | tf_op jit(solution)/shard_map/while/body/ppermute | solution.py:26
  44.1 1.3 %collective-permute-start.4 = (bf16[128,128]{1,0:T(8,128)(2,1)S(1)}, bf16[128,128]{1,0:T(8,128)(2,1)S(1)}, u32[]{:S(2)}, u32[]{:S(2)}) collective-permute-start(bf16[128,128]{1,0:T(8,128)(2,1)S(1)} %fusion.11), channel_id=1, source_target_pairs={{0,1},{1,0},{2,3},{3,2},{4,5},{5,4},{6,7},{7,6},{8,9},{9,8},{10,11... | collective-permute-start | bytes 98312 | tf_op jit(solution)/shard_map/while/body/ppermute | solution.py:26
  46.0 3.4 %copy-start.2 = (bf16[256,16384]{1,0:T(8,128)(2,1)S(1)}, bf16[256,16384]{1,0:T(8,128)(2,1)}, u32[]{:S(2)}) copy-start(bf16[256,16384]{1,0:T(8,128)(2,1)} %w_ref.8) | copy-start | bytes 25165828
  49.4 1.0 %copy-start.6 = (bf16[128,256]{1,0:T(8,128)(2,1)S(1)}, bf16[128,256]{1,0:T(8,128)(2,1)}, u32[]{:S(2)}) copy-start(bf16[128,256]{1,0:T(8,128)(2,1)} %get-tuple-element.48.kv_ref) | copy-start | bytes 196612
  49.4 11.0 %copy-start.3 = (bf16[256,4096]{1,0:T(8,128)(2,1)S(1)}, bf16[256,4096]{1,0:T(8,128)(2,1)}, u32[]{:S(2)}) copy-start(bf16[256,4096]{1,0:T(8,128)(2,1)} %w_ref.9) | copy-start | bytes 6291460
  50.1 1.6 %collective-permute-start.15 = (bf16[128,1024]{1,0:T(8,128)(2,1)S(1)}, bf16[128,1024]{1,0:T(8,128)(2,1)S(1)}, u32[]{:S(2)}, u32[]{:S(2)}) collective-permute-start(bf16[128,1024]{1,0:T(8,128)(2,1)S(1)} %get-tuple-element.52), channel_id=1, source_target_pairs={{0,1},{1,0},{2,3},{3,2},{4,5},{5,4},{6,7},{7,6},{8,9},{9,8},{10,11... | collective-permute-start | bytes 786440 | tf_op jit(solution)/shard_map/ppermute | solution.py:26
  50.4 10.0 %collective-permute-start.14 = (bf16[128,1280]{1,0:T(8,128)(2,1)S(1)}, bf16[128,1280]{1,0:T(8,128)(2,1)S(1)}, u32[]{:S(2)}, u32[]{:S(2)}) collective-permute-start(bf16[128,1280]{1,0:T(8,128)(2,1)S(1)} %pad_maximum_fusion.1), channel_id=1, source_target_pairs={{0,2},{1,3},{2,0},{3,1},{4,6},{5,7},{6,4},{7,5},{8,10},{9,11},{10,... | collective-permute-start | bytes 983048 | tf_op jit(solution)/shard_map/ppermute | solution.py:26
  51.0 1.5 %collective-permute-start.16 = (bf16[128,1024]{1,0:T(8,128)(2,1)S(1)}, bf16[128,1024]{1,0:T(8,128)(2,1)S(1)}, u32[]{:S(2)}, u32[]{:S(2)}) collective-permute-start(bf16[128,1024]{1,0:T(8,128)(2,1)S(1)} %get-tuple-element.53), channel_id=1, source_target_pairs={{0,1},{1,0},{2,3},{3,2},{4,5},{5,4},{6,7},{7,6},{8,9},{9,8},{10,11... | collective-permute-start | bytes 786440 | tf_op jit(solution)/shard_map/ppermute | solution.py:26
  51.0 1.8 %collective-permute-start.17 = (bf16[128,1024]{1,0:T(8,128)(2,1)S(1)}, bf16[128,1024]{1,0:T(8,128)(2,1)S(1)}, u32[]{:S(2)}, u32[]{:S(2)}) collective-permute-start(bf16[128,1024]{1,0:T(8,128)(2,1)S(1)} %get-tuple-element.54), channel_id=1, source_target_pairs={{0,1},{1,0},{2,3},{3,2},{4,5},{5,4},{6,7},{7,6},{8,9},{9,8},{10,11... | collective-permute-start | bytes 786440 | tf_op jit(solution)/shard_map/ppermute | solution.py:26
  51.7 1.5 %collective-permute-start.18 = (bf16[128,1024]{1,0:T(8,128)(2,1)S(1)}, bf16[128,1024]{1,0:T(8,128)(2,1)S(1)}, u32[]{:S(2)}, u32[]{:S(2)}) collective-permute-start(bf16[128,1024]{1,0:T(8,128)(2,1)S(1)} %get-tuple-element.55), channel_id=1, source_target_pairs={{0,1},{1,0},{2,3},{3,2},{4,5},{5,4},{6,7},{7,6},{8,9},{9,8},{10,11... | collective-permute-start | bytes 786440 | tf_op jit(solution)/shard_map/ppermute | solution.py:26

commit v11 on v8

--- a/solution.py
+++ b/solution.py
@@ -46,37 +46,9 @@
     return jnp.concatenate([held, meta], axis=0)
 
 
-def carve_kernel(block_ref, w_ref, *refs):
-    outs, sems = refs[1:-1], refs[-1]
-    rows, share = outs[0].shape
-    parts = sems.shape[1]
-    copies = []
-    for i, out_ref in enumerate(outs):
-        at = pl.multiple_of(block_ref[i] * share, share)
-        for j in range(parts):
-            part = slice(j * (rows // parts), (j + 1) * (rows // parts))
-            source = w_ref.at[part, pl.ds(at, share)]
-            copies.append(pltpu.make_async_copy(source, out_ref.at[part, :], sems.at[i, j]))
-            copies[-1].start()
-    for one in copies:
-        one.wait()
-
-
-def carve(blocks, w_query, share, after):
-    block = jax.ShapeDtypeStruct((w_query.shape[0], share), w_query.dtype)
-    count = len(blocks)
-    return pl.pallas_call(
-        carve_kernel,
-        out_shape=[block] * count,
-        in_specs=[SMEM, HBM, ANY],
-        out_specs=[pl.BlockSpec(memory_space=pltpu.VMEM)] * count,
-        scratch_shapes=[pltpu.SemaphoreType.DMA((count, 4))],
-        compiler_params=params(48),
-        cost_estimate=pl.CostEstimate(
-            flops=0, bytes_accessed=4 * count * w_query.shape[0] * share, transcendentals=0
-        ),
-        name="carve",
-    )(jnp.stack(blocks), w_query, after)
+def column_block(w_query, block, share, after):
+    w_query, _ = lax.optimization_barrier((w_query, after))
+    return lax.dynamic_slice_in_dim(w_query, block * share, share, axis=1)
 
 
 def attention_kernel(core_ref, pos_ref, doc_ref, mine_ref, swap_ref, *refs):
@@ -192,46 +164,12 @@
         out_shape=jax.ShapeDtypeStruct((rows, width), dtype),
         in_specs=[pl.BlockSpec()] * 3,
         out_specs=pl.BlockSpec(),
-        compiler_params=params(16),
+        compiler_params=params(),
         cost_estimate=pl.CostEstimate(
             flops=2 * rows * depth * width, bytes_accessed=2 * depth * width, transcendentals=0
         ),
         name="product",
     )(dq, w_mine, w_other)
-
-
-def own_kernel(block_ref, dq_ref, w_ref, *refs):
-    out_ref, wm_ref, sems = refs[TILES:]
-    depth, share = wm_ref.shape
-    tile = share // TILES
-    copies = []
-    for i in range(TILES):
-        at = pl.multiple_of(block_ref[0] * share + i * tile, tile)
-        target = wm_ref.at[:, i * tile : (i + 1) * tile]
-        copies.append(pltpu.make_async_copy(w_ref.at[:, pl.ds(at, tile)], target, sems.at[i]))
-        copies[i].start()
-    for i in range(TILES):
-        at = slice(i * tile, (i + 1) * tile)
-        acc = dot(dq_ref[:, depth:], refs[i][...], ((1,), (0,)))
-        copies[i].wait()
-        out_ref[:, at] = acc + dot(dq_ref[:, 0:depth], wm_ref[:, at], ((1,), (0,)))
-
-
-def own(block, dq, w_query, w_other):
-    rows, depth = dq.shape
-    share = TILES * w_other[0].shape[1]
-    return pl.pallas_call(
-        own_kernel,
-        out_shape=jax.ShapeDtypeStruct((rows, share), jnp.float32),
-        in_specs=[SMEM, pl.BlockSpec(), HBM] + [pl.BlockSpec()] * TILES,
-        out_specs=pl.BlockSpec(),
-        scratch_shapes=[pltpu.VMEM((depth // 2, share), w_query.dtype), pltpu.SemaphoreType.DMA((TILES,))],
-        compiler_params=params(48),
-        cost_estimate=pl.CostEstimate(
-            flops=2 * rows * depth * share, bytes_accessed=2 * depth * share, transcendentals=0
-        ),
-        name="own",
-    )(block, dq, w_query, *w_other)
 
 
 def finish_kernel(core_ref, kv_ref, w_ref, acc_ref, first_ref, second_ref, out_ref, hold_ref, sems):
@@ -292,14 +230,17 @@
     along_z = [piece] + [swapped(piece, "ctx", 2 * s) for s in range(1, half)]
     both = jnp.stack([queries, dout])
     swap = swapped(both, "head", 1)
-    (far_send,) = carve([head ^ 3], w_query, share, both)
+    far_send = column_block(w_query, head ^ 3, share, both)
     here_z, swap, far_send = lax.optimization_barrier((jnp.stack(along_z), swap, far_send))
     here_x = swapped(here_z, "ctx", 1)
     far_other = swapped(far_send, "head", 1)
     there_z = swapped(here_z, "head", 1)
-    (far_mine,) = carve([head ^ 2], w_query, share, here_z)
-    here_x, far_mine = lax.optimization_barrier((here_x, far_mine))
+    far_mine = column_block(w_query, head ^ 2, share, here_z)
+    near_send = column_block(w_query, head ^ 1, share, here_z)
+    here_x, far_mine, near_send = lax.optimization_barrier((here_x, far_mine, near_send))
     there_x = swapped(here_x, "head", 1)
+    there_x, near_send = lax.optimization_barrier((there_x, near_send))
+    near_other = swapped(near_send, "head", 1)
     dq, back = attention(core, positions, doc_ids, both, swap, (here_z, there_z, here_x, there_x))
 
     cut = CHUNKS[0] * (share // sum(CHUNKS))
@@ -320,12 +261,9 @@
     trips = 1 + jnp.minimum(positions[0], 0)
     kv = lax.fori_loop(0, trips, exchange, jnp.zeros((queries.shape[0], 2 * keys.shape[1]), jnp.bfloat16))
 
-    near_send = carve([(head ^ 1) * TILES + i for i in range(TILES)], w_query, share // TILES, kv)
-    near_other = [swapped(one, "head", 1) for one in near_send]
-    second_part = jnp.concatenate([second_part, kv], axis=1)
-    second_part, first, dq = lax.optimization_barrier((second_part, first, dq))
-    second = swapped(second_part, "head", 2)
-    acc = own(head.reshape(1), dq, w_query, near_other)
+    second = swapped(jnp.concatenate([second_part, kv], axis=1), "head", 2)
+    near_mine = column_block(w_query, head, share, kv)
+    acc = product(dq, near_mine, near_other, 0, share, jnp.float32)
     return finish(core, kv, w_kv, acc, first, second)
 
 

time: 58.3 us -> 56.3 us (0.966)
  local copies, waits for them, and re-layouts: 1.41 us -> 10.2 us
  Pallas kernels: 18 us -> 11.1 us
  waiting for transfers between devices: 18.3 us -> 14.7 us
  starting transfers between devices: 17.3 us -> 16.2 us
  other arithmetic: 2.7 us -> 3.45 us
    pallas_call x4 -> x0, Pallas kernels: 9.35 us -> none  [the longest x3 6.74 us: carve(): pl.pallas_call(carve_kernel, out_shape=[block] * count, in_specs=[SMEM, H...]
    dynamic_slice x0 -> x3, local copies, waits for them, and re-layouts: none -> 8.81 us  [column_block(): return lax.dynamic_slice_in_dim(w_query, block * share, share, axis=1)]
    ppermute x19 -> x16, waiting for transfers between devices: 18.3 us -> 14.7 us  [swapped(): lax.ppermute(value, axis, [(source, source ^ bits) for source in range(co...]
    pallas_call x2 -> x3, Pallas kernels: 4.97 us -> 7.44 us  [product(): pl.pallas_call(functools.partial(product_kernel, first), out_shape=jax.Sh...]
    ppermute x19 -> x16, starting transfers between devices: 17.3 us -> 16.2 us  [swapped(): lax.ppermute(value, axis, [(source, source ^ bits) for source in range(co...]
    concatenate x1, other arithmetic: 0.02 us -> 0.86 us  [on_device(): second = swapped(jnp.concatenate([second_part, kv], axis=1), 'head', 2)]
  transfers between devices with their start and end apart: 19 -> 16, of which waited for: 11 -> 9; matrix products, arithmetic and copies ran while one was open for 4% -> 21% of each run, Pallas kernels for 23% -> 18%
where the time goes in v11:
time: 56.3 us; the launch traced here: 55.9 us
  starting transfers between devices  16.2 us (29%)
  waiting for transfers between devices  14.7 us (26%)
  Pallas kernels  11.1 us (20%)
  local copies, waits for them, and re-layouts  10.2 us (18%)
  other arithmetic  3.45 us (6%)
    ppermute x16, starting transfers between devices, swapped(): lax.ppermute(value, axis, [(source, source ^ bits) for source in range(co...  16.2 us
    ppermute x16, waiting for transfers between devices, swapped(): lax.ppermute(value, axis, [(source, source ^ bits) for source in range(co...  14.7 us
    dynamic_slice x3, local copies, waits for them, and re-layouts, column_block(): return lax.dynamic_slice_in_dim(w_query, block * share, share, axis=1)  8.81 us
    pallas_call x3, Pallas kernels, product(): pl.pallas_call(functools.partial(product_kernel, first), out_shape=jax.Sh...  7.44 us
    pallas_call x1, Pallas kernels, attention(): pl.pallas_call(attention_kernel, out_shape=[jax.ShapeDtypeStruct((rows, 2...  2.37 us
    pallas_call x1, Pallas kernels, finish(): pl.pallas_call(finish_kernel, out_shape=jax.ShapeDtypeStruct((rows, share...  1.28 us
  transfers between devices with their start and end apart: 16, of which 9 were waited for; matrix products, arithmetic and copies ran while one was open for 21% of the time, Pallas kernels for 18%

profile of v11, /device:TPU:0, one launch (start us, length us, event | category | flops | bytes accessed | tf_op | source)
XLA Modules:
  0.0 55.9 jit_solution(3117209107925072562)
XLA Ops:
  0.0 0.7 %reshape.23 = s32[2,64]{1,0:T(2,128)S(1)} reshape(s32[128]{0:T(128)} %param.14) | data formatting | bytes 1024 | tf_op jit(solution)/shard_map/reshape | solution.py:44
  0.9 0.8 %broadcast_select_fusion = bf16[128,128]{1,0:T(8,128)(2,1)S(1)} fusion(bf16[128,128]{1,0:T(8,128)(2,1)} %param.11, bf16[128,128]{1,0:T(8,128)(2,1)} %param.12, pred[]{:T(512)} %bitcast.10), kind=kLoop, calls=%fused_computation.16 | loop fusion | flops 16384 | bytes 98305 | tf_op jit(solution)/shard_map/jit(_where)/select_n | solution.py:43
  1.7 4.1 %collective-permute-start.6 = (bf16[144,128]{1,0:T(8,128)(2,1)S(1)}, bf16[144,128]{1,0:T(8,128)(2,1)S(1)}, u32[]{:S(2)}, u32[]{:S(2)}) collective-permute-start(bf16[144,128]{1,0:T(8,128)(2,1)S(1)} %get-tuple-element.74), channel_id=1, source_target_pairs={{0,16},{4,20},{8,24},{12,28},{16,0},{20,4},{24,8},{28,12},{1,17},{... | collective-permute-start | bytes 110600 | tf_op jit(solution)/shard_map/ppermute | solution.py:26
  5.8 1.6 %collective-permute-start.5 = (bf16[144,128]{1,0:T(8,128)(2,1)S(1)}, bf16[144,128]{1,0:T(8,128)(2,1)S(1)}, u32[]{:S(2)}, u32[]{:S(2)}) collective-permute-start(bf16[144,128]{1,0:T(8,128)(2,1)S(1)} %get-tuple-element.74), channel_id=1, source_target_pairs={{0,8},{4,12},{8,0},{12,4},{16,24},{20,28},{24,16},{28,20},{1,9},{5... | collective-permute-start | bytes 110600 | tf_op jit(solution)/shard_map/ppermute | solution.py:26
  7.4 0.9 %pad_maximum_fusion.3.mine_ref = bf16[2,128,256]{2,1,0:T(8,128)(2,1)S(1)} fusion(bf16[1,128,256]{2,1,0:T(8,128)(2,1)} %bitcast.36, bf16[1,128,256]{2,1,0:T(8,128)(2,1)} %bitcast.37), kind=kLoop, calls=%fused_computation.14 | loop fusion | flops 65536 | bytes 262144 | tf_op jit(solution)/shard_map/stack | solution.py:231
  8.4 3.2 %constant_dynamic-slice_fusion.4 = bf16[256,4096]{1,0:T(8,128)(2,1)} fusion(bf16[256,16384]{1,0:T(8,128)(2,1)} %param.16, s32[]{:T(128)S(6)} %select_n.26), kind=kLoop, calls=%fused_computation.25 | loop fusion | bytes 4194308 | tf_op jit(solution)/shard_map/dynamic_slice | solution.py:51
  11.6 1.6 %collective-permute-done.7 = bf16[144,128]{1,0:T(8,128)(2,1)S(1)} collective-permute-done((bf16[144,128]{1,0:T(8,128)(2,1)S(1)}, bf16[144,128]{1,0:T(8,128)(2,1)S(1)}, u32[]{:S(2)}, u32[]{:S(2)}) %collective-permute-start.7) | collective-permute-done | bytes 36896 | tf_op jit(solution)/shard_map/ppermute | solution.py:26
  13.3 1.6 %collective-permute-start.10 = (bf16[4,144,128]{2,1,0:T(8,128)(2,1)S(1)}, bf16[4,144,128]{2,1,0:T(8,128)(2,1)S(1)}, u32[]{:S(2)}, u32[]{:S(2)}) collective-permute-start(bf16[4,144,128]{2,1,0:T(8,128)(2,1)S(1)} %pad_maximum_fusion.2.refs_0_), channel_id=1, source_target_pairs={{0,4},{4,0},{8,12},{12,8},{16,20},{20,16},{24,28},{28,24},{1,5},{5... | collective-permute-start | bytes 442376 | tf_op jit(solution)/shard_map/ppermute | solution.py:26
  14.9 3.9 %constant_dynamic-slice_fusion.2 = (bf16[256,4096]{1,0:T(8,128)(2,1)}, bf16[256,4096]{1,0:T(8,128)(2,1)S(1)}) fusion(bf16[256,16384]{1,0:T(8,128)(2,1)} %param.16, s32[]{:T(128)S(6)} %select_n.28, s32[]{:T(128)S(6)} %select_n.27), kind=kLoop, calls=%fused_computation.23 | loop fusion | bytes 8388616 | tf_op jit(solution)/shard_map/dynamic_slice | solution.py:51
  18.8 0.8 %collective-permute-done.10.refs_2_ = bf16[4,144,128]{2,1,0:T(8,128)(2,1)S(1)} collective-permute-done((bf16[4,144,128]{2,1,0:T(8,128)(2,1)S(1)}, bf16[4,144,128]{2,1,0:T(8,128)(2,1)S(1)}, u32[]{:S(2)}, u32[]{:S(2)}) %collective-permute-start.10) | collective-permute-done | bytes 147488 | tf_op jit(solution)/shard_map/ppermute | solution.py:26
  19.6 0.5 collective-permute-start.9
  20.1 0.8 %collective-permute-done.11.refs_3_ = bf16[4,144,128]{2,1,0:T(8,128)(2,1)S(1)} collective-permute-done((bf16[4,144,128]{2,1,0:T(8,128)(2,1)S(1)}, bf16[4,144,128]{2,1,0:T(8,128)(2,1)S(1)}, u32[]{:S(2)}, u32[]{:S(2)}) %collective-permute-start.11) | collective-permute-done | bytes 147488 | tf_op jit(solution)/shard_map/ppermute | solution.py:26
  21.2 2.4 %attention.1 = (bf16[128,512]{1,0:T(8,128)(2,1)S(1)}, bf16[8,128,128]{2,1,0:T(8,128)(2,1)S(1)}) custom-call(s32[1]{0:T(128)} %bitcast.4.core_ref, s32[1,128]{1,0:T(1,128)S(1)} %bitcast.34, s32[1,128]{1,0:T(1,128)S(1)} %bitcast.35, bf16[2,128,256]{2,1,0:T(8,128)(2,1)S(1)} %pad_maximum_fusion.3.mine_ref, ...), custom_call_target="tpu_custom_call" | custom-call | flops 671088640 | bytes 1048576 | tf_op jit(solution)/shard_map/attention/pallas_call | solution.py:133
  23.5 3.1 %product.3 = bf16[128,3328]{1,0:T(8,128)(2,1)} custom-call(bf16[128,512]{1,0:T(8,128)(2,1)S(1)} %get-tuple-element.50.dq_ref, bf16[256,4096]{1,0:T(8,128)(2,1)S(1)} %get-tuple-element.51.wm_ref, bf16[256,4096]{1,0:T(8,128)(2,1)} %collective-permute-done.12.wo_ref), custom_call_target="tpu_custom_call" | custom-call | flops 436207616 | bytes 3407872 | tf_op jit(solution)/shard_map/product/pallas_call | solution.py:162
  26.7 1.5 %collective-permute-start.14 = (bf16[128,3328]{1,0:T(8,128)(2,1)}, bf16[128,3328]{1,0:T(8,128)(2,1)S(1)}, u32[]{:S(2)}, u32[]{:S(2)}) collective-permute-start(bf16[128,3328]{1,0:T(8,128)(2,1)} %product.3), channel_id=1, source_target_pairs={{0,2},{1,3},{2,0},{3,1},{4,6},{5,7},{6,4},{7,5},{8,10},{9,11},{10,... | collective-permute-start | bytes 2555912 | tf_op jit(solution)/shard_map/ppermute | solution.py:26
  28.2 1.9 %product.4 = bf16[128,768]{1,0:T(8,128)(2,1)S(1)} custom-call(bf16[128,512]{1,0:T(8,128)(2,1)S(1)} %get-tuple-element.50.dq_ref, bf16[256,4096]{1,0:T(8,128)(2,1)S(1)} %get-tuple-element.51.wm_ref, bf16[256,4096]{1,0:T(8,128)(2,1)} %collective-permute-done.12.wo_ref), custom_call_target="tpu_custom_call" | custom-call | flops 100663296 | bytes 786432 | tf_op jit(solution)/shard_map/product/pallas_call | solution.py:162
  30.1 0.6 %broadcast_in_dim.16 = bf16[128,256]{1,0:T(8,128)(2,1)} broadcast(bf16[]{:T(256)} %constant.36.clone.1), dimensions={} | broadcast | bytes 65538 | tf_op jit(solution)/shard_map/broadcast_in_dim | solution.py:262
  30.7 14.6 %while.10 = (s32[]{:T(128)}, bf16[128,256]{1,0:T(8,128)(2,1)}, s32[]{:T(128)}, bf16[8,128,128]{2,1,0:T(8,128)(2,1)S(1)}, s32[]{:T(128)}, /*index=5*/s32[]{:T(128)}, s32[]{:T(128)}, s32[]{:T(128)}) while((s32[]{:T(128)}, bf16[128,256]{1,0:T(8,128)(2,1)}, s32[]{:T(128)}, bf16[8,128,128]{2,1,0:T(8,128)(2,1)S(1)}, s32[]{:T(128)}, ...), condition=%wide.region_1.2_spmd, body=%wide.region_0.1_spmd.sunk | while | flops 507911 | bytes 2490715 | solution.py:262
  30.7 1.6 %collective-permute-start = (bf16[4,128,128]{2,1,0:T(8,128)(2,1)S(1)}, bf16[4,128,128]{2,1,0:T(8,128)(2,1)S(1)}, u32[]{:S(2)}, u32[]{:S(2)}) collective-permute-start(bf16[4,128,128]{2,1,0:T(8,128)(2,1)S(1)} %constant_dynamic-slice_fusion.6), channel_id=1, source_target_pairs={{0,4},{4,0},{8,12},{12,8},{16,20},{20,16},{24,28},{28,24},{1,5},{5... | collective-permute-start | bytes 393224 | tf_op jit(solution)/shard_map/while/body/ppermute | solution.py:26
  32.2 3.9 %collective-permute-done = bf16[4,128,128]{2,1,0:T(8,128)(2,1)S(1)} collective-permute-done((bf16[4,128,128]{2,1,0:T(8,128)(2,1)S(1)}, bf16[4,128,128]{2,1,0:T(8,128)(2,1)S(1)}, u32[]{:S(2)}, u32[]{:S(2)}) %collective-permute-start) | collective-permute-done | bytes 131104 | tf_op jit(solution)/shard_map/while/body/ppermute | solution.py:26
  36.2 2.3 %collective-permute-start.1 = (bf16[128,128]{1,0:T(8,128)(2,1)S(1)}, bf16[128,128]{1,0:T(8,128)(2,1)S(1)}, u32[]{:S(2)}, u32[]{:S(2)}) collective-permute-start(bf16[128,128]{1,0:T(8,128)(2,1)S(1)} %get-tuple-element.106), channel_id=1, source_target_pairs={{0,24},{4,28},{8,16},{12,20},{16,8},{20,12},{24,0},{28,4},{1,25},{... | collective-permute-start | bytes 98312 | tf_op jit(solution)/shard_map/while/body/ppermute | solution.py:26
  38.6 2.1 %collective-permute-start.3 = (bf16[128,128]{1,0:T(8,128)(2,1)S(1)}, bf16[128,128]{1,0:T(8,128)(2,1)S(1)}, u32[]{:S(2)}, u32[]{:S(2)}) collective-permute-start(bf16[128,128]{1,0:T(8,128)(2,1)S(1)} %get-tuple-element.108), channel_id=1, source_target_pairs={{0,8},{4,12},{8,0},{12,4},{16,24},{20,28},{24,16},{28,20},{1,9},{5... | collective-permute-start | bytes 98312 | tf_op jit(solution)/shard_map/while/body/ppermute | solution.py:26
  40.7 1.3 %collective-permute-done.1 = bf16[128,128]{1,0:T(8,128)(2,1)S(1)} collective-permute-done((bf16[128,128]{1,0:T(8,128)(2,1)S(1)}, bf16[128,128]{1,0:T(8,128)(2,1)S(1)}, u32[]{:S(2)}, u32[]{:S(2)}) %collective-permute-start.1) | collective-permute-done | bytes 32800 | tf_op jit(solution)/shard_map/while/body/ppermute | solution.py:26
  42.0 1.4 %collective-permute-done.2 = bf16[128,128]{1,0:T(8,128)(2,1)S(1)} collective-permute-done((bf16[128,128]{1,0:T(8,128)(2,1)S(1)}, bf16[128,128]{1,0:T(8,128)(2,1)S(1)}, u32[]{:S(2)}, u32[]{:S(2)}) %collective-permute-start.2) | collective-permute-done | bytes 32800 | tf_op jit(solution)/shard_map/while/body/ppermute | solution.py:26
  43.5 1.2 %collective-permute-done.4 = bf16[128,128]{1,0:T(8,128)(2,1)S(1)} collective-permute-done((bf16[128,128]{1,0:T(8,128)(2,1)S(1)}, bf16[128,128]{1,0:T(8,128)(2,1)S(1)}, u32[]{:S(2)}, u32[]{:S(2)}) %collective-permute-start.4) | collective-permute-done | bytes 32800 | tf_op jit(solution)/shard_map/while/body/ppermute | solution.py:26
  44.7 0.6 %pad_maximum_fusion.6 = bf16[128,256]{1,0:T(8,128)(2,1)} fusion(bf16[128,128]{1,0:T(8,128)(2,1)S(1)} %collective-permute-done.4, bf16[128,128]{1,0:T(8,128)(2,1)S(1)} %fusion.11), kind=kLoop, calls=%fused_computation.6.clone.1 | loop fusion | flops 131072 | bytes 131072 | tf_op jit(solution)/shard_map/while/body/concatenate | solution.py:258
  45.3 0.9 %pad_maximum_fusion.1 = bf16[128,1024]{1,0:T(8,128)(2,1)S(1)} fusion(bf16[128,256]{1,0:T(8,128)(2,1)} %get-tuple-element.54.kv_ref, bf16[128,768]{1,0:T(8,128)(2,1)S(1)} %product.4), kind=kLoop, calls=%fused_computation.12 | loop fusion | flops 524288 | bytes 524288 | tf_op jit(solution)/shard_map/concatenate | solution.py:264
  46.2 0.6 %collective-permute-start.15 = (bf16[128,1024]{1,0:T(8,128)(2,1)S(1)}, bf16[128,1024]{1,0:T(8,128)(2,1)S(1)}, u32[]{:S(2)}, u32[]{:S(2)}) collective-permute-start(bf16[128,1024]{1,0:T(8,128)(2,1)S(1)} %pad_maximum_fusion.1), channel_id=1, source_target_pairs={{0,2},{1,3},{2,0},{3,1},{4,6},{5,7},{6,4},{7,5},{8,10},{9,11},{10,... | collective-permute-start | bytes 786440 | tf_op jit(solution)/shard_map/ppermute | solution.py:26
  46.8 1.7 %constant_dynamic-slice_fusion.1.wm_ref = bf16[256,4096]{1,0:T(8,128)(2,1)S(1)} fusion(bf16[256,16384]{1,0:T(8,128)(2,1)} %param.16, s32[]{:T(128)S(6)} %select_n.29), kind=kLoop, calls=%fused_computation.22 | loop fusion | bytes 4194308 | tf_op jit(solution)/shard_map/dynamic_slice | solution.py:51
  48.5 2.5 %product.5.acc_ref = f32[128,4096]{1,0:T(8,128)S(1)} custom-call(bf16[128,512]{1,0:T(8,128)(2,1)S(1)} %get-tuple-element.50.dq_ref, bf16[256,4096]{1,0:T(8,128)(2,1)S(1)} %constant_dynamic-slice_fusion.1.wm_ref, bf16[256,4096]{1,0:T(8,128)(2,1)} %collective-permute-done.13.wo_ref), custom_call_target="tpu_custom_call" | custom-call | flops 536870912 | bytes 4194304 | tf_op jit(solution)/shard_map/product/pallas_call | solution.py:162
  51.0 3.6 %collective-permute-done.15.second_ref = bf16[128,1024]{1,0:T(8,128)(2,1)S(1)} collective-permute-done((bf16[128,1024]{1,0:T(8,128)(2,1)S(1)}, bf16[128,1024]{1,0:T(8,128)(2,1)S(1)}, u32[]{:S(2)}, u32[]{:S(2)}) %collective-permute-start.15) | collective-permute-done | bytes 262176 | tf_op jit(solution)/shard_map/ppermute | solution.py:26
  54.6 1.3 %finish.1 = bf16[128,4096]{1,0:T(8,128)(2,1)} custom-call(s32[1]{0:T(128)} %bitcast.4.core_ref, bf16[128,256]{1,0:T(8,128)(2,1)S(1)} %copy-done.3, bf16[256,4096]{1,0:T(8,128)(2,1)S(1)} %copy-done, f32[128,4096]{1,0:T(8,128)S(1)} %product.5.acc_ref, bf16[128,3328]{1,0:T(8,128)(2,1)S(1)} %collective-permute-done.14.first_ref, ...), custom_call_target="tpu_custom_call" | custom-call | flops 268435456 | bytes 5242880 | tf_op jit(solution)/shard_map/finish/pallas_call | solution.py:208
  (31 shorter events, 0.8 us)
Async XLA Ops:
  1.7 9.8 %collective-permute-start.6 = (bf16[144,128]{1,0:T(8,128)(2,1)S(1)}, bf16[144,128]{1,0:T(8,128)(2,1)S(1)}, u32[]{:S(2)}, u32[]{:S(2)}) collective-permute-start(bf16[144,128]{1,0:T(8,128)(2,1)S(1)} %get-tuple-element.74), channel_id=1, source_target_pairs={{0,16},{4,20},{8,24},{12,28},{16,0},{20,4},{24,8},{28,12},{1,17},{... | collective-permute-start | bytes 110600 | tf_op jit(solution)/shard_map/ppermute | solution.py:26
  5.8 5.7 %collective-permute-start.5 = (bf16[144,128]{1,0:T(8,128)(2,1)S(1)}, bf16[144,128]{1,0:T(8,128)(2,1)S(1)}, u32[]{:S(2)}, u32[]{:S(2)}) collective-permute-start(bf16[144,128]{1,0:T(8,128)(2,1)S(1)} %get-tuple-element.74), channel_id=1, source_target_pairs={{0,8},{4,12},{8,0},{12,4},{16,24},{20,28},{24,16},{28,20},{1,9},{5... | collective-permute-start | bytes 110600 | tf_op jit(solution)/shard_map/ppermute | solution.py:26
  7.4 5.8 %collective-permute-start.7 = (bf16[144,128]{1,0:T(8,128)(2,1)S(1)}, bf16[144,128]{1,0:T(8,128)(2,1)S(1)}, u32[]{:S(2)}, u32[]{:S(2)}) collective-permute-start(bf16[144,128]{1,0:T(8,128)(2,1)S(1)} %get-tuple-element.74), channel_id=1, source_target_pairs={{0,24},{4,28},{8,16},{12,20},{16,8},{20,12},{24,0},{28,4},{1,25},{... | collective-permute-start | bytes 110600 | tf_op jit(solution)/shard_map/ppermute | solution.py:26
  8.3 4.9 %collective-permute-start.8 = (bf16[2,128,256]{2,1,0:T(8,128)(2,1)S(1)}, bf16[2,128,256]{2,1,0:T(8,128)(2,1)S(1)}, u32[]{:S(2)}, u32[]{:S(2)}) collective-permute-start(bf16[2,128,256]{2,1,0:T(8,128)(2,1)S(1)} %pad_maximum_fusion.3.mine_ref), channel_id=1, source_target_pairs={{0,1},{1,0},{2,3},{3,2},{4,5},{5,4},{6,7},{7,6},{8,9},{9,8},{10,11... | collective-permute-start | bytes 393224 | tf_op jit(solution)/shard_map/ppermute | solution.py:26
  13.2 10.3 %collective-permute-start.12 = (bf16[256,4096]{1,0:T(8,128)(2,1)}, bf16[256,4096]{1,0:T(8,128)(2,1)}, u32[]{:S(2)}, u32[]{:S(2)}) collective-permute-start(bf16[256,4096]{1,0:T(8,128)(2,1)} %constant_dynamic-slice_fusion.4), channel_id=1, source_target_pairs={{0,1},{1,0},{2,3},{3,2},{4,5},{5,4},{6,7},{7,6},{8,9},{9,8},{10,11... | collective-permute-start | bytes 6291464 | tf_op jit(solution)/shard_map/ppermute | solution.py:26
  13.3 6.8 %copy-start.1 = (s32[128]{0:T(128)S(1)}, s32[128]{0:T(128)}, u32[]{:S(2)}) copy-start(s32[128]{0:T(128)} %param.14) | copy-start | bytes 1540
  13.3 7.8 %copy-start.2 = (s32[128]{0:T(128)S(1)}, s32[128]{0:T(128)}, u32[]{:S(2)}) copy-start(s32[128]{0:T(128)} %param.15) | copy-start | bytes 1540
  13.3 6.2 %collective-permute-start.10 = (bf16[4,144,128]{2,1,0:T(8,128)(2,1)S(1)}, bf16[4,144,128]{2,1,0:T(8,128)(2,1)S(1)}, u32[]{:S(2)}, u32[]{:S(2)}) collective-permute-start(bf16[4,144,128]{2,1,0:T(8,128)(2,1)S(1)} %pad_maximum_fusion.2.refs_0_), channel_id=1, source_target_pairs={{0,4},{4,0},{8,12},{12,8},{16,20},{20,16},{24,28},{28,24},{1,5},{5... | collective-permute-start | bytes 442376 | tf_op jit(solution)/shard_map/ppermute | solution.py:26
  19.6 1.4 %collective-permute-start.11 = (bf16[4,144,128]{2,1,0:T(8,128)(2,1)S(1)}, bf16[4,144,128]{2,1,0:T(8,128)(2,1)S(1)}, u32[]{:S(2)}, u32[]{:S(2)}) collective-permute-start(bf16[4,144,128]{2,1,0:T(8,128)(2,1)S(1)} %collective-permute-done.10.refs_2_), channel_id=1, source_target_pairs={{0,1},{1,0},{2,3},{3,2},{4,5},{5,4},{6,7},{7,6},{8,9},{9,8},{10,11... | collective-permute-start | bytes 442376 | tf_op jit(solution)/shard_map/ppermute | solution.py:26
  19.6 1.6 %collective-permute-start.9 = (bf16[4,144,128]{2,1,0:T(8,128)(2,1)S(1)}, bf16[4,144,128]{2,1,0:T(8,128)(2,1)S(1)}, u32[]{:S(2)}, u32[]{:S(2)}) collective-permute-start(bf16[4,144,128]{2,1,0:T(8,128)(2,1)S(1)} %pad_maximum_fusion.2.refs_0_), channel_id=1, source_target_pairs={{0,1},{1,0},{2,3},{3,2},{4,5},{5,4},{6,7},{7,6},{8,9},{9,8},{10,11... | collective-permute-start | bytes 442376 | tf_op jit(solution)/shard_map/ppermute | solution.py:26
  20.9 27.6 %collective-permute-start.13 = (bf16[256,4096]{1,0:T(8,128)(2,1)}, bf16[256,4096]{1,0:T(8,128)(2,1)}, u32[]{:S(2)}, u32[]{:S(2)}) collective-permute-start(bf16[256,4096]{1,0:T(8,128)(2,1)} %get-tuple-element.56), channel_id=1, source_target_pairs={{0,1},{1,0},{2,3},{3,2},{4,5},{5,4},{6,7},{7,6},{8,9},{9,8},{10,11... | collective-permute-start | bytes 6291464 | tf_op jit(solution)/shard_map/ppermute | solution.py:26
  26.7 28.0 %collective-permute-start.14 = (bf16[128,3328]{1,0:T(8,128)(2,1)}, bf16[128,3328]{1,0:T(8,128)(2,1)S(1)}, u32[]{:S(2)}, u32[]{:S(2)}) collective-permute-start(bf16[128,3328]{1,0:T(8,128)(2,1)} %product.3), channel_id=1, source_target_pairs={{0,2},{1,3},{2,0},{3,1},{4,6},{5,7},{6,4},{7,5},{8,10},{9,11},{10,... | collective-permute-start | bytes 2555912 | tf_op jit(solution)/shard_map/ppermute | solution.py:26
  30.7 5.5 %collective-permute-start = (bf16[4,128,128]{2,1,0:T(8,128)(2,1)S(1)}, bf16[4,128,128]{2,1,0:T(8,128)(2,1)S(1)}, u32[]{:S(2)}, u32[]{:S(2)}) collective-permute-start(bf16[4,128,128]{2,1,0:T(8,128)(2,1)S(1)} %constant_dynamic-slice_fusion.6), channel_id=1, source_target_pairs={{0,4},{4,0},{8,12},{12,8},{16,20},{20,16},{24,28},{28,24},{1,5},{5... | collective-permute-start | bytes 393224 | tf_op jit(solution)/shard_map/while/body/ppermute | solution.py:26
  36.2 5.8 %collective-permute-start.1 = (bf16[128,128]{1,0:T(8,128)(2,1)S(1)}, bf16[128,128]{1,0:T(8,128)(2,1)S(1)}, u32[]{:S(2)}, u32[]{:S(2)}) collective-permute-start(bf16[128,128]{1,0:T(8,128)(2,1)S(1)} %get-tuple-element.106), channel_id=1, source_target_pairs={{0,24},{4,28},{8,16},{12,20},{16,8},{20,12},{24,0},{28,4},{1,25},{... | collective-permute-start | bytes 98312 | tf_op jit(solution)/shard_map/while/body/ppermute | solution.py:26
  38.6 4.8 %collective-permute-start.2 = (bf16[128,128]{1,0:T(8,128)(2,1)S(1)}, bf16[128,128]{1,0:T(8,128)(2,1)S(1)}, u32[]{:S(2)}, u32[]{:S(2)}) collective-permute-start(bf16[128,128]{1,0:T(8,128)(2,1)S(1)} %get-tuple-element.107), channel_id=1, source_target_pairs={{0,16},{4,20},{8,24},{12,28},{16,0},{20,4},{24,8},{28,12},{1,17},{... | collective-permute-start | bytes 98312 | tf_op jit(solution)/shard_map/while/body/ppermute | solution.py:26
  38.6 4.8 %collective-permute-start.3 = (bf16[128,128]{1,0:T(8,128)(2,1)S(1)}, bf16[128,128]{1,0:T(8,128)(2,1)S(1)}, u32[]{:S(2)}, u32[]{:S(2)}) collective-permute-start(bf16[128,128]{1,0:T(8,128)(2,1)S(1)} %get-tuple-element.108), channel_id=1, source_target_pairs={{0,8},{4,12},{8,0},{12,4},{16,24},{20,28},{24,16},{28,20},{1,9},{5... | collective-permute-start | bytes 98312 | tf_op jit(solution)/shard_map/while/body/ppermute | solution.py:26
  43.4 1.3 %collective-permute-start.4 = (bf16[128,128]{1,0:T(8,128)(2,1)S(1)}, bf16[128,128]{1,0:T(8,128)(2,1)S(1)}, u32[]{:S(2)}, u32[]{:S(2)}) collective-permute-start(bf16[128,128]{1,0:T(8,128)(2,1)S(1)} %fusion.11), channel_id=1, source_target_pairs={{0,1},{1,0},{2,3},{3,2},{4,5},{5,4},{6,7},{7,6},{8,9},{9,8},{10,11... | collective-permute-start | bytes 98312 | tf_op jit(solution)/shard_map/while/body/ppermute | solution.py:26
  46.2 8.4 %collective-permute-start.15 = (bf16[128,1024]{1,0:T(8,128)(2,1)S(1)}, bf16[128,1024]{1,0:T(8,128)(2,1)S(1)}, u32[]{:S(2)}, u32[]{:S(2)}) collective-permute-start(bf16[128,1024]{1,0:T(8,128)(2,1)S(1)} %pad_maximum_fusion.1), channel_id=1, source_target_pairs={{0,2},{1,3},{2,0},{3,1},{4,6},{5,7},{6,4},{7,5},{8,10},{9,11},{10,... | collective-permute-start | bytes 786440 | tf_op jit(solution)/shard_map/ppermute | solution.py:26
  48.5 6.1 %copy-start = (bf16[256,4096]{1,0:T(8,128)(2,1)S(1)}, bf16[256,4096]{1,0:T(8,128)(2,1)}, u32[]{:S(2)}) copy-start(bf16[256,4096]{1,0:T(8,128)(2,1)} %w_ref.1) | copy-start | bytes 6291460
  48.5 6.1 %copy-start.3 = (bf16[128,256]{1,0:T(8,128)(2,1)S(1)}, bf16[128,256]{1,0:T(8,128)(2,1)}, u32[]{:S(2)}) copy-start(bf16[128,256]{1,0:T(8,128)(2,1)} %get-tuple-element.54.kv_ref) | copy-start | bytes 196612

commit v12 on v11

--- a/solution.py
+++ b/solution.py
@@ -10,8 +10,8 @@
 
 RUN = 64
 META_ROWS = 16
-CHUNKS = (13, 3)
 TILES = 4
+GIVES = 2
 ANY = pl.BlockSpec(memory_space=pl.ANY)
 HBM = pl.BlockSpec(memory_space=pltpu.HBM)
 SMEM = pl.BlockSpec(memory_space=pltpu.SMEM)
@@ -51,23 +51,21 @@
     return lax.dynamic_slice_in_dim(w_query, block * share, share, axis=1)
 
 
-def attention_kernel(core_ref, pos_ref, doc_ref, mine_ref, swap_ref, *refs):
+def attention_kernel(core_ref, pos_ref, doc_ref, qm_ref, qo_ref, gm_ref, go_ref, *refs):
     groups = (refs[0:2], refs[2:4])
     dq_ref, back_ref, s_ref, dp_ref = refs[4:]
     count, rows, size = back_ref.shape
     half = count // 2
-    heads = mine_ref.shape[2] // size
+    heads = qm_ref.shape[1] // size
     is_key = core_ref[0] == 0
     inv_root = 1.0 / math.sqrt(size)
 
-    def stack(which):
-        parts = [
-            ref[which, :, h * size : (h + 1) * size] for ref in (mine_ref, swap_ref) for h in range(heads)
-        ]
+    def stack(mine_ref, other_ref):
+        parts = [ref[:, h * size : (h + 1) * size] for ref in (mine_ref, other_ref) for h in range(heads)]
         return jnp.concatenate(parts, axis=0)
 
-    query = stack(0)
-    grad = stack(1)
+    query = stack(qm_ref, qo_ref)
+    grad = stack(gm_ref, go_ref)
     wide = query.shape[0]
     last = jnp.concatenate([pos_ref[...].astype(jnp.float32)] * (2 * heads), axis=1)
     first = jnp.concatenate([(doc_ref[...] * RUN).astype(jnp.float32)] * (2 * heads), axis=1)
@@ -125,9 +123,9 @@
         dq_ref[:, part * size : (part + 1) * size] = block.T.astype(jnp.bfloat16)
 
 
-def attention(core, positions, doc_ids, mine, swap, pieces):
+def attention(core, positions, doc_ids, q_mine, q_other, g_mine, g_other, pieces):
     half, _, size = pieces[0].shape
-    _, rows, width = mine.shape
+    rows, width = q_mine.shape
     count = 2 * half
     wide = 2 * rows * (width // size)
     return pl.pallas_call(
@@ -136,7 +134,7 @@
             jax.ShapeDtypeStruct((rows, 2 * width), jnp.bfloat16),
             jax.ShapeDtypeStruct((count, rows, size), jnp.bfloat16),
         ],
-        in_specs=[SMEM] + [pl.BlockSpec()] * 8,
+        in_specs=[SMEM] + [pl.BlockSpec()] * 10,
         out_specs=[pl.BlockSpec()] * 2,
         scratch_shapes=[pltpu.VMEM((count, rows, wide), jnp.float32)] * 2,
         compiler_params=params(8 + count * rows * wide // 2**17),
@@ -146,7 +144,9 @@
             transcendentals=count * rows * wide,
         ),
         name="attention",
-    )(core, positions.reshape(1, rows), doc_ids.reshape(1, rows), mine, swap, *pieces)
+    )(
+        core, positions.reshape(1, rows), doc_ids.reshape(1, rows), q_mine, q_other, g_mine, g_other, *pieces
+    )
 
 
 def product_kernel(first, dq_ref, wm_ref, wo_ref, out_ref):
@@ -172,43 +172,64 @@
     )(dq, w_mine, w_other)
 
 
-def finish_kernel(core_ref, kv_ref, w_ref, acc_ref, first_ref, second_ref, out_ref, hold_ref, sems):
+def own_kernel(dq_ref, wn_ref, wo_ref, acc_ref, *give_refs):
+    depth, share = wn_ref.shape
+    dq = dq_ref[:, 0:depth]
+    width = share // len(give_refs)
+    for i, give_ref in enumerate(give_refs):
+        give_ref[...] = dot(dq, wo_ref[:, i * width : (i + 1) * width], ((1,), (0,))).astype(jnp.bfloat16)
+    acc_ref[...] = dot(dq, wn_ref[...], ((1,), (0,)))
+
+
+def own(dq, w_near, w_other):
+    rows = dq.shape[0]
+    share = w_near.shape[1]
+    return pl.pallas_call(
+        own_kernel,
+        out_shape=[jax.ShapeDtypeStruct((rows, share), jnp.float32)]
+        + [jax.ShapeDtypeStruct((rows, share // GIVES), jnp.bfloat16)] * GIVES,
+        in_specs=[pl.BlockSpec()] * 3,
+        out_specs=[pl.BlockSpec()] * (1 + GIVES),
+        compiler_params=params(),
+        name="own",
+    )(dq, w_near, w_other)
+
+
+def finish_kernel(core_ref, kv_ref, kv_far_ref, w_ref, acc_ref, far_ref, *refs):
+    out_ref, hold_ref, sems = refs[GIVES:]
     rows, share = acc_ref.shape
     pair = kv_ref.shape[1]
     size = pair // 2
-    cut = first_ref.shape[1]
     tile = share // TILES
     inv_root = 1.0 / math.sqrt(size)
     column = lax.broadcasted_iota(jnp.int32, (1, pair), 1)
     is_key = (column < size) == (core_ref[0] == 0)
-    kv = kv_ref[...].astype(jnp.float32) + second_ref[:, share - cut :].astype(jnp.float32)
+    kv = kv_ref[...].astype(jnp.float32) + kv_far_ref[...].astype(jnp.float32)
     kv = (kv * jnp.where(is_key, inv_root, 1.0)).astype(jnp.bfloat16)
     at_mine = pl.ds(pl.multiple_of(core_ref[0] * size, size), size)
     at_other = pl.ds(pl.multiple_of((1 - core_ref[0]) * size, size), size)
     copies = []
     for i in range(TILES):
-        low, high = i * tile, (i + 1) * tile
-        w = jnp.concatenate([w_ref[at_mine, low:high], w_ref[at_other, low:high]], axis=0)
-        acc = acc_ref[:, low:high] + dot(kv, w, ((1,), (0,)))
-        come = []
-        if low < cut:
-            come.append(first_ref[:, low : min(high, cut)])
-        if high > cut:
-            come.append(second_ref[:, max(low, cut) - cut : high - cut])
-        acc = acc + jnp.concatenate(come, axis=1).astype(jnp.float32)
-        hold_ref[:, low:high] = acc.astype(jnp.bfloat16)
-        copies.append(pltpu.make_async_copy(hold_ref.at[:, low:high], out_ref.at[:, low:high], sems.at[i]))
+        at = slice(i * tile, (i + 1) * tile)
+        w = jnp.concatenate([w_ref[at_mine, at], w_ref[at_other, at]], axis=0)
+        given_ref = refs[i * GIVES // TILES]
+        skip = i * GIVES // TILES * (share // GIVES)
+        given = given_ref[:, i * tile - skip : (i + 1) * tile - skip]
+        acc = acc_ref[:, at] + far_ref[:, at].astype(jnp.float32) + given.astype(jnp.float32)
+        acc = acc + dot(kv, w, ((1,), (0,)))
+        hold_ref[:, at] = acc.astype(jnp.bfloat16)
+        copies.append(pltpu.make_async_copy(hold_ref.at[:, at], out_ref.at[:, at], sems.at[i]))
         copies[i].start()
     for one in copies:
         one.wait()
 
 
-def finish(core, kv, w_kv, acc, first, second):
+def finish(core, kv, kv_far, w_kv, acc, far, given):
     rows, share = acc.shape
     return pl.pallas_call(
         finish_kernel,
         out_shape=jax.ShapeDtypeStruct((rows, share), jnp.bfloat16),
-        in_specs=[SMEM] + [pl.BlockSpec()] * 5,
+        in_specs=[SMEM] + [pl.BlockSpec()] * (5 + GIVES),
         out_specs=ANY,
         scratch_shapes=[pltpu.VMEM((rows, share), jnp.bfloat16), pltpu.SemaphoreType.DMA((TILES,))],
         compiler_params=params(),
@@ -216,7 +237,7 @@
             flops=2 * rows * kv.shape[1] * share, bytes_accessed=10 * rows * share, transcendentals=0
         ),
         name="finish",
-    )(core, kv, w_kv, acc, first, second)
+    )(core, kv, kv_far, w_kv, acc, far, *given)
 
 
 def on_device(queries, keys, values, dout, positions, doc_ids, w_query, w_kv):
@@ -226,45 +247,44 @@
     share = w_kv.shape[1]
     local_heads = queries.shape[1] // keys.shape[1]
 
+    q_other = swapped(queries, "head", 1)
+    g_other = swapped(dout, "head", 1)
     piece = pack(core, positions, keys, values)
     along_z = [piece] + [swapped(piece, "ctx", 2 * s) for s in range(1, half)]
-    both = jnp.stack([queries, dout])
-    swap = swapped(both, "head", 1)
-    far_send = column_block(w_query, head ^ 3, share, both)
-    here_z, swap, far_send = lax.optimization_barrier((jnp.stack(along_z), swap, far_send))
+    far_send = column_block(w_query, head ^ 3, share, piece)
+    far_mine = column_block(w_query, head ^ 2, share, piece)
+    here_z, q_other, g_other, far_send, far_mine = lax.optimization_barrier(
+        (jnp.stack(along_z), q_other, g_other, far_send, far_mine)
+    )
     here_x = swapped(here_z, "ctx", 1)
     far_other = swapped(far_send, "head", 1)
     there_z = swapped(here_z, "head", 1)
-    far_mine = column_block(w_query, head ^ 2, share, here_z)
-    near_send = column_block(w_query, head ^ 1, share, here_z)
-    here_x, far_mine, near_send = lax.optimization_barrier((here_x, far_mine, near_send))
     there_x = swapped(here_x, "head", 1)
-    there_x, near_send = lax.optimization_barrier((there_x, near_send))
-    near_other = swapped(near_send, "head", 1)
-    dq, back = attention(core, positions, doc_ids, both, swap, (here_z, there_z, here_x, there_x))
-
-    cut = CHUNKS[0] * (share // sum(CHUNKS))
-    first_part = product(dq, far_mine, far_other, 0, cut, jnp.bfloat16)
-    second_part = product(dq, far_mine, far_other, cut, share - cut, jnp.bfloat16)
-    first = swapped(first_part, "head", 2)
-
-    def exchange(trip, kv):
-        sent = lax.dynamic_slice_in_dim(back, (1 - trip) * half, half, axis=0)
+    dq, back = attention(
+        core, positions, doc_ids, queries, q_other, dout, g_other, (here_z, there_z, here_x, there_x)
+    )
+
+    part = product(dq, far_mine, far_other, 0, share, jnp.bfloat16)
+    far = swapped(part, "head", 2)
+
+    def exchange(state):
+        left, _ = state
+        sent = lax.dynamic_slice_in_dim(back, left * half, half, axis=0)
         pair = back[:half].astype(jnp.float32) + swapped(sent, "ctx", 1).astype(jnp.float32)
         mine = pair[0]
         for s in range(1, half):
             mine = mine + swapped(pair[s].astype(jnp.bfloat16), "ctx", 2 * s).astype(jnp.float32)
         mine = mine.astype(jnp.bfloat16)
-        return jnp.concatenate([mine, swapped(mine, "head", 1)], axis=1)
-
-    back, first_part, second_part = lax.optimization_barrier((back, first_part, second_part))
+        return left - 1, jnp.concatenate([mine, swapped(mine, "head", 1)], axis=1)
+
+    back, part, positions = lax.optimization_barrier((back, part, positions))
     trips = 1 + jnp.minimum(positions[0], 0)
-    kv = lax.fori_loop(0, trips, exchange, jnp.zeros((queries.shape[0], 2 * keys.shape[1]), jnp.bfloat16))
-
-    second = swapped(jnp.concatenate([second_part, kv], axis=1), "head", 2)
-    near_mine = column_block(w_query, head, share, kv)
-    acc = product(dq, near_mine, near_other, 0, share, jnp.float32)
-    return finish(core, kv, w_kv, acc, first, second)
+    _, kv = lax.while_loop(lambda state: state[0] > 0, exchange, (trips, q_other))
+    kv_far = swapped(kv, "head", 2)
+
+    acc, *give = own(dq, column_block(w_query, head, share, kv), column_block(w_query, head ^ 1, share, kv))
+    given = [swapped(one, "head", 1) for one in give]
+    return finish(core, kv, kv_far, w_kv, acc, far, given)
 
 
 def solution(mesh):

time: 56.3 us -> 53.6 us (0.952)
  waiting for transfers between devices: 14.7 us -> 20.3 us
  Pallas kernels: 11.1 us -> 6.86 us
  local copies, waits for them, and re-layouts: 10.2 us -> 7.53 us
  other arithmetic: 3.45 us -> 1.71 us
    ppermute x16 -> x18, waiting for transfers between devices: 14.7 us -> 20.3 us  [swapped(): lax.ppermute(value, axis, [(source, source ^ bits) for source in range(co...]
    pallas_call x3 -> x1, Pallas kernels: 7.44 us -> 2.31 us  [product(): pl.pallas_call(functools.partial(product_kernel, first), out_shape=jax.Sh...]
    dynamic_slice x3 -> x2, local copies, waits for them, and re-layouts: 8.81 us -> 6.73 us  [column_block(): return lax.dynamic_slice_in_dim(w_query, block * share, share, axis=1)]
    another operation x2 -> x1, other arithmetic: 0.92 us -> 0.04 us  [the longest x1 0.88 us: on_device(): both = jnp.stack([queries, dout])]
    concatenate x2 -> x1, other arithmetic: 1.49 us -> 0.64 us  [exchange(): return (left - 1, jnp.concatenate([mine, swapped(mine, 'head', 1)], axis=1))]
    pallas_call x0 -> x1, Pallas kernels: none -> 0.75 us  [own(): pl.pallas_call(own_kernel, out_shape=[jax.ShapeDtypeStruct((rows, share),...]
    broadcast_in_dim x1 -> x0, local copies, waits for them, and re-layouts: 0.63 us -> none  [on_device(): jnp.zeros((queries.shape[0], 2 * keys.shape[1]), jnp.bfloat16)]
    ppermute x16 -> x18, starting transfers between devices: 16.2 us -> 16.7 us  [swapped(): lax.ppermute(value, axis, [(source, source ^ bits) for source in range(co...]
  transfers between devices with their start and end apart: 16 -> 18, of which waited for: 9 -> 8; matrix products, arithmetic and copies ran while one was open for 21% -> 14% of each run, Pallas kernels for 18% -> 6%
where the time goes in v12:
time: 53.6 us; the launch traced here: 53.3 us
  waiting for transfers between devices  20.3 us (38%)
  starting transfers between devices  16.7 us (31%)
  local copies, waits for them, and re-layouts  7.53 us (14%)
  Pallas kernels  6.86 us (13%)
  other arithmetic  1.71 us (3%)
    ppermute x18, waiting for transfers between devices, swapped(): lax.ppermute(value, axis, [(source, source ^ bits) for source in range(co...  20.3 us
    ppermute x18, starting transfers between devices, swapped(): lax.ppermute(value, axis, [(source, source ^ bits) for source in range(co...  16.7 us
    dynamic_slice x2, local copies, waits for them, and re-layouts, column_block(): return lax.dynamic_slice_in_dim(w_query, block * share, share, axis=1)  6.73 us
    pallas_call x1, Pallas kernels, attention(): pl.pallas_call(attention_kernel, out_shape=[jax.ShapeDtypeStruct((rows, 2...  2.38 us
    pallas_call x1, Pallas kernels, product(): pl.pallas_call(functools.partial(product_kernel, first), out_shape=jax.Sh...  2.31 us
    pallas_call x1, Pallas kernels, finish(): pl.pallas_call(finish_kernel, out_shape=jax.ShapeDtypeStruct((rows, share...  1.41 us
  transfers between devices with their start and end apart: 18, of which 8 were waited for; matrix products, arithmetic and copies ran while one was open for 14% of the time, Pallas kernels for 6%

profile of v12, /device:TPU:0, one launch (start us, length us, event | category | flops | bytes accessed | tf_op | source)
XLA Modules:
  0.0 53.3 jit_solution(1627114552949492981)
XLA Ops:
  0.0 0.7 %reshape.23 = s32[2,64]{1,0:T(2,128)S(1)} reshape(s32[128]{0:T(128)} %param.14) | data formatting | bytes 1024 | tf_op jit(solution)/shard_map/reshape | solution.py:44
  0.9 0.8 %broadcast_select_fusion = bf16[128,128]{1,0:T(8,128)(2,1)S(1)} fusion(bf16[128,128]{1,0:T(8,128)(2,1)} %param.11, bf16[128,128]{1,0:T(8,128)(2,1)} %param.12, pred[]{:T(512)} %bitcast.7), kind=kLoop, calls=%fused_computation.14 | loop fusion | flops 16384 | bytes 98305 | tf_op jit(solution)/shard_map/jit(_where)/select_n | solution.py:43
  1.7 4.1 %collective-permute-start.6 = (bf16[144,128]{1,0:T(8,128)(2,1)S(1)}, bf16[144,128]{1,0:T(8,128)(2,1)S(1)}, u32[]{:S(2)}, u32[]{:S(2)}) collective-permute-start(bf16[144,128]{1,0:T(8,128)(2,1)S(1)} %get-tuple-element.87), channel_id=1, source_target_pairs={{0,16},{4,20},{8,24},{12,28},{16,0},{20,4},{24,8},{28,12},{1,17},{... | collective-permute-start | bytes 110600 | tf_op jit(solution)/shard_map/ppermute | solution.py:26
  5.8 1.3 %collective-permute-start.7 = (bf16[144,128]{1,0:T(8,128)(2,1)S(1)}, bf16[144,128]{1,0:T(8,128)(2,1)S(1)}, u32[]{:S(2)}, u32[]{:S(2)}) collective-permute-start(bf16[144,128]{1,0:T(8,128)(2,1)S(1)} %get-tuple-element.87), channel_id=1, source_target_pairs={{0,24},{4,28},{8,16},{12,20},{16,8},{20,12},{24,0},{28,4},{1,25},{... | collective-permute-start | bytes 110600 | tf_op jit(solution)/shard_map/ppermute | solution.py:26
  7.2 0.2 collective-permute-start.5
  7.4 4.0 %constant_dynamic-slice_fusion.3 = (bf16[256,4096]{1,0:T(8,128)(2,1)S(1)}, bf16[256,4096]{1,0:T(8,128)(2,1)}) fusion(bf16[256,16384]{1,0:T(8,128)(2,1)} %param.16, s32[]{:T(128)S(6)} %select_n.30, s32[]{:T(128)S(6)} %select_n.29), kind=kLoop, calls=%fused_computation.22 | loop fusion | bytes 8388616 | tf_op jit(solution)/shard_map/dynamic_slice | solution.py:51
  11.5 0.5 collective-permute-start.9
  12.0 0.8 %collective-permute-done.9.go_ref = bf16[128,256]{1,0:T(8,128)(2,1)S(1)} collective-permute-done((bf16[128,256]{1,0:T(8,128)(2,1)S(1)}, bf16[128,256]{1,0:T(8,128)(2,1)S(1)}, u32[]{:S(2)}, u32[]{:S(2)}) %collective-permute-start.9) | collective-permute-done | bytes 65568 | tf_op jit(solution)/shard_map/ppermute | solution.py:26
  12.8 0.4 collective-permute-start.13
  13.2 1.5 %collective-permute-start.11 = (bf16[4,144,128]{2,1,0:T(8,128)(2,1)S(1)}, bf16[4,144,128]{2,1,0:T(8,128)(2,1)S(1)}, u32[]{:S(2)}, u32[]{:S(2)}) collective-permute-start(bf16[4,144,128]{2,1,0:T(8,128)(2,1)S(1)} %pad_maximum_fusion.1.refs_0_), channel_id=1, source_target_pairs={{0,4},{4,0},{8,12},{12,8},{16,20},{20,16},{24,28},{28,24},{1,5},{5... | collective-permute-start | bytes 442376 | tf_op jit(solution)/shard_map/ppermute | solution.py:26
  14.7 4.4 %collective-permute-done.11.refs_2_ = bf16[4,144,128]{2,1,0:T(8,128)(2,1)S(1)} collective-permute-done((bf16[4,144,128]{2,1,0:T(8,128)(2,1)S(1)}, bf16[4,144,128]{2,1,0:T(8,128)(2,1)S(1)}, u32[]{:S(2)}, u32[]{:S(2)}) %collective-permute-start.11) | collective-permute-done | bytes 147488 | tf_op jit(solution)/shard_map/ppermute | solution.py:26
  19.1 1.4 %collective-permute-done.12.refs_3_ = bf16[4,144,128]{2,1,0:T(8,128)(2,1)S(1)} collective-permute-done((bf16[4,144,128]{2,1,0:T(8,128)(2,1)S(1)}, bf16[4,144,128]{2,1,0:T(8,128)(2,1)S(1)}, u32[]{:S(2)}, u32[]{:S(2)}) %collective-permute-start.12) | collective-permute-done | bytes 147488 | tf_op jit(solution)/shard_map/ppermute | solution.py:26
  20.5 2.4 %attention.1 = (bf16[128,512]{1,0:T(8,128)(2,1)S(1)}, bf16[8,128,128]{2,1,0:T(8,128)(2,1)S(1)}) custom-call(s32[1]{0:T(128)} %bitcast.4.core_ref, s32[1,128]{1,0:T(1,128)S(1)} %bitcast.32, s32[1,128]{1,0:T(1,128)S(1)} %bitcast.31, bf16[128,256]{1,0:T(8,128)(2,1)S(1)} %copy-done.1, bf16[128,256]{1,0:T(8,128)(2,1)S(1)} %collective-permute-done.8.qo_ref, ...), custom_call_target="tpu_custom_call" | custom-call | flops 671088640 | bytes 1048576 | tf_op jit(solution)/shard_map/attention/pallas_call | solution.py:131
  22.9 2.3 %product.1 = bf16[128,4096]{1,0:T(8,128)(2,1)S(1)} custom-call(bf16[128,512]{1,0:T(8,128)(2,1)S(1)} %get-tuple-element.61.dq_ref, bf16[256,4096]{1,0:T(8,128)(2,1)S(1)} %get-tuple-element.62.wm_ref, bf16[256,4096]{1,0:T(8,128)(2,1)} %collective-permute-done.13.wo_ref), custom_call_target="tpu_custom_call" | custom-call | flops 536870912 | bytes 4194304 | tf_op jit(solution)/shard_map/product/pallas_call | solution.py:162
  25.2 1.6 %collective-permute-start.15 = (bf16[128,4096]{1,0:T(8,128)(2,1)S(1)}, bf16[128,4096]{1,0:T(8,128)(2,1)S(1)}, u32[]{:S(2)}, u32[]{:S(2)}) collective-permute-start(bf16[128,4096]{1,0:T(8,128)(2,1)S(1)} %product.1), channel_id=1, source_target_pairs={{0,2},{1,3},{2,0},{3,1},{4,6},{5,7},{6,4},{7,5},{8,10},{9,11},{10,... | collective-permute-start | bytes 3145736 | tf_op jit(solution)/shard_map/ppermute | solution.py:26
  26.9 15.4 %while.12 = (s32[]{:T(128)}, bf16[128,256]{1,0:T(8,128)(2,1)}, bf16[8,128,128]{2,1,0:T(8,128)(2,1)S(1)}, s32[]{:T(128)}, s32[]{:T(128)}, /*index=5*/s32[]{:T(128)}, s32[]{:T(128)}) while((s32[]{:T(128)}, bf16[128,256]{1,0:T(8,128)(2,1)}, bf16[8,128,128]{2,1,0:T(8,128)(2,1)S(1)}, s32[]{:T(128)}, s32[]{:T(128)}, /*index=5*/s32[]{:T(128)}, ...), condition=%wide.region_1.2_spmd, body=%wide.region_0.1_spmd.sunk | while | flops 507910 | bytes 2490695 | solution.py:282
  26.9 1.6 %collective-permute-start = (bf16[4,128,128]{2,1,0:T(8,128)(2,1)S(1)}, bf16[4,128,128]{2,1,0:T(8,128)(2,1)S(1)}, u32[]{:S(2)}, u32[]{:S(2)}) collective-permute-start(bf16[4,128,128]{2,1,0:T(8,128)(2,1)S(1)} %constant_dynamic-slice_fusion.6), channel_id=1, source_target_pairs={{0,4},{4,0},{8,12},{12,8},{16,20},{20,16},{24,28},{28,24},{1,5},{5... | collective-permute-start | bytes 393224 | tf_op jit(solution)/shard_map/while/body/ppermute | solution.py:26
  28.5 3.8 %collective-permute-done = bf16[4,128,128]{2,1,0:T(8,128)(2,1)S(1)} collective-permute-done((bf16[4,128,128]{2,1,0:T(8,128)(2,1)S(1)}, bf16[4,128,128]{2,1,0:T(8,128)(2,1)S(1)}, u32[]{:S(2)}, u32[]{:S(2)}) %collective-permute-start) | collective-permute-done | bytes 131104 | tf_op jit(solution)/shard_map/while/body/ppermute | solution.py:26
  32.3 3.0 %collective-permute-start.1 = (bf16[128,128]{1,0:T(8,128)(2,1)S(1)}, bf16[128,128]{1,0:T(8,128)(2,1)S(1)}, u32[]{:S(2)}, u32[]{:S(2)}) collective-permute-start(bf16[128,128]{1,0:T(8,128)(2,1)S(1)} %get-tuple-element.112), channel_id=1, source_target_pairs={{0,24},{4,28},{8,16},{12,20},{16,8},{20,12},{24,0},{28,4},{1,25},{... | collective-permute-start | bytes 98312 | tf_op jit(solution)/shard_map/while/body/ppermute | solution.py:26
  35.3 0.3 collective-permute-start.2
  35.6 1.1 %collective-permute-start.3 = (bf16[128,128]{1,0:T(8,128)(2,1)S(1)}, bf16[128,128]{1,0:T(8,128)(2,1)S(1)}, u32[]{:S(2)}, u32[]{:S(2)}) collective-permute-start(bf16[128,128]{1,0:T(8,128)(2,1)S(1)} %get-tuple-element.114), channel_id=1, source_target_pairs={{0,8},{4,12},{8,0},{12,4},{16,24},{20,28},{24,16},{28,20},{1,9},{5... | collective-permute-start | bytes 98312 | tf_op jit(solution)/shard_map/while/body/ppermute | solution.py:26
  36.7 1.4 %collective-permute-done.1 = bf16[128,128]{1,0:T(8,128)(2,1)S(1)} collective-permute-done((bf16[128,128]{1,0:T(8,128)(2,1)S(1)}, bf16[128,128]{1,0:T(8,128)(2,1)S(1)}, u32[]{:S(2)}, u32[]{:S(2)}) %collective-permute-start.1) | collective-permute-done | bytes 32800 | tf_op jit(solution)/shard_map/while/body/ppermute | solution.py:26
  38.2 2.2 %collective-permute-done.2 = bf16[128,128]{1,0:T(8,128)(2,1)S(1)} collective-permute-done((bf16[128,128]{1,0:T(8,128)(2,1)S(1)}, bf16[128,128]{1,0:T(8,128)(2,1)S(1)}, u32[]{:S(2)}, u32[]{:S(2)}) %collective-permute-start.2) | collective-permute-done | bytes 32800 | tf_op jit(solution)/shard_map/while/body/ppermute | solution.py:26
  40.4 1.2 %collective-permute-done.4 = bf16[128,128]{1,0:T(8,128)(2,1)S(1)} collective-permute-done((bf16[128,128]{1,0:T(8,128)(2,1)S(1)}, bf16[128,128]{1,0:T(8,128)(2,1)S(1)}, u32[]{:S(2)}, u32[]{:S(2)}) %collective-permute-start.4) | collective-permute-done | bytes 32800 | tf_op jit(solution)/shard_map/while/body/ppermute | solution.py:26
  41.6 0.6 %pad_maximum_fusion.4 = bf16[128,256]{1,0:T(8,128)(2,1)} fusion(bf16[128,128]{1,0:T(8,128)(2,1)S(1)} %collective-permute-done.4, bf16[128,128]{1,0:T(8,128)(2,1)S(1)} %fusion.11), kind=kLoop, calls=%fused_computation.6.clone.1 | loop fusion | flops 131072 | bytes 131072 | tf_op jit(solution)/shard_map/while/body/concatenate | solution.py:278
  42.3 2.7 %constant_dynamic-slice_fusion.1 = (bf16[256,4096]{1,0:T(8,128)(2,1)S(1)}, bf16[256,4096]{1,0:T(8,128)(2,1)S(1)}) fusion(bf16[256,16384]{1,0:T(8,128)(2,1)} %param.16, s32[]{:T(128)S(6)} %select_n.32, s32[]{:T(128)S(6)} %select_n.31), kind=kLoop, calls=%fused_computation.20 | loop fusion | bytes 8388616 | tf_op jit(solution)/shard_map/dynamic_slice | solution.py:51
  45.0 0.8 %own.1 = (f32[128,4096]{1,0:T(8,128)S(1)}, bf16[128,2048]{1,0:T(8,128)(2,1)S(1)}, bf16[128,2048]{1,0:T(8,128)(2,1)S(1)}) custom-call(bf16[128,512]{1,0:T(8,128)(2,1)S(1)} %get-tuple-element.61.dq_ref, bf16[256,4096]{1,0:T(8,128)(2,1)S(1)} %get-tuple-element.83.wn_ref, bf16[256,4096]{1,0:T(8,128)(2,1)S(1)} %get-tuple-element.82.wo_ref), custom_call_target="tpu_custom_call" | custom-call | tf_op jit(solution)/shard_map/own/pallas_call | solution.py:187
  45.8 0.2 collective-permute-start.16
  46.0 0.4 collective-permute-start.17
  46.3 0.5 collective-permute-start.14
  46.8 5.1 %collective-permute-done.14.kv_far_ref = bf16[128,256]{1,0:T(8,128)(2,1)S(1)} collective-permute-done((bf16[128,256]{1,0:T(8,128)(2,1)S(1)}, bf16[128,256]{1,0:T(8,128)(2,1)S(1)}, u32[]{:S(2)}, u32[]{:S(2)}) %collective-permute-start.14) | collective-permute-done | bytes 65568 | tf_op jit(solution)/shard_map/ppermute | solution.py:26
  51.9 1.4 %finish.1 = bf16[128,4096]{1,0:T(8,128)(2,1)} custom-call(s32[1]{0:T(128)} %bitcast.4.core_ref, bf16[128,256]{1,0:T(8,128)(2,1)S(1)} %copy-done.6, bf16[128,256]{1,0:T(8,128)(2,1)S(1)} %collective-permute-done.14.kv_far_ref, bf16[256,4096]{1,0:T(8,128)(2,1)S(1)} %copy-done, f32[128,4096]{1,0:T(8,128)S(1)} %get-tuple-element.68.acc_ref, ...), custom_call_target="tpu_custom_call" | custom-call | flops 268435456 | bytes 5242880 | tf_op jit(solution)/shard_map/finish/pallas_call | solution.py:229
  (36 shorter events, 0.5 us)
Async XLA Ops:
  1.7 10.2 %collective-permute-start.6 = (bf16[144,128]{1,0:T(8,128)(2,1)S(1)}, bf16[144,128]{1,0:T(8,128)(2,1)S(1)}, u32[]{:S(2)}, u32[]{:S(2)}) collective-permute-start(bf16[144,128]{1,0:T(8,128)(2,1)S(1)} %get-tuple-element.87), channel_id=1, source_target_pairs={{0,16},{4,20},{8,24},{12,28},{16,0},{20,4},{24,8},{28,12},{1,17},{... | collective-permute-start | bytes 110600 | tf_op jit(solution)/shard_map/ppermute | solution.py:26
  5.8 6.1 %collective-permute-start.7 = (bf16[144,128]{1,0:T(8,128)(2,1)S(1)}, bf16[144,128]{1,0:T(8,128)(2,1)S(1)}, u32[]{:S(2)}, u32[]{:S(2)}) collective-permute-start(bf16[144,128]{1,0:T(8,128)(2,1)S(1)} %get-tuple-element.87), channel_id=1, source_target_pairs={{0,24},{4,28},{8,16},{12,20},{16,8},{20,12},{24,0},{28,4},{1,25},{... | collective-permute-start | bytes 110600 | tf_op jit(solution)/shard_map/ppermute | solution.py:26
  7.2 4.8 %collective-permute-start.5 = (bf16[144,128]{1,0:T(8,128)(2,1)S(1)}, bf16[144,128]{1,0:T(8,128)(2,1)S(1)}, u32[]{:S(2)}, u32[]{:S(2)}) collective-permute-start(bf16[144,128]{1,0:T(8,128)(2,1)S(1)} %get-tuple-element.87), channel_id=1, source_target_pairs={{0,8},{4,12},{8,0},{12,4},{16,24},{20,28},{24,16},{28,20},{1,9},{5... | collective-permute-start | bytes 110600 | tf_op jit(solution)/shard_map/ppermute | solution.py:26
  7.4 4.6 %collective-permute-start.8 = (bf16[128,256]{1,0:T(8,128)(2,1)}, bf16[128,256]{1,0:T(8,128)(2,1)S(1)}, u32[]{:S(2)}, u32[]{:S(2)}) collective-permute-start(bf16[128,256]{1,0:T(8,128)(2,1)} %qm_ref.1), channel_id=1, source_target_pairs={{0,1},{1,0},{2,3},{3,2},{4,5},{5,4},{6,7},{7,6},{8,9},{9,8},{10,11... | collective-permute-start | bytes 196616 | tf_op jit(solution)/shard_map/ppermute | solution.py:26
  7.4 4.1 %copy-start.2 = (bf16[128,256]{1,0:T(8,128)(2,1)S(1)}, bf16[128,256]{1,0:T(8,128)(2,1)}, u32[]{:S(2)}) copy-start(bf16[128,256]{1,0:T(8,128)(2,1)} %gm_ref.1) | copy-start | bytes 196612
  7.4 13.1 %copy-start.1 = (bf16[128,256]{1,0:T(8,128)(2,1)S(1)}, bf16[128,256]{1,0:T(8,128)(2,1)}, u32[]{:S(2)}) copy-start(bf16[128,256]{1,0:T(8,128)(2,1)} %qm_ref.1) | copy-start | bytes 196612
  7.4 13.1 %copy-start.3 = (s32[128]{0:T(128)S(1)}, s32[128]{0:T(128)}, u32[]{:S(2)}) copy-start(s32[128]{0:T(128)} %param.15) | copy-start | bytes 1540
  7.4 13.1 %copy-start.4 = (s32[128]{0:T(128)S(1)}, s32[128]{0:T(128)}, u32[]{:S(2)}) copy-start(s32[128]{0:T(128)} %param.14) | copy-start | bytes 1540
  11.5 1.4 %collective-permute-start.9 = (bf16[128,256]{1,0:T(8,128)(2,1)S(1)}, bf16[128,256]{1,0:T(8,128)(2,1)S(1)}, u32[]{:S(2)}, u32[]{:S(2)}) collective-permute-start(bf16[128,256]{1,0:T(8,128)(2,1)S(1)} %copy-done.2), channel_id=1, source_target_pairs={{0,1},{1,0},{2,3},{3,2},{4,5},{5,4},{6,7},{7,6},{8,9},{9,8},{10,11... | collective-permute-start | bytes 196616 | tf_op jit(solution)/shard_map/ppermute | solution.py:26
  12.0 10.9 %copy-start.5 = (bf16[128,256]{1,0:T(8,128)(2,1)}, bf16[128,256]{1,0:T(8,128)(2,1)S(1)}, u32[]{:S(2)}) copy-start(bf16[128,256]{1,0:T(8,128)(2,1)S(1)} %collective-permute-done.8.qo_ref) | copy-start | bytes 196612
  12.8 10.0 %collective-permute-start.13 = (bf16[256,4096]{1,0:T(8,128)(2,1)}, bf16[256,4096]{1,0:T(8,128)(2,1)}, u32[]{:S(2)}, u32[]{:S(2)}) collective-permute-start(bf16[256,4096]{1,0:T(8,128)(2,1)} %get-tuple-element.63), channel_id=1, source_target_pairs={{0,1},{1,0},{2,3},{3,2},{4,5},{5,4},{6,7},{7,6},{8,9},{9,8},{10,11... | collective-permute-start | bytes 6291464 | tf_op jit(solution)/shard_map/ppermute | solution.py:26
  13.2 5.9 %collective-permute-start.11 = (bf16[4,144,128]{2,1,0:T(8,128)(2,1)S(1)}, bf16[4,144,128]{2,1,0:T(8,128)(2,1)S(1)}, u32[]{:S(2)}, u32[]{:S(2)}) collective-permute-start(bf16[4,144,128]{2,1,0:T(8,128)(2,1)S(1)} %pad_maximum_fusion.1.refs_0_), channel_id=1, source_target_pairs={{0,4},{4,0},{8,12},{12,8},{16,20},{20,16},{24,28},{28,24},{1,5},{5... | collective-permute-start | bytes 442376 | tf_op jit(solution)/shard_map/ppermute | solution.py:26
  14.7 4.4 %collective-permute-start.10 = (bf16[4,144,128]{2,1,0:T(8,128)(2,1)S(1)}, bf16[4,144,128]{2,1,0:T(8,128)(2,1)S(1)}, u32[]{:S(2)}, u32[]{:S(2)}) collective-permute-start(bf16[4,144,128]{2,1,0:T(8,128)(2,1)S(1)} %pad_maximum_fusion.1.refs_0_), channel_id=1, source_target_pairs={{0,1},{1,0},{2,3},{3,2},{4,5},{5,4},{6,7},{7,6},{8,9},{9,8},{10,11... | collective-permute-start | bytes 442376 | tf_op jit(solution)/shard_map/ppermute | solution.py:26
  19.1 1.4 %collective-permute-start.12 = (bf16[4,144,128]{2,1,0:T(8,128)(2,1)S(1)}, bf16[4,144,128]{2,1,0:T(8,128)(2,1)S(1)}, u32[]{:S(2)}, u32[]{:S(2)}) collective-permute-start(bf16[4,144,128]{2,1,0:T(8,128)(2,1)S(1)} %collective-permute-done.11.refs_2_), channel_id=1, source_target_pairs={{0,1},{1,0},{2,3},{3,2},{4,5},{5,4},{6,7},{7,6},{8,9},{9,8},{10,11... | collective-permute-start | bytes 442376 | tf_op jit(solution)/shard_map/ppermute | solution.py:26
  25.2 26.7 %collective-permute-start.15 = (bf16[128,4096]{1,0:T(8,128)(2,1)S(1)}, bf16[128,4096]{1,0:T(8,128)(2,1)S(1)}, u32[]{:S(2)}, u32[]{:S(2)}) collective-permute-start(bf16[128,4096]{1,0:T(8,128)(2,1)S(1)} %product.1), channel_id=1, source_target_pairs={{0,2},{1,3},{2,0},{3,1},{4,6},{5,7},{6,4},{7,5},{8,10},{9,11},{10,... | collective-permute-start | bytes 3145736 | tf_op jit(solution)/shard_map/ppermute | solution.py:26
  26.9 5.3 %collective-permute-start = (bf16[4,128,128]{2,1,0:T(8,128)(2,1)S(1)}, bf16[4,128,128]{2,1,0:T(8,128)(2,1)S(1)}, u32[]{:S(2)}, u32[]{:S(2)}) collective-permute-start(bf16[4,128,128]{2,1,0:T(8,128)(2,1)S(1)} %constant_dynamic-slice_fusion.6), channel_id=1, source_target_pairs={{0,4},{4,0},{8,12},{12,8},{16,20},{20,16},{24,28},{28,24},{1,5},{5... | collective-permute-start | bytes 393224 | tf_op jit(solution)/shard_map/while/body/ppermute | solution.py:26
  32.3 5.9 %collective-permute-start.1 = (bf16[128,128]{1,0:T(8,128)(2,1)S(1)}, bf16[128,128]{1,0:T(8,128)(2,1)S(1)}, u32[]{:S(2)}, u32[]{:S(2)}) collective-permute-start(bf16[128,128]{1,0:T(8,128)(2,1)S(1)} %get-tuple-element.112), channel_id=1, source_target_pairs={{0,24},{4,28},{8,16},{12,20},{16,8},{20,12},{24,0},{28,4},{1,25},{... | collective-permute-start | bytes 98312 | tf_op jit(solution)/shard_map/while/body/ppermute | solution.py:26
  35.3 5.1 %collective-permute-start.2 = (bf16[128,128]{1,0:T(8,128)(2,1)S(1)}, bf16[128,128]{1,0:T(8,128)(2,1)S(1)}, u32[]{:S(2)}, u32[]{:S(2)}) collective-permute-start(bf16[128,128]{1,0:T(8,128)(2,1)S(1)} %get-tuple-element.113), channel_id=1, source_target_pairs={{0,16},{4,20},{8,24},{12,28},{16,0},{20,4},{24,8},{28,12},{1,17},{... | collective-permute-start | bytes 98312 | tf_op jit(solution)/shard_map/while/body/ppermute | solution.py:26
  35.6 4.7 %collective-permute-start.3 = (bf16[128,128]{1,0:T(8,128)(2,1)S(1)}, bf16[128,128]{1,0:T(8,128)(2,1)S(1)}, u32[]{:S(2)}, u32[]{:S(2)}) collective-permute-start(bf16[128,128]{1,0:T(8,128)(2,1)S(1)} %get-tuple-element.114), channel_id=1, source_target_pairs={{0,8},{4,12},{8,0},{12,4},{16,24},{20,28},{24,16},{28,20},{1,9},{5... | collective-permute-start | bytes 98312 | tf_op jit(solution)/shard_map/while/body/ppermute | solution.py:26
  40.4 1.3 %collective-permute-start.4 = (bf16[128,128]{1,0:T(8,128)(2,1)S(1)}, bf16[128,128]{1,0:T(8,128)(2,1)S(1)}, u32[]{:S(2)}, u32[]{:S(2)}) collective-permute-start(bf16[128,128]{1,0:T(8,128)(2,1)S(1)} %fusion.11), channel_id=1, source_target_pairs={{0,1},{1,0},{2,3},{3,2},{4,5},{5,4},{6,7},{7,6},{8,9},{9,8},{10,11... | collective-permute-start | bytes 98312 | tf_op jit(solution)/shard_map/while/body/ppermute | solution.py:26
  45.0 1.4 %copy-start.6 = (bf16[128,256]{1,0:T(8,128)(2,1)S(1)}, bf16[128,256]{1,0:T(8,128)(2,1)}, u32[]{:S(2)}) copy-start(bf16[128,256]{1,0:T(8,128)(2,1)} %get-tuple-element.66.kv_ref) | copy-start | bytes 196612
  45.0 6.9 %copy-start = (bf16[256,4096]{1,0:T(8,128)(2,1)S(1)}, bf16[256,4096]{1,0:T(8,128)(2,1)}, u32[]{:S(2)}) copy-start(bf16[256,4096]{1,0:T(8,128)(2,1)} %w_ref.1) | copy-start | bytes 6291460
  45.8 6.1 %collective-permute-start.16 = (bf16[128,2048]{1,0:T(8,128)(2,1)S(1)}, bf16[128,2048]{1,0:T(8,128)(2,1)S(1)}, u32[]{:S(2)}, u32[]{:S(2)}) collective-permute-start(bf16[128,2048]{1,0:T(8,128)(2,1)S(1)} %get-tuple-element.69), channel_id=1, source_target_pairs={{0,1},{1,0},{2,3},{3,2},{4,5},{5,4},{6,7},{7,6},{8,9},{9,8},{10,11... | collective-permute-start | bytes 1572872 | tf_op jit(solution)/shard_map/ppermute | solution.py:26
  46.0 5.9 %collective-permute-start.17 = (bf16[128,2048]{1,0:T(8,128)(2,1)S(1)}, bf16[128,2048]{1,0:T(8,128)(2,1)S(1)}, u32[]{:S(2)}, u32[]{:S(2)}) collective-permute-start(bf16[128,2048]{1,0:T(8,128)(2,1)S(1)} %get-tuple-element.70), channel_id=1, source_target_pairs={{0,1},{1,0},{2,3},{3,2},{4,5},{5,4},{6,7},{7,6},{8,9},{9,8},{10,11... | collective-permute-start | bytes 1572872 | tf_op jit(solution)/shard_map/ppermute | solution.py:26
  46.3 5.6 %collective-permute-start.14 = (bf16[128,256]{1,0:T(8,128)(2,1)S(1)}, bf16[128,256]{1,0:T(8,128)(2,1)S(1)}, u32[]{:S(2)}, u32[]{:S(2)}) collective-permute-start(bf16[128,256]{1,0:T(8,128)(2,1)S(1)} %copy-done.6), channel_id=1, source_target_pairs={{0,2},{1,3},{2,0},{3,1},{4,6},{5,7},{6,4},{7,5},{8,10},{9,11},{10,... | collective-permute-start | bytes 196616 | tf_op jit(solution)/shard_map/ppermute | solution.py:26

commit v13 on v12

--- a/solution.py
+++ b/solution.py
@@ -49,6 +49,37 @@
 def column_block(w_query, block, share, after):
     w_query, _ = lax.optimization_barrier((w_query, after))
     return lax.dynamic_slice_in_dim(w_query, block * share, share, axis=1)
+
+
+def carve_kernel(block_ref, w_ref, *refs):
+    outs, sems = refs[1:-1], refs[-1]
+    rows, share = outs[0].shape
+    parts = sems.shape[1]
+    copies = []
+    for i, out_ref in enumerate(outs):
+        at = pl.multiple_of(block_ref[i] * share, share)
+        for j in range(parts):
+            part = slice(j * (rows // parts), (j + 1) * (rows // parts))
+            source = w_ref.at[part, pl.ds(at, share)]
+            copies.append(pltpu.make_async_copy(source, out_ref.at[part, :], sems.at[i, j]))
+            copies[-1].start()
+    for one in copies:
+        one.wait()
+
+
+def carve(blocks, w_query, share, after):
+    block = jax.ShapeDtypeStruct((w_query.shape[0], share), w_query.dtype)
+    count = len(blocks)
+    return pl.pallas_call(
+        carve_kernel,
+        out_shape=[block] * count,
+        in_specs=[SMEM, HBM, ANY],
+        out_specs=[pl.BlockSpec(memory_space=pltpu.VMEM)] * count,
+        scratch_shapes=[pltpu.SemaphoreType.DMA((count, 4))],
+        compiler_params=params(48),
+        cost_estimate=pl.CostEstimate(flops=0, bytes_accessed=0, transcendentals=0),
+        name="carve",
+    )(jnp.stack(blocks), w_query, after)
 
 
 def attention_kernel(core_ref, pos_ref, doc_ref, qm_ref, qo_ref, gm_ref, go_ref, *refs):
@@ -191,6 +222,7 @@
         in_specs=[pl.BlockSpec()] * 3,
         out_specs=[pl.BlockSpec()] * (1 + GIVES),
         compiler_params=params(),
+        cost_estimate=pl.CostEstimate(flops=0, bytes_accessed=0, transcendentals=0),
         name="own",
     )(dq, w_near, w_other)
 
@@ -267,22 +299,16 @@
     part = product(dq, far_mine, far_other, 0, share, jnp.bfloat16)
     far = swapped(part, "head", 2)
 
-    def exchange(state):
-        left, _ = state
-        sent = lax.dynamic_slice_in_dim(back, left * half, half, axis=0)
-        pair = back[:half].astype(jnp.float32) + swapped(sent, "ctx", 1).astype(jnp.float32)
-        mine = pair[0]
-        for s in range(1, half):
-            mine = mine + swapped(pair[s].astype(jnp.bfloat16), "ctx", 2 * s).astype(jnp.float32)
-        mine = mine.astype(jnp.bfloat16)
-        return left - 1, jnp.concatenate([mine, swapped(mine, "head", 1)], axis=1)
-
-    back, part, positions = lax.optimization_barrier((back, part, positions))
-    trips = 1 + jnp.minimum(positions[0], 0)
-    _, kv = lax.while_loop(lambda state: state[0] > 0, exchange, (trips, q_other))
+    back, part = lax.optimization_barrier((back, part))
+    pair = back[:half].astype(jnp.float32) + swapped(back[half:], "ctx", 1).astype(jnp.float32)
+    mine = pair[0]
+    for s in range(1, half):
+        mine = mine + swapped(pair[s].astype(jnp.bfloat16), "ctx", 2 * s).astype(jnp.float32)
+    mine = mine.astype(jnp.bfloat16)
+    kv = jnp.concatenate([mine, swapped(mine, "head", 1)], axis=1)
     kv_far = swapped(kv, "head", 2)
 
-    acc, *give = own(dq, column_block(w_query, head, share, kv), column_block(w_query, head ^ 1, share, kv))
+    acc, *give = own(dq, *carve([head, head ^ 1], w_query, share, kv))
     given = [swapped(one, "head", 1) for one in give]
     return finish(core, kv, kv_far, w_kv, acc, far, given)
 

time: 53.6 us -> 53.6 us (level)
  local copies, waits for them, and re-layouts: 7.53 us -> 3.52 us
  waiting for transfers between devices: 20.3 us -> 22.9 us
  Pallas kernels: 6.86 us -> 7.95 us
  starting transfers between devices: 16.7 us -> 17.7 us
  other arithmetic: 1.71 us -> 1.16 us
    dynamic_slice x2 -> x1, local copies, waits for them, and re-layouts: 6.73 us -> 2.75 us  [column_block(): return lax.dynamic_slice_in_dim(w_query, block * share, share, axis=1)]
    pallas_call x0 -> x1, Pallas kernels: none -> 2.76 us  [carve(): pl.pallas_call(carve_kernel, out_shape=[block] * count, in_specs=[SMEM, H...]
    ppermute x18, waiting for transfers between devices: 20.3 us -> 22.9 us  [swapped(): lax.ppermute(value, axis, [(source, source ^ bits) for source in range(co...]
    pallas_call x1, Pallas kernels: 2.31 us -> 0.73 us  [product(): pl.pallas_call(functools.partial(product_kernel, first), out_shape=jax.Sh...]
    ppermute x18, starting transfers between devices: 16.7 us -> 17.7 us  [swapped(): lax.ppermute(value, axis, [(source, source ^ bits) for source in range(co...]
    concatenate x1, other arithmetic: 0.64 us -> 0.01 us  [on_device(): kv = jnp.concatenate([mine, swapped(mine, 'head', 1)], axis=1)]
  transfers between devices with their start and end apart: 18 -> 18, of which waited for: 8 -> 8; matrix products, arithmetic and copies ran while one was open for 14% -> 5% of each run, Pallas kernels for 6% -> 11%
where the time goes in v13:
time: 53.6 us; the launch traced here: 53.4 us
  waiting for transfers between devices  22.9 us (43%)
  starting transfers between devices  17.7 us (33%)
  Pallas kernels  7.95 us (15%)
  local copies, waits for them, and re-layouts  3.52 us (7%)
  other arithmetic  1.16 us (2%)
    ppermute x18, waiting for transfers between devices, swapped(): lax.ppermute(value, axis, [(source, source ^ bits) for source in range(co...  22.9 us
    ppermute x18, starting transfers between devices, swapped(): lax.ppermute(value, axis, [(source, source ^ bits) for source in range(co...  17.7 us
    pallas_call x1, Pallas kernels, carve(): pl.pallas_call(carve_kernel, out_shape=[block] * count, in_specs=[SMEM, H...  2.76 us
    dynamic_slice x1, local copies, waits for them, and re-layouts, column_block(): return lax.dynamic_slice_in_dim(w_query, block * share, share, axis=1)  2.75 us
    pallas_call x1, Pallas kernels, attention(): pl.pallas_call(attention_kernel, out_shape=[jax.ShapeDtypeStruct((rows, 2...  2.43 us
    pallas_call x1, Pallas kernels, finish(): pl.pallas_call(finish_kernel, out_shape=jax.ShapeDtypeStruct((rows, share...  1.31 us
  transfers between devices with their start and end apart: 18, of which 8 were waited for; matrix products, arithmetic and copies ran while one was open for 5% of the time, Pallas kernels for 11%

profile of v13, /device:TPU:0, one launch (start us, length us, event | category | flops | bytes accessed | tf_op | source)
XLA Modules:
  0.0 53.4 jit_solution(158974879810094458)
XLA Ops:
  0.0 0.7 %reshape.19 = s32[2,64]{1,0:T(2,128)S(1)} reshape(s32[128]{0:T(128)} %param.12) | data formatting | bytes 1024 | tf_op jit(solution)/shard_map/reshape | solution.py:44
  0.7 0.1 fusion.5
  0.9 0.8 %broadcast_select_fusion = bf16[128,128]{1,0:T(8,128)(2,1)S(1)} fusion(bf16[128,128]{1,0:T(8,128)(2,1)} %param.9, bf16[128,128]{1,0:T(8,128)(2,1)} %param.10, pred[]{:T(512)} %bitcast.3), kind=kLoop, calls=%fused_computation.12 | loop fusion | flops 16384 | bytes 98305 | tf_op jit(solution)/shard_map/jit(_where)/select_n | solution.py:43
  1.6 0.1 fusion.6
  1.7 3.1 %collective-permute-start = (bf16[144,128]{1,0:T(8,128)(2,1)S(1)}, bf16[144,128]{1,0:T(8,128)(2,1)S(1)}, u32[]{:S(2)}, u32[]{:S(2)}) collective-permute-start(bf16[144,128]{1,0:T(8,128)(2,1)S(1)} %get-tuple-element.41), channel_id=1, source_target_pairs={{0,8},{4,12},{8,0},{12,4},{16,24},{20,28},{24,16},{28,20},{1,9},{5... | collective-permute-start | bytes 110600 | tf_op jit(solution)/shard_map/ppermute | solution.py:26
  4.8 2.6 %collective-permute-start.1 = (bf16[144,128]{1,0:T(8,128)(2,1)S(1)}, bf16[144,128]{1,0:T(8,128)(2,1)S(1)}, u32[]{:S(2)}, u32[]{:S(2)}) collective-permute-start(bf16[144,128]{1,0:T(8,128)(2,1)S(1)} %get-tuple-element.41), channel_id=1, source_target_pairs={{0,16},{4,20},{8,24},{12,28},{16,0},{20,4},{24,8},{28,12},{1,17},{... | collective-permute-start | bytes 110600 | tf_op jit(solution)/shard_map/ppermute | solution.py:26
  7.4 0.5 collective-permute-start.4
  7.9 2.7 %constant_dynamic-slice_fusion = (bf16[256,4096]{1,0:T(8,128)(2,1)S(1)}, bf16[256,4096]{1,0:T(8,128)(2,1)S(1)}) fusion(bf16[256,16384]{1,0:T(8,128)(2,1)} %w_ref.2, s32[]{:T(128)S(6)} %select_n.18, s32[]{:T(128)S(6)} %select_n.17), kind=kLoop, calls=%fused_computation.20 | loop fusion | bytes 8388616 | tf_op jit(solution)/shard_map/dynamic_slice | solution.py:51
  10.7 2.5 %collective-permute-done.2 = bf16[144,128]{1,0:T(8,128)(2,1)S(1)} collective-permute-done((bf16[144,128]{1,0:T(8,128)(2,1)S(1)}, bf16[144,128]{1,0:T(8,128)(2,1)S(1)}, u32[]{:S(2)}, u32[]{:S(2)}) %collective-permute-start.2) | collective-permute-done | bytes 36896 | tf_op jit(solution)/shard_map/ppermute | solution.py:26
  13.2 0.1 collective-permute-start.8
  13.3 1.6 %collective-permute-start.6 = (bf16[4,144,128]{2,1,0:T(8,128)(2,1)S(1)}, bf16[4,144,128]{2,1,0:T(8,128)(2,1)S(1)}, u32[]{:S(2)}, u32[]{:S(2)}) collective-permute-start(bf16[4,144,128]{2,1,0:T(8,128)(2,1)S(1)} %pad_maximum_fusion.refs_0_), channel_id=1, source_target_pairs={{0,4},{4,0},{8,12},{12,8},{16,20},{20,16},{24,28},{28,24},{1,5},{5... | collective-permute-start | bytes 442376 | tf_op jit(solution)/shard_map/ppermute | solution.py:26
  14.9 0.2 collective-permute-start.5
  15.0 4.5 %collective-permute-done.6.refs_2_ = bf16[4,144,128]{2,1,0:T(8,128)(2,1)S(1)} collective-permute-done((bf16[4,144,128]{2,1,0:T(8,128)(2,1)S(1)}, bf16[4,144,128]{2,1,0:T(8,128)(2,1)S(1)}, u32[]{:S(2)}, u32[]{:S(2)}) %collective-permute-start.6) | collective-permute-done | bytes 147488 | tf_op jit(solution)/shard_map/ppermute | solution.py:26
  19.6 1.4 %collective-permute-done.7.refs_3_ = bf16[4,144,128]{2,1,0:T(8,128)(2,1)S(1)} collective-permute-done((bf16[4,144,128]{2,1,0:T(8,128)(2,1)S(1)}, bf16[4,144,128]{2,1,0:T(8,128)(2,1)S(1)}, u32[]{:S(2)}, u32[]{:S(2)}) %collective-permute-start.7) | collective-permute-done | bytes 147488 | tf_op jit(solution)/shard_map/ppermute | solution.py:26
  21.0 2.4 %attention.1 = (bf16[128,512]{1,0:T(8,128)(2,1)S(1)}, bf16[8,128,128]{2,1,0:T(8,128)(2,1)S(1)}) custom-call(s32[1]{0:T(128)} %bitcast.core_ref, s32[1,128]{1,0:T(1,128)S(1)} %bitcast.27, s32[1,128]{1,0:T(1,128)S(1)} %bitcast.28, bf16[128,256]{1,0:T(8,128)(2,1)S(1)} %copy-done.1, bf16[128,256]{1,0:T(8,128)(2,1)S(1)} %collective-permute-done.3.qo_ref, ...), custom_call_target="tpu_custom_call" | custom-call | flops 671088640 | bytes 1048576 | tf_op jit(solution)/shard_map/attention/pallas_call | solution.py:162
  23.4 0.7 %product.1 = bf16[128,4096]{1,0:T(8,128)(2,1)S(1)} custom-call(bf16[128,512]{1,0:T(8,128)(2,1)S(1)} %get-tuple-element.24.dq_ref, bf16[256,4096]{1,0:T(8,128)(2,1)S(1)} %get-tuple-element.25.wm_ref, bf16[256,4096]{1,0:T(8,128)(2,1)S(1)} %collective-permute-done.8.wo_ref), custom_call_target="tpu_custom_call" | custom-call | flops 536870912 | bytes 4194304 | tf_op jit(solution)/shard_map/product/pallas_call | solution.py:193
  24.2 1.6 %collective-permute-start.9 = (bf16[4,128,128]{2,1,0:T(8,128)(2,1)S(1)}, bf16[4,128,128]{2,1,0:T(8,128)(2,1)S(1)}, u32[]{:S(2)}, u32[]{:S(2)}) collective-permute-start(bf16[4,128,128]{2,1,0:T(8,128)(2,1)S(1)} %slice.26), channel_id=1, source_target_pairs={{0,4},{4,0},{8,12},{12,8},{16,20},{20,16},{24,28},{28,24},{1,5},{5... | collective-permute-start | bytes 393224 | tf_op jit(solution)/shard_map/ppermute | solution.py:26
  25.7 1.5 %collective-permute-start.15 = (bf16[128,4096]{1,0:T(8,128)(2,1)S(1)}, bf16[128,4096]{1,0:T(8,128)(2,1)S(1)}, u32[]{:S(2)}, u32[]{:S(2)}) collective-permute-start(bf16[128,4096]{1,0:T(8,128)(2,1)S(1)} %product.1), channel_id=1, source_target_pairs={{0,2},{1,3},{2,0},{3,1},{4,6},{5,7},{6,4},{7,5},{8,10},{9,11},{10,... | collective-permute-start | bytes 3145736 | tf_op jit(solution)/shard_map/ppermute | solution.py:26
  27.2 2.5 %collective-permute-done.9 = bf16[4,128,128]{2,1,0:T(8,128)(2,1)S(1)} collective-permute-done((bf16[4,128,128]{2,1,0:T(8,128)(2,1)S(1)}, bf16[4,128,128]{2,1,0:T(8,128)(2,1)S(1)}, u32[]{:S(2)}, u32[]{:S(2)}) %collective-permute-start.9) | collective-permute-done | bytes 131104 | tf_op jit(solution)/shard_map/ppermute | solution.py:26
  29.9 1.9 %collective-permute-start.11 = (bf16[128,128]{1,0:T(8,128)(2,1)S(1)}, bf16[128,128]{1,0:T(8,128)(2,1)S(1)}, u32[]{:S(2)}, u32[]{:S(2)}) collective-permute-start(bf16[128,128]{1,0:T(8,128)(2,1)S(1)} %get-tuple-element.39), channel_id=1, source_target_pairs={{0,16},{4,20},{8,24},{12,28},{16,0},{20,4},{24,8},{28,12},{1,17},{... | collective-permute-start | bytes 98312 | tf_op jit(solution)/shard_map/ppermute | solution.py:26
  31.8 2.4 %collective-permute-start.12 = (bf16[128,128]{1,0:T(8,128)(2,1)S(1)}, bf16[128,128]{1,0:T(8,128)(2,1)S(1)}, u32[]{:S(2)}, u32[]{:S(2)}) collective-permute-start(bf16[128,128]{1,0:T(8,128)(2,1)S(1)} %get-tuple-element.38), channel_id=1, source_target_pairs={{0,24},{4,28},{8,16},{12,20},{16,8},{20,12},{24,0},{28,4},{1,25},{... | collective-permute-start | bytes 98312 | tf_op jit(solution)/shard_map/ppermute | solution.py:26
  34.3 0.5 collective-permute-done.11
  34.8 2.8 %collective-permute-done.12 = bf16[128,128]{1,0:T(8,128)(2,1)S(1)} collective-permute-done((bf16[128,128]{1,0:T(8,128)(2,1)S(1)}, bf16[128,128]{1,0:T(8,128)(2,1)S(1)}, u32[]{:S(2)}, u32[]{:S(2)}) %collective-permute-start.12) | collective-permute-done | bytes 32800 | tf_op jit(solution)/shard_map/ppermute | solution.py:26
  37.7 0.1 pad_add_fusion.block_ref
  37.7 1.1 %collective-permute-done.13 = bf16[128,128]{1,0:T(8,128)(2,1)S(1)} collective-permute-done((bf16[128,128]{1,0:T(8,128)(2,1)S(1)}, bf16[128,128]{1,0:T(8,128)(2,1)S(1)}, u32[]{:S(2)}, u32[]{:S(2)}) %collective-permute-start.13) | collective-permute-done | bytes 32800 | tf_op jit(solution)/shard_map/ppermute | solution.py:26
  38.9 2.8 %carve.1 = (bf16[256,4096]{1,0:T(8,128)(2,1)S(1)}, bf16[256,4096]{1,0:T(8,128)(2,1)S(1)}) custom-call(s32[2]{0:T(128)S(1)} %pad_add_fusion.block_ref, bf16[256,16384]{1,0:T(8,128)(2,1)} %w_ref.2, bf16[128,256]{1,0:T(8,128)(2,1)S(1)} %pad_maximum_fusion.1.refs_0_.kv_ref), custom_call_target="tpu_custom_call" | custom-call | tf_op jit(solution)/shard_map/carve/pallas_call | solution.py:73
  41.6 0.7 %own.1 = (f32[128,4096]{1,0:T(8,128)S(1)}, bf16[128,2048]{1,0:T(8,128)(2,1)S(1)}, bf16[128,2048]{1,0:T(8,128)(2,1)S(1)}) custom-call(bf16[128,512]{1,0:T(8,128)(2,1)S(1)} %get-tuple-element.24.dq_ref, bf16[256,4096]{1,0:T(8,128)(2,1)S(1)} %get-tuple-element.28.wn_ref, bf16[256,4096]{1,0:T(8,128)(2,1)S(1)} %get-tuple-element.29.wo_ref), custom_call_target="tpu_custom_call" | custom-call | tf_op jit(solution)/shard_map/own/pallas_call | solution.py:218
  42.4 0.2 collective-permute-start.16
  42.6 0.3 collective-permute-start.17
  42.9 1.5 %collective-permute-start.14 = (bf16[128,256]{1,0:T(8,128)(2,1)S(1)}, bf16[128,256]{1,0:T(8,128)(2,1)S(1)}, u32[]{:S(2)}, u32[]{:S(2)}) collective-permute-start(bf16[128,256]{1,0:T(8,128)(2,1)S(1)} %pad_maximum_fusion.1.refs_0_.kv_ref), channel_id=1, source_target_pairs={{0,2},{1,3},{2,0},{3,1},{4,6},{5,7},{6,4},{7,5},{8,10},{9,11},{10,... | collective-permute-start | bytes 196616 | tf_op jit(solution)/shard_map/ppermute | solution.py:26
  44.5 7.6 %collective-permute-done.14.kv_far_ref = bf16[128,256]{1,0:T(8,128)(2,1)S(1)} collective-permute-done((bf16[128,256]{1,0:T(8,128)(2,1)S(1)}, bf16[128,256]{1,0:T(8,128)(2,1)S(1)}, u32[]{:S(2)}, u32[]{:S(2)}) %collective-permute-start.14) | collective-permute-done | bytes 65568 | tf_op jit(solution)/shard_map/ppermute | solution.py:26
  52.1 1.3 %finish.1 = bf16[128,4096]{1,0:T(8,128)(2,1)} custom-call(s32[1]{0:T(128)} %bitcast.core_ref, bf16[128,256]{1,0:T(8,128)(2,1)S(1)} %pad_maximum_fusion.1.refs_0_.kv_ref, bf16[128,256]{1,0:T(8,128)(2,1)S(1)} %collective-permute-done.14.kv_far_ref, bf16[256,4096]{1,0:T(8,128)(2,1)S(1)} %copy-done, f32[128,4096]{1,0:T(8,128)S(1)} %get-tuple-element.30.acc_ref, ...), custom_call_target="tpu_custom_call" | custom-call | flops 268435456 | bytes 5242880 | tf_op jit(solution)/shard_map/finish/pallas_call | solution.py:261
  (32 shorter events, 0.3 us)
Async XLA Ops:
  1.7 9.0 %collective-permute-start = (bf16[144,128]{1,0:T(8,128)(2,1)S(1)}, bf16[144,128]{1,0:T(8,128)(2,1)S(1)}, u32[]{:S(2)}, u32[]{:S(2)}) collective-permute-start(bf16[144,128]{1,0:T(8,128)(2,1)S(1)} %get-tuple-element.41), channel_id=1, source_target_pairs={{0,8},{4,12},{8,0},{12,4},{16,24},{20,28},{24,16},{28,20},{1,9},{5... | collective-permute-start | bytes 110600 | tf_op jit(solution)/shard_map/ppermute | solution.py:26
  4.8 5.9 %collective-permute-start.1 = (bf16[144,128]{1,0:T(8,128)(2,1)S(1)}, bf16[144,128]{1,0:T(8,128)(2,1)S(1)}, u32[]{:S(2)}, u32[]{:S(2)}) collective-permute-start(bf16[144,128]{1,0:T(8,128)(2,1)S(1)} %get-tuple-element.41), channel_id=1, source_target_pairs={{0,16},{4,20},{8,24},{12,28},{16,0},{20,4},{24,8},{28,12},{1,17},{... | collective-permute-start | bytes 110600 | tf_op jit(solution)/shard_map/ppermute | solution.py:26
  7.4 5.8 %collective-permute-start.2 = (bf16[144,128]{1,0:T(8,128)(2,1)S(1)}, bf16[144,128]{1,0:T(8,128)(2,1)S(1)}, u32[]{:S(2)}, u32[]{:S(2)}) collective-permute-start(bf16[144,128]{1,0:T(8,128)(2,1)S(1)} %get-tuple-element.41), channel_id=1, source_target_pairs={{0,24},{4,28},{8,16},{12,20},{16,8},{20,12},{24,0},{28,4},{1,25},{... | collective-permute-start | bytes 110600 | tf_op jit(solution)/shard_map/ppermute | solution.py:26
  7.4 5.8 %collective-permute-start.3 = (bf16[128,256]{1,0:T(8,128)(2,1)}, bf16[128,256]{1,0:T(8,128)(2,1)S(1)}, u32[]{:S(2)}, u32[]{:S(2)}) collective-permute-start(bf16[128,256]{1,0:T(8,128)(2,1)} %qm_ref.1), channel_id=1, source_target_pairs={{0,1},{1,0},{2,3},{3,2},{4,5},{5,4},{6,7},{7,6},{8,9},{9,8},{10,11... | collective-permute-start | bytes 196616 | tf_op jit(solution)/shard_map/ppermute | solution.py:26
  7.4 5.8 %collective-permute-start.4 = (bf16[128,256]{1,0:T(8,128)(2,1)}, bf16[128,256]{1,0:T(8,128)(2,1)S(1)}, u32[]{:S(2)}, u32[]{:S(2)}) collective-permute-start(bf16[128,256]{1,0:T(8,128)(2,1)} %gm_ref.1), channel_id=1, source_target_pairs={{0,1},{1,0},{2,3},{3,2},{4,5},{5,4},{6,7},{7,6},{8,9},{9,8},{10,11... | collective-permute-start | bytes 196616 | tf_op jit(solution)/shard_map/ppermute | solution.py:26
  7.9 13.0 %copy-start.1 = (bf16[128,256]{1,0:T(8,128)(2,1)S(1)}, bf16[128,256]{1,0:T(8,128)(2,1)}, u32[]{:S(2)}) copy-start(bf16[128,256]{1,0:T(8,128)(2,1)} %qm_ref.1) | copy-start | bytes 196612
  7.9 13.0 %copy-start.2 = (bf16[128,256]{1,0:T(8,128)(2,1)S(1)}, bf16[128,256]{1,0:T(8,128)(2,1)}, u32[]{:S(2)}) copy-start(bf16[128,256]{1,0:T(8,128)(2,1)} %gm_ref.1) | copy-start | bytes 196612
  7.9 13.0 %copy-start.3 = (s32[128]{0:T(128)S(1)}, s32[128]{0:T(128)}, u32[]{:S(2)}) copy-start(s32[128]{0:T(128)} %param.12) | copy-start | bytes 1540
  7.9 13.0 %copy-start.4 = (s32[128]{0:T(128)S(1)}, s32[128]{0:T(128)}, u32[]{:S(2)}) copy-start(s32[128]{0:T(128)} %param.13) | copy-start | bytes 1540
  13.2 10.2 %collective-permute-start.8 = (bf16[256,4096]{1,0:T(8,128)(2,1)S(1)}, bf16[256,4096]{1,0:T(8,128)(2,1)S(1)}, u32[]{:S(2)}, u32[]{:S(2)}) collective-permute-start(bf16[256,4096]{1,0:T(8,128)(2,1)S(1)} %get-tuple-element.26), channel_id=1, source_target_pairs={{0,1},{1,0},{2,3},{3,2},{4,5},{5,4},{6,7},{7,6},{8,9},{9,8},{10,11... | collective-permute-start | bytes 6291464 | tf_op jit(solution)/shard_map/ppermute | solution.py:26
  13.3 6.3 %collective-permute-start.6 = (bf16[4,144,128]{2,1,0:T(8,128)(2,1)S(1)}, bf16[4,144,128]{2,1,0:T(8,128)(2,1)S(1)}, u32[]{:S(2)}, u32[]{:S(2)}) collective-permute-start(bf16[4,144,128]{2,1,0:T(8,128)(2,1)S(1)} %pad_maximum_fusion.refs_0_), channel_id=1, source_target_pairs={{0,4},{4,0},{8,12},{12,8},{16,20},{20,16},{24,28},{28,24},{1,5},{5... | collective-permute-start | bytes 442376 | tf_op jit(solution)/shard_map/ppermute | solution.py:26
  14.9 4.7 %collective-permute-start.5 = (bf16[4,144,128]{2,1,0:T(8,128)(2,1)S(1)}, bf16[4,144,128]{2,1,0:T(8,128)(2,1)S(1)}, u32[]{:S(2)}, u32[]{:S(2)}) collective-permute-start(bf16[4,144,128]{2,1,0:T(8,128)(2,1)S(1)} %pad_maximum_fusion.refs_0_), channel_id=1, source_target_pairs={{0,1},{1,0},{2,3},{3,2},{4,5},{5,4},{6,7},{7,6},{8,9},{9,8},{10,11... | collective-permute-start | bytes 442376 | tf_op jit(solution)/shard_map/ppermute | solution.py:26
  19.6 1.4 %collective-permute-start.7 = (bf16[4,144,128]{2,1,0:T(8,128)(2,1)S(1)}, bf16[4,144,128]{2,1,0:T(8,128)(2,1)S(1)}, u32[]{:S(2)}, u32[]{:S(2)}) collective-permute-start(bf16[4,144,128]{2,1,0:T(8,128)(2,1)S(1)} %collective-permute-done.6.refs_2_), channel_id=1, source_target_pairs={{0,1},{1,0},{2,3},{3,2},{4,5},{5,4},{6,7},{7,6},{8,9},{9,8},{10,11... | collective-permute-start | bytes 442376 | tf_op jit(solution)/shard_map/ppermute | solution.py:26
  24.2 5.6 %collective-permute-start.9 = (bf16[4,128,128]{2,1,0:T(8,128)(2,1)S(1)}, bf16[4,128,128]{2,1,0:T(8,128)(2,1)S(1)}, u32[]{:S(2)}, u32[]{:S(2)}) collective-permute-start(bf16[4,128,128]{2,1,0:T(8,128)(2,1)S(1)} %slice.26), channel_id=1, source_target_pairs={{0,4},{4,0},{8,12},{12,8},{16,20},{20,16},{24,28},{28,24},{1,5},{5... | collective-permute-start | bytes 393224 | tf_op jit(solution)/shard_map/ppermute | solution.py:26
  25.7 26.3 %collective-permute-start.15 = (bf16[128,4096]{1,0:T(8,128)(2,1)S(1)}, bf16[128,4096]{1,0:T(8,128)(2,1)S(1)}, u32[]{:S(2)}, u32[]{:S(2)}) collective-permute-start(bf16[128,4096]{1,0:T(8,128)(2,1)S(1)} %product.1), channel_id=1, source_target_pairs={{0,2},{1,3},{2,0},{3,1},{4,6},{5,7},{6,4},{7,5},{8,10},{9,11},{10,... | collective-permute-start | bytes 3145736 | tf_op jit(solution)/shard_map/ppermute | solution.py:26
  29.8 4.5 %collective-permute-start.10 = (bf16[128,128]{1,0:T(8,128)(2,1)S(1)}, bf16[128,128]{1,0:T(8,128)(2,1)S(1)}, u32[]{:S(2)}, u32[]{:S(2)}) collective-permute-start(bf16[128,128]{1,0:T(8,128)(2,1)S(1)} %get-tuple-element.37), channel_id=1, source_target_pairs={{0,8},{4,12},{8,0},{12,4},{16,24},{20,28},{24,16},{28,20},{1,9},{5... | collective-permute-start | bytes 98312 | tf_op jit(solution)/shard_map/ppermute | solution.py:26
  29.9 4.9 %collective-permute-start.11 = (bf16[128,128]{1,0:T(8,128)(2,1)S(1)}, bf16[128,128]{1,0:T(8,128)(2,1)S(1)}, u32[]{:S(2)}, u32[]{:S(2)}) collective-permute-start(bf16[128,128]{1,0:T(8,128)(2,1)S(1)} %get-tuple-element.39), channel_id=1, source_target_pairs={{0,16},{4,20},{8,24},{12,28},{16,0},{20,4},{24,8},{28,12},{1,17},{... | collective-permute-start | bytes 98312 | tf_op jit(solution)/shard_map/ppermute | solution.py:26
  31.8 5.7 %collective-permute-start.12 = (bf16[128,128]{1,0:T(8,128)(2,1)S(1)}, bf16[128,128]{1,0:T(8,128)(2,1)S(1)}, u32[]{:S(2)}, u32[]{:S(2)}) collective-permute-start(bf16[128,128]{1,0:T(8,128)(2,1)S(1)} %get-tuple-element.38), channel_id=1, source_target_pairs={{0,24},{4,28},{8,16},{12,20},{16,8},{20,12},{24,0},{28,4},{1,25},{... | collective-permute-start | bytes 98312 | tf_op jit(solution)/shard_map/ppermute | solution.py:26
  37.6 1.3 %collective-permute-start.13 = (bf16[128,128]{1,0:T(8,128)(2,1)S(1)}, bf16[128,128]{1,0:T(8,128)(2,1)S(1)}, u32[]{:S(2)}, u32[]{:S(2)}) collective-permute-start(bf16[128,128]{1,0:T(8,128)(2,1)S(1)} %fusion.3), channel_id=1, source_target_pairs={{0,1},{1,0},{2,3},{3,2},{4,5},{5,4},{6,7},{7,6},{8,9},{9,8},{10,11... | collective-permute-start | bytes 98312 | tf_op jit(solution)/shard_map/ppermute | solution.py:26
  41.6 10.4 %copy-start = (bf16[256,4096]{1,0:T(8,128)(2,1)S(1)}, bf16[256,4096]{1,0:T(8,128)(2,1)}, u32[]{:S(2)}) copy-start(bf16[256,4096]{1,0:T(8,128)(2,1)} %w_ref.3) | copy-start | bytes 6291460
  42.4 9.7 %collective-permute-start.16 = (bf16[128,2048]{1,0:T(8,128)(2,1)S(1)}, bf16[128,2048]{1,0:T(8,128)(2,1)S(1)}, u32[]{:S(2)}, u32[]{:S(2)}) collective-permute-start(bf16[128,2048]{1,0:T(8,128)(2,1)S(1)} %get-tuple-element.31), channel_id=1, source_target_pairs={{0,1},{1,0},{2,3},{3,2},{4,5},{5,4},{6,7},{7,6},{8,9},{9,8},{10,11... | collective-permute-start | bytes 1572872 | tf_op jit(solution)/shard_map/ppermute | solution.py:26
  42.6 9.4 %collective-permute-start.17 = (bf16[128,2048]{1,0:T(8,128)(2,1)S(1)}, bf16[128,2048]{1,0:T(8,128)(2,1)S(1)}, u32[]{:S(2)}, u32[]{:S(2)}) collective-permute-start(bf16[128,2048]{1,0:T(8,128)(2,1)S(1)} %get-tuple-element.32), channel_id=1, source_target_pairs={{0,1},{1,0},{2,3},{3,2},{4,5},{5,4},{6,7},{7,6},{8,9},{9,8},{10,11... | collective-permute-start | bytes 1572872 | tf_op jit(solution)/shard_map/ppermute | solution.py:26
  42.9 9.1 %collective-permute-start.14 = (bf16[128,256]{1,0:T(8,128)(2,1)S(1)}, bf16[128,256]{1,0:T(8,128)(2,1)S(1)}, u32[]{:S(2)}, u32[]{:S(2)}) collective-permute-start(bf16[128,256]{1,0:T(8,128)(2,1)S(1)} %pad_maximum_fusion.1.refs_0_.kv_ref), channel_id=1, source_target_pairs={{0,2},{1,3},{2,0},{3,1},{4,6},{5,7},{6,4},{7,5},{8,10},{9,11},{10,... | collective-permute-start | bytes 196616 | tf_op jit(solution)/shard_map/ppermute | solution.py:26

commit v14 on v13

--- a/solution.py
+++ b/solution.py
@@ -282,12 +282,11 @@
     q_other = swapped(queries, "head", 1)
     g_other = swapped(dout, "head", 1)
     piece = pack(core, positions, keys, values)
+    piece, q_other, g_other = lax.optimization_barrier((piece, q_other, g_other))
     along_z = [piece] + [swapped(piece, "ctx", 2 * s) for s in range(1, half)]
     far_send = column_block(w_query, head ^ 3, share, piece)
     far_mine = column_block(w_query, head ^ 2, share, piece)
-    here_z, q_other, g_other, far_send, far_mine = lax.optimization_barrier(
-        (jnp.stack(along_z), q_other, g_other, far_send, far_mine)
-    )
+    here_z, far_send, far_mine = lax.optimization_barrier((jnp.stack(along_z), far_send, far_mine))
     here_x = swapped(here_z, "ctx", 1)
     far_other = swapped(far_send, "head", 1)
     there_z = swapped(here_z, "head", 1)

time: 53.6 us -> 54.3 us (1.013)
  transfers between devices with their start and end apart: 18 -> 18, of which waited for: 8 -> 9; matrix products, arithmetic and copies ran while one was open for 5% -> 8% of each run, Pallas kernels for 11% -> 11%
where the time goes in v14:
time: 54.3 us; the launch traced here: 54.1 us
  waiting for transfers between devices  23.4 us (43%)
  starting transfers between devices  17.7 us (33%)
  Pallas kernels  8.09 us (15%)
  local copies, waits for them, and re-layouts  3.49 us (6%)
  other arithmetic  1.16 us (2%)
    ppermute x18, waiting for transfers between devices, swapped(): lax.ppermute(value, axis, [(source, source ^ bits) for source in range(co...  23.4 us
    ppermute x18, starting transfers between devices, swapped(): lax.ppermute(value, axis, [(source, source ^ bits) for source in range(co...  17.7 us
    pallas_call x1, Pallas kernels, carve(): pl.pallas_call(carve_kernel, out_shape=[block] * count, in_specs=[SMEM, H...  2.76 us
    dynamic_slice x1, local copies, waits for them, and re-layouts, column_block(): return lax.dynamic_slice_in_dim(w_query, block * share, share, axis=1)  2.71 us
    pallas_call x1, Pallas kernels, attention(): pl.pallas_call(attention_kernel, out_shape=[jax.ShapeDtypeStruct((rows, 2...  2.42 us
    pallas_call x1, Pallas kernels, finish(): pl.pallas_call(finish_kernel, out_shape=jax.ShapeDtypeStruct((rows, share...  1.43 us
  transfers between devices with their start and end apart: 18, of which 9 were waited for; matrix products, arithmetic and copies ran while one was open for 8% of the time, Pallas kernels for 11%

profile of v14, /device:TPU:0, one launch (start us, length us, event | category | flops | bytes accessed | tf_op | source)
XLA Modules:
  0.0 54.1 jit_solution(6378765921374923912)
XLA Ops:
  0.0 0.5 collective-permute-start
  0.5 0.7 %reshape.19 = s32[2,64]{1,0:T(2,128)S(1)} reshape(s32[128]{0:T(128)} %param.12) | data formatting | bytes 1024 | tf_op jit(solution)/shard_map/reshape | solution.py:44
  1.2 0.1 fusion.5
  1.4 0.8 %broadcast_select_fusion = bf16[128,128]{1,0:T(8,128)(2,1)S(1)} fusion(bf16[128,128]{1,0:T(8,128)(2,1)} %param.9, bf16[128,128]{1,0:T(8,128)(2,1)} %param.10, pred[]{:T(512)} %bitcast.3), kind=kLoop, calls=%fused_computation.12 | loop fusion | flops 16384 | bytes 98305 | tf_op jit(solution)/shard_map/jit(_where)/select_n | solution.py:43
  2.2 0.1 pad_maximum_fusion.2
  2.3 3.1 %collective-permute-start.2 = (bf16[144,128]{1,0:T(8,128)(2,1)S(1)}, bf16[144,128]{1,0:T(8,128)(2,1)S(1)}, u32[]{:S(2)}, u32[]{:S(2)}) collective-permute-start(bf16[144,128]{1,0:T(8,128)(2,1)S(1)} %pad_maximum_fusion.2), channel_id=1, source_target_pairs={{0,8},{4,12},{8,0},{12,4},{16,24},{20,28},{24,16},{28,20},{1,9},{5... | collective-permute-start | bytes 110600 | tf_op jit(solution)/shard_map/ppermute | solution.py:26
  5.4 2.6 %collective-permute-start.3 = (bf16[144,128]{1,0:T(8,128)(2,1)S(1)}, bf16[144,128]{1,0:T(8,128)(2,1)S(1)}, u32[]{:S(2)}, u32[]{:S(2)}) collective-permute-start(bf16[144,128]{1,0:T(8,128)(2,1)S(1)} %pad_maximum_fusion.2), channel_id=1, source_target_pairs={{0,16},{4,20},{8,24},{12,28},{16,0},{20,4},{24,8},{28,12},{1,17},{... | collective-permute-start | bytes 110600 | tf_op jit(solution)/shard_map/ppermute | solution.py:26
  8.0 2.7 %constant_dynamic-slice_fusion = (bf16[256,4096]{1,0:T(8,128)(2,1)S(1)}, bf16[256,4096]{1,0:T(8,128)(2,1)S(1)}) fusion(bf16[256,16384]{1,0:T(8,128)(2,1)} %w_ref.2, s32[]{:T(128)S(6)} %select_n.18, s32[]{:T(128)S(6)} %select_n.17), kind=kLoop, calls=%fused_computation.20 | loop fusion | bytes 8388616 | tf_op jit(solution)/shard_map/dynamic_slice | solution.py:51
  10.7 0.3 collective-permute-done.3
  11.0 2.8 %collective-permute-done.4 = bf16[144,128]{1,0:T(8,128)(2,1)S(1)} collective-permute-done((bf16[144,128]{1,0:T(8,128)(2,1)S(1)}, bf16[144,128]{1,0:T(8,128)(2,1)S(1)}, u32[]{:S(2)}, u32[]{:S(2)}) %collective-permute-start.4) | collective-permute-done | bytes 36896 | tf_op jit(solution)/shard_map/ppermute | solution.py:26
  13.9 1.6 %collective-permute-start.6 = (bf16[4,144,128]{2,1,0:T(8,128)(2,1)S(1)}, bf16[4,144,128]{2,1,0:T(8,128)(2,1)S(1)}, u32[]{:S(2)}, u32[]{:S(2)}) collective-permute-start(bf16[4,144,128]{2,1,0:T(8,128)(2,1)S(1)} %pad_maximum_fusion.refs_0_), channel_id=1, source_target_pairs={{0,4},{4,0},{8,12},{12,8},{16,20},{20,16},{24,28},{28,24},{1,5},{5... | collective-permute-start | bytes 442376 | tf_op jit(solution)/shard_map/ppermute | solution.py:26
  15.4 0.2 collective-permute-start.5
  15.6 4.5 %collective-permute-done.6.refs_2_ = bf16[4,144,128]{2,1,0:T(8,128)(2,1)S(1)} collective-permute-done((bf16[4,144,128]{2,1,0:T(8,128)(2,1)S(1)}, bf16[4,144,128]{2,1,0:T(8,128)(2,1)S(1)}, u32[]{:S(2)}, u32[]{:S(2)}) %collective-permute-start.6) | collective-permute-done | bytes 147488 | tf_op jit(solution)/shard_map/ppermute | solution.py:26
  20.1 1.4 %collective-permute-done.7.refs_3_ = bf16[4,144,128]{2,1,0:T(8,128)(2,1)S(1)} collective-permute-done((bf16[4,144,128]{2,1,0:T(8,128)(2,1)S(1)}, bf16[4,144,128]{2,1,0:T(8,128)(2,1)S(1)}, u32[]{:S(2)}, u32[]{:S(2)}) %collective-permute-start.7) | collective-permute-done | bytes 147488 | tf_op jit(solution)/shard_map/ppermute | solution.py:26
  21.5 2.4 %attention.1 = (bf16[128,512]{1,0:T(8,128)(2,1)S(1)}, bf16[8,128,128]{2,1,0:T(8,128)(2,1)S(1)}) custom-call(s32[1]{0:T(128)} %bitcast.core_ref, s32[1,128]{1,0:T(1,128)S(1)} %bitcast.26, s32[1,128]{1,0:T(1,128)S(1)} %bitcast.27, bf16[128,256]{1,0:T(8,128)(2,1)S(1)} %copy-done.1, bf16[128,256]{1,0:T(8,128)(2,1)S(1)} %collective-permute-done.qo_ref, ...), custom_call_target="tpu_custom_call" | custom-call | flops 671088640 | bytes 1048576 | tf_op jit(solution)/shard_map/attention/pallas_call | solution.py:162
  24.0 0.7 %product.1 = bf16[128,4096]{1,0:T(8,128)(2,1)S(1)} custom-call(bf16[128,512]{1,0:T(8,128)(2,1)S(1)} %get-tuple-element.26.dq_ref, bf16[256,4096]{1,0:T(8,128)(2,1)S(1)} %get-tuple-element.27.wm_ref, bf16[256,4096]{1,0:T(8,128)(2,1)S(1)} %collective-permute-done.8.wo_ref), custom_call_target="tpu_custom_call" | custom-call | flops 536870912 | bytes 4194304 | tf_op jit(solution)/shard_map/product/pallas_call | solution.py:193
  24.7 1.6 %collective-permute-start.9 = (bf16[4,128,128]{2,1,0:T(8,128)(2,1)S(1)}, bf16[4,128,128]{2,1,0:T(8,128)(2,1)S(1)}, u32[]{:S(2)}, u32[]{:S(2)}) collective-permute-start(bf16[4,128,128]{2,1,0:T(8,128)(2,1)S(1)} %slice.26), channel_id=1, source_target_pairs={{0,4},{4,0},{8,12},{12,8},{16,20},{20,16},{24,28},{28,24},{1,5},{5... | collective-permute-start | bytes 393224 | tf_op jit(solution)/shard_map/ppermute | solution.py:26
  26.3 1.5 %collective-permute-start.15 = (bf16[128,4096]{1,0:T(8,128)(2,1)S(1)}, bf16[128,4096]{1,0:T(8,128)(2,1)S(1)}, u32[]{:S(2)}, u32[]{:S(2)}) collective-permute-start(bf16[128,4096]{1,0:T(8,128)(2,1)S(1)} %product.1), channel_id=1, source_target_pairs={{0,2},{1,3},{2,0},{3,1},{4,6},{5,7},{6,4},{7,5},{8,10},{9,11},{10,... | collective-permute-start | bytes 3145736 | tf_op jit(solution)/shard_map/ppermute | solution.py:26
  27.8 2.5 %collective-permute-done.9 = bf16[4,128,128]{2,1,0:T(8,128)(2,1)S(1)} collective-permute-done((bf16[4,128,128]{2,1,0:T(8,128)(2,1)S(1)}, bf16[4,128,128]{2,1,0:T(8,128)(2,1)S(1)}, u32[]{:S(2)}, u32[]{:S(2)}) %collective-permute-start.9) | collective-permute-done | bytes 131104 | tf_op jit(solution)/shard_map/ppermute | solution.py:26
  30.5 1.4 %collective-permute-start.11 = (bf16[128,128]{1,0:T(8,128)(2,1)S(1)}, bf16[128,128]{1,0:T(8,128)(2,1)S(1)}, u32[]{:S(2)}, u32[]{:S(2)}) collective-permute-start(bf16[128,128]{1,0:T(8,128)(2,1)S(1)} %get-tuple-element.41), channel_id=1, source_target_pairs={{0,16},{4,20},{8,24},{12,28},{16,0},{20,4},{24,8},{28,12},{1,17},{... | collective-permute-start | bytes 98312 | tf_op jit(solution)/shard_map/ppermute | solution.py:26
  31.8 3.0 %collective-permute-start.12 = (bf16[128,128]{1,0:T(8,128)(2,1)S(1)}, bf16[128,128]{1,0:T(8,128)(2,1)S(1)}, u32[]{:S(2)}, u32[]{:S(2)}) collective-permute-start(bf16[128,128]{1,0:T(8,128)(2,1)S(1)} %get-tuple-element.40), channel_id=1, source_target_pairs={{0,24},{4,28},{8,16},{12,20},{16,8},{20,12},{24,0},{28,4},{1,25},{... | collective-permute-start | bytes 98312 | tf_op jit(solution)/shard_map/ppermute | solution.py:26
  34.8 0.8 %collective-permute-done.11 = bf16[128,128]{1,0:T(8,128)(2,1)S(1)} collective-permute-done((bf16[128,128]{1,0:T(8,128)(2,1)S(1)}, bf16[128,128]{1,0:T(8,128)(2,1)S(1)}, u32[]{:S(2)}, u32[]{:S(2)}) %collective-permute-start.11) | collective-permute-done | bytes 32800 | tf_op jit(solution)/shard_map/ppermute | solution.py:26
  35.7 1.9 %collective-permute-done.12 = bf16[128,128]{1,0:T(8,128)(2,1)S(1)} collective-permute-done((bf16[128,128]{1,0:T(8,128)(2,1)S(1)}, bf16[128,128]{1,0:T(8,128)(2,1)S(1)}, u32[]{:S(2)}, u32[]{:S(2)}) %collective-permute-start.12) | collective-permute-done | bytes 32800 | tf_op jit(solution)/shard_map/ppermute | solution.py:26
  37.6 0.1 pad_add_fusion.block_ref
  37.7 1.1 %collective-permute-done.13 = bf16[128,128]{1,0:T(8,128)(2,1)S(1)} collective-permute-done((bf16[128,128]{1,0:T(8,128)(2,1)S(1)}, bf16[128,128]{1,0:T(8,128)(2,1)S(1)}, u32[]{:S(2)}, u32[]{:S(2)}) %collective-permute-start.13) | collective-permute-done | bytes 32800 | tf_op jit(solution)/shard_map/ppermute | solution.py:26
  38.9 2.8 %carve.1 = (bf16[256,4096]{1,0:T(8,128)(2,1)S(1)}, bf16[256,4096]{1,0:T(8,128)(2,1)S(1)}) custom-call(s32[2]{0:T(128)S(1)} %pad_add_fusion.block_ref, bf16[256,16384]{1,0:T(8,128)(2,1)} %w_ref.2, bf16[128,256]{1,0:T(8,128)(2,1)S(1)} %pad_maximum_fusion.1.refs_0_.kv_ref), custom_call_target="tpu_custom_call" | custom-call | tf_op jit(solution)/shard_map/carve/pallas_call | solution.py:73
  41.6 0.7 %own.1 = (f32[128,4096]{1,0:T(8,128)S(1)}, bf16[128,2048]{1,0:T(8,128)(2,1)S(1)}, bf16[128,2048]{1,0:T(8,128)(2,1)S(1)}) custom-call(bf16[128,512]{1,0:T(8,128)(2,1)S(1)} %get-tuple-element.26.dq_ref, bf16[256,4096]{1,0:T(8,128)(2,1)S(1)} %get-tuple-element.30.wn_ref, bf16[256,4096]{1,0:T(8,128)(2,1)S(1)} %get-tuple-element.31.wo_ref), custom_call_target="tpu_custom_call" | custom-call | tf_op jit(solution)/shard_map/own/pallas_call | solution.py:218
  42.4 0.2 collective-permute-start.16
  42.6 0.3 collective-permute-start.17
  43.0 1.5 %collective-permute-start.14 = (bf16[128,256]{1,0:T(8,128)(2,1)S(1)}, bf16[128,256]{1,0:T(8,128)(2,1)S(1)}, u32[]{:S(2)}, u32[]{:S(2)}) collective-permute-start(bf16[128,256]{1,0:T(8,128)(2,1)S(1)} %pad_maximum_fusion.1.refs_0_.kv_ref), channel_id=1, source_target_pairs={{0,2},{1,3},{2,0},{3,1},{4,6},{5,7},{6,4},{7,5},{8,10},{9,11},{10,... | collective-permute-start | bytes 196616 | tf_op jit(solution)/shard_map/ppermute | solution.py:26
  44.5 8.1 %collective-permute-done.14.kv_far_ref = bf16[128,256]{1,0:T(8,128)(2,1)S(1)} collective-permute-done((bf16[128,256]{1,0:T(8,128)(2,1)S(1)}, bf16[128,256]{1,0:T(8,128)(2,1)S(1)}, u32[]{:S(2)}, u32[]{:S(2)}) %collective-permute-start.14) | collective-permute-done | bytes 65568 | tf_op jit(solution)/shard_map/ppermute | solution.py:26
  52.6 1.4 %finish.1 = bf16[128,4096]{1,0:T(8,128)(2,1)} custom-call(s32[1]{0:T(128)} %bitcast.core_ref, bf16[128,256]{1,0:T(8,128)(2,1)S(1)} %pad_maximum_fusion.1.refs_0_.kv_ref, bf16[128,256]{1,0:T(8,128)(2,1)S(1)} %collective-permute-done.14.kv_far_ref, bf16[256,4096]{1,0:T(8,128)(2,1)S(1)} %copy-done, f32[128,4096]{1,0:T(8,128)S(1)} %get-tuple-element.32.acc_ref, ...), custom_call_target="tpu_custom_call" | custom-call | flops 268435456 | bytes 5242880 | tf_op jit(solution)/shard_map/finish/pallas_call | solution.py:261
  (32 shorter events, 0.5 us)
Async XLA Ops:
  0.0 2.3 %collective-permute-start = (bf16[128,256]{1,0:T(8,128)(2,1)}, bf16[128,256]{1,0:T(8,128)(2,1)S(1)}, u32[]{:S(2)}, u32[]{:S(2)}) collective-permute-start(bf16[128,256]{1,0:T(8,128)(2,1)} %qm_ref.1), channel_id=1, source_target_pairs={{0,1},{1,0},{2,3},{3,2},{4,5},{5,4},{6,7},{7,6},{8,9},{9,8},{10,11... | collective-permute-start | bytes 196616 | tf_op jit(solution)/shard_map/ppermute | solution.py:26
  0.5 1.9 %collective-permute-start.1 = (bf16[128,256]{1,0:T(8,128)(2,1)}, bf16[128,256]{1,0:T(8,128)(2,1)S(1)}, u32[]{:S(2)}, u32[]{:S(2)}) collective-permute-start(bf16[128,256]{1,0:T(8,128)(2,1)} %gm_ref.1), channel_id=1, source_target_pairs={{0,1},{1,0},{2,3},{3,2},{4,5},{5,4},{6,7},{7,6},{8,9},{9,8},{10,11... | collective-permute-start | bytes 196616 | tf_op jit(solution)/shard_map/ppermute | solution.py:26
  2.3 19.2 %copy-start.1 = (bf16[128,256]{1,0:T(8,128)(2,1)S(1)}, bf16[128,256]{1,0:T(8,128)(2,1)}, u32[]{:S(2)}) copy-start(bf16[128,256]{1,0:T(8,128)(2,1)} %qm_ref.1) | copy-start | bytes 196612
  2.3 19.2 %copy-start.2 = (bf16[128,256]{1,0:T(8,128)(2,1)S(1)}, bf16[128,256]{1,0:T(8,128)(2,1)}, u32[]{:S(2)}) copy-start(bf16[128,256]{1,0:T(8,128)(2,1)} %gm_ref.1) | copy-start | bytes 196612
  2.3 19.2 %copy-start.3 = (s32[128]{0:T(128)S(1)}, s32[128]{0:T(128)}, u32[]{:S(2)}) copy-start(s32[128]{0:T(128)} %param.12) | copy-start | bytes 1540
  2.3 19.2 %copy-start.4 = (s32[128]{0:T(128)S(1)}, s32[128]{0:T(128)}, u32[]{:S(2)}) copy-start(s32[128]{0:T(128)} %param.13) | copy-start | bytes 1540
  2.3 8.4 %collective-permute-start.2 = (bf16[144,128]{1,0:T(8,128)(2,1)S(1)}, bf16[144,128]{1,0:T(8,128)(2,1)S(1)}, u32[]{:S(2)}, u32[]{:S(2)}) collective-permute-start(bf16[144,128]{1,0:T(8,128)(2,1)S(1)} %pad_maximum_fusion.2), channel_id=1, source_target_pairs={{0,8},{4,12},{8,0},{12,4},{16,24},{20,28},{24,16},{28,20},{1,9},{5... | collective-permute-start | bytes 110600 | tf_op jit(solution)/shard_map/ppermute | solution.py:26
  5.4 5.6 %collective-permute-start.3 = (bf16[144,128]{1,0:T(8,128)(2,1)S(1)}, bf16[144,128]{1,0:T(8,128)(2,1)S(1)}, u32[]{:S(2)}, u32[]{:S(2)}) collective-permute-start(bf16[144,128]{1,0:T(8,128)(2,1)S(1)} %pad_maximum_fusion.2), channel_id=1, source_target_pairs={{0,16},{4,20},{8,24},{12,28},{16,0},{20,4},{24,8},{28,12},{1,17},{... | collective-permute-start | bytes 110600 | tf_op jit(solution)/shard_map/ppermute | solution.py:26
  8.0 5.8 %collective-permute-start.4 = (bf16[144,128]{1,0:T(8,128)(2,1)S(1)}, bf16[144,128]{1,0:T(8,128)(2,1)S(1)}, u32[]{:S(2)}, u32[]{:S(2)}) collective-permute-start(bf16[144,128]{1,0:T(8,128)(2,1)S(1)} %pad_maximum_fusion.2), channel_id=1, source_target_pairs={{0,24},{4,28},{8,16},{12,20},{16,8},{20,12},{24,0},{28,4},{1,25},{... | collective-permute-start | bytes 110600 | tf_op jit(solution)/shard_map/ppermute | solution.py:26
  13.8 10.2 %collective-permute-start.8 = (bf16[256,4096]{1,0:T(8,128)(2,1)S(1)}, bf16[256,4096]{1,0:T(8,128)(2,1)S(1)}, u32[]{:S(2)}, u32[]{:S(2)}) collective-permute-start(bf16[256,4096]{1,0:T(8,128)(2,1)S(1)} %get-tuple-element.28), channel_id=1, source_target_pairs={{0,1},{1,0},{2,3},{3,2},{4,5},{5,4},{6,7},{7,6},{8,9},{9,8},{10,11... | collective-permute-start | bytes 6291464 | tf_op jit(solution)/shard_map/ppermute | solution.py:26
  13.9 6.3 %collective-permute-start.6 = (bf16[4,144,128]{2,1,0:T(8,128)(2,1)S(1)}, bf16[4,144,128]{2,1,0:T(8,128)(2,1)S(1)}, u32[]{:S(2)}, u32[]{:S(2)}) collective-permute-start(bf16[4,144,128]{2,1,0:T(8,128)(2,1)S(1)} %pad_maximum_fusion.refs_0_), channel_id=1, source_target_pairs={{0,4},{4,0},{8,12},{12,8},{16,20},{20,16},{24,28},{28,24},{1,5},{5... | collective-permute-start | bytes 442376 | tf_op jit(solution)/shard_map/ppermute | solution.py:26
  15.4 4.7 %collective-permute-start.5 = (bf16[4,144,128]{2,1,0:T(8,128)(2,1)S(1)}, bf16[4,144,128]{2,1,0:T(8,128)(2,1)S(1)}, u32[]{:S(2)}, u32[]{:S(2)}) collective-permute-start(bf16[4,144,128]{2,1,0:T(8,128)(2,1)S(1)} %pad_maximum_fusion.refs_0_), channel_id=1, source_target_pairs={{0,1},{1,0},{2,3},{3,2},{4,5},{5,4},{6,7},{7,6},{8,9},{9,8},{10,11... | collective-permute-start | bytes 442376 | tf_op jit(solution)/shard_map/ppermute | solution.py:26
  20.1 1.4 %collective-permute-start.7 = (bf16[4,144,128]{2,1,0:T(8,128)(2,1)S(1)}, bf16[4,144,128]{2,1,0:T(8,128)(2,1)S(1)}, u32[]{:S(2)}, u32[]{:S(2)}) collective-permute-start(bf16[4,144,128]{2,1,0:T(8,128)(2,1)S(1)} %collective-permute-done.6.refs_2_), channel_id=1, source_target_pairs={{0,1},{1,0},{2,3},{3,2},{4,5},{5,4},{6,7},{7,6},{8,9},{9,8},{10,11... | collective-permute-start | bytes 442376 | tf_op jit(solution)/shard_map/ppermute | solution.py:26
  24.7 5.6 %collective-permute-start.9 = (bf16[4,128,128]{2,1,0:T(8,128)(2,1)S(1)}, bf16[4,128,128]{2,1,0:T(8,128)(2,1)S(1)}, u32[]{:S(2)}, u32[]{:S(2)}) collective-permute-start(bf16[4,128,128]{2,1,0:T(8,128)(2,1)S(1)} %slice.26), channel_id=1, source_target_pairs={{0,4},{4,0},{8,12},{12,8},{16,20},{20,16},{24,28},{28,24},{1,5},{5... | collective-permute-start | bytes 393224 | tf_op jit(solution)/shard_map/ppermute | solution.py:26
  26.3 26.3 %collective-permute-start.15 = (bf16[128,4096]{1,0:T(8,128)(2,1)S(1)}, bf16[128,4096]{1,0:T(8,128)(2,1)S(1)}, u32[]{:S(2)}, u32[]{:S(2)}) collective-permute-start(bf16[128,4096]{1,0:T(8,128)(2,1)S(1)} %product.1), channel_id=1, source_target_pairs={{0,2},{1,3},{2,0},{3,1},{4,6},{5,7},{6,4},{7,5},{8,10},{9,11},{10,... | collective-permute-start | bytes 3145736 | tf_op jit(solution)/shard_map/ppermute | solution.py:26
  30.4 4.5 %collective-permute-start.10 = (bf16[128,128]{1,0:T(8,128)(2,1)S(1)}, bf16[128,128]{1,0:T(8,128)(2,1)S(1)}, u32[]{:S(2)}, u32[]{:S(2)}) collective-permute-start(bf16[128,128]{1,0:T(8,128)(2,1)S(1)} %get-tuple-element.39), channel_id=1, source_target_pairs={{0,8},{4,12},{8,0},{12,4},{16,24},{20,28},{24,16},{28,20},{1,9},{5... | collective-permute-start | bytes 98312 | tf_op jit(solution)/shard_map/ppermute | solution.py:26
  30.5 5.2 %collective-permute-start.11 = (bf16[128,128]{1,0:T(8,128)(2,1)S(1)}, bf16[128,128]{1,0:T(8,128)(2,1)S(1)}, u32[]{:S(2)}, u32[]{:S(2)}) collective-permute-start(bf16[128,128]{1,0:T(8,128)(2,1)S(1)} %get-tuple-element.41), channel_id=1, source_target_pairs={{0,16},{4,20},{8,24},{12,28},{16,0},{20,4},{24,8},{28,12},{1,17},{... | collective-permute-start | bytes 98312 | tf_op jit(solution)/shard_map/ppermute | solution.py:26
  31.8 5.7 %collective-permute-start.12 = (bf16[128,128]{1,0:T(8,128)(2,1)S(1)}, bf16[128,128]{1,0:T(8,128)(2,1)S(1)}, u32[]{:S(2)}, u32[]{:S(2)}) collective-permute-start(bf16[128,128]{1,0:T(8,128)(2,1)S(1)} %get-tuple-element.40), channel_id=1, source_target_pairs={{0,24},{4,28},{8,16},{12,20},{16,8},{20,12},{24,0},{28,4},{1,25},{... | collective-permute-start | bytes 98312 | tf_op jit(solution)/shard_map/ppermute | solution.py:26
  37.6 1.3 %collective-permute-start.13 = (bf16[128,128]{1,0:T(8,128)(2,1)S(1)}, bf16[128,128]{1,0:T(8,128)(2,1)S(1)}, u32[]{:S(2)}, u32[]{:S(2)}) collective-permute-start(bf16[128,128]{1,0:T(8,128)(2,1)S(1)} %fusion.3), channel_id=1, source_target_pairs={{0,1},{1,0},{2,3},{3,2},{4,5},{5,4},{6,7},{7,6},{8,9},{9,8},{10,11... | collective-permute-start | bytes 98312 | tf_op jit(solution)/shard_map/ppermute | solution.py:26
  41.6 11.0 %copy-start = (bf16[256,4096]{1,0:T(8,128)(2,1)S(1)}, bf16[256,4096]{1,0:T(8,128)(2,1)}, u32[]{:S(2)}) copy-start(bf16[256,4096]{1,0:T(8,128)(2,1)} %w_ref.3) | copy-start | bytes 6291460
  42.4 10.2 %collective-permute-start.16 = (bf16[128,2048]{1,0:T(8,128)(2,1)S(1)}, bf16[128,2048]{1,0:T(8,128)(2,1)S(1)}, u32[]{:S(2)}, u32[]{:S(2)}) collective-permute-start(bf16[128,2048]{1,0:T(8,128)(2,1)S(1)} %get-tuple-element.33), channel_id=1, source_target_pairs={{0,1},{1,0},{2,3},{3,2},{4,5},{5,4},{6,7},{7,6},{8,9},{9,8},{10,11... | collective-permute-start | bytes 1572872 | tf_op jit(solution)/shard_map/ppermute | solution.py:26
  42.6 10.0 %collective-permute-start.17 = (bf16[128,2048]{1,0:T(8,128)(2,1)S(1)}, bf16[128,2048]{1,0:T(8,128)(2,1)S(1)}, u32[]{:S(2)}, u32[]{:S(2)}) collective-permute-start(bf16[128,2048]{1,0:T(8,128)(2,1)S(1)} %get-tuple-element.34), channel_id=1, source_target_pairs={{0,1},{1,0},{2,3},{3,2},{4,5},{5,4},{6,7},{7,6},{8,9},{9,8},{10,11... | collective-permute-start | bytes 1572872 | tf_op jit(solution)/shard_map/ppermute | solution.py:26
  43.0 9.6 %collective-permute-start.14 = (bf16[128,256]{1,0:T(8,128)(2,1)S(1)}, bf16[128,256]{1,0:T(8,128)(2,1)S(1)}, u32[]{:S(2)}, u32[]{:S(2)}) collective-permute-start(bf16[128,256]{1,0:T(8,128)(2,1)S(1)} %pad_maximum_fusion.1.refs_0_.kv_ref), channel_id=1, source_target_pairs={{0,2},{1,3},{2,0},{3,1},{4,6},{5,7},{6,4},{7,5},{8,10},{9,11},{10,... | collective-permute-start | bytes 196616 | tf_op jit(solution)/shard_map/ppermute | solution.py:26

commit v15 on v14

--- a/solution.py
+++ b/solution.py
@@ -83,10 +83,10 @@
 
 
 def attention_kernel(core_ref, pos_ref, doc_ref, qm_ref, qo_ref, gm_ref, go_ref, *refs):
-    groups = (refs[0:2], refs[2:4])
-    dq_ref, back_ref, s_ref, dp_ref = refs[4:]
+    groups = [refs[i : i + 2] for i in range(0, len(refs) - 4, 2)]
+    dq_ref, back_ref, s_ref, dp_ref = refs[-4:]
     count, rows, size = back_ref.shape
-    half = count // 2
+    part = count // len(groups)
     heads = qm_ref.shape[1] // size
     is_key = core_ref[0] == 0
     inv_root = 1.0 / math.sqrt(size)
@@ -104,7 +104,7 @@
 
     def everywhere(body, state):
         for group, (here_ref, there_ref) in enumerate(groups):
-            state = each(half, lambda s, now: body(s, group * half + s, here_ref, there_ref, now), state)
+            state = each(part, lambda s, now: body(s, group * part + s, here_ref, there_ref, now), state)
         return state
 
     def scores(s, slot, here_ref, there_ref, top):
@@ -119,9 +119,9 @@
             start = meta[run : run + 1, 0:1] * float(RUN)
             pos = offset + start
             allowed = (pos <= last) & (pos >= first)
-            part = jnp.where(allowed, score[run * RUN : (run + 1) * RUN], -1e30)
-            s_ref[slot, run * RUN : (run + 1) * RUN, :] = part
-            top = jnp.maximum(top, jnp.max(part, axis=0, keepdims=True))
+            held = jnp.where(allowed, score[run * RUN : (run + 1) * RUN], -1e30)
+            s_ref[slot, run * RUN : (run + 1) * RUN, :] = held
+            top = jnp.maximum(top, jnp.max(held, axis=0, keepdims=True))
         return top
 
     top = everywhere(scores, jnp.full((1, wide), -1e30, jnp.float32))
@@ -149,15 +149,15 @@
         return dq + dot(key, dscore, ((0,), (0,)))
 
     dq = everywhere(gradients, jnp.zeros((size, wide), jnp.float32)) * inv_root
-    for part in range(wide // rows):
-        block = dq[:, part * rows : (part + 1) * rows]
-        dq_ref[:, part * size : (part + 1) * size] = block.T.astype(jnp.bfloat16)
+    for h in range(wide // rows):
+        block = dq[:, h * rows : (h + 1) * rows]
+        dq_ref[:, h * size : (h + 1) * size] = block.T.astype(jnp.bfloat16)
 
 
 def attention(core, positions, doc_ids, q_mine, q_other, g_mine, g_other, pieces):
-    half, _, size = pieces[0].shape
     rows, width = q_mine.shape
-    count = 2 * half
+    size = pieces[0].shape[2]
+    count = sum(one.shape[0] for one in pieces) // 2
     wide = 2 * rows * (width // size)
     return pl.pallas_call(
         attention_kernel,
@@ -165,7 +165,7 @@
             jax.ShapeDtypeStruct((rows, 2 * width), jnp.bfloat16),
             jax.ShapeDtypeStruct((count, rows, size), jnp.bfloat16),
         ],
-        in_specs=[SMEM] + [pl.BlockSpec()] * 10,
+        in_specs=[SMEM] + [pl.BlockSpec()] * (6 + len(pieces)),
         out_specs=[pl.BlockSpec()] * 2,
         scratch_shapes=[pltpu.VMEM((count, rows, wide), jnp.float32)] * 2,
         compiler_params=params(8 + count * rows * wide // 2**17),
@@ -284,16 +284,21 @@
     piece = pack(core, positions, keys, values)
     piece, q_other, g_other = lax.optimization_barrier((piece, q_other, g_other))
     along_z = [piece] + [swapped(piece, "ctx", 2 * s) for s in range(1, half)]
-    far_send = column_block(w_query, head ^ 3, share, piece)
-    far_mine = column_block(w_query, head ^ 2, share, piece)
-    here_z, far_send, far_mine = lax.optimization_barrier((jnp.stack(along_z), far_send, far_mine))
-    here_x = swapped(here_z, "ctx", 1)
+    early = (half + 1) // 2
+    z_early, z_late = jnp.stack(along_z[:early]), jnp.stack(along_z[early:])
+    x_early = swapped(z_early, "ctx", 1)
+    far_send = column_block(w_query, head ^ 3, share, z_early)
+    far_mine = column_block(w_query, head ^ 2, share, z_early)
+    there_early = swapped(z_early, "head", 1)
+    z_late, x_early, there_early, far_send, far_mine = lax.optimization_barrier(
+        (z_late, x_early, there_early, far_send, far_mine)
+    )
+    x_late = swapped(z_late, "ctx", 1)
     far_other = swapped(far_send, "head", 1)
-    there_z = swapped(here_z, "head", 1)
-    there_x = swapped(here_x, "head", 1)
-    dq, back = attention(
-        core, positions, doc_ids, queries, q_other, dout, g_other, (here_z, there_z, here_x, there_x)
-    )
+    pieces = [z_early, there_early]
+    for here in (z_late, x_early, x_late):
+        pieces += [here, swapped(here, "head", 1)]
+    dq, back = attention(core, positions, doc_ids, queries, q_other, dout, g_other, pieces)
 
     part = product(dq, far_mine, far_other, 0, share, jnp.bfloat16)
     far = swapped(part, "head", 2)

time: 54.3 us -> 52.6 us (0.969)
  waiting for transfers between devices: 23.4 us -> 19.7 us
  starting transfers between devices: 17.7 us -> 19.8 us
    ppermute x18 -> x21, waiting for transfers between devices: 23.4 us -> 19.7 us  [swapped(): lax.ppermute(value, axis, [(source, source ^ bits) for source in range(co...]
    ppermute x18 -> x21, starting transfers between devices: 17.7 us -> 19.8 us  [swapped(): lax.ppermute(value, axis, [(source, source ^ bits) for source in range(co...]
  transfers between devices with their start and end apart: 18 -> 21, of which waited for: 9 -> 8; matrix products, arithmetic and copies ran while one was open for 8% -> 9% of each run, Pallas kernels for 11% -> 11%
where the time goes in v15:
time: 52.6 us; the launch traced here: 52.4 us
  starting transfers between devices  19.8 us (38%)
  waiting for transfers between devices  19.7 us (37%)
  Pallas kernels  8.12 us (15%)
  local copies, waits for them, and re-layouts  3.36 us (6%)
  other arithmetic  1.16 us (2%)
    ppermute x21, starting transfers between devices, swapped(): lax.ppermute(value, axis, [(source, source ^ bits) for source in range(co...  19.8 us
    ppermute x21, waiting for transfers between devices, swapped(): lax.ppermute(value, axis, [(source, source ^ bits) for source in range(co...  19.7 us
    pallas_call x1, Pallas kernels, carve(): pl.pallas_call(carve_kernel, out_shape=[block] * count, in_specs=[SMEM, H...  2.76 us
    dynamic_slice x1, local copies, waits for them, and re-layouts, column_block(): return lax.dynamic_slice_in_dim(w_query, block * share, share, axis=1)  2.58 us
    pallas_call x1, Pallas kernels, attention(): pl.pallas_call(attention_kernel, out_shape=[jax.ShapeDtypeStruct((rows, 2...  2.45 us
    pallas_call x1, Pallas kernels, finish(): pl.pallas_call(finish_kernel, out_shape=jax.ShapeDtypeStruct((rows, share...  1.43 us
  transfers between devices with their start and end apart: 21, of which 8 were waited for; matrix products, arithmetic and copies ran while one was open for 9% of the time, Pallas kernels for 11%

profile of v15, /device:TPU:0, one launch (start us, length us, event | category | flops | bytes accessed | tf_op | source)
XLA Modules:
  0.0 52.4 jit_solution(11161538829707481587)
XLA Ops:
  0.0 0.5 collective-permute-start
  0.5 0.7 %reshape.19 = s32[2,64]{1,0:T(2,128)S(1)} reshape(s32[128]{0:T(128)} %param.12) | data formatting | bytes 1024 | tf_op jit(solution)/shard_map/reshape | solution.py:44
  1.2 0.1 fusion.5
  1.4 0.8 %broadcast_select_fusion = bf16[128,128]{1,0:T(8,128)(2,1)S(1)} fusion(bf16[128,128]{1,0:T(8,128)(2,1)} %param.9, bf16[128,128]{1,0:T(8,128)(2,1)} %param.10, pred[]{:T(512)} %bitcast.3), kind=kLoop, calls=%fused_computation.13 | loop fusion | flops 16384 | bytes 98305 | tf_op jit(solution)/shard_map/jit(_where)/select_n | solution.py:43
  2.2 0.1 pad_maximum_fusion.3
  2.3 3.1 %collective-permute-start.2 = (bf16[144,128]{1,0:T(8,128)(2,1)S(1)}, bf16[144,128]{1,0:T(8,128)(2,1)S(1)}, u32[]{:S(2)}, u32[]{:S(2)}) collective-permute-start(bf16[144,128]{1,0:T(8,128)(2,1)S(1)} %pad_maximum_fusion.3), channel_id=1, source_target_pairs={{0,8},{4,12},{8,0},{12,4},{16,24},{20,28},{24,16},{28,20},{1,9},{5... | collective-permute-start | bytes 110600 | tf_op jit(solution)/shard_map/ppermute | solution.py:26
  5.4 2.6 %collective-permute-start.3 = (bf16[144,128]{1,0:T(8,128)(2,1)S(1)}, bf16[144,128]{1,0:T(8,128)(2,1)S(1)}, u32[]{:S(2)}, u32[]{:S(2)}) collective-permute-start(bf16[144,128]{1,0:T(8,128)(2,1)S(1)} %pad_maximum_fusion.3), channel_id=1, source_target_pairs={{0,16},{4,20},{8,24},{12,28},{16,0},{20,4},{24,8},{28,12},{1,17},{... | collective-permute-start | bytes 110600 | tf_op jit(solution)/shard_map/ppermute | solution.py:26
  8.0 1.8 %collective-permute-start.5 = (bf16[2,144,128]{2,1,0:T(8,128)(2,1)S(1)}, bf16[2,144,128]{2,1,0:T(8,128)(2,1)S(1)}, u32[]{:S(2)}, u32[]{:S(2)}) collective-permute-start(bf16[2,144,128]{2,1,0:T(8,128)(2,1)S(1)} %pad_maximum_fusion.refs_0_), channel_id=1, source_target_pairs={{0,4},{4,0},{8,12},{12,8},{16,20},{20,16},{24,28},{28,24},{1,5},{5... | collective-permute-start | bytes 221192 | tf_op jit(solution)/shard_map/ppermute | solution.py:26
  9.8 2.6 %constant_dynamic-slice_fusion = (bf16[256,4096]{1,0:T(8,128)(2,1)S(1)}, bf16[256,4096]{1,0:T(8,128)(2,1)S(1)}) fusion(bf16[256,16384]{1,0:T(8,128)(2,1)} %w_ref.2, s32[]{:T(128)S(6)} %select_n.18, s32[]{:T(128)S(6)} %select_n.17), kind=kLoop, calls=%fused_computation.21 | loop fusion | bytes 8388616 | tf_op jit(solution)/shard_map/dynamic_slice | solution.py:51
  12.4 1.3 %collective-permute-done.4 = bf16[144,128]{1,0:T(8,128)(2,1)S(1)} collective-permute-done((bf16[144,128]{1,0:T(8,128)(2,1)S(1)}, bf16[144,128]{1,0:T(8,128)(2,1)S(1)}, u32[]{:S(2)}, u32[]{:S(2)}) %collective-permute-start.4) | collective-permute-done | bytes 36896 | tf_op jit(solution)/shard_map/ppermute | solution.py:26
  13.8 1.6 %collective-permute-start.9 = (bf16[2,144,128]{2,1,0:T(8,128)(2,1)S(1)}, bf16[2,144,128]{2,1,0:T(8,128)(2,1)S(1)}, u32[]{:S(2)}, u32[]{:S(2)}) collective-permute-start(bf16[2,144,128]{2,1,0:T(8,128)(2,1)S(1)} %pad_maximum_fusion.1.refs_2_), channel_id=1, source_target_pairs={{0,4},{4,0},{8,12},{12,8},{16,20},{20,16},{24,28},{28,24},{1,5},{5... | collective-permute-start | bytes 221192 | tf_op jit(solution)/shard_map/ppermute | solution.py:26
  15.4 0.2 collective-permute-start.7
  15.5 0.3 collective-permute-start.8
  15.9 2.6 %collective-permute-done.9.refs_6_ = bf16[2,144,128]{2,1,0:T(8,128)(2,1)S(1)} collective-permute-done((bf16[2,144,128]{2,1,0:T(8,128)(2,1)S(1)}, bf16[2,144,128]{2,1,0:T(8,128)(2,1)S(1)}, u32[]{:S(2)}, u32[]{:S(2)}) %collective-permute-start.9) | collective-permute-done | bytes 73760 | tf_op jit(solution)/shard_map/ppermute | solution.py:26
  18.5 1.3 %collective-permute-done.10.refs_7_ = bf16[2,144,128]{2,1,0:T(8,128)(2,1)S(1)} collective-permute-done((bf16[2,144,128]{2,1,0:T(8,128)(2,1)S(1)}, bf16[2,144,128]{2,1,0:T(8,128)(2,1)S(1)}, u32[]{:S(2)}, u32[]{:S(2)}) %collective-permute-start.10) | collective-permute-done | bytes 73760 | tf_op jit(solution)/shard_map/ppermute | solution.py:26
  19.8 2.4 %attention.1 = (bf16[128,512]{1,0:T(8,128)(2,1)S(1)}, bf16[8,128,128]{2,1,0:T(8,128)(2,1)S(1)}) custom-call(s32[1]{0:T(128)} %bitcast.core_ref, s32[1,128]{1,0:T(1,128)S(1)} %bitcast.26, s32[1,128]{1,0:T(1,128)S(1)} %bitcast.27, bf16[128,256]{1,0:T(8,128)(2,1)S(1)} %copy-done.1, bf16[128,256]{1,0:T(8,128)(2,1)S(1)} %collective-permute-done.qo_ref, ...), custom_call_target="tpu_custom_call" | custom-call | flops 671088640 | bytes 1048576 | tf_op jit(solution)/shard_map/attention/pallas_call | solution.py:162
  22.3 0.7 %product.1 = bf16[128,4096]{1,0:T(8,128)(2,1)S(1)} custom-call(bf16[128,512]{1,0:T(8,128)(2,1)S(1)} %get-tuple-element.30.dq_ref, bf16[256,4096]{1,0:T(8,128)(2,1)S(1)} %get-tuple-element.31.wm_ref, bf16[256,4096]{1,0:T(8,128)(2,1)S(1)} %collective-permute-done.11.wo_ref), custom_call_target="tpu_custom_call" | custom-call | flops 536870912 | bytes 4194304 | tf_op jit(solution)/shard_map/product/pallas_call | solution.py:193
  23.0 1.6 %collective-permute-start.12 = (bf16[4,128,128]{2,1,0:T(8,128)(2,1)S(1)}, bf16[4,128,128]{2,1,0:T(8,128)(2,1)S(1)}, u32[]{:S(2)}, u32[]{:S(2)}) collective-permute-start(bf16[4,128,128]{2,1,0:T(8,128)(2,1)S(1)} %slice.26), channel_id=1, source_target_pairs={{0,4},{4,0},{8,12},{12,8},{16,20},{20,16},{24,28},{28,24},{1,5},{5... | collective-permute-start | bytes 393224 | tf_op jit(solution)/shard_map/ppermute | solution.py:26
  24.6 1.5 %collective-permute-start.18 = (bf16[128,4096]{1,0:T(8,128)(2,1)S(1)}, bf16[128,4096]{1,0:T(8,128)(2,1)S(1)}, u32[]{:S(2)}, u32[]{:S(2)}) collective-permute-start(bf16[128,4096]{1,0:T(8,128)(2,1)S(1)} %product.1), channel_id=1, source_target_pairs={{0,2},{1,3},{2,0},{3,1},{4,6},{5,7},{6,4},{7,5},{8,10},{9,11},{10,... | collective-permute-start | bytes 3145736 | tf_op jit(solution)/shard_map/ppermute | solution.py:26
  26.1 2.5 %collective-permute-done.12 = bf16[4,128,128]{2,1,0:T(8,128)(2,1)S(1)} collective-permute-done((bf16[4,128,128]{2,1,0:T(8,128)(2,1)S(1)}, bf16[4,128,128]{2,1,0:T(8,128)(2,1)S(1)}, u32[]{:S(2)}, u32[]{:S(2)}) %collective-permute-start.12) | collective-permute-done | bytes 131104 | tf_op jit(solution)/shard_map/ppermute | solution.py:26
  28.8 3.0 %collective-permute-start.14 = (bf16[128,128]{1,0:T(8,128)(2,1)S(1)}, bf16[128,128]{1,0:T(8,128)(2,1)S(1)}, u32[]{:S(2)}, u32[]{:S(2)}) collective-permute-start(bf16[128,128]{1,0:T(8,128)(2,1)S(1)} %get-tuple-element.45), channel_id=1, source_target_pairs={{0,16},{4,20},{8,24},{12,28},{16,0},{20,4},{24,8},{28,12},{1,17},{... | collective-permute-start | bytes 98312 | tf_op jit(solution)/shard_map/ppermute | solution.py:26
  31.8 1.4 %collective-permute-start.15 = (bf16[128,128]{1,0:T(8,128)(2,1)S(1)}, bf16[128,128]{1,0:T(8,128)(2,1)S(1)}, u32[]{:S(2)}, u32[]{:S(2)}) collective-permute-start(bf16[128,128]{1,0:T(8,128)(2,1)S(1)} %get-tuple-element.44), channel_id=1, source_target_pairs={{0,24},{4,28},{8,16},{12,20},{16,8},{20,12},{24,0},{28,4},{1,25},{... | collective-permute-start | bytes 98312 | tf_op jit(solution)/shard_map/ppermute | solution.py:26
  33.1 0.7 %collective-permute-done.14 = bf16[128,128]{1,0:T(8,128)(2,1)S(1)} collective-permute-done((bf16[128,128]{1,0:T(8,128)(2,1)S(1)}, bf16[128,128]{1,0:T(8,128)(2,1)S(1)}, u32[]{:S(2)}, u32[]{:S(2)}) %collective-permute-start.14) | collective-permute-done | bytes 32800 | tf_op jit(solution)/shard_map/ppermute | solution.py:26
  33.9 3.6 %collective-permute-done.15 = bf16[128,128]{1,0:T(8,128)(2,1)S(1)} collective-permute-done((bf16[128,128]{1,0:T(8,128)(2,1)S(1)}, bf16[128,128]{1,0:T(8,128)(2,1)S(1)}, u32[]{:S(2)}, u32[]{:S(2)}) %collective-permute-start.15) | collective-permute-done | bytes 32800 | tf_op jit(solution)/shard_map/ppermute | solution.py:26
  37.7 1.1 %collective-permute-done.16 = bf16[128,128]{1,0:T(8,128)(2,1)S(1)} collective-permute-done((bf16[128,128]{1,0:T(8,128)(2,1)S(1)}, bf16[128,128]{1,0:T(8,128)(2,1)S(1)}, u32[]{:S(2)}, u32[]{:S(2)}) %collective-permute-start.16) | collective-permute-done | bytes 32800 | tf_op jit(solution)/shard_map/ppermute | solution.py:26
  38.8 2.8 %carve.1 = (bf16[256,4096]{1,0:T(8,128)(2,1)S(1)}, bf16[256,4096]{1,0:T(8,128)(2,1)S(1)}) custom-call(s32[2]{0:T(128)S(1)} %pad_add_fusion.block_ref, bf16[256,16384]{1,0:T(8,128)(2,1)} %w_ref.2, bf16[128,256]{1,0:T(8,128)(2,1)S(1)} %pad_maximum_fusion.2.refs_0_.kv_ref), custom_call_target="tpu_custom_call" | custom-call | tf_op jit(solution)/shard_map/carve/pallas_call | solution.py:73
  41.6 0.7 %own.1 = (f32[128,4096]{1,0:T(8,128)S(1)}, bf16[128,2048]{1,0:T(8,128)(2,1)S(1)}, bf16[128,2048]{1,0:T(8,128)(2,1)S(1)}) custom-call(bf16[128,512]{1,0:T(8,128)(2,1)S(1)} %get-tuple-element.30.dq_ref, bf16[256,4096]{1,0:T(8,128)(2,1)S(1)} %get-tuple-element.34.wn_ref, bf16[256,4096]{1,0:T(8,128)(2,1)S(1)} %get-tuple-element.35.wo_ref), custom_call_target="tpu_custom_call" | custom-call | tf_op jit(solution)/shard_map/own/pallas_call | solution.py:218
  42.3 0.2 collective-permute-start.19
  42.6 0.3 collective-permute-start.20
  42.9 1.5 %collective-permute-start.17 = (bf16[128,256]{1,0:T(8,128)(2,1)S(1)}, bf16[128,256]{1,0:T(8,128)(2,1)S(1)}, u32[]{:S(2)}, u32[]{:S(2)}) collective-permute-start(bf16[128,256]{1,0:T(8,128)(2,1)S(1)} %pad_maximum_fusion.2.refs_0_.kv_ref), channel_id=1, source_target_pairs={{0,2},{1,3},{2,0},{3,1},{4,6},{5,7},{6,4},{7,5},{8,10},{9,11},{10,... | collective-permute-start | bytes 196616 | tf_op jit(solution)/shard_map/ppermute | solution.py:26
  44.4 6.5 %collective-permute-done.17.kv_far_ref = bf16[128,256]{1,0:T(8,128)(2,1)S(1)} collective-permute-done((bf16[128,256]{1,0:T(8,128)(2,1)S(1)}, bf16[128,256]{1,0:T(8,128)(2,1)S(1)}, u32[]{:S(2)}, u32[]{:S(2)}) %collective-permute-start.17) | collective-permute-done | bytes 65568 | tf_op jit(solution)/shard_map/ppermute | solution.py:26
  50.9 1.4 %finish.1 = bf16[128,4096]{1,0:T(8,128)(2,1)} custom-call(s32[1]{0:T(128)} %bitcast.core_ref, bf16[128,256]{1,0:T(8,128)(2,1)S(1)} %pad_maximum_fusion.2.refs_0_.kv_ref, bf16[128,256]{1,0:T(8,128)(2,1)S(1)} %collective-permute-done.17.kv_far_ref, bf16[256,4096]{1,0:T(8,128)(2,1)S(1)} %copy-done, f32[128,4096]{1,0:T(8,128)S(1)} %get-tuple-element.36.acc_ref, ...), custom_call_target="tpu_custom_call" | custom-call | flops 268435456 | bytes 5242880 | tf_op jit(solution)/shard_map/finish/pallas_call | solution.py:261
  (39 shorter events, 0.5 us)
Async XLA Ops:
  0.0 2.2 %collective-permute-start = (bf16[128,256]{1,0:T(8,128)(2,1)}, bf16[128,256]{1,0:T(8,128)(2,1)S(1)}, u32[]{:S(2)}, u32[]{:S(2)}) collective-permute-start(bf16[128,256]{1,0:T(8,128)(2,1)} %qm_ref.1), channel_id=1, source_target_pairs={{0,1},{1,0},{2,3},{3,2},{4,5},{5,4},{6,7},{7,6},{8,9},{9,8},{10,11... | collective-permute-start | bytes 196616 | tf_op jit(solution)/shard_map/ppermute | solution.py:26
  0.5 1.8 %collective-permute-start.1 = (bf16[128,256]{1,0:T(8,128)(2,1)}, bf16[128,256]{1,0:T(8,128)(2,1)S(1)}, u32[]{:S(2)}, u32[]{:S(2)}) collective-permute-start(bf16[128,256]{1,0:T(8,128)(2,1)} %gm_ref.1), channel_id=1, source_target_pairs={{0,1},{1,0},{2,3},{3,2},{4,5},{5,4},{6,7},{7,6},{8,9},{9,8},{10,11... | collective-permute-start | bytes 196616 | tf_op jit(solution)/shard_map/ppermute | solution.py:26
  2.3 5.7 %collective-permute-start.2 = (bf16[144,128]{1,0:T(8,128)(2,1)S(1)}, bf16[144,128]{1,0:T(8,128)(2,1)S(1)}, u32[]{:S(2)}, u32[]{:S(2)}) collective-permute-start(bf16[144,128]{1,0:T(8,128)(2,1)S(1)} %pad_maximum_fusion.3), channel_id=1, source_target_pairs={{0,8},{4,12},{8,0},{12,4},{16,24},{20,28},{24,16},{28,20},{1,9},{5... | collective-permute-start | bytes 110600 | tf_op jit(solution)/shard_map/ppermute | solution.py:26
  5.4 7.0 %collective-permute-start.3 = (bf16[144,128]{1,0:T(8,128)(2,1)S(1)}, bf16[144,128]{1,0:T(8,128)(2,1)S(1)}, u32[]{:S(2)}, u32[]{:S(2)}) collective-permute-start(bf16[144,128]{1,0:T(8,128)(2,1)S(1)} %pad_maximum_fusion.3), channel_id=1, source_target_pairs={{0,16},{4,20},{8,24},{12,28},{16,0},{20,4},{24,8},{28,12},{1,17},{... | collective-permute-start | bytes 110600 | tf_op jit(solution)/shard_map/ppermute | solution.py:26
  7.9 5.8 %collective-permute-start.4 = (bf16[144,128]{1,0:T(8,128)(2,1)S(1)}, bf16[144,128]{1,0:T(8,128)(2,1)S(1)}, u32[]{:S(2)}, u32[]{:S(2)}) collective-permute-start(bf16[144,128]{1,0:T(8,128)(2,1)S(1)} %pad_maximum_fusion.3), channel_id=1, source_target_pairs={{0,24},{4,28},{8,16},{12,20},{16,8},{20,12},{24,0},{28,4},{1,25},{... | collective-permute-start | bytes 110600 | tf_op jit(solution)/shard_map/ppermute | solution.py:26
  8.0 11.8 %copy-start.1 = (bf16[128,256]{1,0:T(8,128)(2,1)S(1)}, bf16[128,256]{1,0:T(8,128)(2,1)}, u32[]{:S(2)}) copy-start(bf16[128,256]{1,0:T(8,128)(2,1)} %qm_ref.1) | copy-start | bytes 196612
  8.0 11.8 %copy-start.2 = (bf16[128,256]{1,0:T(8,128)(2,1)S(1)}, bf16[128,256]{1,0:T(8,128)(2,1)}, u32[]{:S(2)}) copy-start(bf16[128,256]{1,0:T(8,128)(2,1)} %gm_ref.1) | copy-start | bytes 196612
  8.0 11.8 %copy-start.3 = (s32[128]{0:T(128)S(1)}, s32[128]{0:T(128)}, u32[]{:S(2)}) copy-start(s32[128]{0:T(128)} %param.12) | copy-start | bytes 1540
  8.0 11.8 %copy-start.4 = (s32[128]{0:T(128)S(1)}, s32[128]{0:T(128)}, u32[]{:S(2)}) copy-start(s32[128]{0:T(128)} %param.13) | copy-start | bytes 1540
  8.0 5.7 %collective-permute-start.5 = (bf16[2,144,128]{2,1,0:T(8,128)(2,1)S(1)}, bf16[2,144,128]{2,1,0:T(8,128)(2,1)S(1)}, u32[]{:S(2)}, u32[]{:S(2)}) collective-permute-start(bf16[2,144,128]{2,1,0:T(8,128)(2,1)S(1)} %pad_maximum_fusion.refs_0_), channel_id=1, source_target_pairs={{0,4},{4,0},{8,12},{12,8},{16,20},{20,16},{24,28},{28,24},{1,5},{5... | collective-permute-start | bytes 221192 | tf_op jit(solution)/shard_map/ppermute | solution.py:26
  9.8 3.9 %collective-permute-start.6 = (bf16[2,144,128]{2,1,0:T(8,128)(2,1)S(1)}, bf16[2,144,128]{2,1,0:T(8,128)(2,1)S(1)}, u32[]{:S(2)}, u32[]{:S(2)}) collective-permute-start(bf16[2,144,128]{2,1,0:T(8,128)(2,1)S(1)} %pad_maximum_fusion.refs_0_), channel_id=1, source_target_pairs={{0,1},{1,0},{2,3},{3,2},{4,5},{5,4},{6,7},{7,6},{8,9},{9,8},{10,11... | collective-permute-start | bytes 221192 | tf_op jit(solution)/shard_map/ppermute | solution.py:26
  13.7 8.5 %collective-permute-start.11 = (bf16[256,4096]{1,0:T(8,128)(2,1)S(1)}, bf16[256,4096]{1,0:T(8,128)(2,1)S(1)}, u32[]{:S(2)}, u32[]{:S(2)}) collective-permute-start(bf16[256,4096]{1,0:T(8,128)(2,1)S(1)} %get-tuple-element.32), channel_id=1, source_target_pairs={{0,1},{1,0},{2,3},{3,2},{4,5},{5,4},{6,7},{7,6},{8,9},{9,8},{10,11... | collective-permute-start | bytes 6291464 | tf_op jit(solution)/shard_map/ppermute | solution.py:26
  13.8 4.7 %collective-permute-start.9 = (bf16[2,144,128]{2,1,0:T(8,128)(2,1)S(1)}, bf16[2,144,128]{2,1,0:T(8,128)(2,1)S(1)}, u32[]{:S(2)}, u32[]{:S(2)}) collective-permute-start(bf16[2,144,128]{2,1,0:T(8,128)(2,1)S(1)} %pad_maximum_fusion.1.refs_2_), channel_id=1, source_target_pairs={{0,4},{4,0},{8,12},{12,8},{16,20},{20,16},{24,28},{28,24},{1,5},{5... | collective-permute-start | bytes 221192 | tf_op jit(solution)/shard_map/ppermute | solution.py:26
  15.4 3.1 %collective-permute-start.7 = (bf16[2,144,128]{2,1,0:T(8,128)(2,1)S(1)}, bf16[2,144,128]{2,1,0:T(8,128)(2,1)S(1)}, u32[]{:S(2)}, u32[]{:S(2)}) collective-permute-start(bf16[2,144,128]{2,1,0:T(8,128)(2,1)S(1)} %pad_maximum_fusion.1.refs_2_), channel_id=1, source_target_pairs={{0,1},{1,0},{2,3},{3,2},{4,5},{5,4},{6,7},{7,6},{8,9},{9,8},{10,11... | collective-permute-start | bytes 221192 | tf_op jit(solution)/shard_map/ppermute | solution.py:26
  15.5 3.0 %collective-permute-start.8 = (bf16[2,144,128]{2,1,0:T(8,128)(2,1)S(1)}, bf16[2,144,128]{2,1,0:T(8,128)(2,1)S(1)}, u32[]{:S(2)}, u32[]{:S(2)}) collective-permute-start(bf16[2,144,128]{2,1,0:T(8,128)(2,1)S(1)} %collective-permute-done.5.refs_4_), channel_id=1, source_target_pairs={{0,1},{1,0},{2,3},{3,2},{4,5},{5,4},{6,7},{7,6},{8,9},{9,8},{10,11... | collective-permute-start | bytes 221192 | tf_op jit(solution)/shard_map/ppermute | solution.py:26
  18.5 1.3 %collective-permute-start.10 = (bf16[2,144,128]{2,1,0:T(8,128)(2,1)S(1)}, bf16[2,144,128]{2,1,0:T(8,128)(2,1)S(1)}, u32[]{:S(2)}, u32[]{:S(2)}) collective-permute-start(bf16[2,144,128]{2,1,0:T(8,128)(2,1)S(1)} %collective-permute-done.9.refs_6_), channel_id=1, source_target_pairs={{0,1},{1,0},{2,3},{3,2},{4,5},{5,4},{6,7},{7,6},{8,9},{9,8},{10,11... | collective-permute-start | bytes 221192 | tf_op jit(solution)/shard_map/ppermute | solution.py:26
  23.0 5.6 %collective-permute-start.12 = (bf16[4,128,128]{2,1,0:T(8,128)(2,1)S(1)}, bf16[4,128,128]{2,1,0:T(8,128)(2,1)S(1)}, u32[]{:S(2)}, u32[]{:S(2)}) collective-permute-start(bf16[4,128,128]{2,1,0:T(8,128)(2,1)S(1)} %slice.26), channel_id=1, source_target_pairs={{0,4},{4,0},{8,12},{12,8},{16,20},{20,16},{24,28},{28,24},{1,5},{5... | collective-permute-start | bytes 393224 | tf_op jit(solution)/shard_map/ppermute | solution.py:26
  24.6 26.3 %collective-permute-start.18 = (bf16[128,4096]{1,0:T(8,128)(2,1)S(1)}, bf16[128,4096]{1,0:T(8,128)(2,1)S(1)}, u32[]{:S(2)}, u32[]{:S(2)}) collective-permute-start(bf16[128,4096]{1,0:T(8,128)(2,1)S(1)} %product.1), channel_id=1, source_target_pairs={{0,2},{1,3},{2,0},{3,1},{4,6},{5,7},{6,4},{7,5},{8,10},{9,11},{10,... | collective-permute-start | bytes 3145736 | tf_op jit(solution)/shard_map/ppermute | solution.py:26
  28.7 4.5 %collective-permute-start.13 = (bf16[128,128]{1,0:T(8,128)(2,1)S(1)}, bf16[128,128]{1,0:T(8,128)(2,1)S(1)}, u32[]{:S(2)}, u32[]{:S(2)}) collective-permute-start(bf16[128,128]{1,0:T(8,128)(2,1)S(1)} %get-tuple-element.43), channel_id=1, source_target_pairs={{0,8},{4,12},{8,0},{12,4},{16,24},{20,28},{24,16},{28,20},{1,9},{5... | collective-permute-start | bytes 98312 | tf_op jit(solution)/shard_map/ppermute | solution.py:26
  28.8 5.1 %collective-permute-start.14 = (bf16[128,128]{1,0:T(8,128)(2,1)S(1)}, bf16[128,128]{1,0:T(8,128)(2,1)S(1)}, u32[]{:S(2)}, u32[]{:S(2)}) collective-permute-start(bf16[128,128]{1,0:T(8,128)(2,1)S(1)} %get-tuple-element.45), channel_id=1, source_target_pairs={{0,16},{4,20},{8,24},{12,28},{16,0},{20,4},{24,8},{28,12},{1,17},{... | collective-permute-start | bytes 98312 | tf_op jit(solution)/shard_map/ppermute | solution.py:26
  31.8 5.7 %collective-permute-start.15 = (bf16[128,128]{1,0:T(8,128)(2,1)S(1)}, bf16[128,128]{1,0:T(8,128)(2,1)S(1)}, u32[]{:S(2)}, u32[]{:S(2)}) collective-permute-start(bf16[128,128]{1,0:T(8,128)(2,1)S(1)} %get-tuple-element.44), channel_id=1, source_target_pairs={{0,24},{4,28},{8,16},{12,20},{16,8},{20,12},{24,0},{28,4},{1,25},{... | collective-permute-start | bytes 98312 | tf_op jit(solution)/shard_map/ppermute | solution.py:26
  37.5 1.3 %collective-permute-start.16 = (bf16[128,128]{1,0:T(8,128)(2,1)S(1)}, bf16[128,128]{1,0:T(8,128)(2,1)S(1)}, u32[]{:S(2)}, u32[]{:S(2)}) collective-permute-start(bf16[128,128]{1,0:T(8,128)(2,1)S(1)} %fusion.3), channel_id=1, source_target_pairs={{0,1},{1,0},{2,3},{3,2},{4,5},{5,4},{6,7},{7,6},{8,9},{9,8},{10,11... | collective-permute-start | bytes 98312 | tf_op jit(solution)/shard_map/ppermute | solution.py:26
  41.6 9.3 %copy-start = (bf16[256,4096]{1,0:T(8,128)(2,1)S(1)}, bf16[256,4096]{1,0:T(8,128)(2,1)}, u32[]{:S(2)}) copy-start(bf16[256,4096]{1,0:T(8,128)(2,1)} %w_ref.3) | copy-start | bytes 6291460
  42.3 8.6 %collective-permute-start.19 = (bf16[128,2048]{1,0:T(8,128)(2,1)S(1)}, bf16[128,2048]{1,0:T(8,128)(2,1)S(1)}, u32[]{:S(2)}, u32[]{:S(2)}) collective-permute-start(bf16[128,2048]{1,0:T(8,128)(2,1)S(1)} %get-tuple-element.37), channel_id=1, source_target_pairs={{0,1},{1,0},{2,3},{3,2},{4,5},{5,4},{6,7},{7,6},{8,9},{9,8},{10,11... | collective-permute-start | bytes 1572872 | tf_op jit(solution)/shard_map/ppermute | solution.py:26
  42.6 8.3 %collective-permute-start.20 = (bf16[128,2048]{1,0:T(8,128)(2,1)S(1)}, bf16[128,2048]{1,0:T(8,128)(2,1)S(1)}, u32[]{:S(2)}, u32[]{:S(2)}) collective-permute-start(bf16[128,2048]{1,0:T(8,128)(2,1)S(1)} %get-tuple-element.38), channel_id=1, source_target_pairs={{0,1},{1,0},{2,3},{3,2},{4,5},{5,4},{6,7},{7,6},{8,9},{9,8},{10,11... | collective-permute-start | bytes 1572872 | tf_op jit(solution)/shard_map/ppermute | solution.py:26
  42.9 8.0 %collective-permute-start.17 = (bf16[128,256]{1,0:T(8,128)(2,1)S(1)}, bf16[128,256]{1,0:T(8,128)(2,1)S(1)}, u32[]{:S(2)}, u32[]{:S(2)}) collective-permute-start(bf16[128,256]{1,0:T(8,128)(2,1)S(1)} %pad_maximum_fusion.2.refs_0_.kv_ref), channel_id=1, source_target_pairs={{0,2},{1,3},{2,0},{3,1},{4,6},{5,7},{6,4},{7,5},{8,10},{9,11},{10,... | collective-permute-start | bytes 196616 | tf_op jit(solution)/shard_map/ppermute | solution.py:26

commit v16 on v15

--- a/solution.py
+++ b/solution.py
@@ -11,6 +11,7 @@
 RUN = 64
 META_ROWS = 16
 TILES = 4
+HALVES = 2
 GIVES = 2
 ANY = pl.BlockSpec(memory_space=pl.ANY)
 HBM = pl.BlockSpec(memory_space=pltpu.HBM)
@@ -180,27 +181,31 @@
     )
 
 
-def product_kernel(first, dq_ref, wm_ref, wo_ref, out_ref):
-    depth = wm_ref.shape[0]
-    at = slice(first, first + out_ref.shape[1])
-    acc = dot(dq_ref[:, 0:depth], wm_ref[:, at], ((1,), (0,)))
-    acc = acc + dot(dq_ref[:, depth:], wo_ref[:, at], ((1,), (0,)))
-    out_ref[...] = acc.astype(out_ref.dtype)
-
-
-def product(dq, w_mine, w_other, first, width, dtype):
+def product_kernel(dq_ref, wm_ref, *refs):
+    others, out_ref = refs[:-1], refs[-1]
+    depth, share = wm_ref.shape
+    width = share // len(others)
+    for i, wo_ref in enumerate(others):
+        at = slice(i * width, (i + 1) * width)
+        acc = dot(dq_ref[:, 0:depth], wm_ref[:, at], ((1,), (0,)))
+        acc = acc + dot(dq_ref[:, depth:], wo_ref[...], ((1,), (0,)))
+        out_ref[:, at] = acc.astype(out_ref.dtype)
+
+
+def product(dq, w_mine, w_other, dtype):
     rows, depth = dq.shape
-    return pl.pallas_call(
-        functools.partial(product_kernel, first),
-        out_shape=jax.ShapeDtypeStruct((rows, width), dtype),
-        in_specs=[pl.BlockSpec()] * 3,
+    share = w_mine.shape[1]
+    return pl.pallas_call(
+        product_kernel,
+        out_shape=jax.ShapeDtypeStruct((rows, share), dtype),
+        in_specs=[pl.BlockSpec()] * (2 + len(w_other)),
         out_specs=pl.BlockSpec(),
         compiler_params=params(),
         cost_estimate=pl.CostEstimate(
-            flops=2 * rows * depth * width, bytes_accessed=2 * depth * width, transcendentals=0
+            flops=2 * rows * depth * share, bytes_accessed=2 * depth * share, transcendentals=0
         ),
         name="product",
-    )(dq, w_mine, w_other)
+    )(dq, w_mine, *w_other)
 
 
 def own_kernel(dq_ref, wn_ref, wo_ref, acc_ref, *give_refs):
@@ -287,20 +292,23 @@
     early = (half + 1) // 2
     z_early, z_late = jnp.stack(along_z[:early]), jnp.stack(along_z[early:])
     x_early = swapped(z_early, "ctx", 1)
-    far_send = column_block(w_query, head ^ 3, share, z_early)
-    far_mine = column_block(w_query, head ^ 2, share, z_early)
     there_early = swapped(z_early, "head", 1)
-    z_late, x_early, there_early, far_send, far_mine = lax.optimization_barrier(
-        (z_late, x_early, there_early, far_send, far_mine)
-    )
+    z_late, x_early, there_early = lax.optimization_barrier((z_late, x_early, there_early))
     x_late = swapped(z_late, "ctx", 1)
-    far_other = swapped(far_send, "head", 1)
+    far_send = [column_block(w_query, (head ^ 3) * HALVES + i, share // HALVES, z_late) for i in range(HALVES)]
+    far_mine = column_block(w_query, head ^ 2, share, z_late)
     pieces = [z_early, there_early]
-    for here in (z_late, x_early, x_late):
+    for here in (z_late, x_early):
         pieces += [here, swapped(here, "head", 1)]
+    x_late, far_mine, *rest = lax.optimization_barrier((x_late, far_mine, *far_send, *pieces))
+    far_send, pieces = rest[:HALVES], rest[HALVES:]
+    pieces += [x_late, swapped(x_late, "head", 1)]
+    far_other = [swapped(one, "head", 1) for one in far_send[:1]]
+    pieces[-1], *rest = lax.optimization_barrier((pieces[-1], *far_send[1:]))
+    far_other += [swapped(one, "head", 1) for one in rest]
     dq, back = attention(core, positions, doc_ids, queries, q_other, dout, g_other, pieces)
 
-    part = product(dq, far_mine, far_other, 0, share, jnp.bfloat16)
+    part = product(dq, far_mine, far_other, jnp.bfloat16)
     far = swapped(part, "head", 2)
 
     back, part = lax.optimization_barrier((back, part))

time: 52.6 us -> 53.2 us (1.011)
  local copies, waits for them, and re-layouts: 3.36 us -> 4.24 us
    dynamic_slice x1 -> x2, local copies, waits for them, and re-layouts: 2.58 us -> 3.45 us  [column_block(): return lax.dynamic_slice_in_dim(w_query, block * share, share, axis=1)]
    ppermute x21 -> x22, starting transfers between devices: 19.8 us -> 19.5 us  [swapped(): lax.ppermute(value, axis, [(source, source ^ bits) for source in range(co...]
    ppermute x21 -> x22, waiting for transfers between devices: 19.7 us -> 19.9 us  [swapped(): lax.ppermute(value, axis, [(source, source ^ bits) for source in range(co...]
  transfers between devices with their start and end apart: 21 -> 22, of which waited for: 8 -> 9; matrix products, arithmetic and copies ran while one was open for 9% -> 10% of each run, Pallas kernels for 11% -> 11%
where the time goes in v16:
time: 53.2 us; the launch traced here: 53 us
  waiting for transfers between devices  19.9 us (37%)
  starting transfers between devices  19.5 us (37%)
  Pallas kernels  7.94 us (15%)
  local copies, waits for them, and re-layouts  4.24 us (8%)
  other arithmetic  1.16 us (2%)
    ppermute x22, waiting for transfers between devices, swapped(): lax.ppermute(value, axis, [(source, source ^ bits) for source in range(co...  19.9 us
    ppermute x22, starting transfers between devices, swapped(): lax.ppermute(value, axis, [(source, source ^ bits) for source in range(co...  19.5 us
    dynamic_slice x2, local copies, waits for them, and re-layouts, column_block(): return lax.dynamic_slice_in_dim(w_query, block * share, share, axis=1)  3.45 us
    pallas_call x1, Pallas kernels, carve(): pl.pallas_call(carve_kernel, out_shape=[block] * count, in_specs=[SMEM, H...  2.76 us
    pallas_call x1, Pallas kernels, attention(): pl.pallas_call(attention_kernel, out_shape=[jax.ShapeDtypeStruct((rows, 2...  2.42 us
    pallas_call x1, Pallas kernels, finish(): pl.pallas_call(finish_kernel, out_shape=jax.ShapeDtypeStruct((rows, share...  1.32 us
  transfers between devices with their start and end apart: 22, of which 9 were waited for; matrix products, arithmetic and copies ran while one was open for 10% of the time, Pallas kernels for 11%

profile of v16, /device:TPU:0, one launch (start us, length us, event | category | flops | bytes accessed | tf_op | source)
XLA Modules:
  0.0 53.0 jit_solution(5232410676124172473)
XLA Ops:
  0.0 0.5 collective-permute-start
  0.5 0.7 %reshape.19 = s32[2,64]{1,0:T(2,128)S(1)} reshape(s32[128]{0:T(128)} %param.12) | data formatting | bytes 1024 | tf_op jit(solution)/shard_map/reshape | solution.py:45
  1.4 0.8 %broadcast_select_fusion = bf16[128,128]{1,0:T(8,128)(2,1)S(1)} fusion(bf16[128,128]{1,0:T(8,128)(2,1)} %param.9, bf16[128,128]{1,0:T(8,128)(2,1)} %param.10, pred[]{:T(512)} %bitcast.3), kind=kLoop, calls=%fused_computation.13 | loop fusion | flops 16384 | bytes 98305 | tf_op jit(solution)/shard_map/jit(_where)/select_n | solution.py:44
  2.3 3.1 %collective-permute-start.4 = (bf16[144,128]{1,0:T(8,128)(2,1)S(1)}, bf16[144,128]{1,0:T(8,128)(2,1)S(1)}, u32[]{:S(2)}, u32[]{:S(2)}) collective-permute-start(bf16[144,128]{1,0:T(8,128)(2,1)S(1)} %pad_maximum_fusion.3), channel_id=1, source_target_pairs={{0,8},{4,12},{8,0},{12,4},{16,24},{20,28},{24,16},{28,20},{1,9},{5... | collective-permute-start | bytes 110600 | tf_op jit(solution)/shard_map/ppermute | solution.py:27
  5.4 2.6 %collective-permute-start.2 = (bf16[144,128]{1,0:T(8,128)(2,1)S(1)}, bf16[144,128]{1,0:T(8,128)(2,1)S(1)}, u32[]{:S(2)}, u32[]{:S(2)}) collective-permute-start(bf16[144,128]{1,0:T(8,128)(2,1)S(1)} %pad_maximum_fusion.3), channel_id=1, source_target_pairs={{0,16},{4,20},{8,24},{12,28},{16,0},{20,4},{24,8},{28,12},{1,17},{... | collective-permute-start | bytes 110600 | tf_op jit(solution)/shard_map/ppermute | solution.py:27
  8.0 1.8 %collective-permute-start.5 = (bf16[2,144,128]{2,1,0:T(8,128)(2,1)S(1)}, bf16[2,144,128]{2,1,0:T(8,128)(2,1)S(1)}, u32[]{:S(2)}, u32[]{:S(2)}) collective-permute-start(bf16[2,144,128]{2,1,0:T(8,128)(2,1)S(1)} %pad_maximum_fusion.1.refs_0_), channel_id=1, source_target_pairs={{0,4},{4,0},{8,12},{12,8},{16,20},{20,16},{24,28},{28,24},{1,5},{5... | collective-permute-start | bytes 221192 | tf_op jit(solution)/shard_map/ppermute | solution.py:27
  9.7 1.2 %collective-permute-done.2 = bf16[144,128]{1,0:T(8,128)(2,1)S(1)} collective-permute-done((bf16[144,128]{1,0:T(8,128)(2,1)S(1)}, bf16[144,128]{1,0:T(8,128)(2,1)S(1)}, u32[]{:S(2)}, u32[]{:S(2)}) %collective-permute-start.2) | collective-permute-done | bytes 36896 | tf_op jit(solution)/shard_map/ppermute | solution.py:27
  10.9 2.8 %collective-permute-done.3 = bf16[144,128]{1,0:T(8,128)(2,1)S(1)} collective-permute-done((bf16[144,128]{1,0:T(8,128)(2,1)S(1)}, bf16[144,128]{1,0:T(8,128)(2,1)S(1)}, u32[]{:S(2)}, u32[]{:S(2)}) %collective-permute-start.3) | collective-permute-done | bytes 36896 | tf_op jit(solution)/shard_map/ppermute | solution.py:27
  13.7 1.6 %collective-permute-start.7 = (bf16[2,144,128]{2,1,0:T(8,128)(2,1)S(1)}, bf16[2,144,128]{2,1,0:T(8,128)(2,1)S(1)}, u32[]{:S(2)}, u32[]{:S(2)}) collective-permute-start(bf16[2,144,128]{2,1,0:T(8,128)(2,1)S(1)} %pad_maximum_fusion.refs_2_), channel_id=1, source_target_pairs={{0,4},{4,0},{8,12},{12,8},{16,20},{20,16},{24,28},{28,24},{1,5},{5... | collective-permute-start | bytes 221192 | tf_op jit(solution)/shard_map/ppermute | solution.py:27
  15.3 0.5 collective-permute-start.9
  15.8 1.7 %constant_dynamic-slice_fusion.2.wm_ref = bf16[256,4096]{1,0:T(8,128)(2,1)S(1)} fusion(bf16[256,16384]{1,0:T(8,128)(2,1)} %w_ref.2, s32[]{:T(128)S(6)} %select_n.20), kind=kLoop, calls=%fused_computation.22 | loop fusion | bytes 4194308 | tf_op jit(solution)/shard_map/dynamic_slice | solution.py:52
  17.6 1.7 %constant_dynamic-slice_fusion = (bf16[256,2048]{1,0:T(8,128)(2,1)S(1)}, bf16[256,2048]{1,0:T(8,128)(2,1)S(1)}) fusion(bf16[256,16384]{1,0:T(8,128)(2,1)} %w_ref.2, s32[]{:T(128)S(6)} %select_n.22, s32[]{:T(128)S(6)} %select_n.21), kind=kLoop, calls=%fused_computation.20 | loop fusion | bytes 4194312 | tf_op jit(solution)/shard_map/dynamic_slice | solution.py:52
  19.4 0.5 collective-permute-start.11
  19.9 0.8 %collective-permute-done.10.refs_7_ = bf16[2,144,128]{2,1,0:T(8,128)(2,1)S(1)} collective-permute-done((bf16[2,144,128]{2,1,0:T(8,128)(2,1)S(1)}, bf16[2,144,128]{2,1,0:T(8,128)(2,1)S(1)}, u32[]{:S(2)}, u32[]{:S(2)}) %collective-permute-start.10) | collective-permute-done | bytes 73760 | tf_op jit(solution)/shard_map/ppermute | solution.py:27
  20.9 2.4 %attention.1 = (bf16[128,512]{1,0:T(8,128)(2,1)S(1)}, bf16[8,128,128]{2,1,0:T(8,128)(2,1)S(1)}) custom-call(s32[1]{0:T(128)} %bitcast.core_ref, s32[1,128]{1,0:T(1,128)S(1)} %bitcast.26, s32[1,128]{1,0:T(1,128)S(1)} %bitcast.27, bf16[128,256]{1,0:T(8,128)(2,1)S(1)} %copy-done.1, bf16[128,256]{1,0:T(8,128)(2,1)S(1)} %collective-permute-done.qo_ref, ...), custom_call_target="tpu_custom_call" | custom-call | flops 671088640 | bytes 1048576 | tf_op jit(solution)/shard_map/attention/pallas_call | solution.py:163
  23.3 0.4 collective-permute-done.12.refs_1_
  23.7 0.7 %product.1 = bf16[128,4096]{1,0:T(8,128)(2,1)S(1)} custom-call(bf16[128,512]{1,0:T(8,128)(2,1)S(1)} %get-tuple-element.49.dq_ref, bf16[256,4096]{1,0:T(8,128)(2,1)S(1)} %constant_dynamic-slice_fusion.2.wm_ref, bf16[256,2048]{1,0:T(8,128)(2,1)S(1)} %collective-permute-done.11.refs_0_, bf16[256,2048]{1,0:T(8,128)(2,1)S(1)} %collective-permute-done.12.refs_1_), custom_call_target="tpu_custom_call" | custom-call | flops 536870912 | bytes 4194304 | tf_op jit(solution)/shard_map/product/pallas_call | solution.py:198
  24.5 0.6 %collective-permute-start.13 = (bf16[4,128,128]{2,1,0:T(8,128)(2,1)S(1)}, bf16[4,128,128]{2,1,0:T(8,128)(2,1)S(1)}, u32[]{:S(2)}, u32[]{:S(2)}) collective-permute-start(bf16[4,128,128]{2,1,0:T(8,128)(2,1)S(1)} %slice.26), channel_id=1, source_target_pairs={{0,4},{4,0},{8,12},{12,8},{16,20},{20,16},{24,28},{28,24},{1,5},{5... | collective-permute-start | bytes 393224 | tf_op jit(solution)/shard_map/ppermute | solution.py:27
  25.1 1.5 %collective-permute-start.19 = (bf16[128,4096]{1,0:T(8,128)(2,1)S(1)}, bf16[128,4096]{1,0:T(8,128)(2,1)S(1)}, u32[]{:S(2)}, u32[]{:S(2)}) collective-permute-start(bf16[128,4096]{1,0:T(8,128)(2,1)S(1)} %product.1), channel_id=1, source_target_pairs={{0,2},{1,3},{2,0},{3,1},{4,6},{5,7},{6,4},{7,5},{8,10},{9,11},{10,... | collective-permute-start | bytes 3145736 | tf_op jit(solution)/shard_map/ppermute | solution.py:27
  26.6 3.7 %collective-permute-done.13 = bf16[4,128,128]{2,1,0:T(8,128)(2,1)S(1)} collective-permute-done((bf16[4,128,128]{2,1,0:T(8,128)(2,1)S(1)}, bf16[4,128,128]{2,1,0:T(8,128)(2,1)S(1)}, u32[]{:S(2)}, u32[]{:S(2)}) %collective-permute-start.13) | collective-permute-done | bytes 131104 | tf_op jit(solution)/shard_map/ppermute | solution.py:27
  30.4 3.0 %collective-permute-start.15 = (bf16[128,128]{1,0:T(8,128)(2,1)S(1)}, bf16[128,128]{1,0:T(8,128)(2,1)S(1)}, u32[]{:S(2)}, u32[]{:S(2)}) collective-permute-start(bf16[128,128]{1,0:T(8,128)(2,1)S(1)} %get-tuple-element.65), channel_id=1, source_target_pairs={{0,16},{4,20},{8,24},{12,28},{16,0},{20,4},{24,8},{28,12},{1,17},{... | collective-permute-start | bytes 98312 | tf_op jit(solution)/shard_map/ppermute | solution.py:27
  33.4 1.4 %collective-permute-start.16 = (bf16[128,128]{1,0:T(8,128)(2,1)S(1)}, bf16[128,128]{1,0:T(8,128)(2,1)S(1)}, u32[]{:S(2)}, u32[]{:S(2)}) collective-permute-start(bf16[128,128]{1,0:T(8,128)(2,1)S(1)} %get-tuple-element.64), channel_id=1, source_target_pairs={{0,24},{4,28},{8,16},{12,20},{16,8},{20,12},{24,0},{28,4},{1,25},{... | collective-permute-start | bytes 98312 | tf_op jit(solution)/shard_map/ppermute | solution.py:27
  34.8 1.0 %collective-permute-done.15 = bf16[128,128]{1,0:T(8,128)(2,1)S(1)} collective-permute-done((bf16[128,128]{1,0:T(8,128)(2,1)S(1)}, bf16[128,128]{1,0:T(8,128)(2,1)S(1)}, u32[]{:S(2)}, u32[]{:S(2)}) %collective-permute-start.15) | collective-permute-done | bytes 32800 | tf_op jit(solution)/shard_map/ppermute | solution.py:27
  35.8 3.3 %collective-permute-done.16 = bf16[128,128]{1,0:T(8,128)(2,1)S(1)} collective-permute-done((bf16[128,128]{1,0:T(8,128)(2,1)S(1)}, bf16[128,128]{1,0:T(8,128)(2,1)S(1)}, u32[]{:S(2)}, u32[]{:S(2)}) %collective-permute-start.16) | collective-permute-done | bytes 32800 | tf_op jit(solution)/shard_map/ppermute | solution.py:27
  39.3 1.1 %collective-permute-done.17 = bf16[128,128]{1,0:T(8,128)(2,1)S(1)} collective-permute-done((bf16[128,128]{1,0:T(8,128)(2,1)S(1)}, bf16[128,128]{1,0:T(8,128)(2,1)S(1)}, u32[]{:S(2)}, u32[]{:S(2)}) %collective-permute-start.17) | collective-permute-done | bytes 32800 | tf_op jit(solution)/shard_map/ppermute | solution.py:27
  40.4 2.8 %carve.1 = (bf16[256,4096]{1,0:T(8,128)(2,1)S(1)}, bf16[256,4096]{1,0:T(8,128)(2,1)S(1)}) custom-call(s32[2]{0:T(128)S(1)} %pad_add_fusion.block_ref, bf16[256,16384]{1,0:T(8,128)(2,1)} %w_ref.2, bf16[128,256]{1,0:T(8,128)(2,1)S(1)} %pad_maximum_fusion.2.refs_0_.kv_ref), custom_call_target="tpu_custom_call" | custom-call | tf_op jit(solution)/shard_map/carve/pallas_call | solution.py:74
  43.2 0.7 %own.1 = (f32[128,4096]{1,0:T(8,128)S(1)}, bf16[128,2048]{1,0:T(8,128)(2,1)S(1)}, bf16[128,2048]{1,0:T(8,128)(2,1)S(1)}) custom-call(bf16[128,512]{1,0:T(8,128)(2,1)S(1)} %get-tuple-element.49.dq_ref, bf16[256,4096]{1,0:T(8,128)(2,1)S(1)} %get-tuple-element.54.wn_ref, bf16[256,4096]{1,0:T(8,128)(2,1)S(1)} %get-tuple-element.55.wo_ref), custom_call_target="tpu_custom_call" | custom-call | tf_op jit(solution)/shard_map/own/pallas_call | solution.py:223
  43.9 0.2 collective-permute-start.20
  44.2 0.4 collective-permute-start.21
  44.5 1.5 %collective-permute-start.18 = (bf16[128,256]{1,0:T(8,128)(2,1)S(1)}, bf16[128,256]{1,0:T(8,128)(2,1)S(1)}, u32[]{:S(2)}, u32[]{:S(2)}) collective-permute-start(bf16[128,256]{1,0:T(8,128)(2,1)S(1)} %pad_maximum_fusion.2.refs_0_.kv_ref), channel_id=1, source_target_pairs={{0,2},{1,3},{2,0},{3,1},{4,6},{5,7},{6,4},{7,5},{8,10},{9,11},{10,... | collective-permute-start | bytes 196616 | tf_op jit(solution)/shard_map/ppermute | solution.py:27
  46.0 5.6 %collective-permute-done.18.kv_far_ref = bf16[128,256]{1,0:T(8,128)(2,1)S(1)} collective-permute-done((bf16[128,256]{1,0:T(8,128)(2,1)S(1)}, bf16[128,256]{1,0:T(8,128)(2,1)S(1)}, u32[]{:S(2)}, u32[]{:S(2)}) %collective-permute-start.18) | collective-permute-done | bytes 65568 | tf_op jit(solution)/shard_map/ppermute | solution.py:27
  51.6 1.3 %finish.1 = bf16[128,4096]{1,0:T(8,128)(2,1)} custom-call(s32[1]{0:T(128)} %bitcast.core_ref, bf16[128,256]{1,0:T(8,128)(2,1)S(1)} %pad_maximum_fusion.2.refs_0_.kv_ref, bf16[128,256]{1,0:T(8,128)(2,1)S(1)} %collective-permute-done.18.kv_far_ref, bf16[256,4096]{1,0:T(8,128)(2,1)S(1)} %copy-done, f32[128,4096]{1,0:T(8,128)S(1)} %get-tuple-element.56.acc_ref, ...), custom_call_target="tpu_custom_call" | custom-call | flops 268435456 | bytes 5242880 | tf_op jit(solution)/shard_map/finish/pallas_call | solution.py:266
  (42 shorter events, 0.9 us)
Async XLA Ops:
  0.0 2.2 %collective-permute-start = (bf16[128,256]{1,0:T(8,128)(2,1)}, bf16[128,256]{1,0:T(8,128)(2,1)S(1)}, u32[]{:S(2)}, u32[]{:S(2)}) collective-permute-start(bf16[128,256]{1,0:T(8,128)(2,1)} %qm_ref.1), channel_id=1, source_target_pairs={{0,1},{1,0},{2,3},{3,2},{4,5},{5,4},{6,7},{7,6},{8,9},{9,8},{10,11... | collective-permute-start | bytes 196616 | tf_op jit(solution)/shard_map/ppermute | solution.py:27
  0.5 1.8 %collective-permute-start.1 = (bf16[128,256]{1,0:T(8,128)(2,1)}, bf16[128,256]{1,0:T(8,128)(2,1)S(1)}, u32[]{:S(2)}, u32[]{:S(2)}) collective-permute-start(bf16[128,256]{1,0:T(8,128)(2,1)} %gm_ref.1), channel_id=1, source_target_pairs={{0,1},{1,0},{2,3},{3,2},{4,5},{5,4},{6,7},{7,6},{8,9},{9,8},{10,11... | collective-permute-start | bytes 196616 | tf_op jit(solution)/shard_map/ppermute | solution.py:27
  2.3 5.7 %collective-permute-start.4 = (bf16[144,128]{1,0:T(8,128)(2,1)S(1)}, bf16[144,128]{1,0:T(8,128)(2,1)S(1)}, u32[]{:S(2)}, u32[]{:S(2)}) collective-permute-start(bf16[144,128]{1,0:T(8,128)(2,1)S(1)} %pad_maximum_fusion.3), channel_id=1, source_target_pairs={{0,8},{4,12},{8,0},{12,4},{16,24},{20,28},{24,16},{28,20},{1,9},{5... | collective-permute-start | bytes 110600 | tf_op jit(solution)/shard_map/ppermute | solution.py:27
  5.4 5.6 %collective-permute-start.2 = (bf16[144,128]{1,0:T(8,128)(2,1)S(1)}, bf16[144,128]{1,0:T(8,128)(2,1)S(1)}, u32[]{:S(2)}, u32[]{:S(2)}) collective-permute-start(bf16[144,128]{1,0:T(8,128)(2,1)S(1)} %pad_maximum_fusion.3), channel_id=1, source_target_pairs={{0,16},{4,20},{8,24},{12,28},{16,0},{20,4},{24,8},{28,12},{1,17},{... | collective-permute-start | bytes 110600 | tf_op jit(solution)/shard_map/ppermute | solution.py:27
  7.9 5.8 %collective-permute-start.3 = (bf16[144,128]{1,0:T(8,128)(2,1)S(1)}, bf16[144,128]{1,0:T(8,128)(2,1)S(1)}, u32[]{:S(2)}, u32[]{:S(2)}) collective-permute-start(bf16[144,128]{1,0:T(8,128)(2,1)S(1)} %pad_maximum_fusion.3), channel_id=1, source_target_pairs={{0,24},{4,28},{8,16},{12,20},{16,8},{20,12},{24,0},{28,4},{1,25},{... | collective-permute-start | bytes 110600 | tf_op jit(solution)/shard_map/ppermute | solution.py:27
  8.0 5.8 %collective-permute-start.5 = (bf16[2,144,128]{2,1,0:T(8,128)(2,1)S(1)}, bf16[2,144,128]{2,1,0:T(8,128)(2,1)S(1)}, u32[]{:S(2)}, u32[]{:S(2)}) collective-permute-start(bf16[2,144,128]{2,1,0:T(8,128)(2,1)S(1)} %pad_maximum_fusion.1.refs_0_), channel_id=1, source_target_pairs={{0,4},{4,0},{8,12},{12,8},{16,20},{20,16},{24,28},{28,24},{1,5},{5... | collective-permute-start | bytes 221192 | tf_op jit(solution)/shard_map/ppermute | solution.py:27
  9.7 4.0 %collective-permute-start.6 = (bf16[2,144,128]{2,1,0:T(8,128)(2,1)S(1)}, bf16[2,144,128]{2,1,0:T(8,128)(2,1)S(1)}, u32[]{:S(2)}, u32[]{:S(2)}) collective-permute-start(bf16[2,144,128]{2,1,0:T(8,128)(2,1)S(1)} %pad_maximum_fusion.1.refs_0_), channel_id=1, source_target_pairs={{0,1},{1,0},{2,3},{3,2},{4,5},{5,4},{6,7},{7,6},{8,9},{9,8},{10,11... | collective-permute-start | bytes 221192 | tf_op jit(solution)/shard_map/ppermute | solution.py:27
  13.7 5.6 %collective-permute-start.7 = (bf16[2,144,128]{2,1,0:T(8,128)(2,1)S(1)}, bf16[2,144,128]{2,1,0:T(8,128)(2,1)S(1)}, u32[]{:S(2)}, u32[]{:S(2)}) collective-permute-start(bf16[2,144,128]{2,1,0:T(8,128)(2,1)S(1)} %pad_maximum_fusion.refs_2_), channel_id=1, source_target_pairs={{0,4},{4,0},{8,12},{12,8},{16,20},{20,16},{24,28},{28,24},{1,5},{5... | collective-permute-start | bytes 221192 | tf_op jit(solution)/shard_map/ppermute | solution.py:27
  15.3 4.0 %collective-permute-start.8 = (bf16[2,144,128]{2,1,0:T(8,128)(2,1)S(1)}, bf16[2,144,128]{2,1,0:T(8,128)(2,1)S(1)}, u32[]{:S(2)}, u32[]{:S(2)}) collective-permute-start(bf16[2,144,128]{2,1,0:T(8,128)(2,1)S(1)} %pad_maximum_fusion.refs_2_), channel_id=1, source_target_pairs={{0,1},{1,0},{2,3},{3,2},{4,5},{5,4},{6,7},{7,6},{8,9},{9,8},{10,11... | collective-permute-start | bytes 221192 | tf_op jit(solution)/shard_map/ppermute | solution.py:27
  15.3 4.0 %collective-permute-start.9 = (bf16[2,144,128]{2,1,0:T(8,128)(2,1)S(1)}, bf16[2,144,128]{2,1,0:T(8,128)(2,1)S(1)}, u32[]{:S(2)}, u32[]{:S(2)}) collective-permute-start(bf16[2,144,128]{2,1,0:T(8,128)(2,1)S(1)} %collective-permute-done.5.refs_4_), channel_id=1, source_target_pairs={{0,1},{1,0},{2,3},{3,2},{4,5},{5,4},{6,7},{7,6},{8,9},{9,8},{10,11... | collective-permute-start | bytes 221192 | tf_op jit(solution)/shard_map/ppermute | solution.py:27
  17.5 3.3 %copy-start.1 = (bf16[128,256]{1,0:T(8,128)(2,1)S(1)}, bf16[128,256]{1,0:T(8,128)(2,1)}, u32[]{:S(2)}) copy-start(bf16[128,256]{1,0:T(8,128)(2,1)} %qm_ref.1) | copy-start | bytes 196612
  17.6 3.3 %copy-start.2 = (bf16[128,256]{1,0:T(8,128)(2,1)S(1)}, bf16[128,256]{1,0:T(8,128)(2,1)}, u32[]{:S(2)}) copy-start(bf16[128,256]{1,0:T(8,128)(2,1)} %gm_ref.1) | copy-start | bytes 196612
  17.6 3.3 %copy-start.3 = (s32[128]{0:T(128)S(1)}, s32[128]{0:T(128)}, u32[]{:S(2)}) copy-start(s32[128]{0:T(128)} %param.12) | copy-start | bytes 1540
  17.6 3.3 %copy-start.4 = (s32[128]{0:T(128)S(1)}, s32[128]{0:T(128)}, u32[]{:S(2)}) copy-start(s32[128]{0:T(128)} %param.13) | copy-start | bytes 1540
  19.3 1.3 %collective-permute-start.10 = (bf16[2,144,128]{2,1,0:T(8,128)(2,1)S(1)}, bf16[2,144,128]{2,1,0:T(8,128)(2,1)S(1)}, u32[]{:S(2)}, u32[]{:S(2)}) collective-permute-start(bf16[2,144,128]{2,1,0:T(8,128)(2,1)S(1)} %collective-permute-done.7.refs_6_), channel_id=1, source_target_pairs={{0,1},{1,0},{2,3},{3,2},{4,5},{5,4},{6,7},{7,6},{8,9},{9,8},{10,11... | collective-permute-start | bytes 221192 | tf_op jit(solution)/shard_map/ppermute | solution.py:27
  19.4 3.8 %collective-permute-start.11 = (bf16[256,2048]{1,0:T(8,128)(2,1)S(1)}, bf16[256,2048]{1,0:T(8,128)(2,1)S(1)}, u32[]{:S(2)}, u32[]{:S(2)}) collective-permute-start(bf16[256,2048]{1,0:T(8,128)(2,1)S(1)} %get-tuple-element.51), channel_id=1, source_target_pairs={{0,1},{1,0},{2,3},{3,2},{4,5},{5,4},{6,7},{7,6},{8,9},{9,8},{10,11... | collective-permute-start | bytes 3145736 | tf_op jit(solution)/shard_map/ppermute | solution.py:27
  20.7 3.0 %collective-permute-start.12 = (bf16[256,2048]{1,0:T(8,128)(2,1)S(1)}, bf16[256,2048]{1,0:T(8,128)(2,1)S(1)}, u32[]{:S(2)}, u32[]{:S(2)}) collective-permute-start(bf16[256,2048]{1,0:T(8,128)(2,1)S(1)} %get-tuple-element.52), channel_id=1, source_target_pairs={{0,1},{1,0},{2,3},{3,2},{4,5},{5,4},{6,7},{7,6},{8,9},{9,8},{10,11... | collective-permute-start | bytes 3145736 | tf_op jit(solution)/shard_map/ppermute | solution.py:27
  24.5 5.8 %collective-permute-start.13 = (bf16[4,128,128]{2,1,0:T(8,128)(2,1)S(1)}, bf16[4,128,128]{2,1,0:T(8,128)(2,1)S(1)}, u32[]{:S(2)}, u32[]{:S(2)}) collective-permute-start(bf16[4,128,128]{2,1,0:T(8,128)(2,1)S(1)} %slice.26), channel_id=1, source_target_pairs={{0,4},{4,0},{8,12},{12,8},{16,20},{20,16},{24,28},{28,24},{1,5},{5... | collective-permute-start | bytes 393224 | tf_op jit(solution)/shard_map/ppermute | solution.py:27
  25.1 26.6 %collective-permute-start.19 = (bf16[128,4096]{1,0:T(8,128)(2,1)S(1)}, bf16[128,4096]{1,0:T(8,128)(2,1)S(1)}, u32[]{:S(2)}, u32[]{:S(2)}) collective-permute-start(bf16[128,4096]{1,0:T(8,128)(2,1)S(1)} %product.1), channel_id=1, source_target_pairs={{0,2},{1,3},{2,0},{3,1},{4,6},{5,7},{6,4},{7,5},{8,10},{9,11},{10,... | collective-permute-start | bytes 3145736 | tf_op jit(solution)/shard_map/ppermute | solution.py:27
  30.4 4.5 %collective-permute-start.14 = (bf16[128,128]{1,0:T(8,128)(2,1)S(1)}, bf16[128,128]{1,0:T(8,128)(2,1)S(1)}, u32[]{:S(2)}, u32[]{:S(2)}) collective-permute-start(bf16[128,128]{1,0:T(8,128)(2,1)S(1)} %get-tuple-element.63), channel_id=1, source_target_pairs={{0,8},{4,12},{8,0},{12,4},{16,24},{20,28},{24,16},{28,20},{1,9},{5... | collective-permute-start | bytes 98312 | tf_op jit(solution)/shard_map/ppermute | solution.py:27
  30.4 5.3 %collective-permute-start.15 = (bf16[128,128]{1,0:T(8,128)(2,1)S(1)}, bf16[128,128]{1,0:T(8,128)(2,1)S(1)}, u32[]{:S(2)}, u32[]{:S(2)}) collective-permute-start(bf16[128,128]{1,0:T(8,128)(2,1)S(1)} %get-tuple-element.65), channel_id=1, source_target_pairs={{0,16},{4,20},{8,24},{12,28},{16,0},{20,4},{24,8},{28,12},{1,17},{... | collective-permute-start | bytes 98312 | tf_op jit(solution)/shard_map/ppermute | solution.py:27
  33.4 5.7 %collective-permute-start.16 = (bf16[128,128]{1,0:T(8,128)(2,1)S(1)}, bf16[128,128]{1,0:T(8,128)(2,1)S(1)}, u32[]{:S(2)}, u32[]{:S(2)}) collective-permute-start(bf16[128,128]{1,0:T(8,128)(2,1)S(1)} %get-tuple-element.64), channel_id=1, source_target_pairs={{0,24},{4,28},{8,16},{12,20},{16,8},{20,12},{24,0},{28,4},{1,25},{... | collective-permute-start | bytes 98312 | tf_op jit(solution)/shard_map/ppermute | solution.py:27
  39.1 1.3 %collective-permute-start.17 = (bf16[128,128]{1,0:T(8,128)(2,1)S(1)}, bf16[128,128]{1,0:T(8,128)(2,1)S(1)}, u32[]{:S(2)}, u32[]{:S(2)}) collective-permute-start(bf16[128,128]{1,0:T(8,128)(2,1)S(1)} %fusion.3), channel_id=1, source_target_pairs={{0,1},{1,0},{2,3},{3,2},{4,5},{5,4},{6,7},{7,6},{8,9},{9,8},{10,11... | collective-permute-start | bytes 98312 | tf_op jit(solution)/shard_map/ppermute | solution.py:27
  43.2 8.4 %copy-start = (bf16[256,4096]{1,0:T(8,128)(2,1)S(1)}, bf16[256,4096]{1,0:T(8,128)(2,1)}, u32[]{:S(2)}) copy-start(bf16[256,4096]{1,0:T(8,128)(2,1)} %w_ref.3) | copy-start | bytes 6291460
  43.9 7.7 %collective-permute-start.20 = (bf16[128,2048]{1,0:T(8,128)(2,1)S(1)}, bf16[128,2048]{1,0:T(8,128)(2,1)S(1)}, u32[]{:S(2)}, u32[]{:S(2)}) collective-permute-start(bf16[128,2048]{1,0:T(8,128)(2,1)S(1)} %get-tuple-element.57), channel_id=1, source_target_pairs={{0,1},{1,0},{2,3},{3,2},{4,5},{5,4},{6,7},{7,6},{8,9},{9,8},{10,11... | collective-permute-start | bytes 1572872 | tf_op jit(solution)/shard_map/ppermute | solution.py:27
  44.2 7.5 %collective-permute-start.21 = (bf16[128,2048]{1,0:T(8,128)(2,1)S(1)}, bf16[128,2048]{1,0:T(8,128)(2,1)S(1)}, u32[]{:S(2)}, u32[]{:S(2)}) collective-permute-start(bf16[128,2048]{1,0:T(8,128)(2,1)S(1)} %get-tuple-element.58), channel_id=1, source_target_pairs={{0,1},{1,0},{2,3},{3,2},{4,5},{5,4},{6,7},{7,6},{8,9},{9,8},{10,11... | collective-permute-start | bytes 1572872 | tf_op jit(solution)/shard_map/ppermute | solution.py:27
  44.5 7.1 %collective-permute-start.18 = (bf16[128,256]{1,0:T(8,128)(2,1)S(1)}, bf16[128,256]{1,0:T(8,128)(2,1)S(1)}, u32[]{:S(2)}, u32[]{:S(2)}) collective-permute-start(bf16[128,256]{1,0:T(8,128)(2,1)S(1)} %pad_maximum_fusion.2.refs_0_.kv_ref), channel_id=1, source_target_pairs={{0,2},{1,3},{2,0},{3,1},{4,6},{5,7},{6,4},{7,5},{8,10},{9,11},{10,... | collective-permute-start | bytes 196616 | tf_op jit(solution)/shard_map/ppermute | solution.py:27

commit v17 on v15

--- a/solution.py
+++ b/solution.py
@@ -289,15 +289,13 @@
     x_early = swapped(z_early, "ctx", 1)
     far_send = column_block(w_query, head ^ 3, share, z_early)
     far_mine = column_block(w_query, head ^ 2, share, z_early)
-    there_early = swapped(z_early, "head", 1)
-    z_late, x_early, there_early, far_send, far_mine = lax.optimization_barrier(
-        (z_late, x_early, there_early, far_send, far_mine)
-    )
+    z_late, x_early, far_send, far_mine = lax.optimization_barrier((z_late, x_early, far_send, far_mine))
     x_late = swapped(z_late, "ctx", 1)
     far_other = swapped(far_send, "head", 1)
-    pieces = [z_early, there_early]
-    for here in (z_late, x_early, x_late):
-        pieces += [here, swapped(here, "head", 1)]
+    here_z = jnp.concatenate([z_early, z_late])
+    there_z = swapped(here_z, "head", 1)
+    here_x = jnp.concatenate([x_early, x_late])
+    pieces = (here_z, there_z, here_x, swapped(here_x, "head", 1))
     dq, back = attention(core, positions, doc_ids, queries, q_other, dout, g_other, pieces)
 
     part = product(dq, far_mine, far_other, 0, share, jnp.bfloat16)

time: 52.6 us -> 52.7 us (level)
    ppermute x21 -> x19, starting transfers between devices: 19.8 us -> 19.6 us  [swapped(): lax.ppermute(value, axis, [(source, source ^ bits) for source in range(co...]
    ppermute x21 -> x19, waiting for transfers between devices: 19.7 us -> 19.9 us  [swapped(): lax.ppermute(value, axis, [(source, source ^ bits) for source in range(co...]
  transfers between devices with their start and end apart: 21 -> 19, of which waited for: 8 -> 8; matrix products, arithmetic and copies ran while one was open for 9% -> 9% of each run, Pallas kernels for 11% -> 11%
where the time goes in v17:
time: 52.7 us; the launch traced here: 52.5 us
  waiting for transfers between devices  19.9 us (38%)
  starting transfers between devices  19.6 us (37%)
  Pallas kernels  8.08 us (15%)
  local copies, waits for them, and re-layouts  3.51 us (7%)
  other arithmetic  1.17 us (2%)
    ppermute x19, waiting for transfers between devices, swapped(): lax.ppermute(value, axis, [(source, source ^ bits) for source in range(co...  19.9 us
    ppermute x19, starting transfers between devices, swapped(): lax.ppermute(value, axis, [(source, source ^ bits) for source in range(co...  19.6 us
    pallas_call x1, Pallas kernels, carve(): pl.pallas_call(carve_kernel, out_shape=[block] * count, in_specs=[SMEM, H...  2.76 us
    dynamic_slice x1, local copies, waits for them, and re-layouts, column_block(): return lax.dynamic_slice_in_dim(w_query, block * share, share, axis=1)  2.71 us
    pallas_call x1, Pallas kernels, attention(): pl.pallas_call(attention_kernel, out_shape=[jax.ShapeDtypeStruct((rows, 2...  2.42 us
    pallas_call x1, Pallas kernels, finish(): pl.pallas_call(finish_kernel, out_shape=jax.ShapeDtypeStruct((rows, share...  1.43 us
  transfers between devices with their start and end apart: 19, of which 8 were waited for; matrix products, arithmetic and copies ran while one was open for 9% of the time, Pallas kernels for 11%

profile of v17, /device:TPU:0, one launch (start us, length us, event | category | flops | bytes accessed | tf_op | source)
XLA Modules:
  0.0 52.5 jit_solution(10058846054806871758)
XLA Ops:
  0.0 0.5 collective-permute-start
  0.5 0.7 %reshape.19 = s32[2,64]{1,0:T(2,128)S(1)} reshape(s32[128]{0:T(128)} %param.12) | data formatting | bytes 1024 | tf_op jit(solution)/shard_map/reshape | solution.py:44
  1.2 0.1 fusion.5
  1.4 0.8 %broadcast_select_fusion = bf16[128,128]{1,0:T(8,128)(2,1)S(1)} fusion(bf16[128,128]{1,0:T(8,128)(2,1)} %param.9, bf16[128,128]{1,0:T(8,128)(2,1)} %param.10, pred[]{:T(512)} %bitcast.3), kind=kLoop, calls=%fused_computation.14 | loop fusion | flops 16384 | bytes 98305 | tf_op jit(solution)/shard_map/jit(_where)/select_n | solution.py:43
  2.2 0.1 pad_maximum_fusion.4
  2.3 3.1 %collective-permute-start.2 = (bf16[144,128]{1,0:T(8,128)(2,1)S(1)}, bf16[144,128]{1,0:T(8,128)(2,1)S(1)}, u32[]{:S(2)}, u32[]{:S(2)}) collective-permute-start(bf16[144,128]{1,0:T(8,128)(2,1)S(1)} %pad_maximum_fusion.4), channel_id=1, source_target_pairs={{0,8},{4,12},{8,0},{12,4},{16,24},{20,28},{24,16},{28,20},{1,9},{5... | collective-permute-start | bytes 110600 | tf_op jit(solution)/shard_map/ppermute | solution.py:26
  5.4 2.6 %collective-permute-start.3 = (bf16[144,128]{1,0:T(8,128)(2,1)S(1)}, bf16[144,128]{1,0:T(8,128)(2,1)S(1)}, u32[]{:S(2)}, u32[]{:S(2)}) collective-permute-start(bf16[144,128]{1,0:T(8,128)(2,1)S(1)} %pad_maximum_fusion.4), channel_id=1, source_target_pairs={{0,16},{4,20},{8,24},{12,28},{16,0},{20,4},{24,8},{28,12},{1,17},{... | collective-permute-start | bytes 110600 | tf_op jit(solution)/shard_map/ppermute | solution.py:26
  8.0 1.8 %collective-permute-start.5 = (bf16[2,144,128]{2,1,0:T(8,128)(2,1)S(1)}, bf16[2,144,128]{2,1,0:T(8,128)(2,1)S(1)}, u32[]{:S(2)}, u32[]{:S(2)}) collective-permute-start(bf16[2,144,128]{2,1,0:T(8,128)(2,1)S(1)} %pad_maximum_fusion.2), channel_id=1, source_target_pairs={{0,4},{4,0},{8,12},{12,8},{16,20},{20,16},{24,28},{28,24},{1,5},{5... | collective-permute-start | bytes 221192 | tf_op jit(solution)/shard_map/ppermute | solution.py:26
  9.8 2.7 %constant_dynamic-slice_fusion = (bf16[256,4096]{1,0:T(8,128)(2,1)S(1)}, bf16[256,4096]{1,0:T(8,128)(2,1)S(1)}) fusion(bf16[256,16384]{1,0:T(8,128)(2,1)} %w_ref.2, s32[]{:T(128)S(6)} %select_n.18, s32[]{:T(128)S(6)} %select_n.17), kind=kLoop, calls=%fused_computation.24 | loop fusion | bytes 8388616 | tf_op jit(solution)/shard_map/dynamic_slice | solution.py:51
  12.5 1.2 %collective-permute-done.4 = bf16[144,128]{1,0:T(8,128)(2,1)S(1)} collective-permute-done((bf16[144,128]{1,0:T(8,128)(2,1)S(1)}, bf16[144,128]{1,0:T(8,128)(2,1)S(1)}, u32[]{:S(2)}, u32[]{:S(2)}) %collective-permute-start.4) | collective-permute-done | bytes 36896 | tf_op jit(solution)/shard_map/ppermute | solution.py:26
  13.8 1.6 %collective-permute-start.7 = (bf16[2,144,128]{2,1,0:T(8,128)(2,1)S(1)}, bf16[2,144,128]{2,1,0:T(8,128)(2,1)S(1)}, u32[]{:S(2)}, u32[]{:S(2)}) collective-permute-start(bf16[2,144,128]{2,1,0:T(8,128)(2,1)S(1)} %pad_maximum_fusion.1), channel_id=1, source_target_pairs={{0,4},{4,0},{8,12},{12,8},{16,20},{20,16},{24,28},{28,24},{1,5},{5... | collective-permute-start | bytes 221192 | tf_op jit(solution)/shard_map/ppermute | solution.py:26
  15.4 0.2 collective-permute-start.6
  15.6 2.9 %collective-permute-done.7 = bf16[2,144,128]{2,1,0:T(8,128)(2,1)S(1)} collective-permute-done((bf16[2,144,128]{2,1,0:T(8,128)(2,1)S(1)}, bf16[2,144,128]{2,1,0:T(8,128)(2,1)S(1)}, u32[]{:S(2)}, u32[]{:S(2)}) %collective-permute-start.7) | collective-permute-done | bytes 73760 | tf_op jit(solution)/shard_map/ppermute | solution.py:26
  18.6 1.3 %collective-permute-done.8.refs_3_ = bf16[4,144,128]{2,1,0:T(8,128)(2,1)S(1)} collective-permute-done((bf16[4,144,128]{2,1,0:T(8,128)(2,1)S(1)}, bf16[4,144,128]{2,1,0:T(8,128)(2,1)S(1)}, u32[]{:S(2)}, u32[]{:S(2)}) %collective-permute-start.8) | collective-permute-done | bytes 147488 | tf_op jit(solution)/shard_map/ppermute | solution.py:26
  20.0 2.4 %attention.1 = (bf16[128,512]{1,0:T(8,128)(2,1)S(1)}, bf16[8,128,128]{2,1,0:T(8,128)(2,1)S(1)}) custom-call(s32[1]{0:T(128)} %bitcast.core_ref, s32[1,128]{1,0:T(1,128)S(1)} %bitcast.26, s32[1,128]{1,0:T(1,128)S(1)} %bitcast.27, bf16[128,256]{1,0:T(8,128)(2,1)S(1)} %copy-done.1, bf16[128,256]{1,0:T(8,128)(2,1)S(1)} %collective-permute-done.qo_ref, ...), custom_call_target="tpu_custom_call" | custom-call | flops 671088640 | bytes 1048576 | tf_op jit(solution)/shard_map/attention/pallas_call | solution.py:162
  22.4 0.7 %product.1 = bf16[128,4096]{1,0:T(8,128)(2,1)S(1)} custom-call(bf16[128,512]{1,0:T(8,128)(2,1)S(1)} %get-tuple-element.28.dq_ref, bf16[256,4096]{1,0:T(8,128)(2,1)S(1)} %get-tuple-element.29.wm_ref, bf16[256,4096]{1,0:T(8,128)(2,1)S(1)} %collective-permute-done.9.wo_ref), custom_call_target="tpu_custom_call" | custom-call | flops 536870912 | bytes 4194304 | tf_op jit(solution)/shard_map/product/pallas_call | solution.py:193
  23.2 1.6 %collective-permute-start.10 = (bf16[4,128,128]{2,1,0:T(8,128)(2,1)S(1)}, bf16[4,128,128]{2,1,0:T(8,128)(2,1)S(1)}, u32[]{:S(2)}, u32[]{:S(2)}) collective-permute-start(bf16[4,128,128]{2,1,0:T(8,128)(2,1)S(1)} %slice.26), channel_id=1, source_target_pairs={{0,4},{4,0},{8,12},{12,8},{16,20},{20,16},{24,28},{28,24},{1,5},{5... | collective-permute-start | bytes 393224 | tf_op jit(solution)/shard_map/ppermute | solution.py:26
  24.7 1.5 %collective-permute-start.16 = (bf16[128,4096]{1,0:T(8,128)(2,1)S(1)}, bf16[128,4096]{1,0:T(8,128)(2,1)S(1)}, u32[]{:S(2)}, u32[]{:S(2)}) collective-permute-start(bf16[128,4096]{1,0:T(8,128)(2,1)S(1)} %product.1), channel_id=1, source_target_pairs={{0,2},{1,3},{2,0},{3,1},{4,6},{5,7},{6,4},{7,5},{8,10},{9,11},{10,... | collective-permute-start | bytes 3145736 | tf_op jit(solution)/shard_map/ppermute | solution.py:26
  26.2 2.5 %collective-permute-done.10 = bf16[4,128,128]{2,1,0:T(8,128)(2,1)S(1)} collective-permute-done((bf16[4,128,128]{2,1,0:T(8,128)(2,1)S(1)}, bf16[4,128,128]{2,1,0:T(8,128)(2,1)S(1)}, u32[]{:S(2)}, u32[]{:S(2)}) %collective-permute-start.10) | collective-permute-done | bytes 131104 | tf_op jit(solution)/shard_map/ppermute | solution.py:26
  28.9 3.0 %collective-permute-start.12 = (bf16[128,128]{1,0:T(8,128)(2,1)S(1)}, bf16[128,128]{1,0:T(8,128)(2,1)S(1)}, u32[]{:S(2)}, u32[]{:S(2)}) collective-permute-start(bf16[128,128]{1,0:T(8,128)(2,1)S(1)} %get-tuple-element.43), channel_id=1, source_target_pairs={{0,16},{4,20},{8,24},{12,28},{16,0},{20,4},{24,8},{28,12},{1,17},{... | collective-permute-start | bytes 98312 | tf_op jit(solution)/shard_map/ppermute | solution.py:26
  31.9 1.4 %collective-permute-start.13 = (bf16[128,128]{1,0:T(8,128)(2,1)S(1)}, bf16[128,128]{1,0:T(8,128)(2,1)S(1)}, u32[]{:S(2)}, u32[]{:S(2)}) collective-permute-start(bf16[128,128]{1,0:T(8,128)(2,1)S(1)} %get-tuple-element.42), channel_id=1, source_target_pairs={{0,24},{4,28},{8,16},{12,20},{16,8},{20,12},{24,0},{28,4},{1,25},{... | collective-permute-start | bytes 98312 | tf_op jit(solution)/shard_map/ppermute | solution.py:26
  33.3 0.7 %collective-permute-done.12 = bf16[128,128]{1,0:T(8,128)(2,1)S(1)} collective-permute-done((bf16[128,128]{1,0:T(8,128)(2,1)S(1)}, bf16[128,128]{1,0:T(8,128)(2,1)S(1)}, u32[]{:S(2)}, u32[]{:S(2)}) %collective-permute-start.12) | collective-permute-done | bytes 32800 | tf_op jit(solution)/shard_map/ppermute | solution.py:26
  34.0 3.6 %collective-permute-done.13 = bf16[128,128]{1,0:T(8,128)(2,1)S(1)} collective-permute-done((bf16[128,128]{1,0:T(8,128)(2,1)S(1)}, bf16[128,128]{1,0:T(8,128)(2,1)S(1)}, u32[]{:S(2)}, u32[]{:S(2)}) %collective-permute-start.13) | collective-permute-done | bytes 32800 | tf_op jit(solution)/shard_map/ppermute | solution.py:26
  37.7 0.1 pad_add_fusion.block_ref
  37.8 1.1 %collective-permute-done.14 = bf16[128,128]{1,0:T(8,128)(2,1)S(1)} collective-permute-done((bf16[128,128]{1,0:T(8,128)(2,1)S(1)}, bf16[128,128]{1,0:T(8,128)(2,1)S(1)}, u32[]{:S(2)}, u32[]{:S(2)}) %collective-permute-start.14) | collective-permute-done | bytes 32800 | tf_op jit(solution)/shard_map/ppermute | solution.py:26
  38.9 2.8 %carve.1 = (bf16[256,4096]{1,0:T(8,128)(2,1)S(1)}, bf16[256,4096]{1,0:T(8,128)(2,1)S(1)}) custom-call(s32[2]{0:T(128)S(1)} %pad_add_fusion.block_ref, bf16[256,16384]{1,0:T(8,128)(2,1)} %w_ref.2, bf16[128,256]{1,0:T(8,128)(2,1)S(1)} %pad_maximum_fusion.3.refs_0_.kv_ref), custom_call_target="tpu_custom_call" | custom-call | tf_op jit(solution)/shard_map/carve/pallas_call | solution.py:73
  41.7 0.7 %own.1 = (f32[128,4096]{1,0:T(8,128)S(1)}, bf16[128,2048]{1,0:T(8,128)(2,1)S(1)}, bf16[128,2048]{1,0:T(8,128)(2,1)S(1)}) custom-call(bf16[128,512]{1,0:T(8,128)(2,1)S(1)} %get-tuple-element.28.dq_ref, bf16[256,4096]{1,0:T(8,128)(2,1)S(1)} %get-tuple-element.32.wn_ref, bf16[256,4096]{1,0:T(8,128)(2,1)S(1)} %get-tuple-element.33.wo_ref), custom_call_target="tpu_custom_call" | custom-call | tf_op jit(solution)/shard_map/own/pallas_call | solution.py:218
  42.4 0.2 collective-permute-start.17
  42.7 0.3 collective-permute-start.18
  43.0 1.5 %collective-permute-start.15 = (bf16[128,256]{1,0:T(8,128)(2,1)S(1)}, bf16[128,256]{1,0:T(8,128)(2,1)S(1)}, u32[]{:S(2)}, u32[]{:S(2)}) collective-permute-start(bf16[128,256]{1,0:T(8,128)(2,1)S(1)} %pad_maximum_fusion.3.refs_0_.kv_ref), channel_id=1, source_target_pairs={{0,2},{1,3},{2,0},{3,1},{4,6},{5,7},{6,4},{7,5},{8,10},{9,11},{10,... | collective-permute-start | bytes 196616 | tf_op jit(solution)/shard_map/ppermute | solution.py:26
  44.5 6.5 %collective-permute-done.15.kv_far_ref = bf16[128,256]{1,0:T(8,128)(2,1)S(1)} collective-permute-done((bf16[128,256]{1,0:T(8,128)(2,1)S(1)}, bf16[128,256]{1,0:T(8,128)(2,1)S(1)}, u32[]{:S(2)}, u32[]{:S(2)}) %collective-permute-start.15) | collective-permute-done | bytes 65568 | tf_op jit(solution)/shard_map/ppermute | solution.py:26
  51.1 1.4 %finish.1 = bf16[128,4096]{1,0:T(8,128)(2,1)} custom-call(s32[1]{0:T(128)} %bitcast.core_ref, bf16[128,256]{1,0:T(8,128)(2,1)S(1)} %pad_maximum_fusion.3.refs_0_.kv_ref, bf16[128,256]{1,0:T(8,128)(2,1)S(1)} %collective-permute-done.15.kv_far_ref, bf16[256,4096]{1,0:T(8,128)(2,1)S(1)} %copy-done, f32[128,4096]{1,0:T(8,128)S(1)} %get-tuple-element.34.acc_ref, ...), custom_call_target="tpu_custom_call" | custom-call | flops 268435456 | bytes 5242880 | tf_op jit(solution)/shard_map/finish/pallas_call | solution.py:261
  (38 shorter events, 0.6 us)
Async XLA Ops:
  0.0 2.2 %collective-permute-start = (bf16[128,256]{1,0:T(8,128)(2,1)}, bf16[128,256]{1,0:T(8,128)(2,1)S(1)}, u32[]{:S(2)}, u32[]{:S(2)}) collective-permute-start(bf16[128,256]{1,0:T(8,128)(2,1)} %qm_ref.1), channel_id=1, source_target_pairs={{0,1},{1,0},{2,3},{3,2},{4,5},{5,4},{6,7},{7,6},{8,9},{9,8},{10,11... | collective-permute-start | bytes 196616 | tf_op jit(solution)/shard_map/ppermute | solution.py:26
  0.5 1.8 %collective-permute-start.1 = (bf16[128,256]{1,0:T(8,128)(2,1)}, bf16[128,256]{1,0:T(8,128)(2,1)S(1)}, u32[]{:S(2)}, u32[]{:S(2)}) collective-permute-start(bf16[128,256]{1,0:T(8,128)(2,1)} %gm_ref.1), channel_id=1, source_target_pairs={{0,1},{1,0},{2,3},{3,2},{4,5},{5,4},{6,7},{7,6},{8,9},{9,8},{10,11... | collective-permute-start | bytes 196616 | tf_op jit(solution)/shard_map/ppermute | solution.py:26
  2.3 5.7 %collective-permute-start.2 = (bf16[144,128]{1,0:T(8,128)(2,1)S(1)}, bf16[144,128]{1,0:T(8,128)(2,1)S(1)}, u32[]{:S(2)}, u32[]{:S(2)}) collective-permute-start(bf16[144,128]{1,0:T(8,128)(2,1)S(1)} %pad_maximum_fusion.4), channel_id=1, source_target_pairs={{0,8},{4,12},{8,0},{12,4},{16,24},{20,28},{24,16},{28,20},{1,9},{5... | collective-permute-start | bytes 110600 | tf_op jit(solution)/shard_map/ppermute | solution.py:26
  5.4 7.1 %collective-permute-start.3 = (bf16[144,128]{1,0:T(8,128)(2,1)S(1)}, bf16[144,128]{1,0:T(8,128)(2,1)S(1)}, u32[]{:S(2)}, u32[]{:S(2)}) collective-permute-start(bf16[144,128]{1,0:T(8,128)(2,1)S(1)} %pad_maximum_fusion.4), channel_id=1, source_target_pairs={{0,16},{4,20},{8,24},{12,28},{16,0},{20,4},{24,8},{28,12},{1,17},{... | collective-permute-start | bytes 110600 | tf_op jit(solution)/shard_map/ppermute | solution.py:26
  7.9 5.8 %collective-permute-start.4 = (bf16[144,128]{1,0:T(8,128)(2,1)S(1)}, bf16[144,128]{1,0:T(8,128)(2,1)S(1)}, u32[]{:S(2)}, u32[]{:S(2)}) collective-permute-start(bf16[144,128]{1,0:T(8,128)(2,1)S(1)} %pad_maximum_fusion.4), channel_id=1, source_target_pairs={{0,24},{4,28},{8,16},{12,20},{16,8},{20,12},{24,0},{28,4},{1,25},{... | collective-permute-start | bytes 110600 | tf_op jit(solution)/shard_map/ppermute | solution.py:26
  8.0 12.0 %copy-start.1 = (bf16[128,256]{1,0:T(8,128)(2,1)S(1)}, bf16[128,256]{1,0:T(8,128)(2,1)}, u32[]{:S(2)}) copy-start(bf16[128,256]{1,0:T(8,128)(2,1)} %qm_ref.1) | copy-start | bytes 196612
  8.0 12.0 %copy-start.2 = (bf16[128,256]{1,0:T(8,128)(2,1)S(1)}, bf16[128,256]{1,0:T(8,128)(2,1)}, u32[]{:S(2)}) copy-start(bf16[128,256]{1,0:T(8,128)(2,1)} %gm_ref.1) | copy-start | bytes 196612
  8.0 12.0 %copy-start.3 = (s32[128]{0:T(128)S(1)}, s32[128]{0:T(128)}, u32[]{:S(2)}) copy-start(s32[128]{0:T(128)} %param.12) | copy-start | bytes 1540
  8.0 12.0 %copy-start.4 = (s32[128]{0:T(128)S(1)}, s32[128]{0:T(128)}, u32[]{:S(2)}) copy-start(s32[128]{0:T(128)} %param.13) | copy-start | bytes 1540
  8.0 5.7 %collective-permute-start.5 = (bf16[2,144,128]{2,1,0:T(8,128)(2,1)S(1)}, bf16[2,144,128]{2,1,0:T(8,128)(2,1)S(1)}, u32[]{:S(2)}, u32[]{:S(2)}) collective-permute-start(bf16[2,144,128]{2,1,0:T(8,128)(2,1)S(1)} %pad_maximum_fusion.2), channel_id=1, source_target_pairs={{0,4},{4,0},{8,12},{12,8},{16,20},{20,16},{24,28},{28,24},{1,5},{5... | collective-permute-start | bytes 221192 | tf_op jit(solution)/shard_map/ppermute | solution.py:26
  13.7 8.7 %collective-permute-start.9 = (bf16[256,4096]{1,0:T(8,128)(2,1)S(1)}, bf16[256,4096]{1,0:T(8,128)(2,1)S(1)}, u32[]{:S(2)}, u32[]{:S(2)}) collective-permute-start(bf16[256,4096]{1,0:T(8,128)(2,1)S(1)} %get-tuple-element.30), channel_id=1, source_target_pairs={{0,1},{1,0},{2,3},{3,2},{4,5},{5,4},{6,7},{7,6},{8,9},{9,8},{10,11... | collective-permute-start | bytes 6291464 | tf_op jit(solution)/shard_map/ppermute | solution.py:26
  13.8 4.7 %collective-permute-start.7 = (bf16[2,144,128]{2,1,0:T(8,128)(2,1)S(1)}, bf16[2,144,128]{2,1,0:T(8,128)(2,1)S(1)}, u32[]{:S(2)}, u32[]{:S(2)}) collective-permute-start(bf16[2,144,128]{2,1,0:T(8,128)(2,1)S(1)} %pad_maximum_fusion.1), channel_id=1, source_target_pairs={{0,4},{4,0},{8,12},{12,8},{16,20},{20,16},{24,28},{28,24},{1,5},{5... | collective-permute-start | bytes 221192 | tf_op jit(solution)/shard_map/ppermute | solution.py:26
  15.4 3.2 %collective-permute-start.6 = (bf16[4,144,128]{2,1,0:T(8,128)(2,1)S(1)}, bf16[4,144,128]{2,1,0:T(8,128)(2,1)S(1)}, u32[]{:S(2)}, u32[]{:S(2)}) collective-permute-start(bf16[4,144,128]{2,1,0:T(8,128)(2,1)S(1)} %pad_maximum_fusion.refs_0_), channel_id=1, source_target_pairs={{0,1},{1,0},{2,3},{3,2},{4,5},{5,4},{6,7},{7,6},{8,9},{9,8},{10,11... | collective-permute-start | bytes 442376 | tf_op jit(solution)/shard_map/ppermute | solution.py:26
  18.5 1.4 %collective-permute-start.8 = (bf16[4,144,128]{2,1,0:T(8,128)(2,1)S(1)}, bf16[4,144,128]{2,1,0:T(8,128)(2,1)S(1)}, u32[]{:S(2)}, u32[]{:S(2)}) collective-permute-start(bf16[4,144,128]{2,1,0:T(8,128)(2,1)S(1)} %constant_dynamic-update-slice_fusion.refs_2_), channel_id=1, source_target_pairs={{0,1},{1,0},{2,3},{3,2},{4,5},{5,4},{6,7},{7,6},{8,9},{9,8},{10,11... | collective-permute-start | bytes 442376 | tf_op jit(solution)/shard_map/ppermute | solution.py:26
  23.2 5.6 %collective-permute-start.10 = (bf16[4,128,128]{2,1,0:T(8,128)(2,1)S(1)}, bf16[4,128,128]{2,1,0:T(8,128)(2,1)S(1)}, u32[]{:S(2)}, u32[]{:S(2)}) collective-permute-start(bf16[4,128,128]{2,1,0:T(8,128)(2,1)S(1)} %slice.26), channel_id=1, source_target_pairs={{0,4},{4,0},{8,12},{12,8},{16,20},{20,16},{24,28},{28,24},{1,5},{5... | collective-permute-start | bytes 393224 | tf_op jit(solution)/shard_map/ppermute | solution.py:26
  24.7 26.3 %collective-permute-start.16 = (bf16[128,4096]{1,0:T(8,128)(2,1)S(1)}, bf16[128,4096]{1,0:T(8,128)(2,1)S(1)}, u32[]{:S(2)}, u32[]{:S(2)}) collective-permute-start(bf16[128,4096]{1,0:T(8,128)(2,1)S(1)} %product.1), channel_id=1, source_target_pairs={{0,2},{1,3},{2,0},{3,1},{4,6},{5,7},{6,4},{7,5},{8,10},{9,11},{10,... | collective-permute-start | bytes 3145736 | tf_op jit(solution)/shard_map/ppermute | solution.py:26
  28.8 4.5 %collective-permute-start.11 = (bf16[128,128]{1,0:T(8,128)(2,1)S(1)}, bf16[128,128]{1,0:T(8,128)(2,1)S(1)}, u32[]{:S(2)}, u32[]{:S(2)}) collective-permute-start(bf16[128,128]{1,0:T(8,128)(2,1)S(1)} %get-tuple-element.41), channel_id=1, source_target_pairs={{0,8},{4,12},{8,0},{12,4},{16,24},{20,28},{24,16},{28,20},{1,9},{5... | collective-permute-start | bytes 98312 | tf_op jit(solution)/shard_map/ppermute | solution.py:26
  28.9 5.1 %collective-permute-start.12 = (bf16[128,128]{1,0:T(8,128)(2,1)S(1)}, bf16[128,128]{1,0:T(8,128)(2,1)S(1)}, u32[]{:S(2)}, u32[]{:S(2)}) collective-permute-start(bf16[128,128]{1,0:T(8,128)(2,1)S(1)} %get-tuple-element.43), channel_id=1, source_target_pairs={{0,16},{4,20},{8,24},{12,28},{16,0},{20,4},{24,8},{28,12},{1,17},{... | collective-permute-start | bytes 98312 | tf_op jit(solution)/shard_map/ppermute | solution.py:26
  31.9 5.7 %collective-permute-start.13 = (bf16[128,128]{1,0:T(8,128)(2,1)S(1)}, bf16[128,128]{1,0:T(8,128)(2,1)S(1)}, u32[]{:S(2)}, u32[]{:S(2)}) collective-permute-start(bf16[128,128]{1,0:T(8,128)(2,1)S(1)} %get-tuple-element.42), channel_id=1, source_target_pairs={{0,24},{4,28},{8,16},{12,20},{16,8},{20,12},{24,0},{28,4},{1,25},{... | collective-permute-start | bytes 98312 | tf_op jit(solution)/shard_map/ppermute | solution.py:26
  37.6 1.3 %collective-permute-start.14 = (bf16[128,128]{1,0:T(8,128)(2,1)S(1)}, bf16[128,128]{1,0:T(8,128)(2,1)S(1)}, u32[]{:S(2)}, u32[]{:S(2)}) collective-permute-start(bf16[128,128]{1,0:T(8,128)(2,1)S(1)} %fusion.3), channel_id=1, source_target_pairs={{0,1},{1,0},{2,3},{3,2},{4,5},{5,4},{6,7},{7,6},{8,9},{9,8},{10,11... | collective-permute-start | bytes 98312 | tf_op jit(solution)/shard_map/ppermute | solution.py:26
  41.7 9.4 %copy-start = (bf16[256,4096]{1,0:T(8,128)(2,1)S(1)}, bf16[256,4096]{1,0:T(8,128)(2,1)}, u32[]{:S(2)}) copy-start(bf16[256,4096]{1,0:T(8,128)(2,1)} %w_ref.3) | copy-start | bytes 6291460
  42.4 8.6 %collective-permute-start.17 = (bf16[128,2048]{1,0:T(8,128)(2,1)S(1)}, bf16[128,2048]{1,0:T(8,128)(2,1)S(1)}, u32[]{:S(2)}, u32[]{:S(2)}) collective-permute-start(bf16[128,2048]{1,0:T(8,128)(2,1)S(1)} %get-tuple-element.35), channel_id=1, source_target_pairs={{0,1},{1,0},{2,3},{3,2},{4,5},{5,4},{6,7},{7,6},{8,9},{9,8},{10,11... | collective-permute-start | bytes 1572872 | tf_op jit(solution)/shard_map/ppermute | solution.py:26
  42.7 8.4 %collective-permute-start.18 = (bf16[128,2048]{1,0:T(8,128)(2,1)S(1)}, bf16[128,2048]{1,0:T(8,128)(2,1)S(1)}, u32[]{:S(2)}, u32[]{:S(2)}) collective-permute-start(bf16[128,2048]{1,0:T(8,128)(2,1)S(1)} %get-tuple-element.36), channel_id=1, source_target_pairs={{0,1},{1,0},{2,3},{3,2},{4,5},{5,4},{6,7},{7,6},{8,9},{9,8},{10,11... | collective-permute-start | bytes 1572872 | tf_op jit(solution)/shard_map/ppermute | solution.py:26
  43.0 8.0 %collective-permute-start.15 = (bf16[128,256]{1,0:T(8,128)(2,1)S(1)}, bf16[128,256]{1,0:T(8,128)(2,1)S(1)}, u32[]{:S(2)}, u32[]{:S(2)}) collective-permute-start(bf16[128,256]{1,0:T(8,128)(2,1)S(1)} %pad_maximum_fusion.3.refs_0_.kv_ref), channel_id=1, source_target_pairs={{0,2},{1,3},{2,0},{3,1},{4,6},{5,7},{6,4},{7,5},{8,10},{9,11},{10,... | collective-permute-start | bytes 196616 | tf_op jit(solution)/shard_map/ppermute | solution.py:26

commit v18 on v17

--- a/solution.py
+++ b/solution.py
@@ -11,6 +11,7 @@
 RUN = 64
 META_ROWS = 16
 TILES = 4
+HALVES = 2
 GIVES = 2
 ANY = pl.BlockSpec(memory_space=pl.ANY)
 HBM = pl.BlockSpec(memory_space=pltpu.HBM)
@@ -180,27 +181,30 @@
     )
 
 
-def product_kernel(first, dq_ref, wm_ref, wo_ref, out_ref):
-    depth = wm_ref.shape[0]
-    at = slice(first, first + out_ref.shape[1])
-    acc = dot(dq_ref[:, 0:depth], wm_ref[:, at], ((1,), (0,)))
-    acc = acc + dot(dq_ref[:, depth:], wo_ref[:, at], ((1,), (0,)))
-    out_ref[...] = acc.astype(out_ref.dtype)
-
-
-def product(dq, w_mine, w_other, first, width, dtype):
+def product_kernel(dq_ref, *refs):
+    out_ref = refs[-1]
+    for i in range(HALVES):
+        mine_ref, other_ref = refs[i], refs[HALVES + i]
+        depth, width = mine_ref.shape
+        acc = dot(dq_ref[:, 0:depth], mine_ref[...], ((1,), (0,)))
+        acc = acc + dot(dq_ref[:, depth:], other_ref[...], ((1,), (0,)))
+        out_ref[:, i * width : (i + 1) * width] = acc.astype(out_ref.dtype)
+
+
+def product(dq, w_mine, w_other, dtype):
     rows, depth = dq.shape
-    return pl.pallas_call(
-        functools.partial(product_kernel, first),
-        out_shape=jax.ShapeDtypeStruct((rows, width), dtype),
-        in_specs=[pl.BlockSpec()] * 3,
+    share = HALVES * w_mine[0].shape[1]
+    return pl.pallas_call(
+        product_kernel,
+        out_shape=jax.ShapeDtypeStruct((rows, share), dtype),
+        in_specs=[pl.BlockSpec()] * (1 + 2 * HALVES),
         out_specs=pl.BlockSpec(),
         compiler_params=params(),
         cost_estimate=pl.CostEstimate(
-            flops=2 * rows * depth * width, bytes_accessed=2 * depth * width, transcendentals=0
+            flops=2 * rows * depth * share, bytes_accessed=2 * depth * share, transcendentals=0
         ),
         name="product",
-    )(dq, w_mine, w_other)
+    )(dq, *w_mine, *w_other)
 
 
 def own_kernel(dq_ref, wn_ref, wo_ref, acc_ref, *give_refs):
@@ -287,18 +291,25 @@
     early = (half + 1) // 2
     z_early, z_late = jnp.stack(along_z[:early]), jnp.stack(along_z[early:])
     x_early = swapped(z_early, "ctx", 1)
-    far_send = column_block(w_query, head ^ 3, share, z_early)
-    far_mine = column_block(w_query, head ^ 2, share, z_early)
-    z_late, x_early, far_send, far_mine = lax.optimization_barrier((z_late, x_early, far_send, far_mine))
+    z_late, x_early = lax.optimization_barrier((z_late, x_early))
     x_late = swapped(z_late, "ctx", 1)
-    far_other = swapped(far_send, "head", 1)
     here_z = jnp.concatenate([z_early, z_late])
     there_z = swapped(here_z, "head", 1)
+
+    def halves(block):
+        return [column_block(w_query, block * HALVES + i, share // HALVES, z_late) for i in range(HALVES)]
+
+    x_late, there_z, *far = lax.optimization_barrier((x_late, there_z, *halves(head ^ 3), *halves(head ^ 2)))
+    far_send, far_mine = far[:HALVES], far[HALVES:]
     here_x = jnp.concatenate([x_early, x_late])
-    pieces = (here_z, there_z, here_x, swapped(here_x, "head", 1))
+    there_x = swapped(here_x, "head", 1)
+    far_other = [swapped(far_send[0], "head", 1)]
+    there_x, *rest = lax.optimization_barrier((there_x, *far_send[1:]))
+    far_other += [swapped(one, "head", 1) for one in rest]
+    pieces = (here_z, there_z, here_x, there_x)
     dq, back = attention(core, positions, doc_ids, queries, q_other, dout, g_other, pieces)
 
-    part = product(dq, far_mine, far_other, 0, share, jnp.bfloat16)
+    part = product(dq, far_mine, far_other, jnp.bfloat16)
     far = swapped(part, "head", 2)
 
     back, part = lax.optimization_barrier((back, part))

time: 52.7 us -> 53.1 us (level)
    ppermute x19 -> x20, starting transfers between devices: 19.6 us -> 20 us  [swapped(): lax.ppermute(value, axis, [(source, source ^ bits) for source in range(co...]
    ppermute x19 -> x20, waiting for transfers between devices: 19.9 us -> 20 us  [swapped(): lax.ppermute(value, axis, [(source, source ^ bits) for source in range(co...]
  transfers between devices with their start and end apart: 19 -> 20, of which waited for: 8 -> 10; matrix products, arithmetic and copies ran while one was open for 9% -> 9% of each run, Pallas kernels for 11% -> 11%
where the time goes in v18:
time: 53.1 us; the launch traced here: 52.9 us
  starting transfers between devices  20 us (38%)
  waiting for transfers between devices  20 us (38%)
  Pallas kernels  8.03 us (15%)
  local copies, waits for them, and re-layouts  3.49 us (7%)
  other arithmetic  1.17 us (2%)
    ppermute x20, waiting for transfers between devices, swapped(): lax.ppermute(value, axis, [(source, source ^ bits) for source in range(co...  20 us
    ppermute x20, starting transfers between devices, swapped(): lax.ppermute(value, axis, [(source, source ^ bits) for source in range(co...  20 us
    pallas_call x1, Pallas kernels, carve(): pl.pallas_call(carve_kernel, out_shape=[block] * count, in_specs=[SMEM, H...  2.76 us
    dynamic_slice x1, local copies, waits for them, and re-layouts, column_block(): return lax.dynamic_slice_in_dim(w_query, block * share, share, axis=1)  2.68 us
    pallas_call x1, Pallas kernels, attention(): pl.pallas_call(attention_kernel, out_shape=[jax.ShapeDtypeStruct((rows, 2...  2.37 us
    pallas_call x1, Pallas kernels, finish(): pl.pallas_call(finish_kernel, out_shape=jax.ShapeDtypeStruct((rows, share...  1.43 us
  transfers between devices with their start and end apart: 20, of which 10 were waited for; matrix products, arithmetic and copies ran while one was open for 9% of the time, Pallas kernels for 11%

profile of v18, /device:TPU:0, one launch (start us, length us, event | category | flops | bytes accessed | tf_op | source)
XLA Modules:
  0.0 52.9 jit_solution(17263248979677887123)
XLA Ops:
  0.0 0.5 collective-permute-start
  0.5 0.7 %reshape.19 = s32[2,64]{1,0:T(2,128)S(1)} reshape(s32[128]{0:T(128)} %param.12) | data formatting | bytes 1024 | tf_op jit(solution)/shard_map/reshape | solution.py:45
  1.4 0.8 %broadcast_select_fusion = bf16[128,128]{1,0:T(8,128)(2,1)S(1)} fusion(bf16[128,128]{1,0:T(8,128)(2,1)} %param.9, bf16[128,128]{1,0:T(8,128)(2,1)} %param.10, pred[]{:T(512)} %bitcast.3), kind=kLoop, calls=%fused_computation.14 | loop fusion | flops 16384 | bytes 98305 | tf_op jit(solution)/shard_map/jit(_where)/select_n | solution.py:44
  2.3 3.1 %collective-permute-start.2 = (bf16[144,128]{1,0:T(8,128)(2,1)S(1)}, bf16[144,128]{1,0:T(8,128)(2,1)S(1)}, u32[]{:S(2)}, u32[]{:S(2)}) collective-permute-start(bf16[144,128]{1,0:T(8,128)(2,1)S(1)} %pad_maximum_fusion.4), channel_id=1, source_target_pairs={{0,8},{4,12},{8,0},{12,4},{16,24},{20,28},{24,16},{28,20},{1,9},{5... | collective-permute-start | bytes 110600 | tf_op jit(solution)/shard_map/ppermute | solution.py:27
  5.4 2.6 %collective-permute-start.3 = (bf16[144,128]{1,0:T(8,128)(2,1)S(1)}, bf16[144,128]{1,0:T(8,128)(2,1)S(1)}, u32[]{:S(2)}, u32[]{:S(2)}) collective-permute-start(bf16[144,128]{1,0:T(8,128)(2,1)S(1)} %pad_maximum_fusion.4), channel_id=1, source_target_pairs={{0,16},{4,20},{8,24},{12,28},{16,0},{20,4},{24,8},{28,12},{1,17},{... | collective-permute-start | bytes 110600 | tf_op jit(solution)/shard_map/ppermute | solution.py:27
  8.0 1.8 %collective-permute-start.5 = (bf16[2,144,128]{2,1,0:T(8,128)(2,1)S(1)}, bf16[2,144,128]{2,1,0:T(8,128)(2,1)S(1)}, u32[]{:S(2)}, u32[]{:S(2)}) collective-permute-start(bf16[2,144,128]{2,1,0:T(8,128)(2,1)S(1)} %pad_maximum_fusion.2), channel_id=1, source_target_pairs={{0,4},{4,0},{8,12},{12,8},{16,20},{20,16},{24,28},{28,24},{1,5},{5... | collective-permute-start | bytes 221192 | tf_op jit(solution)/shard_map/ppermute | solution.py:27
  9.7 1.2 %collective-permute-done.3 = bf16[144,128]{1,0:T(8,128)(2,1)S(1)} collective-permute-done((bf16[144,128]{1,0:T(8,128)(2,1)S(1)}, bf16[144,128]{1,0:T(8,128)(2,1)S(1)}, u32[]{:S(2)}, u32[]{:S(2)}) %collective-permute-start.3) | collective-permute-done | bytes 36896 | tf_op jit(solution)/shard_map/ppermute | solution.py:27
  10.9 2.8 %collective-permute-done.4 = bf16[144,128]{1,0:T(8,128)(2,1)S(1)} collective-permute-done((bf16[144,128]{1,0:T(8,128)(2,1)S(1)}, bf16[144,128]{1,0:T(8,128)(2,1)S(1)}, u32[]{:S(2)}, u32[]{:S(2)}) %collective-permute-start.4) | collective-permute-done | bytes 36896 | tf_op jit(solution)/shard_map/ppermute | solution.py:27
  13.8 1.6 %collective-permute-start.6 = (bf16[2,144,128]{2,1,0:T(8,128)(2,1)S(1)}, bf16[2,144,128]{2,1,0:T(8,128)(2,1)S(1)}, u32[]{:S(2)}, u32[]{:S(2)}) collective-permute-start(bf16[2,144,128]{2,1,0:T(8,128)(2,1)S(1)} %pad_maximum_fusion.1), channel_id=1, source_target_pairs={{0,4},{4,0},{8,12},{12,8},{16,20},{20,16},{24,28},{28,24},{1,5},{5... | collective-permute-start | bytes 221192 | tf_op jit(solution)/shard_map/ppermute | solution.py:27
  15.4 2.7 %constant_dynamic-slice_fusion = (bf16[256,2048]{1,0:T(8,128)(2,1)S(1)}, bf16[256,2048]{1,0:T(8,128)(2,1)S(1)}, bf16[256,2048]{1,0:T(8,128)(2,1)S(1)}, bf16[256,2048]{1,0:T(8,128)(2,1)S(1)}) fusion(bf16[256,16384]{1,0:T(8,128)(2,1)} %w_ref.2, s32[]{:T(128)S(6)} %select_n.26, s32[]{:T(128)S(6)} %select_n.25, s32[]{:T(128)S(6)} %select_n.24, s32[]{:T(128)S(6)} %select_n.23), kind=kLoop, calls=%fused_computation.22 | loop fusion | bytes 8388624 | tf_op jit(solution)/shard_map/dynamic_slice | solution.py:52
  18.1 0.2 collective-permute-done.6
  18.2 0.4 collective-permute-start.8
  18.8 0.9 %collective-permute-done.8.refs_3_ = bf16[4,144,128]{2,1,0:T(8,128)(2,1)S(1)} collective-permute-done((bf16[4,144,128]{2,1,0:T(8,128)(2,1)S(1)}, bf16[4,144,128]{2,1,0:T(8,128)(2,1)S(1)}, u32[]{:S(2)}, u32[]{:S(2)}) %collective-permute-start.8) | collective-permute-done | bytes 147488 | tf_op jit(solution)/shard_map/ppermute | solution.py:27
  19.7 0.4 collective-permute-start.10
  20.1 2.4 %attention.1 = (bf16[128,512]{1,0:T(8,128)(2,1)S(1)}, bf16[8,128,128]{2,1,0:T(8,128)(2,1)S(1)}) custom-call(s32[1]{0:T(128)} %bitcast.core_ref, s32[1,128]{1,0:T(1,128)S(1)} %bitcast.26, s32[1,128]{1,0:T(1,128)S(1)} %bitcast.27, bf16[128,256]{1,0:T(8,128)(2,1)S(1)} %copy-done.1, bf16[128,256]{1,0:T(8,128)(2,1)S(1)} %collective-permute-done.qo_ref, ...), custom_call_target="tpu_custom_call" | custom-call | flops 671088640 | bytes 1048576 | tf_op jit(solution)/shard_map/attention/pallas_call | solution.py:163
  22.5 0.4 collective-permute-done.10.refs_3_
  22.8 0.7 %product.1 = bf16[128,4096]{1,0:T(8,128)(2,1)S(1)} custom-call(bf16[128,512]{1,0:T(8,128)(2,1)S(1)} %get-tuple-element.38.dq_ref, bf16[256,2048]{1,0:T(8,128)(2,1)S(1)} %get-tuple-element.39.refs_0_, bf16[256,2048]{1,0:T(8,128)(2,1)S(1)} %get-tuple-element.40.refs_1_, bf16[256,2048]{1,0:T(8,128)(2,1)S(1)} %collective-permute-done.9.refs_2_, ...), custom_call_target="tpu_custom_call" | custom-call | flops 536870912 | bytes 4194304 | tf_op jit(solution)/shard_map/product/pallas_call | solution.py:197
  23.6 1.4 %collective-permute-start.11 = (bf16[4,128,128]{2,1,0:T(8,128)(2,1)S(1)}, bf16[4,128,128]{2,1,0:T(8,128)(2,1)S(1)}, u32[]{:S(2)}, u32[]{:S(2)}) collective-permute-start(bf16[4,128,128]{2,1,0:T(8,128)(2,1)S(1)} %slice.26), channel_id=1, source_target_pairs={{0,4},{4,0},{8,12},{12,8},{16,20},{20,16},{24,28},{28,24},{1,5},{5... | collective-permute-start | bytes 393224 | tf_op jit(solution)/shard_map/ppermute | solution.py:27
  25.0 1.5 %collective-permute-start.17 = (bf16[128,4096]{1,0:T(8,128)(2,1)S(1)}, bf16[128,4096]{1,0:T(8,128)(2,1)S(1)}, u32[]{:S(2)}, u32[]{:S(2)}) collective-permute-start(bf16[128,4096]{1,0:T(8,128)(2,1)S(1)} %product.1), channel_id=1, source_target_pairs={{0,2},{1,3},{2,0},{3,1},{4,6},{5,7},{6,4},{7,5},{8,10},{9,11},{10,... | collective-permute-start | bytes 3145736 | tf_op jit(solution)/shard_map/ppermute | solution.py:27
  26.5 2.8 %collective-permute-done.11 = bf16[4,128,128]{2,1,0:T(8,128)(2,1)S(1)} collective-permute-done((bf16[4,128,128]{2,1,0:T(8,128)(2,1)S(1)}, bf16[4,128,128]{2,1,0:T(8,128)(2,1)S(1)}, u32[]{:S(2)}, u32[]{:S(2)}) %collective-permute-start.11) | collective-permute-done | bytes 131104 | tf_op jit(solution)/shard_map/ppermute | solution.py:27
  29.4 3.0 %collective-permute-start.13 = (bf16[128,128]{1,0:T(8,128)(2,1)S(1)}, bf16[128,128]{1,0:T(8,128)(2,1)S(1)}, u32[]{:S(2)}, u32[]{:S(2)}) collective-permute-start(bf16[128,128]{1,0:T(8,128)(2,1)S(1)} %get-tuple-element.57), channel_id=1, source_target_pairs={{0,16},{4,20},{8,24},{12,28},{16,0},{20,4},{24,8},{28,12},{1,17},{... | collective-permute-start | bytes 98312 | tf_op jit(solution)/shard_map/ppermute | solution.py:27
  32.4 1.3 %collective-permute-start.14 = (bf16[128,128]{1,0:T(8,128)(2,1)S(1)}, bf16[128,128]{1,0:T(8,128)(2,1)S(1)}, u32[]{:S(2)}, u32[]{:S(2)}) collective-permute-start(bf16[128,128]{1,0:T(8,128)(2,1)S(1)} %get-tuple-element.56), channel_id=1, source_target_pairs={{0,24},{4,28},{8,16},{12,20},{16,8},{20,12},{24,0},{28,4},{1,25},{... | collective-permute-start | bytes 98312 | tf_op jit(solution)/shard_map/ppermute | solution.py:27
  33.8 0.8 %collective-permute-done.13 = bf16[128,128]{1,0:T(8,128)(2,1)S(1)} collective-permute-done((bf16[128,128]{1,0:T(8,128)(2,1)S(1)}, bf16[128,128]{1,0:T(8,128)(2,1)S(1)}, u32[]{:S(2)}, u32[]{:S(2)}) %collective-permute-start.13) | collective-permute-done | bytes 32800 | tf_op jit(solution)/shard_map/ppermute | solution.py:27
  34.6 3.5 %collective-permute-done.14 = bf16[128,128]{1,0:T(8,128)(2,1)S(1)} collective-permute-done((bf16[128,128]{1,0:T(8,128)(2,1)S(1)}, bf16[128,128]{1,0:T(8,128)(2,1)S(1)}, u32[]{:S(2)}, u32[]{:S(2)}) %collective-permute-start.14) | collective-permute-done | bytes 32800 | tf_op jit(solution)/shard_map/ppermute | solution.py:27
  38.3 1.1 %collective-permute-done.15 = bf16[128,128]{1,0:T(8,128)(2,1)S(1)} collective-permute-done((bf16[128,128]{1,0:T(8,128)(2,1)S(1)}, bf16[128,128]{1,0:T(8,128)(2,1)S(1)}, u32[]{:S(2)}, u32[]{:S(2)}) %collective-permute-start.15) | collective-permute-done | bytes 32800 | tf_op jit(solution)/shard_map/ppermute | solution.py:27
  39.5 2.8 %carve.1 = (bf16[256,4096]{1,0:T(8,128)(2,1)S(1)}, bf16[256,4096]{1,0:T(8,128)(2,1)S(1)}) custom-call(s32[2]{0:T(128)S(1)} %pad_add_fusion.block_ref, bf16[256,16384]{1,0:T(8,128)(2,1)} %w_ref.2, bf16[128,256]{1,0:T(8,128)(2,1)S(1)} %pad_maximum_fusion.3.refs_0_.kv_ref), custom_call_target="tpu_custom_call" | custom-call | tf_op jit(solution)/shard_map/carve/pallas_call | solution.py:74
  42.2 0.7 %own.1 = (f32[128,4096]{1,0:T(8,128)S(1)}, bf16[128,2048]{1,0:T(8,128)(2,1)S(1)}, bf16[128,2048]{1,0:T(8,128)(2,1)S(1)}) custom-call(bf16[128,512]{1,0:T(8,128)(2,1)S(1)} %get-tuple-element.38.dq_ref, bf16[256,4096]{1,0:T(8,128)(2,1)S(1)} %get-tuple-element.44.wn_ref, bf16[256,4096]{1,0:T(8,128)(2,1)S(1)} %get-tuple-element.45.wo_ref), custom_call_target="tpu_custom_call" | custom-call | tf_op jit(solution)/shard_map/own/pallas_call | solution.py:222
  43.0 0.2 collective-permute-start.18
  43.2 0.4 collective-permute-start.19
  43.6 1.5 %collective-permute-start.16 = (bf16[128,256]{1,0:T(8,128)(2,1)S(1)}, bf16[128,256]{1,0:T(8,128)(2,1)S(1)}, u32[]{:S(2)}, u32[]{:S(2)}) collective-permute-start(bf16[128,256]{1,0:T(8,128)(2,1)S(1)} %pad_maximum_fusion.3.refs_0_.kv_ref), channel_id=1, source_target_pairs={{0,2},{1,3},{2,0},{3,1},{4,6},{5,7},{6,4},{7,5},{8,10},{9,11},{10,... | collective-permute-start | bytes 196616 | tf_op jit(solution)/shard_map/ppermute | solution.py:27
  45.1 6.4 %collective-permute-done.16.kv_far_ref = bf16[128,256]{1,0:T(8,128)(2,1)S(1)} collective-permute-done((bf16[128,256]{1,0:T(8,128)(2,1)S(1)}, bf16[128,256]{1,0:T(8,128)(2,1)S(1)}, u32[]{:S(2)}, u32[]{:S(2)}) %collective-permute-start.16) | collective-permute-done | bytes 65568 | tf_op jit(solution)/shard_map/ppermute | solution.py:27
  51.5 1.4 %finish.1 = bf16[128,4096]{1,0:T(8,128)(2,1)} custom-call(s32[1]{0:T(128)} %bitcast.core_ref, bf16[128,256]{1,0:T(8,128)(2,1)S(1)} %pad_maximum_fusion.3.refs_0_.kv_ref, bf16[128,256]{1,0:T(8,128)(2,1)S(1)} %collective-permute-done.16.kv_far_ref, bf16[256,4096]{1,0:T(8,128)(2,1)S(1)} %copy-done, f32[128,4096]{1,0:T(8,128)S(1)} %get-tuple-element.46.acc_ref, ...), custom_call_target="tpu_custom_call" | custom-call | flops 268435456 | bytes 5242880 | tf_op jit(solution)/shard_map/finish/pallas_call | solution.py:265
  (40 shorter events, 0.8 us)
Async XLA Ops:
  0.0 2.2 %collective-permute-start = (bf16[128,256]{1,0:T(8,128)(2,1)}, bf16[128,256]{1,0:T(8,128)(2,1)S(1)}, u32[]{:S(2)}, u32[]{:S(2)}) collective-permute-start(bf16[128,256]{1,0:T(8,128)(2,1)} %qm_ref.1), channel_id=1, source_target_pairs={{0,1},{1,0},{2,3},{3,2},{4,5},{5,4},{6,7},{7,6},{8,9},{9,8},{10,11... | collective-permute-start | bytes 196616 | tf_op jit(solution)/shard_map/ppermute | solution.py:27
  0.5 1.8 %collective-permute-start.1 = (bf16[128,256]{1,0:T(8,128)(2,1)}, bf16[128,256]{1,0:T(8,128)(2,1)S(1)}, u32[]{:S(2)}, u32[]{:S(2)}) collective-permute-start(bf16[128,256]{1,0:T(8,128)(2,1)} %gm_ref.1), channel_id=1, source_target_pairs={{0,1},{1,0},{2,3},{3,2},{4,5},{5,4},{6,7},{7,6},{8,9},{9,8},{10,11... | collective-permute-start | bytes 196616 | tf_op jit(solution)/shard_map/ppermute | solution.py:27
  2.3 5.7 %collective-permute-start.2 = (bf16[144,128]{1,0:T(8,128)(2,1)S(1)}, bf16[144,128]{1,0:T(8,128)(2,1)S(1)}, u32[]{:S(2)}, u32[]{:S(2)}) collective-permute-start(bf16[144,128]{1,0:T(8,128)(2,1)S(1)} %pad_maximum_fusion.4), channel_id=1, source_target_pairs={{0,8},{4,12},{8,0},{12,4},{16,24},{20,28},{24,16},{28,20},{1,9},{5... | collective-permute-start | bytes 110600 | tf_op jit(solution)/shard_map/ppermute | solution.py:27
  5.4 5.6 %collective-permute-start.3 = (bf16[144,128]{1,0:T(8,128)(2,1)S(1)}, bf16[144,128]{1,0:T(8,128)(2,1)S(1)}, u32[]{:S(2)}, u32[]{:S(2)}) collective-permute-start(bf16[144,128]{1,0:T(8,128)(2,1)S(1)} %pad_maximum_fusion.4), channel_id=1, source_target_pairs={{0,16},{4,20},{8,24},{12,28},{16,0},{20,4},{24,8},{28,12},{1,17},{... | collective-permute-start | bytes 110600 | tf_op jit(solution)/shard_map/ppermute | solution.py:27
  7.9 5.8 %collective-permute-start.4 = (bf16[144,128]{1,0:T(8,128)(2,1)S(1)}, bf16[144,128]{1,0:T(8,128)(2,1)S(1)}, u32[]{:S(2)}, u32[]{:S(2)}) collective-permute-start(bf16[144,128]{1,0:T(8,128)(2,1)S(1)} %pad_maximum_fusion.4), channel_id=1, source_target_pairs={{0,24},{4,28},{8,16},{12,20},{16,8},{20,12},{24,0},{28,4},{1,25},{... | collective-permute-start | bytes 110600 | tf_op jit(solution)/shard_map/ppermute | solution.py:27
  8.0 5.8 %collective-permute-start.5 = (bf16[2,144,128]{2,1,0:T(8,128)(2,1)S(1)}, bf16[2,144,128]{2,1,0:T(8,128)(2,1)S(1)}, u32[]{:S(2)}, u32[]{:S(2)}) collective-permute-start(bf16[2,144,128]{2,1,0:T(8,128)(2,1)S(1)} %pad_maximum_fusion.2), channel_id=1, source_target_pairs={{0,4},{4,0},{8,12},{12,8},{16,20},{20,16},{24,28},{28,24},{1,5},{5... | collective-permute-start | bytes 221192 | tf_op jit(solution)/shard_map/ppermute | solution.py:27
  13.8 6.3 %copy-start.1 = (bf16[128,256]{1,0:T(8,128)(2,1)S(1)}, bf16[128,256]{1,0:T(8,128)(2,1)}, u32[]{:S(2)}) copy-start(bf16[128,256]{1,0:T(8,128)(2,1)} %qm_ref.1) | copy-start | bytes 196612
  13.8 6.3 %copy-start.2 = (bf16[128,256]{1,0:T(8,128)(2,1)S(1)}, bf16[128,256]{1,0:T(8,128)(2,1)}, u32[]{:S(2)}) copy-start(bf16[128,256]{1,0:T(8,128)(2,1)} %gm_ref.1) | copy-start | bytes 196612
  13.8 6.3 %copy-start.3 = (s32[128]{0:T(128)S(1)}, s32[128]{0:T(128)}, u32[]{:S(2)}) copy-start(s32[128]{0:T(128)} %param.12) | copy-start | bytes 1540
  13.8 6.3 %copy-start.4 = (s32[128]{0:T(128)S(1)}, s32[128]{0:T(128)}, u32[]{:S(2)}) copy-start(s32[128]{0:T(128)} %param.13) | copy-start | bytes 1540
  13.8 4.4 %collective-permute-start.6 = (bf16[2,144,128]{2,1,0:T(8,128)(2,1)S(1)}, bf16[2,144,128]{2,1,0:T(8,128)(2,1)S(1)}, u32[]{:S(2)}, u32[]{:S(2)}) collective-permute-start(bf16[2,144,128]{2,1,0:T(8,128)(2,1)S(1)} %pad_maximum_fusion.1), channel_id=1, source_target_pairs={{0,4},{4,0},{8,12},{12,8},{16,20},{20,16},{24,28},{28,24},{1,5},{5... | collective-permute-start | bytes 221192 | tf_op jit(solution)/shard_map/ppermute | solution.py:27
  15.4 2.9 %collective-permute-start.7 = (bf16[4,144,128]{2,1,0:T(8,128)(2,1)S(1)}, bf16[4,144,128]{2,1,0:T(8,128)(2,1)S(1)}, u32[]{:S(2)}, u32[]{:S(2)}) collective-permute-start(bf16[4,144,128]{2,1,0:T(8,128)(2,1)S(1)} %pad_maximum_fusion.refs_0_), channel_id=1, source_target_pairs={{0,1},{1,0},{2,3},{3,2},{4,5},{5,4},{6,7},{7,6},{8,9},{9,8},{10,11... | collective-permute-start | bytes 442376 | tf_op jit(solution)/shard_map/ppermute | solution.py:27
  18.2 1.4 %collective-permute-start.8 = (bf16[4,144,128]{2,1,0:T(8,128)(2,1)S(1)}, bf16[4,144,128]{2,1,0:T(8,128)(2,1)S(1)}, u32[]{:S(2)}, u32[]{:S(2)}) collective-permute-start(bf16[4,144,128]{2,1,0:T(8,128)(2,1)S(1)} %constant_dynamic-update-slice_fusion.refs_2_), channel_id=1, source_target_pairs={{0,1},{1,0},{2,3},{3,2},{4,5},{5,4},{6,7},{7,6},{8,9},{9,8},{10,11... | collective-permute-start | bytes 442376 | tf_op jit(solution)/shard_map/ppermute | solution.py:27
  18.7 3.8 %collective-permute-start.9 = (bf16[256,2048]{1,0:T(8,128)(2,1)S(1)}, bf16[256,2048]{1,0:T(8,128)(2,1)S(1)}, u32[]{:S(2)}, u32[]{:S(2)}) collective-permute-start(bf16[256,2048]{1,0:T(8,128)(2,1)S(1)} %get-tuple-element.41), channel_id=1, source_target_pairs={{0,1},{1,0},{2,3},{3,2},{4,5},{5,4},{6,7},{7,6},{8,9},{9,8},{10,11... | collective-permute-start | bytes 3145736 | tf_op jit(solution)/shard_map/ppermute | solution.py:27
  19.7 3.2 %collective-permute-start.10 = (bf16[256,2048]{1,0:T(8,128)(2,1)S(1)}, bf16[256,2048]{1,0:T(8,128)(2,1)S(1)}, u32[]{:S(2)}, u32[]{:S(2)}) collective-permute-start(bf16[256,2048]{1,0:T(8,128)(2,1)S(1)} %get-tuple-element.42), channel_id=1, source_target_pairs={{0,1},{1,0},{2,3},{3,2},{4,5},{5,4},{6,7},{7,6},{8,9},{9,8},{10,11... | collective-permute-start | bytes 3145736 | tf_op jit(solution)/shard_map/ppermute | solution.py:27
  23.6 5.7 %collective-permute-start.11 = (bf16[4,128,128]{2,1,0:T(8,128)(2,1)S(1)}, bf16[4,128,128]{2,1,0:T(8,128)(2,1)S(1)}, u32[]{:S(2)}, u32[]{:S(2)}) collective-permute-start(bf16[4,128,128]{2,1,0:T(8,128)(2,1)S(1)} %slice.26), channel_id=1, source_target_pairs={{0,4},{4,0},{8,12},{12,8},{16,20},{20,16},{24,28},{28,24},{1,5},{5... | collective-permute-start | bytes 393224 | tf_op jit(solution)/shard_map/ppermute | solution.py:27
  25.0 26.5 %collective-permute-start.17 = (bf16[128,4096]{1,0:T(8,128)(2,1)S(1)}, bf16[128,4096]{1,0:T(8,128)(2,1)S(1)}, u32[]{:S(2)}, u32[]{:S(2)}) collective-permute-start(bf16[128,4096]{1,0:T(8,128)(2,1)S(1)} %product.1), channel_id=1, source_target_pairs={{0,2},{1,3},{2,0},{3,1},{4,6},{5,7},{6,4},{7,5},{8,10},{9,11},{10,... | collective-permute-start | bytes 3145736 | tf_op jit(solution)/shard_map/ppermute | solution.py:27
  29.3 4.5 %collective-permute-start.12 = (bf16[128,128]{1,0:T(8,128)(2,1)S(1)}, bf16[128,128]{1,0:T(8,128)(2,1)S(1)}, u32[]{:S(2)}, u32[]{:S(2)}) collective-permute-start(bf16[128,128]{1,0:T(8,128)(2,1)S(1)} %get-tuple-element.55), channel_id=1, source_target_pairs={{0,8},{4,12},{8,0},{12,4},{16,24},{20,28},{24,16},{28,20},{1,9},{5... | collective-permute-start | bytes 98312 | tf_op jit(solution)/shard_map/ppermute | solution.py:27
  29.4 5.2 %collective-permute-start.13 = (bf16[128,128]{1,0:T(8,128)(2,1)S(1)}, bf16[128,128]{1,0:T(8,128)(2,1)S(1)}, u32[]{:S(2)}, u32[]{:S(2)}) collective-permute-start(bf16[128,128]{1,0:T(8,128)(2,1)S(1)} %get-tuple-element.57), channel_id=1, source_target_pairs={{0,16},{4,20},{8,24},{12,28},{16,0},{20,4},{24,8},{28,12},{1,17},{... | collective-permute-start | bytes 98312 | tf_op jit(solution)/shard_map/ppermute | solution.py:27
  32.4 5.7 %collective-permute-start.14 = (bf16[128,128]{1,0:T(8,128)(2,1)S(1)}, bf16[128,128]{1,0:T(8,128)(2,1)S(1)}, u32[]{:S(2)}, u32[]{:S(2)}) collective-permute-start(bf16[128,128]{1,0:T(8,128)(2,1)S(1)} %get-tuple-element.56), channel_id=1, source_target_pairs={{0,24},{4,28},{8,16},{12,20},{16,8},{20,12},{24,0},{28,4},{1,25},{... | collective-permute-start | bytes 98312 | tf_op jit(solution)/shard_map/ppermute | solution.py:27
  38.2 1.3 %collective-permute-start.15 = (bf16[128,128]{1,0:T(8,128)(2,1)S(1)}, bf16[128,128]{1,0:T(8,128)(2,1)S(1)}, u32[]{:S(2)}, u32[]{:S(2)}) collective-permute-start(bf16[128,128]{1,0:T(8,128)(2,1)S(1)} %fusion.3), channel_id=1, source_target_pairs={{0,1},{1,0},{2,3},{3,2},{4,5},{5,4},{6,7},{7,6},{8,9},{9,8},{10,11... | collective-permute-start | bytes 98312 | tf_op jit(solution)/shard_map/ppermute | solution.py:27
  42.2 9.3 %copy-start = (bf16[256,4096]{1,0:T(8,128)(2,1)S(1)}, bf16[256,4096]{1,0:T(8,128)(2,1)}, u32[]{:S(2)}) copy-start(bf16[256,4096]{1,0:T(8,128)(2,1)} %w_ref.3) | copy-start | bytes 6291460
  43.0 8.5 %collective-permute-start.18 = (bf16[128,2048]{1,0:T(8,128)(2,1)S(1)}, bf16[128,2048]{1,0:T(8,128)(2,1)S(1)}, u32[]{:S(2)}, u32[]{:S(2)}) collective-permute-start(bf16[128,2048]{1,0:T(8,128)(2,1)S(1)} %get-tuple-element.47), channel_id=1, source_target_pairs={{0,1},{1,0},{2,3},{3,2},{4,5},{5,4},{6,7},{7,6},{8,9},{9,8},{10,11... | collective-permute-start | bytes 1572872 | tf_op jit(solution)/shard_map/ppermute | solution.py:27
  43.2 8.3 %collective-permute-start.19 = (bf16[128,2048]{1,0:T(8,128)(2,1)S(1)}, bf16[128,2048]{1,0:T(8,128)(2,1)S(1)}, u32[]{:S(2)}, u32[]{:S(2)}) collective-permute-start(bf16[128,2048]{1,0:T(8,128)(2,1)S(1)} %get-tuple-element.48), channel_id=1, source_target_pairs={{0,1},{1,0},{2,3},{3,2},{4,5},{5,4},{6,7},{7,6},{8,9},{9,8},{10,11... | collective-permute-start | bytes 1572872 | tf_op jit(solution)/shard_map/ppermute | solution.py:27
  43.6 7.9 %collective-permute-start.16 = (bf16[128,256]{1,0:T(8,128)(2,1)S(1)}, bf16[128,256]{1,0:T(8,128)(2,1)S(1)}, u32[]{:S(2)}, u32[]{:S(2)}) collective-permute-start(bf16[128,256]{1,0:T(8,128)(2,1)S(1)} %pad_maximum_fusion.3.refs_0_.kv_ref), channel_id=1, source_target_pairs={{0,2},{1,3},{2,0},{3,1},{4,6},{5,7},{6,4},{7,5},{8,10},{9,11},{10,... | collective-permute-start | bytes 196616 | tf_op jit(solution)/shard_map/ppermute | solution.py:27

commit v19 on v15

--- a/solution.py
+++ b/solution.py
@@ -112,7 +112,7 @@
         there = there_ref[s, 0:rows, :]
         key = jnp.where(is_key, here, there)
         value = jnp.where(is_key, there, here)
-        score = dot(key, query, ((1,), (1,))) * inv_root
+        score = dot(key, query, ((1,), (1,)))
         dp_ref[slot] = dot(value, grad, ((1,), (1,)))
         meta = here_ref[s, rows : rows + META_ROWS, :].astype(jnp.float32)
         for run in range(rows // RUN):
@@ -128,7 +128,7 @@
 
     def weights(slot, state):
         total, mixed = state
-        weight = jnp.exp(s_ref[slot] - top)
+        weight = jnp.exp((s_ref[slot] - top) * inv_root)
         s_ref[slot] = weight
         total = total + jnp.sum(weight, axis=0, keepdims=True)
         mixed = mixed + jnp.sum(weight * dp_ref[slot], axis=0, keepdims=True)
@@ -227,49 +227,56 @@
     )(dq, w_near, w_other)
 
 
-def finish_kernel(core_ref, kv_ref, kv_far_ref, w_ref, acc_ref, far_ref, *refs):
-    out_ref, hold_ref, sems = refs[GIVES:]
-    rows, share = acc_ref.shape
-    pair = kv_ref.shape[1]
-    size = pair // 2
+def gather_kernel(acc_ref, far_ref, *refs):
+    given, out_ref = refs[:GIVES], refs[GIVES]
+    width = out_ref.shape[1] // GIVES
+    for i in range(GIVES):
+        at = slice(i * width, (i + 1) * width)
+        out_ref[:, at] = acc_ref[:, at] + far_ref[:, at].astype(jnp.float32) + given[i][...].astype(jnp.float32)
+
+
+def gathered(acc, far, given):
+    return pl.pallas_call(
+        gather_kernel,
+        out_shape=jax.ShapeDtypeStruct(acc.shape, acc.dtype),
+        in_specs=[pl.BlockSpec()] * (2 + GIVES),
+        out_specs=pl.BlockSpec(),
+        input_output_aliases={0: 0},
+        compiler_params=params(),
+        cost_estimate=pl.CostEstimate(flops=0, bytes_accessed=0, transcendentals=0),
+        name="gathered",
+    )(acc, far, *given)
+
+
+def finish_kernel(core_ref, kv_ref, kv_far_ref, w_ref, sum_ref, out_ref, hold_ref, sems):
+    rows, share = sum_ref.shape
+    size = kv_ref.shape[1] // 2
     tile = share // TILES
-    inv_root = 1.0 / math.sqrt(size)
-    column = lax.broadcasted_iota(jnp.int32, (1, pair), 1)
-    is_key = (column < size) == (core_ref[0] == 0)
     kv = kv_ref[...].astype(jnp.float32) + kv_far_ref[...].astype(jnp.float32)
-    kv = (kv * jnp.where(is_key, inv_root, 1.0)).astype(jnp.bfloat16)
-    at_mine = pl.ds(pl.multiple_of(core_ref[0] * size, size), size)
-    at_other = pl.ds(pl.multiple_of((1 - core_ref[0]) * size, size), size)
+    mine, other = kv[:, :size], kv[:, size:]
+    is_key = core_ref[0] == 0
+    key = jnp.where(is_key, mine, other) * (1.0 / math.sqrt(size))
+    kv = jnp.concatenate([key, jnp.where(is_key, other, mine)], axis=1).astype(jnp.bfloat16)
     copies = []
     for i in range(TILES):
         at = slice(i * tile, (i + 1) * tile)
-        w = jnp.concatenate([w_ref[at_mine, at], w_ref[at_other, at]], axis=0)
-        given_ref = refs[i * GIVES // TILES]
-        skip = i * GIVES // TILES * (share // GIVES)
-        given = given_ref[:, i * tile - skip : (i + 1) * tile - skip]
-        acc = acc_ref[:, at] + far_ref[:, at].astype(jnp.float32) + given.astype(jnp.float32)
-        acc = acc + dot(kv, w, ((1,), (0,)))
-        hold_ref[:, at] = acc.astype(jnp.bfloat16)
+        hold_ref[:, at] = (sum_ref[:, at] + dot(kv, w_ref[:, at], ((1,), (0,)))).astype(jnp.bfloat16)
         copies.append(pltpu.make_async_copy(hold_ref.at[:, at], out_ref.at[:, at], sems.at[i]))
         copies[i].start()
     for one in copies:
         one.wait()
 
 
-def finish(core, kv, kv_far, w_kv, acc, far, given):
-    rows, share = acc.shape
+def finish(core, kv, kv_far, w_kv, total):
     return pl.pallas_call(
         finish_kernel,
-        out_shape=jax.ShapeDtypeStruct((rows, share), jnp.bfloat16),
-        in_specs=[SMEM] + [pl.BlockSpec()] * (5 + GIVES),
+        out_shape=jax.ShapeDtypeStruct(total.shape, jnp.bfloat16),
+        in_specs=[SMEM] + [pl.BlockSpec()] * 4,
         out_specs=ANY,
-        scratch_shapes=[pltpu.VMEM((rows, share), jnp.bfloat16), pltpu.SemaphoreType.DMA((TILES,))],
+        scratch_shapes=[pltpu.VMEM(total.shape, jnp.bfloat16), pltpu.SemaphoreType.DMA((TILES,))],
         compiler_params=params(),
-        cost_estimate=pl.CostEstimate(
-            flops=2 * rows * kv.shape[1] * share, bytes_accessed=10 * rows * share, transcendentals=0
-        ),
         name="finish",
-    )(core, kv, kv_far, w_kv, acc, far, *given)
+    )(core, kv, kv_far, w_kv, total)
 
 
 def on_device(queries, keys, values, dout, positions, doc_ids, w_query, w_kv):
@@ -314,7 +321,7 @@
 
     acc, *give = own(dq, *carve([head, head ^ 1], w_query, share, kv))
     given = [swapped(one, "head", 1) for one in give]
-    return finish(core, kv, kv_far, w_kv, acc, far, given)
+    return finish(core, kv, kv_far, w_kv, gathered(acc, far, given))
 
 
 def solution(mesh):

time: 52.6 us -> 53.3 us (1.013)
  Pallas kernels: 8.12 us -> 9.2 us
  waiting for transfers between devices: 19.7 us -> 19 us
    pallas_call x1 -> x2, Pallas kernels: 1.43 us -> 2.43 us  [the longest x1 1.24 us: finish(): pl.pallas_call(finish_kernel, out_shape=jax.ShapeDtypeStruct(total.shape,...]
    ppermute x21, waiting for transfers between devices: 19.7 us -> 19 us  [swapped(): lax.ppermute(value, axis, [(source, source ^ bits) for source in range(co...]
  transfers between devices with their start and end apart: 21 -> 21, of which waited for: 8 -> 9; matrix products, arithmetic and copies ran while one was open for 9% -> 8% of each run, Pallas kernels for 11% -> 14%
where the time goes in v19:
time: 53.3 us; the launch traced here: 53.1 us
  starting transfers between devices  19.8 us (37%)
  waiting for transfers between devices  19 us (36%)
  Pallas kernels  9.2 us (17%)
  local copies, waits for them, and re-layouts  3.74 us (7%)
  other arithmetic  1.16 us (2%)
    ppermute x21, starting transfers between devices, swapped(): lax.ppermute(value, axis, [(source, source ^ bits) for source in range(co...  19.8 us
    ppermute x21, waiting for transfers between devices, swapped(): lax.ppermute(value, axis, [(source, source ^ bits) for source in range(co...  19 us
    pallas_call x1, Pallas kernels, carve(): pl.pallas_call(carve_kernel, out_shape=[block] * count, in_specs=[SMEM, H...  2.76 us
    dynamic_slice x1, local copies, waits for them, and re-layouts, column_block(): return lax.dynamic_slice_in_dim(w_query, block * share, share, axis=1)  2.58 us
    pallas_call x1, Pallas kernels, attention(): pl.pallas_call(attention_kernel, out_shape=[jax.ShapeDtypeStruct((rows, 2...  2.52 us
    pallas_call x1, Pallas kernels, finish(): pl.pallas_call(finish_kernel, out_shape=jax.ShapeDtypeStruct(total.shape,...  1.24 us
    pallas_call x1, Pallas kernels, gathered(): pl.pallas_call(gather_kernel, out_shape=jax.ShapeDtypeStruct(acc.shape, a...  1.2 us
  transfers between devices with their start and end apart: 21, of which 9 were waited for; matrix products, arithmetic and copies ran while one was open for 8% of the time, Pallas kernels for 14%

profile of v19, /device:TPU:0, one launch (start us, length us, event | category | flops | bytes accessed | tf_op | source)
XLA Modules:
  0.0 53.1 jit_solution(1113187905664866928)
XLA Ops:
  0.0 0.5 collective-permute-start
  0.5 0.7 %reshape.19 = s32[2,64]{1,0:T(2,128)S(1)} reshape(s32[128]{0:T(128)} %param.12) | data formatting | bytes 1024 | tf_op jit(solution)/shard_map/reshape | solution.py:44
  1.4 0.8 %broadcast_select_fusion = bf16[128,128]{1,0:T(8,128)(2,1)S(1)} fusion(bf16[128,128]{1,0:T(8,128)(2,1)} %param.9, bf16[128,128]{1,0:T(8,128)(2,1)} %param.10, pred[]{:T(512)} %bitcast.3), kind=kLoop, calls=%fused_computation.13 | loop fusion | flops 16384 | bytes 98305 | tf_op jit(solution)/shard_map/jit(_where)/select_n | solution.py:43
  2.3 3.1 %collective-permute-start.2 = (bf16[144,128]{1,0:T(8,128)(2,1)S(1)}, bf16[144,128]{1,0:T(8,128)(2,1)S(1)}, u32[]{:S(2)}, u32[]{:S(2)}) collective-permute-start(bf16[144,128]{1,0:T(8,128)(2,1)S(1)} %pad_maximum_fusion.3), channel_id=1, source_target_pairs={{0,8},{4,12},{8,0},{12,4},{16,24},{20,28},{24,16},{28,20},{1,9},{5... | collective-permute-start | bytes 110600 | tf_op jit(solution)/shard_map/ppermute | solution.py:26
  5.4 2.6 %collective-permute-start.3 = (bf16[144,128]{1,0:T(8,128)(2,1)S(1)}, bf16[144,128]{1,0:T(8,128)(2,1)S(1)}, u32[]{:S(2)}, u32[]{:S(2)}) collective-permute-start(bf16[144,128]{1,0:T(8,128)(2,1)S(1)} %pad_maximum_fusion.3), channel_id=1, source_target_pairs={{0,16},{4,20},{8,24},{12,28},{16,0},{20,4},{24,8},{28,12},{1,17},{... | collective-permute-start | bytes 110600 | tf_op jit(solution)/shard_map/ppermute | solution.py:26
  8.0 1.8 %collective-permute-start.5 = (bf16[2,144,128]{2,1,0:T(8,128)(2,1)S(1)}, bf16[2,144,128]{2,1,0:T(8,128)(2,1)S(1)}, u32[]{:S(2)}, u32[]{:S(2)}) collective-permute-start(bf16[2,144,128]{2,1,0:T(8,128)(2,1)S(1)} %pad_maximum_fusion.refs_0_), channel_id=1, source_target_pairs={{0,4},{4,0},{8,12},{12,8},{16,20},{20,16},{24,28},{28,24},{1,5},{5... | collective-permute-start | bytes 221192 | tf_op jit(solution)/shard_map/ppermute | solution.py:26
  9.8 2.6 %constant_dynamic-slice_fusion = (bf16[256,4096]{1,0:T(8,128)(2,1)S(1)}, bf16[256,4096]{1,0:T(8,128)(2,1)S(1)}) fusion(bf16[256,16384]{1,0:T(8,128)(2,1)} %w_ref.2, s32[]{:T(128)S(6)} %select_n.18, s32[]{:T(128)S(6)} %select_n.17), kind=kLoop, calls=%fused_computation.21 | loop fusion | bytes 8388616 | tf_op jit(solution)/shard_map/dynamic_slice | solution.py:51
  12.4 1.3 %collective-permute-done.4 = bf16[144,128]{1,0:T(8,128)(2,1)S(1)} collective-permute-done((bf16[144,128]{1,0:T(8,128)(2,1)S(1)}, bf16[144,128]{1,0:T(8,128)(2,1)S(1)}, u32[]{:S(2)}, u32[]{:S(2)}) %collective-permute-start.4) | collective-permute-done | bytes 36896 | tf_op jit(solution)/shard_map/ppermute | solution.py:26
  13.8 1.6 %collective-permute-start.9 = (bf16[2,144,128]{2,1,0:T(8,128)(2,1)S(1)}, bf16[2,144,128]{2,1,0:T(8,128)(2,1)S(1)}, u32[]{:S(2)}, u32[]{:S(2)}) collective-permute-start(bf16[2,144,128]{2,1,0:T(8,128)(2,1)S(1)} %pad_maximum_fusion.1.refs_2_), channel_id=1, source_target_pairs={{0,4},{4,0},{8,12},{12,8},{16,20},{20,16},{24,28},{28,24},{1,5},{5... | collective-permute-start | bytes 221192 | tf_op jit(solution)/shard_map/ppermute | solution.py:26
  15.5 0.3 collective-permute-start.8
  15.9 2.6 %collective-permute-done.9.refs_6_ = bf16[2,144,128]{2,1,0:T(8,128)(2,1)S(1)} collective-permute-done((bf16[2,144,128]{2,1,0:T(8,128)(2,1)S(1)}, bf16[2,144,128]{2,1,0:T(8,128)(2,1)S(1)}, u32[]{:S(2)}, u32[]{:S(2)}) %collective-permute-start.9) | collective-permute-done | bytes 73760 | tf_op jit(solution)/shard_map/ppermute | solution.py:26
  18.5 1.3 %collective-permute-done.10.refs_7_ = bf16[2,144,128]{2,1,0:T(8,128)(2,1)S(1)} collective-permute-done((bf16[2,144,128]{2,1,0:T(8,128)(2,1)S(1)}, bf16[2,144,128]{2,1,0:T(8,128)(2,1)S(1)}, u32[]{:S(2)}, u32[]{:S(2)}) %collective-permute-start.10) | collective-permute-done | bytes 73760 | tf_op jit(solution)/shard_map/ppermute | solution.py:26
  19.8 2.5 %attention.1 = (bf16[128,512]{1,0:T(8,128)(2,1)S(1)}, bf16[8,128,128]{2,1,0:T(8,128)(2,1)S(1)}) custom-call(s32[1]{0:T(128)} %bitcast.core_ref, s32[1,128]{1,0:T(1,128)S(1)} %bitcast.26, s32[1,128]{1,0:T(1,128)S(1)} %bitcast.27, bf16[128,256]{1,0:T(8,128)(2,1)S(1)} %copy-done.1, bf16[128,256]{1,0:T(8,128)(2,1)S(1)} %collective-permute-done.qo_ref, ...), custom_call_target="tpu_custom_call" | custom-call | flops 671088640 | bytes 1048576 | tf_op jit(solution)/shard_map/attention/pallas_call | solution.py:162
  22.3 0.7 %product.1 = bf16[128,4096]{1,0:T(8,128)(2,1)S(1)} custom-call(bf16[128,512]{1,0:T(8,128)(2,1)S(1)} %get-tuple-element.30.dq_ref, bf16[256,4096]{1,0:T(8,128)(2,1)S(1)} %get-tuple-element.31.wm_ref, bf16[256,4096]{1,0:T(8,128)(2,1)S(1)} %collective-permute-done.11.wo_ref), custom_call_target="tpu_custom_call" | custom-call | flops 536870912 | bytes 4194304 | tf_op jit(solution)/shard_map/product/pallas_call | solution.py:193
  23.1 1.6 %collective-permute-start.12 = (bf16[4,128,128]{2,1,0:T(8,128)(2,1)S(1)}, bf16[4,128,128]{2,1,0:T(8,128)(2,1)S(1)}, u32[]{:S(2)}, u32[]{:S(2)}) collective-permute-start(bf16[4,128,128]{2,1,0:T(8,128)(2,1)S(1)} %slice.26), channel_id=1, source_target_pairs={{0,4},{4,0},{8,12},{12,8},{16,20},{20,16},{24,28},{28,24},{1,5},{5... | collective-permute-start | bytes 393224 | tf_op jit(solution)/shard_map/ppermute | solution.py:26
  24.7 1.5 %collective-permute-start.18 = (bf16[128,4096]{1,0:T(8,128)(2,1)S(1)}, bf16[128,4096]{1,0:T(8,128)(2,1)S(1)}, u32[]{:S(2)}, u32[]{:S(2)}) collective-permute-start(bf16[128,4096]{1,0:T(8,128)(2,1)S(1)} %product.1), channel_id=1, source_target_pairs={{0,2},{1,3},{2,0},{3,1},{4,6},{5,7},{6,4},{7,5},{8,10},{9,11},{10,... | collective-permute-start | bytes 3145736 | tf_op jit(solution)/shard_map/ppermute | solution.py:26
  26.2 2.6 %collective-permute-done.12 = bf16[4,128,128]{2,1,0:T(8,128)(2,1)S(1)} collective-permute-done((bf16[4,128,128]{2,1,0:T(8,128)(2,1)S(1)}, bf16[4,128,128]{2,1,0:T(8,128)(2,1)S(1)}, u32[]{:S(2)}, u32[]{:S(2)}) %collective-permute-start.12) | collective-permute-done | bytes 131104 | tf_op jit(solution)/shard_map/ppermute | solution.py:26
  28.9 3.0 %collective-permute-start.14 = (bf16[128,128]{1,0:T(8,128)(2,1)S(1)}, bf16[128,128]{1,0:T(8,128)(2,1)S(1)}, u32[]{:S(2)}, u32[]{:S(2)}) collective-permute-start(bf16[128,128]{1,0:T(8,128)(2,1)S(1)} %get-tuple-element.45), channel_id=1, source_target_pairs={{0,16},{4,20},{8,24},{12,28},{16,0},{20,4},{24,8},{28,12},{1,17},{... | collective-permute-start | bytes 98312 | tf_op jit(solution)/shard_map/ppermute | solution.py:26
  31.9 1.4 %collective-permute-start.15 = (bf16[128,128]{1,0:T(8,128)(2,1)S(1)}, bf16[128,128]{1,0:T(8,128)(2,1)S(1)}, u32[]{:S(2)}, u32[]{:S(2)}) collective-permute-start(bf16[128,128]{1,0:T(8,128)(2,1)S(1)} %get-tuple-element.44), channel_id=1, source_target_pairs={{0,24},{4,28},{8,16},{12,20},{16,8},{20,12},{24,0},{28,4},{1,25},{... | collective-permute-start | bytes 98312 | tf_op jit(solution)/shard_map/ppermute | solution.py:26
  33.2 0.7 %collective-permute-done.14 = bf16[128,128]{1,0:T(8,128)(2,1)S(1)} collective-permute-done((bf16[128,128]{1,0:T(8,128)(2,1)S(1)}, bf16[128,128]{1,0:T(8,128)(2,1)S(1)}, u32[]{:S(2)}, u32[]{:S(2)}) %collective-permute-start.14) | collective-permute-done | bytes 32800 | tf_op jit(solution)/shard_map/ppermute | solution.py:26
  34.0 3.6 %collective-permute-done.15 = bf16[128,128]{1,0:T(8,128)(2,1)S(1)} collective-permute-done((bf16[128,128]{1,0:T(8,128)(2,1)S(1)}, bf16[128,128]{1,0:T(8,128)(2,1)S(1)}, u32[]{:S(2)}, u32[]{:S(2)}) %collective-permute-start.15) | collective-permute-done | bytes 32800 | tf_op jit(solution)/shard_map/ppermute | solution.py:26
  37.8 1.1 %collective-permute-done.16 = bf16[128,128]{1,0:T(8,128)(2,1)S(1)} collective-permute-done((bf16[128,128]{1,0:T(8,128)(2,1)S(1)}, bf16[128,128]{1,0:T(8,128)(2,1)S(1)}, u32[]{:S(2)}, u32[]{:S(2)}) %collective-permute-start.16) | collective-permute-done | bytes 32800 | tf_op jit(solution)/shard_map/ppermute | solution.py:26
  38.9 2.8 %carve.1 = (bf16[256,4096]{1,0:T(8,128)(2,1)S(1)}, bf16[256,4096]{1,0:T(8,128)(2,1)S(1)}) custom-call(s32[2]{0:T(128)S(1)} %pad_add_fusion.block_ref, bf16[256,16384]{1,0:T(8,128)(2,1)} %w_ref.2, bf16[128,256]{1,0:T(8,128)(2,1)S(1)} %pad_maximum_fusion.2.refs_0_.kv_ref), custom_call_target="tpu_custom_call" | custom-call | tf_op jit(solution)/shard_map/carve/pallas_call | solution.py:73
  41.7 0.8 %own.1 = (f32[128,4096]{1,0:T(8,128)S(1)}, bf16[128,2048]{1,0:T(8,128)(2,1)S(1)}, bf16[128,2048]{1,0:T(8,128)(2,1)S(1)}) custom-call(bf16[128,512]{1,0:T(8,128)(2,1)S(1)} %get-tuple-element.30.dq_ref, bf16[256,4096]{1,0:T(8,128)(2,1)S(1)} %get-tuple-element.34.wn_ref, bf16[256,4096]{1,0:T(8,128)(2,1)S(1)} %get-tuple-element.35.wo_ref), custom_call_target="tpu_custom_call" | custom-call | tf_op jit(solution)/shard_map/own/pallas_call | solution.py:218
  42.4 0.2 collective-permute-start.19
  42.6 0.4 collective-permute-start.20
  43.0 1.5 %collective-permute-start.17 = (bf16[128,256]{1,0:T(8,128)(2,1)S(1)}, bf16[128,256]{1,0:T(8,128)(2,1)S(1)}, u32[]{:S(2)}, u32[]{:S(2)}) collective-permute-start(bf16[128,256]{1,0:T(8,128)(2,1)S(1)} %pad_maximum_fusion.2.refs_0_.kv_ref), channel_id=1, source_target_pairs={{0,2},{1,3},{2,0},{3,1},{4,6},{5,7},{6,4},{7,5},{8,10},{9,11},{10,... | collective-permute-start | bytes 196616 | tf_op jit(solution)/shard_map/ppermute | solution.py:26
  44.5 0.6 %collective-permute-done.20.refs_1_ = bf16[128,2048]{1,0:T(8,128)(2,1)S(1)} collective-permute-done((bf16[128,2048]{1,0:T(8,128)(2,1)S(1)}, bf16[128,2048]{1,0:T(8,128)(2,1)S(1)}, u32[]{:S(2)}, u32[]{:S(2)}) %collective-permute-start.20) | collective-permute-done | bytes 524320 | tf_op jit(solution)/shard_map/ppermute | solution.py:26
  45.1 5.1 %collective-permute-done.18.far_ref = bf16[128,4096]{1,0:T(8,128)(2,1)S(1)} collective-permute-done((bf16[128,4096]{1,0:T(8,128)(2,1)S(1)}, bf16[128,4096]{1,0:T(8,128)(2,1)S(1)}, u32[]{:S(2)}, u32[]{:S(2)}) %collective-permute-start.18) | collective-permute-done | bytes 1048608 | tf_op jit(solution)/shard_map/ppermute | solution.py:26
  50.3 1.2 %gathered.1.sum_ref = f32[128,4096]{1,0:T(8,128)S(1)} custom-call(f32[128,4096]{1,0:T(8,128)S(1)} %get-tuple-element.36.acc_ref, bf16[128,4096]{1,0:T(8,128)(2,1)S(1)} %collective-permute-done.18.far_ref, bf16[128,2048]{1,0:T(8,128)(2,1)S(1)} %collective-permute-done.19.refs_0_, ...), custom_call_target="tpu_custom_call", output_to_operand_aliasing={{}: (0, {})} | custom-call | tf_op jit(solution)/shard_map/gathered/pallas_call | solution.py:239
  51.5 0.4 copy-done
  51.9 1.2 %finish.1 = bf16[128,4096]{1,0:T(8,128)(2,1)} custom-call(s32[1]{0:T(128)} %bitcast.core_ref, bf16[128,256]{1,0:T(8,128)(2,1)S(1)} %pad_maximum_fusion.2.refs_0_.kv_ref, bf16[128,256]{1,0:T(8,128)(2,1)S(1)} %collective-permute-done.17.kv_far_ref, bf16[256,4096]{1,0:T(8,128)(2,1)S(1)} %copy-done, f32[128,4096]{1,0:T(8,128)S(1)} %gathered.1.sum_ref), custom_call_target="tpu_custom_call" | custom-call | tf_op jit(solution)/shard_map/finish/pallas_call | solution.py:271
  (40 shorter events, 0.9 us)
Async XLA Ops:
  0.0 2.2 %collective-permute-start = (bf16[128,256]{1,0:T(8,128)(2,1)}, bf16[128,256]{1,0:T(8,128)(2,1)S(1)}, u32[]{:S(2)}, u32[]{:S(2)}) collective-permute-start(bf16[128,256]{1,0:T(8,128)(2,1)} %qm_ref.1), channel_id=1, source_target_pairs={{0,1},{1,0},{2,3},{3,2},{4,5},{5,4},{6,7},{7,6},{8,9},{9,8},{10,11... | collective-permute-start | bytes 196616 | tf_op jit(solution)/shard_map/ppermute | solution.py:26
  0.5 1.8 %collective-permute-start.1 = (bf16[128,256]{1,0:T(8,128)(2,1)}, bf16[128,256]{1,0:T(8,128)(2,1)S(1)}, u32[]{:S(2)}, u32[]{:S(2)}) collective-permute-start(bf16[128,256]{1,0:T(8,128)(2,1)} %gm_ref.1), channel_id=1, source_target_pairs={{0,1},{1,0},{2,3},{3,2},{4,5},{5,4},{6,7},{7,6},{8,9},{9,8},{10,11... | collective-permute-start | bytes 196616 | tf_op jit(solution)/shard_map/ppermute | solution.py:26
  2.3 5.7 %collective-permute-start.2 = (bf16[144,128]{1,0:T(8,128)(2,1)S(1)}, bf16[144,128]{1,0:T(8,128)(2,1)S(1)}, u32[]{:S(2)}, u32[]{:S(2)}) collective-permute-start(bf16[144,128]{1,0:T(8,128)(2,1)S(1)} %pad_maximum_fusion.3), channel_id=1, source_target_pairs={{0,8},{4,12},{8,0},{12,4},{16,24},{20,28},{24,16},{28,20},{1,9},{5... | collective-permute-start | bytes 110600 | tf_op jit(solution)/shard_map/ppermute | solution.py:26
  5.4 7.0 %collective-permute-start.3 = (bf16[144,128]{1,0:T(8,128)(2,1)S(1)}, bf16[144,128]{1,0:T(8,128)(2,1)S(1)}, u32[]{:S(2)}, u32[]{:S(2)}) collective-permute-start(bf16[144,128]{1,0:T(8,128)(2,1)S(1)} %pad_maximum_fusion.3), channel_id=1, source_target_pairs={{0,16},{4,20},{8,24},{12,28},{16,0},{20,4},{24,8},{28,12},{1,17},{... | collective-permute-start | bytes 110600 | tf_op jit(solution)/shard_map/ppermute | solution.py:26
  7.9 5.8 %collective-permute-start.4 = (bf16[144,128]{1,0:T(8,128)(2,1)S(1)}, bf16[144,128]{1,0:T(8,128)(2,1)S(1)}, u32[]{:S(2)}, u32[]{:S(2)}) collective-permute-start(bf16[144,128]{1,0:T(8,128)(2,1)S(1)} %pad_maximum_fusion.3), channel_id=1, source_target_pairs={{0,24},{4,28},{8,16},{12,20},{16,8},{20,12},{24,0},{28,4},{1,25},{... | collective-permute-start | bytes 110600 | tf_op jit(solution)/shard_map/ppermute | solution.py:26
  8.0 11.8 %copy-start.1 = (bf16[128,256]{1,0:T(8,128)(2,1)S(1)}, bf16[128,256]{1,0:T(8,128)(2,1)}, u32[]{:S(2)}) copy-start(bf16[128,256]{1,0:T(8,128)(2,1)} %qm_ref.1) | copy-start | bytes 196612
  8.0 11.8 %copy-start.2 = (bf16[128,256]{1,0:T(8,128)(2,1)S(1)}, bf16[128,256]{1,0:T(8,128)(2,1)}, u32[]{:S(2)}) copy-start(bf16[128,256]{1,0:T(8,128)(2,1)} %gm_ref.1) | copy-start | bytes 196612
  8.0 11.8 %copy-start.3 = (s32[128]{0:T(128)S(1)}, s32[128]{0:T(128)}, u32[]{:S(2)}) copy-start(s32[128]{0:T(128)} %param.12) | copy-start | bytes 1540
  8.0 11.8 %copy-start.4 = (s32[128]{0:T(128)S(1)}, s32[128]{0:T(128)}, u32[]{:S(2)}) copy-start(s32[128]{0:T(128)} %param.13) | copy-start | bytes 1540
  8.0 5.7 %collective-permute-start.5 = (bf16[2,144,128]{2,1,0:T(8,128)(2,1)S(1)}, bf16[2,144,128]{2,1,0:T(8,128)(2,1)S(1)}, u32[]{:S(2)}, u32[]{:S(2)}) collective-permute-start(bf16[2,144,128]{2,1,0:T(8,128)(2,1)S(1)} %pad_maximum_fusion.refs_0_), channel_id=1, source_target_pairs={{0,4},{4,0},{8,12},{12,8},{16,20},{20,16},{24,28},{28,24},{1,5},{5... | collective-permute-start | bytes 221192 | tf_op jit(solution)/shard_map/ppermute | solution.py:26
  9.8 3.9 %collective-permute-start.6 = (bf16[2,144,128]{2,1,0:T(8,128)(2,1)S(1)}, bf16[2,144,128]{2,1,0:T(8,128)(2,1)S(1)}, u32[]{:S(2)}, u32[]{:S(2)}) collective-permute-start(bf16[2,144,128]{2,1,0:T(8,128)(2,1)S(1)} %pad_maximum_fusion.refs_0_), channel_id=1, source_target_pairs={{0,1},{1,0},{2,3},{3,2},{4,5},{5,4},{6,7},{7,6},{8,9},{9,8},{10,11... | collective-permute-start | bytes 221192 | tf_op jit(solution)/shard_map/ppermute | solution.py:26
  13.7 8.6 %collective-permute-start.11 = (bf16[256,4096]{1,0:T(8,128)(2,1)S(1)}, bf16[256,4096]{1,0:T(8,128)(2,1)S(1)}, u32[]{:S(2)}, u32[]{:S(2)}) collective-permute-start(bf16[256,4096]{1,0:T(8,128)(2,1)S(1)} %get-tuple-element.32), channel_id=1, source_target_pairs={{0,1},{1,0},{2,3},{3,2},{4,5},{5,4},{6,7},{7,6},{8,9},{9,8},{10,11... | collective-permute-start | bytes 6291464 | tf_op jit(solution)/shard_map/ppermute | solution.py:26
  13.8 4.7 %collective-permute-start.9 = (bf16[2,144,128]{2,1,0:T(8,128)(2,1)S(1)}, bf16[2,144,128]{2,1,0:T(8,128)(2,1)S(1)}, u32[]{:S(2)}, u32[]{:S(2)}) collective-permute-start(bf16[2,144,128]{2,1,0:T(8,128)(2,1)S(1)} %pad_maximum_fusion.1.refs_2_), channel_id=1, source_target_pairs={{0,4},{4,0},{8,12},{12,8},{16,20},{20,16},{24,28},{28,24},{1,5},{5... | collective-permute-start | bytes 221192 | tf_op jit(solution)/shard_map/ppermute | solution.py:26
  15.4 3.1 %collective-permute-start.7 = (bf16[2,144,128]{2,1,0:T(8,128)(2,1)S(1)}, bf16[2,144,128]{2,1,0:T(8,128)(2,1)S(1)}, u32[]{:S(2)}, u32[]{:S(2)}) collective-permute-start(bf16[2,144,128]{2,1,0:T(8,128)(2,1)S(1)} %pad_maximum_fusion.1.refs_2_), channel_id=1, source_target_pairs={{0,1},{1,0},{2,3},{3,2},{4,5},{5,4},{6,7},{7,6},{8,9},{9,8},{10,11... | collective-permute-start | bytes 221192 | tf_op jit(solution)/shard_map/ppermute | solution.py:26
  15.5 3.0 %collective-permute-start.8 = (bf16[2,144,128]{2,1,0:T(8,128)(2,1)S(1)}, bf16[2,144,128]{2,1,0:T(8,128)(2,1)S(1)}, u32[]{:S(2)}, u32[]{:S(2)}) collective-permute-start(bf16[2,144,128]{2,1,0:T(8,128)(2,1)S(1)} %collective-permute-done.5.refs_4_), channel_id=1, source_target_pairs={{0,1},{1,0},{2,3},{3,2},{4,5},{5,4},{6,7},{7,6},{8,9},{9,8},{10,11... | collective-permute-start | bytes 221192 | tf_op jit(solution)/shard_map/ppermute | solution.py:26
  18.5 1.3 %collective-permute-start.10 = (bf16[2,144,128]{2,1,0:T(8,128)(2,1)S(1)}, bf16[2,144,128]{2,1,0:T(8,128)(2,1)S(1)}, u32[]{:S(2)}, u32[]{:S(2)}) collective-permute-start(bf16[2,144,128]{2,1,0:T(8,128)(2,1)S(1)} %collective-permute-done.9.refs_6_), channel_id=1, source_target_pairs={{0,1},{1,0},{2,3},{3,2},{4,5},{5,4},{6,7},{7,6},{8,9},{9,8},{10,11... | collective-permute-start | bytes 221192 | tf_op jit(solution)/shard_map/ppermute | solution.py:26
  23.1 5.6 %collective-permute-start.12 = (bf16[4,128,128]{2,1,0:T(8,128)(2,1)S(1)}, bf16[4,128,128]{2,1,0:T(8,128)(2,1)S(1)}, u32[]{:S(2)}, u32[]{:S(2)}) collective-permute-start(bf16[4,128,128]{2,1,0:T(8,128)(2,1)S(1)} %slice.26), channel_id=1, source_target_pairs={{0,4},{4,0},{8,12},{12,8},{16,20},{20,16},{24,28},{28,24},{1,5},{5... | collective-permute-start | bytes 393224 | tf_op jit(solution)/shard_map/ppermute | solution.py:26
  24.7 25.6 %collective-permute-start.18 = (bf16[128,4096]{1,0:T(8,128)(2,1)S(1)}, bf16[128,4096]{1,0:T(8,128)(2,1)S(1)}, u32[]{:S(2)}, u32[]{:S(2)}) collective-permute-start(bf16[128,4096]{1,0:T(8,128)(2,1)S(1)} %product.1), channel_id=1, source_target_pairs={{0,2},{1,3},{2,0},{3,1},{4,6},{5,7},{6,4},{7,5},{8,10},{9,11},{10,... | collective-permute-start | bytes 3145736 | tf_op jit(solution)/shard_map/ppermute | solution.py:26
  28.8 4.5 %collective-permute-start.13 = (bf16[128,128]{1,0:T(8,128)(2,1)S(1)}, bf16[128,128]{1,0:T(8,128)(2,1)S(1)}, u32[]{:S(2)}, u32[]{:S(2)}) collective-permute-start(bf16[128,128]{1,0:T(8,128)(2,1)S(1)} %get-tuple-element.43), channel_id=1, source_target_pairs={{0,8},{4,12},{8,0},{12,4},{16,24},{20,28},{24,16},{28,20},{1,9},{5... | collective-permute-start | bytes 98312 | tf_op jit(solution)/shard_map/ppermute | solution.py:26
  28.9 5.1 %collective-permute-start.14 = (bf16[128,128]{1,0:T(8,128)(2,1)S(1)}, bf16[128,128]{1,0:T(8,128)(2,1)S(1)}, u32[]{:S(2)}, u32[]{:S(2)}) collective-permute-start(bf16[128,128]{1,0:T(8,128)(2,1)S(1)} %get-tuple-element.45), channel_id=1, source_target_pairs={{0,16},{4,20},{8,24},{12,28},{16,0},{20,4},{24,8},{28,12},{1,17},{... | collective-permute-start | bytes 98312 | tf_op jit(solution)/shard_map/ppermute | solution.py:26
  31.9 5.7 %collective-permute-start.15 = (bf16[128,128]{1,0:T(8,128)(2,1)S(1)}, bf16[128,128]{1,0:T(8,128)(2,1)S(1)}, u32[]{:S(2)}, u32[]{:S(2)}) collective-permute-start(bf16[128,128]{1,0:T(8,128)(2,1)S(1)} %get-tuple-element.44), channel_id=1, source_target_pairs={{0,24},{4,28},{8,16},{12,20},{16,8},{20,12},{24,0},{28,4},{1,25},{... | collective-permute-start | bytes 98312 | tf_op jit(solution)/shard_map/ppermute | solution.py:26
  37.6 1.3 %collective-permute-start.16 = (bf16[128,128]{1,0:T(8,128)(2,1)S(1)}, bf16[128,128]{1,0:T(8,128)(2,1)S(1)}, u32[]{:S(2)}, u32[]{:S(2)}) collective-permute-start(bf16[128,128]{1,0:T(8,128)(2,1)S(1)} %fusion.3), channel_id=1, source_target_pairs={{0,1},{1,0},{2,3},{3,2},{4,5},{5,4},{6,7},{7,6},{8,9},{9,8},{10,11... | collective-permute-start | bytes 98312 | tf_op jit(solution)/shard_map/ppermute | solution.py:26
  42.4 2.1 %collective-permute-start.19 = (bf16[128,2048]{1,0:T(8,128)(2,1)S(1)}, bf16[128,2048]{1,0:T(8,128)(2,1)S(1)}, u32[]{:S(2)}, u32[]{:S(2)}) collective-permute-start(bf16[128,2048]{1,0:T(8,128)(2,1)S(1)} %get-tuple-element.37), channel_id=1, source_target_pairs={{0,1},{1,0},{2,3},{3,2},{4,5},{5,4},{6,7},{7,6},{8,9},{9,8},{10,11... | collective-permute-start | bytes 1572872 | tf_op jit(solution)/shard_map/ppermute | solution.py:26
  42.6 2.5 %collective-permute-start.20 = (bf16[128,2048]{1,0:T(8,128)(2,1)S(1)}, bf16[128,2048]{1,0:T(8,128)(2,1)S(1)}, u32[]{:S(2)}, u32[]{:S(2)}) collective-permute-start(bf16[128,2048]{1,0:T(8,128)(2,1)S(1)} %get-tuple-element.38), channel_id=1, source_target_pairs={{0,1},{1,0},{2,3},{3,2},{4,5},{5,4},{6,7},{7,6},{8,9},{9,8},{10,11... | collective-permute-start | bytes 1572872 | tf_op jit(solution)/shard_map/ppermute | solution.py:26
  43.0 8.5 %collective-permute-start.17 = (bf16[128,256]{1,0:T(8,128)(2,1)S(1)}, bf16[128,256]{1,0:T(8,128)(2,1)S(1)}, u32[]{:S(2)}, u32[]{:S(2)}) collective-permute-start(bf16[128,256]{1,0:T(8,128)(2,1)S(1)} %pad_maximum_fusion.2.refs_0_.kv_ref), channel_id=1, source_target_pairs={{0,2},{1,3},{2,0},{3,1},{4,6},{5,7},{6,4},{7,5},{8,10},{9,11},{10,... | collective-permute-start | bytes 196616 | tf_op jit(solution)/shard_map/ppermute | solution.py:26
  50.3 1.6 %copy-start = (bf16[256,4096]{1,0:T(8,128)(2,1)S(1)}, bf16[256,4096]{1,0:T(8,128)(2,1)}, u32[]{:S(2)}) copy-start(bf16[256,4096]{1,0:T(8,128)(2,1)} %w_ref.3) | copy-start | bytes 6291460

commit v20 on v17

--- a/solution.py
+++ b/solution.py
@@ -233,22 +233,19 @@
     pair = kv_ref.shape[1]
     size = pair // 2
     tile = share // TILES
-    inv_root = 1.0 / math.sqrt(size)
-    column = lax.broadcasted_iota(jnp.int32, (1, pair), 1)
-    is_key = (column < size) == (core_ref[0] == 0)
     kv = kv_ref[...].astype(jnp.float32) + kv_far_ref[...].astype(jnp.float32)
-    kv = (kv * jnp.where(is_key, inv_root, 1.0)).astype(jnp.bfloat16)
-    at_mine = pl.ds(pl.multiple_of(core_ref[0] * size, size), size)
-    at_other = pl.ds(pl.multiple_of((1 - core_ref[0]) * size, size), size)
+    mine, other = kv[:, :size], kv[:, size:]
+    is_key = core_ref[0] == 0
+    key = jnp.where(is_key, mine, other) * (1.0 / math.sqrt(size))
+    kv = jnp.concatenate([key, jnp.where(is_key, other, mine)], axis=1).astype(jnp.bfloat16)
     copies = []
     for i in range(TILES):
         at = slice(i * tile, (i + 1) * tile)
-        w = jnp.concatenate([w_ref[at_mine, at], w_ref[at_other, at]], axis=0)
         given_ref = refs[i * GIVES // TILES]
         skip = i * GIVES // TILES * (share // GIVES)
         given = given_ref[:, i * tile - skip : (i + 1) * tile - skip]
         acc = acc_ref[:, at] + far_ref[:, at].astype(jnp.float32) + given.astype(jnp.float32)
-        acc = acc + dot(kv, w, ((1,), (0,)))
+        acc = acc + dot(kv, w_ref[:, at], ((1,), (0,)))
         hold_ref[:, at] = acc.astype(jnp.bfloat16)
         copies.append(pltpu.make_async_copy(hold_ref.at[:, at], out_ref.at[:, at], sems.at[i]))
         copies[i].start()
@@ -279,10 +276,7 @@
     share = w_kv.shape[1]
     local_heads = queries.shape[1] // keys.shape[1]
 
-    q_other = swapped(queries, "head", 1)
-    g_other = swapped(dout, "head", 1)
     piece = pack(core, positions, keys, values)
-    piece, q_other, g_other = lax.optimization_barrier((piece, q_other, g_other))
     along_z = [piece] + [swapped(piece, "ctx", 2 * s) for s in range(1, half)]
     early = (half + 1) // 2
     z_early, z_late = jnp.stack(along_z[:early]), jnp.stack(along_z[early:])
@@ -294,6 +288,9 @@
     far_other = swapped(far_send, "head", 1)
     here_z = jnp.concatenate([z_early, z_late])
     there_z = swapped(here_z, "head", 1)
+    queries, dout, here_z = lax.optimization_barrier((queries, dout, here_z))
+    q_other, g_other = swapped(queries, "head", 1), swapped(dout, "head", 1)
+    x_late, q_other, g_other = lax.optimization_barrier((x_late, q_other, g_other))
     here_x = jnp.concatenate([x_early, x_late])
     pieces = (here_z, there_z, here_x, swapped(here_x, "head", 1))
     dq, back = attention(core, positions, doc_ids, queries, q_other, dout, g_other, pieces)

time: 52.7 us -> 52.2 us (level)
  transfers between devices with their start and end apart: 19 -> 19, of which waited for: 8 -> 10; matrix products, arithmetic and copies ran while one was open for 9% -> 5% of each run, Pallas kernels for 11% -> 11%
where the time goes in v20:
time: 52.2 us; the launch traced here: 52 us
  starting transfers between devices  19.6 us (38%)
  waiting for transfers between devices  19.5 us (37%)
  Pallas kernels  8.08 us (15%)
  local copies, waits for them, and re-layouts  3.4 us (7%)
  other arithmetic  1.18 us (2%)
    ppermute x19, starting transfers between devices, swapped(): lax.ppermute(value, axis, [(source, source ^ bits) for source in range(co...  19.6 us
    ppermute x19, waiting for transfers between devices, swapped(): lax.ppermute(value, axis, [(source, source ^ bits) for source in range(co...  19.5 us
    pallas_call x1, Pallas kernels, carve(): pl.pallas_call(carve_kernel, out_shape=[block] * count, in_specs=[SMEM, H...  2.76 us
    dynamic_slice x1, local copies, waits for them, and re-layouts, column_block(): return lax.dynamic_slice_in_dim(w_query, block * share, share, axis=1)  2.59 us
    pallas_call x1, Pallas kernels, attention(): pl.pallas_call(attention_kernel, out_shape=[jax.ShapeDtypeStruct((rows, 2...  2.41 us
    pallas_call x1, Pallas kernels, finish(): pl.pallas_call(finish_kernel, out_shape=jax.ShapeDtypeStruct((rows, share...  1.43 us
  transfers between devices with their start and end apart: 19, of which 10 were waited for; matrix products, arithmetic and copies ran while one was open for 5% of the time, Pallas kernels for 11%

profile of v20, /device:TPU:0, one launch (start us, length us, event | category | flops | bytes accessed | tf_op | source)
XLA Modules:
  0.0 52.0 jit_solution(16639728592818849694)
XLA Ops:
  0.0 0.7 %reshape.19 = s32[2,64]{1,0:T(2,128)S(1)} reshape(s32[128]{0:T(128)} %param.12) | data formatting | bytes 1024 | tf_op jit(solution)/shard_map/reshape | solution.py:44
  0.7 0.1 fusion.5
  0.9 0.8 %broadcast_select_fusion = bf16[128,128]{1,0:T(8,128)(2,1)S(1)} fusion(bf16[128,128]{1,0:T(8,128)(2,1)} %param.9, bf16[128,128]{1,0:T(8,128)(2,1)} %param.10, pred[]{:T(512)} %bitcast.3), kind=kLoop, calls=%fused_computation.14 | loop fusion | flops 16384 | bytes 98305 | tf_op jit(solution)/shard_map/jit(_where)/select_n | solution.py:43
  1.7 3.1 %collective-permute-start = (bf16[144,128]{1,0:T(8,128)(2,1)S(1)}, bf16[144,128]{1,0:T(8,128)(2,1)S(1)}, u32[]{:S(2)}, u32[]{:S(2)}) collective-permute-start(bf16[144,128]{1,0:T(8,128)(2,1)S(1)} %get-tuple-element.51), channel_id=1, source_target_pairs={{0,8},{4,12},{8,0},{12,4},{16,24},{20,28},{24,16},{28,20},{1,9},{5... | collective-permute-start | bytes 110600 | tf_op jit(solution)/shard_map/ppermute | solution.py:26
  4.8 2.6 %collective-permute-start.1 = (bf16[144,128]{1,0:T(8,128)(2,1)S(1)}, bf16[144,128]{1,0:T(8,128)(2,1)S(1)}, u32[]{:S(2)}, u32[]{:S(2)}) collective-permute-start(bf16[144,128]{1,0:T(8,128)(2,1)S(1)} %get-tuple-element.51), channel_id=1, source_target_pairs={{0,16},{4,20},{8,24},{12,28},{16,0},{20,4},{24,8},{28,12},{1,17},{... | collective-permute-start | bytes 110600 | tf_op jit(solution)/shard_map/ppermute | solution.py:26
  7.5 1.8 %collective-permute-start.3 = (bf16[2,144,128]{2,1,0:T(8,128)(2,1)S(1)}, bf16[2,144,128]{2,1,0:T(8,128)(2,1)S(1)}, u32[]{:S(2)}, u32[]{:S(2)}) collective-permute-start(bf16[2,144,128]{2,1,0:T(8,128)(2,1)S(1)} %pad_maximum_fusion.2), channel_id=1, source_target_pairs={{0,4},{4,0},{8,12},{12,8},{16,20},{20,16},{24,28},{28,24},{1,5},{5... | collective-permute-start | bytes 221192 | tf_op jit(solution)/shard_map/ppermute | solution.py:26
  9.3 2.6 %constant_dynamic-slice_fusion = (bf16[256,4096]{1,0:T(8,128)(2,1)S(1)}, bf16[256,4096]{1,0:T(8,128)(2,1)S(1)}) fusion(bf16[256,16384]{1,0:T(8,128)(2,1)} %w_ref.2, s32[]{:T(128)S(6)} %select_n.18, s32[]{:T(128)S(6)} %select_n.17), kind=kLoop, calls=%fused_computation.24 | loop fusion | bytes 8388616 | tf_op jit(solution)/shard_map/dynamic_slice | solution.py:51
  11.9 1.3 %collective-permute-done.2 = bf16[144,128]{1,0:T(8,128)(2,1)S(1)} collective-permute-done((bf16[144,128]{1,0:T(8,128)(2,1)S(1)}, bf16[144,128]{1,0:T(8,128)(2,1)S(1)}, u32[]{:S(2)}, u32[]{:S(2)}) %collective-permute-start.2) | collective-permute-done | bytes 36896 | tf_op jit(solution)/shard_map/ppermute | solution.py:26
  13.3 1.6 %collective-permute-start.4 = (bf16[2,144,128]{2,1,0:T(8,128)(2,1)S(1)}, bf16[2,144,128]{2,1,0:T(8,128)(2,1)S(1)}, u32[]{:S(2)}, u32[]{:S(2)}) collective-permute-start(bf16[2,144,128]{2,1,0:T(8,128)(2,1)S(1)} %pad_maximum_fusion.1), channel_id=1, source_target_pairs={{0,4},{4,0},{8,12},{12,8},{16,20},{20,16},{24,28},{28,24},{1,5},{5... | collective-permute-start | bytes 221192 | tf_op jit(solution)/shard_map/ppermute | solution.py:26
  14.9 0.2 collective-permute-start.7
  15.1 0.3 collective-permute-start.5
  15.4 0.2 collective-permute-start.6
  15.6 2.1 %collective-permute-done.5.qo_ref = bf16[128,256]{1,0:T(8,128)(2,1)S(1)} collective-permute-done((bf16[128,256]{1,0:T(8,128)(2,1)S(1)}, bf16[128,256]{1,0:T(8,128)(2,1)S(1)}, u32[]{:S(2)}, u32[]{:S(2)}) %collective-permute-start.5) | collective-permute-done | bytes 65568 | tf_op jit(solution)/shard_map/ppermute | solution.py:26
  17.8 0.1 collective-permute-done.4
  18.1 1.3 %collective-permute-done.8.refs_3_ = bf16[4,144,128]{2,1,0:T(8,128)(2,1)S(1)} collective-permute-done((bf16[4,144,128]{2,1,0:T(8,128)(2,1)S(1)}, bf16[4,144,128]{2,1,0:T(8,128)(2,1)S(1)}, u32[]{:S(2)}, u32[]{:S(2)}) %collective-permute-start.8) | collective-permute-done | bytes 147488 | tf_op jit(solution)/shard_map/ppermute | solution.py:26
  19.4 2.4 %attention.1 = (bf16[128,512]{1,0:T(8,128)(2,1)S(1)}, bf16[8,128,128]{2,1,0:T(8,128)(2,1)S(1)}) custom-call(s32[1]{0:T(128)} %bitcast.core_ref, s32[1,128]{1,0:T(1,128)S(1)} %bitcast.27, s32[1,128]{1,0:T(1,128)S(1)} %bitcast.28, bf16[128,256]{1,0:T(8,128)(2,1)S(1)} %copy-done.1, bf16[128,256]{1,0:T(8,128)(2,1)S(1)} %collective-permute-done.5.qo_ref, ...), custom_call_target="tpu_custom_call" | custom-call | flops 671088640 | bytes 1048576 | tf_op jit(solution)/shard_map/attention/pallas_call | solution.py:162
  21.8 0.7 %product.1 = bf16[128,4096]{1,0:T(8,128)(2,1)S(1)} custom-call(bf16[128,512]{1,0:T(8,128)(2,1)S(1)} %get-tuple-element.34.dq_ref, bf16[256,4096]{1,0:T(8,128)(2,1)S(1)} %get-tuple-element.35.wm_ref, bf16[256,4096]{1,0:T(8,128)(2,1)S(1)} %collective-permute-done.9.wo_ref), custom_call_target="tpu_custom_call" | custom-call | flops 536870912 | bytes 4194304 | tf_op jit(solution)/shard_map/product/pallas_call | solution.py:193
  22.6 1.6 %collective-permute-start.10 = (bf16[4,128,128]{2,1,0:T(8,128)(2,1)S(1)}, bf16[4,128,128]{2,1,0:T(8,128)(2,1)S(1)}, u32[]{:S(2)}, u32[]{:S(2)}) collective-permute-start(bf16[4,128,128]{2,1,0:T(8,128)(2,1)S(1)} %slice.26), channel_id=1, source_target_pairs={{0,4},{4,0},{8,12},{12,8},{16,20},{20,16},{24,28},{28,24},{1,5},{5... | collective-permute-start | bytes 393224 | tf_op jit(solution)/shard_map/ppermute | solution.py:26
  24.2 1.5 %collective-permute-start.16 = (bf16[128,4096]{1,0:T(8,128)(2,1)S(1)}, bf16[128,4096]{1,0:T(8,128)(2,1)S(1)}, u32[]{:S(2)}, u32[]{:S(2)}) collective-permute-start(bf16[128,4096]{1,0:T(8,128)(2,1)S(1)} %product.1), channel_id=1, source_target_pairs={{0,2},{1,3},{2,0},{3,1},{4,6},{5,7},{6,4},{7,5},{8,10},{9,11},{10,... | collective-permute-start | bytes 3145736 | tf_op jit(solution)/shard_map/ppermute | solution.py:26
  25.7 2.5 %collective-permute-done.10 = bf16[4,128,128]{2,1,0:T(8,128)(2,1)S(1)} collective-permute-done((bf16[4,128,128]{2,1,0:T(8,128)(2,1)S(1)}, bf16[4,128,128]{2,1,0:T(8,128)(2,1)S(1)}, u32[]{:S(2)}, u32[]{:S(2)}) %collective-permute-start.10) | collective-permute-done | bytes 131104 | tf_op jit(solution)/shard_map/ppermute | solution.py:26
  28.4 3.0 %collective-permute-start.12 = (bf16[128,128]{1,0:T(8,128)(2,1)S(1)}, bf16[128,128]{1,0:T(8,128)(2,1)S(1)}, u32[]{:S(2)}, u32[]{:S(2)}) collective-permute-start(bf16[128,128]{1,0:T(8,128)(2,1)S(1)} %get-tuple-element.49), channel_id=1, source_target_pairs={{0,16},{4,20},{8,24},{12,28},{16,0},{20,4},{24,8},{28,12},{1,17},{... | collective-permute-start | bytes 98312 | tf_op jit(solution)/shard_map/ppermute | solution.py:26
  31.4 1.4 %collective-permute-start.13 = (bf16[128,128]{1,0:T(8,128)(2,1)S(1)}, bf16[128,128]{1,0:T(8,128)(2,1)S(1)}, u32[]{:S(2)}, u32[]{:S(2)}) collective-permute-start(bf16[128,128]{1,0:T(8,128)(2,1)S(1)} %get-tuple-element.48), channel_id=1, source_target_pairs={{0,24},{4,28},{8,16},{12,20},{16,8},{20,12},{24,0},{28,4},{1,25},{... | collective-permute-start | bytes 98312 | tf_op jit(solution)/shard_map/ppermute | solution.py:26
  32.7 0.7 %collective-permute-done.12 = bf16[128,128]{1,0:T(8,128)(2,1)S(1)} collective-permute-done((bf16[128,128]{1,0:T(8,128)(2,1)S(1)}, bf16[128,128]{1,0:T(8,128)(2,1)S(1)}, u32[]{:S(2)}, u32[]{:S(2)}) %collective-permute-start.12) | collective-permute-done | bytes 32800 | tf_op jit(solution)/shard_map/ppermute | solution.py:26
  33.5 3.6 %collective-permute-done.13 = bf16[128,128]{1,0:T(8,128)(2,1)S(1)} collective-permute-done((bf16[128,128]{1,0:T(8,128)(2,1)S(1)}, bf16[128,128]{1,0:T(8,128)(2,1)S(1)}, u32[]{:S(2)}, u32[]{:S(2)}) %collective-permute-start.13) | collective-permute-done | bytes 32800 | tf_op jit(solution)/shard_map/ppermute | solution.py:26
  37.3 1.1 %collective-permute-done.14 = bf16[128,128]{1,0:T(8,128)(2,1)S(1)} collective-permute-done((bf16[128,128]{1,0:T(8,128)(2,1)S(1)}, bf16[128,128]{1,0:T(8,128)(2,1)S(1)}, u32[]{:S(2)}, u32[]{:S(2)}) %collective-permute-start.14) | collective-permute-done | bytes 32800 | tf_op jit(solution)/shard_map/ppermute | solution.py:26
  38.4 2.8 %carve.1 = (bf16[256,4096]{1,0:T(8,128)(2,1)S(1)}, bf16[256,4096]{1,0:T(8,128)(2,1)S(1)}) custom-call(s32[2]{0:T(128)S(1)} %pad_add_fusion.block_ref, bf16[256,16384]{1,0:T(8,128)(2,1)} %w_ref.2, bf16[128,256]{1,0:T(8,128)(2,1)S(1)} %pad_maximum_fusion.3.refs_0_.kv_ref), custom_call_target="tpu_custom_call" | custom-call | tf_op jit(solution)/shard_map/carve/pallas_call | solution.py:73
  41.2 0.7 %own.1 = (f32[128,4096]{1,0:T(8,128)S(1)}, bf16[128,2048]{1,0:T(8,128)(2,1)S(1)}, bf16[128,2048]{1,0:T(8,128)(2,1)S(1)}) custom-call(bf16[128,512]{1,0:T(8,128)(2,1)S(1)} %get-tuple-element.34.dq_ref, bf16[256,4096]{1,0:T(8,128)(2,1)S(1)} %get-tuple-element.38.wn_ref, bf16[256,4096]{1,0:T(8,128)(2,1)S(1)} %get-tuple-element.39.wo_ref), custom_call_target="tpu_custom_call" | custom-call | tf_op jit(solution)/shard_map/own/pallas_call | solution.py:218
  41.9 0.2 collective-permute-start.17
  42.2 0.3 collective-permute-start.18
  42.5 1.5 %collective-permute-start.15 = (bf16[128,256]{1,0:T(8,128)(2,1)S(1)}, bf16[128,256]{1,0:T(8,128)(2,1)S(1)}, u32[]{:S(2)}, u32[]{:S(2)}) collective-permute-start(bf16[128,256]{1,0:T(8,128)(2,1)S(1)} %pad_maximum_fusion.3.refs_0_.kv_ref), channel_id=1, source_target_pairs={{0,2},{1,3},{2,0},{3,1},{4,6},{5,7},{6,4},{7,5},{8,10},{9,11},{10,... | collective-permute-start | bytes 196616 | tf_op jit(solution)/shard_map/ppermute | solution.py:26
  44.0 6.5 %collective-permute-done.15.kv_far_ref = bf16[128,256]{1,0:T(8,128)(2,1)S(1)} collective-permute-done((bf16[128,256]{1,0:T(8,128)(2,1)S(1)}, bf16[128,256]{1,0:T(8,128)(2,1)S(1)}, u32[]{:S(2)}, u32[]{:S(2)}) %collective-permute-start.15) | collective-permute-done | bytes 65568 | tf_op jit(solution)/shard_map/ppermute | solution.py:26
  50.5 1.4 %finish.1 = bf16[128,4096]{1,0:T(8,128)(2,1)} custom-call(s32[1]{0:T(128)} %bitcast.core_ref, bf16[128,256]{1,0:T(8,128)(2,1)S(1)} %pad_maximum_fusion.3.refs_0_.kv_ref, bf16[128,256]{1,0:T(8,128)(2,1)S(1)} %collective-permute-done.15.kv_far_ref, bf16[256,4096]{1,0:T(8,128)(2,1)S(1)} %copy-done, f32[128,4096]{1,0:T(8,128)S(1)} %get-tuple-element.40.acc_ref, ...), custom_call_target="tpu_custom_call" | custom-call | flops 268435456 | bytes 5242880 | tf_op jit(solution)/shard_map/finish/pallas_call | solution.py:258
  (38 shorter events, 0.8 us)
Async XLA Ops:
  1.7 5.7 %collective-permute-start = (bf16[144,128]{1,0:T(8,128)(2,1)S(1)}, bf16[144,128]{1,0:T(8,128)(2,1)S(1)}, u32[]{:S(2)}, u32[]{:S(2)}) collective-permute-start(bf16[144,128]{1,0:T(8,128)(2,1)S(1)} %get-tuple-element.51), channel_id=1, source_target_pairs={{0,8},{4,12},{8,0},{12,4},{16,24},{20,28},{24,16},{28,20},{1,9},{5... | collective-permute-start | bytes 110600 | tf_op jit(solution)/shard_map/ppermute | solution.py:26
  4.8 7.0 %collective-permute-start.1 = (bf16[144,128]{1,0:T(8,128)(2,1)S(1)}, bf16[144,128]{1,0:T(8,128)(2,1)S(1)}, u32[]{:S(2)}, u32[]{:S(2)}) collective-permute-start(bf16[144,128]{1,0:T(8,128)(2,1)S(1)} %get-tuple-element.51), channel_id=1, source_target_pairs={{0,16},{4,20},{8,24},{12,28},{16,0},{20,4},{24,8},{28,12},{1,17},{... | collective-permute-start | bytes 110600 | tf_op jit(solution)/shard_map/ppermute | solution.py:26
  7.4 5.8 %collective-permute-start.2 = (bf16[144,128]{1,0:T(8,128)(2,1)S(1)}, bf16[144,128]{1,0:T(8,128)(2,1)S(1)}, u32[]{:S(2)}, u32[]{:S(2)}) collective-permute-start(bf16[144,128]{1,0:T(8,128)(2,1)S(1)} %get-tuple-element.51), channel_id=1, source_target_pairs={{0,24},{4,28},{8,16},{12,20},{16,8},{20,12},{24,0},{28,4},{1,25},{... | collective-permute-start | bytes 110600 | tf_op jit(solution)/shard_map/ppermute | solution.py:26
  7.4 7.6 %copy-start.1 = (bf16[128,256]{1,0:T(8,128)(2,1)S(1)}, bf16[128,256]{1,0:T(8,128)(2,1)}, u32[]{:S(2)}) copy-start(bf16[128,256]{1,0:T(8,128)(2,1)} %qm_ref) | copy-start | bytes 196612
  7.5 8.0 %copy-start.2 = (bf16[128,256]{1,0:T(8,128)(2,1)S(1)}, bf16[128,256]{1,0:T(8,128)(2,1)}, u32[]{:S(2)}) copy-start(bf16[128,256]{1,0:T(8,128)(2,1)} %gm_ref) | copy-start | bytes 196612
  7.5 12.0 %copy-start.3 = (s32[128]{0:T(128)S(1)}, s32[128]{0:T(128)}, u32[]{:S(2)}) copy-start(s32[128]{0:T(128)} %param.12) | copy-start | bytes 1540
  7.5 11.9 %copy-start.4 = (s32[128]{0:T(128)S(1)}, s32[128]{0:T(128)}, u32[]{:S(2)}) copy-start(s32[128]{0:T(128)} %param.13) | copy-start | bytes 1540
  7.5 5.7 %collective-permute-start.3 = (bf16[2,144,128]{2,1,0:T(8,128)(2,1)S(1)}, bf16[2,144,128]{2,1,0:T(8,128)(2,1)S(1)}, u32[]{:S(2)}, u32[]{:S(2)}) collective-permute-start(bf16[2,144,128]{2,1,0:T(8,128)(2,1)S(1)} %pad_maximum_fusion.2), channel_id=1, source_target_pairs={{0,4},{4,0},{8,12},{12,8},{16,20},{20,16},{24,28},{28,24},{1,5},{5... | collective-permute-start | bytes 221192 | tf_op jit(solution)/shard_map/ppermute | solution.py:26
  13.2 8.6 %collective-permute-start.9 = (bf16[256,4096]{1,0:T(8,128)(2,1)S(1)}, bf16[256,4096]{1,0:T(8,128)(2,1)S(1)}, u32[]{:S(2)}, u32[]{:S(2)}) collective-permute-start(bf16[256,4096]{1,0:T(8,128)(2,1)S(1)} %get-tuple-element.36), channel_id=1, source_target_pairs={{0,1},{1,0},{2,3},{3,2},{4,5},{5,4},{6,7},{7,6},{8,9},{9,8},{10,11... | collective-permute-start | bytes 6291464 | tf_op jit(solution)/shard_map/ppermute | solution.py:26
  13.3 4.7 %collective-permute-start.4 = (bf16[2,144,128]{2,1,0:T(8,128)(2,1)S(1)}, bf16[2,144,128]{2,1,0:T(8,128)(2,1)S(1)}, u32[]{:S(2)}, u32[]{:S(2)}) collective-permute-start(bf16[2,144,128]{2,1,0:T(8,128)(2,1)S(1)} %pad_maximum_fusion.1), channel_id=1, source_target_pairs={{0,4},{4,0},{8,12},{12,8},{16,20},{20,16},{24,28},{28,24},{1,5},{5... | collective-permute-start | bytes 221192 | tf_op jit(solution)/shard_map/ppermute | solution.py:26
  14.9 3.2 %collective-permute-start.7 = (bf16[4,144,128]{2,1,0:T(8,128)(2,1)S(1)}, bf16[4,144,128]{2,1,0:T(8,128)(2,1)S(1)}, u32[]{:S(2)}, u32[]{:S(2)}) collective-permute-start(bf16[4,144,128]{2,1,0:T(8,128)(2,1)S(1)} %pad_maximum_fusion.refs_0_), channel_id=1, source_target_pairs={{0,1},{1,0},{2,3},{3,2},{4,5},{5,4},{6,7},{7,6},{8,9},{9,8},{10,11... | collective-permute-start | bytes 442376 | tf_op jit(solution)/shard_map/ppermute | solution.py:26
  15.1 2.6 %collective-permute-start.5 = (bf16[128,256]{1,0:T(8,128)(2,1)S(1)}, bf16[128,256]{1,0:T(8,128)(2,1)S(1)}, u32[]{:S(2)}, u32[]{:S(2)}) collective-permute-start(bf16[128,256]{1,0:T(8,128)(2,1)S(1)} %copy-done.1), channel_id=1, source_target_pairs={{0,1},{1,0},{2,3},{3,2},{4,5},{5,4},{6,7},{7,6},{8,9},{9,8},{10,11... | collective-permute-start | bytes 196616 | tf_op jit(solution)/shard_map/ppermute | solution.py:26
  15.4 2.4 %collective-permute-start.6 = (bf16[128,256]{1,0:T(8,128)(2,1)S(1)}, bf16[128,256]{1,0:T(8,128)(2,1)S(1)}, u32[]{:S(2)}, u32[]{:S(2)}) collective-permute-start(bf16[128,256]{1,0:T(8,128)(2,1)S(1)} %copy-done.2), channel_id=1, source_target_pairs={{0,1},{1,0},{2,3},{3,2},{4,5},{5,4},{6,7},{7,6},{8,9},{9,8},{10,11... | collective-permute-start | bytes 196616 | tf_op jit(solution)/shard_map/ppermute | solution.py:26
  18.0 1.4 %collective-permute-start.8 = (bf16[4,144,128]{2,1,0:T(8,128)(2,1)S(1)}, bf16[4,144,128]{2,1,0:T(8,128)(2,1)S(1)}, u32[]{:S(2)}, u32[]{:S(2)}) collective-permute-start(bf16[4,144,128]{2,1,0:T(8,128)(2,1)S(1)} %constant_dynamic-update-slice_fusion.refs_2_), channel_id=1, source_target_pairs={{0,1},{1,0},{2,3},{3,2},{4,5},{5,4},{6,7},{7,6},{8,9},{9,8},{10,11... | collective-permute-start | bytes 442376 | tf_op jit(solution)/shard_map/ppermute | solution.py:26
  22.6 5.6 %collective-permute-start.10 = (bf16[4,128,128]{2,1,0:T(8,128)(2,1)S(1)}, bf16[4,128,128]{2,1,0:T(8,128)(2,1)S(1)}, u32[]{:S(2)}, u32[]{:S(2)}) collective-permute-start(bf16[4,128,128]{2,1,0:T(8,128)(2,1)S(1)} %slice.26), channel_id=1, source_target_pairs={{0,4},{4,0},{8,12},{12,8},{16,20},{20,16},{24,28},{28,24},{1,5},{5... | collective-permute-start | bytes 393224 | tf_op jit(solution)/shard_map/ppermute | solution.py:26
  24.2 26.3 %collective-permute-start.16 = (bf16[128,4096]{1,0:T(8,128)(2,1)S(1)}, bf16[128,4096]{1,0:T(8,128)(2,1)S(1)}, u32[]{:S(2)}, u32[]{:S(2)}) collective-permute-start(bf16[128,4096]{1,0:T(8,128)(2,1)S(1)} %product.1), channel_id=1, source_target_pairs={{0,2},{1,3},{2,0},{3,1},{4,6},{5,7},{6,4},{7,5},{8,10},{9,11},{10,... | collective-permute-start | bytes 3145736 | tf_op jit(solution)/shard_map/ppermute | solution.py:26
  28.3 4.5 %collective-permute-start.11 = (bf16[128,128]{1,0:T(8,128)(2,1)S(1)}, bf16[128,128]{1,0:T(8,128)(2,1)S(1)}, u32[]{:S(2)}, u32[]{:S(2)}) collective-permute-start(bf16[128,128]{1,0:T(8,128)(2,1)S(1)} %get-tuple-element.47), channel_id=1, source_target_pairs={{0,8},{4,12},{8,0},{12,4},{16,24},{20,28},{24,16},{28,20},{1,9},{5... | collective-permute-start | bytes 98312 | tf_op jit(solution)/shard_map/ppermute | solution.py:26
  28.4 5.1 %collective-permute-start.12 = (bf16[128,128]{1,0:T(8,128)(2,1)S(1)}, bf16[128,128]{1,0:T(8,128)(2,1)S(1)}, u32[]{:S(2)}, u32[]{:S(2)}) collective-permute-start(bf16[128,128]{1,0:T(8,128)(2,1)S(1)} %get-tuple-element.49), channel_id=1, source_target_pairs={{0,16},{4,20},{8,24},{12,28},{16,0},{20,4},{24,8},{28,12},{1,17},{... | collective-permute-start | bytes 98312 | tf_op jit(solution)/shard_map/ppermute | solution.py:26
  31.4 5.7 %collective-permute-start.13 = (bf16[128,128]{1,0:T(8,128)(2,1)S(1)}, bf16[128,128]{1,0:T(8,128)(2,1)S(1)}, u32[]{:S(2)}, u32[]{:S(2)}) collective-permute-start(bf16[128,128]{1,0:T(8,128)(2,1)S(1)} %get-tuple-element.48), channel_id=1, source_target_pairs={{0,24},{4,28},{8,16},{12,20},{16,8},{20,12},{24,0},{28,4},{1,25},{... | collective-permute-start | bytes 98312 | tf_op jit(solution)/shard_map/ppermute | solution.py:26
  37.1 1.3 %collective-permute-start.14 = (bf16[128,128]{1,0:T(8,128)(2,1)S(1)}, bf16[128,128]{1,0:T(8,128)(2,1)S(1)}, u32[]{:S(2)}, u32[]{:S(2)}) collective-permute-start(bf16[128,128]{1,0:T(8,128)(2,1)S(1)} %fusion.3), channel_id=1, source_target_pairs={{0,1},{1,0},{2,3},{3,2},{4,5},{5,4},{6,7},{7,6},{8,9},{9,8},{10,11... | collective-permute-start | bytes 98312 | tf_op jit(solution)/shard_map/ppermute | solution.py:26
  41.2 9.3 %copy-start = (bf16[256,4096]{1,0:T(8,128)(2,1)S(1)}, bf16[256,4096]{1,0:T(8,128)(2,1)}, u32[]{:S(2)}) copy-start(bf16[256,4096]{1,0:T(8,128)(2,1)} %w_ref.3) | copy-start | bytes 6291460
  41.9 8.6 %collective-permute-start.17 = (bf16[128,2048]{1,0:T(8,128)(2,1)S(1)}, bf16[128,2048]{1,0:T(8,128)(2,1)S(1)}, u32[]{:S(2)}, u32[]{:S(2)}) collective-permute-start(bf16[128,2048]{1,0:T(8,128)(2,1)S(1)} %get-tuple-element.41), channel_id=1, source_target_pairs={{0,1},{1,0},{2,3},{3,2},{4,5},{5,4},{6,7},{7,6},{8,9},{9,8},{10,11... | collective-permute-start | bytes 1572872 | tf_op jit(solution)/shard_map/ppermute | solution.py:26
  42.2 8.3 %collective-permute-start.18 = (bf16[128,2048]{1,0:T(8,128)(2,1)S(1)}, bf16[128,2048]{1,0:T(8,128)(2,1)S(1)}, u32[]{:S(2)}, u32[]{:S(2)}) collective-permute-start(bf16[128,2048]{1,0:T(8,128)(2,1)S(1)} %get-tuple-element.42), channel_id=1, source_target_pairs={{0,1},{1,0},{2,3},{3,2},{4,5},{5,4},{6,7},{7,6},{8,9},{9,8},{10,11... | collective-permute-start | bytes 1572872 | tf_op jit(solution)/shard_map/ppermute | solution.py:26
  42.5 8.0 %collective-permute-start.15 = (bf16[128,256]{1,0:T(8,128)(2,1)S(1)}, bf16[128,256]{1,0:T(8,128)(2,1)S(1)}, u32[]{:S(2)}, u32[]{:S(2)}) collective-permute-start(bf16[128,256]{1,0:T(8,128)(2,1)S(1)} %pad_maximum_fusion.3.refs_0_.kv_ref), channel_id=1, source_target_pairs={{0,2},{1,3},{2,0},{3,1},{4,6},{5,7},{6,4},{7,5},{8,10},{9,11},{10,... | collective-permute-start | bytes 196616 | tf_op jit(solution)/shard_map/ppermute | solution.py:26

commit v21 on v20

--- a/solution.py
+++ b/solution.py
@@ -278,7 +278,7 @@
 
     piece = pack(core, positions, keys, values)
     along_z = [piece] + [swapped(piece, "ctx", 2 * s) for s in range(1, half)]
-    early = (half + 1) // 2
+    early = 1
     z_early, z_late = jnp.stack(along_z[:early]), jnp.stack(along_z[early:])
     x_early = swapped(z_early, "ctx", 1)
     far_send = column_block(w_query, head ^ 3, share, z_early)

time: 52.2 us -> 52.8 us (1.011)
  waiting for transfers between devices: 19.5 us -> 20.4 us
    ppermute x19, waiting for transfers between devices: 19.5 us -> 20.4 us  [swapped(): lax.ppermute(value, axis, [(source, source ^ bits) for source in range(co...]
where the time goes in v21:
time: 52.8 us; the launch traced here: 52.6 us
  waiting for transfers between devices  20.4 us (39%)
  starting transfers between devices  19.5 us (37%)
  Pallas kernels  7.94 us (15%)
  local copies, waits for them, and re-layouts  3.43 us (6%)
  other arithmetic  1.17 us (2%)
    ppermute x19, waiting for transfers between devices, swapped(): lax.ppermute(value, axis, [(source, source ^ bits) for source in range(co...  20.4 us
    ppermute x19, starting transfers between devices, swapped(): lax.ppermute(value, axis, [(source, source ^ bits) for source in range(co...  19.5 us
    pallas_call x1, Pallas kernels, carve(): pl.pallas_call(carve_kernel, out_shape=[block] * count, in_specs=[SMEM, H...  2.76 us
    dynamic_slice x1, local copies, waits for them, and re-layouts, column_block(): return lax.dynamic_slice_in_dim(w_query, block * share, share, axis=1)  2.63 us
    pallas_call x1, Pallas kernels, attention(): pl.pallas_call(attention_kernel, out_shape=[jax.ShapeDtypeStruct((rows, 2...  2.38 us
    pallas_call x1, Pallas kernels, finish(): pl.pallas_call(finish_kernel, out_shape=jax.ShapeDtypeStruct((rows, share...  1.33 us
  transfers between devices with their start and end apart: 19, of which 10 were waited for; matrix products, arithmetic and copies ran while one was open for 5% of the time, Pallas kernels for 11%

profile of v21, /device:TPU:0, one launch (start us, length us, event | category | flops | bytes accessed | tf_op | source)
XLA Modules:
  0.0 52.6 jit_solution(15871551727186952551)
XLA Ops:
  0.0 0.7 %reshape.19 = s32[2,64]{1,0:T(2,128)S(1)} reshape(s32[128]{0:T(128)} %param.12) | data formatting | bytes 1024 | tf_op jit(solution)/shard_map/reshape | solution.py:44
  0.7 0.1 fusion.5
  0.9 0.8 %broadcast_select_fusion = bf16[128,128]{1,0:T(8,128)(2,1)S(1)} fusion(bf16[128,128]{1,0:T(8,128)(2,1)} %param.9, bf16[128,128]{1,0:T(8,128)(2,1)} %param.10, pred[]{:T(512)} %bitcast.3), kind=kLoop, calls=%fused_computation.13 | loop fusion | flops 16384 | bytes 98305 | tf_op jit(solution)/shard_map/jit(_where)/select_n | solution.py:43
  1.7 3.1 %collective-permute-start = (bf16[144,128]{1,0:T(8,128)(2,1)S(1)}, bf16[144,128]{1,0:T(8,128)(2,1)S(1)}, u32[]{:S(2)}, u32[]{:S(2)}) collective-permute-start(bf16[144,128]{1,0:T(8,128)(2,1)S(1)} %get-tuple-element.51), channel_id=1, source_target_pairs={{0,8},{4,12},{8,0},{12,4},{16,24},{20,28},{24,16},{28,20},{1,9},{5... | collective-permute-start | bytes 110600 | tf_op jit(solution)/shard_map/ppermute | solution.py:26
  4.8 2.6 %collective-permute-start.1 = (bf16[144,128]{1,0:T(8,128)(2,1)S(1)}, bf16[144,128]{1,0:T(8,128)(2,1)S(1)}, u32[]{:S(2)}, u32[]{:S(2)}) collective-permute-start(bf16[144,128]{1,0:T(8,128)(2,1)S(1)} %get-tuple-element.51), channel_id=1, source_target_pairs={{0,16},{4,20},{8,24},{12,28},{16,0},{20,4},{24,8},{28,12},{1,17},{... | collective-permute-start | bytes 110600 | tf_op jit(solution)/shard_map/ppermute | solution.py:26
  7.4 1.7 %collective-permute-start.3 = (bf16[1,144,128]{2,1,0:T(8,128)(2,1)S(1)}, bf16[1,144,128]{2,1,0:T(8,128)(2,1)S(1)}, u32[]{:S(2)}, u32[]{:S(2)}) collective-permute-start(bf16[1,144,128]{2,1,0:T(8,128)(2,1)S(1)} %get-tuple-element.50), channel_id=1, source_target_pairs={{0,4},{4,0},{8,12},{12,8},{16,20},{20,16},{24,28},{28,24},{1,5},{5... | collective-permute-start | bytes 110600 | tf_op jit(solution)/shard_map/ppermute | solution.py:26
  9.1 2.6 %constant_dynamic-slice_fusion = (bf16[256,4096]{1,0:T(8,128)(2,1)S(1)}, bf16[256,4096]{1,0:T(8,128)(2,1)S(1)}) fusion(bf16[256,16384]{1,0:T(8,128)(2,1)} %w_ref.2, s32[]{:T(128)S(6)} %select_n.18, s32[]{:T(128)S(6)} %select_n.17), kind=kLoop, calls=%fused_computation.23 | loop fusion | bytes 8388616 | tf_op jit(solution)/shard_map/dynamic_slice | solution.py:51
  11.8 1.4 %collective-permute-done.2 = bf16[144,128]{1,0:T(8,128)(2,1)S(1)} collective-permute-done((bf16[144,128]{1,0:T(8,128)(2,1)S(1)}, bf16[144,128]{1,0:T(8,128)(2,1)S(1)}, u32[]{:S(2)}, u32[]{:S(2)}) %collective-permute-start.2) | collective-permute-done | bytes 36896 | tf_op jit(solution)/shard_map/ppermute | solution.py:26
  13.3 1.6 %collective-permute-start.4 = (bf16[3,144,128]{2,1,0:T(8,128)(2,1)S(1)}, bf16[3,144,128]{2,1,0:T(8,128)(2,1)S(1)}, u32[]{:S(2)}, u32[]{:S(2)}) collective-permute-start(bf16[3,144,128]{2,1,0:T(8,128)(2,1)S(1)} %pad_maximum_fusion.1), channel_id=1, source_target_pairs={{0,4},{4,0},{8,12},{12,8},{16,20},{20,16},{24,28},{28,24},{1,5},{5... | collective-permute-start | bytes 331784 | tf_op jit(solution)/shard_map/ppermute | solution.py:26
  14.9 0.2 collective-permute-start.7
  15.1 0.3 collective-permute-start.5
  15.4 0.2 collective-permute-start.6
  15.6 2.1 %collective-permute-done.5.qo_ref = bf16[128,256]{1,0:T(8,128)(2,1)S(1)} collective-permute-done((bf16[128,256]{1,0:T(8,128)(2,1)S(1)}, bf16[128,256]{1,0:T(8,128)(2,1)S(1)}, u32[]{:S(2)}, u32[]{:S(2)}) %collective-permute-start.5) | collective-permute-done | bytes 65568 | tf_op jit(solution)/shard_map/ppermute | solution.py:26
  17.8 0.9 %collective-permute-done.4 = bf16[3,144,128]{2,1,0:T(8,128)(2,1)S(1)} collective-permute-done((bf16[3,144,128]{2,1,0:T(8,128)(2,1)S(1)}, bf16[3,144,128]{2,1,0:T(8,128)(2,1)S(1)}, u32[]{:S(2)}, u32[]{:S(2)}) %collective-permute-start.4) | collective-permute-done | bytes 110624 | tf_op jit(solution)/shard_map/ppermute | solution.py:26
  18.9 1.3 %collective-permute-done.8.refs_3_ = bf16[4,144,128]{2,1,0:T(8,128)(2,1)S(1)} collective-permute-done((bf16[4,144,128]{2,1,0:T(8,128)(2,1)S(1)}, bf16[4,144,128]{2,1,0:T(8,128)(2,1)S(1)}, u32[]{:S(2)}, u32[]{:S(2)}) %collective-permute-start.8) | collective-permute-done | bytes 147488 | tf_op jit(solution)/shard_map/ppermute | solution.py:26
  20.2 2.4 %attention.1 = (bf16[128,512]{1,0:T(8,128)(2,1)S(1)}, bf16[8,128,128]{2,1,0:T(8,128)(2,1)S(1)}) custom-call(s32[1]{0:T(128)} %bitcast.core_ref, s32[1,128]{1,0:T(1,128)S(1)} %bitcast.27, s32[1,128]{1,0:T(1,128)S(1)} %bitcast.28, bf16[128,256]{1,0:T(8,128)(2,1)S(1)} %copy-done.1, bf16[128,256]{1,0:T(8,128)(2,1)S(1)} %collective-permute-done.5.qo_ref, ...), custom_call_target="tpu_custom_call" | custom-call | flops 671088640 | bytes 1048576 | tf_op jit(solution)/shard_map/attention/pallas_call | solution.py:162
  22.6 0.7 %product.1 = bf16[128,4096]{1,0:T(8,128)(2,1)S(1)} custom-call(bf16[128,512]{1,0:T(8,128)(2,1)S(1)} %get-tuple-element.34.dq_ref, bf16[256,4096]{1,0:T(8,128)(2,1)S(1)} %get-tuple-element.35.wm_ref, bf16[256,4096]{1,0:T(8,128)(2,1)S(1)} %collective-permute-done.9.wo_ref), custom_call_target="tpu_custom_call" | custom-call | flops 536870912 | bytes 4194304 | tf_op jit(solution)/shard_map/product/pallas_call | solution.py:193
  23.4 1.6 %collective-permute-start.10 = (bf16[4,128,128]{2,1,0:T(8,128)(2,1)S(1)}, bf16[4,128,128]{2,1,0:T(8,128)(2,1)S(1)}, u32[]{:S(2)}, u32[]{:S(2)}) collective-permute-start(bf16[4,128,128]{2,1,0:T(8,128)(2,1)S(1)} %slice.26), channel_id=1, source_target_pairs={{0,4},{4,0},{8,12},{12,8},{16,20},{20,16},{24,28},{28,24},{1,5},{5... | collective-permute-start | bytes 393224 | tf_op jit(solution)/shard_map/ppermute | solution.py:26
  24.9 1.5 %collective-permute-start.16 = (bf16[128,4096]{1,0:T(8,128)(2,1)S(1)}, bf16[128,4096]{1,0:T(8,128)(2,1)S(1)}, u32[]{:S(2)}, u32[]{:S(2)}) collective-permute-start(bf16[128,4096]{1,0:T(8,128)(2,1)S(1)} %product.1), channel_id=1, source_target_pairs={{0,2},{1,3},{2,0},{3,1},{4,6},{5,7},{6,4},{7,5},{8,10},{9,11},{10,... | collective-permute-start | bytes 3145736 | tf_op jit(solution)/shard_map/ppermute | solution.py:26
  26.5 2.5 %collective-permute-done.10 = bf16[4,128,128]{2,1,0:T(8,128)(2,1)S(1)} collective-permute-done((bf16[4,128,128]{2,1,0:T(8,128)(2,1)S(1)}, bf16[4,128,128]{2,1,0:T(8,128)(2,1)S(1)}, u32[]{:S(2)}, u32[]{:S(2)}) %collective-permute-start.10) | collective-permute-done | bytes 131104 | tf_op jit(solution)/shard_map/ppermute | solution.py:26
  29.1 2.8 %collective-permute-start.12 = (bf16[128,128]{1,0:T(8,128)(2,1)S(1)}, bf16[128,128]{1,0:T(8,128)(2,1)S(1)}, u32[]{:S(2)}, u32[]{:S(2)}) collective-permute-start(bf16[128,128]{1,0:T(8,128)(2,1)S(1)} %get-tuple-element.49), channel_id=1, source_target_pairs={{0,16},{4,20},{8,24},{12,28},{16,0},{20,4},{24,8},{28,12},{1,17},{... | collective-permute-start | bytes 98312 | tf_op jit(solution)/shard_map/ppermute | solution.py:26
  31.9 1.6 %collective-permute-start.13 = (bf16[128,128]{1,0:T(8,128)(2,1)S(1)}, bf16[128,128]{1,0:T(8,128)(2,1)S(1)}, u32[]{:S(2)}, u32[]{:S(2)}) collective-permute-start(bf16[128,128]{1,0:T(8,128)(2,1)S(1)} %get-tuple-element.48), channel_id=1, source_target_pairs={{0,24},{4,28},{8,16},{12,20},{16,8},{20,12},{24,0},{28,4},{1,25},{... | collective-permute-start | bytes 98312 | tf_op jit(solution)/shard_map/ppermute | solution.py:26
  33.5 0.6 %collective-permute-done.12 = bf16[128,128]{1,0:T(8,128)(2,1)S(1)} collective-permute-done((bf16[128,128]{1,0:T(8,128)(2,1)S(1)}, bf16[128,128]{1,0:T(8,128)(2,1)S(1)}, u32[]{:S(2)}, u32[]{:S(2)}) %collective-permute-start.12) | collective-permute-done | bytes 32800 | tf_op jit(solution)/shard_map/ppermute | solution.py:26
  34.1 3.5 %collective-permute-done.13 = bf16[128,128]{1,0:T(8,128)(2,1)S(1)} collective-permute-done((bf16[128,128]{1,0:T(8,128)(2,1)S(1)}, bf16[128,128]{1,0:T(8,128)(2,1)S(1)}, u32[]{:S(2)}, u32[]{:S(2)}) %collective-permute-start.13) | collective-permute-done | bytes 32800 | tf_op jit(solution)/shard_map/ppermute | solution.py:26
  37.8 1.1 %collective-permute-done.14 = bf16[128,128]{1,0:T(8,128)(2,1)S(1)} collective-permute-done((bf16[128,128]{1,0:T(8,128)(2,1)S(1)}, bf16[128,128]{1,0:T(8,128)(2,1)S(1)}, u32[]{:S(2)}, u32[]{:S(2)}) %collective-permute-start.14) | collective-permute-done | bytes 32800 | tf_op jit(solution)/shard_map/ppermute | solution.py:26
  39.0 2.8 %carve.1 = (bf16[256,4096]{1,0:T(8,128)(2,1)S(1)}, bf16[256,4096]{1,0:T(8,128)(2,1)S(1)}) custom-call(s32[2]{0:T(128)S(1)} %pad_add_fusion.block_ref, bf16[256,16384]{1,0:T(8,128)(2,1)} %w_ref.2, bf16[128,256]{1,0:T(8,128)(2,1)S(1)} %pad_maximum_fusion.2.refs_0_.kv_ref), custom_call_target="tpu_custom_call" | custom-call | tf_op jit(solution)/shard_map/carve/pallas_call | solution.py:73
  41.7 0.7 %own.1 = (f32[128,4096]{1,0:T(8,128)S(1)}, bf16[128,2048]{1,0:T(8,128)(2,1)S(1)}, bf16[128,2048]{1,0:T(8,128)(2,1)S(1)}) custom-call(bf16[128,512]{1,0:T(8,128)(2,1)S(1)} %get-tuple-element.34.dq_ref, bf16[256,4096]{1,0:T(8,128)(2,1)S(1)} %get-tuple-element.38.wn_ref, bf16[256,4096]{1,0:T(8,128)(2,1)S(1)} %get-tuple-element.39.wo_ref), custom_call_target="tpu_custom_call" | custom-call | tf_op jit(solution)/shard_map/own/pallas_call | solution.py:218
  42.5 0.2 collective-permute-start.17
  42.7 0.4 collective-permute-start.18
  43.0 1.5 %collective-permute-start.15 = (bf16[128,256]{1,0:T(8,128)(2,1)S(1)}, bf16[128,256]{1,0:T(8,128)(2,1)S(1)}, u32[]{:S(2)}, u32[]{:S(2)}) collective-permute-start(bf16[128,256]{1,0:T(8,128)(2,1)S(1)} %pad_maximum_fusion.2.refs_0_.kv_ref), channel_id=1, source_target_pairs={{0,2},{1,3},{2,0},{3,1},{4,6},{5,7},{6,4},{7,5},{8,10},{9,11},{10,... | collective-permute-start | bytes 196616 | tf_op jit(solution)/shard_map/ppermute | solution.py:26
  44.6 6.7 %collective-permute-done.15.kv_far_ref = bf16[128,256]{1,0:T(8,128)(2,1)S(1)} collective-permute-done((bf16[128,256]{1,0:T(8,128)(2,1)S(1)}, bf16[128,256]{1,0:T(8,128)(2,1)S(1)}, u32[]{:S(2)}, u32[]{:S(2)}) %collective-permute-start.15) | collective-permute-done | bytes 65568 | tf_op jit(solution)/shard_map/ppermute | solution.py:26
  51.3 1.3 %finish.1 = bf16[128,4096]{1,0:T(8,128)(2,1)} custom-call(s32[1]{0:T(128)} %bitcast.core_ref, bf16[128,256]{1,0:T(8,128)(2,1)S(1)} %pad_maximum_fusion.2.refs_0_.kv_ref, bf16[128,256]{1,0:T(8,128)(2,1)S(1)} %collective-permute-done.15.kv_far_ref, bf16[256,4096]{1,0:T(8,128)(2,1)S(1)} %copy-done, f32[128,4096]{1,0:T(8,128)S(1)} %get-tuple-element.40.acc_ref, ...), custom_call_target="tpu_custom_call" | custom-call | flops 268435456 | bytes 5242880 | tf_op jit(solution)/shard_map/finish/pallas_call | solution.py:258
  (37 shorter events, 0.7 us)
Async XLA Ops:
  1.7 10.0 %collective-permute-start = (bf16[144,128]{1,0:T(8,128)(2,1)S(1)}, bf16[144,128]{1,0:T(8,128)(2,1)S(1)}, u32[]{:S(2)}, u32[]{:S(2)}) collective-permute-start(bf16[144,128]{1,0:T(8,128)(2,1)S(1)} %get-tuple-element.51), channel_id=1, source_target_pairs={{0,8},{4,12},{8,0},{12,4},{16,24},{20,28},{24,16},{28,20},{1,9},{5... | collective-permute-start | bytes 110600 | tf_op jit(solution)/shard_map/ppermute | solution.py:26
  4.8 7.0 %collective-permute-start.1 = (bf16[144,128]{1,0:T(8,128)(2,1)S(1)}, bf16[144,128]{1,0:T(8,128)(2,1)S(1)}, u32[]{:S(2)}, u32[]{:S(2)}) collective-permute-start(bf16[144,128]{1,0:T(8,128)(2,1)S(1)} %get-tuple-element.51), channel_id=1, source_target_pairs={{0,16},{4,20},{8,24},{12,28},{16,0},{20,4},{24,8},{28,12},{1,17},{... | collective-permute-start | bytes 110600 | tf_op jit(solution)/shard_map/ppermute | solution.py:26
  7.4 5.8 %collective-permute-start.2 = (bf16[144,128]{1,0:T(8,128)(2,1)S(1)}, bf16[144,128]{1,0:T(8,128)(2,1)S(1)}, u32[]{:S(2)}, u32[]{:S(2)}) collective-permute-start(bf16[144,128]{1,0:T(8,128)(2,1)S(1)} %get-tuple-element.51), channel_id=1, source_target_pairs={{0,24},{4,28},{8,16},{12,20},{16,8},{20,12},{24,0},{28,4},{1,25},{... | collective-permute-start | bytes 110600 | tf_op jit(solution)/shard_map/ppermute | solution.py:26
  7.4 5.8 %collective-permute-start.3 = (bf16[1,144,128]{2,1,0:T(8,128)(2,1)S(1)}, bf16[1,144,128]{2,1,0:T(8,128)(2,1)S(1)}, u32[]{:S(2)}, u32[]{:S(2)}) collective-permute-start(bf16[1,144,128]{2,1,0:T(8,128)(2,1)S(1)} %get-tuple-element.50), channel_id=1, source_target_pairs={{0,4},{4,0},{8,12},{12,8},{16,20},{20,16},{24,28},{28,24},{1,5},{5... | collective-permute-start | bytes 110600 | tf_op jit(solution)/shard_map/ppermute | solution.py:26
  9.1 6.0 %copy-start.1 = (bf16[128,256]{1,0:T(8,128)(2,1)S(1)}, bf16[128,256]{1,0:T(8,128)(2,1)}, u32[]{:S(2)}) copy-start(bf16[128,256]{1,0:T(8,128)(2,1)} %qm_ref) | copy-start | bytes 196612
  9.1 6.3 %copy-start.2 = (bf16[128,256]{1,0:T(8,128)(2,1)S(1)}, bf16[128,256]{1,0:T(8,128)(2,1)}, u32[]{:S(2)}) copy-start(bf16[128,256]{1,0:T(8,128)(2,1)} %gm_ref) | copy-start | bytes 196612
  9.1 11.1 %copy-start.3 = (s32[128]{0:T(128)S(1)}, s32[128]{0:T(128)}, u32[]{:S(2)}) copy-start(s32[128]{0:T(128)} %param.12) | copy-start | bytes 1540
  9.1 11.1 %copy-start.4 = (s32[128]{0:T(128)S(1)}, s32[128]{0:T(128)}, u32[]{:S(2)}) copy-start(s32[128]{0:T(128)} %param.13) | copy-start | bytes 1540
  13.2 9.4 %collective-permute-start.9 = (bf16[256,4096]{1,0:T(8,128)(2,1)S(1)}, bf16[256,4096]{1,0:T(8,128)(2,1)S(1)}, u32[]{:S(2)}, u32[]{:S(2)}) collective-permute-start(bf16[256,4096]{1,0:T(8,128)(2,1)S(1)} %get-tuple-element.36), channel_id=1, source_target_pairs={{0,1},{1,0},{2,3},{3,2},{4,5},{5,4},{6,7},{7,6},{8,9},{9,8},{10,11... | collective-permute-start | bytes 6291464 | tf_op jit(solution)/shard_map/ppermute | solution.py:26
  13.3 5.5 %collective-permute-start.4 = (bf16[3,144,128]{2,1,0:T(8,128)(2,1)S(1)}, bf16[3,144,128]{2,1,0:T(8,128)(2,1)S(1)}, u32[]{:S(2)}, u32[]{:S(2)}) collective-permute-start(bf16[3,144,128]{2,1,0:T(8,128)(2,1)S(1)} %pad_maximum_fusion.1), channel_id=1, source_target_pairs={{0,4},{4,0},{8,12},{12,8},{16,20},{20,16},{24,28},{28,24},{1,5},{5... | collective-permute-start | bytes 331784 | tf_op jit(solution)/shard_map/ppermute | solution.py:26
  14.9 4.0 %collective-permute-start.7 = (bf16[4,144,128]{2,1,0:T(8,128)(2,1)S(1)}, bf16[4,144,128]{2,1,0:T(8,128)(2,1)S(1)}, u32[]{:S(2)}, u32[]{:S(2)}) collective-permute-start(bf16[4,144,128]{2,1,0:T(8,128)(2,1)S(1)} %pad_maximum_fusion.refs_0_), channel_id=1, source_target_pairs={{0,1},{1,0},{2,3},{3,2},{4,5},{5,4},{6,7},{7,6},{8,9},{9,8},{10,11... | collective-permute-start | bytes 442376 | tf_op jit(solution)/shard_map/ppermute | solution.py:26
  15.1 2.6 %collective-permute-start.5 = (bf16[128,256]{1,0:T(8,128)(2,1)S(1)}, bf16[128,256]{1,0:T(8,128)(2,1)S(1)}, u32[]{:S(2)}, u32[]{:S(2)}) collective-permute-start(bf16[128,256]{1,0:T(8,128)(2,1)S(1)} %copy-done.1), channel_id=1, source_target_pairs={{0,1},{1,0},{2,3},{3,2},{4,5},{5,4},{6,7},{7,6},{8,9},{9,8},{10,11... | collective-permute-start | bytes 196616 | tf_op jit(solution)/shard_map/ppermute | solution.py:26
  15.4 2.4 %collective-permute-start.6 = (bf16[128,256]{1,0:T(8,128)(2,1)S(1)}, bf16[128,256]{1,0:T(8,128)(2,1)S(1)}, u32[]{:S(2)}, u32[]{:S(2)}) collective-permute-start(bf16[128,256]{1,0:T(8,128)(2,1)S(1)} %copy-done.2), channel_id=1, source_target_pairs={{0,1},{1,0},{2,3},{3,2},{4,5},{5,4},{6,7},{7,6},{8,9},{9,8},{10,11... | collective-permute-start | bytes 196616 | tf_op jit(solution)/shard_map/ppermute | solution.py:26
  18.8 1.4 %collective-permute-start.8 = (bf16[4,144,128]{2,1,0:T(8,128)(2,1)S(1)}, bf16[4,144,128]{2,1,0:T(8,128)(2,1)S(1)}, u32[]{:S(2)}, u32[]{:S(2)}) collective-permute-start(bf16[4,144,128]{2,1,0:T(8,128)(2,1)S(1)} %constant_dynamic-update-slice_fusion.refs_2_), channel_id=1, source_target_pairs={{0,1},{1,0},{2,3},{3,2},{4,5},{5,4},{6,7},{7,6},{8,9},{9,8},{10,11... | collective-permute-start | bytes 442376 | tf_op jit(solution)/shard_map/ppermute | solution.py:26
  23.4 5.6 %collective-permute-start.10 = (bf16[4,128,128]{2,1,0:T(8,128)(2,1)S(1)}, bf16[4,128,128]{2,1,0:T(8,128)(2,1)S(1)}, u32[]{:S(2)}, u32[]{:S(2)}) collective-permute-start(bf16[4,128,128]{2,1,0:T(8,128)(2,1)S(1)} %slice.26), channel_id=1, source_target_pairs={{0,4},{4,0},{8,12},{12,8},{16,20},{20,16},{24,28},{28,24},{1,5},{5... | collective-permute-start | bytes 393224 | tf_op jit(solution)/shard_map/ppermute | solution.py:26
  24.9 26.3 %collective-permute-start.16 = (bf16[128,4096]{1,0:T(8,128)(2,1)S(1)}, bf16[128,4096]{1,0:T(8,128)(2,1)S(1)}, u32[]{:S(2)}, u32[]{:S(2)}) collective-permute-start(bf16[128,4096]{1,0:T(8,128)(2,1)S(1)} %product.1), channel_id=1, source_target_pairs={{0,2},{1,3},{2,0},{3,1},{4,6},{5,7},{6,4},{7,5},{8,10},{9,11},{10,... | collective-permute-start | bytes 3145736 | tf_op jit(solution)/shard_map/ppermute | solution.py:26
  29.1 4.5 %collective-permute-start.11 = (bf16[128,128]{1,0:T(8,128)(2,1)S(1)}, bf16[128,128]{1,0:T(8,128)(2,1)S(1)}, u32[]{:S(2)}, u32[]{:S(2)}) collective-permute-start(bf16[128,128]{1,0:T(8,128)(2,1)S(1)} %get-tuple-element.47), channel_id=1, source_target_pairs={{0,8},{4,12},{8,0},{12,4},{16,24},{20,28},{24,16},{28,20},{1,9},{5... | collective-permute-start | bytes 98312 | tf_op jit(solution)/shard_map/ppermute | solution.py:26
  29.1 5.0 %collective-permute-start.12 = (bf16[128,128]{1,0:T(8,128)(2,1)S(1)}, bf16[128,128]{1,0:T(8,128)(2,1)S(1)}, u32[]{:S(2)}, u32[]{:S(2)}) collective-permute-start(bf16[128,128]{1,0:T(8,128)(2,1)S(1)} %get-tuple-element.49), channel_id=1, source_target_pairs={{0,16},{4,20},{8,24},{12,28},{16,0},{20,4},{24,8},{28,12},{1,17},{... | collective-permute-start | bytes 98312 | tf_op jit(solution)/shard_map/ppermute | solution.py:26
  31.9 5.7 %collective-permute-start.13 = (bf16[128,128]{1,0:T(8,128)(2,1)S(1)}, bf16[128,128]{1,0:T(8,128)(2,1)S(1)}, u32[]{:S(2)}, u32[]{:S(2)}) collective-permute-start(bf16[128,128]{1,0:T(8,128)(2,1)S(1)} %get-tuple-element.48), channel_id=1, source_target_pairs={{0,24},{4,28},{8,16},{12,20},{16,8},{20,12},{24,0},{28,4},{1,25},{... | collective-permute-start | bytes 98312 | tf_op jit(solution)/shard_map/ppermute | solution.py:26
  37.7 1.3 %collective-permute-start.14 = (bf16[128,128]{1,0:T(8,128)(2,1)S(1)}, bf16[128,128]{1,0:T(8,128)(2,1)S(1)}, u32[]{:S(2)}, u32[]{:S(2)}) collective-permute-start(bf16[128,128]{1,0:T(8,128)(2,1)S(1)} %fusion.3), channel_id=1, source_target_pairs={{0,1},{1,0},{2,3},{3,2},{4,5},{5,4},{6,7},{7,6},{8,9},{9,8},{10,11... | collective-permute-start | bytes 98312 | tf_op jit(solution)/shard_map/ppermute | solution.py:26
  41.7 9.6 %copy-start = (bf16[256,4096]{1,0:T(8,128)(2,1)S(1)}, bf16[256,4096]{1,0:T(8,128)(2,1)}, u32[]{:S(2)}) copy-start(bf16[256,4096]{1,0:T(8,128)(2,1)} %w_ref.3) | copy-start | bytes 6291460
  42.5 8.8 %collective-permute-start.17 = (bf16[128,2048]{1,0:T(8,128)(2,1)S(1)}, bf16[128,2048]{1,0:T(8,128)(2,1)S(1)}, u32[]{:S(2)}, u32[]{:S(2)}) collective-permute-start(bf16[128,2048]{1,0:T(8,128)(2,1)S(1)} %get-tuple-element.41), channel_id=1, source_target_pairs={{0,1},{1,0},{2,3},{3,2},{4,5},{5,4},{6,7},{7,6},{8,9},{9,8},{10,11... | collective-permute-start | bytes 1572872 | tf_op jit(solution)/shard_map/ppermute | solution.py:26
  42.7 8.6 %collective-permute-start.18 = (bf16[128,2048]{1,0:T(8,128)(2,1)S(1)}, bf16[128,2048]{1,0:T(8,128)(2,1)S(1)}, u32[]{:S(2)}, u32[]{:S(2)}) collective-permute-start(bf16[128,2048]{1,0:T(8,128)(2,1)S(1)} %get-tuple-element.42), channel_id=1, source_target_pairs={{0,1},{1,0},{2,3},{3,2},{4,5},{5,4},{6,7},{7,6},{8,9},{9,8},{10,11... | collective-permute-start | bytes 1572872 | tf_op jit(solution)/shard_map/ppermute | solution.py:26
  43.0 8.2 %collective-permute-start.15 = (bf16[128,256]{1,0:T(8,128)(2,1)S(1)}, bf16[128,256]{1,0:T(8,128)(2,1)S(1)}, u32[]{:S(2)}, u32[]{:S(2)}) collective-permute-start(bf16[128,256]{1,0:T(8,128)(2,1)S(1)} %pad_maximum_fusion.2.refs_0_.kv_ref), channel_id=1, source_target_pairs={{0,2},{1,3},{2,0},{3,1},{4,6},{5,7},{6,4},{7,5},{8,10},{9,11},{10,... | collective-permute-start | bytes 196616 | tf_op jit(solution)/shard_map/ppermute | solution.py:26

commit v22 on v20

--- a/solution.py
+++ b/solution.py
@@ -283,16 +283,18 @@
     x_early = swapped(z_early, "ctx", 1)
     far_send = column_block(w_query, head ^ 3, share, z_early)
     far_mine = column_block(w_query, head ^ 2, share, z_early)
-    z_late, x_early, far_send, far_mine = lax.optimization_barrier((z_late, x_early, far_send, far_mine))
+    there_early = swapped(z_early, "head", 1)
+    z_late, x_early, there_early, far_send, far_mine = lax.optimization_barrier(
+        (z_late, x_early, there_early, far_send, far_mine)
+    )
     x_late = swapped(z_late, "ctx", 1)
     far_other = swapped(far_send, "head", 1)
-    here_z = jnp.concatenate([z_early, z_late])
-    there_z = swapped(here_z, "head", 1)
-    queries, dout, here_z = lax.optimization_barrier((queries, dout, here_z))
+    queries, dout, z_late = lax.optimization_barrier((queries, dout, z_late))
     q_other, g_other = swapped(queries, "head", 1), swapped(dout, "head", 1)
     x_late, q_other, g_other = lax.optimization_barrier((x_late, q_other, g_other))
-    here_x = jnp.concatenate([x_early, x_late])
-    pieces = (here_z, there_z, here_x, swapped(here_x, "head", 1))
+    pieces = [z_early, there_early]
+    for here in (z_late, x_early, x_late):
+        pieces += [here, swapped(here, "head", 1)]
     dq, back = attention(core, positions, doc_ids, queries, q_other, dout, g_other, pieces)
 
     part = product(dq, far_mine, far_other, 0, share, jnp.bfloat16)

time: 52.2 us -> 52 us (level)
    ppermute x19 -> x21, waiting for transfers between devices: 19.5 us -> 19.2 us  [swapped(): lax.ppermute(value, axis, [(source, source ^ bits) for source in range(co...]
    ppermute x19 -> x21, starting transfers between devices: 19.6 us -> 19.6 us  [swapped(): lax.ppermute(value, axis, [(source, source ^ bits) for source in range(co...]
  transfers between devices with their start and end apart: 19 -> 21, of which waited for: 10 -> 10; matrix products, arithmetic and copies ran while one was open for 5% -> 6% of each run, Pallas kernels for 11% -> 12%
where the time goes in v22:
time: 52 us; the launch traced here: 51.8 us
  starting transfers between devices  19.6 us (38%)
  waiting for transfers between devices  19.2 us (37%)
  Pallas kernels  8.13 us (16%)
  local copies, waits for them, and re-layouts  3.49 us (7%)
  other arithmetic  1.16 us (2%)
    ppermute x21, starting transfers between devices, swapped(): lax.ppermute(value, axis, [(source, source ^ bits) for source in range(co...  19.6 us
    ppermute x21, waiting for transfers between devices, swapped(): lax.ppermute(value, axis, [(source, source ^ bits) for source in range(co...  19.2 us
    pallas_call x1, Pallas kernels, carve(): pl.pallas_call(carve_kernel, out_shape=[block] * count, in_specs=[SMEM, H...  2.76 us
    dynamic_slice x1, local copies, waits for them, and re-layouts, column_block(): return lax.dynamic_slice_in_dim(w_query, block * share, share, axis=1)  2.71 us
    pallas_call x1, Pallas kernels, attention(): pl.pallas_call(attention_kernel, out_shape=[jax.ShapeDtypeStruct((rows, 2...  2.45 us
    pallas_call x1, Pallas kernels, finish(): pl.pallas_call(finish_kernel, out_shape=jax.ShapeDtypeStruct((rows, share...  1.44 us
  transfers between devices with their start and end apart: 21, of which 10 were waited for; matrix products, arithmetic and copies ran while one was open for 6% of the time, Pallas kernels for 12%

profile of v22, /device:TPU:0, one launch (start us, length us, event | category | flops | bytes accessed | tf_op | source)
XLA Modules:
  0.0 51.8 jit_solution(13778943014256117221)
XLA Ops:
  0.0 0.7 %reshape.19 = s32[2,64]{1,0:T(2,128)S(1)} reshape(s32[128]{0:T(128)} %param.12) | data formatting | bytes 1024 | tf_op jit(solution)/shard_map/reshape | solution.py:44
  0.9 0.8 %broadcast_select_fusion = bf16[128,128]{1,0:T(8,128)(2,1)S(1)} fusion(bf16[128,128]{1,0:T(8,128)(2,1)} %param.9, bf16[128,128]{1,0:T(8,128)(2,1)} %param.10, pred[]{:T(512)} %bitcast.3), kind=kLoop, calls=%fused_computation.13 | loop fusion | flops 16384 | bytes 98305 | tf_op jit(solution)/shard_map/jit(_where)/select_n | solution.py:43
  1.7 3.1 %collective-permute-start.2 = (bf16[144,128]{1,0:T(8,128)(2,1)S(1)}, bf16[144,128]{1,0:T(8,128)(2,1)S(1)}, u32[]{:S(2)}, u32[]{:S(2)}) collective-permute-start(bf16[144,128]{1,0:T(8,128)(2,1)S(1)} %get-tuple-element.53), channel_id=1, source_target_pairs={{0,8},{4,12},{8,0},{12,4},{16,24},{20,28},{24,16},{28,20},{1,9},{5... | collective-permute-start | bytes 110600 | tf_op jit(solution)/shard_map/ppermute | solution.py:26
  4.8 2.6 %collective-permute-start = (bf16[144,128]{1,0:T(8,128)(2,1)S(1)}, bf16[144,128]{1,0:T(8,128)(2,1)S(1)}, u32[]{:S(2)}, u32[]{:S(2)}) collective-permute-start(bf16[144,128]{1,0:T(8,128)(2,1)S(1)} %get-tuple-element.53), channel_id=1, source_target_pairs={{0,16},{4,20},{8,24},{12,28},{16,0},{20,4},{24,8},{28,12},{1,17},{... | collective-permute-start | bytes 110600 | tf_op jit(solution)/shard_map/ppermute | solution.py:26
  7.5 1.8 %collective-permute-start.3 = (bf16[2,144,128]{2,1,0:T(8,128)(2,1)S(1)}, bf16[2,144,128]{2,1,0:T(8,128)(2,1)S(1)}, u32[]{:S(2)}, u32[]{:S(2)}) collective-permute-start(bf16[2,144,128]{2,1,0:T(8,128)(2,1)S(1)} %pad_maximum_fusion.1.refs_0_), channel_id=1, source_target_pairs={{0,4},{4,0},{8,12},{12,8},{16,20},{20,16},{24,28},{28,24},{1,5},{5... | collective-permute-start | bytes 221192 | tf_op jit(solution)/shard_map/ppermute | solution.py:26
  9.3 2.7 %constant_dynamic-slice_fusion = (bf16[256,4096]{1,0:T(8,128)(2,1)S(1)}, bf16[256,4096]{1,0:T(8,128)(2,1)S(1)}) fusion(bf16[256,16384]{1,0:T(8,128)(2,1)} %w_ref.2, s32[]{:T(128)S(6)} %select_n.18, s32[]{:T(128)S(6)} %select_n.17), kind=kLoop, calls=%fused_computation.21 | loop fusion | bytes 8388616 | tf_op jit(solution)/shard_map/dynamic_slice | solution.py:51
  12.0 1.2 %collective-permute-done.1 = bf16[144,128]{1,0:T(8,128)(2,1)S(1)} collective-permute-done((bf16[144,128]{1,0:T(8,128)(2,1)S(1)}, bf16[144,128]{1,0:T(8,128)(2,1)S(1)}, u32[]{:S(2)}, u32[]{:S(2)}) %collective-permute-start.1) | collective-permute-done | bytes 36896 | tf_op jit(solution)/shard_map/ppermute | solution.py:26
  13.3 1.6 %collective-permute-start.5 = (bf16[2,144,128]{2,1,0:T(8,128)(2,1)S(1)}, bf16[2,144,128]{2,1,0:T(8,128)(2,1)S(1)}, u32[]{:S(2)}, u32[]{:S(2)}) collective-permute-start(bf16[2,144,128]{2,1,0:T(8,128)(2,1)S(1)} %pad_maximum_fusion.refs_2_), channel_id=1, source_target_pairs={{0,4},{4,0},{8,12},{12,8},{16,20},{20,16},{24,28},{28,24},{1,5},{5... | collective-permute-start | bytes 221192 | tf_op jit(solution)/shard_map/ppermute | solution.py:26
  14.8 0.2 collective-permute-start.6
  15.0 0.3 collective-permute-start.7
  15.5 2.0 %collective-permute-done.6.qo_ref = bf16[128,256]{1,0:T(8,128)(2,1)S(1)} collective-permute-done((bf16[128,256]{1,0:T(8,128)(2,1)S(1)}, bf16[128,256]{1,0:T(8,128)(2,1)S(1)}, u32[]{:S(2)}, u32[]{:S(2)}) %collective-permute-start.6) | collective-permute-done | bytes 65568 | tf_op jit(solution)/shard_map/ppermute | solution.py:26
  17.7 0.3 collective-permute-done.5.refs_6_
  18.1 0.7 %collective-permute-done.9.refs_5_ = bf16[2,144,128]{2,1,0:T(8,128)(2,1)S(1)} collective-permute-done((bf16[2,144,128]{2,1,0:T(8,128)(2,1)S(1)}, bf16[2,144,128]{2,1,0:T(8,128)(2,1)S(1)}, u32[]{:S(2)}, u32[]{:S(2)}) %collective-permute-start.9) | collective-permute-done | bytes 73760 | tf_op jit(solution)/shard_map/ppermute | solution.py:26
  18.8 0.4 collective-permute-done.10.refs_7_
  19.2 2.4 %attention.1 = (bf16[128,512]{1,0:T(8,128)(2,1)S(1)}, bf16[8,128,128]{2,1,0:T(8,128)(2,1)S(1)}) custom-call(s32[1]{0:T(128)} %bitcast.core_ref, s32[1,128]{1,0:T(1,128)S(1)} %bitcast.27, s32[1,128]{1,0:T(1,128)S(1)} %bitcast.28, bf16[128,256]{1,0:T(8,128)(2,1)S(1)} %copy-done.1, bf16[128,256]{1,0:T(8,128)(2,1)S(1)} %collective-permute-done.6.qo_ref, ...), custom_call_target="tpu_custom_call" | custom-call | flops 671088640 | bytes 1048576 | tf_op jit(solution)/shard_map/attention/pallas_call | solution.py:162
  21.7 0.7 %product.1 = bf16[128,4096]{1,0:T(8,128)(2,1)S(1)} custom-call(bf16[128,512]{1,0:T(8,128)(2,1)S(1)} %get-tuple-element.36.dq_ref, bf16[256,4096]{1,0:T(8,128)(2,1)S(1)} %get-tuple-element.37.wm_ref, bf16[256,4096]{1,0:T(8,128)(2,1)S(1)} %collective-permute-done.11.wo_ref), custom_call_target="tpu_custom_call" | custom-call | flops 536870912 | bytes 4194304 | tf_op jit(solution)/shard_map/product/pallas_call | solution.py:193
  22.5 1.5 %collective-permute-start.12 = (bf16[4,128,128]{2,1,0:T(8,128)(2,1)S(1)}, bf16[4,128,128]{2,1,0:T(8,128)(2,1)S(1)}, u32[]{:S(2)}, u32[]{:S(2)}) collective-permute-start(bf16[4,128,128]{2,1,0:T(8,128)(2,1)S(1)} %slice.26), channel_id=1, source_target_pairs={{0,4},{4,0},{8,12},{12,8},{16,20},{20,16},{24,28},{28,24},{1,5},{5... | collective-permute-start | bytes 393224 | tf_op jit(solution)/shard_map/ppermute | solution.py:26
  24.0 1.5 %collective-permute-start.18 = (bf16[128,4096]{1,0:T(8,128)(2,1)S(1)}, bf16[128,4096]{1,0:T(8,128)(2,1)S(1)}, u32[]{:S(2)}, u32[]{:S(2)}) collective-permute-start(bf16[128,4096]{1,0:T(8,128)(2,1)S(1)} %product.1), channel_id=1, source_target_pairs={{0,2},{1,3},{2,0},{3,1},{4,6},{5,7},{6,4},{7,5},{8,10},{9,11},{10,... | collective-permute-start | bytes 3145736 | tf_op jit(solution)/shard_map/ppermute | solution.py:26
  25.5 2.6 %collective-permute-done.12 = bf16[4,128,128]{2,1,0:T(8,128)(2,1)S(1)} collective-permute-done((bf16[4,128,128]{2,1,0:T(8,128)(2,1)S(1)}, bf16[4,128,128]{2,1,0:T(8,128)(2,1)S(1)}, u32[]{:S(2)}, u32[]{:S(2)}) %collective-permute-start.12) | collective-permute-done | bytes 131104 | tf_op jit(solution)/shard_map/ppermute | solution.py:26
  28.2 0.2 collective-permute-start.13
  28.3 3.0 %collective-permute-start.14 = (bf16[128,128]{1,0:T(8,128)(2,1)S(1)}, bf16[128,128]{1,0:T(8,128)(2,1)S(1)}, u32[]{:S(2)}, u32[]{:S(2)}) collective-permute-start(bf16[128,128]{1,0:T(8,128)(2,1)S(1)} %get-tuple-element.51), channel_id=1, source_target_pairs={{0,16},{4,20},{8,24},{12,28},{16,0},{20,4},{24,8},{28,12},{1,17},{... | collective-permute-start | bytes 98312 | tf_op jit(solution)/shard_map/ppermute | solution.py:26
  31.4 1.2 %collective-permute-start.15 = (bf16[128,128]{1,0:T(8,128)(2,1)S(1)}, bf16[128,128]{1,0:T(8,128)(2,1)S(1)}, u32[]{:S(2)}, u32[]{:S(2)}) collective-permute-start(bf16[128,128]{1,0:T(8,128)(2,1)S(1)} %get-tuple-element.50), channel_id=1, source_target_pairs={{0,24},{4,28},{8,16},{12,20},{16,8},{20,12},{24,0},{28,4},{1,25},{... | collective-permute-start | bytes 98312 | tf_op jit(solution)/shard_map/ppermute | solution.py:26
  32.6 0.7 %collective-permute-done.14 = bf16[128,128]{1,0:T(8,128)(2,1)S(1)} collective-permute-done((bf16[128,128]{1,0:T(8,128)(2,1)S(1)}, bf16[128,128]{1,0:T(8,128)(2,1)S(1)}, u32[]{:S(2)}, u32[]{:S(2)}) %collective-permute-start.14) | collective-permute-done | bytes 32800 | tf_op jit(solution)/shard_map/ppermute | solution.py:26
  33.4 3.7 %collective-permute-done.15 = bf16[128,128]{1,0:T(8,128)(2,1)S(1)} collective-permute-done((bf16[128,128]{1,0:T(8,128)(2,1)S(1)}, bf16[128,128]{1,0:T(8,128)(2,1)S(1)}, u32[]{:S(2)}, u32[]{:S(2)}) %collective-permute-start.15) | collective-permute-done | bytes 32800 | tf_op jit(solution)/shard_map/ppermute | solution.py:26
  37.3 1.1 %collective-permute-done.16 = bf16[128,128]{1,0:T(8,128)(2,1)S(1)} collective-permute-done((bf16[128,128]{1,0:T(8,128)(2,1)S(1)}, bf16[128,128]{1,0:T(8,128)(2,1)S(1)}, u32[]{:S(2)}, u32[]{:S(2)}) %collective-permute-start.16) | collective-permute-done | bytes 32800 | tf_op jit(solution)/shard_map/ppermute | solution.py:26
  38.4 2.8 %carve.1 = (bf16[256,4096]{1,0:T(8,128)(2,1)S(1)}, bf16[256,4096]{1,0:T(8,128)(2,1)S(1)}) custom-call(s32[2]{0:T(128)S(1)} %pad_add_fusion.block_ref, bf16[256,16384]{1,0:T(8,128)(2,1)} %w_ref.2, bf16[128,256]{1,0:T(8,128)(2,1)S(1)} %pad_maximum_fusion.2.refs_0_.kv_ref), custom_call_target="tpu_custom_call" | custom-call | tf_op jit(solution)/shard_map/carve/pallas_call | solution.py:73
  41.2 0.8 %own.1 = (f32[128,4096]{1,0:T(8,128)S(1)}, bf16[128,2048]{1,0:T(8,128)(2,1)S(1)}, bf16[128,2048]{1,0:T(8,128)(2,1)S(1)}) custom-call(bf16[128,512]{1,0:T(8,128)(2,1)S(1)} %get-tuple-element.36.dq_ref, bf16[256,4096]{1,0:T(8,128)(2,1)S(1)} %get-tuple-element.40.wn_ref, bf16[256,4096]{1,0:T(8,128)(2,1)S(1)} %get-tuple-element.41.wo_ref), custom_call_target="tpu_custom_call" | custom-call | tf_op jit(solution)/shard_map/own/pallas_call | solution.py:218
  41.9 0.2 collective-permute-start.19
  42.2 0.4 collective-permute-start.20
  42.5 1.5 %collective-permute-start.17 = (bf16[128,256]{1,0:T(8,128)(2,1)S(1)}, bf16[128,256]{1,0:T(8,128)(2,1)S(1)}, u32[]{:S(2)}, u32[]{:S(2)}) collective-permute-start(bf16[128,256]{1,0:T(8,128)(2,1)S(1)} %pad_maximum_fusion.2.refs_0_.kv_ref), channel_id=1, source_target_pairs={{0,2},{1,3},{2,0},{3,1},{4,6},{5,7},{6,4},{7,5},{8,10},{9,11},{10,... | collective-permute-start | bytes 196616 | tf_op jit(solution)/shard_map/ppermute | solution.py:26
  44.0 6.3 %collective-permute-done.17.kv_far_ref = bf16[128,256]{1,0:T(8,128)(2,1)S(1)} collective-permute-done((bf16[128,256]{1,0:T(8,128)(2,1)S(1)}, bf16[128,256]{1,0:T(8,128)(2,1)S(1)}, u32[]{:S(2)}, u32[]{:S(2)}) %collective-permute-start.17) | collective-permute-done | bytes 65568 | tf_op jit(solution)/shard_map/ppermute | solution.py:26
  50.4 1.4 %finish.1 = bf16[128,4096]{1,0:T(8,128)(2,1)} custom-call(s32[1]{0:T(128)} %bitcast.core_ref, bf16[128,256]{1,0:T(8,128)(2,1)S(1)} %pad_maximum_fusion.2.refs_0_.kv_ref, bf16[128,256]{1,0:T(8,128)(2,1)S(1)} %collective-permute-done.17.kv_far_ref, bf16[256,4096]{1,0:T(8,128)(2,1)S(1)} %copy-done, f32[128,4096]{1,0:T(8,128)S(1)} %get-tuple-element.42.acc_ref, ...), custom_call_target="tpu_custom_call" | custom-call | flops 268435456 | bytes 5242880 | tf_op jit(solution)/shard_map/finish/pallas_call | solution.py:258
  (39 shorter events, 1.0 us)
Async XLA Ops:
  1.7 5.7 %collective-permute-start.2 = (bf16[144,128]{1,0:T(8,128)(2,1)S(1)}, bf16[144,128]{1,0:T(8,128)(2,1)S(1)}, u32[]{:S(2)}, u32[]{:S(2)}) collective-permute-start(bf16[144,128]{1,0:T(8,128)(2,1)S(1)} %get-tuple-element.53), channel_id=1, source_target_pairs={{0,8},{4,12},{8,0},{12,4},{16,24},{20,28},{24,16},{28,20},{1,9},{5... | collective-permute-start | bytes 110600 | tf_op jit(solution)/shard_map/ppermute | solution.py:26
  4.8 7.2 %collective-permute-start = (bf16[144,128]{1,0:T(8,128)(2,1)S(1)}, bf16[144,128]{1,0:T(8,128)(2,1)S(1)}, u32[]{:S(2)}, u32[]{:S(2)}) collective-permute-start(bf16[144,128]{1,0:T(8,128)(2,1)S(1)} %get-tuple-element.53), channel_id=1, source_target_pairs={{0,16},{4,20},{8,24},{12,28},{16,0},{20,4},{24,8},{28,12},{1,17},{... | collective-permute-start | bytes 110600 | tf_op jit(solution)/shard_map/ppermute | solution.py:26
  7.4 5.8 %collective-permute-start.1 = (bf16[144,128]{1,0:T(8,128)(2,1)S(1)}, bf16[144,128]{1,0:T(8,128)(2,1)S(1)}, u32[]{:S(2)}, u32[]{:S(2)}) collective-permute-start(bf16[144,128]{1,0:T(8,128)(2,1)S(1)} %get-tuple-element.53), channel_id=1, source_target_pairs={{0,24},{4,28},{8,16},{12,20},{16,8},{20,12},{24,0},{28,4},{1,25},{... | collective-permute-start | bytes 110600 | tf_op jit(solution)/shard_map/ppermute | solution.py:26
  7.4 7.4 %copy-start.1 = (bf16[128,256]{1,0:T(8,128)(2,1)S(1)}, bf16[128,256]{1,0:T(8,128)(2,1)}, u32[]{:S(2)}) copy-start(bf16[128,256]{1,0:T(8,128)(2,1)} %qm_ref) | copy-start | bytes 196612
  7.5 7.6 %copy-start.2 = (bf16[128,256]{1,0:T(8,128)(2,1)S(1)}, bf16[128,256]{1,0:T(8,128)(2,1)}, u32[]{:S(2)}) copy-start(bf16[128,256]{1,0:T(8,128)(2,1)} %gm_ref) | copy-start | bytes 196612
  7.5 11.8 %copy-start.3 = (s32[128]{0:T(128)S(1)}, s32[128]{0:T(128)}, u32[]{:S(2)}) copy-start(s32[128]{0:T(128)} %param.12) | copy-start | bytes 1540
  7.5 11.8 %copy-start.4 = (s32[128]{0:T(128)S(1)}, s32[128]{0:T(128)}, u32[]{:S(2)}) copy-start(s32[128]{0:T(128)} %param.13) | copy-start | bytes 1540
  7.5 5.7 %collective-permute-start.3 = (bf16[2,144,128]{2,1,0:T(8,128)(2,1)S(1)}, bf16[2,144,128]{2,1,0:T(8,128)(2,1)S(1)}, u32[]{:S(2)}, u32[]{:S(2)}) collective-permute-start(bf16[2,144,128]{2,1,0:T(8,128)(2,1)S(1)} %pad_maximum_fusion.1.refs_0_), channel_id=1, source_target_pairs={{0,4},{4,0},{8,12},{12,8},{16,20},{20,16},{24,28},{28,24},{1,5},{5... | collective-permute-start | bytes 221192 | tf_op jit(solution)/shard_map/ppermute | solution.py:26
  9.3 3.9 %collective-permute-start.4 = (bf16[2,144,128]{2,1,0:T(8,128)(2,1)S(1)}, bf16[2,144,128]{2,1,0:T(8,128)(2,1)S(1)}, u32[]{:S(2)}, u32[]{:S(2)}) collective-permute-start(bf16[2,144,128]{2,1,0:T(8,128)(2,1)S(1)} %pad_maximum_fusion.1.refs_0_), channel_id=1, source_target_pairs={{0,1},{1,0},{2,3},{3,2},{4,5},{5,4},{6,7},{7,6},{8,9},{9,8},{10,11... | collective-permute-start | bytes 221192 | tf_op jit(solution)/shard_map/ppermute | solution.py:26
  13.2 8.5 %collective-permute-start.11 = (bf16[256,4096]{1,0:T(8,128)(2,1)S(1)}, bf16[256,4096]{1,0:T(8,128)(2,1)S(1)}, u32[]{:S(2)}, u32[]{:S(2)}) collective-permute-start(bf16[256,4096]{1,0:T(8,128)(2,1)S(1)} %get-tuple-element.38), channel_id=1, source_target_pairs={{0,1},{1,0},{2,3},{3,2},{4,5},{5,4},{6,7},{7,6},{8,9},{9,8},{10,11... | collective-permute-start | bytes 6291464 | tf_op jit(solution)/shard_map/ppermute | solution.py:26
  13.3 4.7 %collective-permute-start.5 = (bf16[2,144,128]{2,1,0:T(8,128)(2,1)S(1)}, bf16[2,144,128]{2,1,0:T(8,128)(2,1)S(1)}, u32[]{:S(2)}, u32[]{:S(2)}) collective-permute-start(bf16[2,144,128]{2,1,0:T(8,128)(2,1)S(1)} %pad_maximum_fusion.refs_2_), channel_id=1, source_target_pairs={{0,4},{4,0},{8,12},{12,8},{16,20},{20,16},{24,28},{28,24},{1,5},{5... | collective-permute-start | bytes 221192 | tf_op jit(solution)/shard_map/ppermute | solution.py:26
  14.8 2.7 %collective-permute-start.6 = (bf16[128,256]{1,0:T(8,128)(2,1)S(1)}, bf16[128,256]{1,0:T(8,128)(2,1)S(1)}, u32[]{:S(2)}, u32[]{:S(2)}) collective-permute-start(bf16[128,256]{1,0:T(8,128)(2,1)S(1)} %copy-done.1), channel_id=1, source_target_pairs={{0,1},{1,0},{2,3},{3,2},{4,5},{5,4},{6,7},{7,6},{8,9},{9,8},{10,11... | collective-permute-start | bytes 196616 | tf_op jit(solution)/shard_map/ppermute | solution.py:26
  15.0 2.7 %collective-permute-start.7 = (bf16[128,256]{1,0:T(8,128)(2,1)S(1)}, bf16[128,256]{1,0:T(8,128)(2,1)S(1)}, u32[]{:S(2)}, u32[]{:S(2)}) collective-permute-start(bf16[128,256]{1,0:T(8,128)(2,1)S(1)} %copy-done.2), channel_id=1, source_target_pairs={{0,1},{1,0},{2,3},{3,2},{4,5},{5,4},{6,7},{7,6},{8,9},{9,8},{10,11... | collective-permute-start | bytes 196616 | tf_op jit(solution)/shard_map/ppermute | solution.py:26
  15.4 2.7 %collective-permute-start.8 = (bf16[2,144,128]{2,1,0:T(8,128)(2,1)S(1)}, bf16[2,144,128]{2,1,0:T(8,128)(2,1)S(1)}, u32[]{:S(2)}, u32[]{:S(2)}) collective-permute-start(bf16[2,144,128]{2,1,0:T(8,128)(2,1)S(1)} %pad_maximum_fusion.refs_2_), channel_id=1, source_target_pairs={{0,1},{1,0},{2,3},{3,2},{4,5},{5,4},{6,7},{7,6},{8,9},{9,8},{10,11... | collective-permute-start | bytes 221192 | tf_op jit(solution)/shard_map/ppermute | solution.py:26
  17.5 1.3 %collective-permute-start.9 = (bf16[2,144,128]{2,1,0:T(8,128)(2,1)S(1)}, bf16[2,144,128]{2,1,0:T(8,128)(2,1)S(1)}, u32[]{:S(2)}, u32[]{:S(2)}) collective-permute-start(bf16[2,144,128]{2,1,0:T(8,128)(2,1)S(1)} %collective-permute-done.3.refs_4_), channel_id=1, source_target_pairs={{0,1},{1,0},{2,3},{3,2},{4,5},{5,4},{6,7},{7,6},{8,9},{9,8},{10,11... | collective-permute-start | bytes 221192 | tf_op jit(solution)/shard_map/ppermute | solution.py:26
  18.0 1.3 %collective-permute-start.10 = (bf16[2,144,128]{2,1,0:T(8,128)(2,1)S(1)}, bf16[2,144,128]{2,1,0:T(8,128)(2,1)S(1)}, u32[]{:S(2)}, u32[]{:S(2)}) collective-permute-start(bf16[2,144,128]{2,1,0:T(8,128)(2,1)S(1)} %collective-permute-done.5.refs_6_), channel_id=1, source_target_pairs={{0,1},{1,0},{2,3},{3,2},{4,5},{5,4},{6,7},{7,6},{8,9},{9,8},{10,11... | collective-permute-start | bytes 221192 | tf_op jit(solution)/shard_map/ppermute | solution.py:26
  22.5 5.6 %collective-permute-start.12 = (bf16[4,128,128]{2,1,0:T(8,128)(2,1)S(1)}, bf16[4,128,128]{2,1,0:T(8,128)(2,1)S(1)}, u32[]{:S(2)}, u32[]{:S(2)}) collective-permute-start(bf16[4,128,128]{2,1,0:T(8,128)(2,1)S(1)} %slice.26), channel_id=1, source_target_pairs={{0,4},{4,0},{8,12},{12,8},{16,20},{20,16},{24,28},{28,24},{1,5},{5... | collective-permute-start | bytes 393224 | tf_op jit(solution)/shard_map/ppermute | solution.py:26
  24.0 26.4 %collective-permute-start.18 = (bf16[128,4096]{1,0:T(8,128)(2,1)S(1)}, bf16[128,4096]{1,0:T(8,128)(2,1)S(1)}, u32[]{:S(2)}, u32[]{:S(2)}) collective-permute-start(bf16[128,4096]{1,0:T(8,128)(2,1)S(1)} %product.1), channel_id=1, source_target_pairs={{0,2},{1,3},{2,0},{3,1},{4,6},{5,7},{6,4},{7,5},{8,10},{9,11},{10,... | collective-permute-start | bytes 3145736 | tf_op jit(solution)/shard_map/ppermute | solution.py:26
  28.2 4.5 %collective-permute-start.13 = (bf16[128,128]{1,0:T(8,128)(2,1)S(1)}, bf16[128,128]{1,0:T(8,128)(2,1)S(1)}, u32[]{:S(2)}, u32[]{:S(2)}) collective-permute-start(bf16[128,128]{1,0:T(8,128)(2,1)S(1)} %get-tuple-element.49), channel_id=1, source_target_pairs={{0,8},{4,12},{8,0},{12,4},{16,24},{20,28},{24,16},{28,20},{1,9},{5... | collective-permute-start | bytes 98312 | tf_op jit(solution)/shard_map/ppermute | solution.py:26
  28.3 5.0 %collective-permute-start.14 = (bf16[128,128]{1,0:T(8,128)(2,1)S(1)}, bf16[128,128]{1,0:T(8,128)(2,1)S(1)}, u32[]{:S(2)}, u32[]{:S(2)}) collective-permute-start(bf16[128,128]{1,0:T(8,128)(2,1)S(1)} %get-tuple-element.51), channel_id=1, source_target_pairs={{0,16},{4,20},{8,24},{12,28},{16,0},{20,4},{24,8},{28,12},{1,17},{... | collective-permute-start | bytes 98312 | tf_op jit(solution)/shard_map/ppermute | solution.py:26
  31.4 5.7 %collective-permute-start.15 = (bf16[128,128]{1,0:T(8,128)(2,1)S(1)}, bf16[128,128]{1,0:T(8,128)(2,1)S(1)}, u32[]{:S(2)}, u32[]{:S(2)}) collective-permute-start(bf16[128,128]{1,0:T(8,128)(2,1)S(1)} %get-tuple-element.50), channel_id=1, source_target_pairs={{0,24},{4,28},{8,16},{12,20},{16,8},{20,12},{24,0},{28,4},{1,25},{... | collective-permute-start | bytes 98312 | tf_op jit(solution)/shard_map/ppermute | solution.py:26
  37.1 1.3 %collective-permute-start.16 = (bf16[128,128]{1,0:T(8,128)(2,1)S(1)}, bf16[128,128]{1,0:T(8,128)(2,1)S(1)}, u32[]{:S(2)}, u32[]{:S(2)}) collective-permute-start(bf16[128,128]{1,0:T(8,128)(2,1)S(1)} %fusion.3), channel_id=1, source_target_pairs={{0,1},{1,0},{2,3},{3,2},{4,5},{5,4},{6,7},{7,6},{8,9},{9,8},{10,11... | collective-permute-start | bytes 98312 | tf_op jit(solution)/shard_map/ppermute | solution.py:26
  41.2 9.2 %copy-start = (bf16[256,4096]{1,0:T(8,128)(2,1)S(1)}, bf16[256,4096]{1,0:T(8,128)(2,1)}, u32[]{:S(2)}) copy-start(bf16[256,4096]{1,0:T(8,128)(2,1)} %w_ref.3) | copy-start | bytes 6291460
  41.9 8.4 %collective-permute-start.19 = (bf16[128,2048]{1,0:T(8,128)(2,1)S(1)}, bf16[128,2048]{1,0:T(8,128)(2,1)S(1)}, u32[]{:S(2)}, u32[]{:S(2)}) collective-permute-start(bf16[128,2048]{1,0:T(8,128)(2,1)S(1)} %get-tuple-element.43), channel_id=1, source_target_pairs={{0,1},{1,0},{2,3},{3,2},{4,5},{5,4},{6,7},{7,6},{8,9},{9,8},{10,11... | collective-permute-start | bytes 1572872 | tf_op jit(solution)/shard_map/ppermute | solution.py:26
  42.2 8.2 %collective-permute-start.20 = (bf16[128,2048]{1,0:T(8,128)(2,1)S(1)}, bf16[128,2048]{1,0:T(8,128)(2,1)S(1)}, u32[]{:S(2)}, u32[]{:S(2)}) collective-permute-start(bf16[128,2048]{1,0:T(8,128)(2,1)S(1)} %get-tuple-element.44), channel_id=1, source_target_pairs={{0,1},{1,0},{2,3},{3,2},{4,5},{5,4},{6,7},{7,6},{8,9},{9,8},{10,11... | collective-permute-start | bytes 1572872 | tf_op jit(solution)/shard_map/ppermute | solution.py:26
  42.5 7.8 %collective-permute-start.17 = (bf16[128,256]{1,0:T(8,128)(2,1)S(1)}, bf16[128,256]{1,0:T(8,128)(2,1)S(1)}, u32[]{:S(2)}, u32[]{:S(2)}) collective-permute-start(bf16[128,256]{1,0:T(8,128)(2,1)S(1)} %pad_maximum_fusion.2.refs_0_.kv_ref), channel_id=1, source_target_pairs={{0,2},{1,3},{2,0},{3,1},{4,6},{5,7},{6,4},{7,5},{8,10},{9,11},{10,... | collective-permute-start | bytes 196616 | tf_op jit(solution)/shard_map/ppermute | solution.py:26

commit v23 on v22

--- a/solution.py
+++ b/solution.py
@@ -277,7 +277,8 @@
     local_heads = queries.shape[1] // keys.shape[1]
 
     piece = pack(core, positions, keys, values)
-    along_z = [piece] + [swapped(piece, "ctx", 2 * s) for s in range(1, half)]
+    ways = [1] + list(range(half - 1, 1, -1))
+    along_z = [piece] + [swapped(piece, "ctx", 2 * way) for way in ways]
     early = (half + 1) // 2
     z_early, z_late = jnp.stack(along_z[:early]), jnp.stack(along_z[early:])
     x_early = swapped(z_early, "ctx", 1)
@@ -303,8 +304,8 @@
     back, part = lax.optimization_barrier((back, part))
     pair = back[:half].astype(jnp.float32) + swapped(back[half:], "ctx", 1).astype(jnp.float32)
     mine = pair[0]
-    for s in range(1, half):
-        mine = mine + swapped(pair[s].astype(jnp.bfloat16), "ctx", 2 * s).astype(jnp.float32)
+    for s, way in enumerate(ways, 1):
+        mine = mine + swapped(pair[s].astype(jnp.bfloat16), "ctx", 2 * way).astype(jnp.float32)
     mine = mine.astype(jnp.bfloat16)
     kv = jnp.concatenate([mine, swapped(mine, "head", 1)], axis=1)
     kv_far = swapped(kv, "head", 2)

time: 52 us -> 51.4 us (0.988)
  starting transfers between devices: 19.6 us -> 18.7 us
    ppermute x21, starting transfers between devices: 19.6 us -> 18.7 us  [swapped(): lax.ppermute(value, axis, [(source, source ^ bits) for source in range(co...]
  transfers between devices with their start and end apart: 21 -> 21, of which waited for: 10 -> 11; matrix products, arithmetic and copies ran while one was open for 6% -> 6% of each run, Pallas kernels for 12% -> 12%
where the time goes in v23:
time: 51.4 us; the launch traced here: 51.2 us
  waiting for transfers between devices  19.5 us (38%)
  starting transfers between devices  18.7 us (36%)
  Pallas kernels  8.13 us (16%)
  local copies, waits for them, and re-layouts  3.49 us (7%)
  other arithmetic  1.16 us (2%)
    ppermute x21, waiting for transfers between devices, swapped(): lax.ppermute(value, axis, [(source, source ^ bits) for source in range(co...  19.5 us
    ppermute x21, starting transfers between devices, swapped(): lax.ppermute(value, axis, [(source, source ^ bits) for source in range(co...  18.7 us
    pallas_call x1, Pallas kernels, carve(): pl.pallas_call(carve_kernel, out_shape=[block] * count, in_specs=[SMEM, H...  2.76 us
    dynamic_slice x1, local copies, waits for them, and re-layouts, column_block(): return lax.dynamic_slice_in_dim(w_query, block * share, share, axis=1)  2.71 us
    pallas_call x1, Pallas kernels, attention(): pl.pallas_call(attention_kernel, out_shape=[jax.ShapeDtypeStruct((rows, 2...  2.45 us
    pallas_call x1, Pallas kernels, finish(): pl.pallas_call(finish_kernel, out_shape=jax.ShapeDtypeStruct((rows, share...  1.43 us
  transfers between devices with their start and end apart: 21, of which 11 were waited for; matrix products, arithmetic and copies ran while one was open for 6% of the time, Pallas kernels for 12%

profile of v23, /device:TPU:0, one launch (start us, length us, event | category | flops | bytes accessed | tf_op | source)
XLA Modules:
  0.0 51.2 jit_solution(13968859426804728302)
XLA Ops:
  0.0 0.7 %reshape.19 = s32[2,64]{1,0:T(2,128)S(1)} reshape(s32[128]{0:T(128)} %param.12) | data formatting | bytes 1024 | tf_op jit(solution)/shard_map/reshape | solution.py:44
  0.9 0.8 %broadcast_select_fusion = bf16[128,128]{1,0:T(8,128)(2,1)S(1)} fusion(bf16[128,128]{1,0:T(8,128)(2,1)} %param.9, bf16[128,128]{1,0:T(8,128)(2,1)} %param.10, pred[]{:T(512)} %bitcast.3), kind=kLoop, calls=%fused_computation.13 | loop fusion | flops 16384 | bytes 98305 | tf_op jit(solution)/shard_map/jit(_where)/select_n | solution.py:43
  1.7 3.1 %collective-permute-start.2 = (bf16[144,128]{1,0:T(8,128)(2,1)S(1)}, bf16[144,128]{1,0:T(8,128)(2,1)S(1)}, u32[]{:S(2)}, u32[]{:S(2)}) collective-permute-start(bf16[144,128]{1,0:T(8,128)(2,1)S(1)} %get-tuple-element.53), channel_id=1, source_target_pairs={{0,8},{4,12},{8,0},{12,4},{16,24},{20,28},{24,16},{28,20},{1,9},{5... | collective-permute-start | bytes 110600 | tf_op jit(solution)/shard_map/ppermute | solution.py:26
  4.8 2.5 %collective-permute-start = (bf16[144,128]{1,0:T(8,128)(2,1)S(1)}, bf16[144,128]{1,0:T(8,128)(2,1)S(1)}, u32[]{:S(2)}, u32[]{:S(2)}) collective-permute-start(bf16[144,128]{1,0:T(8,128)(2,1)S(1)} %get-tuple-element.53), channel_id=1, source_target_pairs={{0,24},{4,28},{8,16},{12,20},{16,8},{20,12},{24,0},{28,4},{1,25},{... | collective-permute-start | bytes 110600 | tf_op jit(solution)/shard_map/ppermute | solution.py:26
  7.5 1.6 %collective-permute-start.3 = (bf16[2,144,128]{2,1,0:T(8,128)(2,1)S(1)}, bf16[2,144,128]{2,1,0:T(8,128)(2,1)S(1)}, u32[]{:S(2)}, u32[]{:S(2)}) collective-permute-start(bf16[2,144,128]{2,1,0:T(8,128)(2,1)S(1)} %pad_maximum_fusion.1.refs_0_), channel_id=1, source_target_pairs={{0,4},{4,0},{8,12},{12,8},{16,20},{20,16},{24,28},{28,24},{1,5},{5... | collective-permute-start | bytes 221192 | tf_op jit(solution)/shard_map/ppermute | solution.py:26
  9.0 2.7 %constant_dynamic-slice_fusion = (bf16[256,4096]{1,0:T(8,128)(2,1)S(1)}, bf16[256,4096]{1,0:T(8,128)(2,1)S(1)}) fusion(bf16[256,16384]{1,0:T(8,128)(2,1)} %w_ref.2, s32[]{:T(128)S(6)} %select_n.18, s32[]{:T(128)S(6)} %select_n.17), kind=kLoop, calls=%fused_computation.21 | loop fusion | bytes 8388616 | tf_op jit(solution)/shard_map/dynamic_slice | solution.py:51
  11.8 0.8 %collective-permute-done.1 = bf16[144,128]{1,0:T(8,128)(2,1)S(1)} collective-permute-done((bf16[144,128]{1,0:T(8,128)(2,1)S(1)}, bf16[144,128]{1,0:T(8,128)(2,1)S(1)}, u32[]{:S(2)}, u32[]{:S(2)}) %collective-permute-start.1) | collective-permute-done | bytes 36896 | tf_op jit(solution)/shard_map/ppermute | solution.py:26
  12.7 1.6 %collective-permute-start.5 = (bf16[2,144,128]{2,1,0:T(8,128)(2,1)S(1)}, bf16[2,144,128]{2,1,0:T(8,128)(2,1)S(1)}, u32[]{:S(2)}, u32[]{:S(2)}) collective-permute-start(bf16[2,144,128]{2,1,0:T(8,128)(2,1)S(1)} %pad_maximum_fusion.refs_2_), channel_id=1, source_target_pairs={{0,4},{4,0},{8,12},{12,8},{16,20},{20,16},{24,28},{28,24},{1,5},{5... | collective-permute-start | bytes 221192 | tf_op jit(solution)/shard_map/ppermute | solution.py:26
  14.2 0.2 collective-permute-start.6
  14.4 0.3 collective-permute-start.7
  14.9 2.0 %collective-permute-done.6.qo_ref = bf16[128,256]{1,0:T(8,128)(2,1)S(1)} collective-permute-done((bf16[128,256]{1,0:T(8,128)(2,1)S(1)}, bf16[128,256]{1,0:T(8,128)(2,1)S(1)}, u32[]{:S(2)}, u32[]{:S(2)}) %collective-permute-start.6) | collective-permute-done | bytes 65568 | tf_op jit(solution)/shard_map/ppermute | solution.py:26
  17.1 0.3 collective-permute-done.5.refs_6_
  17.4 0.7 %collective-permute-done.9.refs_5_ = bf16[2,144,128]{2,1,0:T(8,128)(2,1)S(1)} collective-permute-done((bf16[2,144,128]{2,1,0:T(8,128)(2,1)S(1)}, bf16[2,144,128]{2,1,0:T(8,128)(2,1)S(1)}, u32[]{:S(2)}, u32[]{:S(2)}) %collective-permute-start.9) | collective-permute-done | bytes 73760 | tf_op jit(solution)/shard_map/ppermute | solution.py:26
  18.2 0.4 collective-permute-done.10.refs_7_
  18.6 2.5 %attention.1 = (bf16[128,512]{1,0:T(8,128)(2,1)S(1)}, bf16[8,128,128]{2,1,0:T(8,128)(2,1)S(1)}) custom-call(s32[1]{0:T(128)} %bitcast.core_ref, s32[1,128]{1,0:T(1,128)S(1)} %bitcast.27, s32[1,128]{1,0:T(1,128)S(1)} %bitcast.28, bf16[128,256]{1,0:T(8,128)(2,1)S(1)} %copy-done.1, bf16[128,256]{1,0:T(8,128)(2,1)S(1)} %collective-permute-done.6.qo_ref, ...), custom_call_target="tpu_custom_call" | custom-call | flops 671088640 | bytes 1048576 | tf_op jit(solution)/shard_map/attention/pallas_call | solution.py:162
  21.1 0.7 %product.1 = bf16[128,4096]{1,0:T(8,128)(2,1)S(1)} custom-call(bf16[128,512]{1,0:T(8,128)(2,1)S(1)} %get-tuple-element.36.dq_ref, bf16[256,4096]{1,0:T(8,128)(2,1)S(1)} %get-tuple-element.37.wm_ref, bf16[256,4096]{1,0:T(8,128)(2,1)S(1)} %collective-permute-done.11.wo_ref), custom_call_target="tpu_custom_call" | custom-call | flops 536870912 | bytes 4194304 | tf_op jit(solution)/shard_map/product/pallas_call | solution.py:193
  21.9 1.6 %collective-permute-start.12 = (bf16[4,128,128]{2,1,0:T(8,128)(2,1)S(1)}, bf16[4,128,128]{2,1,0:T(8,128)(2,1)S(1)}, u32[]{:S(2)}, u32[]{:S(2)}) collective-permute-start(bf16[4,128,128]{2,1,0:T(8,128)(2,1)S(1)} %slice.26), channel_id=1, source_target_pairs={{0,4},{4,0},{8,12},{12,8},{16,20},{20,16},{24,28},{28,24},{1,5},{5... | collective-permute-start | bytes 393224 | tf_op jit(solution)/shard_map/ppermute | solution.py:26
  23.4 1.5 %collective-permute-start.18 = (bf16[128,4096]{1,0:T(8,128)(2,1)S(1)}, bf16[128,4096]{1,0:T(8,128)(2,1)S(1)}, u32[]{:S(2)}, u32[]{:S(2)}) collective-permute-start(bf16[128,4096]{1,0:T(8,128)(2,1)S(1)} %product.1), channel_id=1, source_target_pairs={{0,2},{1,3},{2,0},{3,1},{4,6},{5,7},{6,4},{7,5},{8,10},{9,11},{10,... | collective-permute-start | bytes 3145736 | tf_op jit(solution)/shard_map/ppermute | solution.py:26
  24.9 2.6 %collective-permute-done.12 = bf16[4,128,128]{2,1,0:T(8,128)(2,1)S(1)} collective-permute-done((bf16[4,128,128]{2,1,0:T(8,128)(2,1)S(1)}, bf16[4,128,128]{2,1,0:T(8,128)(2,1)S(1)}, u32[]{:S(2)}, u32[]{:S(2)}) %collective-permute-start.12) | collective-permute-done | bytes 131104 | tf_op jit(solution)/shard_map/ppermute | solution.py:26
  27.5 1.2 %collective-permute-start.13 = (bf16[128,128]{1,0:T(8,128)(2,1)S(1)}, bf16[128,128]{1,0:T(8,128)(2,1)S(1)}, u32[]{:S(2)}, u32[]{:S(2)}) collective-permute-start(bf16[128,128]{1,0:T(8,128)(2,1)S(1)} %get-tuple-element.49), channel_id=1, source_target_pairs={{0,8},{4,12},{8,0},{12,4},{16,24},{20,28},{24,16},{28,20},{1,9},{5... | collective-permute-start | bytes 98312 | tf_op jit(solution)/shard_map/ppermute | solution.py:26
  28.8 2.5 %collective-permute-start.14 = (bf16[128,128]{1,0:T(8,128)(2,1)S(1)}, bf16[128,128]{1,0:T(8,128)(2,1)S(1)}, u32[]{:S(2)}, u32[]{:S(2)}) collective-permute-start(bf16[128,128]{1,0:T(8,128)(2,1)S(1)} %get-tuple-element.51), channel_id=1, source_target_pairs={{0,24},{4,28},{8,16},{12,20},{16,8},{20,12},{24,0},{28,4},{1,25},{... | collective-permute-start | bytes 98312 | tf_op jit(solution)/shard_map/ppermute | solution.py:26
  31.3 0.3 collective-permute-done.13
  31.5 3.0 %collective-permute-done.14 = bf16[128,128]{1,0:T(8,128)(2,1)S(1)} collective-permute-done((bf16[128,128]{1,0:T(8,128)(2,1)S(1)}, bf16[128,128]{1,0:T(8,128)(2,1)S(1)}, u32[]{:S(2)}, u32[]{:S(2)}) %collective-permute-start.14) | collective-permute-done | bytes 32800 | tf_op jit(solution)/shard_map/ppermute | solution.py:26
  34.5 1.6 %collective-permute-done.15 = bf16[128,128]{1,0:T(8,128)(2,1)S(1)} collective-permute-done((bf16[128,128]{1,0:T(8,128)(2,1)S(1)}, bf16[128,128]{1,0:T(8,128)(2,1)S(1)}, u32[]{:S(2)}, u32[]{:S(2)}) %collective-permute-start.15) | collective-permute-done | bytes 32800 | tf_op jit(solution)/shard_map/ppermute | solution.py:26
  36.3 1.1 %collective-permute-done.16 = bf16[128,128]{1,0:T(8,128)(2,1)S(1)} collective-permute-done((bf16[128,128]{1,0:T(8,128)(2,1)S(1)}, bf16[128,128]{1,0:T(8,128)(2,1)S(1)}, u32[]{:S(2)}, u32[]{:S(2)}) %collective-permute-start.16) | collective-permute-done | bytes 32800 | tf_op jit(solution)/shard_map/ppermute | solution.py:26
  37.4 2.8 %carve.1 = (bf16[256,4096]{1,0:T(8,128)(2,1)S(1)}, bf16[256,4096]{1,0:T(8,128)(2,1)S(1)}) custom-call(s32[2]{0:T(128)S(1)} %pad_add_fusion.block_ref, bf16[256,16384]{1,0:T(8,128)(2,1)} %w_ref.2, bf16[128,256]{1,0:T(8,128)(2,1)S(1)} %pad_maximum_fusion.2.refs_0_.kv_ref), custom_call_target="tpu_custom_call" | custom-call | tf_op jit(solution)/shard_map/carve/pallas_call | solution.py:73
  40.2 0.8 %own.1 = (f32[128,4096]{1,0:T(8,128)S(1)}, bf16[128,2048]{1,0:T(8,128)(2,1)S(1)}, bf16[128,2048]{1,0:T(8,128)(2,1)S(1)}) custom-call(bf16[128,512]{1,0:T(8,128)(2,1)S(1)} %get-tuple-element.36.dq_ref, bf16[256,4096]{1,0:T(8,128)(2,1)S(1)} %get-tuple-element.40.wn_ref, bf16[256,4096]{1,0:T(8,128)(2,1)S(1)} %get-tuple-element.41.wo_ref), custom_call_target="tpu_custom_call" | custom-call | tf_op jit(solution)/shard_map/own/pallas_call | solution.py:218
  41.0 0.2 collective-permute-start.19
  41.2 0.4 collective-permute-start.20
  41.5 1.5 %collective-permute-start.17 = (bf16[128,256]{1,0:T(8,128)(2,1)S(1)}, bf16[128,256]{1,0:T(8,128)(2,1)S(1)}, u32[]{:S(2)}, u32[]{:S(2)}) collective-permute-start(bf16[128,256]{1,0:T(8,128)(2,1)S(1)} %pad_maximum_fusion.2.refs_0_.kv_ref), channel_id=1, source_target_pairs={{0,2},{1,3},{2,0},{3,1},{4,6},{5,7},{6,4},{7,5},{8,10},{9,11},{10,... | collective-permute-start | bytes 196616 | tf_op jit(solution)/shard_map/ppermute | solution.py:26
  43.1 6.7 %collective-permute-done.17.kv_far_ref = bf16[128,256]{1,0:T(8,128)(2,1)S(1)} collective-permute-done((bf16[128,256]{1,0:T(8,128)(2,1)S(1)}, bf16[128,256]{1,0:T(8,128)(2,1)S(1)}, u32[]{:S(2)}, u32[]{:S(2)}) %collective-permute-start.17) | collective-permute-done | bytes 65568 | tf_op jit(solution)/shard_map/ppermute | solution.py:26
  49.8 1.4 %finish.1 = bf16[128,4096]{1,0:T(8,128)(2,1)} custom-call(s32[1]{0:T(128)} %bitcast.core_ref, bf16[128,256]{1,0:T(8,128)(2,1)S(1)} %pad_maximum_fusion.2.refs_0_.kv_ref, bf16[128,256]{1,0:T(8,128)(2,1)S(1)} %collective-permute-done.17.kv_far_ref, bf16[256,4096]{1,0:T(8,128)(2,1)S(1)} %copy-done, f32[128,4096]{1,0:T(8,128)S(1)} %get-tuple-element.42.acc_ref, ...), custom_call_target="tpu_custom_call" | custom-call | flops 268435456 | bytes 5242880 | tf_op jit(solution)/shard_map/finish/pallas_call | solution.py:258
  (39 shorter events, 1.1 us)
Async XLA Ops:
  1.7 5.7 %collective-permute-start.2 = (bf16[144,128]{1,0:T(8,128)(2,1)S(1)}, bf16[144,128]{1,0:T(8,128)(2,1)S(1)}, u32[]{:S(2)}, u32[]{:S(2)}) collective-permute-start(bf16[144,128]{1,0:T(8,128)(2,1)S(1)} %get-tuple-element.53), channel_id=1, source_target_pairs={{0,8},{4,12},{8,0},{12,4},{16,24},{20,28},{24,16},{28,20},{1,9},{5... | collective-permute-start | bytes 110600 | tf_op jit(solution)/shard_map/ppermute | solution.py:26
  4.8 6.9 %collective-permute-start = (bf16[144,128]{1,0:T(8,128)(2,1)S(1)}, bf16[144,128]{1,0:T(8,128)(2,1)S(1)}, u32[]{:S(2)}, u32[]{:S(2)}) collective-permute-start(bf16[144,128]{1,0:T(8,128)(2,1)S(1)} %get-tuple-element.53), channel_id=1, source_target_pairs={{0,24},{4,28},{8,16},{12,20},{16,8},{20,12},{24,0},{28,4},{1,25},{... | collective-permute-start | bytes 110600 | tf_op jit(solution)/shard_map/ppermute | solution.py:26
  7.3 5.3 %collective-permute-start.1 = (bf16[144,128]{1,0:T(8,128)(2,1)S(1)}, bf16[144,128]{1,0:T(8,128)(2,1)S(1)}, u32[]{:S(2)}, u32[]{:S(2)}) collective-permute-start(bf16[144,128]{1,0:T(8,128)(2,1)S(1)} %get-tuple-element.53), channel_id=1, source_target_pairs={{0,16},{4,20},{8,24},{12,28},{16,0},{20,4},{24,8},{28,12},{1,17},{... | collective-permute-start | bytes 110600 | tf_op jit(solution)/shard_map/ppermute | solution.py:26
  7.4 6.8 %copy-start.1 = (bf16[128,256]{1,0:T(8,128)(2,1)S(1)}, bf16[128,256]{1,0:T(8,128)(2,1)}, u32[]{:S(2)}) copy-start(bf16[128,256]{1,0:T(8,128)(2,1)} %qm_ref) | copy-start | bytes 196612
  7.5 6.9 %copy-start.2 = (bf16[128,256]{1,0:T(8,128)(2,1)S(1)}, bf16[128,256]{1,0:T(8,128)(2,1)}, u32[]{:S(2)}) copy-start(bf16[128,256]{1,0:T(8,128)(2,1)} %gm_ref) | copy-start | bytes 196612
  7.5 11.2 %copy-start.3 = (s32[128]{0:T(128)S(1)}, s32[128]{0:T(128)}, u32[]{:S(2)}) copy-start(s32[128]{0:T(128)} %param.12) | copy-start | bytes 1540
  7.5 11.2 %copy-start.4 = (s32[128]{0:T(128)S(1)}, s32[128]{0:T(128)}, u32[]{:S(2)}) copy-start(s32[128]{0:T(128)} %param.13) | copy-start | bytes 1540
  7.5 5.1 %collective-permute-start.3 = (bf16[2,144,128]{2,1,0:T(8,128)(2,1)S(1)}, bf16[2,144,128]{2,1,0:T(8,128)(2,1)S(1)}, u32[]{:S(2)}, u32[]{:S(2)}) collective-permute-start(bf16[2,144,128]{2,1,0:T(8,128)(2,1)S(1)} %pad_maximum_fusion.1.refs_0_), channel_id=1, source_target_pairs={{0,4},{4,0},{8,12},{12,8},{16,20},{20,16},{24,28},{28,24},{1,5},{5... | collective-permute-start | bytes 221192 | tf_op jit(solution)/shard_map/ppermute | solution.py:26
  9.0 3.5 %collective-permute-start.4 = (bf16[2,144,128]{2,1,0:T(8,128)(2,1)S(1)}, bf16[2,144,128]{2,1,0:T(8,128)(2,1)S(1)}, u32[]{:S(2)}, u32[]{:S(2)}) collective-permute-start(bf16[2,144,128]{2,1,0:T(8,128)(2,1)S(1)} %pad_maximum_fusion.1.refs_0_), channel_id=1, source_target_pairs={{0,1},{1,0},{2,3},{3,2},{4,5},{5,4},{6,7},{7,6},{8,9},{9,8},{10,11... | collective-permute-start | bytes 221192 | tf_op jit(solution)/shard_map/ppermute | solution.py:26
  12.6 8.5 %collective-permute-start.11 = (bf16[256,4096]{1,0:T(8,128)(2,1)S(1)}, bf16[256,4096]{1,0:T(8,128)(2,1)S(1)}, u32[]{:S(2)}, u32[]{:S(2)}) collective-permute-start(bf16[256,4096]{1,0:T(8,128)(2,1)S(1)} %get-tuple-element.38), channel_id=1, source_target_pairs={{0,1},{1,0},{2,3},{3,2},{4,5},{5,4},{6,7},{7,6},{8,9},{9,8},{10,11... | collective-permute-start | bytes 6291464 | tf_op jit(solution)/shard_map/ppermute | solution.py:26
  12.7 4.7 %collective-permute-start.5 = (bf16[2,144,128]{2,1,0:T(8,128)(2,1)S(1)}, bf16[2,144,128]{2,1,0:T(8,128)(2,1)S(1)}, u32[]{:S(2)}, u32[]{:S(2)}) collective-permute-start(bf16[2,144,128]{2,1,0:T(8,128)(2,1)S(1)} %pad_maximum_fusion.refs_2_), channel_id=1, source_target_pairs={{0,4},{4,0},{8,12},{12,8},{16,20},{20,16},{24,28},{28,24},{1,5},{5... | collective-permute-start | bytes 221192 | tf_op jit(solution)/shard_map/ppermute | solution.py:26
  14.2 2.7 %collective-permute-start.6 = (bf16[128,256]{1,0:T(8,128)(2,1)S(1)}, bf16[128,256]{1,0:T(8,128)(2,1)S(1)}, u32[]{:S(2)}, u32[]{:S(2)}) collective-permute-start(bf16[128,256]{1,0:T(8,128)(2,1)S(1)} %copy-done.1), channel_id=1, source_target_pairs={{0,1},{1,0},{2,3},{3,2},{4,5},{5,4},{6,7},{7,6},{8,9},{9,8},{10,11... | collective-permute-start | bytes 196616 | tf_op jit(solution)/shard_map/ppermute | solution.py:26
  14.4 2.7 %collective-permute-start.7 = (bf16[128,256]{1,0:T(8,128)(2,1)S(1)}, bf16[128,256]{1,0:T(8,128)(2,1)S(1)}, u32[]{:S(2)}, u32[]{:S(2)}) collective-permute-start(bf16[128,256]{1,0:T(8,128)(2,1)S(1)} %copy-done.2), channel_id=1, source_target_pairs={{0,1},{1,0},{2,3},{3,2},{4,5},{5,4},{6,7},{7,6},{8,9},{9,8},{10,11... | collective-permute-start | bytes 196616 | tf_op jit(solution)/shard_map/ppermute | solution.py:26
  14.7 2.7 %collective-permute-start.8 = (bf16[2,144,128]{2,1,0:T(8,128)(2,1)S(1)}, bf16[2,144,128]{2,1,0:T(8,128)(2,1)S(1)}, u32[]{:S(2)}, u32[]{:S(2)}) collective-permute-start(bf16[2,144,128]{2,1,0:T(8,128)(2,1)S(1)} %pad_maximum_fusion.refs_2_), channel_id=1, source_target_pairs={{0,1},{1,0},{2,3},{3,2},{4,5},{5,4},{6,7},{7,6},{8,9},{9,8},{10,11... | collective-permute-start | bytes 221192 | tf_op jit(solution)/shard_map/ppermute | solution.py:26
  16.9 1.3 %collective-permute-start.9 = (bf16[2,144,128]{2,1,0:T(8,128)(2,1)S(1)}, bf16[2,144,128]{2,1,0:T(8,128)(2,1)S(1)}, u32[]{:S(2)}, u32[]{:S(2)}) collective-permute-start(bf16[2,144,128]{2,1,0:T(8,128)(2,1)S(1)} %collective-permute-done.3.refs_4_), channel_id=1, source_target_pairs={{0,1},{1,0},{2,3},{3,2},{4,5},{5,4},{6,7},{7,6},{8,9},{9,8},{10,11... | collective-permute-start | bytes 221192 | tf_op jit(solution)/shard_map/ppermute | solution.py:26
  17.4 1.3 %collective-permute-start.10 = (bf16[2,144,128]{2,1,0:T(8,128)(2,1)S(1)}, bf16[2,144,128]{2,1,0:T(8,128)(2,1)S(1)}, u32[]{:S(2)}, u32[]{:S(2)}) collective-permute-start(bf16[2,144,128]{2,1,0:T(8,128)(2,1)S(1)} %collective-permute-done.5.refs_6_), channel_id=1, source_target_pairs={{0,1},{1,0},{2,3},{3,2},{4,5},{5,4},{6,7},{7,6},{8,9},{9,8},{10,11... | collective-permute-start | bytes 221192 | tf_op jit(solution)/shard_map/ppermute | solution.py:26
  21.9 5.6 %collective-permute-start.12 = (bf16[4,128,128]{2,1,0:T(8,128)(2,1)S(1)}, bf16[4,128,128]{2,1,0:T(8,128)(2,1)S(1)}, u32[]{:S(2)}, u32[]{:S(2)}) collective-permute-start(bf16[4,128,128]{2,1,0:T(8,128)(2,1)S(1)} %slice.26), channel_id=1, source_target_pairs={{0,4},{4,0},{8,12},{12,8},{16,20},{20,16},{24,28},{28,24},{1,5},{5... | collective-permute-start | bytes 393224 | tf_op jit(solution)/shard_map/ppermute | solution.py:26
  23.4 26.4 %collective-permute-start.18 = (bf16[128,4096]{1,0:T(8,128)(2,1)S(1)}, bf16[128,4096]{1,0:T(8,128)(2,1)S(1)}, u32[]{:S(2)}, u32[]{:S(2)}) collective-permute-start(bf16[128,4096]{1,0:T(8,128)(2,1)S(1)} %product.1), channel_id=1, source_target_pairs={{0,2},{1,3},{2,0},{3,1},{4,6},{5,7},{6,4},{7,5},{8,10},{9,11},{10,... | collective-permute-start | bytes 3145736 | tf_op jit(solution)/shard_map/ppermute | solution.py:26
  27.5 4.0 %collective-permute-start.13 = (bf16[128,128]{1,0:T(8,128)(2,1)S(1)}, bf16[128,128]{1,0:T(8,128)(2,1)S(1)}, u32[]{:S(2)}, u32[]{:S(2)}) collective-permute-start(bf16[128,128]{1,0:T(8,128)(2,1)S(1)} %get-tuple-element.49), channel_id=1, source_target_pairs={{0,8},{4,12},{8,0},{12,4},{16,24},{20,28},{24,16},{28,20},{1,9},{5... | collective-permute-start | bytes 98312 | tf_op jit(solution)/shard_map/ppermute | solution.py:26
  28.8 5.7 %collective-permute-start.14 = (bf16[128,128]{1,0:T(8,128)(2,1)S(1)}, bf16[128,128]{1,0:T(8,128)(2,1)S(1)}, u32[]{:S(2)}, u32[]{:S(2)}) collective-permute-start(bf16[128,128]{1,0:T(8,128)(2,1)S(1)} %get-tuple-element.51), channel_id=1, source_target_pairs={{0,24},{4,28},{8,16},{12,20},{16,8},{20,12},{24,0},{28,4},{1,25},{... | collective-permute-start | bytes 98312 | tf_op jit(solution)/shard_map/ppermute | solution.py:26
  31.3 4.9 %collective-permute-start.15 = (bf16[128,128]{1,0:T(8,128)(2,1)S(1)}, bf16[128,128]{1,0:T(8,128)(2,1)S(1)}, u32[]{:S(2)}, u32[]{:S(2)}) collective-permute-start(bf16[128,128]{1,0:T(8,128)(2,1)S(1)} %get-tuple-element.50), channel_id=1, source_target_pairs={{0,16},{4,20},{8,24},{12,28},{16,0},{20,4},{24,8},{28,12},{1,17},{... | collective-permute-start | bytes 98312 | tf_op jit(solution)/shard_map/ppermute | solution.py:26
  36.1 1.3 %collective-permute-start.16 = (bf16[128,128]{1,0:T(8,128)(2,1)S(1)}, bf16[128,128]{1,0:T(8,128)(2,1)S(1)}, u32[]{:S(2)}, u32[]{:S(2)}) collective-permute-start(bf16[128,128]{1,0:T(8,128)(2,1)S(1)} %fusion.3), channel_id=1, source_target_pairs={{0,1},{1,0},{2,3},{3,2},{4,5},{5,4},{6,7},{7,6},{8,9},{9,8},{10,11... | collective-permute-start | bytes 98312 | tf_op jit(solution)/shard_map/ppermute | solution.py:26
  40.2 9.6 %copy-start = (bf16[256,4096]{1,0:T(8,128)(2,1)S(1)}, bf16[256,4096]{1,0:T(8,128)(2,1)}, u32[]{:S(2)}) copy-start(bf16[256,4096]{1,0:T(8,128)(2,1)} %w_ref.3) | copy-start | bytes 6291460
  41.0 8.8 %collective-permute-start.19 = (bf16[128,2048]{1,0:T(8,128)(2,1)S(1)}, bf16[128,2048]{1,0:T(8,128)(2,1)S(1)}, u32[]{:S(2)}, u32[]{:S(2)}) collective-permute-start(bf16[128,2048]{1,0:T(8,128)(2,1)S(1)} %get-tuple-element.43), channel_id=1, source_target_pairs={{0,1},{1,0},{2,3},{3,2},{4,5},{5,4},{6,7},{7,6},{8,9},{9,8},{10,11... | collective-permute-start | bytes 1572872 | tf_op jit(solution)/shard_map/ppermute | solution.py:26
  41.2 8.6 %collective-permute-start.20 = (bf16[128,2048]{1,0:T(8,128)(2,1)S(1)}, bf16[128,2048]{1,0:T(8,128)(2,1)S(1)}, u32[]{:S(2)}, u32[]{:S(2)}) collective-permute-start(bf16[128,2048]{1,0:T(8,128)(2,1)S(1)} %get-tuple-element.44), channel_id=1, source_target_pairs={{0,1},{1,0},{2,3},{3,2},{4,5},{5,4},{6,7},{7,6},{8,9},{9,8},{10,11... | collective-permute-start | bytes 1572872 | tf_op jit(solution)/shard_map/ppermute | solution.py:26
  41.5 8.2 %collective-permute-start.17 = (bf16[128,256]{1,0:T(8,128)(2,1)S(1)}, bf16[128,256]{1,0:T(8,128)(2,1)S(1)}, u32[]{:S(2)}, u32[]{:S(2)}) collective-permute-start(bf16[128,256]{1,0:T(8,128)(2,1)S(1)} %pad_maximum_fusion.2.refs_0_.kv_ref), channel_id=1, source_target_pairs={{0,2},{1,3},{2,0},{3,1},{4,6},{5,7},{6,4},{7,5},{8,10},{9,11},{10,... | collective-permute-start | bytes 196616 | tf_op jit(solution)/shard_map/ppermute | solution.py:26
